TPU v7x, 32 devices: a whole 2x2x4 slice. The times are simulated.
32 devices in a mesh: slab: 2 (over y), dom: 4 (over z), band: 2 (over x), sub: 2 (over core).
Axes of the slice: x: 2, y: 2, z: 4, core: 2. Of those that a mesh axis runs over, the one named last changes fastest.
Arguments:
- panel: float32 [256, 12, 32, 128], P(('slab', 'band', 'sub'), 'dom'), parts along dimension 0, may hold values from -6 to 6
- potential: float32 [24, 32, 128], P(('slab', 'dom')), parts along dimension 0, may hold values from 0 to 1
- point_offsets: int32 [384, 3, 128], P(('slab', 'dom')), parts along dimension 0, may hold values from -1 to 12287, as said below
- point_coefs: float32 [384, 3, 8, 128], P(('slab', 'dom')), parts along dimension 0, may hold values from -0.2 to 0.2
- correlation: float32 [384, 8, 8], P(('slab', 'dom')), parts along dimension 0, may hold values from -6 to 6
Outputs:
- filtered: float32 [256, 12, 32, 128], P(('slab', 'band', 'sub'), 'dom'), parts along dimension 0
- gram: float32 [256, 128], P(('slab', 'band', 'sub')), parts along dimension 0
There are 2 independent parts, one for each index of `slab`. A program takes and returns all parts, laid end to end along the dimension named above; each array names one. Nothing has to cross between parts.
Inputs may be any that keep to these rules, and one draw needn't show every extreme that they name: `point_offsets`: entry [h * 48 + j, r, k] is the k-th point, as a flat index within grid block h, of the projector of atom j of home block (h + r - 1) mod 4; -1 marks a padded entry, and the live entries of one atom in one block come first.
All inputs are finite; a program needn't handle non-finite values.
Results may differ from a plain program's by a relative error of at most 0.0003.
Values sent between devices are 32-bit elements; how exact they have to be, the bound alone decides.
No kernel may reach another device: no remote copies, remote signals or barrier semaphores. Data moves between devices by JAX's collectives and lax.ppermute only.
A program may use at most 64 MiB of HBM per device.

v0:
```python
import math

import jax
import jax.numpy as jnp
from jax import lax
from jax.sharding import PartitionSpec as P

DEGREE = 12


center_level = 3.6
half_width = 3.4


def with_halo(block, sides, width):
    for axis, dim in sides:
        count = lax.axis_size(axis)
        forward = [(i, i + 1) for i in range(count - 1)]
        forward.append((count - 1, 0))
        backward = [(target, source) for source, target in forward]
        low = lax.ppermute(
            lax.slice_in_dim(block, block.shape[dim] - width, None, axis=dim), axis, forward
        )
        high = lax.ppermute(lax.slice_in_dim(block, 0, width, axis=dim), axis, backward)
        block = jnp.concatenate([low, block, high], axis=dim)
    return block


def passed_along(x, axis, by):
    size = lax.axis_size(axis)
    return lax.ppermute(x, axis, [(i, (i + by) % size) for i in range(size)])


def operator(extended, local_potential):
    centre_part = extended[:, 1:-1]
    along_x = extended[:, 2:] + extended[:, :-2]
    along_y = jnp.roll(centre_part, 1, axis=2) + jnp.roll(centre_part, -1, axis=2)
    zero_plane = jnp.zeros_like(centre_part[..., :1])
    along_z = jnp.concatenate([centre_part[..., 1:], zero_plane], axis=3) + jnp.concatenate(
        [zero_plane, centre_part[..., :-1]], axis=3
    )
    hamiltonian = (local_potential + 3.0) * centre_part - 0.5 * (along_x + along_y + along_z)
    return (hamiltonian - center_level * centre_part) / half_width


def apply_once(field, local_potential):
    extended = with_halo(field, (("dom", 1),), 1)
    return operator(extended, local_potential)


def on_device(panel, potential, point_offsets, point_coefs, correlation):
    first_field = apply_once(panel, potential)

    def one_step(step_index, carry):
        before, current = carry
        return (current, 2.0 * apply_once(current, potential) - before)

    before, current = lax.fori_loop(0, DEGREE - 1, one_step, (panel, first_field))
    orbitals = current.shape[0]
    flat_panel = current.reshape(orbitals, -1)
    live_mask = point_offsets >= 0
    safe_offsets = jnp.maximum(point_offsets, 0)
    picked = jnp.where(live_mask[None], flat_panel[:, safe_offsets], 0.0)
    partial_value = jnp.einsum(
        "oark,arpk->roap", picked, point_coefs, precision=lax.Precision.HIGHEST
    )
    from_right = passed_along(partial_value[0], "dom", -1)
    from_left = passed_along(partial_value[2], "dom", 1)
    projections = partial_value[1] + from_right + from_left
    weighted = jnp.einsum("apq,oaq->oap", correlation, projections, precision=lax.Precision.HIGHEST)
    domains = lax.axis_size("dom")
    inv_points = 1.0 / (flat_panel.shape[1] * domains)
    atom_scale = 1.0 / math.sqrt(point_offsets.shape[0] * domains)
    left_rows = jnp.concatenate([flat_panel, projections.reshape(orbitals, -1)], axis=1)
    right_rows = jnp.concatenate(
        [flat_panel * inv_points, weighted.reshape(orbitals, -1) * atom_scale], axis=1
    )
    left_all, right_all = (
        lax.all_to_all(left_rows, ("band", "sub"), split_axis=1, concat_axis=0, tiled=True),
        lax.all_to_all(right_rows, ("band", "sub"), split_axis=1, concat_axis=0, tiled=True),
    )
    whole_gram = jnp.einsum("or,pr->op", left_all, right_all, precision=lax.Precision.HIGHEST)
    total_gram = lax.psum(whole_gram, ("dom", "band", "sub"))
    gram_rows = lax.dynamic_slice_in_dim(
        total_gram, lax.axis_index(("band", "sub")) * orbitals, orbitals, 0
    )
    return (current, gram_rows)


def solution(mesh):
    placed = (
        P(("slab", "band", "sub"), "dom", None, None),
        P(("slab", "dom"), None, None),
        P(("slab", "dom"), None, None),
        P(("slab", "dom"), None, None, None),
        P(("slab", "dom"), None, None),
    )
    return jax.shard_map(
        on_device,
        mesh=mesh,
        in_specs=placed,
        out_specs=(P(("slab", "band", "sub"), "dom", None, None), P(("slab", "band", "sub"), None)),
        check_vma=False,
    )
```

profile of v0, /device:TPU:0, one launch (start us, length us, event | category | flops | bytes accessed | tf_op | source)
XLA Modules:
  0.0 610.8 jit_solution(13469655597077252600)
XLA Ops:
  8.7 5.1 collective-permute-start.2
  13.8 2.2 fusion.34
  20.3 5.8 collective-permute-done.2
  26.2 11.0 %collective-permute-done.3 = f32[32,1,32,128]{3,2,1,0:T(8,128)S(1)} collective-permute-done((f32[32,1,32,128]{3,2,1,0:T(8,128)S(1)}, f32[32,1,32,128]{3,2,1,0:T(8,128)S(1)}, u32[]{:S(2)}, u32[]{:S(2)}) %collective-permute-start.3) | collective-permute-done | bytes 524320 | tf_op jit(solution)/shard_map/ppermute | solution.py:21
  37.1 5.2 fusion.17
  42.3 320.7 %while.14 = (s32[]{:T(128)}, f32[32,3,32,128]{3,2,1,0:T(8,128)}, f32[32,3,32,128]{3,2,1,0:T(8,128)S(1)}, f32[3,32,128]{2,1,0:T(8,128)S(1)}, s32[]{:T(128)}) while((s32[]{:T(128)}, f32[32,3,32,128]{3,2,1,0:T(8,128)}, f32[32,3,32,128]{3,2,1,0:T(8,128)S(1)}, f32[3,32,128]{2,1,0:T(8,128)S(1)}, s32[]{:T(128)}) %tuple.53), condition=%wide.region_1.2_spmd, body=%wide.region_0.1_spmd.sunk | while | flops 6303746 | bytes 55779552 | solution.py:58
  45.0 2.2 collective-permute-start.1
  47.2 2.1 fusion.48
  50.0 10.3 %collective-permute-done = f32[32,1,32,128]{3,2,1,0:T(8,128)S(1)} collective-permute-done((f32[32,1,32,128]{3,2,1,0:T(8,128)}, f32[32,1,32,128]{3,2,1,0:T(8,128)S(1)}, u32[]{:S(2)}, u32[]{:S(2)}) %collective-permute-start) | collective-permute-done | bytes 524320 | tf_op jit(solution)/shard_map/while/body/eval_jaxpr/ppermute | solution.py:21
  60.3 8.7 %collective-permute-done.1 = f32[32,1,32,128]{3,2,1,0:T(8,128)S(1)} collective-permute-done((f32[32,1,32,128]{3,2,1,0:T(8,128)}, f32[32,1,32,128]{3,2,1,0:T(8,128)S(1)}, u32[]{:S(2)}, u32[]{:S(2)}) %collective-permute-start.1) | collective-permute-done | bytes 524320 | tf_op jit(solution)/shard_map/while/body/eval_jaxpr/ppermute | solution.py:24
  73.2 3.5 collective-permute-start.1
  76.7 2.1 fusion.48
  79.5 10.3 %collective-permute-done = f32[32,1,32,128]{3,2,1,0:T(8,128)S(1)} collective-permute-done((f32[32,1,32,128]{3,2,1,0:T(8,128)}, f32[32,1,32,128]{3,2,1,0:T(8,128)S(1)}, u32[]{:S(2)}, u32[]{:S(2)}) %collective-permute-start) | collective-permute-done | bytes 524320 | tf_op jit(solution)/shard_map/while/body/eval_jaxpr/ppermute | solution.py:21
  89.8 7.9 %collective-permute-done.1 = f32[32,1,32,128]{3,2,1,0:T(8,128)S(1)} collective-permute-done((f32[32,1,32,128]{3,2,1,0:T(8,128)}, f32[32,1,32,128]{3,2,1,0:T(8,128)S(1)}, u32[]{:S(2)}, u32[]{:S(2)}) %collective-permute-start.1) | collective-permute-done | bytes 524320 | tf_op jit(solution)/shard_map/while/body/eval_jaxpr/ppermute | solution.py:24
  101.6 3.8 collective-permute-start.1
  105.4 2.1 fusion.48
  108.2 10.3 %collective-permute-done = f32[32,1,32,128]{3,2,1,0:T(8,128)S(1)} collective-permute-done((f32[32,1,32,128]{3,2,1,0:T(8,128)}, f32[32,1,32,128]{3,2,1,0:T(8,128)S(1)}, u32[]{:S(2)}, u32[]{:S(2)}) %collective-permute-start) | collective-permute-done | bytes 524320 | tf_op jit(solution)/shard_map/while/body/eval_jaxpr/ppermute | solution.py:21
  118.4 8.0 %collective-permute-done.1 = f32[32,1,32,128]{3,2,1,0:T(8,128)S(1)} collective-permute-done((f32[32,1,32,128]{3,2,1,0:T(8,128)}, f32[32,1,32,128]{3,2,1,0:T(8,128)S(1)}, u32[]{:S(2)}, u32[]{:S(2)}) %collective-permute-start.1) | collective-permute-done | bytes 524320 | tf_op jit(solution)/shard_map/while/body/eval_jaxpr/ppermute | solution.py:24
  131.4 2.7 collective-permute-start.1
  134.1 2.1 fusion.48
  136.9 10.3 %collective-permute-done = f32[32,1,32,128]{3,2,1,0:T(8,128)S(1)} collective-permute-done((f32[32,1,32,128]{3,2,1,0:T(8,128)}, f32[32,1,32,128]{3,2,1,0:T(8,128)S(1)}, u32[]{:S(2)}, u32[]{:S(2)}) %collective-permute-start) | collective-permute-done | bytes 524320 | tf_op jit(solution)/shard_map/while/body/eval_jaxpr/ppermute | solution.py:21
  147.2 9.2 %collective-permute-done.1 = f32[32,1,32,128]{3,2,1,0:T(8,128)S(1)} collective-permute-done((f32[32,1,32,128]{3,2,1,0:T(8,128)}, f32[32,1,32,128]{3,2,1,0:T(8,128)S(1)}, u32[]{:S(2)}, u32[]{:S(2)}) %collective-permute-start.1) | collective-permute-done | bytes 524320 | tf_op jit(solution)/shard_map/while/body/eval_jaxpr/ppermute | solution.py:24
  160.6 3.5 collective-permute-start.1
  164.1 2.1 fusion.48
  166.9 10.2 %collective-permute-done = f32[32,1,32,128]{3,2,1,0:T(8,128)S(1)} collective-permute-done((f32[32,1,32,128]{3,2,1,0:T(8,128)}, f32[32,1,32,128]{3,2,1,0:T(8,128)S(1)}, u32[]{:S(2)}, u32[]{:S(2)}) %collective-permute-start) | collective-permute-done | bytes 524320 | tf_op jit(solution)/shard_map/while/body/eval_jaxpr/ppermute | solution.py:21
  177.1 8.0 %collective-permute-done.1 = f32[32,1,32,128]{3,2,1,0:T(8,128)S(1)} collective-permute-done((f32[32,1,32,128]{3,2,1,0:T(8,128)}, f32[32,1,32,128]{3,2,1,0:T(8,128)S(1)}, u32[]{:S(2)}, u32[]{:S(2)}) %collective-permute-start.1) | collective-permute-done | bytes 524320 | tf_op jit(solution)/shard_map/while/body/eval_jaxpr/ppermute | solution.py:24
  189.8 3.1 collective-permute-start.1
  192.9 2.1 fusion.48
  195.7 10.3 %collective-permute-done = f32[32,1,32,128]{3,2,1,0:T(8,128)S(1)} collective-permute-done((f32[32,1,32,128]{3,2,1,0:T(8,128)}, f32[32,1,32,128]{3,2,1,0:T(8,128)S(1)}, u32[]{:S(2)}, u32[]{:S(2)}) %collective-permute-start) | collective-permute-done | bytes 524320 | tf_op jit(solution)/shard_map/while/body/eval_jaxpr/ppermute | solution.py:21
  205.9 8.1 %collective-permute-done.1 = f32[32,1,32,128]{3,2,1,0:T(8,128)S(1)} collective-permute-done((f32[32,1,32,128]{3,2,1,0:T(8,128)}, f32[32,1,32,128]{3,2,1,0:T(8,128)S(1)}, u32[]{:S(2)}, u32[]{:S(2)}) %collective-permute-start.1) | collective-permute-done | bytes 524320 | tf_op jit(solution)/shard_map/while/body/eval_jaxpr/ppermute | solution.py:24
  219.0 2.8 collective-permute-start.1
  221.7 2.1 fusion.48
  224.5 10.3 %collective-permute-done = f32[32,1,32,128]{3,2,1,0:T(8,128)S(1)} collective-permute-done((f32[32,1,32,128]{3,2,1,0:T(8,128)}, f32[32,1,32,128]{3,2,1,0:T(8,128)S(1)}, u32[]{:S(2)}, u32[]{:S(2)}) %collective-permute-start) | collective-permute-done | bytes 524320 | tf_op jit(solution)/shard_map/while/body/eval_jaxpr/ppermute | solution.py:21
  234.8 9.2 %collective-permute-done.1 = f32[32,1,32,128]{3,2,1,0:T(8,128)S(1)} collective-permute-done((f32[32,1,32,128]{3,2,1,0:T(8,128)}, f32[32,1,32,128]{3,2,1,0:T(8,128)S(1)}, u32[]{:S(2)}, u32[]{:S(2)}) %collective-permute-start.1) | collective-permute-done | bytes 524320 | tf_op jit(solution)/shard_map/while/body/eval_jaxpr/ppermute | solution.py:24
  248.2 3.5 collective-permute-start.1
  251.7 2.1 fusion.48
  254.5 10.3 %collective-permute-done = f32[32,1,32,128]{3,2,1,0:T(8,128)S(1)} collective-permute-done((f32[32,1,32,128]{3,2,1,0:T(8,128)}, f32[32,1,32,128]{3,2,1,0:T(8,128)S(1)}, u32[]{:S(2)}, u32[]{:S(2)}) %collective-permute-start) | collective-permute-done | bytes 524320 | tf_op jit(solution)/shard_map/while/body/eval_jaxpr/ppermute | solution.py:21
  264.7 7.9 %collective-permute-done.1 = f32[32,1,32,128]{3,2,1,0:T(8,128)S(1)} collective-permute-done((f32[32,1,32,128]{3,2,1,0:T(8,128)}, f32[32,1,32,128]{3,2,1,0:T(8,128)S(1)}, u32[]{:S(2)}, u32[]{:S(2)}) %collective-permute-start.1) | collective-permute-done | bytes 524320 | tf_op jit(solution)/shard_map/while/body/eval_jaxpr/ppermute | solution.py:24
  277.4 3.0 collective-permute-start.1
  283.2 10.3 %collective-permute-done = f32[32,1,32,128]{3,2,1,0:T(8,128)S(1)} collective-permute-done((f32[32,1,32,128]{3,2,1,0:T(8,128)}, f32[32,1,32,128]{3,2,1,0:T(8,128)S(1)}, u32[]{:S(2)}, u32[]{:S(2)}) %collective-permute-start) | collective-permute-done | bytes 524320 | tf_op jit(solution)/shard_map/while/body/eval_jaxpr/ppermute | solution.py:21
  293.5 8.0 %collective-permute-done.1 = f32[32,1,32,128]{3,2,1,0:T(8,128)S(1)} collective-permute-done((f32[32,1,32,128]{3,2,1,0:T(8,128)}, f32[32,1,32,128]{3,2,1,0:T(8,128)S(1)}, u32[]{:S(2)}, u32[]{:S(2)}) %collective-permute-start.1) | collective-permute-done | bytes 524320 | tf_op jit(solution)/shard_map/while/body/eval_jaxpr/ppermute | solution.py:24
  306.4 2.7 collective-permute-start.1
  312.0 10.3 %collective-permute-done = f32[32,1,32,128]{3,2,1,0:T(8,128)S(1)} collective-permute-done((f32[32,1,32,128]{3,2,1,0:T(8,128)}, f32[32,1,32,128]{3,2,1,0:T(8,128)S(1)}, u32[]{:S(2)}, u32[]{:S(2)}) %collective-permute-start) | collective-permute-done | bytes 524320 | tf_op jit(solution)/shard_map/while/body/eval_jaxpr/ppermute | solution.py:21
  322.2 9.2 %collective-permute-done.1 = f32[32,1,32,128]{3,2,1,0:T(8,128)S(1)} collective-permute-done((f32[32,1,32,128]{3,2,1,0:T(8,128)}, f32[32,1,32,128]{3,2,1,0:T(8,128)S(1)}, u32[]{:S(2)}, u32[]{:S(2)}) %collective-permute-start.1) | collective-permute-done | bytes 524320 | tf_op jit(solution)/shard_map/while/body/eval_jaxpr/ppermute | solution.py:24
  335.6 3.5 collective-permute-start.1
  339.2 2.1 fusion.48
  342.0 10.2 %collective-permute-done = f32[32,1,32,128]{3,2,1,0:T(8,128)S(1)} collective-permute-done((f32[32,1,32,128]{3,2,1,0:T(8,128)}, f32[32,1,32,128]{3,2,1,0:T(8,128)S(1)}, u32[]{:S(2)}, u32[]{:S(2)}) %collective-permute-start) | collective-permute-done | bytes 524320 | tf_op jit(solution)/shard_map/while/body/eval_jaxpr/ppermute | solution.py:21
  352.2 8.0 %collective-permute-done.1 = f32[32,1,32,128]{3,2,1,0:T(8,128)S(1)} collective-permute-done((f32[32,1,32,128]{3,2,1,0:T(8,128)}, f32[32,1,32,128]{3,2,1,0:T(8,128)S(1)}, u32[]{:S(2)}, u32[]{:S(2)}) %collective-permute-start.1) | collective-permute-done | bytes 524320 | tf_op jit(solution)/shard_map/while/body/eval_jaxpr/ppermute | solution.py:24
  363.1 4.0 copy.18
  367.0 64.4 %gather_fusion = f32[18432,32]{1,0:T(8,128)} fusion(f32[32,12288]{0,1:T(8,128)} %bitcast.38, s32[18432]{0:T(1024)S(1)} %broadcast_clamp_fusion), kind=kCustom, calls=%fused_computation | custom fusion | bytes 4792320 | tf_op jit(solution)/shard_map/gather | solution.py:63
  431.4 5.5 copy.20
  436.9 4.5 fusion.18
  444.3 4.8 broadcast_multiply_fusion
  449.1 5.6 copy.22
  454.7 4.4 copy.26
  462.6 2.5 all_to_all.32
  466.5 3.6 all-to-all-start.1
  470.2 2.7 pad_maximum_fusion.2
  472.9 3.3 all_to_all.28
  476.3 2.7 copy.24
  479.0 11.8 %all-to-all-done.1 = f32[32,4,3168]{2,0,1:T(8,128)S(1)} async-done(((f32[32,4,3168]{2,0,1:T(8,128)}), f32[32,4,3168]{2,0,1:T(8,128)S(1)}, u32[]{:S(2)}, u32[]{:S(2)}) %all-to-all-start.1) | async-done | bytes 1622048 | tf_op jit(solution)/shard_map/all_to_all | solution.py:80
  490.8 24.3 %all_to_all.38 = f32[32,4,3168]{2,0,1:T(8,128)S(1)} all-to-all(f32[32,4,3168]{2,0,1:T(8,128)} %copy.24), channel_id=1, replica_groups=mesh['slab'=2,'dom'=4,'band'=2,'sub'=2] {'band','sub'}, dimensions={1} | all-to-all | bytes 3244032 | tf_op jit(solution)/shard_map/all_to_all | solution.py:79
  515.1 2.3 fusion.38
  517.5 85.2 %all-reduce.6.cloned.1.call-done = f32[128,128]{1,0:T(8,128)} async-done(((f32[128,128]{1,0:T(8,128)}), f32[128,128]{1,0:T(8,128)}) %all-reduce.6.cloned.1.call-update) | async-done | bytes 65552 | tf_op jit(solution)/shard_map/psum | solution.py:83
  (196 shorter events, 76.5 us)
Async XLA Ops:
  7.2 429.8 %copy-start = (f32[48,3,8,128]{3,2,1,0:T(8,128)S(1)}, f32[48,3,8,128]{3,2,1,0:T(8,128)}, u32[]{:S(2)}) copy-start(f32[48,3,8,128]{3,2,1,0:T(8,128)} %param.10) | copy-start | bytes 1769476
  8.6 9.5 %copy-start.2 = (f32[32,3,32,128]{3,2,1,0:T(8,128)}, f32[32,3,32,128]{3,2,1,0:T(8,128)S(1)}, u32[]{:S(2)}) copy-start(f32[32,3,32,128]{3,2,1,0:T(8,128)S(1)} %copy.42) | copy-start | bytes 4718596
  8.7 17.4 %collective-permute-start.2 = (f32[32,1,32,128]{3,2,1,0:T(8,128)S(1)}, f32[32,1,32,128]{3,2,1,0:T(8,128)S(1)}, u32[]{:S(2)}, u32[]{:S(2)}) collective-permute-start(f32[32,1,32,128]{3,2,1,0:T(8,128)S(1)} %get-tuple-element.78), channel_id=1, source_target_pairs={{4,0},{8,4},{12,8},{0,12},{5,1},{9,5},{13,9},{1,13},{6,2},{10,6},{... | collective-permute-start | bytes 1572872 | tf_op jit(solution)/shard_map/ppermute | solution.py:24
  13.8 23.3 %collective-permute-start.3 = (f32[32,1,32,128]{3,2,1,0:T(8,128)S(1)}, f32[32,1,32,128]{3,2,1,0:T(8,128)S(1)}, u32[]{:S(2)}, u32[]{:S(2)}) collective-permute-start(f32[32,1,32,128]{3,2,1,0:T(8,128)S(1)} %get-tuple-element.79), channel_id=1, source_target_pairs={{0,4},{4,8},{8,12},{12,0},{1,5},{5,9},{9,13},{13,1},{2,6},{6,10},{... | collective-permute-start | bytes 1572872 | tf_op jit(solution)/shard_map/ppermute | solution.py:21
  43.4 16.9 %collective-permute-start = (f32[32,1,32,128]{3,2,1,0:T(8,128)}, f32[32,1,32,128]{3,2,1,0:T(8,128)S(1)}, u32[]{:S(2)}, u32[]{:S(2)}) collective-permute-start(f32[32,1,32,128]{3,2,1,0:T(8,128)} %get-tuple-element.115), channel_id=1, source_target_pairs={{0,4},{4,8},{8,12},{12,0},{1,5},{5,9},{9,13},{13,1},{2,6},{6,10},{... | collective-permute-start | bytes 1572872 | tf_op jit(solution)/shard_map/while/body/eval_jaxpr/ppermute | solution.py:21
  45.0 24.0 %collective-permute-start.1 = (f32[32,1,32,128]{3,2,1,0:T(8,128)}, f32[32,1,32,128]{3,2,1,0:T(8,128)S(1)}, u32[]{:S(2)}, u32[]{:S(2)}) collective-permute-start(f32[32,1,32,128]{3,2,1,0:T(8,128)} %get-tuple-element.116), channel_id=1, source_target_pairs={{4,0},{8,4},{12,8},{0,12},{5,1},{9,5},{13,9},{1,13},{6,2},{10,6},{... | collective-permute-start | bytes 1572872 | tf_op jit(solution)/shard_map/while/body/eval_jaxpr/ppermute | solution.py:24
  49.4 19.6 %copy-start.3 = (f32[32,3,32,128]{3,2,1,0:T(8,128)S(1)}, f32[32,3,32,128]{3,2,1,0:T(8,128)}, u32[]{:S(2)}) copy-start(f32[32,3,32,128]{3,2,1,0:T(8,128)} %get-tuple-element.129) | copy-start | bytes 4718596 | tf_op jit(solution)/shard_map/while
  49.4 19.6 %copy-start.4 = (f32[32,3,31,128]{3,2,1,0:T(8,128)S(1)}, f32[32,3,31,128]{3,2,1,0:T(8,128)}, u32[]{:S(2)}) copy-start(f32[32,3,31,128]{3,2,1,0:T(8,128)} %get-tuple-element.120) | copy-start | bytes 4571140 | tf_op jit(solution)/shard_map/while
  49.4 19.6 %copy-start.5 = (f32[32,3,31,128]{3,2,1,0:T(8,128)S(1)}, f32[32,3,31,128]{3,2,1,0:T(8,128)}, u32[]{:S(2)}) copy-start(f32[32,3,31,128]{3,2,1,0:T(8,128)} %get-tuple-element.117) | copy-start | bytes 4571140 | tf_op jit(solution)/shard_map/while
  72.9 16.9 %collective-permute-start = (f32[32,1,32,128]{3,2,1,0:T(8,128)}, f32[32,1,32,128]{3,2,1,0:T(8,128)S(1)}, u32[]{:S(2)}, u32[]{:S(2)}) collective-permute-start(f32[32,1,32,128]{3,2,1,0:T(8,128)} %get-tuple-element.115), channel_id=1, source_target_pairs={{0,4},{4,8},{8,12},{12,0},{1,5},{5,9},{9,13},{13,1},{2,6},{6,10},{... | collective-permute-start | bytes 1572872 | tf_op jit(solution)/shard_map/while/body/eval_jaxpr/ppermute | solution.py:21
  73.2 24.5 %collective-permute-start.1 = (f32[32,1,32,128]{3,2,1,0:T(8,128)}, f32[32,1,32,128]{3,2,1,0:T(8,128)S(1)}, u32[]{:S(2)}, u32[]{:S(2)}) collective-permute-start(f32[32,1,32,128]{3,2,1,0:T(8,128)} %get-tuple-element.116), channel_id=1, source_target_pairs={{4,0},{8,4},{12,8},{0,12},{5,1},{9,5},{13,9},{1,13},{6,2},{10,6},{... | collective-permute-start | bytes 1572872 | tf_op jit(solution)/shard_map/while/body/eval_jaxpr/ppermute | solution.py:24
  78.9 18.8 %copy-start.3 = (f32[32,3,32,128]{3,2,1,0:T(8,128)S(1)}, f32[32,3,32,128]{3,2,1,0:T(8,128)}, u32[]{:S(2)}) copy-start(f32[32,3,32,128]{3,2,1,0:T(8,128)} %get-tuple-element.129) | copy-start | bytes 4718596 | tf_op jit(solution)/shard_map/while
  78.9 18.8 %copy-start.4 = (f32[32,3,31,128]{3,2,1,0:T(8,128)S(1)}, f32[32,3,31,128]{3,2,1,0:T(8,128)}, u32[]{:S(2)}) copy-start(f32[32,3,31,128]{3,2,1,0:T(8,128)} %get-tuple-element.120) | copy-start | bytes 4571140 | tf_op jit(solution)/shard_map/while
  78.9 18.7 %copy-start.5 = (f32[32,3,31,128]{3,2,1,0:T(8,128)S(1)}, f32[32,3,31,128]{3,2,1,0:T(8,128)}, u32[]{:S(2)}) copy-start(f32[32,3,31,128]{3,2,1,0:T(8,128)} %get-tuple-element.117) | copy-start | bytes 4571140 | tf_op jit(solution)/shard_map/while
  101.6 16.9 %collective-permute-start = (f32[32,1,32,128]{3,2,1,0:T(8,128)}, f32[32,1,32,128]{3,2,1,0:T(8,128)S(1)}, u32[]{:S(2)}, u32[]{:S(2)}) collective-permute-start(f32[32,1,32,128]{3,2,1,0:T(8,128)} %get-tuple-element.115), channel_id=1, source_target_pairs={{0,4},{4,8},{8,12},{12,0},{1,5},{5,9},{9,13},{13,1},{2,6},{6,10},{... | collective-permute-start | bytes 1572872 | tf_op jit(solution)/shard_map/while/body/eval_jaxpr/ppermute | solution.py:21
  101.6 24.8 %collective-permute-start.1 = (f32[32,1,32,128]{3,2,1,0:T(8,128)}, f32[32,1,32,128]{3,2,1,0:T(8,128)S(1)}, u32[]{:S(2)}, u32[]{:S(2)}) collective-permute-start(f32[32,1,32,128]{3,2,1,0:T(8,128)} %get-tuple-element.116), channel_id=1, source_target_pairs={{4,0},{8,4},{12,8},{0,12},{5,1},{9,5},{13,9},{1,13},{6,2},{10,6},{... | collective-permute-start | bytes 1572872 | tf_op jit(solution)/shard_map/while/body/eval_jaxpr/ppermute | solution.py:24
  107.6 18.8 %copy-start.3 = (f32[32,3,32,128]{3,2,1,0:T(8,128)S(1)}, f32[32,3,32,128]{3,2,1,0:T(8,128)}, u32[]{:S(2)}) copy-start(f32[32,3,32,128]{3,2,1,0:T(8,128)} %get-tuple-element.129) | copy-start | bytes 4718596 | tf_op jit(solution)/shard_map/while
  107.6 18.8 %copy-start.4 = (f32[32,3,31,128]{3,2,1,0:T(8,128)S(1)}, f32[32,3,31,128]{3,2,1,0:T(8,128)}, u32[]{:S(2)}) copy-start(f32[32,3,31,128]{3,2,1,0:T(8,128)} %get-tuple-element.120) | copy-start | bytes 4571140 | tf_op jit(solution)/shard_map/while
  107.6 18.8 %copy-start.5 = (f32[32,3,31,128]{3,2,1,0:T(8,128)S(1)}, f32[32,3,31,128]{3,2,1,0:T(8,128)}, u32[]{:S(2)}) copy-start(f32[32,3,31,128]{3,2,1,0:T(8,128)} %get-tuple-element.117) | copy-start | bytes 4571140 | tf_op jit(solution)/shard_map/while
  130.3 16.9 %collective-permute-start = (f32[32,1,32,128]{3,2,1,0:T(8,128)}, f32[32,1,32,128]{3,2,1,0:T(8,128)S(1)}, u32[]{:S(2)}, u32[]{:S(2)}) collective-permute-start(f32[32,1,32,128]{3,2,1,0:T(8,128)} %get-tuple-element.115), channel_id=1, source_target_pairs={{0,4},{4,8},{8,12},{12,0},{1,5},{5,9},{9,13},{13,1},{2,6},{6,10},{... | collective-permute-start | bytes 1572872 | tf_op jit(solution)/shard_map/while/body/eval_jaxpr/ppermute | solution.py:21
  131.4 25.0 %collective-permute-start.1 = (f32[32,1,32,128]{3,2,1,0:T(8,128)}, f32[32,1,32,128]{3,2,1,0:T(8,128)S(1)}, u32[]{:S(2)}, u32[]{:S(2)}) collective-permute-start(f32[32,1,32,128]{3,2,1,0:T(8,128)} %get-tuple-element.116), channel_id=1, source_target_pairs={{4,0},{8,4},{12,8},{0,12},{5,1},{9,5},{13,9},{1,13},{6,2},{10,6},{... | collective-permute-start | bytes 1572872 | tf_op jit(solution)/shard_map/while/body/eval_jaxpr/ppermute | solution.py:24
  136.3 20.1 %copy-start.3 = (f32[32,3,32,128]{3,2,1,0:T(8,128)S(1)}, f32[32,3,32,128]{3,2,1,0:T(8,128)}, u32[]{:S(2)}) copy-start(f32[32,3,32,128]{3,2,1,0:T(8,128)} %get-tuple-element.129) | copy-start | bytes 4718596 | tf_op jit(solution)/shard_map/while
  136.3 20.1 %copy-start.4 = (f32[32,3,31,128]{3,2,1,0:T(8,128)S(1)}, f32[32,3,31,128]{3,2,1,0:T(8,128)}, u32[]{:S(2)}) copy-start(f32[32,3,31,128]{3,2,1,0:T(8,128)} %get-tuple-element.120) | copy-start | bytes 4571140 | tf_op jit(solution)/shard_map/while
  136.3 20.1 %copy-start.5 = (f32[32,3,31,128]{3,2,1,0:T(8,128)S(1)}, f32[32,3,31,128]{3,2,1,0:T(8,128)}, u32[]{:S(2)}) copy-start(f32[32,3,31,128]{3,2,1,0:T(8,128)} %get-tuple-element.117) | copy-start | bytes 4571140 | tf_op jit(solution)/shard_map/while
  160.3 16.9 %collective-permute-start = (f32[32,1,32,128]{3,2,1,0:T(8,128)}, f32[32,1,32,128]{3,2,1,0:T(8,128)S(1)}, u32[]{:S(2)}, u32[]{:S(2)}) collective-permute-start(f32[32,1,32,128]{3,2,1,0:T(8,128)} %get-tuple-element.115), channel_id=1, source_target_pairs={{0,4},{4,8},{8,12},{12,0},{1,5},{5,9},{9,13},{13,1},{2,6},{6,10},{... | collective-permute-start | bytes 1572872 | tf_op jit(solution)/shard_map/while/body/eval_jaxpr/ppermute | solution.py:21
  160.6 24.6 %collective-permute-start.1 = (f32[32,1,32,128]{3,2,1,0:T(8,128)}, f32[32,1,32,128]{3,2,1,0:T(8,128)S(1)}, u32[]{:S(2)}, u32[]{:S(2)}) collective-permute-start(f32[32,1,32,128]{3,2,1,0:T(8,128)} %get-tuple-element.116), channel_id=1, source_target_pairs={{4,0},{8,4},{12,8},{0,12},{5,1},{9,5},{13,9},{1,13},{6,2},{10,6},{... | collective-permute-start | bytes 1572872 | tf_op jit(solution)/shard_map/while/body/eval_jaxpr/ppermute | solution.py:24
  166.3 18.9 %copy-start.3 = (f32[32,3,32,128]{3,2,1,0:T(8,128)S(1)}, f32[32,3,32,128]{3,2,1,0:T(8,128)}, u32[]{:S(2)}) copy-start(f32[32,3,32,128]{3,2,1,0:T(8,128)} %get-tuple-element.129) | copy-start | bytes 4718596 | tf_op jit(solution)/shard_map/while
  166.3 18.9 %copy-start.4 = (f32[32,3,31,128]{3,2,1,0:T(8,128)S(1)}, f32[32,3,31,128]{3,2,1,0:T(8,128)}, u32[]{:S(2)}) copy-start(f32[32,3,31,128]{3,2,1,0:T(8,128)} %get-tuple-element.120) | copy-start | bytes 4571140 | tf_op jit(solution)/shard_map/while
  166.3 18.9 %copy-start.5 = (f32[32,3,31,128]{3,2,1,0:T(8,128)S(1)}, f32[32,3,31,128]{3,2,1,0:T(8,128)}, u32[]{:S(2)}) copy-start(f32[32,3,31,128]{3,2,1,0:T(8,128)} %get-tuple-element.117) | copy-start | bytes 4571140 | tf_op jit(solution)/shard_map/while
  189.0 16.9 %collective-permute-start = (f32[32,1,32,128]{3,2,1,0:T(8,128)}, f32[32,1,32,128]{3,2,1,0:T(8,128)S(1)}, u32[]{:S(2)}, u32[]{:S(2)}) collective-permute-start(f32[32,1,32,128]{3,2,1,0:T(8,128)} %get-tuple-element.115), channel_id=1, source_target_pairs={{0,4},{4,8},{8,12},{12,0},{1,5},{5,9},{9,13},{13,1},{2,6},{6,10},{... | collective-permute-start | bytes 1572872 | tf_op jit(solution)/shard_map/while/body/eval_jaxpr/ppermute | solution.py:21
  189.8 24.2 %collective-permute-start.1 = (f32[32,1,32,128]{3,2,1,0:T(8,128)}, f32[32,1,32,128]{3,2,1,0:T(8,128)S(1)}, u32[]{:S(2)}, u32[]{:S(2)}) collective-permute-start(f32[32,1,32,128]{3,2,1,0:T(8,128)} %get-tuple-element.116), channel_id=1, source_target_pairs={{4,0},{8,4},{12,8},{0,12},{5,1},{9,5},{13,9},{1,13},{6,2},{10,6},{... | collective-permute-start | bytes 1572872 | tf_op jit(solution)/shard_map/while/body/eval_jaxpr/ppermute | solution.py:24
  195.1 19.0 %copy-start.3 = (f32[32,3,32,128]{3,2,1,0:T(8,128)S(1)}, f32[32,3,32,128]{3,2,1,0:T(8,128)}, u32[]{:S(2)}) copy-start(f32[32,3,32,128]{3,2,1,0:T(8,128)} %get-tuple-element.129) | copy-start | bytes 4718596 | tf_op jit(solution)/shard_map/while
  195.1 18.9 %copy-start.4 = (f32[32,3,31,128]{3,2,1,0:T(8,128)S(1)}, f32[32,3,31,128]{3,2,1,0:T(8,128)}, u32[]{:S(2)}) copy-start(f32[32,3,31,128]{3,2,1,0:T(8,128)} %get-tuple-element.120) | copy-start | bytes 4571140 | tf_op jit(solution)/shard_map/while
  195.1 18.9 %copy-start.5 = (f32[32,3,31,128]{3,2,1,0:T(8,128)S(1)}, f32[32,3,31,128]{3,2,1,0:T(8,128)}, u32[]{:S(2)}) copy-start(f32[32,3,31,128]{3,2,1,0:T(8,128)} %get-tuple-element.117) | copy-start | bytes 4571140 | tf_op jit(solution)/shard_map/while
  217.9 16.9 %collective-permute-start = (f32[32,1,32,128]{3,2,1,0:T(8,128)}, f32[32,1,32,128]{3,2,1,0:T(8,128)S(1)}, u32[]{:S(2)}, u32[]{:S(2)}) collective-permute-start(f32[32,1,32,128]{3,2,1,0:T(8,128)} %get-tuple-element.115), channel_id=1, source_target_pairs={{0,4},{4,8},{8,12},{12,0},{1,5},{5,9},{9,13},{13,1},{2,6},{6,10},{... | collective-permute-start | bytes 1572872 | tf_op jit(solution)/shard_map/while/body/eval_jaxpr/ppermute | solution.py:21
  219.0 25.0 %collective-permute-start.1 = (f32[32,1,32,128]{3,2,1,0:T(8,128)}, f32[32,1,32,128]{3,2,1,0:T(8,128)S(1)}, u32[]{:S(2)}, u32[]{:S(2)}) collective-permute-start(f32[32,1,32,128]{3,2,1,0:T(8,128)} %get-tuple-element.116), channel_id=1, source_target_pairs={{4,0},{8,4},{12,8},{0,12},{5,1},{9,5},{13,9},{1,13},{6,2},{10,6},{... | collective-permute-start | bytes 1572872 | tf_op jit(solution)/shard_map/while/body/eval_jaxpr/ppermute | solution.py:24
  223.9 20.1 %copy-start.3 = (f32[32,3,32,128]{3,2,1,0:T(8,128)S(1)}, f32[32,3,32,128]{3,2,1,0:T(8,128)}, u32[]{:S(2)}) copy-start(f32[32,3,32,128]{3,2,1,0:T(8,128)} %get-tuple-element.129) | copy-start | bytes 4718596 | tf_op jit(solution)/shard_map/while
  223.9 20.1 %copy-start.4 = (f32[32,3,31,128]{3,2,1,0:T(8,128)S(1)}, f32[32,3,31,128]{3,2,1,0:T(8,128)}, u32[]{:S(2)}) copy-start(f32[32,3,31,128]{3,2,1,0:T(8,128)} %get-tuple-element.120) | copy-start | bytes 4571140 | tf_op jit(solution)/shard_map/while
  223.9 20.1 %copy-start.5 = (f32[32,3,31,128]{3,2,1,0:T(8,128)S(1)}, f32[32,3,31,128]{3,2,1,0:T(8,128)}, u32[]{:S(2)}) copy-start(f32[32,3,31,128]{3,2,1,0:T(8,128)} %get-tuple-element.117) | copy-start | bytes 4571140 | tf_op jit(solution)/shard_map/while
  247.9 16.9 %collective-permute-start = (f32[32,1,32,128]{3,2,1,0:T(8,128)}, f32[32,1,32,128]{3,2,1,0:T(8,128)S(1)}, u32[]{:S(2)}, u32[]{:S(2)}) collective-permute-start(f32[32,1,32,128]{3,2,1,0:T(8,128)} %get-tuple-element.115), channel_id=1, source_target_pairs={{0,4},{4,8},{8,12},{12,0},{1,5},{5,9},{9,13},{13,1},{2,6},{6,10},{... | collective-permute-start | bytes 1572872 | tf_op jit(solution)/shard_map/while/body/eval_jaxpr/ppermute | solution.py:21
  248.2 24.5 %collective-permute-start.1 = (f32[32,1,32,128]{3,2,1,0:T(8,128)}, f32[32,1,32,128]{3,2,1,0:T(8,128)S(1)}, u32[]{:S(2)}, u32[]{:S(2)}) collective-permute-start(f32[32,1,32,128]{3,2,1,0:T(8,128)} %get-tuple-element.116), channel_id=1, source_target_pairs={{4,0},{8,4},{12,8},{0,12},{5,1},{9,5},{13,9},{1,13},{6,2},{10,6},{... | collective-permute-start | bytes 1572872 | tf_op jit(solution)/shard_map/while/body/eval_jaxpr/ppermute | solution.py:24
  253.9 18.8 %copy-start.3 = (f32[32,3,32,128]{3,2,1,0:T(8,128)S(1)}, f32[32,3,32,128]{3,2,1,0:T(8,128)}, u32[]{:S(2)}) copy-start(f32[32,3,32,128]{3,2,1,0:T(8,128)} %get-tuple-element.129) | copy-start | bytes 4718596 | tf_op jit(solution)/shard_map/while
  253.9 18.8 %copy-start.4 = (f32[32,3,31,128]{3,2,1,0:T(8,128)S(1)}, f32[32,3,31,128]{3,2,1,0:T(8,128)}, u32[]{:S(2)}) copy-start(f32[32,3,31,128]{3,2,1,0:T(8,128)} %get-tuple-element.120) | copy-start | bytes 4571140 | tf_op jit(solution)/shard_map/while
  253.9 18.8 %copy-start.5 = (f32[32,3,31,128]{3,2,1,0:T(8,128)S(1)}, f32[32,3,31,128]{3,2,1,0:T(8,128)}, u32[]{:S(2)}) copy-start(f32[32,3,31,128]{3,2,1,0:T(8,128)} %get-tuple-element.117) | copy-start | bytes 4571140 | tf_op jit(solution)/shard_map/while
  276.6 16.9 %collective-permute-start = (f32[32,1,32,128]{3,2,1,0:T(8,128)}, f32[32,1,32,128]{3,2,1,0:T(8,128)S(1)}, u32[]{:S(2)}, u32[]{:S(2)}) collective-permute-start(f32[32,1,32,128]{3,2,1,0:T(8,128)} %get-tuple-element.115), channel_id=1, source_target_pairs={{0,4},{4,8},{8,12},{12,0},{1,5},{5,9},{9,13},{13,1},{2,6},{6,10},{... | collective-permute-start | bytes 1572872 | tf_op jit(solution)/shard_map/while/body/eval_jaxpr/ppermute | solution.py:21
  277.4 24.1 %collective-permute-start.1 = (f32[32,1,32,128]{3,2,1,0:T(8,128)}, f32[32,1,32,128]{3,2,1,0:T(8,128)S(1)}, u32[]{:S(2)}, u32[]{:S(2)}) collective-permute-start(f32[32,1,32,128]{3,2,1,0:T(8,128)} %get-tuple-element.116), channel_id=1, source_target_pairs={{4,0},{8,4},{12,8},{0,12},{5,1},{9,5},{13,9},{1,13},{6,2},{10,6},{... | collective-permute-start | bytes 1572872 | tf_op jit(solution)/shard_map/while/body/eval_jaxpr/ppermute | solution.py:24
  282.6 18.9 %copy-start.3 = (f32[32,3,32,128]{3,2,1,0:T(8,128)S(1)}, f32[32,3,32,128]{3,2,1,0:T(8,128)}, u32[]{:S(2)}) copy-start(f32[32,3,32,128]{3,2,1,0:T(8,128)} %get-tuple-element.129) | copy-start | bytes 4718596 | tf_op jit(solution)/shard_map/while
  282.6 18.9 %copy-start.4 = (f32[32,3,31,128]{3,2,1,0:T(8,128)S(1)}, f32[32,3,31,128]{3,2,1,0:T(8,128)}, u32[]{:S(2)}) copy-start(f32[32,3,31,128]{3,2,1,0:T(8,128)} %get-tuple-element.120) | copy-start | bytes 4571140 | tf_op jit(solution)/shard_map/while
  282.6 18.9 %copy-start.5 = (f32[32,3,31,128]{3,2,1,0:T(8,128)S(1)}, f32[32,3,31,128]{3,2,1,0:T(8,128)}, u32[]{:S(2)}) copy-start(f32[32,3,31,128]{3,2,1,0:T(8,128)} %get-tuple-element.117) | copy-start | bytes 4571140 | tf_op jit(solution)/shard_map/while
  305.4 16.9 %collective-permute-start = (f32[32,1,32,128]{3,2,1,0:T(8,128)}, f32[32,1,32,128]{3,2,1,0:T(8,128)S(1)}, u32[]{:S(2)}, u32[]{:S(2)}) collective-permute-start(f32[32,1,32,128]{3,2,1,0:T(8,128)} %get-tuple-element.115), channel_id=1, source_target_pairs={{0,4},{4,8},{8,12},{12,0},{1,5},{5,9},{9,13},{13,1},{2,6},{6,10},{... | collective-permute-start | bytes 1572872 | tf_op jit(solution)/shard_map/while/body/eval_jaxpr/ppermute | solution.py:21
  306.4 25.0 %collective-permute-start.1 = (f32[32,1,32,128]{3,2,1,0:T(8,128)}, f32[32,1,32,128]{3,2,1,0:T(8,128)S(1)}, u32[]{:S(2)}, u32[]{:S(2)}) collective-permute-start(f32[32,1,32,128]{3,2,1,0:T(8,128)} %get-tuple-element.116), channel_id=1, source_target_pairs={{4,0},{8,4},{12,8},{0,12},{5,1},{9,5},{13,9},{1,13},{6,2},{10,6},{... | collective-permute-start | bytes 1572872 | tf_op jit(solution)/shard_map/while/body/eval_jaxpr/ppermute | solution.py:24
  311.4 20.1 %copy-start.3 = (f32[32,3,32,128]{3,2,1,0:T(8,128)S(1)}, f32[32,3,32,128]{3,2,1,0:T(8,128)}, u32[]{:S(2)}) copy-start(f32[32,3,32,128]{3,2,1,0:T(8,128)} %get-tuple-element.129) | copy-start | bytes 4718596 | tf_op jit(solution)/shard_map/while
  311.4 20.1 %copy-start.4 = (f32[32,3,31,128]{3,2,1,0:T(8,128)S(1)}, f32[32,3,31,128]{3,2,1,0:T(8,128)}, u32[]{:S(2)}) copy-start(f32[32,3,31,128]{3,2,1,0:T(8,128)} %get-tuple-element.120) | copy-start | bytes 4571140 | tf_op jit(solution)/shard_map/while
  311.4 20.1 %copy-start.5 = (f32[32,3,31,128]{3,2,1,0:T(8,128)S(1)}, f32[32,3,31,128]{3,2,1,0:T(8,128)}, u32[]{:S(2)}) copy-start(f32[32,3,31,128]{3,2,1,0:T(8,128)} %get-tuple-element.117) | copy-start | bytes 4571140 | tf_op jit(solution)/shard_map/while
  335.4 16.9 %collective-permute-start = (f32[32,1,32,128]{3,2,1,0:T(8,128)}, f32[32,1,32,128]{3,2,1,0:T(8,128)S(1)}, u32[]{:S(2)}, u32[]{:S(2)}) collective-permute-start(f32[32,1,32,128]{3,2,1,0:T(8,128)} %get-tuple-element.115), channel_id=1, source_target_pairs={{0,4},{4,8},{8,12},{12,0},{1,5},{5,9},{9,13},{13,1},{2,6},{6,10},{... | collective-permute-start | bytes 1572872 | tf_op jit(solution)/shard_map/while/body/eval_jaxpr/ppermute | solution.py:21
  335.6 24.6 %collective-permute-start.1 = (f32[32,1,32,128]{3,2,1,0:T(8,128)}, f32[32,1,32,128]{3,2,1,0:T(8,128)S(1)}, u32[]{:S(2)}, u32[]{:S(2)}) collective-permute-start(f32[32,1,32,128]{3,2,1,0:T(8,128)} %get-tuple-element.116), channel_id=1, source_target_pairs={{4,0},{8,4},{12,8},{0,12},{5,1},{9,5},{13,9},{1,13},{6,2},{10,6},{... | collective-permute-start | bytes 1572872 | tf_op jit(solution)/shard_map/while/body/eval_jaxpr/ppermute | solution.py:24
  341.4 18.8 %copy-start.3 = (f32[32,3,32,128]{3,2,1,0:T(8,128)S(1)}, f32[32,3,32,128]{3,2,1,0:T(8,128)}, u32[]{:S(2)}) copy-start(f32[32,3,32,128]{3,2,1,0:T(8,128)} %get-tuple-element.129) | copy-start | bytes 4718596 | tf_op jit(solution)/shard_map/while
  341.4 18.8 %copy-start.4 = (f32[32,3,31,128]{3,2,1,0:T(8,128)S(1)}, f32[32,3,31,128]{3,2,1,0:T(8,128)}, u32[]{:S(2)}) copy-start(f32[32,3,31,128]{3,2,1,0:T(8,128)} %get-tuple-element.120) | copy-start | bytes 4571140 | tf_op jit(solution)/shard_map/while
  341.4 18.8 %copy-start.5 = (f32[32,3,31,128]{3,2,1,0:T(8,128)S(1)}, f32[32,3,31,128]{3,2,1,0:T(8,128)}, u32[]{:S(2)}) copy-start(f32[32,3,31,128]{3,2,1,0:T(8,128)} %get-tuple-element.117) | copy-start | bytes 4571140 | tf_op jit(solution)/shard_map/while
  442.2 16.8 %collective-permute-start.4 = (f32[32,48,8]{0,2,1:T(8,128)}, f32[32,48,8]{0,2,1:T(8,128)S(1)}, u32[]{:S(2)}, u32[]{:S(2)}) collective-permute-start(f32[32,48,8]{0,2,1:T(8,128)} %get-tuple-element.80), channel_id=1, source_target_pairs={{0,12},{4,0},{8,4},{12,8},{1,13},{5,1},{9,5},{13,9},{2,14},{6,2},{... | collective-permute-start | bytes 147464 | tf_op jit(solution)/shard_map/ppermute | solution.py:31
  444.3 14.8 %collective-permute-start.5 = (f32[32,48,8]{0,2,1:T(8,128)}, f32[32,48,8]{0,2,1:T(8,128)S(1)}, u32[]{:S(2)}, u32[]{:S(2)}) collective-permute-start(f32[32,48,8]{0,2,1:T(8,128)} %get-tuple-element.81), channel_id=1, source_target_pairs={{0,4},{4,8},{8,12},{12,0},{1,5},{5,9},{9,13},{13,1},{2,6},{6,10},{... | collective-permute-start | bytes 147464 | tf_op jit(solution)/shard_map/ppermute | solution.py:31
  454.7 4.4 copy-start.7
  466.5 24.3 %all-to-all-start.1 = ((f32[32,4,3168]{2,0,1:T(8,128)}), f32[32,4,3168]{2,0,1:T(8,128)S(1)}, u32[]{:S(2)}, u32[]{:S(2)}) async-start(f32[32,4,3168]{2,0,1:T(8,128)} %copy.28), calls=%async_computation.1 | async-start | bytes 3276800 | tf_op jit(solution)/shard_map/all_to_all | solution.py:80
  470.0 132.6 %all-reduce.6.cloned.1.call-start = ((), (), s32[]{:S(2)}) async-start(), calls=%async_computation.2 | async-start | bytes 131072 | tf_op jit(solution)/shard_map/psum | solution.py:83
  (4 other events, 13.6 us)
Sparse Core Ops, SparseCore 0:
  517.6 85.0 all-reduce.5
where the time goes:
time: 613 us; the launch traced here: 611 us
  waiting for transfers between devices  319 us (52%)
  local copies, waits for them, and re-layouts  160 us (26%)
  starting transfers between devices  52.9 us (9%)
  other arithmetic  31.9 us (5%)
  blocking collectives  24.3 us (4%)
  between operations  14.2 us (2%)
  matrix products  7.95 us (1%)
    ppermute x12, waiting for transfers between devices, with_halo(): lax.ppermute(lax.slice_in_dim(block, block.shape[dim] - width, None, axis...  124 us
    ppermute x12, waiting for transfers between devices, with_halo(): lax.ppermute(lax.slice_in_dim(block, 0, width, axis=dim), axis, backward)  98.1 us
    psum x1, waiting for transfers between devices, on_device(): total_gram = lax.psum(whole_gram, ('dom', 'band', 'sub'))  85.2 us
    gather x2, local copies, waits for them, and re-layouts, on_device(): picked = jnp.where(live_mask[None], flat_panel[:, safe_offsets], 0.0)  69.9 us
    ppermute x12, starting transfers between devices, with_halo(): lax.ppermute(lax.slice_in_dim(block, 0, width, axis=dim), axis, backward)  39.5 us
    slice x24, local copies, waits for them, and re-layouts, operator(): jnp.roll(centre_part, -1, axis=2)  26.5 us
    all_to_all x1, blocking collectives, on_device(): lax.all_to_all(left_rows, ('band', 'sub'), split_axis=1, concat_axis=0, t...  24.3 us
    sub x11, other arithmetic, one_step(): return (current, 2.0 * apply_once(current, potential) - before)  17.1 us
  transfers between devices with their start and end apart: 28, of which 26 were waited for; matrix products, arithmetic and copies ran while one was open for 9% of the time, Pallas kernels for 0%

commit v1 on v0

v1 whole, which is shorter than its diff:
```python
import functools
import math

import jax
import jax.numpy as jnp
from jax import lax
from jax.experimental import pallas as pl
from jax.experimental.pallas import tpu as pltpu
from jax.sharding import PartitionSpec as P

DEGREE = 12

CENTER_LEVEL = 3.6
HALF_WIDTH = 3.4
SHIFT = 3.0

MAX_CHUNKS = 2
MIB = 1024 * 1024

VMEM = pl.BlockSpec(memory_space=pltpu.VMEM)
SMEM = pl.BlockSpec(memory_space=pltpu.SMEM)
NT = (((1,), (1,)), ((), ()))
TN = (((0,), (0,)), ((), ()))


def params(mib):
    return pltpu.CompilerParams(vmem_limit_bytes=mib * MIB)


def split_bf16(x):
    high = x.astype(jnp.bfloat16)
    return high, (x - high.astype(jnp.float32)).astype(jnp.bfloat16)


def swap_over(x, axes, size, by):
    return lax.ppermute(x, axes, [(i, i ^ by) for i in range(size)])


def filter_kernel(n_dom, me_ref, *refs):
    potentials = refs[:n_dom]
    ins = refs[n_dom : 2 * n_dom]
    outs = refs[2 * n_dom : 3 * n_dom]
    even, odd, diagonal = refs[3 * n_dom :]
    me = me_ref[0]
    planes = ins[0].shape[1]
    total = n_dom * planes
    step_scale = 1.0 / HALF_WIDTH
    for m in range(n_dom):
        first = (me ^ m) * planes
        for i in range(planes):
            even[first + i] = ins[m][:, i]
            diagonal[first + i] = (potentials[m][i] + (SHIFT - CENTER_LEVEL)) * (2.0 * step_scale)
    rows, lanes = even.shape[2], even.shape[3]
    lane = lax.broadcasted_iota(jnp.int32, (1, rows, lanes), 2)
    scale_low = jnp.where(lane == 0, 0.0, step_scale)
    scale_high = jnp.where(lane == lanes - 1, 0.0, step_scale)

    def twice_operator(source, x):
        below = jnp.where(x == 0, total - 1, x - 1)
        above = jnp.where(x == total - 1, 0, x + 1)
        centre = source[x]
        near = source[below] + source[above]
        near += pltpu.roll(centre, 1, 1) + pltpu.roll(centre, rows - 1, 1)
        result = diagonal[x][None] * centre - step_scale * near
        result -= scale_low * pltpu.roll(centre, 1, 2)
        return result - scale_high * pltpu.roll(centre, lanes - 1, 2)

    def first_plane(x, _):
        odd[x] = 0.5 * twice_operator(even, x)
        return 0

    def next_plane(source, target, x, _):
        target[x] = twice_operator(source, x) - target[x]
        return 0

    onto_even = functools.partial(next_plane, odd, even)
    onto_odd = functools.partial(next_plane, even, odd)
    lax.fori_loop(0, total, first_plane, 0)
    lax.fori_loop(0, total, onto_even, 0)

    def two_steps(_, carry):
        lax.fori_loop(0, total, onto_odd, 0)
        lax.fori_loop(0, total, onto_even, 0)
        return carry

    lax.fori_loop(0, DEGREE // 2 - 1, two_steps, 0)
    for m in range(n_dom):
        first = (me ^ m) * planes
        for i in range(planes):
            outs[m][:, i] = even[first + i]


def filter_orbitals(me, potentials, blocks):
    n_dom = len(blocks)
    orbitals, planes, rows, lanes = blocks[0].shape
    field = pltpu.VMEM((n_dom * planes, orbitals, rows, lanes), jnp.float32)
    cells = n_dom * blocks[0].size
    return pl.pallas_call(
        functools.partial(filter_kernel, n_dom),
        out_shape=[jax.ShapeDtypeStruct(blocks[0].shape, jnp.float32)] * n_dom,
        in_specs=[SMEM] + [VMEM] * (2 * n_dom),
        out_specs=[VMEM] * n_dom,
        scratch_shapes=[field, field, pltpu.VMEM((n_dom * planes, rows, lanes), jnp.float32)],
        compiler_params=params(16),
        cost_estimate=pl.CostEstimate(
            flops=12 * DEGREE * cells, bytes_accessed=8 * cells, transcendentals=0
        ),
        name="chebyshev",
    )(me, *potentials, *blocks)


def assemble_kernel(me_ref, *refs):
    *pieces, out = refs
    per = pieces[0].shape[0]
    for m, piece in enumerate(pieces):
        out[pl.ds((me_ref[0] ^ m) * per, per)] = piece[...]


def assemble(me, pieces):
    per = pieces[0].shape[0]
    return pl.pallas_call(
        assemble_kernel,
        out_shape=jax.ShapeDtypeStruct((per * len(pieces),) + pieces[0].shape[1:], jnp.float32),
        in_specs=[SMEM] + [VMEM] * len(pieces),
        out_specs=VMEM,
        compiler_params=params(8),
        name="assemble",
    )(me, *pieces)


def regroup_kernel(cells, group_ref, *refs):
    *pieces, high_out, low_out = refs
    orbitals = pieces[0].shape[0] // cells
    pairs = cells // 2

    for j, piece in enumerate(pieces):
        target = group_ref[0] ^ j

        def one_row(row, _, piece=piece, target=target):
            for half in range(2):
                picked = piece[pl.ds(row + half * pairs, orbitals, stride=cells), :]
                high, low = split_bf16(picked)
                lanes = picked.shape[1]
                high_out[target, row, :, half * lanes : (half + 1) * lanes] = high
                low_out[target, row, :, half * lanes : (half + 1) * lanes] = low
            return 0

        lax.fori_loop(0, pairs, one_row, 0, unroll=4)


def regroup(group, pieces):
    orbitals = pieces[0].shape[0]
    lanes = pieces[0].shape[3]
    cells = pieces[0].size // (orbitals * lanes)
    shape = jax.ShapeDtypeStruct((len(pieces), cells // 2, orbitals, 2 * lanes), jnp.bfloat16)
    return pl.pallas_call(
        functools.partial(regroup_kernel, cells),
        out_shape=[shape, shape],
        in_specs=[SMEM] + [VMEM] * len(pieces),
        out_specs=[VMEM, VMEM],
        compiler_params=params(16),
        name="regroup",
    )(group, *[piece.reshape(orbitals * cells, lanes) for piece in pieces])


def projector_kernel(groups, group_ref, offsets_ref, coefs_ref, high_out, low_out):
    pairs = high_out.shape[0]
    per_group = offsets_ref.shape[0] // groups
    channels, spread = coefs_ref.shape[2], coefs_ref.shape[3]
    step = pl.program_id(0)
    shell = step // (per_group // 2)
    first_atom = group_ref[0] * per_group + 2 * (step % (per_group // 2))
    lanes = high_out.shape[2] // 2
    row_index = lax.broadcasted_iota(jnp.int32, (2 * pairs, channels, spread), 0)
    lane_index = lax.broadcasted_iota(jnp.int32, (lanes, spread), 0)
    dense = []
    for i in range(2):
        offsets = offsets_ref[first_atom + i, pl.ds(shell, 1), :]
        coefs = coefs_ref[first_atom + i, shell]
        at_row = row_index == (offsets // lanes)[None]
        at_row &= (offsets >= 0)[None]
        high, low = split_bf16(coefs)
        left = [
            jnp.where(at_row, part.astype(jnp.float32)[None], 0.0)
            .reshape(2 * pairs * channels, spread)
            .astype(jnp.bfloat16)
            for part in (high, low)
        ]
        at_lane = jnp.where(lane_index == (offsets & (lanes - 1)), 1.0, 0.0).astype(jnp.bfloat16)
        values = lax.dot_general(
            jnp.concatenate(left, axis=1),
            jnp.concatenate([at_lane, at_lane], axis=1),
            NT,
            preferred_element_type=jnp.float32,
        )
        dense.append(values.reshape(2 * pairs, channels, lanes))
    both = jnp.concatenate(dense, axis=1)
    high, low = split_bf16(both)
    for half in range(2):
        high_out[:, :, half * lanes : (half + 1) * lanes] = high[half * pairs : (half + 1) * pairs]
        low_out[:, :, half * lanes : (half + 1) * lanes] = low[half * pairs : (half + 1) * pairs]


def build_projectors(groups, group, offsets, coefs, cells, lanes):
    atoms, shells, channels, spread = coefs.shape
    per_group = atoms // groups
    rows = per_group * shells * channels
    shape = jax.ShapeDtypeStruct((cells // 2, rows, 2 * lanes), jnp.bfloat16)
    spec = pl.BlockSpec((cells // 2, 2 * channels, 2 * lanes), lambda i: (0, i, 0))
    return pl.pallas_call(
        functools.partial(projector_kernel, groups),
        grid=(shells * per_group // 2,),
        out_shape=[shape, shape],
        in_specs=[SMEM, VMEM, VMEM],
        out_specs=[spec, spec],
        compiler_params=params(16),
        cost_estimate=pl.CostEstimate(
            flops=4 * rows * cells * lanes * spread,
            bytes_accessed=8 * rows * cells * lanes,
            transcendentals=0,
        ),
        name="projectors",
    )(group, offsets, coefs)


def product_kernel(n_chunks, *refs):
    w_high, w_low = refs[:2]
    f_high, f_low = refs[2 : 2 + n_chunks], refs[2 + n_chunks : 2 + 2 * n_chunks]
    grid_out, proj_out = refs[2 + 2 * n_chunks :]
    orbitals = grid_out.shape[0]
    groups = f_high[0].shape[0]

    @pl.when(pl.program_id(0) == 0)
    def _():
        grid_out[...] = jnp.zeros_like(grid_out)
        proj_out[...] = jnp.zeros_like(proj_out)

    total = 0.0
    for h in range(w_high.shape[0]):
        fields = [
            jnp.concatenate([part[g, h] for g in range(groups) for part in parts], axis=0)
            for parts in (f_high, f_low)
        ]
        right = jnp.concatenate(fields, axis=0)
        left_high = jnp.concatenate([fields[0], w_high[h]], axis=0)
        left_low = jnp.concatenate([fields[1], w_low[h]], axis=0)
        wide = lax.dot_general(left_high, right, NT, preferred_element_type=jnp.float32)
        low = lax.dot_general(left_low, fields[0], NT, preferred_element_type=jnp.float32)
        total += wide[:, :orbitals] + wide[:, orbitals:] + low
    grid_out[...] += total[:orbitals]
    proj_out[...] += total[orbitals:]


def products(projectors, highs, lows):
    pairs, rows, depth = projectors[0].shape
    groups, _, per, _ = highs[0].shape
    n_chunks = len(highs)
    orbitals = groups * per * n_chunks
    block = 6
    w_spec = pl.BlockSpec((block, rows, depth), lambda i: (i, 0, 0))
    f_spec = pl.BlockSpec((groups, block, per, depth), lambda i: (0, i, 0, 0))
    whole = lambda i: (0, 0)
    return pl.pallas_call(
        functools.partial(product_kernel, n_chunks),
        grid=(pairs // block,),
        out_shape=[
            jax.ShapeDtypeStruct((orbitals, orbitals), jnp.float32),
            jax.ShapeDtypeStruct((rows, orbitals), jnp.float32),
        ],
        in_specs=[w_spec] * 2 + [f_spec] * (2 * n_chunks),
        out_specs=[
            pl.BlockSpec((orbitals, orbitals), whole),
            pl.BlockSpec((rows, orbitals), whole),
        ],
        compiler_params=params(24),
        name="products",
    )(*projectors, *highs, *lows)


def gram_kernel(
    scale_point, scale_atom, proj_ref, right_ref, left_ref, corr_ref, grid_ref, out
):
    rows = right_ref.shape[0]
    projections = proj_ref[rows : 2 * rows, :] + right_ref[...] + left_ref[...]
    highest = lax.Precision.HIGHEST
    weighted = jnp.dot(
        corr_ref[...], projections, precision=highest, preferred_element_type=jnp.float32
    )
    atom_part = lax.dot_general(
        projections, weighted, TN, precision=highest, preferred_element_type=jnp.float32
    )
    out[...] = grid_ref[...] * scale_point + atom_part * scale_atom


def whole_columns(panel, potential, me):
    n_dom = lax.axis_size("dom")
    orbitals = panel.shape[0]
    n_chunks = math.gcd(MAX_CHUNKS, orbitals // n_dom)
    per_chunk = orbitals // n_chunks
    per_block = per_chunk // n_dom
    potentials = [potential] + [swap_over(potential, "dom", n_dom, m) for m in range(1, n_dom)]
    arrived = []
    for c in range(n_chunks):
        blocks = []
        for m in range(n_dom):
            first = c * per_chunk + (me ^ m) * per_block
            block = lax.dynamic_slice_in_dim(panel, first, per_block, 0)
            blocks.append(swap_over(block, "dom", n_dom, m) if m else block)
        arrived.append(blocks)
    for blocks in arrived:
        done = filter_orbitals(me.reshape(1), potentials, blocks)
        yield assemble(
            me.reshape(1), [swap_over(b, "dom", n_dom, m) if m else b for m, b in enumerate(done)]
        )


def plane_by_plane(panel, potential):
    n_dom = lax.axis_size("dom")
    diagonal = (potential + (SHIFT - CENTER_LEVEL)) * (2.0 / HALF_WIDTH)

    def twice_operator(field):
        low = lax.ppermute(field[:, -1:], "dom", [(i, (i + 1) % n_dom) for i in range(n_dom)])
        high = lax.ppermute(field[:, :1], "dom", [(i, (i - 1) % n_dom) for i in range(n_dom)])
        extended = jnp.concatenate([low, field, high], axis=1)
        near = extended[:, 2:] + extended[:, :-2]
        near += jnp.roll(field, 1, axis=2) + jnp.roll(field, -1, axis=2)
        padded = jnp.pad(field, ((0, 0), (0, 0), (0, 0), (1, 1)))
        near += padded[..., 2:] + padded[..., :-2]
        return diagonal * field - near / HALF_WIDTH

    def one_step(_, carry):
        before, current = carry
        return current, twice_operator(current) - before

    start = (panel, 0.5 * twice_operator(panel))
    return lax.fori_loop(0, DEGREE - 1, one_step, start)[1]


def on_device(panel, potential, point_offsets, point_coefs, correlation):
    orbitals, planes, rows, lanes = panel.shape
    n_dom, n_band, n_sub = (lax.axis_size(axis) for axis in ("dom", "band", "sub"))
    groups = n_band * n_sub
    me = lax.axis_index("dom")
    group = lax.axis_index(("band", "sub"))
    group_ref = group.reshape(1)

    cells = planes * rows
    projectors = build_projectors(groups, group_ref, point_offsets, point_coefs, cells, lanes)
    channels = correlation.shape[1]
    own_atoms = point_offsets.shape[0] // groups
    own_corr = lax.dynamic_slice_in_dim(correlation, group * own_atoms, own_atoms, 0)
    same_atom = jnp.eye(own_atoms, dtype=jnp.float32)
    corr_matrix = (same_atom[:, None, :, None] * own_corr[:, :, None, :]).reshape(
        own_atoms * channels, own_atoms * channels
    )

    if orbitals % n_dom == 0:
        chunks = whole_columns(panel, potential, me)
    else:
        chunks = [plane_by_plane(panel, potential)]
    filtered, highs, lows = [], [], []
    for own in chunks:
        filtered.append(own)
        pieces = []
        for m in range(n_band):
            over_band = swap_over(own, "band", n_band, m) if m else own
            pieces += [over_band] + [swap_over(over_band, "sub", n_sub, k) for k in range(1, n_sub)]
        high, low = regroup(group_ref, pieces)
        highs.append(high)
        lows.append(low)

    grid_part, proj = products(projectors, highs, lows)
    rows_atom = own_atoms * channels
    from_right = lax.ppermute(
        proj[:rows_atom], "dom", [(i, (i - 1) % n_dom) for i in range(n_dom)]
    )
    from_left = lax.ppermute(
        proj[2 * rows_atom :], "dom", [(i, (i + 1) % n_dom) for i in range(n_dom)]
    )
    scale_point = 1.0 / (cells * lanes * n_dom * groups)
    scale_atom = 1.0 / math.sqrt(point_offsets.shape[0] * n_dom)
    share = pl.pallas_call(
        functools.partial(gram_kernel, scale_point, scale_atom),
        out_shape=jax.ShapeDtypeStruct(grid_part.shape, jnp.float32),
        in_specs=[VMEM] * 5,
        out_specs=VMEM,
        compiler_params=params(8),
        name="gram_share",
    )(proj, from_right, from_left, corr_matrix, grid_part)

    gram_rows = 0.0
    for m in range(groups):
        part = lax.dynamic_slice_in_dim(share, (group ^ m) * orbitals, orbitals, 0)
        gram_rows += swap_over(part, ("band", "sub"), groups, m) if m else part
    if n_dom <= 8:
        gram_rows = sum(
            [gram_rows] + [swap_over(gram_rows, "dom", n_dom, m) for m in range(1, n_dom)]
        )
    else:
        gram_rows = lax.psum(gram_rows, "dom")
    return (jnp.concatenate(filtered, axis=0), gram_rows)


def solution(mesh):
    placed = (
        P(("slab", "band", "sub"), "dom", None, None),
        P(("slab", "dom"), None, None),
        P(("slab", "dom"), None, None),
        P(("slab", "dom"), None, None, None),
        P(("slab", "dom"), None, None),
    )
    return jax.shard_map(
        on_device,
        mesh=mesh,
        in_specs=placed,
        out_specs=(P(("slab", "band", "sub"), "dom", None, None), P(("slab", "band", "sub"), None)),
        check_vma=False,
    )
```

time: 613 us -> 149 us (0.24)
  waiting for transfers between devices: 319 us -> 45.8 us
  local copies, waits for them, and re-layouts: 160 us -> 3.26 us
  Pallas kernels: 0 us -> 53.5 us
  other arithmetic: 31.9 us -> 2.01 us
  blocking collectives: 24.3 us -> 0 us
  between operations: 14.2 us -> 0.91 us
  starting transfers between devices: 52.9 us -> 43.1 us
  matrix products: 7.95 us -> 0 us
    ppermute x26 -> x29, waiting for transfers between devices: 222 us -> 45.8 us  [the longest x27 40.4 us: swap_over(): return lax.ppermute(x, axes, [(i, i ^ by) for i in range(size)])]
    psum x1 -> x0, waiting for transfers between devices: 85.2 us -> none  [on_device(): total_gram = lax.psum(whole_gram, ('dom', 'band', 'sub'))]
    gather x2 -> x0, local copies, waits for them, and re-layouts: 69.9 us -> none  [on_device(): picked = jnp.where(live_mask[None], flat_panel[:, safe_offsets], 0.0)]
    pallas_call x0 -> x9, Pallas kernels: none -> 53.5 us  [the longest x2 30 us: filter_orbitals(): pl.pallas_call(functools.partial(filter_kernel, n_dom), out_shape=[jax.Sh...]
    slice x48 -> x1, local copies, waits for them, and re-layouts: 46.4 us -> 0.01 us  [on_device(): proj[2 * rows_atom:]]
    all_to_all x1 -> x0, blocking collectives: 24.3 us -> none  [on_device(): lax.all_to_all(left_rows, ('band', 'sub'), split_axis=1, concat_axis=0, t...]
    while x89 -> x0, local copies, waits for them, and re-layouts: 18 us -> none
    sub x11 -> x0, other arithmetic: 17.1 us -> none  [one_step(): return (current, 2.0 * apply_once(current, potential) - before)]
  transfers between devices with their start and end apart: 28 -> 29, of which waited for: 26 -> 11; matrix products, arithmetic and copies ran while one was open for 9% -> 1% of each run, Pallas kernels for 0% -> 28%
where the time goes in v1:
time: 149 us
  Pallas kernels  53.5 us (36%)
  waiting for transfers between devices  45.8 us (31%)
  starting transfers between devices  43.1 us (29%)
  local copies, waits for them, and re-layouts  3.26 us (2%)
  other arithmetic  2.01 us (1%)
    ppermute x27, starting transfers between devices, swap_over(): return lax.ppermute(x, axes, [(i, i ^ by) for i in range(size)])  40.8 us
    ppermute x27, waiting for transfers between devices, swap_over(): return lax.ppermute(x, axes, [(i, i ^ by) for i in range(size)])  40.4 us
    pallas_call x2, Pallas kernels, filter_orbitals(): pl.pallas_call(functools.partial(filter_kernel, n_dom), out_shape=[jax.Sh...  30 us
    pallas_call x1, Pallas kernels, build_projectors(): pl.pallas_call(functools.partial(projector_kernel, groups), grid=(shells...  8.15 us
    pallas_call x2, Pallas kernels, regroup(): pl.pallas_call(functools.partial(regroup_kernel, cells), out_shape=[shape...  7.45 us
    pallas_call x1, Pallas kernels, products(): pl.pallas_call(functools.partial(product_kernel, n_chunks), grid=(pairs /...  7.32 us
    ppermute x1, waiting for transfers between devices, on_device(): lax.ppermute(proj[2 * rows_atom:], 'dom', [(i, (i + 1) % n_dom) for i in...  3.83 us
  transfers between devices with their start and end apart: 29, of which 11 were waited for; matrix products, arithmetic and copies ran while one was open for 1% of the time, Pallas kernels for 28%

profile of v1, /device:TPU:0, one launch (start us, length us, event | category | flops | bytes accessed | tf_op | source)
XLA Modules:
  0.0 148.6 jit_solution(14052423258381584164)
XLA Ops:
  0.6 0.0 copy-start
  0.7 1.6 %constant_dynamic-slice_fusion.8 = (f32[4,3,32,128]{3,2,1,0:T(8,128)S(1)}, f32[4,3,32,128]{3,2,1,0:T(8,128)S(1)}, f32[4,3,32,128]{3,2,1,0:T(8,128)S(1)}, f32[4,3...) fusion(f32[32,3,32,128]{3,2,1,0:T(8,128)} %param.5, ...), kind=kLoop, calls=%fused_computation.14 | loop fusion | bytes 3145760 | tf_op jit(solution)/shard_map/dynamic_slice | solution.py:307
  2.3 3.1 %collective-permute-start.3 = (f32[4,3,32,128]{3,2,1,0:T(8,128)S(1)}, f32[4,3,32,128]{3,2,1,0:T(8,128)S(1)}, u32[]{:S(2)}, u32[]{:S(2)}) collective-permute-start(f32[4,3,32,128]{3,2,1,0:T(8,128)S(1)} %get-tuple-element.38), channel_id=1, source_target_pairs={{0,4},{4,0},{8,12},{12,8},{1,5},{5,1},{9,13},{13,9},{2,6},{6,2},{1... | collective-permute-start | bytes 589832 | tf_op jit(solution)/shard_map/ppermute | solution.py:36
  5.4 2.6 %collective-permute-start.4 = (f32[4,3,32,128]{3,2,1,0:T(8,128)S(1)}, f32[4,3,32,128]{3,2,1,0:T(8,128)S(1)}, u32[]{:S(2)}, u32[]{:S(2)}) collective-permute-start(f32[4,3,32,128]{3,2,1,0:T(8,128)S(1)} %get-tuple-element.37), channel_id=1, source_target_pairs={{0,8},{4,12},{8,0},{12,4},{1,9},{5,13},{9,1},{13,5},{2,10},{6,14},... | collective-permute-start | bytes 589832 | tf_op jit(solution)/shard_map/ppermute | solution.py:36
  8.0 0.0 collective-permute-start.5
  8.0 0.9 collective-permute-start
  8.9 3.5 %collective-permute-start.1 = (f32[3,32,128]{2,1,0:T(8,128)S(1)}, f32[3,32,128]{2,1,0:T(8,128)S(1)}, u32[]{:S(2)}, u32[]{:S(2)}) collective-permute-start(f32[3,32,128]{2,1,0:T(8,128)S(1)} %copy-done.1), channel_id=1, source_target_pairs={{0,8},{4,12},{8,0},{12,4},{1,9},{5,13},{9,1},{13,5},{2,10},{6,14},... | collective-permute-start | bytes 147464 | tf_op jit(solution)/shard_map/ppermute | solution.py:36
  12.4 7.2 %collective-permute-done.refs_1_ = f32[3,32,128]{2,1,0:T(8,128)S(1)} collective-permute-done((f32[3,32,128]{2,1,0:T(8,128)S(1)}, f32[3,32,128]{2,1,0:T(8,128)S(1)}, u32[]{:S(2)}, u32[]{:S(2)}) %collective-permute-start) | collective-permute-done | bytes 49184 | tf_op jit(solution)/shard_map/ppermute | solution.py:36
  19.6 2.5 %collective-permute-start.2 = (f32[3,32,128]{2,1,0:T(8,128)S(1)}, f32[3,32,128]{2,1,0:T(8,128)S(1)}, u32[]{:S(2)}, u32[]{:S(2)}) collective-permute-start(f32[3,32,128]{2,1,0:T(8,128)S(1)} %copy-done.1), channel_id=1, source_target_pairs={{0,12},{4,8},{8,4},{12,0},{1,13},{5,9},{9,5},{13,1},{2,14},{6,10},... | collective-permute-start | bytes 147464 | tf_op jit(solution)/shard_map/ppermute | solution.py:36
  22.1 6.9 %collective-permute-done.1.refs_2_ = f32[3,32,128]{2,1,0:T(8,128)S(1)} collective-permute-done((f32[3,32,128]{2,1,0:T(8,128)S(1)}, f32[3,32,128]{2,1,0:T(8,128)S(1)}, u32[]{:S(2)}, u32[]{:S(2)}) %collective-permute-start.1) | collective-permute-done | bytes 49184 | tf_op jit(solution)/shard_map/ppermute | solution.py:36
  29.1 0.0 collective-permute-start.10
  29.1 2.5 %collective-permute-start.11 = (f32[4,3,32,128]{3,2,1,0:T(8,128)S(1)}, f32[4,3,32,128]{3,2,1,0:T(8,128)S(1)}, u32[]{:S(2)}, u32[]{:S(2)}) collective-permute-start(f32[4,3,32,128]{3,2,1,0:T(8,128)S(1)} %get-tuple-element.40), channel_id=1, source_target_pairs={{0,12},{4,8},{8,4},{12,0},{1,13},{5,9},{9,5},{13,1},{2,14},{6,10},... | collective-permute-start | bytes 589832 | tf_op jit(solution)/shard_map/ppermute | solution.py:36
  31.5 0.0 collective-permute-done.3.refs_5_
  31.5 6.9 %collective-permute-start.9 = (f32[4,3,32,128]{3,2,1,0:T(8,128)S(1)}, f32[4,3,32,128]{3,2,1,0:T(8,128)S(1)}, u32[]{:S(2)}, u32[]{:S(2)}) collective-permute-start(f32[4,3,32,128]{3,2,1,0:T(8,128)S(1)} %get-tuple-element.35), channel_id=1, source_target_pairs={{0,4},{4,0},{8,12},{12,8},{1,5},{5,1},{9,13},{13,9},{2,6},{6,2},{1... | collective-permute-start | bytes 589832 | tf_op jit(solution)/shard_map/ppermute | solution.py:36
  38.4 15.0 %chebyshev.2 = (f32[4,3,32,128]{3,2,1,0:T(8,128)S(1)}, f32[4,3,32,128]{3,2,1,0:T(8,128)S(1)}, f32[4,3,32,128]{3,2,1,0:T(8,128)S(1)}, f32[4,3,32,128]{3,2,1,0:T(8,128)S(1)}) custom-call(s32[1]{0:T(128)} %bitcast.me_ref, f32[3,32,128]{2,1,0:T(8,128)S(1)} %copy-done.1, f32[3,32,128]{2,1,0:T(8,128)S(1)} %collective-permute-done.refs_1_, ...), custom_call_target="tpu_custom_call" | custom-call | flops 28311552 | bytes 1572864 | tf_op jit(solution)/shard_map/chebyshev/pallas_call | solution.py:98
  53.4 0.1 collective-permute-start.6
  53.5 1.4 collective-permute-start.7
  55.0 0.0 collective-permute-done.10.refs_6_
  55.0 2.9 %collective-permute-start.8 = (f32[4,3,32,128]{3,2,1,0:T(8,128)S(1)}, f32[4,3,32,128]{3,2,1,0:T(8,128)S(1)}, u32[]{:S(2)}, u32[]{:S(2)}) collective-permute-start(f32[4,3,32,128]{3,2,1,0:T(8,128)S(1)} %get-tuple-element.21), channel_id=1, source_target_pairs={{0,12},{4,8},{8,4},{12,0},{1,13},{5,9},{9,5},{13,1},{2,14},{6,10},... | collective-permute-start | bytes 589832 | tf_op jit(solution)/shard_map/ppermute | solution.py:36
  57.9 0.0 collective-permute-done.9.refs_5_
  57.9 15.0 %chebyshev.3 = (f32[4,3,32,128]{3,2,1,0:T(8,128)S(1)}, f32[4,3,32,128]{3,2,1,0:T(8,128)S(1)}, f32[4,3,32,128]{3,2,1,0:T(8,128)S(1)}, f32[4,3,32,128]{3,2,1,0:T(8,128)S(1)}) custom-call(s32[1]{0:T(128)} %bitcast.me_ref, f32[3,32,128]{2,1,0:T(8,128)S(1)} %copy-done.1, f32[3,32,128]{2,1,0:T(8,128)S(1)} %collective-permute-done.refs_1_, ...), custom_call_target="tpu_custom_call" | custom-call | flops 28311552 | bytes 1572864 | tf_op jit(solution)/shard_map/chebyshev/pallas_call | solution.py:98
  72.9 0.1 collective-permute-start.12
  73.0 1.5 collective-permute-start.13
  74.4 2.9 %collective-permute-start.14 = (f32[4,3,32,128]{3,2,1,0:T(8,128)S(1)}, f32[4,3,32,128]{3,2,1,0:T(8,128)S(1)}, u32[]{:S(2)}, u32[]{:S(2)}) collective-permute-start(f32[4,3,32,128]{3,2,1,0:T(8,128)S(1)} %get-tuple-element.25), channel_id=1, source_target_pairs={{0,12},{4,8},{8,4},{12,0},{1,13},{5,9},{9,5},{13,1},{2,14},{6,10},... | collective-permute-start | bytes 589832 | tf_op jit(solution)/shard_map/ppermute | solution.py:36
  77.4 0.0 collective-permute-done.7.refs_2_
  77.4 0.0 collective-permute-done.8.refs_3_
  77.4 0.1 assemble.2
  77.4 1.6 %collective-permute-start.16 = (f32[16,3,32,128]{3,2,1,0:T(8,128)S(1)}, f32[16,3,32,128]{3,2,1,0:T(8,128)S(1)}, u32[]{:S(2)}, u32[]{:S(2)}) collective-permute-start(f32[16,3,32,128]{3,2,1,0:T(8,128)S(1)} %assemble.2), channel_id=1, source_target_pairs={{0,2},{2,0},{1,3},{3,1},{4,6},{6,4},{5,7},{7,5},{8,10},{10,8},{9,1... | collective-permute-start | bytes 2359304 | tf_op jit(solution)/shard_map/ppermute | solution.py:36
  79.0 1.1 collective-permute-done.12.refs_1_
  80.1 3.8 %collective-permute-done.13.refs_2_ = f32[4,3,32,128]{3,2,1,0:T(8,128)S(1)} collective-permute-done((f32[4,3,32,128]{3,2,1,0:T(8,128)S(1)}, f32[4,3,32,128]{3,2,1,0:T(8,128)S(1)}, u32[]{:S(2)}, u32[]{:S(2)}) %collective-permute-start.13) | collective-permute-done | bytes 196640 | tf_op jit(solution)/shard_map/ppermute | solution.py:36
  83.9 0.1 assemble.3
  83.9 1.6 %collective-permute-start.19 = (f32[16,3,32,128]{3,2,1,0:T(8,128)S(1)}, f32[16,3,32,128]{3,2,1,0:T(8,128)S(1)}, u32[]{:S(2)}, u32[]{:S(2)}) collective-permute-start(f32[16,3,32,128]{3,2,1,0:T(8,128)S(1)} %assemble.3), channel_id=1, source_target_pairs={{0,2},{2,0},{1,3},{3,1},{4,6},{6,4},{5,7},{7,5},{8,10},{10,8},{9,1... | collective-permute-start | bytes 2359304 | tf_op jit(solution)/shard_map/ppermute | solution.py:36
  85.5 9.6 %collective-permute-done.16 = f32[16,3,32,128]{3,2,1,0:T(8,128)S(1)} collective-permute-done((f32[16,3,32,128]{3,2,1,0:T(8,128)S(1)}, f32[16,3,32,128]{3,2,1,0:T(8,128)S(1)}, u32[]{:S(2)}, u32[]{:S(2)}) %collective-permute-start.16) | collective-permute-done | bytes 786464 | tf_op jit(solution)/shard_map/ppermute | solution.py:36
  95.1 0.5 collective-permute-start.18
  95.7 7.9 %collective-permute-done.19 = f32[16,3,32,128]{3,2,1,0:T(8,128)S(1)} collective-permute-done((f32[16,3,32,128]{3,2,1,0:T(8,128)S(1)}, f32[16,3,32,128]{3,2,1,0:T(8,128)S(1)}, u32[]{:S(2)}, u32[]{:S(2)}) %collective-permute-start.19) | collective-permute-done | bytes 786464 | tf_op jit(solution)/shard_map/ppermute | solution.py:36
  103.6 0.1 constant_dynamic-slice_fusion.3
  103.7 0.1 copy.10
  103.8 0.0 copy-start.2
  103.8 1.1 copy-done.2
  104.9 8.1 %projectors.1 = (bf16[48,288,256]{2,1,0:T(8,128)(2,1)S(1)}, bf16[48,288,256]{2,1,0:T(8,128)(2,1)S(1)}) custom-call(s32[1]{0:T(128)} %bitcast.1.group_ref, s32[48,3,128]{2,1,0:T(4,128)S(1)} %copy.9.offsets_ref, f32[48,3,8,128]{3,2,1,0:T(8,128)S(1)} %copy-done.2), custom_call_target="tpu_custom_call" | custom-call | flops 1811939328 | bytes 28311552 | tf_op jit(solution)/shard_map/projectors/pallas_call | solution.py:210
  113.1 0.0 collective-permute-done.15
  113.1 3.7 %regroup.2 = (bf16[4,48,16,256]{3,2,1,0:T(8,128)(2,1)S(1)}, bf16[4,48,16,256]{3,2,1,0:T(8,128)(2,1)S(1)}) custom-call(s32[1]{0:T(128)} %bitcast.1.group_ref, f32[1536,128]{1,0:T(8,128)S(1)} %bitcast.10, f32[1536,128]{1,0:T(8,128)} %bitcast.3.refs_1_, f32[1536,128]{1,0:T(8,128)S(1)} %bitcast.12, f32[1536,128]{1,0:T(8,128)} %bitcast.5.refs_3_), custom_call_target="tpu_custom_call" | custom-call | tf_op jit(solution)/shard_map/regroup/pallas_call | solution.py:156
  116.8 0.0 collective-permute-done.18
  116.8 3.7 %regroup.3 = (bf16[4,48,16,256]{3,2,1,0:T(8,128)(2,1)S(1)}, bf16[4,48,16,256]{3,2,1,0:T(8,128)(2,1)S(1)}) custom-call(s32[1]{0:T(128)} %bitcast.1.group_ref, f32[1536,128]{1,0:T(8,128)S(1)} %bitcast.11, f32[1536,128]{1,0:T(8,128)} %bitcast.7.refs_1_, f32[1536,128]{1,0:T(8,128)S(1)} %bitcast.13, f32[1536,128]{1,0:T(8,128)} %bitcast.9.refs_3_), custom_call_target="tpu_custom_call" | custom-call | tf_op jit(solution)/shard_map/regroup/pallas_call | solution.py:156
  120.6 7.3 %products.1 = (f32[128,128]{1,0:T(8,128)S(1)}, f32[288,128]{1,0:T(8,128)S(1)}) custom-call(bf16[48,288,256]{2,1,0:T(8,128)(2,1)S(1)} %get-tuple-element.26.refs_0_, bf16[48,288,256]{2,1,0:T(8,128)(2,1)S(1)} %get-tuple-element.27.refs_1_, bf16[4,48,16,256]{3,2,1,0:T(8,128)(2,1)S(1)} %get-tuple-element.28.refs_2_, ...), custom_call_target="tpu_custom_call" | custom-call | tf_op jit(solution)/shard_map/products/pallas_call | solution.py:263
  127.9 2.3 %collective-permute-start.21 = (f32[96,128]{1,0:T(8,128)S(1)}, f32[96,128]{1,0:T(8,128)S(1)}, u32[]{:S(2)}, u32[]{:S(2)}) collective-permute-start(f32[96,128]{1,0:T(8,128)S(1)} %get-tuple-element.43), channel_id=1, source_target_pairs={{0,12},{4,0},{8,4},{12,8},{1,13},{5,1},{9,5},{13,9},{2,14},{6,2},{... | collective-permute-start | bytes 147464 | tf_op jit(solution)/shard_map/ppermute | solution.py:374
  130.2 0.0 collective-permute-start.22
  130.2 0.1 broadcast_multiply_fusion
  130.3 0.3 mul.60.corr_ref
  130.6 1.6 %collective-permute-done.21.right_ref = f32[96,128]{1,0:T(8,128)S(1)} collective-permute-done((f32[96,128]{1,0:T(8,128)S(1)}, f32[96,128]{1,0:T(8,128)S(1)}, u32[]{:S(2)}, u32[]{:S(2)}) %collective-permute-start.21) | collective-permute-done | bytes 49184 | tf_op jit(solution)/shard_map/ppermute | solution.py:374
  132.2 3.8 %collective-permute-done.22.left_ref = f32[96,128]{1,0:T(8,128)S(1)} collective-permute-done((f32[96,128]{1,0:T(8,128)S(1)}, f32[96,128]{1,0:T(8,128)S(1)}, u32[]{:S(2)}, u32[]{:S(2)}) %collective-permute-start.22) | collective-permute-done | bytes 49184 | tf_op jit(solution)/shard_map/ppermute | solution.py:377
  136.1 0.4 gram_share.1
  136.5 0.1 collective-permute-start.23
  136.6 1.6 %collective-permute-start.24 = (f32[32,128]{1,0:T(8,128)S(1)}, f32[32,128]{1,0:T(8,128)S(1)}, u32[]{:S(2)}, u32[]{:S(2)}) collective-permute-start(f32[32,128]{1,0:T(8,128)S(1)} %get-tuple-element.46), channel_id=1, source_target_pairs={{0,2},{1,3},{2,0},{3,1},{4,6},{5,7},{6,4},{7,5},{8,10},{9,11},{10,... | collective-permute-start | bytes 49160 | tf_op jit(solution)/shard_map/ppermute | solution.py:36
  138.2 0.3 collective-permute-start.25
  138.5 0.0 collective-permute-done.23
  138.5 1.9 %collective-permute-done.24 = f32[32,128]{1,0:T(8,128)S(1)} collective-permute-done((f32[32,128]{1,0:T(8,128)S(1)}, f32[32,128]{1,0:T(8,128)S(1)}, u32[]{:S(2)}, u32[]{:S(2)}) %collective-permute-start.24) | collective-permute-done | bytes 16416 | tf_op jit(solution)/shard_map/ppermute | solution.py:36
  140.4 0.9 collective-permute-done.25
  141.3 0.1 collective-permute-start.26
  141.4 1.0 collective-permute-start.27
  142.4 3.4 %collective-permute-start.28 = (f32[32,128]{1,0:T(8,128)S(1)}, f32[32,128]{1,0:T(8,128)S(1)}, u32[]{:S(2)}, u32[]{:S(2)}) collective-permute-start(f32[32,128]{1,0:T(8,128)S(1)} %add_add_fusion.1), channel_id=1, source_target_pairs={{0,12},{4,8},{8,4},{12,0},{1,13},{5,9},{9,5},{13,1},{2,14},{6,10},... | collective-permute-start | bytes 49160 | tf_op jit(solution)/shard_map/ppermute | solution.py:36
  145.8 1.3 pad_maximum_fusion
  147.1 0.9 collective-permute-done.28
  148.0 0.6 add_add_fusion
  (23 shorter events, 0.1 us)
Async XLA Ops:
  0.6 103.0 %copy-start = (f32[48,8,8]{0,2,1:T(8,128)S(1)}, f32[48,8,8]{0,2,1:T(8,128)}, u32[]{:S(2)}) copy-start(f32[48,8,8]{0,2,1:T(8,128)} %param.9) | copy-start | bytes 36868
  0.7 7.3 %copy-start.1 = (f32[3,32,128]{2,1,0:T(8,128)S(1)}, f32[3,32,128]{2,1,0:T(8,128)}, u32[]{:S(2)}) copy-start(f32[3,32,128]{2,1,0:T(8,128)} %refs_0_.3) | copy-start | bytes 147460
  2.3 29.2 %collective-permute-start.3 = (f32[4,3,32,128]{3,2,1,0:T(8,128)S(1)}, f32[4,3,32,128]{3,2,1,0:T(8,128)S(1)}, u32[]{:S(2)}, u32[]{:S(2)}) collective-permute-start(f32[4,3,32,128]{3,2,1,0:T(8,128)S(1)} %get-tuple-element.38), channel_id=1, source_target_pairs={{0,4},{4,0},{8,12},{12,8},{1,5},{5,1},{9,13},{13,9},{2,6},{6,2},{1... | collective-permute-start | bytes 589832 | tf_op jit(solution)/shard_map/ppermute | solution.py:36
  5.4 33.0 %collective-permute-start.4 = (f32[4,3,32,128]{3,2,1,0:T(8,128)S(1)}, f32[4,3,32,128]{3,2,1,0:T(8,128)S(1)}, u32[]{:S(2)}, u32[]{:S(2)}) collective-permute-start(f32[4,3,32,128]{3,2,1,0:T(8,128)S(1)} %get-tuple-element.37), channel_id=1, source_target_pairs={{0,8},{4,12},{8,0},{12,4},{1,9},{5,13},{9,1},{13,5},{2,10},{6,14},... | collective-permute-start | bytes 589832 | tf_op jit(solution)/shard_map/ppermute | solution.py:36
  8.0 30.4 %collective-permute-start.5 = (f32[4,3,32,128]{3,2,1,0:T(8,128)S(1)}, f32[4,3,32,128]{3,2,1,0:T(8,128)S(1)}, u32[]{:S(2)}, u32[]{:S(2)}) collective-permute-start(f32[4,3,32,128]{3,2,1,0:T(8,128)S(1)} %get-tuple-element.34), channel_id=1, source_target_pairs={{0,12},{4,8},{8,4},{12,0},{1,13},{5,9},{9,5},{13,1},{2,14},{6,10},... | collective-permute-start | bytes 589832 | tf_op jit(solution)/shard_map/ppermute | solution.py:36
  8.0 11.6 %collective-permute-start = (f32[3,32,128]{2,1,0:T(8,128)S(1)}, f32[3,32,128]{2,1,0:T(8,128)S(1)}, u32[]{:S(2)}, u32[]{:S(2)}) collective-permute-start(f32[3,32,128]{2,1,0:T(8,128)S(1)} %copy-done.1), channel_id=1, source_target_pairs={{0,4},{4,0},{8,12},{12,8},{1,5},{5,1},{9,13},{13,9},{2,6},{6,2},{1... | collective-permute-start | bytes 147464 | tf_op jit(solution)/shard_map/ppermute | solution.py:36
  8.9 20.1 %collective-permute-start.1 = (f32[3,32,128]{2,1,0:T(8,128)S(1)}, f32[3,32,128]{2,1,0:T(8,128)S(1)}, u32[]{:S(2)}, u32[]{:S(2)}) collective-permute-start(f32[3,32,128]{2,1,0:T(8,128)S(1)} %copy-done.1), channel_id=1, source_target_pairs={{0,8},{4,12},{8,0},{12,4},{1,9},{5,13},{9,1},{13,5},{2,10},{6,14},... | collective-permute-start | bytes 147464 | tf_op jit(solution)/shard_map/ppermute | solution.py:36
  19.6 9.4 %collective-permute-start.2 = (f32[3,32,128]{2,1,0:T(8,128)S(1)}, f32[3,32,128]{2,1,0:T(8,128)S(1)}, u32[]{:S(2)}, u32[]{:S(2)}) collective-permute-start(f32[3,32,128]{2,1,0:T(8,128)S(1)} %copy-done.1), channel_id=1, source_target_pairs={{0,12},{4,8},{8,4},{12,0},{1,13},{5,9},{9,5},{13,1},{2,14},{6,10},... | collective-permute-start | bytes 147464 | tf_op jit(solution)/shard_map/ppermute | solution.py:36
  29.1 25.9 %collective-permute-start.10 = (f32[4,3,32,128]{3,2,1,0:T(8,128)S(1)}, f32[4,3,32,128]{3,2,1,0:T(8,128)S(1)}, u32[]{:S(2)}, u32[]{:S(2)}) collective-permute-start(f32[4,3,32,128]{3,2,1,0:T(8,128)S(1)} %get-tuple-element.41), channel_id=1, source_target_pairs={{0,8},{4,12},{8,0},{12,4},{1,9},{5,13},{9,1},{13,5},{2,10},{6,14},... | collective-permute-start | bytes 589832 | tf_op jit(solution)/shard_map/ppermute | solution.py:36
  29.1 28.8 %collective-permute-start.11 = (f32[4,3,32,128]{3,2,1,0:T(8,128)S(1)}, f32[4,3,32,128]{3,2,1,0:T(8,128)S(1)}, u32[]{:S(2)}, u32[]{:S(2)}) collective-permute-start(f32[4,3,32,128]{3,2,1,0:T(8,128)S(1)} %get-tuple-element.40), channel_id=1, source_target_pairs={{0,12},{4,8},{8,4},{12,0},{1,13},{5,9},{9,5},{13,1},{2,14},{6,10},... | collective-permute-start | bytes 589832 | tf_op jit(solution)/shard_map/ppermute | solution.py:36
  31.5 26.3 %collective-permute-start.9 = (f32[4,3,32,128]{3,2,1,0:T(8,128)S(1)}, f32[4,3,32,128]{3,2,1,0:T(8,128)S(1)}, u32[]{:S(2)}, u32[]{:S(2)}) collective-permute-start(f32[4,3,32,128]{3,2,1,0:T(8,128)S(1)} %get-tuple-element.35), channel_id=1, source_target_pairs={{0,4},{4,0},{8,12},{12,8},{1,5},{5,1},{9,13},{13,9},{2,6},{6,2},{1... | collective-permute-start | bytes 589832 | tf_op jit(solution)/shard_map/ppermute | solution.py:36
  53.4 21.0 %collective-permute-start.6 = (f32[4,3,32,128]{3,2,1,0:T(8,128)S(1)}, f32[4,3,32,128]{3,2,1,0:T(8,128)S(1)}, u32[]{:S(2)}, u32[]{:S(2)}) collective-permute-start(f32[4,3,32,128]{3,2,1,0:T(8,128)S(1)} %get-tuple-element.19), channel_id=1, source_target_pairs={{0,4},{4,0},{8,12},{12,8},{1,5},{5,1},{9,13},{13,9},{2,6},{6,2},{1... | collective-permute-start | bytes 589832 | tf_op jit(solution)/shard_map/ppermute | solution.py:36
  53.5 23.9 %collective-permute-start.7 = (f32[4,3,32,128]{3,2,1,0:T(8,128)S(1)}, f32[4,3,32,128]{3,2,1,0:T(8,128)S(1)}, u32[]{:S(2)}, u32[]{:S(2)}) collective-permute-start(f32[4,3,32,128]{3,2,1,0:T(8,128)S(1)} %get-tuple-element.20), channel_id=1, source_target_pairs={{0,8},{4,12},{8,0},{12,4},{1,9},{5,13},{9,1},{13,5},{2,10},{6,14},... | collective-permute-start | bytes 589832 | tf_op jit(solution)/shard_map/ppermute | solution.py:36
  55.0 22.4 %collective-permute-start.8 = (f32[4,3,32,128]{3,2,1,0:T(8,128)S(1)}, f32[4,3,32,128]{3,2,1,0:T(8,128)S(1)}, u32[]{:S(2)}, u32[]{:S(2)}) collective-permute-start(f32[4,3,32,128]{3,2,1,0:T(8,128)S(1)} %get-tuple-element.21), channel_id=1, source_target_pairs={{0,12},{4,8},{8,4},{12,0},{1,13},{5,9},{9,5},{13,1},{2,14},{6,10},... | collective-permute-start | bytes 589832 | tf_op jit(solution)/shard_map/ppermute | solution.py:36
  72.9 7.2 %collective-permute-start.12 = (f32[4,3,32,128]{3,2,1,0:T(8,128)S(1)}, f32[4,3,32,128]{3,2,1,0:T(8,128)S(1)}, u32[]{:S(2)}, u32[]{:S(2)}) collective-permute-start(f32[4,3,32,128]{3,2,1,0:T(8,128)S(1)} %get-tuple-element.23), channel_id=1, source_target_pairs={{0,4},{4,0},{8,12},{12,8},{1,5},{5,1},{9,13},{13,9},{2,6},{6,2},{1... | collective-permute-start | bytes 589832 | tf_op jit(solution)/shard_map/ppermute | solution.py:36
  73.0 10.9 %collective-permute-start.13 = (f32[4,3,32,128]{3,2,1,0:T(8,128)S(1)}, f32[4,3,32,128]{3,2,1,0:T(8,128)S(1)}, u32[]{:S(2)}, u32[]{:S(2)}) collective-permute-start(f32[4,3,32,128]{3,2,1,0:T(8,128)S(1)} %get-tuple-element.24), channel_id=1, source_target_pairs={{0,8},{4,12},{8,0},{12,4},{1,9},{5,13},{9,1},{13,5},{2,10},{6,14},... | collective-permute-start | bytes 589832 | tf_op jit(solution)/shard_map/ppermute | solution.py:36
  74.4 9.4 %collective-permute-start.14 = (f32[4,3,32,128]{3,2,1,0:T(8,128)S(1)}, f32[4,3,32,128]{3,2,1,0:T(8,128)S(1)}, u32[]{:S(2)}, u32[]{:S(2)}) collective-permute-start(f32[4,3,32,128]{3,2,1,0:T(8,128)S(1)} %get-tuple-element.25), channel_id=1, source_target_pairs={{0,12},{4,8},{8,4},{12,0},{1,13},{5,9},{9,5},{13,1},{2,14},{6,10},... | collective-permute-start | bytes 589832 | tf_op jit(solution)/shard_map/ppermute | solution.py:36
  77.4 26.2 %copy-start.3 = (s32[48,3,128]{2,0,1:T(8,128)S(1)}, s32[48,3,128]{2,0,1:T(8,128)}, u32[]{:S(2)}) copy-start(s32[48,3,128]{2,0,1:T(8,128)} %param.7) | copy-start | bytes 221188
  77.4 17.7 %collective-permute-start.16 = (f32[16,3,32,128]{3,2,1,0:T(8,128)S(1)}, f32[16,3,32,128]{3,2,1,0:T(8,128)S(1)}, u32[]{:S(2)}, u32[]{:S(2)}) collective-permute-start(f32[16,3,32,128]{3,2,1,0:T(8,128)S(1)} %assemble.2), channel_id=1, source_target_pairs={{0,2},{2,0},{1,3},{3,1},{4,6},{6,4},{5,7},{7,5},{8,10},{10,8},{9,1... | collective-permute-start | bytes 2359304 | tf_op jit(solution)/shard_map/ppermute | solution.py:36
  83.9 19.6 %collective-permute-start.19 = (f32[16,3,32,128]{3,2,1,0:T(8,128)S(1)}, f32[16,3,32,128]{3,2,1,0:T(8,128)S(1)}, u32[]{:S(2)}, u32[]{:S(2)}) collective-permute-start(f32[16,3,32,128]{3,2,1,0:T(8,128)S(1)} %assemble.3), channel_id=1, source_target_pairs={{0,2},{2,0},{1,3},{3,1},{4,6},{6,4},{5,7},{7,5},{8,10},{10,8},{9,1... | collective-permute-start | bytes 2359304 | tf_op jit(solution)/shard_map/ppermute | solution.py:36
  85.5 27.6 %collective-permute-start.15 = (f32[16,3,32,128]{3,2,1,0:T(8,128)S(1)}, f32[16,3,32,128]{3,2,1,0:T(8,128)}, u32[]{:S(2)}, u32[]{:S(2)}) collective-permute-start(f32[16,3,32,128]{3,2,1,0:T(8,128)S(1)} %assemble.2), channel_id=1, source_target_pairs={{0,1},{1,0},{2,3},{3,2},{4,5},{5,4},{6,7},{7,6},{8,9},{9,8},{10,11... | collective-permute-start | bytes 2359304 | tf_op jit(solution)/shard_map/ppermute | solution.py:36
  95.1 17.9 %collective-permute-start.17 = (f32[16,3,32,128]{3,2,1,0:T(8,128)S(1)}, f32[16,3,32,128]{3,2,1,0:T(8,128)}, u32[]{:S(2)}, u32[]{:S(2)}) collective-permute-start(f32[16,3,32,128]{3,2,1,0:T(8,128)S(1)} %collective-permute-done.16), channel_id=1, source_target_pairs={{0,1},{1,0},{2,3},{3,2},{4,5},{5,4},{6,7},{7,6},{8,9},{9,8},{10,11... | collective-permute-start | bytes 2359304 | tf_op jit(solution)/shard_map/ppermute | solution.py:36
  95.1 21.7 %collective-permute-start.18 = (f32[16,3,32,128]{3,2,1,0:T(8,128)S(1)}, f32[16,3,32,128]{3,2,1,0:T(8,128)}, u32[]{:S(2)}, u32[]{:S(2)}) collective-permute-start(f32[16,3,32,128]{3,2,1,0:T(8,128)S(1)} %assemble.3), channel_id=1, source_target_pairs={{0,1},{1,0},{2,3},{3,2},{4,5},{5,4},{6,7},{7,6},{8,9},{9,8},{10,11... | collective-permute-start | bytes 2359304 | tf_op jit(solution)/shard_map/ppermute | solution.py:36
  103.6 13.3 %collective-permute-start.20 = (f32[16,3,32,128]{3,2,1,0:T(8,128)S(1)}, f32[16,3,32,128]{3,2,1,0:T(8,128)}, u32[]{:S(2)}, u32[]{:S(2)}) collective-permute-start(f32[16,3,32,128]{3,2,1,0:T(8,128)S(1)} %collective-permute-done.19), channel_id=1, source_target_pairs={{0,1},{1,0},{2,3},{3,2},{4,5},{5,4},{6,7},{7,6},{8,9},{9,8},{10,11... | collective-permute-start | bytes 2359304 | tf_op jit(solution)/shard_map/ppermute | solution.py:36
  103.8 1.1 copy-start.2
  127.9 4.3 %collective-permute-start.21 = (f32[96,128]{1,0:T(8,128)S(1)}, f32[96,128]{1,0:T(8,128)S(1)}, u32[]{:S(2)}, u32[]{:S(2)}) collective-permute-start(f32[96,128]{1,0:T(8,128)S(1)} %get-tuple-element.43), channel_id=1, source_target_pairs={{0,12},{4,0},{8,4},{12,8},{1,13},{5,1},{9,5},{13,9},{2,14},{6,2},{... | collective-permute-start | bytes 147464 | tf_op jit(solution)/shard_map/ppermute | solution.py:374
  130.2 5.9 %collective-permute-start.22 = (f32[96,128]{1,0:T(8,128)S(1)}, f32[96,128]{1,0:T(8,128)S(1)}, u32[]{:S(2)}, u32[]{:S(2)}) collective-permute-start(f32[96,128]{1,0:T(8,128)S(1)} %get-tuple-element.42), channel_id=1, source_target_pairs={{0,4},{4,8},{8,12},{12,0},{1,5},{5,9},{9,13},{13,1},{2,6},{6,10},{... | collective-permute-start | bytes 147464 | tf_op jit(solution)/shard_map/ppermute | solution.py:377
  136.5 1.9 %collective-permute-start.23 = (f32[32,128]{1,0:T(8,128)S(1)}, f32[32,128]{1,0:T(8,128)S(1)}, u32[]{:S(2)}, u32[]{:S(2)}) collective-permute-start(f32[32,128]{1,0:T(8,128)S(1)} %get-tuple-element.44), channel_id=1, source_target_pairs={{0,1},{1,0},{2,3},{3,2},{4,5},{5,4},{6,7},{7,6},{8,9},{9,8},{10,11... | collective-permute-start | bytes 49160 | tf_op jit(solution)/shard_map/ppermute | solution.py:36
  136.6 3.8 %collective-permute-start.24 = (f32[32,128]{1,0:T(8,128)S(1)}, f32[32,128]{1,0:T(8,128)S(1)}, u32[]{:S(2)}, u32[]{:S(2)}) collective-permute-start(f32[32,128]{1,0:T(8,128)S(1)} %get-tuple-element.46), channel_id=1, source_target_pairs={{0,2},{1,3},{2,0},{3,1},{4,6},{5,7},{6,4},{7,5},{8,10},{9,11},{10,... | collective-permute-start | bytes 49160 | tf_op jit(solution)/shard_map/ppermute | solution.py:36
  138.2 3.2 %collective-permute-start.25 = (f32[32,128]{1,0:T(8,128)S(1)}, f32[32,128]{1,0:T(8,128)S(1)}, u32[]{:S(2)}, u32[]{:S(2)}) collective-permute-start(f32[32,128]{1,0:T(8,128)S(1)} %get-tuple-element.45), channel_id=1, source_target_pairs={{0,3},{1,2},{2,1},{3,0},{4,7},{5,6},{6,5},{7,4},{8,11},{9,10},{10,... | collective-permute-start | bytes 49160 | tf_op jit(solution)/shard_map/ppermute | solution.py:36
  141.3 5.7 %collective-permute-start.26 = (f32[32,128]{1,0:T(8,128)S(1)}, f32[32,128]{1,0:T(8,128)S(1)}, u32[]{:S(2)}, u32[]{:S(2)}) collective-permute-start(f32[32,128]{1,0:T(8,128)S(1)} %add_add_fusion.1), channel_id=1, source_target_pairs={{0,4},{4,0},{8,12},{12,8},{1,5},{5,1},{9,13},{13,9},{2,6},{6,2},{1... | collective-permute-start | bytes 49160 | tf_op jit(solution)/shard_map/ppermute | solution.py:36
  141.4 5.6 %collective-permute-start.27 = (f32[32,128]{1,0:T(8,128)S(1)}, f32[32,128]{1,0:T(8,128)S(1)}, u32[]{:S(2)}, u32[]{:S(2)}) collective-permute-start(f32[32,128]{1,0:T(8,128)S(1)} %add_add_fusion.1), channel_id=1, source_target_pairs={{0,8},{4,12},{8,0},{12,4},{1,9},{5,13},{9,1},{13,5},{2,10},{6,14},... | collective-permute-start | bytes 49160 | tf_op jit(solution)/shard_map/ppermute | solution.py:36
  142.4 5.5 %collective-permute-start.28 = (f32[32,128]{1,0:T(8,128)S(1)}, f32[32,128]{1,0:T(8,128)S(1)}, u32[]{:S(2)}, u32[]{:S(2)}) collective-permute-start(f32[32,128]{1,0:T(8,128)S(1)} %add_add_fusion.1), channel_id=1, source_target_pairs={{0,12},{4,8},{8,4},{12,0},{1,13},{5,9},{9,5},{13,1},{2,14},{6,10},... | collective-permute-start | bytes 49160 | tf_op jit(solution)/shard_map/ppermute | solution.py:36

commit v2 on v0

v2 whole, which is shorter than its diff:
```python
import functools
import math

import jax
import jax.numpy as jnp
from jax import lax
from jax.experimental import pallas as pl
from jax.experimental.pallas import tpu as pltpu
from jax.sharding import PartitionSpec as P

DEGREE = 12

CENTER_LEVEL = 3.6
HALF_WIDTH = 3.4
SHIFT = 3.0

TOGETHER = 4
SUBLANES = 8
MIB = 1024 * 1024

VMEM = pl.BlockSpec(memory_space=pltpu.VMEM)
SMEM = pl.BlockSpec(memory_space=pltpu.SMEM)
NT = (((1,), (1,)), ((), ()))
TN = (((0,), (0,)), ((), ()))


def params(mib):
    return pltpu.CompilerParams(vmem_limit_bytes=mib * MIB)


def split_bf16(x):
    high = x.astype(jnp.bfloat16)
    return high, (x - high.astype(jnp.float32)).astype(jnp.bfloat16)


def shifted(x, by):
    size = lax.axis_size("dom")
    return lax.ppermute(x, "dom", [(i, (i - by) % size) for i in range(size)])


def swapped(x, axes, size, by):
    return lax.ppermute(x, axes, [(i, i ^ by) for i in range(size)])


def filter_kernel(n_dom, planes, rows, first, *refs):
    refs = list(refs)
    given = None if first else refs.pop(0)
    ins, outs = refs[:n_dom], refs[n_dom : 2 * n_dom]
    refs = refs[2 * n_dom :]
    diagonal = refs.pop(0) if first else given
    even, odd = refs
    half_planes = n_dom * planes // 2
    cells = planes * rows
    lanes = even.shape[3]
    scale = 1.0 / HALF_WIDTH

    for x in range(half_planes):
        for half in range(2):
            m, i = divmod(half * half_planes + x, planes)
            part = slice(half * TOGETHER, (half + 1) * TOGETHER)
            for y in range(rows):
                even[x, y, part] = ins[m][pl.ds(i * rows + y, TOGETHER, stride=cells), :]
                if first:
                    at = TOGETHER * cells + i * rows + y
                    level = ins[m][at : at + 1, :] + (SHIFT - CENTER_LEVEL)
                    diagonal[x, y, part] = jnp.broadcast_to(
                        level * (2.0 * scale), (TOGETHER, lanes)
                    )

    block = SUBLANES
    lane = lax.broadcasted_iota(jnp.int32, (block, SUBLANES, lanes), 2)
    at_start, at_end = lane == 0, lane == lanes - 1

    def twice_operator(source, x, y):
        here = slice(y, y + block)
        centre = source[x, here]
        if x == 0:
            near = pltpu.roll(source[half_planes - 1, here], TOGETHER, 1) + source[x + 1, here]
        elif x == half_planes - 1:
            near = pltpu.roll(source[0, here], TOGETHER, 1) + source[x - 1, here]
        else:
            near = source[x - 1, here] + source[x + 1, here]
        before = (y - 1) % rows
        after = (y + block) % rows
        near += jnp.concatenate([source[x, before : before + 1], centre[:-1]], axis=0)
        near += jnp.concatenate([centre[1:], source[x, after : after + 1]], axis=0)
        low = pltpu.roll(centre, 1, 2)
        high = pltpu.roll(centre, lanes - 1, 2)
        near += jnp.where(at_start, high, jnp.where(at_end, low, low + high))
        return diagonal[x, here] * centre - scale * near

    places = [(x, y) for x in range(half_planes) for y in range(0, rows, block)]

    def next_field(source, target):
        for x, y in places:
            target[x, y : y + block] = twice_operator(source, x, y) - target[x, y : y + block]

    for x, y in places:
        odd[x, y : y + block] = 0.5 * twice_operator(even, x, y)
    next_field(odd, even)

    def two_steps(_, carry):
        next_field(even, odd)
        next_field(odd, even)
        return carry

    lax.fori_loop(0, DEGREE // 2 - 1, two_steps, 0)
    for m in range(n_dom):
        for i in range(planes):
            half, x = divmod(m * planes + i, half_planes)
            for y in range(rows):
                at = (i * rows + y) * TOGETHER
                outs[m][at : at + TOGETHER, :] = even[
                    x, y, half * TOGETHER : (half + 1) * TOGETHER
                ]


def filter_orbitals(diagonal, blocks, planes, rows):
    n_dom = len(blocks)
    first = diagonal is None
    cells = planes * rows
    lanes = blocks[0].shape[1]
    field = (n_dom * planes // 2, rows, SUBLANES, lanes)
    out = jax.ShapeDtypeStruct((cells * TOGETHER, lanes), jnp.float32)
    extra = [jax.ShapeDtypeStruct(field, jnp.float32)] if first else []
    given = [] if first else [diagonal]
    size = n_dom * cells * TOGETHER * lanes
    return pl.pallas_call(
        functools.partial(filter_kernel, n_dom, planes, rows, first),
        out_shape=[out] * n_dom + extra,
        in_specs=[VMEM] * (n_dom + len(given)),
        out_specs=[VMEM] * (n_dom + len(extra)),
        scratch_shapes=[pltpu.VMEM(field, jnp.float32)] * 2,
        compiler_params=params(12),
        cost_estimate=pl.CostEstimate(
            flops=12 * DEGREE * size, bytes_accessed=8 * size, transcendentals=0
        ),
        name="chebyshev",
    )(*given, *blocks)


def assemble_kernel(me_ref, *refs):
    *pieces, orbital_first, cell_first = refs
    n_dom = len(pieces)
    cells = cell_first.shape[0]
    me = me_ref[0]
    for m, piece in enumerate(pieces):
        start = lax.rem(me + m, n_dom) * TOGETHER
        for t in range(TOGETHER):
            orbital_first[start + t] = piece[pl.ds(t, cells, stride=TOGETHER), :]
    for cell in range(cells):
        here = slice(cell * TOGETHER, (cell + 1) * TOGETHER)
        tile = jnp.concatenate([piece[here, :] for piece in pieces], axis=0)
        cell_first[cell] = pltpu.roll(tile, me * TOGETHER, 0)


def assemble(me, pieces):
    n_dom = len(pieces)
    rows, lanes = pieces[0].shape
    cells, orbitals = rows // TOGETHER, n_dom * TOGETHER
    return pl.pallas_call(
        assemble_kernel,
        out_shape=[
            jax.ShapeDtypeStruct((orbitals, cells, lanes), jnp.float32),
            jax.ShapeDtypeStruct((cells, orbitals, lanes), jnp.float32),
        ],
        in_specs=[SMEM] + [VMEM] * n_dom,
        out_specs=[VMEM] * 2,
        compiler_params=params(8),
        name="assemble",
    )(me.reshape(1), *pieces)


def projector_kernel(groups, group_ref, offsets_ref, coefs_ref, high_out, low_out):
    per_group = offsets_ref.shape[0] // groups
    _, shells, channels, spread = coefs_ref.shape
    lanes = spread
    cells = high_out.shape[1] // lanes
    pairs = per_group // 2
    row_index = lax.broadcasted_iota(jnp.int32, (cells, channels, spread), 0)
    lane_index = lax.broadcasted_iota(jnp.int32, (lanes, spread), 0)

    def two_atoms(step, carry):
        shell = step // pairs
        first_atom = group_ref[0] * per_group + 2 * (step % pairs)
        dense = []
        for i in range(2):
            offsets = offsets_ref[first_atom + i, pl.ds(shell, 1), :]
            coefs = coefs_ref[first_atom + i, shell]
            at_row = row_index == (offsets // lanes)[None]
            at_row &= (offsets >= 0)[None]
            left = [
                jnp.where(at_row, part.astype(jnp.float32)[None], 0.0)
                .reshape(cells * channels, spread)
                .astype(jnp.bfloat16)
                for part in split_bf16(coefs)
            ]
            at_lane = jnp.where(lane_index == (offsets & (lanes - 1)), 1.0, 0.0)
            at_lane = at_lane.astype(jnp.bfloat16)
            values = lax.dot_general(
                jnp.concatenate(left, axis=1),
                jnp.concatenate([at_lane, at_lane], axis=1),
                NT,
                preferred_element_type=jnp.float32,
            )
            dense.append(values.reshape(cells, channels, lanes))
        high, low = split_bf16(jnp.concatenate(dense, axis=1))
        rows = pl.ds(pl.multiple_of(step * 2 * channels, 2 * channels), 2 * channels)
        for cell in range(cells):
            high_out[rows, cell * lanes : (cell + 1) * lanes] = high[cell]
            low_out[rows, cell * lanes : (cell + 1) * lanes] = low[cell]
        return carry

    lax.fori_loop(0, shells * pairs, two_atoms, 0)


def build_projectors(groups, group, offsets, coefs, cells, lanes):
    atoms, shells, channels, spread = coefs.shape
    rows = atoms // groups * shells * channels
    shape = jax.ShapeDtypeStruct((rows, cells * lanes), jnp.bfloat16)
    return pl.pallas_call(
        functools.partial(projector_kernel, groups),
        out_shape=[shape, shape],
        in_specs=[SMEM, VMEM, VMEM],
        out_specs=[VMEM, VMEM],
        compiler_params=params(20),
        cost_estimate=pl.CostEstimate(
            flops=4 * rows * cells * lanes * spread,
            bytes_accessed=8 * rows * cells * lanes,
            transcendentals=0,
        ),
        name="projectors",
    )(group, offsets, coefs)


def product_kernel(n_chunks, w_high, w_low, *refs):
    *fields, grid_out, proj_out = refs
    orbitals = grid_out.shape[0]
    cells, _, lanes = fields[0].shape
    n_groups = len(fields) // n_chunks
    block = 12
    grid_out[...] = jnp.zeros_like(grid_out)
    proj_out[...] = jnp.zeros_like(proj_out)

    def one_block(step, carry):
        highs, lows = [], []
        for g in range(n_groups):
            for c in range(n_chunks):
                field = fields[c * n_groups + g][pl.ds(step * block, block)]
                high, low = split_bf16(field)
                highs.append(jnp.concatenate([high[k] for k in range(block)], axis=1))
                lows.append(jnp.concatenate([low[k] for k in range(block)], axis=1))
        high, low = jnp.concatenate(highs, axis=0), jnp.concatenate(lows, axis=0)
        depth = block * lanes
        part = pl.ds(pl.multiple_of(step * depth, depth), depth)
        left_high = jnp.concatenate([high, w_high[:, part]], axis=0)
        left_low = jnp.concatenate([low, w_low[:, part]], axis=0)
        right = jnp.concatenate([high, low], axis=0)
        wide = lax.dot_general(left_high, right, NT, preferred_element_type=jnp.float32)
        narrow = lax.dot_general(left_low, high, NT, preferred_element_type=jnp.float32)
        total = wide[:, :orbitals] + wide[:, orbitals:] + narrow
        grid_out[...] += total[:orbitals]
        proj_out[...] += total[orbitals:]
        return carry

    lax.fori_loop(0, cells // block, one_block, 0)


def products(projectors, fields):
    rows = projectors[0].shape[0]
    n_chunks, n_groups = len(fields), len(fields[0])
    orbitals = n_chunks * n_groups * fields[0][0].shape[1]
    return pl.pallas_call(
        functools.partial(product_kernel, n_chunks),
        out_shape=[
            jax.ShapeDtypeStruct((orbitals, orbitals), jnp.float32),
            jax.ShapeDtypeStruct((rows, orbitals), jnp.float32),
        ],
        in_specs=[VMEM] * (2 + n_chunks * n_groups),
        out_specs=[VMEM] * 2,
        compiler_params=params(32),
        name="products",
    )(*projectors, *[field for chunk in fields for field in chunk])


def gram_kernel(
    scales, groups, group_ref, proj_ref, right_ref, left_ref, corr_ref, grid_ref, kept, sent
):
    rows = right_ref.shape[0]
    orbitals = grid_ref.shape[0]
    projections = proj_ref[rows : 2 * rows, :] + right_ref[...] + left_ref[...]
    highest = lax.Precision.HIGHEST
    weighted = jnp.dot(
        corr_ref[...], projections, precision=highest, preferred_element_type=jnp.float32
    )
    atom_part = lax.dot_general(
        projections, weighted, TN, precision=highest, preferred_element_type=jnp.float32
    )
    share = grid_ref[...] * scales[0] + atom_part * scales[1]
    column = lax.broadcasted_iota(jnp.int32, share.shape, 1)
    width = orbitals // groups
    bit = 1
    while bit < groups:
        span = width * bit
        turned = jnp.where(
            (column & span) == 0,
            pltpu.roll(share, orbitals - span, 1),
            pltpu.roll(share, span, 1),
        )
        share = jnp.where((group_ref[0] & bit) != 0, turned, share)
        bit *= 2
    kept[...] = share[: orbitals // 2]
    sent[...] = share[orbitals // 2 :]


def gram_share(scales, groups, group, proj, right, left, corr, grid_part):
    half = jax.ShapeDtypeStruct((grid_part.shape[0] // 2, grid_part.shape[1]), jnp.float32)
    return pl.pallas_call(
        functools.partial(gram_kernel, scales, groups),
        out_shape=[half, half],
        in_specs=[SMEM] + [VMEM] * 5,
        out_specs=[VMEM] * 2,
        compiler_params=params(8),
        name="gram_share",
    )(group, proj, right, left, corr, grid_part)


def whole_columns(panel, potential, me, projectors):
    n_dom = lax.axis_size("dom")
    orbitals, planes, rows, lanes = panel.shape
    cells = planes * rows
    flat = panel.reshape(orbitals * cells, lanes)
    levels = potential.reshape(cells, lanes)
    size = TOGETHER * cells
    n_chunks = orbitals // (n_dom * TOGETHER)
    arrived = []
    for c in range(n_chunks):
        blocks = []
        for m in range(n_dom):
            first = (c * n_dom + lax.rem(me - m + n_dom, n_dom)) * size
            block = lax.dynamic_slice_in_dim(flat, first, size, 0)
            if c == 0:
                block = jnp.concatenate([block, levels], axis=0)
            blocks.append(shifted(block, m) if m else block)
        arrived.append(blocks)
    arrived[0], projectors = lax.optimization_barrier((arrived[0], projectors))
    diagonal = None
    filtered, fields = [], []
    for blocks in arrived:
        done = filter_orbitals(diagonal, blocks, planes, rows)
        if diagonal is None:
            diagonal = done[n_dom]
        pieces = [shifted(done[(n_dom - m) % n_dom], m) if m else done[0] for m in range(n_dom)]
        orbital_first, cell_first = assemble(me, pieces)
        filtered.append(orbital_first)
        fields.append(cell_first)
    filtered = jnp.concatenate(filtered, axis=0).reshape(panel.shape)
    return filtered, fields, projectors


def plane_by_plane(panel, potential):
    n_dom = lax.axis_size("dom")
    orbitals, planes, rows, lanes = panel.shape
    diagonal = (potential + (SHIFT - CENTER_LEVEL)) * (2.0 / HALF_WIDTH)

    def twice_operator(field):
        low, high = shifted(field[:, -1:], -1), shifted(field[:, :1], 1)
        extended = jnp.concatenate([low, field, high], axis=1)
        near = extended[:, 2:] + extended[:, :-2]
        near += jnp.roll(field, 1, axis=2) + jnp.roll(field, -1, axis=2)
        padded = jnp.pad(field, ((0, 0), (0, 0), (0, 0), (1, 1)))
        near += padded[..., 2:] + padded[..., :-2]
        return diagonal * field - near / HALF_WIDTH

    def one_step(_, carry):
        before, current = carry
        return current, twice_operator(current) - before

    start = (panel, 0.5 * twice_operator(panel))
    filtered = lax.fori_loop(0, DEGREE - 1, one_step, start)[1]
    return filtered, [filtered.reshape(orbitals, planes * rows, lanes).swapaxes(0, 1)]


def on_device(panel, potential, point_offsets, point_coefs, correlation):
    orbitals, planes, rows, lanes = panel.shape
    n_dom, n_band, n_sub = (lax.axis_size(axis) for axis in ("dom", "band", "sub"))
    groups = n_band * n_sub
    me = lax.axis_index("dom")
    group = lax.axis_index(("band", "sub"))
    group_ref = group.reshape(1)

    cells = planes * rows
    projectors = build_projectors(groups, group_ref, point_offsets, point_coefs, cells, lanes)
    channels = correlation.shape[1]
    own_atoms = point_offsets.shape[0] // groups
    own_corr = lax.dynamic_slice_in_dim(correlation, group * own_atoms, own_atoms, 0)
    same_atom = jnp.eye(own_atoms, dtype=jnp.float32)
    corr_matrix = (same_atom[:, None, :, None] * own_corr[:, :, None, :]).reshape(
        own_atoms * channels, own_atoms * channels
    )

    if orbitals % (n_dom * TOGETHER) == 0 and (n_dom * planes) % 2 == 0:
        filtered, own_fields, projectors = whole_columns(panel, potential, me, projectors)
    else:
        filtered, own_fields = plane_by_plane(panel, potential)
    fields = []
    for own in own_fields:
        chunk = []
        for m in range(n_band):
            over_band = swapped(own, "band", n_band, m) if m else own
            chunk += [over_band] + [swapped(over_band, "sub", n_sub, k) for k in range(1, n_sub)]
        fields.append(chunk)

    grid_part, proj = products(projectors, fields)
    rows_atom = own_atoms * channels
    from_right = shifted(proj[:rows_atom], 1)
    from_left = shifted(proj[2 * rows_atom :], -1)
    scale_point = 1.0 / (cells * lanes * n_dom * groups)
    scale_atom = 1.0 / math.sqrt(point_offsets.shape[0] * n_dom)
    kept, sent = gram_share(
        (scale_point, scale_atom), groups, group_ref, proj, from_right, from_left, corr_matrix,
        grid_part,
    )
    by = groups // 2
    while by:
        kept += swapped(sent, ("band", "sub"), groups, by)
        by //= 2
        if by:
            kept, sent = kept[: by * orbitals], kept[by * orbitals :]
    by = 1
    while by < n_dom:
        kept += swapped(kept, "dom", n_dom, by)
        by *= 2
    return filtered, kept


def solution(mesh):
    placed = (
        P(("slab", "band", "sub"), "dom", None, None),
        P(("slab", "dom"), None, None),
        P(("slab", "dom"), None, None),
        P(("slab", "dom"), None, None, None),
        P(("slab", "dom"), None, None),
    )
    return jax.shard_map(
        on_device,
        mesh=mesh,
        in_specs=placed,
        out_specs=(P(("slab", "band", "sub"), "dom", None, None), P(("slab", "band", "sub"), None)),
        check_vma=False,
    )
```

time: 613 us -> 147 us (0.24)
  waiting for transfers between devices: 319 us -> 64.9 us
  local copies, waits for them, and re-layouts: 160 us -> 16.4 us
  other arithmetic: 31.9 us -> 2.07 us
  Pallas kernels: 0 us -> 28.8 us
  blocking collectives: 24.3 us -> 0 us
  starting transfers between devices: 52.9 us -> 33.9 us
  between operations: 14.2 us -> 0.9 us
  matrix products: 7.95 us -> 0 us
    ppermute x26 -> x24, waiting for transfers between devices: 222 us -> 64.9 us  [the longest x10 34.1 us: swapped(): return lax.ppermute(x, axes, [(i, i ^ by) for i in range(size)])]
    psum x1 -> x0, waiting for transfers between devices: 85.2 us -> none  [on_device(): total_gram = lax.psum(whole_gram, ('dom', 'band', 'sub'))]
    gather x2 -> x0, local copies, waits for them, and re-layouts: 69.9 us -> none  [on_device(): picked = jnp.where(live_mask[None], flat_panel[:, safe_offsets], 0.0)]
    slice x48 -> x2, local copies, waits for them, and re-layouts: 46.4 us -> 0.01 us  [the longest x1 0.01 us: on_device(): from_left = shifted(proj[2 * rows_atom:], -1)]
    pallas_call x0 -> x7, Pallas kernels: none -> 28.8 us  [the longest x2 12.1 us: filter_orbitals(): pl.pallas_call(functools.partial(filter_kernel, n_dom, planes, rows, firs...]
    all_to_all x1 -> x0, blocking collectives: 24.3 us -> none  [on_device(): lax.all_to_all(left_rows, ('band', 'sub'), split_axis=1, concat_axis=0, t...]
    while x89 -> x0, local copies, waits for them, and re-layouts: 18 us -> none
    sub x11 -> x0, other arithmetic: 17.1 us -> none  [one_step(): return (current, 2.0 * apply_once(current, potential) - before)]
  transfers between devices with their start and end apart: 28 -> 24, of which waited for: 26 -> 12; matrix products, arithmetic and copies ran while one was open for 9% -> 1% of each run, Pallas kernels for 0% -> 13%
where the time goes in v2:
time: 147 us
  waiting for transfers between devices  64.9 us (44%)
  starting transfers between devices  33.9 us (23%)
  Pallas kernels  28.8 us (20%)
  local copies, waits for them, and re-layouts  16.4 us (11%)
  other arithmetic  2.07 us (1%)
    ppermute x10, waiting for transfers between devices, swapped(): return lax.ppermute(x, axes, [(i, i ^ by) for i in range(size)])  34.1 us
    ppermute x14, waiting for transfers between devices, shifted(): return lax.ppermute(x, 'dom', [(i, (i - by) % size) for i in range(size)])  30.8 us
    ppermute x14, starting transfers between devices, shifted(): return lax.ppermute(x, 'dom', [(i, (i - by) % size) for i in range(size)])  28.7 us
    unnamed x25, local copies, waits for them, and re-layouts  13.6 us
    pallas_call x2, Pallas kernels, filter_orbitals(): pl.pallas_call(functools.partial(filter_kernel, n_dom, planes, rows, firs...  12.1 us
    pallas_call x1, Pallas kernels, products(): pl.pallas_call(functools.partial(product_kernel, n_chunks), out_shape=[ja...  8.76 us
    pallas_call x1, Pallas kernels, build_projectors(): pl.pallas_call(functools.partial(projector_kernel, groups), out_shape=[sh...  7.04 us
    ppermute x10, starting transfers between devices, swapped(): return lax.ppermute(x, axes, [(i, i ^ by) for i in range(size)])  5.16 us
  transfers between devices with their start and end apart: 24, of which 12 were waited for; matrix products, arithmetic and copies ran while one was open for 1% of the time, Pallas kernels for 13%

profile of v2, /device:TPU:0, one launch (start us, length us, event | category | flops | bytes accessed | tf_op | source)
XLA Modules:
  0.0 147.0 jit_solution(5797532763793947187)
XLA Ops:
  0.6 0.0 copy-start
  0.7 2.3 %constant_dynamic-slice_fusion.1 = (f32[384,128]{1,0:T(8,128)S(1)}, f32[384,128]{1,0:T(8,128)S(1)}, f32[384,128]{1,0:T(8,128)}, f32[384,128]{1,0:T(8,128)S(1)}, ...) fusion(f32[3072,128]{1,0:T(8,128)} %bitcast.5, ...), kind=kLoop, calls=%fused_computation.10 | loop fusion | bytes 3145760 | tf_op jit(solution)/shard_map/dynamic_slice | solution.py:341
  3.0 0.1 pad_maximum_fusion.1
  3.0 5.1 %collective-permute-start = (f32[480,128]{1,0:T(8,128)S(1)}, f32[480,128]{1,0:T(8,128)S(1)}, u32[]{:S(2)}, u32[]{:S(2)}) collective-permute-start(f32[480,128]{1,0:T(8,128)S(1)} %get-tuple-element.63), channel_id=1, source_target_pairs={{0,12},{4,0},{8,4},{12,8},{1,13},{5,1},{9,5},{13,9},{2,14},{6,2},{... | collective-permute-start | bytes 737288 | tf_op jit(solution)/shard_map/ppermute | solution.py:38
  8.1 0.0 collective-permute-start.1
  8.1 1.0 collective-permute-start.2
  9.2 2.8 %collective-permute-start.6 = (f32[384,128]{1,0:T(8,128)}, f32[384,128]{1,0:T(8,128)S(1)}, u32[]{:S(2)}, u32[]{:S(2)}) collective-permute-start(f32[384,128]{1,0:T(8,128)} %get-tuple-element.54), channel_id=1, source_target_pairs={{0,12},{4,0},{8,4},{12,8},{1,13},{5,1},{9,5},{13,9},{2,14},{6,2},{... | collective-permute-start | bytes 589832 | tf_op jit(solution)/shard_map/ppermute | solution.py:38
  12.0 1.1 collective-permute-start.7
  13.2 7.0 %projectors.1 = (bf16[288,12288]{1,0:T(8,128)(2,1)S(1)}, bf16[288,12288]{1,0:T(8,128)(2,1)S(1)}) custom-call(s32[1]{0:T(128)} %bitcast.3.group_ref, s32[48,3,128]{2,1,0:T(4,128)S(1)} %copy.9.offsets_ref, f32[48,3,8,128]{3,2,1,0:T(8,128)S(1)} %copy-done.9), custom_call_target="tpu_custom_call" | custom-call | flops 1811939328 | bytes 28311552 | tf_op jit(solution)/shard_map/projectors/pallas_call | solution.py:221
  20.2 2.8 %copy-done.1 = bf16[288,12288]{1,0:T(8,128)(2,1)} copy-done((bf16[288,12288]{1,0:T(8,128)(2,1)}, bf16[288,12288]{1,0:T(8,128)(2,1)S(1)}, u32[]{:S(2)}) %copy-start.1) | copy-done | bytes 7077912
  23.1 2.9 %copy-done.3 = bf16[288,12288]{1,0:T(8,128)(2,1)} copy-done((bf16[288,12288]{1,0:T(8,128)(2,1)}, bf16[288,12288]{1,0:T(8,128)(2,1)S(1)}, u32[]{:S(2)}) %copy-start.3) | copy-done | bytes 7077912
  26.0 0.0 collective-permute-done.refs_1_
  26.0 0.0 collective-permute-start.8
  26.0 12.6 %collective-permute-done.1.refs_2_ = f32[480,128]{1,0:T(8,128)S(1)} collective-permute-done((f32[480,128]{1,0:T(8,128)S(1)}, f32[480,128]{1,0:T(8,128)S(1)}, u32[]{:S(2)}, u32[]{:S(2)}) %collective-permute-start.1) | collective-permute-done | bytes 245792 | tf_op jit(solution)/shard_map/ppermute | solution.py:38
  38.6 0.0 collective-permute-done.2.refs_3_
  38.6 6.2 %chebyshev.2 = (f32[384,128]{1,0:T(8,128)S(1)}, f32[384,128]{1,0:T(8,128)S(1)}, f32[384,128]{1,0:T(8,128)S(1)}, f32[384,128]{1,0:T(8,128)S(1)}, f32[6,32,8,128]{3,2,1,0:T(8,128)S(1)}) custom-call(f32[480,128]{1,0:T(8,128)S(1)} %get-tuple-element.29.refs_0_, f32[480,128]{1,0:T(8,128)S(1)} %collective-permute-done.refs_1_, ...), custom_call_target="tpu_custom_call" | custom-call | flops 28311552 | bytes 1572864 | tf_op jit(solution)/shard_map/chebyshev/pallas_call | solution.py:128
  44.8 0.1 collective-permute-start.3
  44.9 4.7 %collective-permute-start.4 = (f32[384,128]{1,0:T(8,128)S(1)}, f32[384,128]{1,0:T(8,128)S(1)}, u32[]{:S(2)}, u32[]{:S(2)}) collective-permute-start(f32[384,128]{1,0:T(8,128)S(1)} %get-tuple-element.35), channel_id=1, source_target_pairs={{0,8},{4,12},{8,0},{12,4},{1,9},{5,13},{9,1},{13,5},{2,10},{6,14},... | collective-permute-start | bytes 589832 | tf_op jit(solution)/shard_map/ppermute | solution.py:38
  49.6 0.0 collective-permute-done.6.refs_2_
  49.6 1.9 %collective-permute-start.5 = (f32[384,128]{1,0:T(8,128)S(1)}, f32[384,128]{1,0:T(8,128)S(1)}, u32[]{:S(2)}, u32[]{:S(2)}) collective-permute-start(f32[384,128]{1,0:T(8,128)S(1)} %get-tuple-element.36), channel_id=1, source_target_pairs={{0,4},{4,8},{8,12},{12,0},{1,5},{5,9},{9,13},{13,1},{2,6},{6,10},{... | collective-permute-start | bytes 589832 | tf_op jit(solution)/shard_map/ppermute | solution.py:38
  51.6 5.9 %chebyshev.3 = (f32[384,128]{1,0:T(8,128)S(1)}, f32[384,128]{1,0:T(8,128)S(1)}, f32[384,128]{1,0:T(8,128)S(1)}, f32[384,128]{1,0:T(8,128)S(1)}) custom-call(f32[6,32,8,128]{3,2,1,0:T(8,128)S(1)} %get-tuple-element.38.refs_0_, f32[384,128]{1,0:T(8,128)S(1)} %get-tuple-element.55.refs_1_, f32[384,128]{1,0:T(8,128)S(1)} %collective-permute-done.6.refs_2_, ...), custom_call_target="tpu_custom_call" | custom-call | flops 28311552 | bytes 1572864 | tf_op jit(solution)/shard_map/chebyshev/pallas_call | solution.py:128
  57.4 1.9 %collective-permute-start.9 = (f32[384,128]{1,0:T(8,128)S(1)}, f32[384,128]{1,0:T(8,128)S(1)}, u32[]{:S(2)}, u32[]{:S(2)}) collective-permute-start(f32[384,128]{1,0:T(8,128)S(1)} %get-tuple-element.40), channel_id=1, source_target_pairs={{0,12},{4,0},{8,4},{12,8},{1,13},{5,1},{9,5},{13,9},{2,14},{6,2},{... | collective-permute-start | bytes 589832 | tf_op jit(solution)/shard_map/ppermute | solution.py:38
  59.3 4.7 %collective-permute-start.10 = (f32[384,128]{1,0:T(8,128)S(1)}, f32[384,128]{1,0:T(8,128)S(1)}, u32[]{:S(2)}, u32[]{:S(2)}) collective-permute-start(f32[384,128]{1,0:T(8,128)S(1)} %get-tuple-element.41), channel_id=1, source_target_pairs={{0,8},{4,12},{8,0},{12,4},{1,9},{5,13},{9,1},{13,5},{2,10},{6,14},... | collective-permute-start | bytes 589832 | tf_op jit(solution)/shard_map/ppermute | solution.py:38
  64.0 0.0 collective-permute-done.3.refs_1_
  64.0 1.9 %collective-permute-start.11 = (f32[384,128]{1,0:T(8,128)S(1)}, f32[384,128]{1,0:T(8,128)S(1)}, u32[]{:S(2)}, u32[]{:S(2)}) collective-permute-start(f32[384,128]{1,0:T(8,128)S(1)} %get-tuple-element.42), channel_id=1, source_target_pairs={{0,4},{4,8},{8,12},{12,0},{1,5},{5,9},{9,13},{13,1},{2,6},{6,10},{... | collective-permute-start | bytes 589832 | tf_op jit(solution)/shard_map/ppermute | solution.py:38
  66.0 9.3 %collective-permute-done.4.refs_2_ = f32[384,128]{1,0:T(8,128)S(1)} collective-permute-done((f32[384,128]{1,0:T(8,128)S(1)}, f32[384,128]{1,0:T(8,128)S(1)}, u32[]{:S(2)}, u32[]{:S(2)}) %collective-permute-start.4) | collective-permute-done | bytes 196640 | tf_op jit(solution)/shard_map/ppermute | solution.py:38
  75.3 0.0 collective-permute-done.5.refs_3_
  75.3 0.2 assemble.2
  75.5 0.9 copy-done.5
  76.4 1.5 %collective-permute-start.13 = (f32[96,16,128]{2,1,0:T(8,128)S(1)}, f32[96,16,128]{2,1,0:T(8,128)S(1)}, u32[]{:S(2)}, u32[]{:S(2)}) collective-permute-start(f32[96,16,128]{2,1,0:T(8,128)S(1)} %get-tuple-element.46.refs_0_), channel_id=1, source_target_pairs={{0,2},{2,0},{1,3},{3,1},{4,6},{6,4},{5,7},{7,5},{8,10},{10,8},{9,1... | collective-permute-start | bytes 2359304 | tf_op jit(solution)/shard_map/ppermute | solution.py:42
  77.8 0.0 collective-permute-done.9.refs_1_
  77.8 3.0 %collective-permute-done.10.refs_2_ = f32[384,128]{1,0:T(8,128)S(1)} collective-permute-done((f32[384,128]{1,0:T(8,128)S(1)}, f32[384,128]{1,0:T(8,128)S(1)}, u32[]{:S(2)}, u32[]{:S(2)}) %collective-permute-start.10) | collective-permute-done | bytes 196640 | tf_op jit(solution)/shard_map/ppermute | solution.py:38
  80.8 0.0 collective-permute-done.11.refs_3_
  80.8 0.2 assemble.3
  81.0 0.0 copy-start.7
  81.0 0.9 copy-done.7
  81.9 1.5 %collective-permute-start.16 = (f32[96,16,128]{2,1,0:T(8,128)S(1)}, f32[96,16,128]{2,1,0:T(8,128)S(1)}, u32[]{:S(2)}, u32[]{:S(2)}) collective-permute-start(f32[96,16,128]{2,1,0:T(8,128)S(1)} %get-tuple-element.47.refs_4_), channel_id=1, source_target_pairs={{0,2},{2,0},{1,3},{3,1},{4,6},{6,4},{5,7},{7,5},{8,10},{10,8},{9,1... | collective-permute-start | bytes 2359304 | tf_op jit(solution)/shard_map/ppermute | solution.py:42
  83.4 0.5 collective-permute-start.15
  83.9 11.2 %collective-permute-done.13.refs_2_ = f32[96,16,128]{2,1,0:T(8,128)S(1)} collective-permute-done((f32[96,16,128]{2,1,0:T(8,128)S(1)}, f32[96,16,128]{2,1,0:T(8,128)S(1)}, u32[]{:S(2)}, u32[]{:S(2)}) %collective-permute-start.13) | collective-permute-done | bytes 786464 | tf_op jit(solution)/shard_map/ppermute | solution.py:42
  95.2 10.0 %collective-permute-done.16.refs_6_ = f32[96,16,128]{2,1,0:T(8,128)S(1)} collective-permute-done((f32[96,16,128]{2,1,0:T(8,128)S(1)}, f32[96,16,128]{2,1,0:T(8,128)S(1)}, u32[]{:S(2)}, u32[]{:S(2)}) %collective-permute-start.16) | collective-permute-done | bytes 786464 | tf_op jit(solution)/shard_map/ppermute | solution.py:42
  105.2 0.1 constant_dynamic-slice_fusion
  105.3 0.1 copy.10
  105.4 0.0 collective-permute-done.12.refs_1_
  105.4 2.2 %collective-permute-done.17.refs_7_ = f32[96,16,128]{2,1,0:T(8,128)} collective-permute-done((f32[96,16,128]{2,1,0:T(8,128)S(1)}, f32[96,16,128]{2,1,0:T(8,128)}, u32[]{:S(2)}, u32[]{:S(2)}) %collective-permute-start.17) | collective-permute-done | bytes 786464 | tf_op jit(solution)/shard_map/ppermute | solution.py:42
  107.6 3.0 %copy-done.2 = bf16[288,12288]{1,0:T(8,128)(2,1)S(1)} copy-done((bf16[288,12288]{1,0:T(8,128)(2,1)S(1)}, bf16[288,12288]{1,0:T(8,128)(2,1)}, u32[]{:S(2)}) %copy-start.2) | copy-done | bytes 7077912
  110.6 3.0 %copy-done.4 = bf16[288,12288]{1,0:T(8,128)(2,1)S(1)} copy-done((bf16[288,12288]{1,0:T(8,128)(2,1)S(1)}, bf16[288,12288]{1,0:T(8,128)(2,1)}, u32[]{:S(2)}) %copy-start.4) | copy-done | bytes 7077912
  113.6 8.8 %products.1 = (f32[128,128]{1,0:T(8,128)S(1)}, f32[288,128]{1,0:T(8,128)S(1)}) custom-call(bf16[288,12288]{1,0:T(8,128)(2,1)S(1)} %copy-done.2, bf16[288,12288]{1,0:T(8,128)(2,1)S(1)} %copy-done.4, f32[96,16,128]{2,1,0:T(8,128)S(1)} %get-tuple-element.46.refs_0_, f32[96,16,128]{2,1,0:T(8,128)} %collective-permute-done.12.refs_1_, ...), custom_call_target="tpu_custom_call" | custom-call | tf_op jit(solution)/shard_map/products/pallas_call | solution.py:273
  122.4 0.0 copy-start.8
  122.4 0.1 collective-permute-start.18
  122.5 3.4 %collective-permute-start.19 = (f32[96,128]{1,0:T(8,128)S(1)}, f32[96,128]{1,0:T(8,128)S(1)}, u32[]{:S(2)}, u32[]{:S(2)}) collective-permute-start(f32[96,128]{1,0:T(8,128)S(1)} %get-tuple-element.60), channel_id=1, source_target_pairs={{0,4},{4,8},{8,12},{12,0},{1,5},{5,9},{9,13},{13,1},{2,6},{6,10},{... | collective-permute-start | bytes 147464 | tf_op jit(solution)/shard_map/ppermute | solution.py:38
  125.9 0.1 broadcast_multiply_fusion
  126.0 0.3 mul.60.corr_ref
  126.3 1.6 %collective-permute-done.18.right_ref = f32[96,128]{1,0:T(8,128)S(1)} collective-permute-done((f32[96,128]{1,0:T(8,128)S(1)}, f32[96,128]{1,0:T(8,128)S(1)}, u32[]{:S(2)}, u32[]{:S(2)}) %collective-permute-start.18) | collective-permute-done | bytes 49184 | tf_op jit(solution)/shard_map/ppermute | solution.py:38
  127.9 4.3 %collective-permute-done.19.left_ref = f32[96,128]{1,0:T(8,128)S(1)} collective-permute-done((f32[96,128]{1,0:T(8,128)S(1)}, f32[96,128]{1,0:T(8,128)S(1)}, u32[]{:S(2)}, u32[]{:S(2)}) %collective-permute-start.19) | collective-permute-done | bytes 49184 | tf_op jit(solution)/shard_map/ppermute | solution.py:38
  132.2 0.6 gram_share.1
  132.8 1.6 %collective-permute-start.20 = (f32[64,128]{1,0:T(8,128)S(1)}, f32[64,128]{1,0:T(8,128)S(1)}, u32[]{:S(2)}, u32[]{:S(2)}) collective-permute-start(f32[64,128]{1,0:T(8,128)S(1)} %get-tuple-element.51), channel_id=1, source_target_pairs={{0,2},{1,3},{2,0},{3,1},{4,6},{5,7},{6,4},{7,5},{8,10},{9,11},{10,... | collective-permute-start | bytes 98312 | tf_op jit(solution)/shard_map/ppermute | solution.py:42
  134.3 2.4 %collective-permute-done.20 = f32[64,128]{1,0:T(8,128)S(1)} collective-permute-done((f32[64,128]{1,0:T(8,128)S(1)}, f32[64,128]{1,0:T(8,128)S(1)}, u32[]{:S(2)}, u32[]{:S(2)}) %collective-permute-start.20) | collective-permute-done | bytes 32800 | tf_op jit(solution)/shard_map/ppermute | solution.py:42
  136.8 0.1 collective-permute-start.21
  136.8 1.2 collective-permute-done.21
  138.0 3.7 %collective-permute-done.22 = f32[32,128]{1,0:T(8,128)S(1)} collective-permute-done((f32[32,128]{1,0:T(8,128)S(1)}, f32[32,128]{1,0:T(8,128)S(1)}, u32[]{:S(2)}, u32[]{:S(2)}) %collective-permute-start.22) | collective-permute-done | bytes 16416 | tf_op jit(solution)/shard_map/ppermute | solution.py:42
  141.8 0.0 collective-permute-start.23
  141.8 1.3 pad_maximum_fusion
  143.0 3.3 %collective-permute-done.23 = f32[32,128]{1,0:T(8,128)S(1)} collective-permute-done((f32[32,128]{1,0:T(8,128)S(1)}, f32[32,128]{1,0:T(8,128)S(1)}, u32[]{:S(2)}, u32[]{:S(2)}) %collective-permute-start.23) | collective-permute-done | bytes 16416 | tf_op jit(solution)/shard_map/ppermute | solution.py:42
  146.4 0.6 add.100
  (30 shorter events, 0.1 us)
Async XLA Ops:
  0.6 104.6 %copy-start = (f32[48,8,8]{0,2,1:T(8,128)S(1)}, f32[48,8,8]{0,2,1:T(8,128)}, u32[]{:S(2)}) copy-start(f32[48,8,8]{0,2,1:T(8,128)} %param.9) | copy-start | bytes 36868
  0.7 2.3 %copy-start.11 = (f32[3,32,128]{2,1,0:T(8,128)S(1)}, f32[3,32,128]{2,1,0:T(8,128)}, u32[]{:S(2)}) copy-start(f32[3,32,128]{2,1,0:T(8,128)} %param.6) | copy-start | bytes 147460
  3.0 10.1 %copy-start.10 = (s32[48,3,128]{2,0,1:T(8,128)S(1)}, s32[48,3,128]{2,0,1:T(8,128)}, u32[]{:S(2)}) copy-start(s32[48,3,128]{2,0,1:T(8,128)} %param.7) | copy-start | bytes 221188
  3.0 10.2 %copy-start.9 = (f32[48,3,8,128]{3,2,1,0:T(8,128)S(1)}, f32[48,3,8,128]{3,2,1,0:T(8,128)}, u32[]{:S(2)}) copy-start(f32[48,3,8,128]{3,2,1,0:T(8,128)} %coefs_ref.1) | copy-start | bytes 1769476
  3.0 22.9 %collective-permute-start = (f32[480,128]{1,0:T(8,128)S(1)}, f32[480,128]{1,0:T(8,128)S(1)}, u32[]{:S(2)}, u32[]{:S(2)}) collective-permute-start(f32[480,128]{1,0:T(8,128)S(1)} %get-tuple-element.63), channel_id=1, source_target_pairs={{0,12},{4,0},{8,4},{12,8},{1,13},{5,1},{9,5},{13,9},{2,14},{6,2},{... | collective-permute-start | bytes 737288 | tf_op jit(solution)/shard_map/ppermute | solution.py:38
  8.1 30.5 %collective-permute-start.1 = (f32[480,128]{1,0:T(8,128)S(1)}, f32[480,128]{1,0:T(8,128)S(1)}, u32[]{:S(2)}, u32[]{:S(2)}) collective-permute-start(f32[480,128]{1,0:T(8,128)S(1)} %get-tuple-element.64), channel_id=1, source_target_pairs={{0,8},{4,12},{8,0},{12,4},{1,9},{5,13},{9,1},{13,5},{2,10},{6,14},... | collective-permute-start | bytes 737288 | tf_op jit(solution)/shard_map/ppermute | solution.py:38
  8.1 30.5 %collective-permute-start.2 = (f32[480,128]{1,0:T(8,128)S(1)}, f32[480,128]{1,0:T(8,128)S(1)}, u32[]{:S(2)}, u32[]{:S(2)}) collective-permute-start(f32[480,128]{1,0:T(8,128)S(1)} %get-tuple-element.62), channel_id=1, source_target_pairs={{0,4},{4,8},{8,12},{12,0},{1,5},{5,9},{9,13},{13,1},{2,6},{6,10},{... | collective-permute-start | bytes 737288 | tf_op jit(solution)/shard_map/ppermute | solution.py:38
  9.2 40.4 %collective-permute-start.6 = (f32[384,128]{1,0:T(8,128)}, f32[384,128]{1,0:T(8,128)S(1)}, u32[]{:S(2)}, u32[]{:S(2)}) collective-permute-start(f32[384,128]{1,0:T(8,128)} %get-tuple-element.54), channel_id=1, source_target_pairs={{0,12},{4,0},{8,4},{12,8},{1,13},{5,1},{9,5},{13,9},{2,14},{6,2},{... | collective-permute-start | bytes 589832 | tf_op jit(solution)/shard_map/ppermute | solution.py:38
  12.0 39.6 %collective-permute-start.7 = (f32[384,128]{1,0:T(8,128)S(1)}, f32[384,128]{1,0:T(8,128)S(1)}, u32[]{:S(2)}, u32[]{:S(2)}) collective-permute-start(f32[384,128]{1,0:T(8,128)S(1)} %get-tuple-element.53), channel_id=1, source_target_pairs={{0,8},{4,12},{8,0},{12,4},{1,9},{5,13},{9,1},{13,5},{2,10},{6,14},... | collective-permute-start | bytes 589832 | tf_op jit(solution)/shard_map/ppermute | solution.py:38
  20.2 2.9 %copy-start.1 = (bf16[288,12288]{1,0:T(8,128)(2,1)}, bf16[288,12288]{1,0:T(8,128)(2,1)S(1)}, u32[]{:S(2)}) copy-start(bf16[288,12288]{1,0:T(8,128)(2,1)S(1)} %get-tuple-element.44.w_high) | copy-start | bytes 21233668
  23.1 2.9 %copy-start.3 = (bf16[288,12288]{1,0:T(8,128)(2,1)}, bf16[288,12288]{1,0:T(8,128)(2,1)S(1)}, u32[]{:S(2)}) copy-start(bf16[288,12288]{1,0:T(8,128)(2,1)S(1)} %get-tuple-element.45.w_low) | copy-start | bytes 21233668
  26.0 25.6 %collective-permute-start.8 = (f32[384,128]{1,0:T(8,128)S(1)}, f32[384,128]{1,0:T(8,128)S(1)}, u32[]{:S(2)}, u32[]{:S(2)}) collective-permute-start(f32[384,128]{1,0:T(8,128)S(1)} %get-tuple-element.52), channel_id=1, source_target_pairs={{0,4},{4,8},{8,12},{12,0},{1,5},{5,9},{9,13},{13,1},{2,6},{6,10},{... | collective-permute-start | bytes 589832 | tf_op jit(solution)/shard_map/ppermute | solution.py:38
  44.8 19.2 %collective-permute-start.3 = (f32[384,128]{1,0:T(8,128)S(1)}, f32[384,128]{1,0:T(8,128)S(1)}, u32[]{:S(2)}, u32[]{:S(2)}) collective-permute-start(f32[384,128]{1,0:T(8,128)S(1)} %get-tuple-element.34), channel_id=1, source_target_pairs={{0,12},{4,0},{8,4},{12,8},{1,13},{5,1},{9,5},{13,9},{2,14},{6,2},{... | collective-permute-start | bytes 589832 | tf_op jit(solution)/shard_map/ppermute | solution.py:38
  44.9 30.4 %collective-permute-start.4 = (f32[384,128]{1,0:T(8,128)S(1)}, f32[384,128]{1,0:T(8,128)S(1)}, u32[]{:S(2)}, u32[]{:S(2)}) collective-permute-start(f32[384,128]{1,0:T(8,128)S(1)} %get-tuple-element.35), channel_id=1, source_target_pairs={{0,8},{4,12},{8,0},{12,4},{1,9},{5,13},{9,1},{13,5},{2,10},{6,14},... | collective-permute-start | bytes 589832 | tf_op jit(solution)/shard_map/ppermute | solution.py:38
  49.6 25.7 %collective-permute-start.5 = (f32[384,128]{1,0:T(8,128)S(1)}, f32[384,128]{1,0:T(8,128)S(1)}, u32[]{:S(2)}, u32[]{:S(2)}) collective-permute-start(f32[384,128]{1,0:T(8,128)S(1)} %get-tuple-element.36), channel_id=1, source_target_pairs={{0,4},{4,8},{8,12},{12,0},{1,5},{5,9},{9,13},{13,1},{2,6},{6,10},{... | collective-permute-start | bytes 589832 | tf_op jit(solution)/shard_map/ppermute | solution.py:38
  57.4 20.4 %collective-permute-start.9 = (f32[384,128]{1,0:T(8,128)S(1)}, f32[384,128]{1,0:T(8,128)S(1)}, u32[]{:S(2)}, u32[]{:S(2)}) collective-permute-start(f32[384,128]{1,0:T(8,128)S(1)} %get-tuple-element.40), channel_id=1, source_target_pairs={{0,12},{4,0},{8,4},{12,8},{1,13},{5,1},{9,5},{13,9},{2,14},{6,2},{... | collective-permute-start | bytes 589832 | tf_op jit(solution)/shard_map/ppermute | solution.py:38
  59.3 21.5 %collective-permute-start.10 = (f32[384,128]{1,0:T(8,128)S(1)}, f32[384,128]{1,0:T(8,128)S(1)}, u32[]{:S(2)}, u32[]{:S(2)}) collective-permute-start(f32[384,128]{1,0:T(8,128)S(1)} %get-tuple-element.41), channel_id=1, source_target_pairs={{0,8},{4,12},{8,0},{12,4},{1,9},{5,13},{9,1},{13,5},{2,10},{6,14},... | collective-permute-start | bytes 589832 | tf_op jit(solution)/shard_map/ppermute | solution.py:38
  64.0 16.8 %collective-permute-start.11 = (f32[384,128]{1,0:T(8,128)S(1)}, f32[384,128]{1,0:T(8,128)S(1)}, u32[]{:S(2)}, u32[]{:S(2)}) collective-permute-start(f32[384,128]{1,0:T(8,128)S(1)} %get-tuple-element.42), channel_id=1, source_target_pairs={{0,4},{4,8},{8,12},{12,0},{1,5},{5,9},{9,13},{13,1},{2,6},{6,10},{... | collective-permute-start | bytes 589832 | tf_op jit(solution)/shard_map/ppermute | solution.py:38
  75.5 0.9 copy-start.5
  76.4 18.8 %collective-permute-start.13 = (f32[96,16,128]{2,1,0:T(8,128)S(1)}, f32[96,16,128]{2,1,0:T(8,128)S(1)}, u32[]{:S(2)}, u32[]{:S(2)}) collective-permute-start(f32[96,16,128]{2,1,0:T(8,128)S(1)} %get-tuple-element.46.refs_0_), channel_id=1, source_target_pairs={{0,2},{2,0},{1,3},{3,1},{4,6},{6,4},{5,7},{7,5},{8,10},{10,8},{9,1... | collective-permute-start | bytes 2359304 | tf_op jit(solution)/shard_map/ppermute | solution.py:42
  81.0 0.9 copy-start.7
  81.9 23.3 %collective-permute-start.16 = (f32[96,16,128]{2,1,0:T(8,128)S(1)}, f32[96,16,128]{2,1,0:T(8,128)S(1)}, u32[]{:S(2)}, u32[]{:S(2)}) collective-permute-start(f32[96,16,128]{2,1,0:T(8,128)S(1)} %get-tuple-element.47.refs_4_), channel_id=1, source_target_pairs={{0,2},{2,0},{1,3},{3,1},{4,6},{6,4},{5,7},{7,5},{8,10},{10,8},{9,1... | collective-permute-start | bytes 2359304 | tf_op jit(solution)/shard_map/ppermute | solution.py:42
  83.4 22.0 %collective-permute-start.12 = (f32[96,16,128]{2,1,0:T(8,128)S(1)}, f32[96,16,128]{2,1,0:T(8,128)}, u32[]{:S(2)}, u32[]{:S(2)}) collective-permute-start(f32[96,16,128]{2,1,0:T(8,128)S(1)} %get-tuple-element.46.refs_0_), channel_id=1, source_target_pairs={{0,1},{1,0},{2,3},{3,2},{4,5},{5,4},{6,7},{7,6},{8,9},{9,8},{10,11... | collective-permute-start | bytes 2359304 | tf_op jit(solution)/shard_map/ppermute | solution.py:42
  83.4 22.0 %collective-permute-start.15 = (f32[96,16,128]{2,1,0:T(8,128)S(1)}, f32[96,16,128]{2,1,0:T(8,128)}, u32[]{:S(2)}, u32[]{:S(2)}) collective-permute-start(f32[96,16,128]{2,1,0:T(8,128)S(1)} %get-tuple-element.47.refs_4_), channel_id=1, source_target_pairs={{0,1},{1,0},{2,3},{3,2},{4,5},{5,4},{6,7},{7,6},{8,9},{9,8},{10,11... | collective-permute-start | bytes 2359304 | tf_op jit(solution)/shard_map/ppermute | solution.py:42
  95.2 10.3 %collective-permute-start.14 = (f32[96,16,128]{2,1,0:T(8,128)S(1)}, f32[96,16,128]{2,1,0:T(8,128)}, u32[]{:S(2)}, u32[]{:S(2)}) collective-permute-start(f32[96,16,128]{2,1,0:T(8,128)S(1)} %collective-permute-done.13.refs_2_), channel_id=1, source_target_pairs={{0,1},{1,0},{2,3},{3,2},{4,5},{5,4},{6,7},{7,6},{8,9},{9,8},{10,11... | collective-permute-start | bytes 2359304 | tf_op jit(solution)/shard_map/ppermute | solution.py:42
  105.2 2.4 %collective-permute-start.17 = (f32[96,16,128]{2,1,0:T(8,128)S(1)}, f32[96,16,128]{2,1,0:T(8,128)}, u32[]{:S(2)}, u32[]{:S(2)}) collective-permute-start(f32[96,16,128]{2,1,0:T(8,128)S(1)} %collective-permute-done.16.refs_6_), channel_id=1, source_target_pairs={{0,1},{1,0},{2,3},{3,2},{4,5},{5,4},{6,7},{7,6},{8,9},{9,8},{10,11... | collective-permute-start | bytes 2359304 | tf_op jit(solution)/shard_map/ppermute | solution.py:42
  107.6 3.0 %copy-start.2 = (bf16[288,12288]{1,0:T(8,128)(2,1)S(1)}, bf16[288,12288]{1,0:T(8,128)(2,1)}, u32[]{:S(2)}) copy-start(bf16[288,12288]{1,0:T(8,128)(2,1)} %copy-done.1) | copy-start | bytes 21233668
  110.6 3.0 %copy-start.4 = (bf16[288,12288]{1,0:T(8,128)(2,1)S(1)}, bf16[288,12288]{1,0:T(8,128)(2,1)}, u32[]{:S(2)}) copy-start(bf16[288,12288]{1,0:T(8,128)(2,1)} %copy-done.3) | copy-start | bytes 21233668
  122.4 19.4 %copy-start.6 = (f32[16,96,128]{2,1,0:T(8,128)S(1)}, f32[16,96,128]{2,1,0:T(8,128)}, u32[]{:S(2)}) copy-start(f32[16,96,128]{2,1,0:T(8,128)} %copy-done.5) | copy-start | bytes 2359300
  122.4 19.4 %copy-start.8 = (f32[16,96,128]{2,1,0:T(8,128)S(1)}, f32[16,96,128]{2,1,0:T(8,128)}, u32[]{:S(2)}) copy-start(f32[16,96,128]{2,1,0:T(8,128)} %copy-done.7) | copy-start | bytes 2359300
  122.4 5.5 %collective-permute-start.18 = (f32[96,128]{1,0:T(8,128)S(1)}, f32[96,128]{1,0:T(8,128)S(1)}, u32[]{:S(2)}, u32[]{:S(2)}) collective-permute-start(f32[96,128]{1,0:T(8,128)S(1)} %get-tuple-element.61), channel_id=1, source_target_pairs={{0,12},{4,0},{8,4},{12,8},{1,13},{5,1},{9,5},{13,9},{2,14},{6,2},{... | collective-permute-start | bytes 147464 | tf_op jit(solution)/shard_map/ppermute | solution.py:38
  122.5 9.7 %collective-permute-start.19 = (f32[96,128]{1,0:T(8,128)S(1)}, f32[96,128]{1,0:T(8,128)S(1)}, u32[]{:S(2)}, u32[]{:S(2)}) collective-permute-start(f32[96,128]{1,0:T(8,128)S(1)} %get-tuple-element.60), channel_id=1, source_target_pairs={{0,4},{4,8},{8,12},{12,0},{1,5},{5,9},{9,13},{13,1},{2,6},{6,10},{... | collective-permute-start | bytes 147464 | tf_op jit(solution)/shard_map/ppermute | solution.py:38
  132.8 4.0 %collective-permute-start.20 = (f32[64,128]{1,0:T(8,128)S(1)}, f32[64,128]{1,0:T(8,128)S(1)}, u32[]{:S(2)}, u32[]{:S(2)}) collective-permute-start(f32[64,128]{1,0:T(8,128)S(1)} %get-tuple-element.51), channel_id=1, source_target_pairs={{0,2},{1,3},{2,0},{3,1},{4,6},{5,7},{6,4},{7,5},{8,10},{9,11},{10,... | collective-permute-start | bytes 98312 | tf_op jit(solution)/shard_map/ppermute | solution.py:42
  136.8 1.2 collective-permute-start.21
  138.0 3.7 %collective-permute-start.22 = (f32[32,128]{1,0:T(8,128)S(1)}, f32[32,128]{1,0:T(8,128)S(1)}, u32[]{:S(2)}, u32[]{:S(2)}) collective-permute-start(f32[32,128]{1,0:T(8,128)S(1)} %slice_add_fusion), channel_id=1, source_target_pairs={{0,4},{4,0},{8,12},{12,8},{1,5},{5,1},{9,13},{13,9},{2,6},{6,2},{1... | collective-permute-start | bytes 49160 | tf_op jit(solution)/shard_map/ppermute | solution.py:42
  141.8 4.6 %collective-permute-start.23 = (f32[32,128]{1,0:T(8,128)S(1)}, f32[32,128]{1,0:T(8,128)S(1)}, u32[]{:S(2)}, u32[]{:S(2)}) collective-permute-start(f32[32,128]{1,0:T(8,128)S(1)} %add.99), channel_id=1, source_target_pairs={{0,8},{4,12},{8,0},{12,4},{1,9},{5,13},{9,1},{13,5},{2,10},{6,14},... | collective-permute-start | bytes 49160 | tf_op jit(solution)/shard_map/ppermute | solution.py:42

commit v3 on v2

--- a/solution.py
+++ b/solution.py
@@ -38,6 +38,10 @@
     return lax.ppermute(x, "dom", [(i, (i - by) % size) for i in range(size)])
 
 
+def transposed(x):
+    return lax.all_to_all(x, "dom", split_axis=0, concat_axis=0, tiled=True)
+
+
 def swapped(x, axes, size, by):
     return lax.ppermute(x, axes, [(i, i ^ by) for i in range(size)])
 
@@ -45,8 +49,8 @@
 def filter_kernel(n_dom, planes, rows, first, *refs):
     refs = list(refs)
     given = None if first else refs.pop(0)
-    ins, outs = refs[:n_dom], refs[n_dom : 2 * n_dom]
-    refs = refs[2 * n_dom :]
+    ins, outs = refs[:2]
+    refs = refs[2:]
     diagonal = refs.pop(0) if first else given
     even, odd = refs
     half_planes = n_dom * planes // 2
@@ -59,10 +63,10 @@
             m, i = divmod(half * half_planes + x, planes)
             part = slice(half * TOGETHER, (half + 1) * TOGETHER)
             for y in range(rows):
-                even[x, y, part] = ins[m][pl.ds(i * rows + y, TOGETHER, stride=cells), :]
+                even[x, y, part] = ins[m, pl.ds(i * rows + y, TOGETHER, stride=cells), :]
                 if first:
                     at = TOGETHER * cells + i * rows + y
-                    level = ins[m][at : at + 1, :] + (SHIFT - CENTER_LEVEL)
+                    level = ins[m, at : at + 1, :] + (SHIFT - CENTER_LEVEL)
                     diagonal[x, y, part] = jnp.broadcast_to(
                         level * (2.0 * scale), (TOGETHER, lanes)
                     )
@@ -110,53 +114,47 @@
             half, x = divmod(m * planes + i, half_planes)
             for y in range(rows):
                 at = (i * rows + y) * TOGETHER
-                outs[m][at : at + TOGETHER, :] = even[
+                outs[m, at : at + TOGETHER, :] = even[
                     x, y, half * TOGETHER : (half + 1) * TOGETHER
                 ]
 
 
 def filter_orbitals(diagonal, blocks, planes, rows):
-    n_dom = len(blocks)
+    n_dom, _, lanes = blocks.shape
     first = diagonal is None
     cells = planes * rows
-    lanes = blocks[0].shape[1]
     field = (n_dom * planes // 2, rows, SUBLANES, lanes)
-    out = jax.ShapeDtypeStruct((cells * TOGETHER, lanes), jnp.float32)
+    out = jax.ShapeDtypeStruct((n_dom, cells * TOGETHER, lanes), jnp.float32)
     extra = [jax.ShapeDtypeStruct(field, jnp.float32)] if first else []
     given = [] if first else [diagonal]
     size = n_dom * cells * TOGETHER * lanes
     return pl.pallas_call(
         functools.partial(filter_kernel, n_dom, planes, rows, first),
-        out_shape=[out] * n_dom + extra,
-        in_specs=[VMEM] * (n_dom + len(given)),
-        out_specs=[VMEM] * (n_dom + len(extra)),
+        out_shape=[out] + extra,
+        in_specs=[VMEM] * (1 + len(given)),
+        out_specs=[VMEM] * (1 + len(extra)),
         scratch_shapes=[pltpu.VMEM(field, jnp.float32)] * 2,
-        compiler_params=params(12),
+        compiler_params=params(8),
         cost_estimate=pl.CostEstimate(
             flops=12 * DEGREE * size, bytes_accessed=8 * size, transcendentals=0
         ),
         name="chebyshev",
-    )(*given, *blocks)
-
-
-def assemble_kernel(me_ref, *refs):
-    *pieces, orbital_first, cell_first = refs
-    n_dom = len(pieces)
+    )(*given, blocks)
+
+
+def assemble_kernel(pieces, orbital_first, cell_first):
+    n_dom = pieces.shape[0]
     cells = cell_first.shape[0]
-    me = me_ref[0]
-    for m, piece in enumerate(pieces):
-        start = lax.rem(me + m, n_dom) * TOGETHER
+    for m in range(n_dom):
         for t in range(TOGETHER):
-            orbital_first[start + t] = piece[pl.ds(t, cells, stride=TOGETHER), :]
+            orbital_first[m * TOGETHER + t] = pieces[m, pl.ds(t, cells, stride=TOGETHER), :]
     for cell in range(cells):
         here = slice(cell * TOGETHER, (cell + 1) * TOGETHER)
-        tile = jnp.concatenate([piece[here, :] for piece in pieces], axis=0)
-        cell_first[cell] = pltpu.roll(tile, me * TOGETHER, 0)
-
-
-def assemble(me, pieces):
-    n_dom = len(pieces)
-    rows, lanes = pieces[0].shape
+        cell_first[cell] = jnp.concatenate([pieces[m, here, :] for m in range(n_dom)], axis=0)
+
+
+def assemble(pieces):
+    n_dom, rows, lanes = pieces.shape
     cells, orbitals = rows // TOGETHER, n_dom * TOGETHER
     return pl.pallas_call(
         assemble_kernel,
@@ -164,11 +162,11 @@
             jax.ShapeDtypeStruct((orbitals, cells, lanes), jnp.float32),
             jax.ShapeDtypeStruct((cells, orbitals, lanes), jnp.float32),
         ],
-        in_specs=[SMEM] + [VMEM] * n_dom,
+        in_specs=[VMEM],
         out_specs=[VMEM] * 2,
         compiler_params=params(8),
         name="assemble",
-    )(me.reshape(1), *pieces)
+    )(pieces)
 
 
 def projector_kernel(groups, group_ref, offsets_ref, coefs_ref, high_out, low_out):
@@ -223,7 +221,7 @@
         out_shape=[shape, shape],
         in_specs=[SMEM, VMEM, VMEM],
         out_specs=[VMEM, VMEM],
-        compiler_params=params(20),
+        compiler_params=params(12),
         cost_estimate=pl.CostEstimate(
             flops=4 * rows * cells * lanes * spread,
             bytes_accessed=8 * rows * cells * lanes,
@@ -233,54 +231,61 @@
     )(group, offsets, coefs)
 
 
-def product_kernel(n_chunks, w_high, w_low, *refs):
+def product_kernel(n_chunks, groups, group_ref, w_high, w_low, *refs):
     *fields, grid_out, proj_out = refs
     orbitals = grid_out.shape[0]
     cells, _, lanes = fields[0].shape
     n_groups = len(fields) // n_chunks
     block = 12
-    grid_out[...] = jnp.zeros_like(grid_out)
-    proj_out[...] = jnp.zeros_like(proj_out)
-
-    def one_block(step, carry):
+
+    def parts(start):
         highs, lows = [], []
         for g in range(n_groups):
             for c in range(n_chunks):
-                field = fields[c * n_groups + g][pl.ds(step * block, block)]
-                high, low = split_bf16(field)
+                high, low = split_bf16(fields[c * n_groups + g][pl.ds(start, block)])
                 highs.append(jnp.concatenate([high[k] for k in range(block)], axis=1))
                 lows.append(jnp.concatenate([low[k] for k in range(block)], axis=1))
-        high, low = jnp.concatenate(highs, axis=0), jnp.concatenate(lows, axis=0)
-        depth = block * lanes
-        part = pl.ds(pl.multiple_of(step * depth, depth), depth)
-        left_high = jnp.concatenate([high, w_high[:, part]], axis=0)
-        left_low = jnp.concatenate([low, w_low[:, part]], axis=0)
+        return jnp.concatenate(highs, axis=0), jnp.concatenate(lows, axis=0)
+
+    def product(left_high, left_low, high, low):
         right = jnp.concatenate([high, low], axis=0)
         wide = lax.dot_general(left_high, right, NT, preferred_element_type=jnp.float32)
         narrow = lax.dot_general(left_low, high, NT, preferred_element_type=jnp.float32)
-        total = wide[:, :orbitals] + wide[:, orbitals:] + narrow
-        grid_out[...] += total[:orbitals]
-        proj_out[...] += total[orbitals:]
+        return wide[:, :orbitals] + wide[:, orbitals:] + narrow
+
+    def grid_block(step, carry):
+        high, low = parts(group_ref[0] * (cells // groups) + step * block)
+        grid_out[...] += product(high, low, high, low)
         return carry
 
-    lax.fori_loop(0, cells // block, one_block, 0)
-
-
-def products(projectors, fields):
+    def proj_block(step, carry):
+        high, low = parts(step * block)
+        depth = block * lanes
+        here = pl.ds(pl.multiple_of(step * depth, depth), depth)
+        proj_out[...] += product(w_high[:, here], w_low[:, here], high, low)
+        return carry
+
+    grid_out[...] = jnp.zeros_like(grid_out)
+    proj_out[...] = jnp.zeros_like(proj_out)
+    lax.fori_loop(0, cells // (groups * block), grid_block, 0)
+    lax.fori_loop(0, cells // block, proj_block, 0)
+
+
+def products(groups, group, projectors, fields):
     rows = projectors[0].shape[0]
     n_chunks, n_groups = len(fields), len(fields[0])
     orbitals = n_chunks * n_groups * fields[0][0].shape[1]
     return pl.pallas_call(
-        functools.partial(product_kernel, n_chunks),
+        functools.partial(product_kernel, n_chunks, groups),
         out_shape=[
             jax.ShapeDtypeStruct((orbitals, orbitals), jnp.float32),
             jax.ShapeDtypeStruct((rows, orbitals), jnp.float32),
         ],
-        in_specs=[VMEM] * (2 + n_chunks * n_groups),
+        in_specs=[SMEM] + [VMEM] * (2 + n_chunks * n_groups),
         out_specs=[VMEM] * 2,
-        compiler_params=params(32),
+        compiler_params=params(12),
         name="products",
-    )(*projectors, *[field for chunk in fields for field in chunk])
+    )(group, *projectors, *[field for chunk in fields for field in chunk])
 
 
 def gram_kernel(
@@ -325,33 +330,27 @@
     )(group, proj, right, left, corr, grid_part)
 
 
-def whole_columns(panel, potential, me, projectors):
+def whole_columns(panel, potential, projectors):
     n_dom = lax.axis_size("dom")
     orbitals, planes, rows, lanes = panel.shape
     cells = planes * rows
-    flat = panel.reshape(orbitals * cells, lanes)
-    levels = potential.reshape(cells, lanes)
-    size = TOGETHER * cells
     n_chunks = orbitals // (n_dom * TOGETHER)
+    by_chunk = panel.reshape(n_chunks, n_dom, TOGETHER * cells, lanes)
+    levels = jnp.broadcast_to(potential.reshape(1, cells, lanes), (n_dom, cells, lanes))
     arrived = []
     for c in range(n_chunks):
-        blocks = []
-        for m in range(n_dom):
-            first = (c * n_dom + lax.rem(me - m + n_dom, n_dom)) * size
-            block = lax.dynamic_slice_in_dim(flat, first, size, 0)
-            if c == 0:
-                block = jnp.concatenate([block, levels], axis=0)
-            blocks.append(shifted(block, m) if m else block)
-        arrived.append(blocks)
+        blocks = by_chunk[c]
+        if c == 0:
+            blocks = jnp.concatenate([blocks, levels], axis=1)
+        arrived.append(transposed(blocks))
     arrived[0], projectors = lax.optimization_barrier((arrived[0], projectors))
     diagonal = None
     filtered, fields = [], []
     for blocks in arrived:
         done = filter_orbitals(diagonal, blocks, planes, rows)
         if diagonal is None:
-            diagonal = done[n_dom]
-        pieces = [shifted(done[(n_dom - m) % n_dom], m) if m else done[0] for m in range(n_dom)]
-        orbital_first, cell_first = assemble(me, pieces)
+            diagonal = done[1]
+        orbital_first, cell_first = assemble(transposed(done[0]))
         filtered.append(orbital_first)
         fields.append(cell_first)
     filtered = jnp.concatenate(filtered, axis=0).reshape(panel.shape)
@@ -385,7 +384,6 @@
     orbitals, planes, rows, lanes = panel.shape
     n_dom, n_band, n_sub = (lax.axis_size(axis) for axis in ("dom", "band", "sub"))
     groups = n_band * n_sub
-    me = lax.axis_index("dom")
     group = lax.axis_index(("band", "sub"))
     group_ref = group.reshape(1)
 
@@ -400,7 +398,7 @@
     )
 
     if orbitals % (n_dom * TOGETHER) == 0 and (n_dom * planes) % 2 == 0:
-        filtered, own_fields, projectors = whole_columns(panel, potential, me, projectors)
+        filtered, own_fields, projectors = whole_columns(panel, potential, projectors)
     else:
         filtered, own_fields = plane_by_plane(panel, potential)
     fields = []
@@ -411,11 +409,11 @@
             chunk += [over_band] + [swapped(over_band, "sub", n_sub, k) for k in range(1, n_sub)]
         fields.append(chunk)
 
-    grid_part, proj = products(projectors, fields)
+    grid_part, proj = products(groups, group_ref, projectors, fields)
     rows_atom = own_atoms * channels
     from_right = shifted(proj[:rows_atom], 1)
     from_left = shifted(proj[2 * rows_atom :], -1)
-    scale_point = 1.0 / (cells * lanes * n_dom * groups)
+    scale_point = 1.0 / (cells * lanes * n_dom)
     scale_atom = 1.0 / math.sqrt(point_offsets.shape[0] * n_dom)
     kept, sent = gram_share(
         (scale_point, scale_atom), groups, group_ref, proj, from_right, from_left, corr_matrix,

time: 147 us -> 163 us (1.11)
  blocking collectives: 0 us -> 30.6 us
  starting transfers between devices: 33.9 us -> 19.2 us
  waiting for transfers between devices: 64.9 us -> 62.9 us
    all_to_all x0 -> x1, blocking collectives: none -> 30.6 us  [transposed(): return lax.all_to_all(x, 'dom', split_axis=0, concat_axis=0, tiled=True)]
    all_to_all x0 -> x3, waiting for transfers between devices: none -> 29.3 us  [transposed(): return lax.all_to_all(x, 'dom', split_axis=0, concat_axis=0, tiled=True)]
    ppermute x14 -> x2, starting transfers between devices: 28.7 us -> 2.08 us  [shifted(): return lax.ppermute(x, 'dom', [(i, (i - by) % size) for i in range(size)])]
    ppermute x14 -> x2, waiting for transfers between devices: 30.8 us -> 4.25 us  [shifted(): return lax.ppermute(x, 'dom', [(i, (i - by) % size) for i in range(size)])]
    all_to_all x0 -> x3, starting transfers between devices: none -> 12 us  [transposed(): return lax.all_to_all(x, 'dom', split_axis=0, concat_axis=0, tiled=True)]
    ppermute x10, waiting for transfers between devices: 34.1 us -> 29.4 us  [swapped(): return lax.ppermute(x, axes, [(i, i ^ by) for i in range(size)])]
    slice x0 -> x1, local copies, waits for them, and re-layouts: none -> 2.41 us  [whole_columns(): blocks = by_chunk[c]]
    dynamic_slice x1 -> x0, local copies, waits for them, and re-layouts: 2.27 us -> none  [whole_columns(): block = lax.dynamic_slice_in_dim(flat, first, size, 0)]
  transfers between devices with their start and end apart: 24 -> 15, of which waited for: 12 -> 10; matrix products, arithmetic and copies ran while one was open for 1% -> 1% of each run, Pallas kernels for 13% -> 13%
where the time goes in v3:
time: 163 us; the launch traced here: 162 us
  waiting for transfers between devices  62.9 us (39%)
  blocking collectives  30.6 us (19%)
  Pallas kernels  30 us (18%)
  starting transfers between devices  19.2 us (12%)
  local copies, waits for them, and re-layouts  16.6 us (10%)
  other arithmetic  2.07 us (1%)
    all_to_all x1, blocking collectives, transposed(): return lax.all_to_all(x, 'dom', split_axis=0, concat_axis=0, tiled=True)  30.6 us
    ppermute x10, waiting for transfers between devices, swapped(): return lax.ppermute(x, axes, [(i, i ^ by) for i in range(size)])  29.4 us
    all_to_all x3, waiting for transfers between devices, transposed(): return lax.all_to_all(x, 'dom', split_axis=0, concat_axis=0, tiled=True)  29.3 us
    pallas_call x2, Pallas kernels, filter_orbitals(): pl.pallas_call(functools.partial(filter_kernel, n_dom, planes, rows, firs...  13.8 us
    unnamed x25, local copies, waits for them, and re-layouts  13.6 us
    all_to_all x3, starting transfers between devices, transposed(): return lax.all_to_all(x, 'dom', split_axis=0, concat_axis=0, tiled=True)  12 us
    pallas_call x1, Pallas kernels, products(): pl.pallas_call(functools.partial(product_kernel, n_chunks, groups), out_s...  8.17 us
    pallas_call x1, Pallas kernels, build_projectors(): pl.pallas_call(functools.partial(projector_kernel, groups), out_shape=[sh...  7.05 us
  transfers between devices with their start and end apart: 15, of which 10 were waited for; matrix products, arithmetic and copies ran while one was open for 1% of the time, Pallas kernels for 13%

profile of v3, /device:TPU:0, one launch (start us, length us, event | category | flops | bytes accessed | tf_op | source)
XLA Modules:
  0.0 162.2 jit_solution(7899753631907604360)
XLA Ops:
  0.6 0.0 copy-start
  0.6 0.0 copy-start.11
  0.7 2.4 %fusion.1 = (f32[16,3,32,128]{3,2,1,0:T(8,128)}, f32[16,3,32,128]{3,2,1,0:T(8,128)S(1)}) fusion(f32[32,3,32,128]{3,2,1,0:T(8,128)} %param.5), kind=kLoop, calls=%fused_computation.7 | loop fusion | bytes 3145728 | tf_op jit(solution)/shard_map/slice | solution.py:342
  3.1 0.0 copy-done.11
  3.1 0.1 pad_maximum_fusion.1
  3.2 0.0 copy-start.10
  3.2 0.0 copy-start.9
  3.2 30.6 %all_to_all.20.refs_0_ = f32[4,480,128]{2,1,0:T(8,128)S(1)} all-to-all(f32[4,480,128]{2,1,0:T(8,128)S(1)} %pad_maximum_fusion.1), channel_id=1, replica_groups=mesh['slab'=2,'dom'=4,'band'=2,'sub'=2] {'dom'}, dimensions={0} | all-to-all | bytes 1966080 | tf_op jit(solution)/shard_map/all_to_all | solution.py:42
  33.8 3.5 %all-to-all-start.2 = ((f32[4,384,128]{2,1,0:T(8,128)}), f32[4,384,128]{2,1,0:T(8,128)S(1)}, u32[]{:S(2)}, u32[]{:S(2)}) async-start(f32[4,384,128]{2,1,0:T(8,128)} %bitcast.3), calls=%async_computation.2 | async-start | bytes 1572864 | tf_op jit(solution)/shard_map/all_to_all | solution.py:42
  37.3 0.0 copy-done.10
  37.3 0.0 copy-done.9
  37.3 7.0 %projectors.1 = (bf16[288,12288]{1,0:T(8,128)(2,1)S(1)}, bf16[288,12288]{1,0:T(8,128)(2,1)S(1)}) custom-call(s32[1]{0:T(128)} %bitcast.2.group_ref, s32[48,3,128]{2,1,0:T(4,128)S(1)} %copy.9.offsets_ref, f32[48,3,8,128]{3,2,1,0:T(8,128)S(1)} %copy-done.9), custom_call_target="tpu_custom_call" | custom-call | flops 1811939328 | bytes 28311552 | tf_op jit(solution)/shard_map/projectors/pallas_call | solution.py:219
  44.4 0.0 copy-start.1
  44.4 2.9 %copy-done.1 = bf16[288,12288]{1,0:T(8,128)(2,1)} copy-done((bf16[288,12288]{1,0:T(8,128)(2,1)}, bf16[288,12288]{1,0:T(8,128)(2,1)S(1)}, u32[]{:S(2)}) %copy-start.1) | copy-done | bytes 7077912
  47.3 2.9 %copy-done.3 = bf16[288,12288]{1,0:T(8,128)(2,1)} copy-done((bf16[288,12288]{1,0:T(8,128)(2,1)}, bf16[288,12288]{1,0:T(8,128)(2,1)S(1)}, u32[]{:S(2)}) %copy-start.3) | copy-done | bytes 7077912
  50.2 7.1 %chebyshev.2 = (f32[4,384,128]{2,1,0:T(8,128)}, f32[6,32,8,128]{3,2,1,0:T(8,128)S(1)}) custom-call(f32[4,480,128]{2,1,0:T(8,128)S(1)} %all_to_all.20.refs_0_), custom_call_target="tpu_custom_call" | custom-call | flops 28311552 | bytes 1572864 | tf_op jit(solution)/shard_map/chebyshev/pallas_call | solution.py:131
  57.3 0.0 all-to-all-done.2.refs_1_
  57.3 5.0 %all-to-all-start.1 = ((f32[4,384,128]{2,1,0:T(8,128)}), f32[4,384,128]{2,1,0:T(8,128)S(1)}, u32[]{:S(2)}, u32[]{:S(2)}) async-start(f32[4,384,128]{2,1,0:T(8,128)} %get-tuple-element.20), calls=%async_computation.1 | async-start | bytes 1572864 | tf_op jit(solution)/shard_map/all_to_all | solution.py:42
  62.3 6.7 %chebyshev.3 = f32[4,384,128]{2,1,0:T(8,128)} custom-call(f32[6,32,8,128]{3,2,1,0:T(8,128)S(1)} %get-tuple-element.22.refs_0_, f32[4,384,128]{2,1,0:T(8,128)S(1)} %all-to-all-done.2.refs_1_), custom_call_target="tpu_custom_call" | custom-call | flops 28311552 | bytes 1572864 | tf_op jit(solution)/shard_map/chebyshev/pallas_call | solution.py:131
  69.1 12.3 %all-to-all-done.1.pieces = f32[4,384,128]{2,1,0:T(8,128)S(1)} async-done(((f32[4,384,128]{2,1,0:T(8,128)}), f32[4,384,128]{2,1,0:T(8,128)S(1)}, u32[]{:S(2)}, u32[]{:S(2)}) %all-to-all-start.1) | async-done | bytes 786464 | tf_op jit(solution)/shard_map/all_to_all | solution.py:42
  81.3 3.5 %all-to-all-start.3 = ((f32[4,384,128]{2,1,0:T(8,128)}), f32[4,384,128]{2,1,0:T(8,128)S(1)}, u32[]{:S(2)}, u32[]{:S(2)}) async-start(f32[4,384,128]{2,1,0:T(8,128)} %chebyshev.3), calls=%async_computation.3 | async-start | bytes 1572864 | tf_op jit(solution)/shard_map/all_to_all | solution.py:42
  84.8 0.2 assemble.2
  85.0 0.0 copy-start.5
  85.0 0.9 copy-done.5
  85.9 1.5 collective-permute-start.1
  87.4 17.0 %all-to-all-done.3.pieces = f32[4,384,128]{2,1,0:T(8,128)S(1)} async-done(((f32[4,384,128]{2,1,0:T(8,128)}), f32[4,384,128]{2,1,0:T(8,128)S(1)}, u32[]{:S(2)}, u32[]{:S(2)}) %all-to-all-start.3) | async-done | bytes 786464 | tf_op jit(solution)/shard_map/all_to_all | solution.py:42
  104.4 0.2 assemble.3
  104.6 0.0 copy-start.7
  104.6 0.9 copy-done.7
  105.4 1.5 collective-permute-start.4
  106.9 0.0 collective-permute-start
  106.9 0.5 collective-permute-start.3
  107.5 0.0 collective-permute-done.1.refs_2_
  107.5 0.0 collective-permute-start.2
  107.5 16.5 %collective-permute-done.4.refs_6_ = f32[96,16,128]{2,1,0:T(8,128)S(1)} collective-permute-done((f32[96,16,128]{2,1,0:T(8,128)S(1)}, f32[96,16,128]{2,1,0:T(8,128)S(1)}, u32[]{:S(2)}, u32[]{:S(2)}) %collective-permute-start.4) | collective-permute-done | bytes 786464 | tf_op jit(solution)/shard_map/ppermute | solution.py:46
  123.9 0.0 collective-permute-start.5
  123.9 0.0 copy-done
  123.9 0.1 constant_dynamic-slice_fusion
  124.0 0.1 copy.10
  124.1 0.0 collective-permute-done.refs_1_
  124.2 0.0 collective-permute-done.3.refs_5_
  124.2 0.0 collective-permute-done.2.refs_3_
  124.2 2.2 %collective-permute-done.5.refs_7_ = f32[96,16,128]{2,1,0:T(8,128)} collective-permute-done((f32[96,16,128]{2,1,0:T(8,128)S(1)}, f32[96,16,128]{2,1,0:T(8,128)}, u32[]{:S(2)}, u32[]{:S(2)}) %collective-permute-start.5) | collective-permute-done | bytes 786464 | tf_op jit(solution)/shard_map/ppermute | solution.py:46
  126.4 3.0 %copy-done.2 = bf16[288,12288]{1,0:T(8,128)(2,1)S(1)} copy-done((bf16[288,12288]{1,0:T(8,128)(2,1)S(1)}, bf16[288,12288]{1,0:T(8,128)(2,1)}, u32[]{:S(2)}) %copy-start.2) | copy-done | bytes 7077912
  129.4 3.0 %copy-done.4 = bf16[288,12288]{1,0:T(8,128)(2,1)S(1)} copy-done((bf16[288,12288]{1,0:T(8,128)(2,1)S(1)}, bf16[288,12288]{1,0:T(8,128)(2,1)}, u32[]{:S(2)}) %copy-start.4) | copy-done | bytes 7077912
  132.4 8.2 %products.1 = (f32[128,128]{1,0:T(8,128)S(1)}, f32[288,128]{1,0:T(8,128)S(1)}) custom-call(s32[1]{0:T(128)} %bitcast.2.group_ref, bf16[288,12288]{1,0:T(8,128)(2,1)S(1)} %copy-done.2, bf16[288,12288]{1,0:T(8,128)(2,1)S(1)} %copy-done.4, f32[96,16,128]{2,1,0:T(8,128)S(1)} %get-tuple-element.26.refs_0_, f32[96,16,128]{2,1,0:T(8,128)} %collective-permute-done.refs_1_, ...), custom_call_target="tpu_custom_call" | custom-call | tf_op jit(solution)/shard_map/products/pallas_call | solution.py:278
  140.6 0.0 copy-start.8
  140.6 0.9 collective-permute-start.6
  141.5 1.2 collective-permute-start.7
  142.7 0.1 broadcast_multiply_fusion
  142.8 0.3 mul.28.corr_ref
  143.1 1.6 %collective-permute-done.6.right_ref = f32[96,128]{1,0:T(8,128)S(1)} collective-permute-done((f32[96,128]{1,0:T(8,128)S(1)}, f32[96,128]{1,0:T(8,128)S(1)}, u32[]{:S(2)}, u32[]{:S(2)}) %collective-permute-start.6) | collective-permute-done | bytes 49184 | tf_op jit(solution)/shard_map/ppermute | solution.py:38
  144.7 2.6 %collective-permute-done.7.left_ref = f32[96,128]{1,0:T(8,128)S(1)} collective-permute-done((f32[96,128]{1,0:T(8,128)S(1)}, f32[96,128]{1,0:T(8,128)S(1)}, u32[]{:S(2)}, u32[]{:S(2)}) %collective-permute-start.7) | collective-permute-done | bytes 49184 | tf_op jit(solution)/shard_map/ppermute | solution.py:38
  147.3 0.6 gram_share.1
  147.9 1.6 collective-permute-start.8
  149.5 2.4 %collective-permute-done.8 = f32[64,128]{1,0:T(8,128)S(1)} collective-permute-done((f32[64,128]{1,0:T(8,128)S(1)}, f32[64,128]{1,0:T(8,128)S(1)}, u32[]{:S(2)}, u32[]{:S(2)}) %collective-permute-start.8) | collective-permute-done | bytes 32800 | tf_op jit(solution)/shard_map/ppermute | solution.py:46
  151.9 0.1 collective-permute-start.9
  152.0 1.2 collective-permute-done.9
  153.2 0.0 collective-permute-start.10
  153.2 3.7 %collective-permute-done.10 = f32[32,128]{1,0:T(8,128)S(1)} collective-permute-done((f32[32,128]{1,0:T(8,128)S(1)}, f32[32,128]{1,0:T(8,128)S(1)}, u32[]{:S(2)}, u32[]{:S(2)}) %collective-permute-start.10) | collective-permute-done | bytes 16416 | tf_op jit(solution)/shard_map/ppermute | solution.py:46
  156.9 0.0 collective-permute-start.11
  157.0 1.3 pad_maximum_fusion
  158.2 3.4 %collective-permute-done.11 = f32[32,128]{1,0:T(8,128)S(1)} collective-permute-done((f32[32,128]{1,0:T(8,128)S(1)}, f32[32,128]{1,0:T(8,128)S(1)}, u32[]{:S(2)}, u32[]{:S(2)}) %collective-permute-start.11) | collective-permute-done | bytes 16416 | tf_op jit(solution)/shard_map/ppermute | solution.py:46
  161.6 0.6 add.23
  (14 shorter events, 0.1 us)
Async XLA Ops:
  0.6 123.3 %copy-start = (f32[48,8,8]{0,2,1:T(8,128)S(1)}, f32[48,8,8]{0,2,1:T(8,128)}, u32[]{:S(2)}) copy-start(f32[48,8,8]{0,2,1:T(8,128)} %param.9) | copy-start | bytes 36868
  0.6 2.4 %copy-start.11 = (f32[3,32,128]{2,1,0:T(8,128)S(1)}, f32[3,32,128]{2,1,0:T(8,128)}, u32[]{:S(2)}) copy-start(f32[3,32,128]{2,1,0:T(8,128)} %param.6) | copy-start | bytes 147460
  3.2 34.1 %copy-start.10 = (s32[48,3,128]{2,0,1:T(8,128)S(1)}, s32[48,3,128]{2,0,1:T(8,128)}, u32[]{:S(2)}) copy-start(s32[48,3,128]{2,0,1:T(8,128)} %param.7) | copy-start | bytes 221188
  3.2 34.2 %copy-start.9 = (f32[48,3,8,128]{3,2,1,0:T(8,128)S(1)}, f32[48,3,8,128]{3,2,1,0:T(8,128)}, u32[]{:S(2)}) copy-start(f32[48,3,8,128]{3,2,1,0:T(8,128)} %coefs_ref.1) | copy-start | bytes 1769476
  33.8 23.6 %all-to-all-start.2 = ((f32[4,384,128]{2,1,0:T(8,128)}), f32[4,384,128]{2,1,0:T(8,128)S(1)}, u32[]{:S(2)}, u32[]{:S(2)}) async-start(f32[4,384,128]{2,1,0:T(8,128)} %bitcast.3), calls=%async_computation.2 | async-start | bytes 1572864 | tf_op jit(solution)/shard_map/all_to_all | solution.py:42
  44.4 2.9 %copy-start.1 = (bf16[288,12288]{1,0:T(8,128)(2,1)}, bf16[288,12288]{1,0:T(8,128)(2,1)S(1)}, u32[]{:S(2)}) copy-start(bf16[288,12288]{1,0:T(8,128)(2,1)S(1)} %get-tuple-element.24.w_high) | copy-start | bytes 21233668
  47.3 2.9 %copy-start.3 = (bf16[288,12288]{1,0:T(8,128)(2,1)}, bf16[288,12288]{1,0:T(8,128)(2,1)S(1)}, u32[]{:S(2)}) copy-start(bf16[288,12288]{1,0:T(8,128)(2,1)S(1)} %get-tuple-element.25.w_low) | copy-start | bytes 21233668
  57.3 24.0 %all-to-all-start.1 = ((f32[4,384,128]{2,1,0:T(8,128)}), f32[4,384,128]{2,1,0:T(8,128)S(1)}, u32[]{:S(2)}, u32[]{:S(2)}) async-start(f32[4,384,128]{2,1,0:T(8,128)} %get-tuple-element.20), calls=%async_computation.1 | async-start | bytes 1572864 | tf_op jit(solution)/shard_map/all_to_all | solution.py:42
  81.3 23.1 %all-to-all-start.3 = ((f32[4,384,128]{2,1,0:T(8,128)}), f32[4,384,128]{2,1,0:T(8,128)S(1)}, u32[]{:S(2)}, u32[]{:S(2)}) async-start(f32[4,384,128]{2,1,0:T(8,128)} %chebyshev.3), calls=%async_computation.3 | async-start | bytes 1572864 | tf_op jit(solution)/shard_map/all_to_all | solution.py:42
  85.0 0.9 copy-start.5
  85.9 21.6 %collective-permute-start.1 = (f32[96,16,128]{2,1,0:T(8,128)S(1)}, f32[96,16,128]{2,1,0:T(8,128)S(1)}, u32[]{:S(2)}, u32[]{:S(2)}) collective-permute-start(f32[96,16,128]{2,1,0:T(8,128)S(1)} %get-tuple-element.26.refs_0_), channel_id=1, source_target_pairs={{0,2},{2,0},{1,3},{3,1},{4,6},{6,4},{5,7},{7,5},{8,10},{10,8},{9,1... | collective-permute-start | bytes 2359304 | tf_op jit(solution)/shard_map/ppermute | solution.py:46
  104.6 0.9 copy-start.7
  105.4 18.5 %collective-permute-start.4 = (f32[96,16,128]{2,1,0:T(8,128)S(1)}, f32[96,16,128]{2,1,0:T(8,128)S(1)}, u32[]{:S(2)}, u32[]{:S(2)}) collective-permute-start(f32[96,16,128]{2,1,0:T(8,128)S(1)} %get-tuple-element.27.refs_4_), channel_id=1, source_target_pairs={{0,2},{2,0},{1,3},{3,1},{4,6},{6,4},{5,7},{7,5},{8,10},{10,8},{9,1... | collective-permute-start | bytes 2359304 | tf_op jit(solution)/shard_map/ppermute | solution.py:46
  106.9 17.2 %collective-permute-start = (f32[96,16,128]{2,1,0:T(8,128)S(1)}, f32[96,16,128]{2,1,0:T(8,128)}, u32[]{:S(2)}, u32[]{:S(2)}) collective-permute-start(f32[96,16,128]{2,1,0:T(8,128)S(1)} %get-tuple-element.26.refs_0_), channel_id=1, source_target_pairs={{0,1},{1,0},{2,3},{3,2},{4,5},{5,4},{6,7},{7,6},{8,9},{9,8},{10,11... | collective-permute-start | bytes 2359304 | tf_op jit(solution)/shard_map/ppermute | solution.py:46
  106.9 17.2 %collective-permute-start.3 = (f32[96,16,128]{2,1,0:T(8,128)S(1)}, f32[96,16,128]{2,1,0:T(8,128)}, u32[]{:S(2)}, u32[]{:S(2)}) collective-permute-start(f32[96,16,128]{2,1,0:T(8,128)S(1)} %get-tuple-element.27.refs_4_), channel_id=1, source_target_pairs={{0,1},{1,0},{2,3},{3,2},{4,5},{5,4},{6,7},{7,6},{8,9},{9,8},{10,11... | collective-permute-start | bytes 2359304 | tf_op jit(solution)/shard_map/ppermute | solution.py:46
  107.5 16.7 %collective-permute-start.2 = (f32[96,16,128]{2,1,0:T(8,128)S(1)}, f32[96,16,128]{2,1,0:T(8,128)}, u32[]{:S(2)}, u32[]{:S(2)}) collective-permute-start(f32[96,16,128]{2,1,0:T(8,128)S(1)} %collective-permute-done.1.refs_2_), channel_id=1, source_target_pairs={{0,1},{1,0},{2,3},{3,2},{4,5},{5,4},{6,7},{7,6},{8,9},{9,8},{10,11... | collective-permute-start | bytes 2359304 | tf_op jit(solution)/shard_map/ppermute | solution.py:46
  123.9 2.4 %collective-permute-start.5 = (f32[96,16,128]{2,1,0:T(8,128)S(1)}, f32[96,16,128]{2,1,0:T(8,128)}, u32[]{:S(2)}, u32[]{:S(2)}) collective-permute-start(f32[96,16,128]{2,1,0:T(8,128)S(1)} %collective-permute-done.4.refs_6_), channel_id=1, source_target_pairs={{0,1},{1,0},{2,3},{3,2},{4,5},{5,4},{6,7},{7,6},{8,9},{9,8},{10,11... | collective-permute-start | bytes 2359304 | tf_op jit(solution)/shard_map/ppermute | solution.py:46
  126.4 3.0 %copy-start.2 = (bf16[288,12288]{1,0:T(8,128)(2,1)S(1)}, bf16[288,12288]{1,0:T(8,128)(2,1)}, u32[]{:S(2)}) copy-start(bf16[288,12288]{1,0:T(8,128)(2,1)} %copy-done.1) | copy-start | bytes 21233668
  129.4 3.0 %copy-start.4 = (bf16[288,12288]{1,0:T(8,128)(2,1)S(1)}, bf16[288,12288]{1,0:T(8,128)(2,1)}, u32[]{:S(2)}) copy-start(bf16[288,12288]{1,0:T(8,128)(2,1)} %copy-done.3) | copy-start | bytes 21233668
  140.6 16.4 %copy-start.6 = (f32[16,96,128]{2,1,0:T(8,128)S(1)}, f32[16,96,128]{2,1,0:T(8,128)}, u32[]{:S(2)}) copy-start(f32[16,96,128]{2,1,0:T(8,128)} %copy-done.5) | copy-start | bytes 2359300
  140.6 16.4 %copy-start.8 = (f32[16,96,128]{2,1,0:T(8,128)S(1)}, f32[16,96,128]{2,1,0:T(8,128)}, u32[]{:S(2)}) copy-start(f32[16,96,128]{2,1,0:T(8,128)} %copy-done.7) | copy-start | bytes 2359300
  140.6 4.1 %collective-permute-start.6 = (f32[96,128]{1,0:T(8,128)S(1)}, f32[96,128]{1,0:T(8,128)S(1)}, u32[]{:S(2)}, u32[]{:S(2)}) collective-permute-start(f32[96,128]{1,0:T(8,128)S(1)} %get-tuple-element.35), channel_id=1, source_target_pairs={{0,12},{4,0},{8,4},{12,8},{1,13},{5,1},{9,5},{13,9},{2,14},{6,2},{... | collective-permute-start | bytes 147464 | tf_op jit(solution)/shard_map/ppermute | solution.py:38
  141.5 5.9 %collective-permute-start.7 = (f32[96,128]{1,0:T(8,128)S(1)}, f32[96,128]{1,0:T(8,128)S(1)}, u32[]{:S(2)}, u32[]{:S(2)}) collective-permute-start(f32[96,128]{1,0:T(8,128)S(1)} %get-tuple-element.34), channel_id=1, source_target_pairs={{0,4},{4,8},{8,12},{12,0},{1,5},{5,9},{9,13},{13,1},{2,6},{6,10},{... | collective-permute-start | bytes 147464 | tf_op jit(solution)/shard_map/ppermute | solution.py:38
  147.9 4.0 %collective-permute-start.8 = (f32[64,128]{1,0:T(8,128)S(1)}, f32[64,128]{1,0:T(8,128)S(1)}, u32[]{:S(2)}, u32[]{:S(2)}) collective-permute-start(f32[64,128]{1,0:T(8,128)S(1)} %get-tuple-element.31), channel_id=1, source_target_pairs={{0,2},{1,3},{2,0},{3,1},{4,6},{5,7},{6,4},{7,5},{8,10},{9,11},{10,... | collective-permute-start | bytes 98312 | tf_op jit(solution)/shard_map/ppermute | solution.py:46
  151.9 1.2 collective-permute-start.9
  153.2 3.7 %collective-permute-start.10 = (f32[32,128]{1,0:T(8,128)S(1)}, f32[32,128]{1,0:T(8,128)S(1)}, u32[]{:S(2)}, u32[]{:S(2)}) collective-permute-start(f32[32,128]{1,0:T(8,128)S(1)} %slice_add_fusion), channel_id=1, source_target_pairs={{0,4},{4,0},{8,12},{12,8},{1,5},{5,1},{9,13},{13,9},{2,6},{6,2},{1... | collective-permute-start | bytes 49160 | tf_op jit(solution)/shard_map/ppermute | solution.py:46
  156.9 4.6 %collective-permute-start.11 = (f32[32,128]{1,0:T(8,128)S(1)}, f32[32,128]{1,0:T(8,128)S(1)}, u32[]{:S(2)}, u32[]{:S(2)}) collective-permute-start(f32[32,128]{1,0:T(8,128)S(1)} %add.22), channel_id=1, source_target_pairs={{0,8},{4,12},{8,0},{12,4},{1,9},{5,13},{9,1},{13,5},{2,10},{6,14},... | collective-permute-start | bytes 49160 | tf_op jit(solution)/shard_map/ppermute | solution.py:46

commit v4 on v3

v4 whole, which is shorter than its diff:
```python
import functools
import math

import jax
import jax.numpy as jnp
from jax import lax
from jax.experimental import pallas as pl
from jax.experimental.pallas import tpu as pltpu
from jax.sharding import PartitionSpec as P

DEGREE = 12

CENTER_LEVEL = 3.6
HALF_WIDTH = 3.4
SHIFT = 3.0

TOGETHER = 4
SUBLANES = 8
MIB = 1024 * 1024

VMEM = pl.BlockSpec(memory_space=pltpu.VMEM)
SMEM = pl.BlockSpec(memory_space=pltpu.SMEM)
NT = (((1,), (1,)), ((), ()))
TN = (((0,), (0,)), ((), ()))


def params(mib):
    return pltpu.CompilerParams(vmem_limit_bytes=mib * MIB)


def split_bf16(x):
    high = x.astype(jnp.bfloat16)
    return high, (x - high.astype(jnp.float32)).astype(jnp.bfloat16)


def shifted(x, by):
    size = lax.axis_size("dom")
    return lax.ppermute(x, "dom", [(i, (i - by) % size) for i in range(size)])


def swapped(x, axes, size, by):
    return lax.ppermute(x, axes, [(i, i ^ by) for i in range(size)])


def filter_kernel(n_dom, planes, rows, starts, first, me_ref, *refs):
    refs = list(refs)
    given = None if first else refs.pop(0)
    ins, outs = refs[:n_dom], refs[n_dom : 2 * n_dom]
    refs = refs[2 * n_dom :]
    diagonal = refs.pop(0) if first else given
    even, odd = refs
    half_planes = n_dom * planes // 2
    cells = planes * rows
    lanes = even.shape[3]
    scale = 1.0 / HALF_WIDTH
    mirrored = (me_ref[0] & 1) != 0
    plane_at = [jnp.where(mirrored, planes - 1 - i, i) for i in range(planes)]

    for x in range(half_planes):
        for half in range(2):
            m, i = divmod(half * half_planes + x, planes)
            part = slice(half * TOGETHER, (half + 1) * TOGETHER)
            base = starts[m] + plane_at[i] * rows
            for y in range(rows):
                even[x, y, part] = ins[m][pl.ds(base + y, TOGETHER, stride=cells), :]
                if first:
                    level = ins[m][pl.ds(base + (TOGETHER * cells + y), 1), :]
                    diagonal[x, y, part] = jnp.broadcast_to(
                        (level + (SHIFT - CENTER_LEVEL)) * (2.0 * scale), (TOGETHER, lanes)
                    )

    block = SUBLANES
    lane = lax.broadcasted_iota(jnp.int32, (block, SUBLANES, lanes), 2)
    at_start, at_end = lane == 0, lane == lanes - 1

    def twice_operator(source, x, y):
        here = slice(y, y + block)
        centre = source[x, here]
        if x == 0:
            near = pltpu.roll(source[half_planes - 1, here], TOGETHER, 1) + source[x + 1, here]
        elif x == half_planes - 1:
            near = pltpu.roll(source[0, here], TOGETHER, 1) + source[x - 1, here]
        else:
            near = source[x - 1, here] + source[x + 1, here]
        before = (y - 1) % rows
        after = (y + block) % rows
        near += jnp.concatenate([source[x, before : before + 1], centre[:-1]], axis=0)
        near += jnp.concatenate([centre[1:], source[x, after : after + 1]], axis=0)
        low = pltpu.roll(centre, 1, 2)
        high = pltpu.roll(centre, lanes - 1, 2)
        near += jnp.where(at_start, high, jnp.where(at_end, low, low + high))
        return diagonal[x, here] * centre - scale * near

    places = [(x, y) for x in range(half_planes) for y in range(0, rows, block)]

    def next_field(source, target):
        for x, y in places:
            target[x, y : y + block] = twice_operator(source, x, y) - target[x, y : y + block]

    for x, y in places:
        odd[x, y : y + block] = 0.5 * twice_operator(even, x, y)
    next_field(odd, even)

    def two_steps(_, carry):
        next_field(even, odd)
        next_field(odd, even)
        return carry

    lax.fori_loop(0, DEGREE // 2 - 1, two_steps, 0)
    for m in range(n_dom):
        for i in range(planes):
            half, x = divmod(m * planes + i, half_planes)
            part = slice(half * TOGETHER, (half + 1) * TOGETHER)
            for y in range(rows):
                here = slice(y * TOGETHER, (y + 1) * TOGETHER)
                outs[m][plane_at[i], here, :] = even[x, y, part]


def filter_orbitals(me, diagonal, blocks, starts, planes, rows):
    n_dom = len(blocks)
    first = diagonal is None
    lanes = blocks[0].shape[1]
    field = (n_dom * planes // 2, rows, SUBLANES, lanes)
    out = jax.ShapeDtypeStruct((planes, rows * TOGETHER, lanes), jnp.float32)
    extra = [jax.ShapeDtypeStruct(field, jnp.float32)] if first else []
    given = [] if first else [diagonal]
    size = n_dom * planes * rows * TOGETHER * lanes
    return pl.pallas_call(
        functools.partial(filter_kernel, n_dom, planes, rows, starts, first),
        out_shape=[out] * n_dom + extra,
        in_specs=[SMEM] + [VMEM] * (n_dom + len(given)),
        out_specs=[VMEM] * (n_dom + len(extra)),
        scratch_shapes=[pltpu.VMEM(field, jnp.float32)] * 2,
        compiler_params=params(8),
        cost_estimate=pl.CostEstimate(
            flops=12 * DEGREE * size, bytes_accessed=8 * size, transcendentals=0
        ),
        name="chebyshev",
    )(me, *given, *blocks)


def assemble_kernel(n_dom, n_band, me_ref, band_ref, *refs):
    pieces, orbital_first, parts = refs[:n_dom], refs[n_dom], refs[n_dom + 1 :]
    cells = orbital_first.shape[1]
    share = cells // n_band
    me = me_ref[0]
    for m, piece in enumerate(pieces):
        start = (me ^ m) * TOGETHER
        for t in range(TOGETHER):
            orbital_first[start + t] = piece[pl.ds(t, cells, stride=TOGETHER), :]
    per_load = SUBLANES // TOGETHER
    together = SUBLANES // TOGETHER
    for p, part in enumerate(parts):
        base = pl.multiple_of((band_ref[0] ^ p) * (share * TOGETHER), SUBLANES)
        for first in range(0, share, per_load):
            loaded = [
                piece[pl.ds(base + first * TOGETHER, SUBLANES), :] for piece in pieces
            ]
            for k in range(per_load):
                here = slice(k * TOGETHER, (k + 1) * TOGETHER)
                for q in range(n_dom // together):
                    tile = jnp.concatenate(
                        [loaded[q * together + i][here] for i in range(together)], axis=0
                    )
                    tile = jnp.where((me & 1) != 0, pltpu.roll(tile, TOGETHER, 0), tile)
                    row = pl.multiple_of((q ^ (me // together)) * SUBLANES, SUBLANES)
                    part[first + k, pl.ds(row, SUBLANES), :] = tile


def assemble(me, band, n_band, pieces):
    n_dom = len(pieces)
    planes, rows, lanes = pieces[0].shape
    cells, orbitals = planes * rows // TOGETHER, n_dom * TOGETHER
    part = jax.ShapeDtypeStruct((cells // n_band, orbitals, lanes), jnp.float32)
    return pl.pallas_call(
        functools.partial(assemble_kernel, n_dom, n_band),
        out_shape=[jax.ShapeDtypeStruct((orbitals, cells, lanes), jnp.float32)] + [part] * n_band,
        in_specs=[SMEM] * 2 + [VMEM] * n_dom,
        out_specs=[VMEM] * (1 + n_band),
        compiler_params=params(8),
        name="assemble",
    )(me, band, *[piece.reshape(planes * rows, lanes) for piece in pieces])


def projector_kernel(n_band, n_sub, band_ref, sub_ref, offsets_ref, coefs_ref, high_out, low_out):
    atoms, shells, channels, spread = coefs_ref.shape
    own = atoms // (n_band * n_sub)
    lanes = spread
    cells = high_out.shape[1] // lanes
    pairs = own // 2
    row_index = lax.broadcasted_iota(jnp.int32, (cells, channels, spread), 0)
    row_index += band_ref[0] * cells
    lane_index = lax.broadcasted_iota(jnp.int32, (lanes, spread), 0)

    def two_atoms(step, carry):
        shell = step // (n_band * pairs)
        band = band_ref[0] ^ ((step // pairs) % n_band)
        first_atom = (sub_ref[0] * n_band + band) * own + 2 * (step % pairs)
        dense = []
        for i in range(2):
            offsets = offsets_ref[first_atom + i, pl.ds(shell, 1), :]
            coefs = coefs_ref[first_atom + i, shell]
            at_row = row_index == (offsets // lanes)[None]
            at_row &= (offsets >= 0)[None]
            left = [
                jnp.where(at_row, part.astype(jnp.float32)[None], 0.0)
                .reshape(cells * channels, spread)
                .astype(jnp.bfloat16)
                for part in split_bf16(coefs)
            ]
            at_lane = jnp.where(lane_index == (offsets & (lanes - 1)), 1.0, 0.0)
            at_lane = at_lane.astype(jnp.bfloat16)
            values = lax.dot_general(
                jnp.concatenate(left, axis=1),
                jnp.concatenate([at_lane, at_lane], axis=1),
                NT,
                preferred_element_type=jnp.float32,
            )
            dense.append(values.reshape(cells, channels, lanes))
        high, low = split_bf16(jnp.concatenate(dense, axis=1))
        rows = pl.ds(pl.multiple_of(step * 2 * channels, 2 * channels), 2 * channels)
        for cell in range(cells):
            high_out[rows, cell * lanes : (cell + 1) * lanes] = high[cell]
            low_out[rows, cell * lanes : (cell + 1) * lanes] = low[cell]
        return carry

    lax.fori_loop(0, shells * n_band * pairs, two_atoms, 0)


def build_projectors(n_band, n_sub, band, sub, offsets, coefs, cells, lanes):
    atoms, shells, channels, spread = coefs.shape
    rows = atoms // n_sub * shells * channels
    shape = jax.ShapeDtypeStruct((rows, cells * lanes), jnp.bfloat16)
    return pl.pallas_call(
        functools.partial(projector_kernel, n_band, n_sub),
        out_shape=[shape, shape],
        in_specs=[SMEM, SMEM, VMEM, VMEM],
        out_specs=[VMEM, VMEM],
        compiler_params=params(8),
        cost_estimate=pl.CostEstimate(
            flops=4 * rows * cells * lanes * spread,
            bytes_accessed=8 * rows * cells * lanes,
            transcendentals=0,
        ),
        name="projectors",
    )(band, sub, offsets, coefs)


def product_kernel(n_chunks, n_sub, sub_ref, w_high, w_low, *refs):
    *fields, grid_out, proj_out = refs
    orbitals = grid_out.shape[0]
    cells, _, lanes = fields[0].shape
    n_groups = len(fields) // n_chunks
    block = 12

    def parts(start):
        highs, lows = [], []
        for g in range(n_groups):
            for c in range(n_chunks):
                high, low = split_bf16(fields[c * n_groups + g][pl.ds(start, block)])
                highs.append(jnp.concatenate([high[k] for k in range(block)], axis=1))
                lows.append(jnp.concatenate([low[k] for k in range(block)], axis=1))
        return jnp.concatenate(highs, axis=0), jnp.concatenate(lows, axis=0)

    def product(left_high, left_low, high, low):
        right = jnp.concatenate([high, low], axis=0)
        wide = lax.dot_general(left_high, right, NT, preferred_element_type=jnp.float32)
        narrow = lax.dot_general(left_low, high, NT, preferred_element_type=jnp.float32)
        return wide[:, :orbitals] + wide[:, orbitals:] + narrow

    def grid_block(step, carry):
        high, low = parts(sub_ref[0] * (cells // n_sub) + step * block)
        grid_out[...] += product(high, low, high, low)
        return carry

    def proj_block(step, carry):
        high, low = parts(step * block)
        depth = block * lanes
        here = pl.ds(pl.multiple_of(step * depth, depth), depth)
        proj_out[...] += product(w_high[:, here], w_low[:, here], high, low)
        return carry

    grid_out[...] = jnp.zeros_like(grid_out)
    proj_out[...] = jnp.zeros_like(proj_out)
    lax.fori_loop(0, cells // (n_sub * block), grid_block, 0)
    lax.fori_loop(0, cells // block, proj_block, 0)


def products(n_sub, sub, projectors, fields):
    rows = projectors[0].shape[0]
    n_chunks, n_groups = len(fields), len(fields[0])
    orbitals = n_chunks * n_groups * fields[0][0].shape[1]
    return pl.pallas_call(
        functools.partial(product_kernel, n_chunks, n_sub),
        out_shape=[
            jax.ShapeDtypeStruct((orbitals, orbitals), jnp.float32),
            jax.ShapeDtypeStruct((rows, orbitals), jnp.float32),
        ],
        in_specs=[SMEM] + [VMEM] * (2 + n_chunks * n_groups),
        out_specs=[VMEM] * 2,
        compiler_params=params(12),
        name="products",
    )(sub, *projectors, *[field for chunk in fields for field in chunk])


def reordered(x, width, by):
    span = width * by
    column = lax.broadcasted_iota(jnp.int32, x.shape, 1)
    up, down = pltpu.roll(x, span, 1), pltpu.roll(x, x.shape[1] - span, 1)
    return jnp.where((column & span) == 0, down, up)


def gram_kernel(scales, groups, seen, own_row, group_ref, corr_ref, grid_ref, proj_ref, *refs):
    *sums, kept, sent = refs
    orbitals = grid_ref.shape[0]
    width = orbitals // groups
    bits = [1 << k for k in range(groups.bit_length() - 1)]
    projections = proj_ref[own_row : own_row + corr_ref.shape[0], :]
    for part, by in zip(sums, seen):
        columns = part[...]
        for bit in bits:
            if by & bit:
                columns = reordered(columns, width, bit)
        projections += columns
    highest = lax.Precision.HIGHEST
    weighted = jnp.dot(
        corr_ref[...], projections, precision=highest, preferred_element_type=jnp.float32
    )
    atom_part = lax.dot_general(
        projections, weighted, TN, precision=highest, preferred_element_type=jnp.float32
    )
    share = grid_ref[...] * scales[0] + atom_part * scales[1]
    for bit in bits:
        share = jnp.where((group_ref[0] & bit) != 0, reordered(share, width, bit), share)
    kept[...] = share[: orbitals // 2]
    sent[...] = share[orbitals // 2 :]


def gram_share(scales, groups, seen, own_row, group, corr, grid_part, proj, sums):
    half = jax.ShapeDtypeStruct((grid_part.shape[0] // 2, grid_part.shape[1]), jnp.float32)
    return pl.pallas_call(
        functools.partial(gram_kernel, scales, groups, seen, own_row),
        out_shape=[half, half],
        in_specs=[SMEM] + [VMEM] * (3 + len(sums)),
        out_specs=[VMEM] * 2,
        compiler_params=params(8),
        name="gram_share",
    )(group, corr, grid_part, proj, *sums)


def whole_columns(panel, potential, me, band):
    n_dom, n_band = lax.axis_size("dom"), lax.axis_size("band")
    orbitals, planes, rows, lanes = panel.shape
    cells = planes * rows
    flat = panel.reshape(orbitals * cells, lanes)
    levels = potential.reshape(cells, lanes)
    size = TOGETHER * cells
    n_chunks = orbitals // (n_dom * TOGETHER)
    own = []
    for m in range(n_dom):
        blocks = [
            lax.dynamic_slice_in_dim(flat, (c * n_dom + (me ^ m)) * size, size, 0)
            for c in range(n_chunks)
        ]
        blocks[0] = jnp.concatenate([blocks[0], levels], axis=0)
        own.append(blocks)
    near = swapped(jnp.concatenate(own[1], axis=0), "dom", n_dom, 1)
    arrived = [
        [own[0][c], near] + [swapped(own[m][c], "dom", n_dom, m) for m in range(2, n_dom)]
        for c in range(1)
    ]
    for c in range(1, n_chunks):
        far = [own[m][c] for m in range(2, n_dom)]
        near, far = lax.optimization_barrier((near, far))
        arrived.append(
            [own[0][c], near]
            + [swapped(b, "dom", n_dom, m) for m, b in enumerate(far, start=2)]
        )
    diagonal = None
    done = []
    for c, blocks in enumerate(arrived):
        starts = [0] * n_dom
        starts[1] = c * size + (cells if c else 0)
        filtered = filter_orbitals(me.reshape(1), diagonal, blocks, starts, planes, rows)
        if diagonal is None:
            diagonal = filtered[n_dom]
        done.append(filtered[:n_dom])
    return [
        [swapped(b, "dom", n_dom, m) if m else b for m, b in enumerate(blocks)] for blocks in done
    ]


def plane_by_plane(panel, potential):
    n_dom = lax.axis_size("dom")
    diagonal = (potential + (SHIFT - CENTER_LEVEL)) * (2.0 / HALF_WIDTH)

    def twice_operator(field):
        low, high = shifted(field[:, -1:], -1), shifted(field[:, :1], 1)
        extended = jnp.concatenate([low, field, high], axis=1)
        near = extended[:, 2:] + extended[:, :-2]
        near += jnp.roll(field, 1, axis=2) + jnp.roll(field, -1, axis=2)
        padded = jnp.pad(field, ((0, 0), (0, 0), (0, 0), (1, 1)))
        near += padded[..., 2:] + padded[..., :-2]
        return diagonal * field - near / HALF_WIDTH

    def one_step(_, carry):
        before, current = carry
        return current, twice_operator(current) - before

    start = (panel, 0.5 * twice_operator(panel))
    return lax.fori_loop(0, DEGREE - 1, one_step, start)[1]


def on_device(panel, potential, point_offsets, point_coefs, correlation):
    orbitals, planes, rows, lanes = panel.shape
    n_dom, n_band, n_sub = (lax.axis_size(axis) for axis in ("dom", "band", "sub"))
    groups = n_band * n_sub
    me, band, sub = (lax.axis_index(axis) for axis in ("dom", "band", "sub"))
    group = band * n_sub + sub

    cells = planes * rows
    share = cells // n_band
    channels = correlation.shape[1]
    own_atoms = point_offsets.shape[0] // groups
    own_corr = lax.dynamic_slice_in_dim(
        correlation, (sub * n_band + band) * own_atoms, own_atoms, 0
    )
    same_atom = jnp.eye(own_atoms, dtype=jnp.float32)
    corr_matrix = (same_atom[:, None, :, None] * own_corr[:, :, None, :]).reshape(
        own_atoms * channels, own_atoms * channels
    )

    def build(offsets):
        return build_projectors(
            n_band, n_sub, band.reshape(1), sub.reshape(1), offsets, point_coefs, share, lanes
        )

    filtered, parts = [], []
    if n_dom in (2, 4) and orbitals % (n_dom * TOGETHER) == 0 and planes * n_dom % 2 == 0:
        chunks = whole_columns(panel, potential, me, band)
        chunks[-1][0], point_offsets = lax.optimization_barrier((chunks[-1][0], point_offsets))
        projectors = build(point_offsets)
        chunks[0], projectors = lax.optimization_barrier((chunks[0], projectors))
        for pieces in chunks:
            orbital_first, *by_band = assemble(me.reshape(1), band.reshape(1), n_band, pieces)
            filtered.append(orbital_first)
            parts.append(by_band)
    else:
        projectors = build(point_offsets)
        filtered = [plane_by_plane(panel, potential)]
        cell_first = filtered[0].reshape(orbitals, cells, lanes).swapaxes(0, 1)
        parts = [
            [
                lax.dynamic_slice_in_dim(cell_first, (band ^ m) * share, share, 0)
                for m in range(n_band)
            ]
        ]
    filtered = jnp.concatenate(filtered, axis=0).reshape(panel.shape)
    fields = []
    for by_band in parts:
        chunk = []
        for m in range(n_band):
            here = swapped(by_band[m], "band", n_band, m) if m else by_band[0]
            chunk += [here] + [swapped(here, "sub", n_sub, k) for k in range(1, n_sub)]
        fields.append(chunk)

    grid_part, proj = products(n_sub, sub.reshape(1), projectors, fields)
    rows_atom = own_atoms * channels
    sums, seen = [], []
    for shell, by in ((1, 0), (0, 1), (2, -1)):
        for m in range(n_band):
            if by == 0 and m == 0:
                continue
            first = (shell * n_band + m) * rows_atom
            pairs = [
                (d * n_band + b, (d - by) % n_dom * n_band + (b ^ m))
                for d in range(n_dom)
                for b in range(n_band)
            ]
            seen.append(m * n_sub)
            sums.append(lax.ppermute(proj[first : first + rows_atom], ("dom", "band"), pairs))
    scale_point = 1.0 / (cells * lanes * n_dom)
    scale_atom = 1.0 / math.sqrt(point_offsets.shape[0] * n_dom)
    kept, sent = gram_share(
        (scale_point, scale_atom), groups, seen, n_band * rows_atom, group.reshape(1),
        corr_matrix, grid_part, proj, sums,
    )
    by = groups // 2
    while by:
        kept += swapped(sent, ("band", "sub"), groups, by)
        by //= 2
        if by:
            kept, sent = kept[: by * orbitals], kept[by * orbitals :]
    by = 1
    while by < n_dom:
        kept += swapped(kept, "dom", n_dom, by)
        by *= 2
    return filtered, kept


def solution(mesh):
    placed = (
        P(("slab", "band", "sub"), "dom", None, None),
        P(("slab", "dom"), None, None),
        P(("slab", "dom"), None, None),
        P(("slab", "dom"), None, None, None),
        P(("slab", "dom"), None, None),
    )
    return jax.shard_map(
        on_device,
        mesh=mesh,
        in_specs=placed,
        out_specs=(P(("slab", "band", "sub"), "dom", None, None), P(("slab", "band", "sub"), None)),
        check_vma=False,
    )
```

time: 163 us -> 137 us (0.84)
  blocking collectives: 30.6 us -> 0 us
  starting transfers between devices: 19.2 us -> 43 us
  waiting for transfers between devices: 62.9 us -> 40.2 us
  Pallas kernels: 30 us -> 32.2 us
    all_to_all x1 -> x0, blocking collectives: 30.6 us -> none  [transposed(): return lax.all_to_all(x, 'dom', split_axis=0, concat_axis=0, tiled=True)]
    ppermute x10 -> x21, starting transfers between devices: 5.12 us -> 35.7 us  [swapped(): return lax.ppermute(x, axes, [(i, i ^ by) for i in range(size)])]
    all_to_all x3 -> x0, waiting for transfers between devices: 29.3 us -> none  [transposed(): return lax.all_to_all(x, 'dom', split_axis=0, concat_axis=0, tiled=True)]
    all_to_all x3 -> x0, starting transfers between devices: 12 us -> none  [transposed(): return lax.all_to_all(x, 'dom', split_axis=0, concat_axis=0, tiled=True)]
    ppermute x10 -> x21, waiting for transfers between devices: 29.4 us -> 34.8 us  [swapped(): return lax.ppermute(x, axes, [(i, i ^ by) for i in range(size)])]
    ppermute x2 -> x5, starting transfers between devices: 2.08 us -> 7.34 us  [on_device(): lax.ppermute(proj[first:first + rows_atom], ('dom', 'band'), pairs)]
    slice x2 -> x1, local copies, waits for them, and re-layouts: 2.42 us -> 0.02 us  [on_device(): proj[first:first + rows_atom]]
    pallas_call x7, Pallas kernels: 30 us -> 32.2 us  [the longest x2 13.7 us: filter_orbitals(): pl.pallas_call(functools.partial(filter_kernel, n_dom, planes, rows, star...]
  transfers between devices with their start and end apart: 15 -> 26, of which waited for: 10 -> 12; matrix products, arithmetic and copies ran while one was open for 1% -> 2% of each run, Pallas kernels for 13% -> 18%
where the time goes in v4:
time: 137 us; the launch traced here: 136 us
  starting transfers between devices  43 us (31%)
  waiting for transfers between devices  40.2 us (29%)
  Pallas kernels  32.2 us (24%)
  local copies, waits for them, and re-layouts  17.8 us (13%)
  other arithmetic  2.09 us (2%)
    ppermute x21, starting transfers between devices, swapped(): return lax.ppermute(x, axes, [(i, i ^ by) for i in range(size)])  35.7 us
    ppermute x21, waiting for transfers between devices, swapped(): return lax.ppermute(x, axes, [(i, i ^ by) for i in range(size)])  34.8 us
    unnamed x26, local copies, waits for them, and re-layouts  15 us
    pallas_call x2, Pallas kernels, filter_orbitals(): pl.pallas_call(functools.partial(filter_kernel, n_dom, planes, rows, star...  13.7 us
    pallas_call x1, Pallas kernels, build_projectors(): pl.pallas_call(functools.partial(projector_kernel, n_band, n_sub), out_sh...  10.5 us
    ppermute x5, starting transfers between devices, on_device(): lax.ppermute(proj[first:first + rows_atom], ('dom', 'band'), pairs)  7.34 us
    pallas_call x1, Pallas kernels, products(): pl.pallas_call(functools.partial(product_kernel, n_chunks, n_sub), out_sh...  6.94 us
    ppermute x5, waiting for transfers between devices, on_device(): lax.ppermute(proj[first:first + rows_atom], ('dom', 'band'), pairs)  5.44 us
  transfers between devices with their start and end apart: 26, of which 12 were waited for; matrix products, arithmetic and copies ran while one was open for 2% of the time, Pallas kernels for 18%

profile of v4, /device:TPU:0, one launch (start us, length us, event | category | flops | bytes accessed | tf_op | source)
XLA Modules:
  0.0 136.2 jit_solution(11679504378802873682)
XLA Ops:
  0.6 0.0 copy-start
  0.7 1.6 %constant_dynamic-slice_fusion.1 = (f32[384,128]{1,0:T(8,128)S(1)}, f32[384,128]{1,0:T(8,128)S(1)}, f32[384,128]{1,0:T(8,128)S(1)}, f32[384,128]{1,0:T(8,128)S(1...) fusion(f32[3072,128]{1,0:T(8,128)} %bitcast.23, ...), kind=kLoop, calls=%fused_computation.10 | loop fusion | bytes 3145760 | tf_op jit(solution)/shard_map/dynamic_slice | solution.py:362
  2.3 3.1 %collective-permute-start = (f32[864,128]{1,0:T(8,128)S(1)}, f32[864,128]{1,0:T(8,128)S(1)}, u32[]{:S(2)}, u32[]{:S(2)}) collective-permute-start(f32[864,128]{1,0:T(8,128)S(1)} %pad_maximum_fusion.1), channel_id=1, source_target_pairs={{0,4},{4,0},{8,12},{12,8},{1,5},{5,1},{9,13},{13,9},{2,6},{6,2},{1... | collective-permute-start | bytes 1327112 | tf_op jit(solution)/shard_map/ppermute | solution.py:42
  5.5 0.0 copy-start.12
  5.5 2.7 %collective-permute-start.1 = (f32[480,128]{1,0:T(8,128)S(1)}, f32[480,128]{1,0:T(8,128)S(1)}, u32[]{:S(2)}, u32[]{:S(2)}) collective-permute-start(f32[480,128]{1,0:T(8,128)S(1)} %get-tuple-element.80), channel_id=1, source_target_pairs={{0,8},{4,12},{8,0},{12,4},{1,9},{5,13},{9,1},{13,5},{2,10},{6,14},... | collective-permute-start | bytes 737288 | tf_op jit(solution)/shard_map/ppermute | solution.py:42
  8.1 0.0 collective-permute-start.2
  8.2 12.7 %collective-permute-done.refs_1_.refs_2_ = f32[864,128]{1,0:T(8,128)S(1)} collective-permute-done((f32[864,128]{1,0:T(8,128)S(1)}, f32[864,128]{1,0:T(8,128)S(1)}, u32[]{:S(2)}, u32[]{:S(2)}) %collective-permute-start) | collective-permute-done | bytes 442400 | tf_op jit(solution)/shard_map/ppermute | solution.py:42
  20.9 3.0 %collective-permute-start.6 = (f32[384,128]{1,0:T(8,128)S(1)}, f32[384,128]{1,0:T(8,128)S(1)}, u32[]{:S(2)}, u32[]{:S(2)}) collective-permute-start(f32[384,128]{1,0:T(8,128)S(1)} %get-tuple-element.40), channel_id=1, source_target_pairs={{0,8},{4,12},{8,0},{12,4},{1,9},{5,13},{9,1},{13,5},{2,10},{6,14},... | collective-permute-start | bytes 589832 | tf_op jit(solution)/shard_map/ppermute | solution.py:42
  23.8 5.0 %collective-permute-start.7 = (f32[384,128]{1,0:T(8,128)S(1)}, f32[384,128]{1,0:T(8,128)S(1)}, u32[]{:S(2)}, u32[]{:S(2)}) collective-permute-start(f32[384,128]{1,0:T(8,128)S(1)} %get-tuple-element.41), channel_id=1, source_target_pairs={{0,12},{4,8},{8,4},{12,0},{1,13},{5,9},{9,5},{13,1},{2,14},{6,10},... | collective-permute-start | bytes 589832 | tf_op jit(solution)/shard_map/ppermute | solution.py:42
  28.8 0.7 collective-permute-done.2.refs_3_
  29.6 6.7 %chebyshev.2 = (f32[3,128,128]{2,1,0:T(8,128)S(1)}, f32[3,128,128]{2,1,0:T(8,128)S(1)}, f32[3,128,128]{2,1,0:T(8,128)S(1)}, f32[3,128,128]{2,1,0:T(8,128)S(1)}, f32[6,32,8,128]{3,2,1,0:T(8,128)S(1)}) custom-call(s32[1]{0:T(128)} %bitcast.me_ref, f32[480,128]{1,0:T(8,128)S(1)} %get-tuple-element.81.refs_0_, ...), custom_call_target="tpu_custom_call" | custom-call | flops 28311552 | bytes 1572864 | tf_op jit(solution)/shard_map/chebyshev/pallas_call | solution.py:128
  36.2 10.4 %collective-permute-start.3 = (f32[3,128,128]{2,1,0:T(8,128)S(1)}, f32[3,128,128]{2,1,0:T(8,128)S(1)}, u32[]{:S(2)}, u32[]{:S(2)}) collective-permute-start(f32[3,128,128]{2,1,0:T(8,128)S(1)} %get-tuple-element.35), channel_id=1, source_target_pairs={{0,4},{4,0},{8,12},{12,8},{1,5},{5,1},{9,13},{13,9},{2,6},{6,2},{1... | collective-permute-start | bytes 589832 | tf_op jit(solution)/shard_map/ppermute | solution.py:42
  46.7 1.3 collective-permute-start.4
  48.0 1.4 %collective-permute-start.5 = (f32[3,128,128]{2,1,0:T(8,128)S(1)}, f32[3,128,128]{2,1,0:T(8,128)S(1)}, u32[]{:S(2)}, u32[]{:S(2)}) collective-permute-start(f32[3,128,128]{2,1,0:T(8,128)S(1)} %get-tuple-element.37), channel_id=1, source_target_pairs={{0,12},{4,8},{8,4},{12,0},{1,13},{5,9},{9,5},{13,1},{2,14},{6,10},... | collective-permute-start | bytes 589832 | tf_op jit(solution)/shard_map/ppermute | solution.py:42
  49.3 7.1 %chebyshev.3 = (f32[3,128,128]{2,1,0:T(8,128)S(1)}, f32[3,128,128]{2,1,0:T(8,128)}, f32[3,128,128]{2,1,0:T(8,128)}, f32[3,128,128]{2,1,0:T(8,128)}) custom-call(s32[1]{0:T(128)} %bitcast.me_ref, f32[6,32,8,128]{3,2,1,0:T(8,128)S(1)} %get-tuple-element.38.refs_0_, f32[384,128]{1,0:T(8,128)S(1)} %get-tuple-element.68.refs_1_, ...), custom_call_target="tpu_custom_call" | custom-call | flops 28311552 | bytes 1572864 | tf_op jit(solution)/shard_map/chebyshev/pallas_call | solution.py:128
  56.4 0.8 collective-permute-start.8
  57.3 2.2 %collective-permute-start.9 = (f32[3,128,128]{2,1,0:T(8,128)}, f32[3,128,128]{2,1,0:T(8,128)S(1)}, u32[]{:S(2)}, u32[]{:S(2)}) collective-permute-start(f32[3,128,128]{2,1,0:T(8,128)} %get-tuple-element.53), channel_id=1, source_target_pairs={{0,8},{4,12},{8,0},{12,4},{1,9},{5,13},{9,1},{13,5},{2,10},{6,14},... | collective-permute-start | bytes 589832 | tf_op jit(solution)/shard_map/ppermute | solution.py:42
  59.4 0.0 collective-permute-done.3
  59.4 1.4 %collective-permute-start.10 = (f32[3,128,128]{2,1,0:T(8,128)}, f32[3,128,128]{2,1,0:T(8,128)S(1)}, u32[]{:S(2)}, u32[]{:S(2)}) collective-permute-start(f32[3,128,128]{2,1,0:T(8,128)} %get-tuple-element.54), channel_id=1, source_target_pairs={{0,12},{4,8},{8,4},{12,0},{1,13},{5,9},{9,5},{13,1},{2,14},{6,10},... | collective-permute-start | bytes 589832 | tf_op jit(solution)/shard_map/ppermute | solution.py:42
  60.9 10.5 %projectors.1 = (bf16[576,6144]{1,0:T(8,128)(2,1)S(1)}, bf16[576,6144]{1,0:T(8,128)(2,1)S(1)}) custom-call(s32[1]{0:T(128)} %bitcast.1.band_ref, s32[1]{0:T(128)} %bitcast.4.sub_ref, s32[48,3,128]{2,1,0:T(4,128)S(1)} %copy.9.offsets_ref, f32[48,3,8,128]{3,2,1,0:T(8,128)S(1)} %copy-done.9), custom_call_target="tpu_custom_call" | custom-call | flops 1811939328 | bytes 28311552 | tf_op jit(solution)/shard_map/projectors/pallas_call | solution.py:234
  71.5 2.8 %copy-done.1 = bf16[576,6144]{1,0:T(8,128)(2,1)} copy-done((bf16[576,6144]{1,0:T(8,128)(2,1)}, bf16[576,6144]{1,0:T(8,128)(2,1)S(1)}, u32[]{:S(2)}) %copy-start.1) | copy-done | bytes 7077912
  74.3 2.9 %copy-done.3 = bf16[576,6144]{1,0:T(8,128)(2,1)} copy-done((bf16[576,6144]{1,0:T(8,128)(2,1)}, bf16[576,6144]{1,0:T(8,128)(2,1)S(1)}, u32[]{:S(2)}) %copy-start.3) | copy-done | bytes 7077912
  77.2 0.0 collective-permute-done.5
  77.2 0.1 assemble.2
  77.4 1.6 %collective-permute-start.12 = (f32[48,16,128]{2,1,0:T(8,128)S(1)}, f32[48,16,128]{2,1,0:T(8,128)S(1)}, u32[]{:S(2)}, u32[]{:S(2)}) collective-permute-start(f32[48,16,128]{2,1,0:T(8,128)S(1)} %get-tuple-element.59), channel_id=1, source_target_pairs={{0,2},{2,0},{1,3},{3,1},{4,6},{6,4},{5,7},{7,5},{8,10},{10,8},{9,1... | collective-permute-start | bytes 1179656 | tf_op jit(solution)/shard_map/ppermute | solution.py:42
  78.9 0.0 collective-permute-done.8
  78.9 0.0 collective-permute-done.9
  78.9 0.7 copy-done.5
  79.6 0.7 copy-done.7
  80.3 0.9 copy-done.6
  81.2 0.9 copy-done.8
  82.2 0.2 assemble.3
  82.3 0.8 collective-permute-start.15
  83.1 0.5 collective-permute-start.14
  83.6 5.4 %collective-permute-done.12.refs_2_ = f32[48,16,128]{2,1,0:T(8,128)S(1)} collective-permute-done((f32[48,16,128]{2,1,0:T(8,128)S(1)}, f32[48,16,128]{2,1,0:T(8,128)S(1)}, u32[]{:S(2)}, u32[]{:S(2)}) %collective-permute-start.12) | collective-permute-done | bytes 393248 | tf_op jit(solution)/shard_map/ppermute | solution.py:42
  89.0 0.0 collective-permute-start.13
  89.0 4.2 %collective-permute-done.15.refs_6_ = f32[48,16,128]{2,1,0:T(8,128)S(1)} collective-permute-done((f32[48,16,128]{2,1,0:T(8,128)S(1)}, f32[48,16,128]{2,1,0:T(8,128)S(1)}, u32[]{:S(2)}, u32[]{:S(2)}) %collective-permute-start.15) | collective-permute-done | bytes 393248 | tf_op jit(solution)/shard_map/ppermute | solution.py:42
  93.2 0.0 collective-permute-start.16
  93.2 0.1 constant_dynamic-slice_fusion
  93.3 0.7 copy.10
  94.1 0.0 collective-permute-done.11.refs_1_
  94.1 1.0 collective-permute-done.16.refs_7_
  95.1 3.0 %copy-done.2 = bf16[576,6144]{1,0:T(8,128)(2,1)S(1)} copy-done((bf16[576,6144]{1,0:T(8,128)(2,1)S(1)}, bf16[576,6144]{1,0:T(8,128)(2,1)}, u32[]{:S(2)}) %copy-start.2) | copy-done | bytes 7077912
  98.1 3.0 %copy-done.4 = bf16[576,6144]{1,0:T(8,128)(2,1)S(1)} copy-done((bf16[576,6144]{1,0:T(8,128)(2,1)S(1)}, bf16[576,6144]{1,0:T(8,128)(2,1)}, u32[]{:S(2)}) %copy-start.4) | copy-done | bytes 7077912
  101.1 6.9 %products.1 = (f32[128,128]{1,0:T(8,128)S(1)}, f32[576,128]{1,0:T(8,128)S(1)}) custom-call(s32[1]{0:T(128)} %bitcast.4.sub_ref, bf16[576,6144]{1,0:T(8,128)(2,1)S(1)} %copy-done.2, bf16[576,6144]{1,0:T(8,128)(2,1)S(1)} %copy-done.4, f32[48,16,128]{2,1,0:T(8,128)S(1)} %get-tuple-element.58.refs_0_, f32[48,16,128]{2,1,0:T(8,128)} %collective-permute-done.11.refs_1_, ...), custom_call_target="tpu_custom_call" | custom-call | tf_op jit(solution)/shard_map/products/pallas_call | solution.py:293
  108.1 1.1 collective-permute-start.17
  109.2 3.3 %collective-permute-start.18 = (f32[96,128]{1,0:T(8,128)S(1)}, f32[96,128]{1,0:T(8,128)S(1)}, u32[]{:S(2)}, u32[]{:S(2)}) collective-permute-start(f32[96,128]{1,0:T(8,128)S(1)} %get-tuple-element.77), channel_id=1, source_target_pairs={{0,12},{2,14},{4,0},{6,2},{8,4},{10,6},{12,8},{14,10},{1,13},{3,15... | collective-permute-start | bytes 147464 | tf_op jit(solution)/shard_map/ppermute | solution.py:481
  112.5 1.0 collective-permute-start.19
  113.4 1.0 collective-permute-start.20
  114.5 0.9 collective-permute-start.21
  115.4 0.1 broadcast_multiply_fusion
  115.5 0.3 mul.64.corr_ref
  115.8 1.6 %collective-permute-done.19.refs_2_ = f32[96,128]{1,0:T(8,128)S(1)} collective-permute-done((f32[96,128]{1,0:T(8,128)S(1)}, f32[96,128]{1,0:T(8,128)S(1)}, u32[]{:S(2)}, u32[]{:S(2)}) %collective-permute-start.19) | collective-permute-done | bytes 49184 | tf_op jit(solution)/shard_map/ppermute | solution.py:481
  117.5 2.4 %collective-permute-done.20.refs_3_ = f32[96,128]{1,0:T(8,128)S(1)} collective-permute-done((f32[96,128]{1,0:T(8,128)S(1)}, f32[96,128]{1,0:T(8,128)S(1)}, u32[]{:S(2)}, u32[]{:S(2)}) %collective-permute-start.20) | collective-permute-done | bytes 49184 | tf_op jit(solution)/shard_map/ppermute | solution.py:481
  119.9 1.4 %collective-permute-done.21.refs_4_ = f32[96,128]{1,0:T(8,128)S(1)} collective-permute-done((f32[96,128]{1,0:T(8,128)S(1)}, f32[96,128]{1,0:T(8,128)S(1)}, u32[]{:S(2)}, u32[]{:S(2)}) %collective-permute-start.21) | collective-permute-done | bytes 49184 | tf_op jit(solution)/shard_map/ppermute | solution.py:481
  121.3 0.7 gram_share.1
  122.0 1.5 %collective-permute-start.22 = (f32[64,128]{1,0:T(8,128)S(1)}, f32[64,128]{1,0:T(8,128)S(1)}, u32[]{:S(2)}, u32[]{:S(2)}) collective-permute-start(f32[64,128]{1,0:T(8,128)S(1)} %get-tuple-element.65), channel_id=1, source_target_pairs={{0,2},{1,3},{2,0},{3,1},{4,6},{5,7},{6,4},{7,5},{8,10},{9,11},{10,... | collective-permute-start | bytes 98312 | tf_op jit(solution)/shard_map/ppermute | solution.py:42
  123.5 2.4 %collective-permute-done.22 = f32[64,128]{1,0:T(8,128)S(1)} collective-permute-done((f32[64,128]{1,0:T(8,128)S(1)}, f32[64,128]{1,0:T(8,128)S(1)}, u32[]{:S(2)}, u32[]{:S(2)}) %collective-permute-start.22) | collective-permute-done | bytes 32800 | tf_op jit(solution)/shard_map/ppermute | solution.py:42
  126.0 0.1 collective-permute-start.23
  126.0 1.2 collective-permute-done.23
  127.2 3.7 %collective-permute-done.24 = f32[32,128]{1,0:T(8,128)S(1)} collective-permute-done((f32[32,128]{1,0:T(8,128)S(1)}, f32[32,128]{1,0:T(8,128)S(1)}, u32[]{:S(2)}, u32[]{:S(2)}) %collective-permute-start.24) | collective-permute-done | bytes 16416 | tf_op jit(solution)/shard_map/ppermute | solution.py:42
  131.0 1.3 pad_maximum_fusion
  132.2 3.4 %collective-permute-done.25 = f32[32,128]{1,0:T(8,128)S(1)} collective-permute-done((f32[32,128]{1,0:T(8,128)S(1)}, f32[32,128]{1,0:T(8,128)S(1)}, u32[]{:S(2)}, u32[]{:S(2)}) %collective-permute-start.25) | collective-permute-done | bytes 16416 | tf_op jit(solution)/shard_map/ppermute | solution.py:42
  135.6 0.6 add.75
  (37 shorter events, 0.2 us)
Async XLA Ops:
  0.6 92.6 %copy-start = (f32[48,8,8]{0,2,1:T(8,128)S(1)}, f32[48,8,8]{0,2,1:T(8,128)}, u32[]{:S(2)}) copy-start(f32[48,8,8]{0,2,1:T(8,128)} %param.9) | copy-start | bytes 36868
  0.7 1.6 %copy-start.10 = (f32[3,32,128]{2,1,0:T(8,128)S(1)}, f32[3,32,128]{2,1,0:T(8,128)}, u32[]{:S(2)}) copy-start(f32[3,32,128]{2,1,0:T(8,128)} %param.6) | copy-start | bytes 147460
  2.3 18.5 %collective-permute-start = (f32[864,128]{1,0:T(8,128)S(1)}, f32[864,128]{1,0:T(8,128)S(1)}, u32[]{:S(2)}, u32[]{:S(2)}) collective-permute-start(f32[864,128]{1,0:T(8,128)S(1)} %pad_maximum_fusion.1), channel_id=1, source_target_pairs={{0,4},{4,0},{8,12},{12,8},{1,5},{5,1},{9,13},{13,9},{2,6},{6,2},{1... | collective-permute-start | bytes 1327112 | tf_op jit(solution)/shard_map/ppermute | solution.py:42
  5.5 55.4 %copy-start.12 = (s32[48,3,128]{2,0,1:T(8,128)S(1)}, s32[48,3,128]{2,0,1:T(8,128)}, u32[]{:S(2)}) copy-start(s32[48,3,128]{2,0,1:T(8,128)} %param.7) | copy-start | bytes 221188
  5.5 23.3 %collective-permute-start.1 = (f32[480,128]{1,0:T(8,128)S(1)}, f32[480,128]{1,0:T(8,128)S(1)}, u32[]{:S(2)}, u32[]{:S(2)}) collective-permute-start(f32[480,128]{1,0:T(8,128)S(1)} %get-tuple-element.80), channel_id=1, source_target_pairs={{0,8},{4,12},{8,0},{12,4},{1,9},{5,13},{9,1},{13,5},{2,10},{6,14},... | collective-permute-start | bytes 737288 | tf_op jit(solution)/shard_map/ppermute | solution.py:42
  8.1 21.4 %collective-permute-start.2 = (f32[480,128]{1,0:T(8,128)S(1)}, f32[480,128]{1,0:T(8,128)S(1)}, u32[]{:S(2)}, u32[]{:S(2)}) collective-permute-start(f32[480,128]{1,0:T(8,128)S(1)} %get-tuple-element.79), channel_id=1, source_target_pairs={{0,12},{4,8},{8,4},{12,0},{1,13},{5,9},{9,5},{13,1},{2,14},{6,10},... | collective-permute-start | bytes 737288 | tf_op jit(solution)/shard_map/ppermute | solution.py:42
  20.9 28.5 %collective-permute-start.6 = (f32[384,128]{1,0:T(8,128)S(1)}, f32[384,128]{1,0:T(8,128)S(1)}, u32[]{:S(2)}, u32[]{:S(2)}) collective-permute-start(f32[384,128]{1,0:T(8,128)S(1)} %get-tuple-element.40), channel_id=1, source_target_pairs={{0,8},{4,12},{8,0},{12,4},{1,9},{5,13},{9,1},{13,5},{2,10},{6,14},... | collective-permute-start | bytes 589832 | tf_op jit(solution)/shard_map/ppermute | solution.py:42
  23.8 25.5 %collective-permute-start.7 = (f32[384,128]{1,0:T(8,128)S(1)}, f32[384,128]{1,0:T(8,128)S(1)}, u32[]{:S(2)}, u32[]{:S(2)}) collective-permute-start(f32[384,128]{1,0:T(8,128)S(1)} %get-tuple-element.41), channel_id=1, source_target_pairs={{0,12},{4,8},{8,4},{12,0},{1,13},{5,9},{9,5},{13,1},{2,14},{6,10},... | collective-permute-start | bytes 589832 | tf_op jit(solution)/shard_map/ppermute | solution.py:42
  29.6 31.3 %copy-start.9 = (f32[48,3,8,128]{3,2,1,0:T(8,128)S(1)}, f32[48,3,8,128]{3,2,1,0:T(8,128)}, u32[]{:S(2)}) copy-start(f32[48,3,8,128]{3,2,1,0:T(8,128)} %coefs_ref.1) | copy-start | bytes 1769476
  36.2 23.2 %collective-permute-start.3 = (f32[3,128,128]{2,1,0:T(8,128)S(1)}, f32[3,128,128]{2,1,0:T(8,128)S(1)}, u32[]{:S(2)}, u32[]{:S(2)}) collective-permute-start(f32[3,128,128]{2,1,0:T(8,128)S(1)} %get-tuple-element.35), channel_id=1, source_target_pairs={{0,4},{4,0},{8,12},{12,8},{1,5},{5,1},{9,13},{13,9},{2,6},{6,2},{1... | collective-permute-start | bytes 589832 | tf_op jit(solution)/shard_map/ppermute | solution.py:42
  46.7 30.6 %collective-permute-start.4 = (f32[3,128,128]{2,1,0:T(8,128)S(1)}, f32[3,128,128]{2,1,0:T(8,128)S(1)}, u32[]{:S(2)}, u32[]{:S(2)}) collective-permute-start(f32[3,128,128]{2,1,0:T(8,128)S(1)} %get-tuple-element.36), channel_id=1, source_target_pairs={{0,8},{4,12},{8,0},{12,4},{1,9},{5,13},{9,1},{13,5},{2,10},{6,14},... | collective-permute-start | bytes 589832 | tf_op jit(solution)/shard_map/ppermute | solution.py:42
  48.0 29.3 %collective-permute-start.5 = (f32[3,128,128]{2,1,0:T(8,128)S(1)}, f32[3,128,128]{2,1,0:T(8,128)S(1)}, u32[]{:S(2)}, u32[]{:S(2)}) collective-permute-start(f32[3,128,128]{2,1,0:T(8,128)S(1)} %get-tuple-element.37), channel_id=1, source_target_pairs={{0,12},{4,8},{8,4},{12,0},{1,13},{5,9},{9,5},{13,1},{2,14},{6,10},... | collective-permute-start | bytes 589832 | tf_op jit(solution)/shard_map/ppermute | solution.py:42
  56.4 22.5 %collective-permute-start.8 = (f32[3,128,128]{2,1,0:T(8,128)}, f32[3,128,128]{2,1,0:T(8,128)S(1)}, u32[]{:S(2)}, u32[]{:S(2)}) collective-permute-start(f32[3,128,128]{2,1,0:T(8,128)} %get-tuple-element.52), channel_id=1, source_target_pairs={{0,4},{4,0},{8,12},{12,8},{1,5},{5,1},{9,13},{13,9},{2,6},{6,2},{1... | collective-permute-start | bytes 589832 | tf_op jit(solution)/shard_map/ppermute | solution.py:42
  57.3 21.7 %collective-permute-start.9 = (f32[3,128,128]{2,1,0:T(8,128)}, f32[3,128,128]{2,1,0:T(8,128)S(1)}, u32[]{:S(2)}, u32[]{:S(2)}) collective-permute-start(f32[3,128,128]{2,1,0:T(8,128)} %get-tuple-element.53), channel_id=1, source_target_pairs={{0,8},{4,12},{8,0},{12,4},{1,9},{5,13},{9,1},{13,5},{2,10},{6,14},... | collective-permute-start | bytes 589832 | tf_op jit(solution)/shard_map/ppermute | solution.py:42
  59.4 20.2 %collective-permute-start.10 = (f32[3,128,128]{2,1,0:T(8,128)}, f32[3,128,128]{2,1,0:T(8,128)S(1)}, u32[]{:S(2)}, u32[]{:S(2)}) collective-permute-start(f32[3,128,128]{2,1,0:T(8,128)} %get-tuple-element.54), channel_id=1, source_target_pairs={{0,12},{4,8},{8,4},{12,0},{1,13},{5,9},{9,5},{13,1},{2,14},{6,10},... | collective-permute-start | bytes 589832 | tf_op jit(solution)/shard_map/ppermute | solution.py:42
  71.4 2.8 %copy-start.1 = (bf16[576,6144]{1,0:T(8,128)(2,1)}, bf16[576,6144]{1,0:T(8,128)(2,1)S(1)}, u32[]{:S(2)}) copy-start(bf16[576,6144]{1,0:T(8,128)(2,1)S(1)} %get-tuple-element.56.w_high) | copy-start | bytes 21233668
  74.3 2.9 %copy-start.3 = (bf16[576,6144]{1,0:T(8,128)(2,1)}, bf16[576,6144]{1,0:T(8,128)(2,1)S(1)}, u32[]{:S(2)}) copy-start(bf16[576,6144]{1,0:T(8,128)(2,1)S(1)} %get-tuple-element.57.w_low) | copy-start | bytes 21233668
  77.4 11.6 %collective-permute-start.12 = (f32[48,16,128]{2,1,0:T(8,128)S(1)}, f32[48,16,128]{2,1,0:T(8,128)S(1)}, u32[]{:S(2)}, u32[]{:S(2)}) collective-permute-start(f32[48,16,128]{2,1,0:T(8,128)S(1)} %get-tuple-element.59), channel_id=1, source_target_pairs={{0,2},{2,0},{1,3},{3,1},{4,6},{6,4},{5,7},{7,5},{8,10},{10,8},{9,1... | collective-permute-start | bytes 1179656 | tf_op jit(solution)/shard_map/ppermute | solution.py:42
  78.9 0.7 copy-start.5
  79.6 0.7 copy-start.7
  80.3 0.9 copy-start.6
  81.2 0.9 copy-start.8
  82.3 10.9 %collective-permute-start.15 = (f32[48,16,128]{2,1,0:T(8,128)S(1)}, f32[48,16,128]{2,1,0:T(8,128)S(1)}, u32[]{:S(2)}, u32[]{:S(2)}) collective-permute-start(f32[48,16,128]{2,1,0:T(8,128)S(1)} %get-tuple-element.61), channel_id=1, source_target_pairs={{0,2},{2,0},{1,3},{3,1},{4,6},{6,4},{5,7},{7,5},{8,10},{10,8},{9,1... | collective-permute-start | bytes 1179656 | tf_op jit(solution)/shard_map/ppermute | solution.py:42
  83.1 10.9 %collective-permute-start.11 = (f32[48,16,128]{2,1,0:T(8,128)S(1)}, f32[48,16,128]{2,1,0:T(8,128)}, u32[]{:S(2)}, u32[]{:S(2)}) collective-permute-start(f32[48,16,128]{2,1,0:T(8,128)S(1)} %get-tuple-element.58.refs_0_), channel_id=1, source_target_pairs={{0,1},{1,0},{2,3},{3,2},{4,5},{5,4},{6,7},{7,6},{8,9},{9,8},{10,11... | collective-permute-start | bytes 1179656 | tf_op jit(solution)/shard_map/ppermute | solution.py:42
  83.1 10.9 %collective-permute-start.14 = (f32[48,16,128]{2,1,0:T(8,128)S(1)}, f32[48,16,128]{2,1,0:T(8,128)}, u32[]{:S(2)}, u32[]{:S(2)}) collective-permute-start(f32[48,16,128]{2,1,0:T(8,128)S(1)} %get-tuple-element.60.refs_4_), channel_id=1, source_target_pairs={{0,1},{1,0},{2,3},{3,2},{4,5},{5,4},{6,7},{7,6},{8,9},{9,8},{10,11... | collective-permute-start | bytes 1179656 | tf_op jit(solution)/shard_map/ppermute | solution.py:42
  89.0 5.1 %collective-permute-start.13 = (f32[48,16,128]{2,1,0:T(8,128)S(1)}, f32[48,16,128]{2,1,0:T(8,128)}, u32[]{:S(2)}, u32[]{:S(2)}) collective-permute-start(f32[48,16,128]{2,1,0:T(8,128)S(1)} %collective-permute-done.12.refs_2_), channel_id=1, source_target_pairs={{0,1},{1,0},{2,3},{3,2},{4,5},{5,4},{6,7},{7,6},{8,9},{9,8},{10,11... | collective-permute-start | bytes 1179656 | tf_op jit(solution)/shard_map/ppermute | solution.py:42
  93.2 1.9 %collective-permute-start.16 = (f32[48,16,128]{2,1,0:T(8,128)S(1)}, f32[48,16,128]{2,1,0:T(8,128)}, u32[]{:S(2)}, u32[]{:S(2)}) collective-permute-start(f32[48,16,128]{2,1,0:T(8,128)S(1)} %collective-permute-done.15.refs_6_), channel_id=1, source_target_pairs={{0,1},{1,0},{2,3},{3,2},{4,5},{5,4},{6,7},{7,6},{8,9},{9,8},{10,11... | collective-permute-start | bytes 1179656 | tf_op jit(solution)/shard_map/ppermute | solution.py:42
  95.1 3.0 %copy-start.2 = (bf16[576,6144]{1,0:T(8,128)(2,1)S(1)}, bf16[576,6144]{1,0:T(8,128)(2,1)}, u32[]{:S(2)}) copy-start(bf16[576,6144]{1,0:T(8,128)(2,1)} %copy-done.1) | copy-start | bytes 21233668
  98.1 3.0 %copy-start.4 = (bf16[576,6144]{1,0:T(8,128)(2,1)S(1)}, bf16[576,6144]{1,0:T(8,128)(2,1)}, u32[]{:S(2)}) copy-start(bf16[576,6144]{1,0:T(8,128)(2,1)} %copy-done.3) | copy-start | bytes 21233668
  101.1 14.3 %copy-start.11 = (f32[12,8,8]{2,1,0:T(8,128)S(1)}, f32[12,8,8]{2,1,0:T(8,128)}, u32[]{:S(2)}) copy-start(f32[12,8,8]{2,1,0:T(8,128)} %copy.10) | copy-start | bytes 9220
  108.1 7.8 %collective-permute-start.17 = (f32[96,128]{1,0:T(8,128)S(1)}, f32[96,128]{1,0:T(8,128)S(1)}, u32[]{:S(2)}, u32[]{:S(2)}) collective-permute-start(f32[96,128]{1,0:T(8,128)S(1)} %get-tuple-element.78), channel_id=1, source_target_pairs={{0,2},{2,0},{4,6},{6,4},{8,10},{10,8},{12,14},{14,12},{1,3},{3,1},... | collective-permute-start | bytes 147464 | tf_op jit(solution)/shard_map/ppermute | solution.py:481
  109.2 6.7 %collective-permute-start.18 = (f32[96,128]{1,0:T(8,128)S(1)}, f32[96,128]{1,0:T(8,128)S(1)}, u32[]{:S(2)}, u32[]{:S(2)}) collective-permute-start(f32[96,128]{1,0:T(8,128)S(1)} %get-tuple-element.77), channel_id=1, source_target_pairs={{0,12},{2,14},{4,0},{6,2},{8,4},{10,6},{12,8},{14,10},{1,13},{3,15... | collective-permute-start | bytes 147464 | tf_op jit(solution)/shard_map/ppermute | solution.py:481
  112.5 5.0 %collective-permute-start.19 = (f32[96,128]{1,0:T(8,128)S(1)}, f32[96,128]{1,0:T(8,128)S(1)}, u32[]{:S(2)}, u32[]{:S(2)}) collective-permute-start(f32[96,128]{1,0:T(8,128)S(1)} %get-tuple-element.76), channel_id=1, source_target_pairs={{0,14},{2,12},{4,2},{6,0},{8,6},{10,4},{12,10},{14,8},{1,15},{3,13... | collective-permute-start | bytes 147464 | tf_op jit(solution)/shard_map/ppermute | solution.py:481
  113.4 6.4 %collective-permute-start.20 = (f32[96,128]{1,0:T(8,128)S(1)}, f32[96,128]{1,0:T(8,128)S(1)}, u32[]{:S(2)}, u32[]{:S(2)}) collective-permute-start(f32[96,128]{1,0:T(8,128)S(1)} %get-tuple-element.75), channel_id=1, source_target_pairs={{0,4},{2,6},{4,8},{6,10},{8,12},{10,14},{12,0},{14,2},{1,5},{3,7},... | collective-permute-start | bytes 147464 | tf_op jit(solution)/shard_map/ppermute | solution.py:481
  114.5 6.8 %collective-permute-start.21 = (f32[96,128]{1,0:T(8,128)S(1)}, f32[96,128]{1,0:T(8,128)S(1)}, u32[]{:S(2)}, u32[]{:S(2)}) collective-permute-start(f32[96,128]{1,0:T(8,128)S(1)} %get-tuple-element.74), channel_id=1, source_target_pairs={{0,6},{2,4},{4,10},{6,8},{8,14},{10,12},{12,2},{14,0},{1,7},{3,5},... | collective-permute-start | bytes 147464 | tf_op jit(solution)/shard_map/ppermute | solution.py:481
  122.0 4.0 %collective-permute-start.22 = (f32[64,128]{1,0:T(8,128)S(1)}, f32[64,128]{1,0:T(8,128)S(1)}, u32[]{:S(2)}, u32[]{:S(2)}) collective-permute-start(f32[64,128]{1,0:T(8,128)S(1)} %get-tuple-element.65), channel_id=1, source_target_pairs={{0,2},{1,3},{2,0},{3,1},{4,6},{5,7},{6,4},{7,5},{8,10},{9,11},{10,... | collective-permute-start | bytes 98312 | tf_op jit(solution)/shard_map/ppermute | solution.py:42
  126.0 1.2 collective-permute-start.23
  127.2 3.7 %collective-permute-start.24 = (f32[32,128]{1,0:T(8,128)S(1)}, f32[32,128]{1,0:T(8,128)S(1)}, u32[]{:S(2)}, u32[]{:S(2)}) collective-permute-start(f32[32,128]{1,0:T(8,128)S(1)} %slice_add_fusion), channel_id=1, source_target_pairs={{0,4},{4,0},{8,12},{12,8},{1,5},{5,1},{9,13},{13,9},{2,6},{6,2},{1... | collective-permute-start | bytes 49160 | tf_op jit(solution)/shard_map/ppermute | solution.py:42
  131.0 4.6 %collective-permute-start.25 = (f32[32,128]{1,0:T(8,128)S(1)}, f32[32,128]{1,0:T(8,128)S(1)}, u32[]{:S(2)}, u32[]{:S(2)}) collective-permute-start(f32[32,128]{1,0:T(8,128)S(1)} %add.74), channel_id=1, source_target_pairs={{0,8},{4,12},{8,0},{12,4},{1,9},{5,13},{9,1},{13,5},{2,10},{6,14},... | collective-permute-start | bytes 49160 | tf_op jit(solution)/shard_map/ppermute | solution.py:42

commit v5 on v4

--- a/solution.py
+++ b/solution.py
@@ -16,6 +16,7 @@
 
 TOGETHER = 4
 SUBLANES = 8
+ME, BAND, SUB, GROUP = range(4)
 MIB = 1024 * 1024
 
 VMEM = pl.BlockSpec(memory_space=pltpu.VMEM)
@@ -42,7 +43,7 @@
     return lax.ppermute(x, axes, [(i, i ^ by) for i in range(size)])
 
 
-def filter_kernel(n_dom, planes, rows, starts, first, me_ref, *refs):
+def filter_kernel(n_dom, planes, rows, starts, first, place, *refs):
     refs = list(refs)
     given = None if first else refs.pop(0)
     ins, outs = refs[:n_dom], refs[n_dom : 2 * n_dom]
@@ -53,7 +54,7 @@
     cells = planes * rows
     lanes = even.shape[3]
     scale = 1.0 / HALF_WIDTH
-    mirrored = (me_ref[0] & 1) != 0
+    mirrored = (place[ME] & 1) != 0
     plane_at = [jnp.where(mirrored, planes - 1 - i, i) for i in range(planes)]
 
     for x in range(half_planes):
@@ -116,7 +117,7 @@
                 outs[m][plane_at[i], here, :] = even[x, y, part]
 
 
-def filter_orbitals(me, diagonal, blocks, starts, planes, rows):
+def filter_orbitals(place, diagonal, blocks, starts, planes, rows):
     n_dom = len(blocks)
     first = diagonal is None
     lanes = blocks[0].shape[1]
@@ -136,14 +137,14 @@
             flops=12 * DEGREE * size, bytes_accessed=8 * size, transcendentals=0
         ),
         name="chebyshev",
-    )(me, *given, *blocks)
-
-
-def assemble_kernel(n_dom, n_band, me_ref, band_ref, *refs):
+    )(place, *given, *blocks)
+
+
+def assemble_kernel(n_dom, n_band, place, *refs):
     pieces, orbital_first, parts = refs[:n_dom], refs[n_dom], refs[n_dom + 1 :]
     cells = orbital_first.shape[1]
     share = cells // n_band
-    me = me_ref[0]
+    me = place[ME]
     for m, piece in enumerate(pieces):
         start = (me ^ m) * TOGETHER
         for t in range(TOGETHER):
@@ -151,7 +152,7 @@
     per_load = SUBLANES // TOGETHER
     together = SUBLANES // TOGETHER
     for p, part in enumerate(parts):
-        base = pl.multiple_of((band_ref[0] ^ p) * (share * TOGETHER), SUBLANES)
+        base = pl.multiple_of((place[BAND] ^ p) * (share * TOGETHER), SUBLANES)
         for first in range(0, share, per_load):
             loaded = [
                 piece[pl.ds(base + first * TOGETHER, SUBLANES), :] for piece in pieces
@@ -167,7 +168,7 @@
                     part[first + k, pl.ds(row, SUBLANES), :] = tile
 
 
-def assemble(me, band, n_band, pieces):
+def assemble(place, n_band, pieces):
     n_dom = len(pieces)
     planes, rows, lanes = pieces[0].shape
     cells, orbitals = planes * rows // TOGETHER, n_dom * TOGETHER
@@ -175,30 +176,30 @@
     return pl.pallas_call(
         functools.partial(assemble_kernel, n_dom, n_band),
         out_shape=[jax.ShapeDtypeStruct((orbitals, cells, lanes), jnp.float32)] + [part] * n_band,
-        in_specs=[SMEM] * 2 + [VMEM] * n_dom,
+        in_specs=[SMEM] + [VMEM] * n_dom,
         out_specs=[VMEM] * (1 + n_band),
         compiler_params=params(8),
         name="assemble",
-    )(me, band, *[piece.reshape(planes * rows, lanes) for piece in pieces])
-
-
-def projector_kernel(n_band, n_sub, band_ref, sub_ref, offsets_ref, coefs_ref, high_out, low_out):
+    )(place, *[piece.reshape(planes * rows, lanes) for piece in pieces])
+
+
+def projector_kernel(n_band, n_sub, place, offsets_ref, coefs_ref, high_out, low_out):
     atoms, shells, channels, spread = coefs_ref.shape
     own = atoms // (n_band * n_sub)
     lanes = spread
     cells = high_out.shape[1] // lanes
     pairs = own // 2
     row_index = lax.broadcasted_iota(jnp.int32, (cells, channels, spread), 0)
-    row_index += band_ref[0] * cells
+    row_index += place[BAND] * cells
     lane_index = lax.broadcasted_iota(jnp.int32, (lanes, spread), 0)
 
     def two_atoms(step, carry):
         shell = step // (n_band * pairs)
-        band = band_ref[0] ^ ((step // pairs) % n_band)
-        first_atom = (sub_ref[0] * n_band + band) * own + 2 * (step % pairs)
+        band = place[BAND] ^ ((step // pairs) % n_band)
+        first_atom = (place[SUB] * n_band + band) * own + 2 * (step % pairs)
         dense = []
         for i in range(2):
-            offsets = offsets_ref[first_atom + i, pl.ds(shell, 1), :]
+            offsets = offsets_ref[shell, pl.ds(first_atom + i, 1), :]
             coefs = coefs_ref[first_atom + i, shell]
             at_row = row_index == (offsets // lanes)[None]
             at_row &= (offsets >= 0)[None]
@@ -227,14 +228,14 @@
     lax.fori_loop(0, shells * n_band * pairs, two_atoms, 0)
 
 
-def build_projectors(n_band, n_sub, band, sub, offsets, coefs, cells, lanes):
+def build_projectors(n_band, n_sub, place, offsets, coefs, cells, lanes):
     atoms, shells, channels, spread = coefs.shape
     rows = atoms // n_sub * shells * channels
     shape = jax.ShapeDtypeStruct((rows, cells * lanes), jnp.bfloat16)
     return pl.pallas_call(
         functools.partial(projector_kernel, n_band, n_sub),
         out_shape=[shape, shape],
-        in_specs=[SMEM, SMEM, VMEM, VMEM],
+        in_specs=[SMEM, VMEM, VMEM],
         out_specs=[VMEM, VMEM],
         compiler_params=params(8),
         cost_estimate=pl.CostEstimate(
@@ -243,11 +244,12 @@
             transcendentals=0,
         ),
         name="projectors",
-    )(band, sub, offsets, coefs)
-
-
-def product_kernel(n_chunks, n_sub, sub_ref, w_high, w_low, *refs):
-    *fields, grid_out, proj_out = refs
+    )(place, offsets.swapaxes(0, 1), coefs)
+
+
+def product_kernel(n_chunks, n_sub, n_blocks, place, w_high, w_low, *refs):
+    refs, proj_out = refs[:-1], refs[-1]
+    fields, grid_out, outs = refs[: -n_blocks - 1], refs[-n_blocks - 1], refs[-n_blocks:]
     orbitals = grid_out.shape[0]
     cells, _, lanes = fields[0].shape
     n_groups = len(fields) // n_chunks
@@ -269,7 +271,7 @@
         return wide[:, :orbitals] + wide[:, orbitals:] + narrow
 
     def grid_block(step, carry):
-        high, low = parts(sub_ref[0] * (cells // n_sub) + step * block)
+        high, low = parts(place[SUB] * (cells // n_sub) + step * block)
         grid_out[...] += product(high, low, high, low)
         return carry
 
@@ -284,23 +286,25 @@
     proj_out[...] = jnp.zeros_like(proj_out)
     lax.fori_loop(0, cells // (n_sub * block), grid_block, 0)
     lax.fori_loop(0, cells // block, proj_block, 0)
-
-
-def products(n_sub, sub, projectors, fields):
+    rows = outs[0].shape[0]
+    for k, out in enumerate(outs):
+        out[...] = proj_out[k * rows : (k + 1) * rows, :]
+
+
+def products(n_sub, n_blocks, place, projectors, fields):
     rows = projectors[0].shape[0]
     n_chunks, n_groups = len(fields), len(fields[0])
     orbitals = n_chunks * n_groups * fields[0][0].shape[1]
+    block = jax.ShapeDtypeStruct((rows // n_blocks, orbitals), jnp.float32)
     return pl.pallas_call(
-        functools.partial(product_kernel, n_chunks, n_sub),
-        out_shape=[
-            jax.ShapeDtypeStruct((orbitals, orbitals), jnp.float32),
-            jax.ShapeDtypeStruct((rows, orbitals), jnp.float32),
-        ],
+        functools.partial(product_kernel, n_chunks, n_sub, n_blocks),
+        out_shape=[jax.ShapeDtypeStruct((orbitals, orbitals), jnp.float32)] + [block] * n_blocks,
         in_specs=[SMEM] + [VMEM] * (2 + n_chunks * n_groups),
-        out_specs=[VMEM] * 2,
-        compiler_params=params(12),
+        out_specs=[VMEM] * (1 + n_blocks),
+        scratch_shapes=[pltpu.VMEM((rows, orbitals), jnp.float32)],
+        compiler_params=params(8),
         name="products",
-    )(sub, *projectors, *[field for chunk in fields for field in chunk])
+    )(place, *projectors, *[field for chunk in fields for field in chunk])
 
 
 def reordered(x, width, by):
@@ -310,12 +314,12 @@
     return jnp.where((column & span) == 0, down, up)
 
 
-def gram_kernel(scales, groups, seen, own_row, group_ref, corr_ref, grid_ref, proj_ref, *refs):
-    *sums, kept, sent = refs
+def gram_kernel(scales, groups, seen, place, corr_ref, grid_ref, proj_ref, *refs):
+    sums, outs = refs[: len(seen)], refs[len(seen) :]
     orbitals = grid_ref.shape[0]
     width = orbitals // groups
     bits = [1 << k for k in range(groups.bit_length() - 1)]
-    projections = proj_ref[own_row : own_row + corr_ref.shape[0], :]
+    projections = proj_ref[...]
     for part, by in zip(sums, seen):
         columns = part[...]
         for bit in bits:
@@ -331,25 +335,31 @@
     )
     share = grid_ref[...] * scales[0] + atom_part * scales[1]
     for bit in bits:
-        share = jnp.where((group_ref[0] & bit) != 0, reordered(share, width, bit), share)
-    kept[...] = share[: orbitals // 2]
-    sent[...] = share[orbitals // 2 :]
-
-
-def gram_share(scales, groups, seen, own_row, group, corr, grid_part, proj, sums):
-    half = jax.ShapeDtypeStruct((grid_part.shape[0] // 2, grid_part.shape[1]), jnp.float32)
+        share = jnp.where((place[GROUP] & bit) != 0, reordered(share, width, bit), share)
+    for k, out in enumerate(outs):
+        out[...] = share[k * width : (k + 1) * width]
+
+
+def gram_share(scales, groups, seen, place, corr, grid_part, proj, sums):
+    rows = jax.ShapeDtypeStruct((grid_part.shape[0] // groups, grid_part.shape[1]), jnp.float32)
     return pl.pallas_call(
-        functools.partial(gram_kernel, scales, groups, seen, own_row),
-        out_shape=[half, half],
+        functools.partial(gram_kernel, scales, groups, seen),
+        out_shape=[rows] * groups,
         in_specs=[SMEM] + [VMEM] * (3 + len(sums)),
-        out_specs=[VMEM] * 2,
+        out_specs=[VMEM] * groups,
         compiler_params=params(8),
         name="gram_share",
-    )(group, corr, grid_part, proj, *sums)
-
-
-def whole_columns(panel, potential, me, band):
-    n_dom, n_band = lax.axis_size("dom"), lax.axis_size("band")
+    )(place, corr, grid_part, proj, *sums)
+
+
+def added(terms):
+    while len(terms) > 1:
+        terms = [a + b for a, b in zip(terms[::2], terms[1::2])]
+    return terms[0]
+
+
+def whole_columns(panel, potential, place, me):
+    n_dom = lax.axis_size("dom")
     orbitals, planes, rows, lanes = panel.shape
     cells = planes * rows
     flat = panel.reshape(orbitals * cells, lanes)
@@ -381,7 +391,7 @@
     for c, blocks in enumerate(arrived):
         starts = [0] * n_dom
         starts[1] = c * size + (cells if c else 0)
-        filtered = filter_orbitals(me.reshape(1), diagonal, blocks, starts, planes, rows)
+        filtered = filter_orbitals(place, diagonal, blocks, starts, planes, rows)
         if diagonal is None:
             diagonal = filtered[n_dom]
         done.append(filtered[:n_dom])
@@ -416,7 +426,7 @@
     n_dom, n_band, n_sub = (lax.axis_size(axis) for axis in ("dom", "band", "sub"))
     groups = n_band * n_sub
     me, band, sub = (lax.axis_index(axis) for axis in ("dom", "band", "sub"))
-    group = band * n_sub + sub
+    place = jnp.stack([me, band, sub, band * n_sub + sub]).astype(jnp.int32)
 
     cells = planes * rows
     share = cells // n_band
@@ -430,19 +440,19 @@
         own_atoms * channels, own_atoms * channels
     )
 
+    place, corr_matrix = lax.optimization_barrier((place, corr_matrix))
+
     def build(offsets):
-        return build_projectors(
-            n_band, n_sub, band.reshape(1), sub.reshape(1), offsets, point_coefs, share, lanes
-        )
+        return build_projectors(n_band, n_sub, place, offsets, point_coefs, share, lanes)
 
     filtered, parts = [], []
     if n_dom in (2, 4) and orbitals % (n_dom * TOGETHER) == 0 and planes * n_dom % 2 == 0:
-        chunks = whole_columns(panel, potential, me, band)
+        chunks = whole_columns(panel, potential, place, me)
         chunks[-1][0], point_offsets = lax.optimization_barrier((chunks[-1][0], point_offsets))
         projectors = build(point_offsets)
         chunks[0], projectors = lax.optimization_barrier((chunks[0], projectors))
         for pieces in chunks:
-            orbital_first, *by_band = assemble(me.reshape(1), band.reshape(1), n_band, pieces)
+            orbital_first, *by_band = assemble(place, n_band, pieces)
             filtered.append(orbital_first)
             parts.append(by_band)
     else:
@@ -464,38 +474,37 @@
             chunk += [here] + [swapped(here, "sub", n_sub, k) for k in range(1, n_sub)]
         fields.append(chunk)
 
-    grid_part, proj = products(n_sub, sub.reshape(1), projectors, fields)
-    rows_atom = own_atoms * channels
+    grid_part, *proj = products(n_sub, 3 * n_band, place, projectors, fields)
     sums, seen = [], []
     for shell, by in ((1, 0), (0, 1), (2, -1)):
         for m in range(n_band):
             if by == 0 and m == 0:
                 continue
-            first = (shell * n_band + m) * rows_atom
             pairs = [
                 (d * n_band + b, (d - by) % n_dom * n_band + (b ^ m))
                 for d in range(n_dom)
                 for b in range(n_band)
             ]
             seen.append(m * n_sub)
-            sums.append(lax.ppermute(proj[first : first + rows_atom], ("dom", "band"), pairs))
+            sums.append(lax.ppermute(proj[shell * n_band + m], ("dom", "band"), pairs))
     scale_point = 1.0 / (cells * lanes * n_dom)
-    scale_atom = 1.0 / math.sqrt(point_offsets.shape[0] * n_dom)
-    kept, sent = gram_share(
-        (scale_point, scale_atom), groups, seen, n_band * rows_atom, group.reshape(1),
-        corr_matrix, grid_part, proj, sums,
-    )
-    by = groups // 2
-    while by:
-        kept += swapped(sent, ("band", "sub"), groups, by)
-        by //= 2
-        if by:
-            kept, sent = kept[: by * orbitals], kept[by * orbitals :]
-    by = 1
-    while by < n_dom:
-        kept += swapped(kept, "dom", n_dom, by)
-        by *= 2
-    return filtered, kept
+    scale_atom = 1.0 / math.sqrt(own_atoms * groups * n_dom)
+    shares = gram_share(
+        (scale_point, scale_atom), groups, seen, place, corr_matrix, grid_part, proj[n_band], sums
+    )
+    gram_rows = added(
+        [swapped(x, ("band", "sub"), groups, m) if m else x for m, x in enumerate(shares)]
+    )
+    if n_dom <= 4:
+        gram_rows = added(
+            [swapped(gram_rows, "dom", n_dom, m) if m else gram_rows for m in range(n_dom)]
+        )
+    else:
+        by = 1
+        while by < n_dom:
+            gram_rows += swapped(gram_rows, "dom", n_dom, by)
+            by *= 2
+    return filtered, gram_rows
 
 
 def solution(mesh):

time: 137 us -> 125 us (0.912)
  local copies, waits for them, and re-layouts: 17.8 us -> 2.76 us
  starting transfers between devices: 43 us -> 49 us
  waiting for transfers between devices: 40.2 us -> 36.6 us
    unnamed x26 -> x8, local copies, waits for them, and re-layouts: 15 us -> 0.02 us
    ppermute x21 -> x23, waiting for transfers between devices: 34.8 us -> 29.5 us  [swapped(): return lax.ppermute(x, axes, [(i, i ^ by) for i in range(size)])]
    ppermute x21 -> x23, starting transfers between devices: 35.7 us -> 40.6 us  [swapped(): return lax.ppermute(x, axes, [(i, i ^ by) for i in range(size)])]
    ppermute x5, waiting for transfers between devices: 5.44 us -> 7.16 us  [on_device(): sums.append(lax.ppermute(proj[shell * n_band + m], ('dom', 'band'), pairs))]
  transfers between devices with their start and end apart: 26 -> 28, of which waited for: 12 -> 13; matrix products, arithmetic and copies ran while one was open for 2% -> 2% of each run, Pallas kernels for 18% -> 21%
where the time goes in v5:
time: 125 us; the launch traced here: 124 us
  starting transfers between devices  49 us (39%)
  waiting for transfers between devices  36.6 us (29%)
  Pallas kernels  33.1 us (26%)
  local copies, waits for them, and re-layouts  2.76 us (2%)
  other arithmetic  2.17 us (2%)
    ppermute x23, starting transfers between devices, swapped(): return lax.ppermute(x, axes, [(i, i ^ by) for i in range(size)])  40.6 us
    ppermute x23, waiting for transfers between devices, swapped(): return lax.ppermute(x, axes, [(i, i ^ by) for i in range(size)])  29.5 us
    pallas_call x2, Pallas kernels, filter_orbitals(): pl.pallas_call(functools.partial(filter_kernel, n_dom, planes, rows, star...  13.1 us
    pallas_call x1, Pallas kernels, build_projectors(): pl.pallas_call(functools.partial(projector_kernel, n_band, n_sub), out_sh...  11.2 us
    ppermute x5, starting transfers between devices, on_device(): sums.append(lax.ppermute(proj[shell * n_band + m], ('dom', 'band'), pairs))  8.4 us
    ppermute x5, waiting for transfers between devices, on_device(): sums.append(lax.ppermute(proj[shell * n_band + m], ('dom', 'band'), pairs))  7.16 us
    pallas_call x1, Pallas kernels, products(): pl.pallas_call(functools.partial(product_kernel, n_chunks, n_sub, n_block...  6.16 us
  transfers between devices with their start and end apart: 28, of which 13 were waited for; matrix products, arithmetic and copies ran while one was open for 2% of the time, Pallas kernels for 21%

profile of v5, /device:TPU:0, one launch (start us, length us, event | category | flops | bytes accessed | tf_op | source)
XLA Modules:
  0.0 124.5 jit_solution(12114517729755321452)
XLA Ops:
  0.6 0.0 copy-start
  0.7 2.3 %constant_dynamic-slice_fusion = (f32[384,128]{1,0:T(8,128)S(1)}, f32[384,128]{1,0:T(8,128)}, f32[384,128]{1,0:T(8,128)S(1)}, f32[384,128]{1,0:T(8,128)S(1)}, f3...) fusion(f32[3072,128]{1,0:T(8,128)} %bitcast.25, ...), kind=kLoop, calls=%fused_computation.10 | loop fusion | bytes 3145760 | tf_op jit(solution)/shard_map/dynamic_slice | solution.py:372
  3.0 3.1 %collective-permute-start = (f32[864,128]{1,0:T(8,128)S(1)}, f32[864,128]{1,0:T(8,128)S(1)}, u32[]{:S(2)}, u32[]{:S(2)}) collective-permute-start(f32[864,128]{1,0:T(8,128)S(1)} %pad_maximum_fusion.1), channel_id=1, source_target_pairs={{0,4},{4,0},{8,12},{12,8},{1,5},{5,1},{9,13},{13,9},{2,6},{6,2},{1... | collective-permute-start | bytes 1327112 | tf_op jit(solution)/shard_map/ppermute | solution.py:43
  6.1 2.7 %collective-permute-start.1 = (f32[480,128]{1,0:T(8,128)S(1)}, f32[480,128]{1,0:T(8,128)S(1)}, u32[]{:S(2)}, u32[]{:S(2)}) collective-permute-start(f32[480,128]{1,0:T(8,128)S(1)} %get-tuple-element.93), channel_id=1, source_target_pairs={{0,8},{4,12},{8,0},{12,4},{1,9},{5,13},{9,1},{13,5},{2,10},{6,14},... | collective-permute-start | bytes 737288 | tf_op jit(solution)/shard_map/ppermute | solution.py:43
  8.8 0.0 collective-permute-start.2
  8.8 0.1 constant_dynamic-slice_fusion.8
  8.9 0.1 copy.8
  9.0 0.1 broadcast_multiply_fusion
  9.2 0.3 mul.56.corr_ref
  9.4 0.0 copy-start.2
  9.5 0.1 pad_add_fusion.place
  9.5 12.0 %collective-permute-done.refs_1_.refs_2_ = f32[864,128]{1,0:T(8,128)S(1)} collective-permute-done((f32[864,128]{1,0:T(8,128)S(1)}, f32[864,128]{1,0:T(8,128)S(1)}, u32[]{:S(2)}, u32[]{:S(2)}) %collective-permute-start) | collective-permute-done | bytes 442400 | tf_op jit(solution)/shard_map/ppermute | solution.py:43
  21.5 3.0 %collective-permute-start.6 = (f32[384,128]{1,0:T(8,128)}, f32[384,128]{1,0:T(8,128)S(1)}, u32[]{:S(2)}, u32[]{:S(2)}) collective-permute-start(f32[384,128]{1,0:T(8,128)} %get-tuple-element.50), channel_id=1, source_target_pairs={{0,8},{4,12},{8,0},{12,4},{1,9},{5,13},{9,1},{13,5},{2,10},{6,14},... | collective-permute-start | bytes 589832 | tf_op jit(solution)/shard_map/ppermute | solution.py:43
  24.5 5.0 %collective-permute-start.7 = (f32[384,128]{1,0:T(8,128)S(1)}, f32[384,128]{1,0:T(8,128)S(1)}, u32[]{:S(2)}, u32[]{:S(2)}) collective-permute-start(f32[384,128]{1,0:T(8,128)S(1)} %get-tuple-element.51), channel_id=1, source_target_pairs={{0,12},{4,8},{8,4},{12,0},{1,13},{5,9},{9,5},{13,1},{2,14},{6,10},... | collective-permute-start | bytes 589832 | tf_op jit(solution)/shard_map/ppermute | solution.py:43
  29.5 0.0 collective-permute-done.1.refs_2_
  29.5 0.7 collective-permute-done.2.refs_3_
  30.2 6.7 %chebyshev.2 = (f32[3,128,128]{2,1,0:T(8,128)S(1)}, f32[3,128,128]{2,1,0:T(8,128)S(1)}, f32[3,128,128]{2,1,0:T(8,128)S(1)}, f32[3,128,128]{2,1,0:T(8,128)S(1)}, f32[6,32,8,128]{3,2,1,0:T(8,128)S(1)}) custom-call(s32[4]{0:T(128)S(1)} %pad_add_fusion.place, f32[480,128]{1,0:T(8,128)S(1)} %get-tuple-element.94.refs_0_, ...), custom_call_target="tpu_custom_call" | custom-call | flops 28311552 | bytes 1572864 | tf_op jit(solution)/shard_map/chebyshev/pallas_call | solution.py:129
  37.0 10.4 %collective-permute-start.3 = (f32[3,128,128]{2,1,0:T(8,128)S(1)}, f32[3,128,128]{2,1,0:T(8,128)S(1)}, u32[]{:S(2)}, u32[]{:S(2)}) collective-permute-start(f32[3,128,128]{2,1,0:T(8,128)S(1)} %get-tuple-element.45), channel_id=1, source_target_pairs={{0,4},{4,0},{8,12},{12,8},{1,5},{5,1},{9,13},{13,9},{2,6},{6,2},{1... | collective-permute-start | bytes 589832 | tf_op jit(solution)/shard_map/ppermute | solution.py:43
  47.4 1.3 %collective-permute-start.4 = (f32[3,128,128]{2,1,0:T(8,128)S(1)}, f32[3,128,128]{2,1,0:T(8,128)S(1)}, u32[]{:S(2)}, u32[]{:S(2)}) collective-permute-start(f32[3,128,128]{2,1,0:T(8,128)S(1)} %get-tuple-element.46), channel_id=1, source_target_pairs={{0,8},{4,12},{8,0},{12,4},{1,9},{5,13},{9,1},{13,5},{2,10},{6,14},... | collective-permute-start | bytes 589832 | tf_op jit(solution)/shard_map/ppermute | solution.py:43
  48.7 1.4 %collective-permute-start.5 = (f32[3,128,128]{2,1,0:T(8,128)S(1)}, f32[3,128,128]{2,1,0:T(8,128)S(1)}, u32[]{:S(2)}, u32[]{:S(2)}) collective-permute-start(f32[3,128,128]{2,1,0:T(8,128)S(1)} %get-tuple-element.47), channel_id=1, source_target_pairs={{0,12},{4,8},{8,4},{12,0},{1,13},{5,9},{9,5},{13,1},{2,14},{6,10},... | collective-permute-start | bytes 589832 | tf_op jit(solution)/shard_map/ppermute | solution.py:43
  50.1 0.0 collective-permute-done.6.refs_3_
  50.1 0.0 collective-permute-done.7.refs_4_
  50.1 6.4 %chebyshev.3 = (f32[3,128,128]{2,1,0:T(8,128)S(1)}, f32[3,128,128]{2,1,0:T(8,128)S(1)}, f32[3,128,128]{2,1,0:T(8,128)S(1)}, f32[3,128,128]{2,1,0:T(8,128)S(1)}) custom-call(s32[4]{0:T(128)S(1)} %pad_add_fusion.place, f32[6,32,8,128]{3,2,1,0:T(8,128)S(1)} %get-tuple-element.48.refs_0_, f32[384,128]{1,0:T(8,128)S(1)} %get-tuple-element.86.refs_1_, ...), custom_call_target="tpu_custom_call" | custom-call | flops 28311552 | bytes 1572864 | tf_op jit(solution)/shard_map/chebyshev/pallas_call | solution.py:129
  56.5 0.9 collective-permute-start.8
  57.4 2.2 %collective-permute-start.9 = (f32[3,128,128]{2,1,0:T(8,128)S(1)}, f32[3,128,128]{2,1,0:T(8,128)S(1)}, u32[]{:S(2)}, u32[]{:S(2)}) collective-permute-start(f32[3,128,128]{2,1,0:T(8,128)S(1)} %get-tuple-element.63), channel_id=1, source_target_pairs={{0,8},{4,12},{8,0},{12,4},{1,9},{5,13},{9,1},{13,5},{2,10},{6,14},... | collective-permute-start | bytes 589832 | tf_op jit(solution)/shard_map/ppermute | solution.py:43
  59.5 0.0 collective-permute-done.3
  59.6 1.4 %collective-permute-start.10 = (f32[3,128,128]{2,1,0:T(8,128)S(1)}, f32[3,128,128]{2,1,0:T(8,128)S(1)}, u32[]{:S(2)}, u32[]{:S(2)}) collective-permute-start(f32[3,128,128]{2,1,0:T(8,128)S(1)} %get-tuple-element.64), channel_id=1, source_target_pairs={{0,12},{4,8},{8,4},{12,0},{1,13},{5,9},{9,5},{13,1},{2,14},{6,10},... | collective-permute-start | bytes 589832 | tf_op jit(solution)/shard_map/ppermute | solution.py:43
  60.9 11.2 %projectors.1 = (bf16[576,6144]{1,0:T(8,128)(2,1)S(1)}, bf16[576,6144]{1,0:T(8,128)(2,1)S(1)}) custom-call(s32[4]{0:T(128)S(1)} %pad_add_fusion.place, s32[3,48,128]{2,1,0:T(8,128)S(1)} %bitcast.24, f32[48,3,8,128]{3,2,1,0:T(8,128)S(1)} %copy-done.1), custom_call_target="tpu_custom_call" | custom-call | flops 1811939328 | bytes 28311552 | tf_op jit(solution)/shard_map/projectors/pallas_call | solution.py:235
  72.1 0.7 assemble.2
  72.8 1.6 %collective-permute-start.12 = (f32[48,16,128]{2,1,0:T(8,128)S(1)}, f32[48,16,128]{2,1,0:T(8,128)S(1)}, u32[]{:S(2)}, u32[]{:S(2)}) collective-permute-start(f32[48,16,128]{2,1,0:T(8,128)S(1)} %get-tuple-element.70), channel_id=1, source_target_pairs={{0,2},{2,0},{1,3},{3,1},{4,6},{6,4},{5,7},{7,5},{8,10},{10,8},{9,1... | collective-permute-start | bytes 1179656 | tf_op jit(solution)/shard_map/ppermute | solution.py:43
  74.4 0.0 collective-permute-done.8
  74.4 4.5 %collective-permute-done.9 = f32[3,128,128]{2,1,0:T(8,128)S(1)} collective-permute-done((f32[3,128,128]{2,1,0:T(8,128)S(1)}, f32[3,128,128]{2,1,0:T(8,128)S(1)}, u32[]{:S(2)}, u32[]{:S(2)}) %collective-permute-start.9) | collective-permute-done | bytes 196640 | tf_op jit(solution)/shard_map/ppermute | solution.py:43
  78.9 0.7 assemble.3
  79.6 1.6 %collective-permute-start.15 = (f32[48,16,128]{2,1,0:T(8,128)S(1)}, f32[48,16,128]{2,1,0:T(8,128)S(1)}, u32[]{:S(2)}, u32[]{:S(2)}) collective-permute-start(f32[48,16,128]{2,1,0:T(8,128)S(1)} %get-tuple-element.72), channel_id=1, source_target_pairs={{0,2},{2,0},{1,3},{3,1},{4,6},{6,4},{5,7},{7,5},{8,10},{10,8},{9,1... | collective-permute-start | bytes 1179656 | tf_op jit(solution)/shard_map/ppermute | solution.py:43
  81.1 0.0 collective-permute-start.11
  81.1 0.5 collective-permute-start.14
  81.6 2.8 %collective-permute-done.12.refs_2_ = f32[48,16,128]{2,1,0:T(8,128)S(1)} collective-permute-done((f32[48,16,128]{2,1,0:T(8,128)S(1)}, f32[48,16,128]{2,1,0:T(8,128)S(1)}, u32[]{:S(2)}, u32[]{:S(2)}) %collective-permute-start.12) | collective-permute-done | bytes 393248 | tf_op jit(solution)/shard_map/ppermute | solution.py:43
  84.4 4.7 %collective-permute-done.15.refs_6_ = f32[48,16,128]{2,1,0:T(8,128)S(1)} collective-permute-done((f32[48,16,128]{2,1,0:T(8,128)S(1)}, f32[48,16,128]{2,1,0:T(8,128)S(1)}, u32[]{:S(2)}, u32[]{:S(2)}) %collective-permute-start.15) | collective-permute-done | bytes 393248 | tf_op jit(solution)/shard_map/ppermute | solution.py:43
  89.1 0.0 collective-permute-start.16
  89.1 0.0 collective-permute-done.11.refs_1_
  89.1 0.0 collective-permute-done.14.refs_5_
  89.1 1.7 %collective-permute-done.16.refs_7_ = f32[48,16,128]{2,1,0:T(8,128)S(1)} collective-permute-done((f32[48,16,128]{2,1,0:T(8,128)S(1)}, f32[48,16,128]{2,1,0:T(8,128)S(1)}, u32[]{:S(2)}, u32[]{:S(2)}) %collective-permute-start.16) | collective-permute-done | bytes 393248 | tf_op jit(solution)/shard_map/ppermute | solution.py:43
  90.8 6.2 %products.1 = (f32[128,128]{1,0:T(8,128)S(1)}, f32[96,128]{1,0:T(8,128)S(1)}, f32[96,128]{1,0:T(8,128)S(1)}, f32[96,128]{1,0:T(8,128)S(1)}, f32[96,128]{1,0:T(8,...) custom-call(s32[4]{0:T(128)S(1)} %pad_add_fusion.place, bf16[576,6144]{1,0:T(8,128)(2,1)S(1)} %get-tuple-element.67.w_high, ...), custom_call_target="tpu_custom_call" | custom-call | tf_op jit(solution)/shard_map/products/pallas_call | solution.py:299
  97.0 1.6 %collective-permute-start.17 = (f32[96,128]{1,0:T(8,128)S(1)}, f32[96,128]{1,0:T(8,128)S(1)}, u32[]{:S(2)}, u32[]{:S(2)}) collective-permute-start(f32[96,128]{1,0:T(8,128)S(1)} %get-tuple-element.75), channel_id=1, source_target_pairs={{0,2},{2,0},{4,6},{6,4},{8,10},{10,8},{12,14},{14,12},{1,3},{3,1},... | collective-permute-start | bytes 147464 | tf_op jit(solution)/shard_map/ppermute | solution.py:489
  98.5 2.4 %collective-permute-start.18 = (f32[96,128]{1,0:T(8,128)S(1)}, f32[96,128]{1,0:T(8,128)S(1)}, u32[]{:S(2)}, u32[]{:S(2)}) collective-permute-start(f32[96,128]{1,0:T(8,128)S(1)} %get-tuple-element.76), channel_id=1, source_target_pairs={{0,12},{2,14},{4,0},{6,2},{8,4},{10,6},{12,8},{14,10},{1,13},{3,15... | collective-permute-start | bytes 147464 | tf_op jit(solution)/shard_map/ppermute | solution.py:489
  101.0 4.2 %collective-permute-start.19 = (f32[96,128]{1,0:T(8,128)S(1)}, f32[96,128]{1,0:T(8,128)S(1)}, u32[]{:S(2)}, u32[]{:S(2)}) collective-permute-start(f32[96,128]{1,0:T(8,128)S(1)} %get-tuple-element.77), channel_id=1, source_target_pairs={{0,14},{2,12},{4,2},{6,0},{8,6},{10,4},{12,10},{14,8},{1,15},{3,13... | collective-permute-start | bytes 147464 | tf_op jit(solution)/shard_map/ppermute | solution.py:489
  105.2 0.0 collective-permute-start.20
  105.2 0.2 collective-permute-start.21
  105.4 1.6 %collective-permute-done.19.refs_2_ = f32[96,128]{1,0:T(8,128)S(1)} collective-permute-done((f32[96,128]{1,0:T(8,128)S(1)}, f32[96,128]{1,0:T(8,128)S(1)}, u32[]{:S(2)}, u32[]{:S(2)}) %collective-permute-start.19) | collective-permute-done | bytes 49184 | tf_op jit(solution)/shard_map/ppermute | solution.py:489
  107.0 4.1 %collective-permute-done.20.refs_3_ = f32[96,128]{1,0:T(8,128)S(1)} collective-permute-done((f32[96,128]{1,0:T(8,128)S(1)}, f32[96,128]{1,0:T(8,128)S(1)}, u32[]{:S(2)}, u32[]{:S(2)}) %collective-permute-start.20) | collective-permute-done | bytes 49184 | tf_op jit(solution)/shard_map/ppermute | solution.py:489
  111.1 1.4 %collective-permute-done.21.refs_4_ = f32[96,128]{1,0:T(8,128)S(1)} collective-permute-done((f32[96,128]{1,0:T(8,128)S(1)}, f32[96,128]{1,0:T(8,128)S(1)}, u32[]{:S(2)}, u32[]{:S(2)}) %collective-permute-start.21) | collective-permute-done | bytes 49184 | tf_op jit(solution)/shard_map/ppermute | solution.py:489
  112.6 1.2 gram_share.1
  113.8 1.0 collective-permute-start.23
  114.8 0.0 collective-permute-start.24
  114.8 1.2 collective-permute-start.22
  116.0 1.6 %collective-permute-done.23 = f32[32,128]{1,0:T(8,128)S(1)} collective-permute-done((f32[32,128]{1,0:T(8,128)S(1)}, f32[32,128]{1,0:T(8,128)S(1)}, u32[]{:S(2)}, u32[]{:S(2)}) %collective-permute-start.23) | collective-permute-done | bytes 16416 | tf_op jit(solution)/shard_map/ppermute | solution.py:43
  117.6 0.4 collective-permute-done.24
  118.0 0.1 collective-permute-start.26
  118.0 2.1 %collective-permute-start.27 = (f32[32,128]{1,0:T(8,128)S(1)}, f32[32,128]{1,0:T(8,128)S(1)}, u32[]{:S(2)}, u32[]{:S(2)}) collective-permute-start(f32[32,128]{1,0:T(8,128)S(1)} %add_add_fusion.1), channel_id=1, source_target_pairs={{0,12},{4,8},{8,4},{12,0},{1,13},{5,9},{9,5},{13,1},{2,14},{6,10},... | collective-permute-start | bytes 49160 | tf_op jit(solution)/shard_map/ppermute | solution.py:43
  120.1 1.4 %collective-permute-start.25 = (f32[32,128]{1,0:T(8,128)S(1)}, f32[32,128]{1,0:T(8,128)S(1)}, u32[]{:S(2)}, u32[]{:S(2)}) collective-permute-start(f32[32,128]{1,0:T(8,128)S(1)} %add_add_fusion.1), channel_id=1, source_target_pairs={{0,4},{4,0},{8,12},{12,8},{1,5},{5,1},{9,13},{13,9},{2,6},{6,2},{1... | collective-permute-start | bytes 49160 | tf_op jit(solution)/shard_map/ppermute | solution.py:43
  121.5 1.2 %pad_maximum_fusion = f32[32,96,128]{2,1,0:T(8,128)} fusion(f32[16,96,128]{2,1,0:T(8,128)S(1)} %get-tuple-element.65, f32[16,96,128]{2,1,0:T(8,128)S(1)} %get-tuple-element.60), kind=kLoop, calls=%fused_computation | loop fusion | flops 393216 | bytes 3145728 | tf_op jit(solution)/shard_map/concatenate | solution.py:468
  122.8 0.9 collective-permute-done.27
  123.6 0.2 collective-permute-done.25
  123.9 0.6 add_add_fusion
  (19 shorter events, 0.1 us)
Async XLA Ops:
  0.6 8.2 %copy-start = (f32[48,8,8]{0,2,1:T(8,128)S(1)}, f32[48,8,8]{0,2,1:T(8,128)}, u32[]{:S(2)}) copy-start(f32[48,8,8]{0,2,1:T(8,128)} %param.9) | copy-start | bytes 36868
  0.7 2.3 %copy-start.3 = (f32[3,32,128]{2,1,0:T(8,128)S(1)}, f32[3,32,128]{2,1,0:T(8,128)}, u32[]{:S(2)}) copy-start(f32[3,32,128]{2,1,0:T(8,128)} %param.6) | copy-start | bytes 147460
  3.0 18.5 %collective-permute-start = (f32[864,128]{1,0:T(8,128)S(1)}, f32[864,128]{1,0:T(8,128)S(1)}, u32[]{:S(2)}, u32[]{:S(2)}) collective-permute-start(f32[864,128]{1,0:T(8,128)S(1)} %pad_maximum_fusion.1), channel_id=1, source_target_pairs={{0,4},{4,0},{8,12},{12,8},{1,5},{5,1},{9,13},{13,9},{2,6},{6,2},{1... | collective-permute-start | bytes 1327112 | tf_op jit(solution)/shard_map/ppermute | solution.py:43
  6.1 23.4 %collective-permute-start.1 = (f32[480,128]{1,0:T(8,128)S(1)}, f32[480,128]{1,0:T(8,128)S(1)}, u32[]{:S(2)}, u32[]{:S(2)}) collective-permute-start(f32[480,128]{1,0:T(8,128)S(1)} %get-tuple-element.93), channel_id=1, source_target_pairs={{0,8},{4,12},{8,0},{12,4},{1,9},{5,13},{9,1},{13,5},{2,10},{6,14},... | collective-permute-start | bytes 737288 | tf_op jit(solution)/shard_map/ppermute | solution.py:43
  8.8 21.4 %collective-permute-start.2 = (f32[480,128]{1,0:T(8,128)S(1)}, f32[480,128]{1,0:T(8,128)S(1)}, u32[]{:S(2)}, u32[]{:S(2)}) collective-permute-start(f32[480,128]{1,0:T(8,128)S(1)} %get-tuple-element.92), channel_id=1, source_target_pairs={{0,12},{4,8},{8,4},{12,0},{1,13},{5,9},{9,5},{13,1},{2,14},{6,10},... | collective-permute-start | bytes 737288 | tf_op jit(solution)/shard_map/ppermute | solution.py:43
  9.4 51.5 %copy-start.1 = (f32[48,3,8,128]{3,2,1,0:T(8,128)S(1)}, f32[48,3,8,128]{3,2,1,0:T(8,128)}, u32[]{:S(2)}) copy-start(f32[48,3,8,128]{3,2,1,0:T(8,128)} %coefs_ref.1) | copy-start | bytes 1769476
  9.4 51.5 %copy-start.2 = (s32[48,3,128]{2,0,1:T(8,128)S(1)}, s32[48,3,128]{2,0,1:T(8,128)}, u32[]{:S(2)}) copy-start(s32[48,3,128]{2,0,1:T(8,128)} %param.7) | copy-start | bytes 221188
  21.5 28.6 %collective-permute-start.6 = (f32[384,128]{1,0:T(8,128)}, f32[384,128]{1,0:T(8,128)S(1)}, u32[]{:S(2)}, u32[]{:S(2)}) collective-permute-start(f32[384,128]{1,0:T(8,128)} %get-tuple-element.50), channel_id=1, source_target_pairs={{0,8},{4,12},{8,0},{12,4},{1,9},{5,13},{9,1},{13,5},{2,10},{6,14},... | collective-permute-start | bytes 589832 | tf_op jit(solution)/shard_map/ppermute | solution.py:43
  24.5 25.6 %collective-permute-start.7 = (f32[384,128]{1,0:T(8,128)S(1)}, f32[384,128]{1,0:T(8,128)S(1)}, u32[]{:S(2)}, u32[]{:S(2)}) collective-permute-start(f32[384,128]{1,0:T(8,128)S(1)} %get-tuple-element.51), channel_id=1, source_target_pairs={{0,12},{4,8},{8,4},{12,0},{1,13},{5,9},{9,5},{13,1},{2,14},{6,10},... | collective-permute-start | bytes 589832 | tf_op jit(solution)/shard_map/ppermute | solution.py:43
  37.0 22.6 %collective-permute-start.3 = (f32[3,128,128]{2,1,0:T(8,128)S(1)}, f32[3,128,128]{2,1,0:T(8,128)S(1)}, u32[]{:S(2)}, u32[]{:S(2)}) collective-permute-start(f32[3,128,128]{2,1,0:T(8,128)S(1)} %get-tuple-element.45), channel_id=1, source_target_pairs={{0,4},{4,0},{8,12},{12,8},{1,5},{5,1},{9,13},{13,9},{2,6},{6,2},{1... | collective-permute-start | bytes 589832 | tf_op jit(solution)/shard_map/ppermute | solution.py:43
  47.4 24.7 %collective-permute-start.4 = (f32[3,128,128]{2,1,0:T(8,128)S(1)}, f32[3,128,128]{2,1,0:T(8,128)S(1)}, u32[]{:S(2)}, u32[]{:S(2)}) collective-permute-start(f32[3,128,128]{2,1,0:T(8,128)S(1)} %get-tuple-element.46), channel_id=1, source_target_pairs={{0,8},{4,12},{8,0},{12,4},{1,9},{5,13},{9,1},{13,5},{2,10},{6,14},... | collective-permute-start | bytes 589832 | tf_op jit(solution)/shard_map/ppermute | solution.py:43
  48.7 23.4 %collective-permute-start.5 = (f32[3,128,128]{2,1,0:T(8,128)S(1)}, f32[3,128,128]{2,1,0:T(8,128)S(1)}, u32[]{:S(2)}, u32[]{:S(2)}) collective-permute-start(f32[3,128,128]{2,1,0:T(8,128)S(1)} %get-tuple-element.47), channel_id=1, source_target_pairs={{0,12},{4,8},{8,4},{12,0},{1,13},{5,9},{9,5},{13,1},{2,14},{6,10},... | collective-permute-start | bytes 589832 | tf_op jit(solution)/shard_map/ppermute | solution.py:43
  56.5 17.9 %collective-permute-start.8 = (f32[3,128,128]{2,1,0:T(8,128)S(1)}, f32[3,128,128]{2,1,0:T(8,128)S(1)}, u32[]{:S(2)}, u32[]{:S(2)}) collective-permute-start(f32[3,128,128]{2,1,0:T(8,128)S(1)} %get-tuple-element.62), channel_id=1, source_target_pairs={{0,4},{4,0},{8,12},{12,8},{1,5},{5,1},{9,13},{13,9},{2,6},{6,2},{1... | collective-permute-start | bytes 589832 | tf_op jit(solution)/shard_map/ppermute | solution.py:43
  57.4 21.5 %collective-permute-start.9 = (f32[3,128,128]{2,1,0:T(8,128)S(1)}, f32[3,128,128]{2,1,0:T(8,128)S(1)}, u32[]{:S(2)}, u32[]{:S(2)}) collective-permute-start(f32[3,128,128]{2,1,0:T(8,128)S(1)} %get-tuple-element.63), channel_id=1, source_target_pairs={{0,8},{4,12},{8,0},{12,4},{1,9},{5,13},{9,1},{13,5},{2,10},{6,14},... | collective-permute-start | bytes 589832 | tf_op jit(solution)/shard_map/ppermute | solution.py:43
  59.6 19.3 %collective-permute-start.10 = (f32[3,128,128]{2,1,0:T(8,128)S(1)}, f32[3,128,128]{2,1,0:T(8,128)S(1)}, u32[]{:S(2)}, u32[]{:S(2)}) collective-permute-start(f32[3,128,128]{2,1,0:T(8,128)S(1)} %get-tuple-element.64), channel_id=1, source_target_pairs={{0,12},{4,8},{8,4},{12,0},{1,13},{5,9},{9,5},{13,1},{2,14},{6,10},... | collective-permute-start | bytes 589832 | tf_op jit(solution)/shard_map/ppermute | solution.py:43
  72.8 11.6 %collective-permute-start.12 = (f32[48,16,128]{2,1,0:T(8,128)S(1)}, f32[48,16,128]{2,1,0:T(8,128)S(1)}, u32[]{:S(2)}, u32[]{:S(2)}) collective-permute-start(f32[48,16,128]{2,1,0:T(8,128)S(1)} %get-tuple-element.70), channel_id=1, source_target_pairs={{0,2},{2,0},{1,3},{3,1},{4,6},{6,4},{5,7},{7,5},{8,10},{10,8},{9,1... | collective-permute-start | bytes 1179656 | tf_op jit(solution)/shard_map/ppermute | solution.py:43
  79.6 9.5 %collective-permute-start.15 = (f32[48,16,128]{2,1,0:T(8,128)S(1)}, f32[48,16,128]{2,1,0:T(8,128)S(1)}, u32[]{:S(2)}, u32[]{:S(2)}) collective-permute-start(f32[48,16,128]{2,1,0:T(8,128)S(1)} %get-tuple-element.72), channel_id=1, source_target_pairs={{0,2},{2,0},{1,3},{3,1},{4,6},{6,4},{5,7},{7,5},{8,10},{10,8},{9,1... | collective-permute-start | bytes 1179656 | tf_op jit(solution)/shard_map/ppermute | solution.py:43
  81.1 8.0 %collective-permute-start.11 = (f32[48,16,128]{2,1,0:T(8,128)S(1)}, f32[48,16,128]{2,1,0:T(8,128)S(1)}, u32[]{:S(2)}, u32[]{:S(2)}) collective-permute-start(f32[48,16,128]{2,1,0:T(8,128)S(1)} %get-tuple-element.69.refs_0_), channel_id=1, source_target_pairs={{0,1},{1,0},{2,3},{3,2},{4,5},{5,4},{6,7},{7,6},{8,9},{9,8},{10,11... | collective-permute-start | bytes 1179656 | tf_op jit(solution)/shard_map/ppermute | solution.py:43
  81.1 8.0 %collective-permute-start.14 = (f32[48,16,128]{2,1,0:T(8,128)S(1)}, f32[48,16,128]{2,1,0:T(8,128)S(1)}, u32[]{:S(2)}, u32[]{:S(2)}) collective-permute-start(f32[48,16,128]{2,1,0:T(8,128)S(1)} %get-tuple-element.71.refs_4_), channel_id=1, source_target_pairs={{0,1},{1,0},{2,3},{3,2},{4,5},{5,4},{6,7},{7,6},{8,9},{9,8},{10,11... | collective-permute-start | bytes 1179656 | tf_op jit(solution)/shard_map/ppermute | solution.py:43
  84.4 4.7 %collective-permute-start.13 = (f32[48,16,128]{2,1,0:T(8,128)S(1)}, f32[48,16,128]{2,1,0:T(8,128)S(1)}, u32[]{:S(2)}, u32[]{:S(2)}) collective-permute-start(f32[48,16,128]{2,1,0:T(8,128)S(1)} %collective-permute-done.12.refs_2_), channel_id=1, source_target_pairs={{0,1},{1,0},{2,3},{3,2},{4,5},{5,4},{6,7},{7,6},{8,9},{9,8},{10,11... | collective-permute-start | bytes 1179656 | tf_op jit(solution)/shard_map/ppermute | solution.py:43
  89.1 1.7 %collective-permute-start.16 = (f32[48,16,128]{2,1,0:T(8,128)S(1)}, f32[48,16,128]{2,1,0:T(8,128)S(1)}, u32[]{:S(2)}, u32[]{:S(2)}) collective-permute-start(f32[48,16,128]{2,1,0:T(8,128)S(1)} %collective-permute-done.15.refs_6_), channel_id=1, source_target_pairs={{0,1},{1,0},{2,3},{3,2},{4,5},{5,4},{6,7},{7,6},{8,9},{9,8},{10,11... | collective-permute-start | bytes 1179656 | tf_op jit(solution)/shard_map/ppermute | solution.py:43
  97.0 8.4 %collective-permute-start.17 = (f32[96,128]{1,0:T(8,128)S(1)}, f32[96,128]{1,0:T(8,128)S(1)}, u32[]{:S(2)}, u32[]{:S(2)}) collective-permute-start(f32[96,128]{1,0:T(8,128)S(1)} %get-tuple-element.75), channel_id=1, source_target_pairs={{0,2},{2,0},{4,6},{6,4},{8,10},{10,8},{12,14},{14,12},{1,3},{3,1},... | collective-permute-start | bytes 147464 | tf_op jit(solution)/shard_map/ppermute | solution.py:489
  98.5 6.9 %collective-permute-start.18 = (f32[96,128]{1,0:T(8,128)S(1)}, f32[96,128]{1,0:T(8,128)S(1)}, u32[]{:S(2)}, u32[]{:S(2)}) collective-permute-start(f32[96,128]{1,0:T(8,128)S(1)} %get-tuple-element.76), channel_id=1, source_target_pairs={{0,12},{2,14},{4,0},{6,2},{8,4},{10,6},{12,8},{14,10},{1,13},{3,15... | collective-permute-start | bytes 147464 | tf_op jit(solution)/shard_map/ppermute | solution.py:489
  101.0 6.0 %collective-permute-start.19 = (f32[96,128]{1,0:T(8,128)S(1)}, f32[96,128]{1,0:T(8,128)S(1)}, u32[]{:S(2)}, u32[]{:S(2)}) collective-permute-start(f32[96,128]{1,0:T(8,128)S(1)} %get-tuple-element.77), channel_id=1, source_target_pairs={{0,14},{2,12},{4,2},{6,0},{8,6},{10,4},{12,10},{14,8},{1,15},{3,13... | collective-permute-start | bytes 147464 | tf_op jit(solution)/shard_map/ppermute | solution.py:489
  105.2 5.9 %collective-permute-start.20 = (f32[96,128]{1,0:T(8,128)S(1)}, f32[96,128]{1,0:T(8,128)S(1)}, u32[]{:S(2)}, u32[]{:S(2)}) collective-permute-start(f32[96,128]{1,0:T(8,128)S(1)} %get-tuple-element.78), channel_id=1, source_target_pairs={{0,4},{2,6},{4,8},{6,10},{8,12},{10,14},{12,0},{14,2},{1,5},{3,7},... | collective-permute-start | bytes 147464 | tf_op jit(solution)/shard_map/ppermute | solution.py:489
  105.2 7.3 %collective-permute-start.21 = (f32[96,128]{1,0:T(8,128)S(1)}, f32[96,128]{1,0:T(8,128)S(1)}, u32[]{:S(2)}, u32[]{:S(2)}) collective-permute-start(f32[96,128]{1,0:T(8,128)S(1)} %get-tuple-element.79), channel_id=1, source_target_pairs={{0,6},{2,4},{4,10},{6,8},{8,14},{10,12},{12,2},{14,0},{1,7},{3,5},... | collective-permute-start | bytes 147464 | tf_op jit(solution)/shard_map/ppermute | solution.py:489
  113.8 3.8 %collective-permute-start.23 = (f32[32,128]{1,0:T(8,128)S(1)}, f32[32,128]{1,0:T(8,128)S(1)}, u32[]{:S(2)}, u32[]{:S(2)}) collective-permute-start(f32[32,128]{1,0:T(8,128)S(1)} %get-tuple-element.82), channel_id=1, source_target_pairs={{0,2},{1,3},{2,0},{3,1},{4,6},{5,7},{6,4},{7,5},{8,10},{9,11},{10,... | collective-permute-start | bytes 49160 | tf_op jit(solution)/shard_map/ppermute | solution.py:43
  114.8 3.2 %collective-permute-start.24 = (f32[32,128]{1,0:T(8,128)S(1)}, f32[32,128]{1,0:T(8,128)S(1)}, u32[]{:S(2)}, u32[]{:S(2)}) collective-permute-start(f32[32,128]{1,0:T(8,128)S(1)} %get-tuple-element.83), channel_id=1, source_target_pairs={{0,3},{1,2},{2,1},{3,0},{4,7},{5,6},{6,5},{7,4},{8,11},{9,10},{10,... | collective-permute-start | bytes 49160 | tf_op jit(solution)/shard_map/ppermute | solution.py:43
  114.8 3.2 %collective-permute-start.22 = (f32[32,128]{1,0:T(8,128)S(1)}, f32[32,128]{1,0:T(8,128)S(1)}, u32[]{:S(2)}, u32[]{:S(2)}) collective-permute-start(f32[32,128]{1,0:T(8,128)S(1)} %get-tuple-element.81), channel_id=1, source_target_pairs={{0,1},{1,0},{2,3},{3,2},{4,5},{5,4},{6,7},{7,6},{8,9},{9,8},{10,11... | collective-permute-start | bytes 49160 | tf_op jit(solution)/shard_map/ppermute | solution.py:43
  118.0 4.8 %collective-permute-start.26 = (f32[32,128]{1,0:T(8,128)S(1)}, f32[32,128]{1,0:T(8,128)S(1)}, u32[]{:S(2)}, u32[]{:S(2)}) collective-permute-start(f32[32,128]{1,0:T(8,128)S(1)} %add_add_fusion.1), channel_id=1, source_target_pairs={{0,8},{4,12},{8,0},{12,4},{1,9},{5,13},{9,1},{13,5},{2,10},{6,14},... | collective-permute-start | bytes 49160 | tf_op jit(solution)/shard_map/ppermute | solution.py:43
  118.0 5.6 %collective-permute-start.27 = (f32[32,128]{1,0:T(8,128)S(1)}, f32[32,128]{1,0:T(8,128)S(1)}, u32[]{:S(2)}, u32[]{:S(2)}) collective-permute-start(f32[32,128]{1,0:T(8,128)S(1)} %add_add_fusion.1), channel_id=1, source_target_pairs={{0,12},{4,8},{8,4},{12,0},{1,13},{5,9},{9,5},{13,1},{2,14},{6,10},... | collective-permute-start | bytes 49160 | tf_op jit(solution)/shard_map/ppermute | solution.py:43
  120.1 3.7 %collective-permute-start.25 = (f32[32,128]{1,0:T(8,128)S(1)}, f32[32,128]{1,0:T(8,128)S(1)}, u32[]{:S(2)}, u32[]{:S(2)}) collective-permute-start(f32[32,128]{1,0:T(8,128)S(1)} %add_add_fusion.1), channel_id=1, source_target_pairs={{0,4},{4,0},{8,12},{12,8},{1,5},{5,1},{9,13},{13,9},{2,6},{6,2},{1... | collective-permute-start | bytes 49160 | tf_op jit(solution)/shard_map/ppermute | solution.py:43

commit v6 on v5

--- a/solution.py
+++ b/solution.py
@@ -140,47 +140,65 @@
     )(place, *given, *blocks)
 
 
-def assemble_kernel(n_dom, n_band, place, *refs):
-    pieces, orbital_first, parts = refs[:n_dom], refs[n_dom], refs[n_dom + 1 :]
-    cells = orbital_first.shape[1]
-    share = cells // n_band
+def cell_first_kernel(n_band, place, *refs):
+    pieces, parts = refs[:-n_band], refs[-n_band:]
+    share = parts[0].shape[0]
     me = place[ME]
-    for m, piece in enumerate(pieces):
-        start = (me ^ m) * TOGETHER
-        for t in range(TOGETHER):
-            orbital_first[start + t] = piece[pl.ds(t, cells, stride=TOGETHER), :]
-    per_load = SUBLANES // TOGETHER
     together = SUBLANES // TOGETHER
+    tiles = len(pieces) // together
     for p, part in enumerate(parts):
         base = pl.multiple_of((place[BAND] ^ p) * (share * TOGETHER), SUBLANES)
-        for first in range(0, share, per_load):
-            loaded = [
-                piece[pl.ds(base + first * TOGETHER, SUBLANES), :] for piece in pieces
-            ]
-            for k in range(per_load):
+        for first in range(0, share, together):
+            loaded = [piece[pl.ds(base + first * TOGETHER, SUBLANES), :] for piece in pieces]
+            for k in range(together):
                 here = slice(k * TOGETHER, (k + 1) * TOGETHER)
-                for q in range(n_dom // together):
+                for q in range(tiles):
                     tile = jnp.concatenate(
                         [loaded[q * together + i][here] for i in range(together)], axis=0
                     )
                     tile = jnp.where((me & 1) != 0, pltpu.roll(tile, TOGETHER, 0), tile)
-                    row = pl.multiple_of((q ^ (me // together)) * SUBLANES, SUBLANES)
-                    part[first + k, pl.ds(row, SUBLANES), :] = tile
-
-
-def assemble(place, n_band, pieces):
-    n_dom = len(pieces)
-    planes, rows, lanes = pieces[0].shape
-    cells, orbitals = planes * rows // TOGETHER, n_dom * TOGETHER
-    part = jax.ShapeDtypeStruct((cells // n_band, orbitals, lanes), jnp.float32)
+                    if tiles == 1:
+                        part[first + k] = tile
+                    else:
+                        row = pl.multiple_of((q ^ (me // together)) * SUBLANES, SUBLANES)
+                        part[first + k, pl.ds(row, SUBLANES), :] = tile
+
+
+def cell_first(place, n_band, pieces):
+    rows, lanes = pieces[0].shape
+    orbitals = len(pieces) * TOGETHER
+    part = jax.ShapeDtypeStruct((rows // (TOGETHER * n_band), orbitals, lanes), jnp.float32)
     return pl.pallas_call(
-        functools.partial(assemble_kernel, n_dom, n_band),
-        out_shape=[jax.ShapeDtypeStruct((orbitals, cells, lanes), jnp.float32)] + [part] * n_band,
-        in_specs=[SMEM] + [VMEM] * n_dom,
-        out_specs=[VMEM] * (1 + n_band),
+        functools.partial(cell_first_kernel, n_band),
+        out_shape=[part] * n_band,
+        in_specs=[SMEM] + [VMEM] * len(pieces),
+        out_specs=[VMEM] * n_band,
         compiler_params=params(8),
-        name="assemble",
-    )(place, *[piece.reshape(planes * rows, lanes) for piece in pieces])
+        name="cell_first",
+    )(place, *pieces)
+
+
+def orbital_first_kernel(n_dom, place, *refs):
+    *pieces, out = refs
+    cells = out.shape[1]
+    for k, piece in enumerate(pieces):
+        chunk, m = divmod(k, n_dom)
+        start = (chunk * n_dom + (place[ME] ^ m)) * TOGETHER
+        for t in range(TOGETHER):
+            out[start + t] = piece[pl.ds(t, cells, stride=TOGETHER), :]
+
+
+def orbital_first(place, n_dom, pieces):
+    rows, lanes = pieces[0].shape
+    shape = (len(pieces) * TOGETHER, rows // TOGETHER, lanes)
+    return pl.pallas_call(
+        functools.partial(orbital_first_kernel, n_dom),
+        out_shape=jax.ShapeDtypeStruct(shape, jnp.float32),
+        in_specs=[SMEM] + [VMEM] * len(pieces),
+        out_specs=VMEM,
+        compiler_params=params(8),
+        name="orbital_first",
+    )(place, *pieces)
 
 
 def projector_kernel(n_band, n_sub, place, offsets_ref, coefs_ref, high_out, low_out):
@@ -194,7 +212,7 @@
     lane_index = lax.broadcasted_iota(jnp.int32, (lanes, spread), 0)
 
     def two_atoms(step, carry):
-        shell = step // (n_band * pairs)
+        shell = lax.rem(2 * (step // (n_band * pairs)), shells)
         band = place[BAND] ^ ((step // pairs) % n_band)
         first_atom = (place[SUB] * n_band + band) * own + 2 * (step % pairs)
         dense = []
@@ -247,21 +265,20 @@
     )(place, offsets.swapaxes(0, 1), coefs)
 
 
-def product_kernel(n_chunks, n_sub, n_blocks, place, w_high, w_low, *refs):
+def product_kernel(spots, n_sub, first_row, n_blocks, with_grid, place, w_high, w_low, *refs):
     refs, proj_out = refs[:-1], refs[-1]
-    fields, grid_out, outs = refs[: -n_blocks - 1], refs[-n_blocks - 1], refs[-n_blocks:]
-    orbitals = grid_out.shape[0]
-    cells, _, lanes = fields[0].shape
-    n_groups = len(fields) // n_chunks
+    n_outs = n_blocks + (1 if with_grid else 0)
+    arrays, outs = refs[:-n_outs], list(refs[-n_outs:])
+    rows, orbitals = proj_out.shape
+    cells, _, lanes = arrays[0].shape
     block = 12
 
     def parts(start):
         highs, lows = [], []
-        for g in range(n_groups):
-            for c in range(n_chunks):
-                high, low = split_bf16(fields[c * n_groups + g][pl.ds(start, block)])
-                highs.append(jnp.concatenate([high[k] for k in range(block)], axis=1))
-                lows.append(jnp.concatenate([low[k] for k in range(block)], axis=1))
+        for at, first, width in spots:
+            high, low = split_bf16(arrays[at][pl.ds(start, block), first : first + width])
+            highs.append(jnp.concatenate([high[k] for k in range(block)], axis=1))
+            lows.append(jnp.concatenate([low[k] for k in range(block)], axis=1))
         return jnp.concatenate(highs, axis=0), jnp.concatenate(lows, axis=0)
 
     def product(left_high, left_low, high, low):
@@ -270,41 +287,48 @@
         narrow = lax.dot_general(left_low, high, NT, preferred_element_type=jnp.float32)
         return wide[:, :orbitals] + wide[:, orbitals:] + narrow
 
-    def grid_block(step, carry):
-        high, low = parts(place[SUB] * (cells // n_sub) + step * block)
-        grid_out[...] += product(high, low, high, low)
-        return carry
+    if with_grid:
+        grid_out = outs.pop(0)
+        grid_out[...] = jnp.zeros_like(grid_out)
+
+        def grid_block(step, carry):
+            high, low = parts(place[SUB] * (cells // n_sub) + step * block)
+            grid_out[...] += product(high, low, high, low)
+            return carry
+
+        lax.fori_loop(0, cells // (n_sub * block), grid_block, 0)
 
     def proj_block(step, carry):
         high, low = parts(step * block)
         depth = block * lanes
         here = pl.ds(pl.multiple_of(step * depth, depth), depth)
-        proj_out[...] += product(w_high[:, here], w_low[:, here], high, low)
+        some = slice(first_row, first_row + rows)
+        proj_out[...] += product(w_high[some, here], w_low[some, here], high, low)
         return carry
 
-    grid_out[...] = jnp.zeros_like(grid_out)
     proj_out[...] = jnp.zeros_like(proj_out)
-    lax.fori_loop(0, cells // (n_sub * block), grid_block, 0)
     lax.fori_loop(0, cells // block, proj_block, 0)
-    rows = outs[0].shape[0]
     for k, out in enumerate(outs):
-        out[...] = proj_out[k * rows : (k + 1) * rows, :]
-
-
-def products(n_sub, n_blocks, place, projectors, fields):
-    rows = projectors[0].shape[0]
-    n_chunks, n_groups = len(fields), len(fields[0])
-    orbitals = n_chunks * n_groups * fields[0][0].shape[1]
+        out[...] = proj_out[k * (rows // n_blocks) : (k + 1) * (rows // n_blocks), :]
+
+
+def products(n_sub, first_row, rows, n_blocks, with_grid, place, projectors, arrays, spots):
+    orbitals = sum(width for _, _, width in spots)
+    grid = [jax.ShapeDtypeStruct((orbitals, orbitals), jnp.float32)] if with_grid else []
     block = jax.ShapeDtypeStruct((rows // n_blocks, orbitals), jnp.float32)
+    flops = 12 * rows * orbitals * projectors[0].shape[1]
     return pl.pallas_call(
-        functools.partial(product_kernel, n_chunks, n_sub, n_blocks),
-        out_shape=[jax.ShapeDtypeStruct((orbitals, orbitals), jnp.float32)] + [block] * n_blocks,
-        in_specs=[SMEM] + [VMEM] * (2 + n_chunks * n_groups),
-        out_specs=[VMEM] * (1 + n_blocks),
+        functools.partial(product_kernel, spots, n_sub, first_row, n_blocks, with_grid),
+        out_shape=grid + [block] * n_blocks,
+        in_specs=[SMEM] + [VMEM] * (2 + len(arrays)),
+        out_specs=[VMEM] * (len(grid) + n_blocks),
         scratch_shapes=[pltpu.VMEM((rows, orbitals), jnp.float32)],
         compiler_params=params(8),
+        cost_estimate=pl.CostEstimate(
+            flops=flops, bytes_accessed=4 * rows * projectors[0].shape[1], transcendentals=0
+        ),
         name="products",
-    )(place, *projectors, *[field for chunk in fields for field in chunk])
+    )(place, *projectors, *arrays)
 
 
 def reordered(x, width, by):
@@ -366,26 +390,29 @@
     levels = potential.reshape(cells, lanes)
     size = TOGETHER * cells
     n_chunks = orbitals // (n_dom * TOGETHER)
-    own = []
-    for m in range(n_dom):
-        blocks = [
-            lax.dynamic_slice_in_dim(flat, (c * n_dom + (me ^ m)) * size, size, 0)
-            for c in range(n_chunks)
-        ]
-        blocks[0] = jnp.concatenate([blocks[0], levels], axis=0)
-        own.append(blocks)
-    near = swapped(jnp.concatenate(own[1], axis=0), "dom", n_dom, 1)
-    arrived = [
-        [own[0][c], near] + [swapped(own[m][c], "dom", n_dom, m) for m in range(2, n_dom)]
-        for c in range(1)
-    ]
+
+    def block(c, m):
+        return lax.dynamic_slice_in_dim(flat, (c * n_dom + (me ^ m)) * size, size, 0)
+
+    def sent(x, m):
+        return swapped(x, "dom", n_dom, m)
+
+    far = [jnp.concatenate([block(0, m), levels], axis=0) for m in range(2, n_dom)]
+    far, flat, levels = lax.optimization_barrier((far, flat, levels))
+    near = [block(0, 1), levels] + [block(c, 1) for c in range(1, n_chunks)]
+    near = sent(jnp.concatenate(near, axis=0), 1)
+    own = [block(c, 0) for c in range(n_chunks)]
+    own[0] = jnp.concatenate([own[0], levels], axis=0)
+    arrived = [[own[0], near] + [sent(x, m) for m, x in enumerate(far, start=2)]]
     for c in range(1, n_chunks):
-        far = [own[m][c] for m in range(2, n_dom)]
-        near, far = lax.optimization_barrier((near, far))
-        arrived.append(
-            [own[0][c], near]
-            + [swapped(b, "dom", n_dom, m) for m, b in enumerate(far, start=2)]
-        )
+        blocks = [own[c], near]
+        for m in range(2, n_dom):
+            x = block(c, m)
+            arrived[c - 1][m - 1], x = lax.optimization_barrier((arrived[c - 1][m - 1], x))
+            blocks.append(sent(x, m))
+        arrived.append(blocks)
+    for blocks in arrived:
+        blocks[1] = arrived[0][1]
     diagonal = None
     done = []
     for c, blocks in enumerate(arrived):
@@ -396,7 +423,8 @@
             diagonal = filtered[n_dom]
         done.append(filtered[:n_dom])
     return [
-        [swapped(b, "dom", n_dom, m) if m else b for m, b in enumerate(blocks)] for blocks in done
+        [(sent(x, m) if m else x).reshape(size, lanes) for m, x in enumerate(blocks)]
+        for blocks in done
     ]
 
 
@@ -445,39 +473,63 @@
     def build(offsets):
         return build_projectors(n_band, n_sub, place, offsets, point_coefs, share, lanes)
 
+    place, corr_matrix = lax.optimization_barrier((place, corr_matrix))
+
+    def build(offsets):
+        return build_projectors(n_band, n_sub, place, offsets, point_coefs, share, lanes)
+
     filtered, parts = [], []
     if n_dom in (2, 4) and orbitals % (n_dom * TOGETHER) == 0 and planes * n_dom % 2 == 0:
         chunks = whole_columns(panel, potential, place, me)
         chunks[-1][0], point_offsets = lax.optimization_barrier((chunks[-1][0], point_offsets))
         projectors = build(point_offsets)
         chunks[0], projectors = lax.optimization_barrier((chunks[0], projectors))
-        for pieces in chunks:
-            orbital_first, *by_band = assemble(place, n_band, pieces)
-            filtered.append(orbital_first)
-            parts.append(by_band)
+        filtered = orbital_first(place, n_dom, [piece for pieces in chunks for piece in pieces])
+        parts = [cell_first(place, n_band, pieces) for pieces in chunks]
     else:
         projectors = build(point_offsets)
-        filtered = [plane_by_plane(panel, potential)]
-        cell_first = filtered[0].reshape(orbitals, cells, lanes).swapaxes(0, 1)
+        filtered = plane_by_plane(panel, potential)
+        by_cell = filtered.reshape(orbitals, cells, lanes).swapaxes(0, 1)
         parts = [
             [
-                lax.dynamic_slice_in_dim(cell_first, (band ^ m) * share, share, 0)
+                lax.dynamic_slice_in_dim(by_cell, (band ^ m) * share, share, 0)
                 for m in range(n_band)
             ]
         ]
-    filtered = jnp.concatenate(filtered, axis=0).reshape(panel.shape)
-    fields = []
-    for by_band in parts:
-        chunk = []
-        for m in range(n_band):
-            here = swapped(by_band[m], "band", n_band, m) if m else by_band[0]
-            chunk += [here] + [swapped(here, "sub", n_sub, k) for k in range(1, n_sub)]
-        fields.append(chunk)
-
-    grid_part, *proj = products(n_sub, 3 * n_band, place, projectors, fields)
+    filtered = filtered.reshape(panel.shape)
+    chunks = len(parts)
+    arrays = [x for by_band in parts for x in by_band[:1]]
+    arrays += [
+        swapped(by_band[m], "band", n_band, m) for by_band in parts for m in range(1, n_band)
+    ]
+    pieces = [jnp.concatenate(arrays[:chunks], axis=1)] + arrays[chunks:]
+    arrays += [swapped(x, "sub", n_sub, k) for k in range(1, n_sub) for x in pieces]
+    width = arrays[0].shape[1]
+    spots = []
+    for m in range(n_band):
+        for k in range(n_sub):
+            for c in range(chunks):
+                at = chunks + c * (n_band - 1) + m - 1 if m else c
+                if k == 0:
+                    spots.append((at, 0, width))
+                else:
+                    base = chunks * n_band + (k - 1) * len(pieces)
+                    if m:
+                        spots.append((base + 1 + at - chunks, 0, width))
+                    else:
+                        spots.append((base, c * width, width))
+
+    rows = own_atoms * channels * n_band
+    outer = products(
+        n_sub, 0, 2 * rows, 2 * n_band, False, place, projectors, arrays, spots
+    )
+    outer, place = lax.optimization_barrier((outer, place))
+    grid_part, *inner = products(
+        n_sub, 2 * rows, rows, n_band, True, place, projectors, arrays, spots
+    )
     sums, seen = [], []
-    for shell, by in ((1, 0), (0, 1), (2, -1)):
-        for m in range(n_band):
+    for by, blocks in ((1, outer[:n_band]), (-1, outer[n_band:]), (0, inner)):
+        for m, x in enumerate(blocks):
             if by == 0 and m == 0:
                 continue
             pairs = [
@@ -486,11 +538,11 @@
                 for b in range(n_band)
             ]
             seen.append(m * n_sub)
-            sums.append(lax.ppermute(proj[shell * n_band + m], ("dom", "band"), pairs))
+            sums.append(lax.ppermute(x, ("dom", "band"), pairs))
     scale_point = 1.0 / (cells * lanes * n_dom)
     scale_atom = 1.0 / math.sqrt(own_atoms * groups * n_dom)
     shares = gram_share(
-        (scale_point, scale_atom), groups, seen, place, corr_matrix, grid_part, proj[n_band], sums
+        (scale_point, scale_atom), groups, seen, place, corr_matrix, grid_part, inner[0], sums
     )
     gram_rows = added(
         [swapped(x, ("band", "sub"), groups, m) if m else x for m, x in enumerate(shares)]

time: 125 us -> 128 us (1.024)
  Pallas kernels: 33.1 us -> 37.5 us
  starting transfers between devices: 49 us -> 47.1 us
  waiting for transfers between devices: 36.6 us -> 38 us
    ppermute x23 -> x22, waiting for transfers between devices: 29.5 us -> 34.7 us  [swapped(): return lax.ppermute(x, axes, [(i, i ^ by) for i in range(size)])]
    ppermute x5, waiting for transfers between devices: 7.16 us -> 3.3 us  [on_device(): sums.append(lax.ppermute(x, ('dom', 'band'), pairs))]
    pallas_call x3 -> x5, Pallas kernels: 7.54 us -> 10.8 us  [the longest x2 7.71 us: products(): pl.pallas_call(functools.partial(product_kernel, spots, n_sub, first_row,...]
    ppermute x23 -> x22, starting transfers between devices: 40.6 us -> 39.1 us  [swapped(): return lax.ppermute(x, axes, [(i, i ^ by) for i in range(size)])]
  transfers between devices with their start and end apart: 28 -> 27, of which waited for: 13 -> 12; matrix products, arithmetic and copies ran while one was open for 2% -> 1% of each run, Pallas kernels for 21% -> 25%
where the time goes in v6:
time: 128 us
  starting transfers between devices  47.1 us (37%)
  waiting for transfers between devices  38 us (30%)
  Pallas kernels  37.5 us (29%)
  local copies, waits for them, and re-layouts  2.51 us (2%)
  other arithmetic  1.87 us (1%)
    ppermute x22, starting transfers between devices, swapped(): return lax.ppermute(x, axes, [(i, i ^ by) for i in range(size)])  39.1 us
    ppermute x22, waiting for transfers between devices, swapped(): return lax.ppermute(x, axes, [(i, i ^ by) for i in range(size)])  34.7 us
    pallas_call x2, Pallas kernels, filter_orbitals(): pl.pallas_call(functools.partial(filter_kernel, n_dom, planes, rows, star...  14 us
    pallas_call x1, Pallas kernels, build_projectors(): pl.pallas_call(functools.partial(projector_kernel, n_band, n_sub), out_sh...  11.5 us
    ppermute x5, starting transfers between devices, on_device(): sums.append(lax.ppermute(x, ('dom', 'band'), pairs))  7.92 us
    pallas_call x2, Pallas kernels, products(): pl.pallas_call(functools.partial(product_kernel, spots, n_sub, first_row,...  7.71 us
    ppermute x5, waiting for transfers between devices, on_device(): sums.append(lax.ppermute(x, ('dom', 'band'), pairs))  3.3 us
  transfers between devices with their start and end apart: 27, of which 12 were waited for; matrix products, arithmetic and copies ran while one was open for 1% of the time, Pallas kernels for 25%

profile of v6, /device:TPU:0, one launch (start us, length us, event | category | flops | bytes accessed | tf_op | source)
XLA Modules:
  0.0 127.8 jit_solution(2721106216167663604)
XLA Ops:
  0.6 0.0 copy-start
  0.7 1.2 constant_dynamic-slice_fusion.6
  1.9 0.0 copy-start.4
  1.9 0.9 pad_maximum_fusion.2
  2.8 0.8 constant_dynamic-slice_fusion
  3.7 3.1 %collective-permute-start = (f32[864,128]{1,0:T(8,128)S(1)}, f32[864,128]{1,0:T(8,128)S(1)}, u32[]{:S(2)}, u32[]{:S(2)}) collective-permute-start(f32[864,128]{1,0:T(8,128)S(1)} %pad_maximum_fusion.1), channel_id=1, source_target_pairs={{0,4},{4,0},{8,12},{12,8},{1,5},{5,1},{9,13},{13,9},{2,6},{6,2},{1... | collective-permute-start | bytes 1327112 | tf_op jit(solution)/shard_map/ppermute | solution.py:43
  6.8 2.6 %collective-permute-start.1 = (f32[480,128]{1,0:T(8,128)S(1)}, f32[480,128]{1,0:T(8,128)S(1)}, u32[]{:S(2)}, u32[]{:S(2)}) collective-permute-start(f32[480,128]{1,0:T(8,128)S(1)} %get-tuple-element.55), channel_id=1, source_target_pairs={{0,8},{4,12},{8,0},{12,4},{1,9},{5,13},{9,1},{13,5},{2,10},{6,14},... | collective-permute-start | bytes 737288 | tf_op jit(solution)/shard_map/ppermute | solution.py:43
  9.4 0.0 collective-permute-start.2
  9.4 0.1 constant_dynamic-slice_fusion.8
  9.5 0.1 copy.8
  9.6 0.1 broadcast_multiply_fusion
  9.7 0.3 mul.56.corr_ref
  10.0 0.1 pad_add_fusion.place
  10.1 0.0 copy-start.1
  10.1 0.0 copy-start.2
  10.1 12.5 %collective-permute-done.1.refs_2_ = f32[480,128]{1,0:T(8,128)S(1)} collective-permute-done((f32[480,128]{1,0:T(8,128)S(1)}, f32[480,128]{1,0:T(8,128)S(1)}, u32[]{:S(2)}, u32[]{:S(2)}) %collective-permute-start.1) | collective-permute-done | bytes 245792 | tf_op jit(solution)/shard_map/ppermute | solution.py:43
  22.7 2.5 %collective-permute-start.7 = (f32[384,128]{1,0:T(8,128)}, f32[384,128]{1,0:T(8,128)S(1)}, u32[]{:S(2)}, u32[]{:S(2)}) collective-permute-start(f32[384,128]{1,0:T(8,128)} %get-tuple-element.64), channel_id=1, source_target_pairs={{0,12},{4,8},{8,4},{12,0},{1,13},{5,9},{9,5},{13,1},{2,14},{6,10},... | collective-permute-start | bytes 589832 | tf_op jit(solution)/shard_map/ppermute | solution.py:43
  25.1 0.0 collective-permute-done.refs_1_.refs_2_
  25.1 2.5 %collective-permute-start.6 = (f32[384,128]{1,0:T(8,128)S(1)}, f32[384,128]{1,0:T(8,128)S(1)}, u32[]{:S(2)}, u32[]{:S(2)}) collective-permute-start(f32[384,128]{1,0:T(8,128)S(1)} %copy-done.5), channel_id=1, source_target_pairs={{0,8},{4,12},{8,0},{12,4},{1,9},{5,13},{9,1},{13,5},{2,10},{6,14},... | collective-permute-start | bytes 589832 | tf_op jit(solution)/shard_map/ppermute | solution.py:43
  27.7 3.2 %collective-permute-done.2.refs_3_ = f32[480,128]{1,0:T(8,128)S(1)} collective-permute-done((f32[480,128]{1,0:T(8,128)S(1)}, f32[480,128]{1,0:T(8,128)S(1)}, u32[]{:S(2)}, u32[]{:S(2)}) %collective-permute-start.2) | collective-permute-done | bytes 245792 | tf_op jit(solution)/shard_map/ppermute | solution.py:43
  30.9 7.2 %chebyshev.2 = (f32[3,128,128]{2,1,0:T(8,128)S(1)}, f32[3,128,128]{2,1,0:T(8,128)S(1)}, f32[3,128,128]{2,1,0:T(8,128)S(1)}, f32[3,128,128]{2,1,0:T(8,128)S(1)}, f32[6,32,8,128]{3,2,1,0:T(8,128)S(1)}) custom-call(s32[4]{0:T(128)S(1)} %pad_add_fusion.place, f32[480,128]{1,0:T(8,128)S(1)} %pad_maximum_fusion.4.refs_0_, ...), custom_call_target="tpu_custom_call" | custom-call | flops 28311552 | bytes 1572864 | tf_op jit(solution)/shard_map/chebyshev/pallas_call | solution.py:129
  38.1 10.2 %collective-permute-start.3 = (f32[3,128,128]{2,1,0:T(8,128)S(1)}, f32[3,128,128]{2,1,0:T(8,128)S(1)}, u32[]{:S(2)}, u32[]{:S(2)}) collective-permute-start(f32[3,128,128]{2,1,0:T(8,128)S(1)} %get-tuple-element.59), channel_id=1, source_target_pairs={{0,4},{4,0},{8,12},{12,8},{1,5},{5,1},{9,13},{13,9},{2,6},{6,2},{1... | collective-permute-start | bytes 589832 | tf_op jit(solution)/shard_map/ppermute | solution.py:43
  48.3 1.4 %collective-permute-start.4 = (f32[3,128,128]{2,1,0:T(8,128)S(1)}, f32[3,128,128]{2,1,0:T(8,128)S(1)}, u32[]{:S(2)}, u32[]{:S(2)}) collective-permute-start(f32[3,128,128]{2,1,0:T(8,128)S(1)} %get-tuple-element.60), channel_id=1, source_target_pairs={{0,8},{4,12},{8,0},{12,4},{1,9},{5,13},{9,1},{13,5},{2,10},{6,14},... | collective-permute-start | bytes 589832 | tf_op jit(solution)/shard_map/ppermute | solution.py:43
  49.7 1.4 %collective-permute-start.5 = (f32[3,128,128]{2,1,0:T(8,128)S(1)}, f32[3,128,128]{2,1,0:T(8,128)S(1)}, u32[]{:S(2)}, u32[]{:S(2)}) collective-permute-start(f32[3,128,128]{2,1,0:T(8,128)S(1)} %get-tuple-element.61), channel_id=1, source_target_pairs={{0,12},{4,8},{8,4},{12,0},{1,13},{5,9},{9,5},{13,1},{2,14},{6,10},... | collective-permute-start | bytes 589832 | tf_op jit(solution)/shard_map/ppermute | solution.py:43
  51.1 0.0 collective-permute-done.6.refs_3_
  51.1 6.9 %chebyshev.3 = (f32[3,128,128]{2,1,0:T(8,128)S(1)}, f32[3,128,128]{2,1,0:T(8,128)S(1)}, f32[3,128,128]{2,1,0:T(8,128)S(1)}, f32[3,128,128]{2,1,0:T(8,128)S(1)}) custom-call(s32[4]{0:T(128)S(1)} %pad_add_fusion.place, f32[6,32,8,128]{3,2,1,0:T(8,128)S(1)} %get-tuple-element.62.refs_0_, f32[384,128]{1,0:T(8,128)S(1)} %get-tuple-element.100.refs_1_, ...), custom_call_target="tpu_custom_call" | custom-call | flops 28311552 | bytes 1572864 | tf_op jit(solution)/shard_map/chebyshev/pallas_call | solution.py:129
  57.9 0.8 collective-permute-start.8
  58.7 2.3 %collective-permute-start.9 = (f32[3,128,128]{2,1,0:T(8,128)S(1)}, f32[3,128,128]{2,1,0:T(8,128)S(1)}, u32[]{:S(2)}, u32[]{:S(2)}) collective-permute-start(f32[3,128,128]{2,1,0:T(8,128)S(1)} %get-tuple-element.75), channel_id=1, source_target_pairs={{0,8},{4,12},{8,0},{12,4},{1,9},{5,13},{9,1},{13,5},{2,10},{6,14},... | collective-permute-start | bytes 589832 | tf_op jit(solution)/shard_map/ppermute | solution.py:43
  61.0 1.4 %collective-permute-start.10 = (f32[3,128,128]{2,1,0:T(8,128)S(1)}, f32[3,128,128]{2,1,0:T(8,128)S(1)}, u32[]{:S(2)}, u32[]{:S(2)}) collective-permute-start(f32[3,128,128]{2,1,0:T(8,128)S(1)} %get-tuple-element.76), channel_id=1, source_target_pairs={{0,12},{4,8},{8,4},{12,0},{1,13},{5,9},{9,5},{13,1},{2,14},{6,10},... | collective-permute-start | bytes 589832 | tf_op jit(solution)/shard_map/ppermute | solution.py:43
  62.4 11.5 %projectors.1 = (bf16[576,6144]{1,0:T(8,128)(2,1)S(1)}, bf16[576,6144]{1,0:T(8,128)(2,1)S(1)}) custom-call(s32[4]{0:T(128)S(1)} %pad_add_fusion.place, s32[3,48,128]{2,1,0:T(8,128)S(1)} %bitcast.32, f32[48,3,8,128]{3,2,1,0:T(8,128)S(1)} %copy-done.1), custom_call_target="tpu_custom_call" | custom-call | flops 1811939328 | bytes 28311552 | tf_op jit(solution)/shard_map/projectors/pallas_call | solution.py:253
  73.9 0.0 collective-permute-done.4
  73.9 0.7 cell_first.2
  74.6 1.6 %collective-permute-start.11 = (f32[48,16,128]{2,1,0:T(8,128)S(1)}, f32[48,16,128]{2,1,0:T(8,128)S(1)}, u32[]{:S(2)}, u32[]{:S(2)}) collective-permute-start(f32[48,16,128]{2,1,0:T(8,128)S(1)} %get-tuple-element.81), channel_id=1, source_target_pairs={{0,2},{2,0},{1,3},{3,1},{4,6},{6,4},{5,7},{7,5},{8,10},{10,8},{9,1... | collective-permute-start | bytes 1179656 | tf_op jit(solution)/shard_map/ppermute | solution.py:43
  76.1 3.7 %collective-permute-done.9 = f32[3,128,128]{2,1,0:T(8,128)S(1)} collective-permute-done((f32[3,128,128]{2,1,0:T(8,128)S(1)}, f32[3,128,128]{2,1,0:T(8,128)S(1)}, u32[]{:S(2)}, u32[]{:S(2)}) %collective-permute-start.9) | collective-permute-done | bytes 196640 | tf_op jit(solution)/shard_map/ppermute | solution.py:43
  79.9 0.7 cell_first.3
  80.5 1.6 %collective-permute-start.12 = (f32[48,16,128]{2,1,0:T(8,128)S(1)}, f32[48,16,128]{2,1,0:T(8,128)S(1)}, u32[]{:S(2)}, u32[]{:S(2)}) collective-permute-start(f32[48,16,128]{2,1,0:T(8,128)S(1)} %get-tuple-element.82), channel_id=1, source_target_pairs={{0,2},{2,0},{1,3},{3,1},{4,6},{6,4},{5,7},{7,5},{8,10},{10,8},{9,1... | collective-permute-start | bytes 1179656 | tf_op jit(solution)/shard_map/ppermute | solution.py:43
  82.1 0.1 pad_maximum_fusion
  82.2 0.1 collective-permute-start.13
  82.3 4.2 %collective-permute-done.11.refs_2_ = f32[48,16,128]{2,1,0:T(8,128)S(1)} collective-permute-done((f32[48,16,128]{2,1,0:T(8,128)S(1)}, f32[48,16,128]{2,1,0:T(8,128)S(1)}, u32[]{:S(2)}, u32[]{:S(2)}) %collective-permute-start.11) | collective-permute-done | bytes 393248 | tf_op jit(solution)/shard_map/ppermute | solution.py:43
  86.4 4.2 %collective-permute-done.12.refs_3_ = f32[48,16,128]{2,1,0:T(8,128)S(1)} collective-permute-done((f32[48,16,128]{2,1,0:T(8,128)S(1)}, f32[48,16,128]{2,1,0:T(8,128)S(1)}, u32[]{:S(2)}, u32[]{:S(2)}) %collective-permute-start.12) | collective-permute-done | bytes 393248 | tf_op jit(solution)/shard_map/ppermute | solution.py:43
  90.6 0.0 collective-permute-done.13.refs_4_
  90.6 1.7 %collective-permute-done.15.refs_6_ = f32[48,16,128]{2,1,0:T(8,128)S(1)} collective-permute-done((f32[48,16,128]{2,1,0:T(8,128)S(1)}, f32[48,16,128]{2,1,0:T(8,128)S(1)}, u32[]{:S(2)}, u32[]{:S(2)}) %collective-permute-start.15) | collective-permute-done | bytes 393248 | tf_op jit(solution)/shard_map/ppermute | solution.py:43
  92.3 3.8 %products.2 = (f32[96,128]{1,0:T(8,128)S(1)}, f32[96,128]{1,0:T(8,128)S(1)}, f32[96,128]{1,0:T(8,128)S(1)}, f32[96,128]{1,0:T(8,128)S(1)}) custom-call(s32[4]{0:T(128)S(1)} %pad_add_fusion.place, bf16[576,6144]{1,0:T(8,128)(2,1)S(1)} %get-tuple-element.77.w_high, bf16[576,6144]{1,0:T(8,128)(2,1)S(1)} %get-tuple-element.78.w_low, ...), custom_call_target="tpu_custom_call" | custom-call | flops 3623878656 | bytes 9437184 | tf_op jit(solution)/shard_map/products/pallas_call | solution.py:320
  96.2 2.7 %collective-permute-start.16 = (f32[96,128]{1,0:T(8,128)S(1)}, f32[96,128]{1,0:T(8,128)S(1)}, u32[]{:S(2)}, u32[]{:S(2)}) collective-permute-start(f32[96,128]{1,0:T(8,128)S(1)} %get-tuple-element.91), channel_id=1, source_target_pairs={{0,12},{2,14},{4,0},{6,2},{8,4},{10,6},{12,8},{14,10},{1,13},{3,15... | collective-permute-start | bytes 147464 | tf_op jit(solution)/shard_map/ppermute | solution.py:541
  98.9 4.4 %collective-permute-start.17 = (f32[96,128]{1,0:T(8,128)S(1)}, f32[96,128]{1,0:T(8,128)S(1)}, u32[]{:S(2)}, u32[]{:S(2)}) collective-permute-start(f32[96,128]{1,0:T(8,128)S(1)} %get-tuple-element.92), channel_id=1, source_target_pairs={{0,14},{2,12},{4,2},{6,0},{8,6},{10,4},{12,10},{14,8},{1,15},{3,13... | collective-permute-start | bytes 147464 | tf_op jit(solution)/shard_map/ppermute | solution.py:541
  103.3 3.9 %products.3 = (f32[128,128]{1,0:T(8,128)S(1)}, f32[96,128]{1,0:T(8,128)S(1)}, f32[96,128]{1,0:T(8,128)S(1)}) custom-call(s32[4]{0:T(128)S(1)} %pad_add_fusion.place, bf16[576,6144]{1,0:T(8,128)(2,1)S(1)} %get-tuple-element.77.w_high, bf16[576,6144]{1,0:T(8,128)(2,1)S(1)} %get-tuple-element.78.w_low, f32[48,16,128]{2,1,0:T(8,128)S(1)} %get-tuple-element.79.refs_0_, ...), custom_call_target="tpu_custom_call" | custom-call | flops 1811939328 | bytes 4718592 | tf_op jit(solution)/shard_map/products/pallas_call | solution.py:320
  107.1 0.9 collective-permute-start.20
  108.0 0.0 collective-permute-done.16.refs_0_
  108.0 0.0 collective-permute-done.17.refs_1_
  108.0 1.1 collective-permute-done.18.refs_2_
  109.1 1.0 collective-permute-done.19.refs_3_
  110.1 1.1 collective-permute-done.20.refs_4_
  111.3 1.2 gram_share.1
  112.5 0.9 collective-permute-start.22
  113.4 0.0 collective-permute-start.23
  113.4 1.4 %collective-permute-start.21 = (f32[32,128]{1,0:T(8,128)S(1)}, f32[32,128]{1,0:T(8,128)S(1)}, u32[]{:S(2)}, u32[]{:S(2)}) collective-permute-start(f32[32,128]{1,0:T(8,128)S(1)} %get-tuple-element.97), channel_id=1, source_target_pairs={{0,1},{1,0},{2,3},{3,2},{4,5},{5,4},{6,7},{7,6},{8,9},{9,8},{10,11... | collective-permute-start | bytes 49160 | tf_op jit(solution)/shard_map/ppermute | solution.py:43
  114.7 1.6 %collective-permute-done.22 = f32[32,128]{1,0:T(8,128)S(1)} collective-permute-done((f32[32,128]{1,0:T(8,128)S(1)}, f32[32,128]{1,0:T(8,128)S(1)}, u32[]{:S(2)}, u32[]{:S(2)}) %collective-permute-start.22) | collective-permute-done | bytes 16416 | tf_op jit(solution)/shard_map/ppermute | solution.py:43
  116.3 0.4 collective-permute-done.23
  116.7 0.0 collective-permute-done.21
  116.7 5.0 %collective-permute-start.25 = (f32[32,128]{1,0:T(8,128)S(1)}, f32[32,128]{1,0:T(8,128)S(1)}, u32[]{:S(2)}, u32[]{:S(2)}) collective-permute-start(f32[32,128]{1,0:T(8,128)S(1)} %add_add_fusion.1), channel_id=1, source_target_pairs={{0,8},{4,12},{8,0},{12,4},{1,9},{5,13},{9,1},{13,5},{2,10},{6,14},... | collective-permute-start | bytes 49160 | tf_op jit(solution)/shard_map/ppermute | solution.py:43
  121.7 0.6 collective-permute-start.24
  122.3 1.8 %orbital_first.1 = f32[32,96,128]{2,1,0:T(8,128)} custom-call(s32[4]{0:T(128)S(1)} %pad_add_fusion.place, f32[384,128]{1,0:T(8,128)S(1)} %bitcast.17, f32[384,128]{1,0:T(8,128)S(1)} %bitcast.19, f32[384,128]{1,0:T(8,128)S(1)} %bitcast.21, f32[384,128]{1,0:T(8,128)S(1)} %bitcast.23, f32[384,128]{1,0:T(8,128)S(1)} %bitcast.25, f32[384,128]{1,0:T(8,128)S(1)} %bitcast.27, ...), custom_call_target="tpu_custom_call" | custom-call | tf_op jit(solution)/shard_map/orbital_first/pallas_call | solution.py:194
  124.1 3.1 %collective-permute-done.26 = f32[32,128]{1,0:T(8,128)S(1)} collective-permute-done((f32[32,128]{1,0:T(8,128)S(1)}, f32[32,128]{1,0:T(8,128)S(1)}, u32[]{:S(2)}, u32[]{:S(2)}) %collective-permute-start.26) | collective-permute-done | bytes 16416 | tf_op jit(solution)/shard_map/ppermute | solution.py:43
  127.2 0.6 add_add_fusion
  (25 shorter events, 0.1 us)
Async XLA Ops:
  0.6 8.7 %copy-start = (f32[48,8,8]{0,2,1:T(8,128)S(1)}, f32[48,8,8]{0,2,1:T(8,128)}, u32[]{:S(2)}) copy-start(f32[48,8,8]{0,2,1:T(8,128)} %param.9) | copy-start | bytes 36868
  0.6 2.2 %copy-start.3 = (f32[32,3,32,128]{3,2,1,0:T(8,128)S(1)}, f32[32,3,32,128]{3,2,1,0:T(8,128)}, u32[]{:S(2)}) copy-start(f32[32,3,32,128]{3,2,1,0:T(8,128)} %param.5) | copy-start | bytes 4718596
  1.9 1.8 %copy-start.4 = (f32[3,32,128]{2,1,0:T(8,128)S(1)}, f32[3,32,128]{2,1,0:T(8,128)}, u32[]{:S(2)}) copy-start(f32[3,32,128]{2,1,0:T(8,128)} %param.6) | copy-start | bytes 147460
  3.6 21.5 %copy-start.5 = (f32[384,128]{1,0:T(8,128)S(1)}, f32[384,128]{1,0:T(8,128)}, u32[]{:S(2)}) copy-start(f32[384,128]{1,0:T(8,128)} %get-tuple-element.63) | copy-start | bytes 589828
  3.7 21.5 %collective-permute-start = (f32[864,128]{1,0:T(8,128)S(1)}, f32[864,128]{1,0:T(8,128)S(1)}, u32[]{:S(2)}, u32[]{:S(2)}) collective-permute-start(f32[864,128]{1,0:T(8,128)S(1)} %pad_maximum_fusion.1), channel_id=1, source_target_pairs={{0,4},{4,0},{8,12},{12,8},{1,5},{5,1},{9,13},{13,9},{2,6},{6,2},{1... | collective-permute-start | bytes 1327112 | tf_op jit(solution)/shard_map/ppermute | solution.py:43
  6.8 15.9 %collective-permute-start.1 = (f32[480,128]{1,0:T(8,128)S(1)}, f32[480,128]{1,0:T(8,128)S(1)}, u32[]{:S(2)}, u32[]{:S(2)}) collective-permute-start(f32[480,128]{1,0:T(8,128)S(1)} %get-tuple-element.55), channel_id=1, source_target_pairs={{0,8},{4,12},{8,0},{12,4},{1,9},{5,13},{9,1},{13,5},{2,10},{6,14},... | collective-permute-start | bytes 737288 | tf_op jit(solution)/shard_map/ppermute | solution.py:43
  9.4 21.6 %collective-permute-start.2 = (f32[480,128]{1,0:T(8,128)S(1)}, f32[480,128]{1,0:T(8,128)S(1)}, u32[]{:S(2)}, u32[]{:S(2)}) collective-permute-start(f32[480,128]{1,0:T(8,128)S(1)} %get-tuple-element.57), channel_id=1, source_target_pairs={{0,12},{4,8},{8,4},{12,0},{1,13},{5,9},{9,5},{13,1},{2,14},{6,10},... | collective-permute-start | bytes 737288 | tf_op jit(solution)/shard_map/ppermute | solution.py:43
  10.1 52.3 %copy-start.1 = (f32[48,3,8,128]{3,2,1,0:T(8,128)S(1)}, f32[48,3,8,128]{3,2,1,0:T(8,128)}, u32[]{:S(2)}) copy-start(f32[48,3,8,128]{3,2,1,0:T(8,128)} %coefs_ref.1) | copy-start | bytes 1769476
  10.1 52.3 %copy-start.2 = (s32[48,3,128]{2,0,1:T(8,128)S(1)}, s32[48,3,128]{2,0,1:T(8,128)}, u32[]{:S(2)}) copy-start(s32[48,3,128]{2,0,1:T(8,128)} %param.7) | copy-start | bytes 221188
  22.7 28.4 %collective-permute-start.7 = (f32[384,128]{1,0:T(8,128)}, f32[384,128]{1,0:T(8,128)S(1)}, u32[]{:S(2)}, u32[]{:S(2)}) collective-permute-start(f32[384,128]{1,0:T(8,128)} %get-tuple-element.64), channel_id=1, source_target_pairs={{0,12},{4,8},{8,4},{12,0},{1,13},{5,9},{9,5},{13,1},{2,14},{6,10},... | collective-permute-start | bytes 589832 | tf_op jit(solution)/shard_map/ppermute | solution.py:43
  25.1 25.9 %collective-permute-start.6 = (f32[384,128]{1,0:T(8,128)S(1)}, f32[384,128]{1,0:T(8,128)S(1)}, u32[]{:S(2)}, u32[]{:S(2)}) collective-permute-start(f32[384,128]{1,0:T(8,128)S(1)} %copy-done.5), channel_id=1, source_target_pairs={{0,8},{4,12},{8,0},{12,4},{1,9},{5,13},{9,1},{13,5},{2,10},{6,14},... | collective-permute-start | bytes 589832 | tf_op jit(solution)/shard_map/ppermute | solution.py:43
  38.1 22.9 %collective-permute-start.3 = (f32[3,128,128]{2,1,0:T(8,128)S(1)}, f32[3,128,128]{2,1,0:T(8,128)S(1)}, u32[]{:S(2)}, u32[]{:S(2)}) collective-permute-start(f32[3,128,128]{2,1,0:T(8,128)S(1)} %get-tuple-element.59), channel_id=1, source_target_pairs={{0,4},{4,0},{8,12},{12,8},{1,5},{5,1},{9,13},{13,9},{2,6},{6,2},{1... | collective-permute-start | bytes 589832 | tf_op jit(solution)/shard_map/ppermute | solution.py:43
  48.3 25.6 %collective-permute-start.4 = (f32[3,128,128]{2,1,0:T(8,128)S(1)}, f32[3,128,128]{2,1,0:T(8,128)S(1)}, u32[]{:S(2)}, u32[]{:S(2)}) collective-permute-start(f32[3,128,128]{2,1,0:T(8,128)S(1)} %get-tuple-element.60), channel_id=1, source_target_pairs={{0,8},{4,12},{8,0},{12,4},{1,9},{5,13},{9,1},{13,5},{2,10},{6,14},... | collective-permute-start | bytes 589832 | tf_op jit(solution)/shard_map/ppermute | solution.py:43
  49.7 24.2 %collective-permute-start.5 = (f32[3,128,128]{2,1,0:T(8,128)S(1)}, f32[3,128,128]{2,1,0:T(8,128)S(1)}, u32[]{:S(2)}, u32[]{:S(2)}) collective-permute-start(f32[3,128,128]{2,1,0:T(8,128)S(1)} %get-tuple-element.61), channel_id=1, source_target_pairs={{0,12},{4,8},{8,4},{12,0},{1,13},{5,9},{9,5},{13,1},{2,14},{6,10},... | collective-permute-start | bytes 589832 | tf_op jit(solution)/shard_map/ppermute | solution.py:43
  57.9 18.2 %collective-permute-start.8 = (f32[3,128,128]{2,1,0:T(8,128)S(1)}, f32[3,128,128]{2,1,0:T(8,128)S(1)}, u32[]{:S(2)}, u32[]{:S(2)}) collective-permute-start(f32[3,128,128]{2,1,0:T(8,128)S(1)} %get-tuple-element.74), channel_id=1, source_target_pairs={{0,4},{4,0},{8,12},{12,8},{1,5},{5,1},{9,13},{13,9},{2,6},{6,2},{1... | collective-permute-start | bytes 589832 | tf_op jit(solution)/shard_map/ppermute | solution.py:43
  58.7 21.2 %collective-permute-start.9 = (f32[3,128,128]{2,1,0:T(8,128)S(1)}, f32[3,128,128]{2,1,0:T(8,128)S(1)}, u32[]{:S(2)}, u32[]{:S(2)}) collective-permute-start(f32[3,128,128]{2,1,0:T(8,128)S(1)} %get-tuple-element.75), channel_id=1, source_target_pairs={{0,8},{4,12},{8,0},{12,4},{1,9},{5,13},{9,1},{13,5},{2,10},{6,14},... | collective-permute-start | bytes 589832 | tf_op jit(solution)/shard_map/ppermute | solution.py:43
  61.0 18.9 %collective-permute-start.10 = (f32[3,128,128]{2,1,0:T(8,128)S(1)}, f32[3,128,128]{2,1,0:T(8,128)S(1)}, u32[]{:S(2)}, u32[]{:S(2)}) collective-permute-start(f32[3,128,128]{2,1,0:T(8,128)S(1)} %get-tuple-element.76), channel_id=1, source_target_pairs={{0,12},{4,8},{8,4},{12,0},{1,13},{5,9},{9,5},{13,1},{2,14},{6,10},... | collective-permute-start | bytes 589832 | tf_op jit(solution)/shard_map/ppermute | solution.py:43
  74.6 11.9 %collective-permute-start.11 = (f32[48,16,128]{2,1,0:T(8,128)S(1)}, f32[48,16,128]{2,1,0:T(8,128)S(1)}, u32[]{:S(2)}, u32[]{:S(2)}) collective-permute-start(f32[48,16,128]{2,1,0:T(8,128)S(1)} %get-tuple-element.81), channel_id=1, source_target_pairs={{0,2},{2,0},{1,3},{3,1},{4,6},{6,4},{5,7},{7,5},{8,10},{10,8},{9,1... | collective-permute-start | bytes 1179656 | tf_op jit(solution)/shard_map/ppermute | solution.py:43
  80.5 10.1 %collective-permute-start.12 = (f32[48,16,128]{2,1,0:T(8,128)S(1)}, f32[48,16,128]{2,1,0:T(8,128)S(1)}, u32[]{:S(2)}, u32[]{:S(2)}) collective-permute-start(f32[48,16,128]{2,1,0:T(8,128)S(1)} %get-tuple-element.82), channel_id=1, source_target_pairs={{0,2},{2,0},{1,3},{3,1},{4,6},{6,4},{5,7},{7,5},{8,10},{10,8},{9,1... | collective-permute-start | bytes 1179656 | tf_op jit(solution)/shard_map/ppermute | solution.py:43
  82.2 8.5 %collective-permute-start.13 = (f32[48,32,128]{2,1,0:T(8,128)S(1)}, f32[48,32,128]{2,1,0:T(8,128)S(1)}, u32[]{:S(2)}, u32[]{:S(2)}) collective-permute-start(f32[48,32,128]{2,1,0:T(8,128)S(1)} %pad_maximum_fusion), channel_id=1, source_target_pairs={{0,1},{1,0},{2,3},{3,2},{4,5},{5,4},{6,7},{7,6},{8,9},{9,8},{10,11... | collective-permute-start | bytes 2359304 | tf_op jit(solution)/shard_map/ppermute | solution.py:43
  86.4 4.2 %collective-permute-start.14 = (f32[48,16,128]{2,1,0:T(8,128)S(1)}, f32[48,16,128]{2,1,0:T(8,128)S(1)}, u32[]{:S(2)}, u32[]{:S(2)}) collective-permute-start(f32[48,16,128]{2,1,0:T(8,128)S(1)} %collective-permute-done.11.refs_2_), channel_id=1, source_target_pairs={{0,1},{1,0},{2,3},{3,2},{4,5},{5,4},{6,7},{7,6},{8,9},{9,8},{10,11... | collective-permute-start | bytes 1179656 | tf_op jit(solution)/shard_map/ppermute | solution.py:43
  90.6 1.7 %collective-permute-start.15 = (f32[48,16,128]{2,1,0:T(8,128)S(1)}, f32[48,16,128]{2,1,0:T(8,128)S(1)}, u32[]{:S(2)}, u32[]{:S(2)}) collective-permute-start(f32[48,16,128]{2,1,0:T(8,128)S(1)} %collective-permute-done.12.refs_3_), channel_id=1, source_target_pairs={{0,1},{1,0},{2,3},{3,2},{4,5},{5,4},{6,7},{7,6},{8,9},{9,8},{10,11... | collective-permute-start | bytes 1179656 | tf_op jit(solution)/shard_map/ppermute | solution.py:43
  96.2 11.8 %collective-permute-start.16 = (f32[96,128]{1,0:T(8,128)S(1)}, f32[96,128]{1,0:T(8,128)S(1)}, u32[]{:S(2)}, u32[]{:S(2)}) collective-permute-start(f32[96,128]{1,0:T(8,128)S(1)} %get-tuple-element.91), channel_id=1, source_target_pairs={{0,12},{2,14},{4,0},{6,2},{8,4},{10,6},{12,8},{14,10},{1,13},{3,15... | collective-permute-start | bytes 147464 | tf_op jit(solution)/shard_map/ppermute | solution.py:541
  98.9 9.1 %collective-permute-start.17 = (f32[96,128]{1,0:T(8,128)S(1)}, f32[96,128]{1,0:T(8,128)S(1)}, u32[]{:S(2)}, u32[]{:S(2)}) collective-permute-start(f32[96,128]{1,0:T(8,128)S(1)} %get-tuple-element.92), channel_id=1, source_target_pairs={{0,14},{2,12},{4,2},{6,0},{8,6},{10,4},{12,10},{14,8},{1,15},{3,13... | collective-permute-start | bytes 147464 | tf_op jit(solution)/shard_map/ppermute | solution.py:541
  103.3 5.9 %collective-permute-start.18 = (f32[96,128]{1,0:T(8,128)S(1)}, f32[96,128]{1,0:T(8,128)S(1)}, u32[]{:S(2)}, u32[]{:S(2)}) collective-permute-start(f32[96,128]{1,0:T(8,128)S(1)} %get-tuple-element.93), channel_id=1, source_target_pairs={{0,4},{2,6},{4,8},{6,10},{8,12},{10,14},{12,0},{14,2},{1,5},{3,7},... | collective-permute-start | bytes 147464 | tf_op jit(solution)/shard_map/ppermute | solution.py:541
  103.3 6.9 %collective-permute-start.19 = (f32[96,128]{1,0:T(8,128)S(1)}, f32[96,128]{1,0:T(8,128)S(1)}, u32[]{:S(2)}, u32[]{:S(2)}) collective-permute-start(f32[96,128]{1,0:T(8,128)S(1)} %get-tuple-element.94), channel_id=1, source_target_pairs={{0,6},{2,4},{4,10},{6,8},{8,14},{10,12},{12,2},{14,0},{1,7},{3,5},... | collective-permute-start | bytes 147464 | tf_op jit(solution)/shard_map/ppermute | solution.py:541
  107.1 4.2 %collective-permute-start.20 = (f32[96,128]{1,0:T(8,128)S(1)}, f32[96,128]{1,0:T(8,128)S(1)}, u32[]{:S(2)}, u32[]{:S(2)}) collective-permute-start(f32[96,128]{1,0:T(8,128)S(1)} %get-tuple-element.95), channel_id=1, source_target_pairs={{0,2},{2,0},{4,6},{6,4},{8,10},{10,8},{12,14},{14,12},{1,3},{3,1},... | collective-permute-start | bytes 147464 | tf_op jit(solution)/shard_map/ppermute | solution.py:541
  112.5 3.8 %collective-permute-start.22 = (f32[32,128]{1,0:T(8,128)S(1)}, f32[32,128]{1,0:T(8,128)S(1)}, u32[]{:S(2)}, u32[]{:S(2)}) collective-permute-start(f32[32,128]{1,0:T(8,128)S(1)} %get-tuple-element.98), channel_id=1, source_target_pairs={{0,2},{1,3},{2,0},{3,1},{4,6},{5,7},{6,4},{7,5},{8,10},{9,11},{10,... | collective-permute-start | bytes 49160 | tf_op jit(solution)/shard_map/ppermute | solution.py:43
  113.4 3.3 %collective-permute-start.23 = (f32[32,128]{1,0:T(8,128)S(1)}, f32[32,128]{1,0:T(8,128)S(1)}, u32[]{:S(2)}, u32[]{:S(2)}) collective-permute-start(f32[32,128]{1,0:T(8,128)S(1)} %get-tuple-element.99), channel_id=1, source_target_pairs={{0,3},{1,2},{2,1},{3,0},{4,7},{5,6},{6,5},{7,4},{8,11},{9,10},{10,... | collective-permute-start | bytes 49160 | tf_op jit(solution)/shard_map/ppermute | solution.py:43
  113.4 3.3 %collective-permute-start.21 = (f32[32,128]{1,0:T(8,128)S(1)}, f32[32,128]{1,0:T(8,128)S(1)}, u32[]{:S(2)}, u32[]{:S(2)}) collective-permute-start(f32[32,128]{1,0:T(8,128)S(1)} %get-tuple-element.97), channel_id=1, source_target_pairs={{0,1},{1,0},{2,3},{3,2},{4,5},{5,4},{6,7},{7,6},{8,9},{9,8},{10,11... | collective-permute-start | bytes 49160 | tf_op jit(solution)/shard_map/ppermute | solution.py:43
  116.7 7.4 %collective-permute-start.25 = (f32[32,128]{1,0:T(8,128)S(1)}, f32[32,128]{1,0:T(8,128)S(1)}, u32[]{:S(2)}, u32[]{:S(2)}) collective-permute-start(f32[32,128]{1,0:T(8,128)S(1)} %add_add_fusion.1), channel_id=1, source_target_pairs={{0,8},{4,12},{8,0},{12,4},{1,9},{5,13},{9,1},{13,5},{2,10},{6,14},... | collective-permute-start | bytes 49160 | tf_op jit(solution)/shard_map/ppermute | solution.py:43
  121.7 5.5 %collective-permute-start.26 = (f32[32,128]{1,0:T(8,128)S(1)}, f32[32,128]{1,0:T(8,128)S(1)}, u32[]{:S(2)}, u32[]{:S(2)}) collective-permute-start(f32[32,128]{1,0:T(8,128)S(1)} %add_add_fusion.1), channel_id=1, source_target_pairs={{0,12},{4,8},{8,4},{12,0},{1,13},{5,9},{9,5},{13,1},{2,14},{6,10},... | collective-permute-start | bytes 49160 | tf_op jit(solution)/shard_map/ppermute | solution.py:43
  121.7 5.5 %collective-permute-start.24 = (f32[32,128]{1,0:T(8,128)S(1)}, f32[32,128]{1,0:T(8,128)S(1)}, u32[]{:S(2)}, u32[]{:S(2)}) collective-permute-start(f32[32,128]{1,0:T(8,128)S(1)} %add_add_fusion.1), channel_id=1, source_target_pairs={{0,4},{4,0},{8,12},{12,8},{1,5},{5,1},{9,13},{13,9},{2,6},{6,2},{1... | collective-permute-start | bytes 49160 | tf_op jit(solution)/shard_map/ppermute | solution.py:43

commit v7 on v6

--- a/solution.py
+++ b/solution.py
@@ -43,19 +43,71 @@
     return lax.ppermute(x, axes, [(i, i ^ by) for i in range(size)])
 
 
-def filter_kernel(n_dom, planes, rows, starts, first, place, *refs):
+def pack_kernel(n_dom, size, contents, place, panel, *refs):
+    levels, outs, sems = refs[0], refs[1:-1], refs[-1]
+    copies = []
+    for out, content in zip(outs, contents):
+        at = 0
+        for kind, c, m in content:
+            if kind == "block":
+                start = pl.multiple_of((c * n_dom + (place[ME] ^ m)) * size, SUBLANES)
+                copies.append((panel.at[pl.ds(start, size)], out.at[pl.ds(at, size)]))
+                at += size
+            else:
+                share = levels.shape[0] if kind == "levels" else out.shape[0] - at
+                start = 0
+                if kind == "share":
+                    start = pl.multiple_of(place[SUB] * share, SUBLANES)
+                copies.append((levels.at[pl.ds(start, share)], out.at[pl.ds(at, share)]))
+                at += share
+    copies = [pltpu.make_async_copy(a, b, sems.at[k]) for k, (a, b) in enumerate(copies)]
+    for copy in copies:
+        copy.start()
+    for copy in copies:
+        copy.wait()
+
+
+def pack(place, n_dom, n_sub, size, panel, levels, contents):
+    rows = {"block": size, "levels": levels.shape[0], "share": levels.shape[0] // n_sub}
+    lanes = panel.shape[1]
+    shapes = [
+        jax.ShapeDtypeStruct((sum(rows[kind] for kind, _, _ in content), lanes), jnp.float32)
+        for content in contents
+    ]
+    return pl.pallas_call(
+        functools.partial(pack_kernel, n_dom, size, contents),
+        out_shape=shapes,
+        in_specs=[SMEM] + [pl.BlockSpec(memory_space=pltpu.HBM)] * 2,
+        out_specs=[VMEM] * len(shapes),
+        scratch_shapes=[pltpu.SemaphoreType.DMA((sum(len(x) for x in contents),))],
+        compiler_params=params(6),
+        name="pack",
+    )(place, panel, levels)
+
+
+def filter_kernel(n_dom, planes, rows, starts, n_levels, place, *refs):
     refs = list(refs)
-    given = None if first else refs.pop(0)
+    first = n_levels > 0
+    given, refs = (refs[:n_levels], refs[n_levels:]) if first else (refs[:1], refs[1:])
     ins, outs = refs[:n_dom], refs[n_dom : 2 * n_dom]
     refs = refs[2 * n_dom :]
-    diagonal = refs.pop(0) if first else given
-    even, odd = refs
+    diagonal = refs.pop(0) if first else given[0]
+    even, odd, levels = refs
     half_planes = n_dom * planes // 2
     cells = planes * rows
     lanes = even.shape[3]
     scale = 1.0 / HALF_WIDTH
     mirrored = (place[ME] & 1) != 0
     plane_at = [jnp.where(mirrored, planes - 1 - i, i) for i in range(planes)]
+
+    if first:
+        levels[0] = given[0][...]
+        levels[1] = ins[1][TOGETHER * cells : (TOGETHER + 1) * cells, :]
+        n_sub = (n_levels - 1) // max(n_dom - 2, 1)
+        for k, piece in enumerate(given[1:]):
+            share = piece.shape[0]
+            at = pl.multiple_of((place[SUB] ^ (k % n_sub)) * share, SUBLANES)
+            levels[2 + k // n_sub, pl.ds(at, share), :] = piece[...]
 
     for x in range(half_planes):
         for half in range(2):
@@ -65,7 +117,7 @@
             for y in range(rows):
                 even[x, y, part] = ins[m][pl.ds(base + y, TOGETHER, stride=cells), :]
                 if first:
-                    level = ins[m][pl.ds(base + (TOGETHER * cells + y), 1), :]
+                    level = levels[m, pl.ds(plane_at[i] * rows + y, 1), :]
                     diagonal[x, y, part] = jnp.broadcast_to(
                         (level + (SHIFT - CENTER_LEVEL)) * (2.0 * scale), (TOGETHER, lanes)
                     )
@@ -117,21 +169,23 @@
                 outs[m][plane_at[i], here, :] = even[x, y, part]
 
 
-def filter_orbitals(place, diagonal, blocks, starts, planes, rows):
+def filter_orbitals(place, diagonal, levels, blocks, starts, planes, rows):
     n_dom = len(blocks)
     first = diagonal is None
     lanes = blocks[0].shape[1]
     field = (n_dom * planes // 2, rows, SUBLANES, lanes)
     out = jax.ShapeDtypeStruct((planes, rows * TOGETHER, lanes), jnp.float32)
     extra = [jax.ShapeDtypeStruct(field, jnp.float32)] if first else []
-    given = [] if first else [diagonal]
+    given = levels if first else [diagonal]
+    n_levels = len(levels) if first else 0
     size = n_dom * planes * rows * TOGETHER * lanes
     return pl.pallas_call(
-        functools.partial(filter_kernel, n_dom, planes, rows, starts, first),
+        functools.partial(filter_kernel, n_dom, planes, rows, starts, n_levels),
         out_shape=[out] * n_dom + extra,
         in_specs=[SMEM] + [VMEM] * (n_dom + len(given)),
         out_specs=[VMEM] * (n_dom + len(extra)),
-        scratch_shapes=[pltpu.VMEM(field, jnp.float32)] * 2,
+        scratch_shapes=[pltpu.VMEM(field, jnp.float32)] * 2
+        + [pltpu.VMEM((n_dom, planes * rows, lanes), jnp.float32)],
         compiler_params=params(8),
         cost_estimate=pl.CostEstimate(
             flops=12 * DEGREE * size, bytes_accessed=8 * size, transcendentals=0
@@ -140,11 +194,12 @@
     )(place, *given, *blocks)
 
 
-def cell_first_kernel(n_band, place, *refs):
+def cell_first_kernel(n_dom, n_band, place, *refs):
     pieces, parts = refs[:-n_band], refs[-n_band:]
     share = parts[0].shape[0]
     me = place[ME]
     together = SUBLANES // TOGETHER
+    per_chunk = n_dom // together
     tiles = len(pieces) // together
     for p, part in enumerate(parts):
         base = pl.multiple_of((place[BAND] ^ p) * (share * TOGETHER), SUBLANES)
@@ -157,19 +212,19 @@
                         [loaded[q * together + i][here] for i in range(together)], axis=0
                     )
                     tile = jnp.where((me & 1) != 0, pltpu.roll(tile, TOGETHER, 0), tile)
-                    if tiles == 1:
-                        part[first + k] = tile
-                    else:
-                        row = pl.multiple_of((q ^ (me // together)) * SUBLANES, SUBLANES)
-                        part[first + k, pl.ds(row, SUBLANES), :] = tile
-
-
-def cell_first(place, n_band, pieces):
+                    chunk, half = divmod(q, per_chunk)
+                    if (chunk + 1) * per_chunk <= tiles:
+                        half = half ^ (me // together)
+                    row = pl.multiple_of((chunk * per_chunk + half) * SUBLANES, SUBLANES)
+                    part[first + k, pl.ds(row, SUBLANES), :] = tile
+
+
+def cell_first(place, n_dom, n_band, pieces):
     rows, lanes = pieces[0].shape
     orbitals = len(pieces) * TOGETHER
     part = jax.ShapeDtypeStruct((rows // (TOGETHER * n_band), orbitals, lanes), jnp.float32)
     return pl.pallas_call(
-        functools.partial(cell_first_kernel, n_band),
+        functools.partial(cell_first_kernel, n_dom, n_band),
         out_shape=[part] * n_band,
         in_specs=[SMEM] + [VMEM] * len(pieces),
         out_specs=[VMEM] * n_band,
@@ -197,6 +252,9 @@
         in_specs=[SMEM] + [VMEM] * len(pieces),
         out_specs=VMEM,
         compiler_params=params(8),
+        cost_estimate=pl.CostEstimate(
+            flops=math.prod(shape), bytes_accessed=8 * math.prod(shape), transcendentals=0
+        ),
         name="orbital_first",
     )(place, *pieces)
 
@@ -213,7 +271,9 @@
 
     def two_atoms(step, carry):
         shell = lax.rem(2 * (step // (n_band * pairs)), shells)
-        band = place[BAND] ^ ((step // pairs) % n_band)
+        seen = (step // pairs) % n_band
+        seen = jnp.where(shell == 1, n_band - 1 - seen, seen)
+        band = place[BAND] ^ seen
         first_atom = (place[SUB] * n_band + band) * own + 2 * (step % pairs)
         dense = []
         for i in range(2):
@@ -272,11 +332,18 @@
     rows, orbitals = proj_out.shape
     cells, _, lanes = arrays[0].shape
     block = 12
+    swap = (place[ME] & 2) != 0
 
     def parts(start):
         highs, lows = [], []
-        for at, first, width in spots:
-            high, low = split_bf16(arrays[at][pl.ds(start, block), first : first + width])
+        for spot in spots:
+            tiles = [
+                arrays[at][pl.ds(start, block), first : first + width] for at, first, width in spot
+            ]
+            if len(tiles) == 2:
+                near, far = tiles
+                tiles = [jnp.where(swap, far, near), jnp.where(swap, near, far)]
+            high, low = split_bf16(jnp.concatenate(tiles, axis=1))
             highs.append(jnp.concatenate([high[k] for k in range(block)], axis=1))
             lows.append(jnp.concatenate([low[k] for k in range(block)], axis=1))
         return jnp.concatenate(highs, axis=0), jnp.concatenate(lows, axis=0)
@@ -313,7 +380,7 @@
 
 
 def products(n_sub, first_row, rows, n_blocks, with_grid, place, projectors, arrays, spots):
-    orbitals = sum(width for _, _, width in spots)
+    orbitals = sum(width for spot in spots for _, _, width in spot)
     grid = [jax.ShapeDtypeStruct((orbitals, orbitals), jnp.float32)] if with_grid else []
     block = jax.ShapeDtypeStruct((rows // n_blocks, orbitals), jnp.float32)
     flops = 12 * rows * orbitals * projectors[0].shape[1]
@@ -382,8 +449,8 @@
     return terms[0]
 
 
-def whole_columns(panel, potential, place, me):
-    n_dom = lax.axis_size("dom")
+def whole_columns(panel, potential, place, early):
+    n_dom, n_sub = lax.axis_size("dom"), lax.axis_size("sub")
     orbitals, planes, rows, lanes = panel.shape
     cells = planes * rows
     flat = panel.reshape(orbitals * cells, lanes)
@@ -391,41 +458,46 @@
     size = TOGETHER * cells
     n_chunks = orbitals // (n_dom * TOGETHER)
 
-    def block(c, m):
-        return lax.dynamic_slice_in_dim(flat, (c * n_dom + (me ^ m)) * size, size, 0)
-
     def sent(x, m):
         return swapped(x, "dom", n_dom, m)
 
-    far = [jnp.concatenate([block(0, m), levels], axis=0) for m in range(2, n_dom)]
-    far, flat, levels = lax.optimization_barrier((far, flat, levels))
-    near = [block(0, 1), levels] + [block(c, 1) for c in range(1, n_chunks)]
-    near = sent(jnp.concatenate(near, axis=0), 1)
-    own = [block(c, 0) for c in range(n_chunks)]
-    own[0] = jnp.concatenate([own[0], levels], axis=0)
-    arrived = [[own[0], near] + [sent(x, m) for m, x in enumerate(far, start=2)]]
+    def packed(place, contents):
+        return pack(place, n_dom, n_sub, size, flat, levels, contents)
+
+    contents = [[("block", 0, 1), ("levels", 0, 0)] + [("block", c, 1) for c in range(1, n_chunks)]]
+    for m in range(2, n_dom):
+        contents.append([("block", 0, m)] + ([("share", 0, 0)] if m == 2 else []))
+    near, *far = packed(place, contents)
+    near, *far = [sent(x, m) for m, x in enumerate([near] + far, start=1)]
+    given = [levels]
+    if far:
+        shares = [far[0][size:]]
+        shares.append(sent(shares[0], 1))
+        for x in shares:
+            given += [x] + [swapped(x, "sub", n_sub, k) for k in range(1, n_sub)]
+    contents = [[("block", c, 0)] for c in range(n_chunks)]
+    contents += [[("block", c, m)] for c in range(1, n_chunks) for m in range(2, n_dom)]
+    rest = packed(place, contents)
+    own, rest = rest[:n_chunks], rest[n_chunks:]
+    near, rest, early = lax.optimization_barrier((near, rest, early))
+    arrived = [[own[0], near] + far]
     for c in range(1, n_chunks):
-        blocks = [own[c], near]
-        for m in range(2, n_dom):
-            x = block(c, m)
-            arrived[c - 1][m - 1], x = lax.optimization_barrier((arrived[c - 1][m - 1], x))
-            blocks.append(sent(x, m))
-        arrived.append(blocks)
-    for blocks in arrived:
-        blocks[1] = arrived[0][1]
+        blocks = [sent(x, m) for m, x in enumerate(rest[: n_dom - 2], start=2)]
+        rest = rest[n_dom - 2 :]
+        arrived.append([own[c], near] + blocks)
     diagonal = None
     done = []
     for c, blocks in enumerate(arrived):
         starts = [0] * n_dom
         starts[1] = c * size + (cells if c else 0)
-        filtered = filter_orbitals(place, diagonal, blocks, starts, planes, rows)
+        filtered = filter_orbitals(place, diagonal, given, blocks, starts, planes, rows)
         if diagonal is None:
             diagonal = filtered[n_dom]
         done.append(filtered[:n_dom])
     return [
         [(sent(x, m) if m else x).reshape(size, lanes) for m, x in enumerate(blocks)]
         for blocks in done
-    ]
+    ], early
 
 
 def plane_by_plane(panel, potential):
@@ -468,24 +540,17 @@
         own_atoms * channels, own_atoms * channels
     )
 
-    place, corr_matrix = lax.optimization_barrier((place, corr_matrix))
-
     def build(offsets):
         return build_projectors(n_band, n_sub, place, offsets, point_coefs, share, lanes)
 
-    place, corr_matrix = lax.optimization_barrier((place, corr_matrix))
-
-    def build(offsets):
-        return build_projectors(n_band, n_sub, place, offsets, point_coefs, share, lanes)
-
-    filtered, parts = [], []
     if n_dom in (2, 4) and orbitals % (n_dom * TOGETHER) == 0 and planes * n_dom % 2 == 0:
-        chunks = whole_columns(panel, potential, place, me)
+        chunks, corr_matrix = whole_columns(panel, potential, place, corr_matrix)
         chunks[-1][0], point_offsets = lax.optimization_barrier((chunks[-1][0], point_offsets))
         projectors = build(point_offsets)
         chunks[0], projectors = lax.optimization_barrier((chunks[0], projectors))
         filtered = orbital_first(place, n_dom, [piece for pieces in chunks for piece in pieces])
-        parts = [cell_first(place, n_band, pieces) for pieces in chunks]
+        parts = [cell_first(place, n_dom, n_band, pieces) for pieces in chunks]
+        tiles = [[(c, 0, n_dom * TOGETHER)] for c in range(len(chunks))]
     else:
         projectors = build(point_offsets)
         filtered = plane_by_plane(panel, potential)
@@ -496,53 +561,54 @@
                 for m in range(n_band)
             ]
         ]
+        tiles = [[(0, 0, orbitals)]]
     filtered = filtered.reshape(panel.shape)
-    chunks = len(parts)
-    arrays = [x for by_band in parts for x in by_band[:1]]
-    arrays += [
-        swapped(by_band[m], "band", n_band, m) for by_band in parts for m in range(1, n_band)
-    ]
-    pieces = [jnp.concatenate(arrays[:chunks], axis=1)] + arrays[chunks:]
+    own = [part[0] for part in parts]
+    pieces = [swapped(part[m], "band", n_band, m) for part in parts for m in range(1, n_band)]
+    pieces[0], filtered = lax.optimization_barrier((pieces[0], filtered))
+    arrays = own + pieces
+    pieces = [jnp.concatenate(own, axis=1)] + pieces
     arrays += [swapped(x, "sub", n_sub, k) for k in range(1, n_sub) for x in pieces]
-    width = arrays[0].shape[1]
+    starts = [sum(x.shape[1] for x in own[:at]) for at in range(len(own))]
     spots = []
     for m in range(n_band):
         for k in range(n_sub):
-            for c in range(chunks):
-                at = chunks + c * (n_band - 1) + m - 1 if m else c
-                if k == 0:
-                    spots.append((at, 0, width))
-                else:
-                    base = chunks * n_band + (k - 1) * len(pieces)
+            for tile in tiles:
+                spot = []
+                for at, first, width in tile:
+                    index = at
                     if m:
-                        spots.append((base + 1 + at - chunks, 0, width))
-                    else:
-                        spots.append((base, c * width, width))
-
-    rows = own_atoms * channels * n_band
-    outer = products(
-        n_sub, 0, 2 * rows, 2 * n_band, False, place, projectors, arrays, spots
-    )
-    outer, place = lax.optimization_barrier((outer, place))
-    grid_part, *inner = products(
-        n_sub, 2 * rows, rows, n_band, True, place, projectors, arrays, spots
+                        index = len(own) + at * (n_band - 1) + m - 1 + k * len(pieces)
+                    elif k:
+                        index = len(own) * n_band + (k - 1) * len(pieces)
+                        first += starts[at]
+                    spot.append((index, first, width))
+                spots.append(spot)
+
+    rows = own_atoms * channels
+    n_sent = 3 * n_band - 1
+    outgoing = products(
+        n_sub, 0, n_sent * rows, n_sent, False, place, projectors, arrays, spots
+    )
+    outgoing, place = lax.optimization_barrier((outgoing, place))
+    grid_part, own_proj = products(
+        n_sub, n_sent * rows, rows, 1, True, place, projectors, arrays, spots
     )
     sums, seen = [], []
-    for by, blocks in ((1, outer[:n_band]), (-1, outer[n_band:]), (0, inner)):
-        for m, x in enumerate(blocks):
-            if by == 0 and m == 0:
-                continue
-            pairs = [
-                (d * n_band + b, (d - by) % n_dom * n_band + (b ^ m))
-                for d in range(n_dom)
-                for b in range(n_band)
-            ]
-            seen.append(m * n_sub)
-            sums.append(lax.ppermute(x, ("dom", "band"), pairs))
+    to = [(by, m) for by in (1, -1) for m in range(n_band)]
+    to += [(0, m) for m in range(n_band - 1, 0, -1)]
+    for x, (by, m) in zip(outgoing, to):
+        pairs = [
+            (d * n_band + b, (d - by) % n_dom * n_band + (b ^ m))
+            for d in range(n_dom)
+            for b in range(n_band)
+        ]
+        seen.append(m * n_sub)
+        sums.append(lax.ppermute(x, ("dom", "band"), pairs))
     scale_point = 1.0 / (cells * lanes * n_dom)
     scale_atom = 1.0 / math.sqrt(own_atoms * groups * n_dom)
     shares = gram_share(
-        (scale_point, scale_atom), groups, seen, place, corr_matrix, grid_part, inner[0], sums
+        (scale_point, scale_atom), groups, seen, place, corr_matrix, grid_part, own_proj, sums
     )
     gram_rows = added(
         [swapped(x, ("band", "sub"), groups, m) if m else x for m, x in enumerate(shares)]

time: 128 us -> 136 us (1.062)
  local copies, waits for them, and re-layouts: 2.51 us -> 6.8 us
  Pallas kernels: 37.5 us -> 41.4 us
    unnamed x12 -> x16, local copies, waits for them, and re-layouts: 0.04 us -> 5.22 us
    pallas_call x2 -> x4, Pallas kernels: 1.31 us -> 4.62 us  [the longest x2 3.31 us: pack(): pl.pallas_call(functools.partial(pack_kernel, n_dom, size, contents), out...]
    ppermute x22 -> x25, waiting for transfers between devices: 34.7 us -> 36.7 us  [swapped(): return lax.ppermute(x, axes, [(i, i ^ by) for i in range(size)])]
    dynamic_slice x2 -> x0, local copies, waits for them, and re-layouts: 2.01 us -> none  [block(): lax.dynamic_slice_in_dim(flat, (c * n_dom + (me ^ m)) * size, size, 0)]
    ppermute x5, waiting for transfers between devices: 3.3 us -> 1.61 us  [on_device(): sums.append(lax.ppermute(x, ('dom', 'band'), pairs))]
    ppermute x22 -> x25, starting transfers between devices: 39.1 us -> 39.4 us  [swapped(): return lax.ppermute(x, axes, [(i, i ^ by) for i in range(size)])]
  transfers between devices with their start and end apart: 27 -> 30, of which waited for: 12 -> 10; matrix products, arithmetic and copies ran while one was open for 1% -> 2% of each run, Pallas kernels for 25% -> 25%
where the time goes in v7:
time: 136 us; the launch traced here: 135 us
  starting transfers between devices  46.3 us (34%)
  Pallas kernels  41.4 us (30%)
  waiting for transfers between devices  38.3 us (28%)
  local copies, waits for them, and re-layouts  6.8 us (5%)
  other arithmetic  1.81 us (1%)
    ppermute x25, starting transfers between devices, swapped(): return lax.ppermute(x, axes, [(i, i ^ by) for i in range(size)])  39.4 us
    ppermute x25, waiting for transfers between devices, swapped(): return lax.ppermute(x, axes, [(i, i ^ by) for i in range(size)])  36.7 us
    pallas_call x2, Pallas kernels, filter_orbitals(): pl.pallas_call(functools.partial(filter_kernel, n_dom, planes, rows, star...  14.2 us
    pallas_call x1, Pallas kernels, build_projectors(): pl.pallas_call(functools.partial(projector_kernel, n_band, n_sub), out_sh...  11.5 us
    pallas_call x2, Pallas kernels, products(): pl.pallas_call(functools.partial(product_kernel, spots, n_sub, first_row,...  8.14 us
    ppermute x5, starting transfers between devices, on_device(): sums.append(lax.ppermute(x, ('dom', 'band'), pairs))  6.91 us
    unnamed x16, local copies, waits for them, and re-layouts  5.22 us
    pallas_call x2, Pallas kernels, pack(): pl.pallas_call(functools.partial(pack_kernel, n_dom, size, contents), out...  3.31 us
  transfers between devices with their start and end apart: 30, of which 10 were waited for; matrix products, arithmetic and copies ran while one was open for 2% of the time, Pallas kernels for 25%

profile of v7, /device:TPU:0, one launch (start us, length us, event | category | flops | bytes accessed | tf_op | source)
XLA Modules:
  0.0 135.5 jit_solution(153920157712814545)
XLA Ops:
  0.6 0.0 copy-start
  0.7 0.1 pad_add_fusion.place
  0.7 1.4 %copy-done.1 = f32[32,3,32,128]{3,2,1,0:T(8,128)S(1)} copy-done((f32[32,3,32,128]{3,2,1,0:T(8,128)S(1)}, f32[32,3,32,128]{3,2,1,0:T(8,128)}, u32[]{:S(2)}) %copy-start.1) | copy-done | bytes 1572888
  2.1 0.8 copy-done.3
  2.9 1.7 %pack.2 = (f32[864,128]{1,0:T(8,128)S(1)}, f32[432,128]{1,0:T(8,128)S(1)}, f32[384,128]{1,0:T(8,128)S(1)}) custom-call(s32[4]{0:T(128)S(1)} %pad_add_fusion.place, f32[3072,128]{1,0:T(8,128)S(1)} %bitcast.16, f32[96,128]{1,0:T(8,128)S(1)} %bitcast.34), custom_call_target="tpu_custom_call" | custom-call | tf_op jit(solution)/shard_map/pack/pallas_call | solution.py:77
  4.7 4.1 %collective-permute-start = (f32[432,128]{1,0:T(8,128)S(1)}, f32[432,128]{1,0:T(8,128)S(1)}, u32[]{:S(2)}, u32[]{:S(2)}) collective-permute-start(f32[432,128]{1,0:T(8,128)S(1)} %get-tuple-element.55), channel_id=1, source_target_pairs={{0,8},{4,12},{8,0},{12,4},{1,9},{5,13},{9,1},{13,5},{2,10},{6,14},... | collective-permute-start | bytes 663560 | tf_op jit(solution)/shard_map/ppermute | solution.py:43
  8.8 1.6 %collective-permute-start.4 = (f32[864,128]{1,0:T(8,128)S(1)}, f32[864,128]{1,0:T(8,128)S(1)}, u32[]{:S(2)}, u32[]{:S(2)}) collective-permute-start(f32[864,128]{1,0:T(8,128)S(1)} %get-tuple-element.57), channel_id=1, source_target_pairs={{0,4},{4,0},{8,12},{12,8},{1,5},{5,1},{9,13},{13,9},{2,6},{6,2},{1... | collective-permute-start | bytes 1327112 | tf_op jit(solution)/shard_map/ppermute | solution.py:43
  10.3 0.1 constant_dynamic-slice_fusion
  10.4 9.4 %collective-permute-done.refs_7_ = f32[432,128]{1,0:T(8,128)S(1)} collective-permute-done((f32[432,128]{1,0:T(8,128)S(1)}, f32[432,128]{1,0:T(8,128)S(1)}, u32[]{:S(2)}, u32[]{:S(2)}) %collective-permute-start) | collective-permute-done | bytes 221216 | tf_op jit(solution)/shard_map/ppermute | solution.py:43
  19.8 0.0 collective-permute-start.2
  19.8 0.1 copy.8
  19.9 0.1 collective-permute-start.1
  20.0 7.7 %collective-permute-done.2.refs_3_ = f32[48,128]{1,0:T(8,128)S(1)} collective-permute-done((f32[48,128]{1,0:T(8,128)S(1)}, f32[48,128]{1,0:T(8,128)S(1)}, u32[]{:S(2)}, u32[]{:S(2)}) %collective-permute-start.2) | collective-permute-done | bytes 24608 | tf_op jit(solution)/shard_map/ppermute | solution.py:43
  27.7 1.0 broadcast_multiply_fusion
  28.7 1.4 %copy-done.2 = f32[32,3,32,128]{3,2,1,0:T(8,128)S(1)} copy-done((f32[32,3,32,128]{3,2,1,0:T(8,128)S(1)}, f32[32,3,32,128]{3,2,1,0:T(8,128)}, u32[]{:S(2)}) %copy-start.2) | copy-done | bytes 1572888
  30.1 0.8 copy-done.4
  30.9 1.6 %pack.3 = (f32[384,128]{1,0:T(8,128)S(1)}, f32[384,128]{1,0:T(8,128)S(1)}, f32[384,128]{1,0:T(8,128)S(1)}, f32[384,128]{1,0:T(8,128)S(1)}) custom-call(s32[4]{0:T(128)S(1)} %pad_add_fusion.place, f32[3072,128]{1,0:T(8,128)S(1)} %bitcast.17, f32[96,128]{1,0:T(8,128)S(1)} %bitcast.35), custom_call_target="tpu_custom_call" | custom-call | tf_op jit(solution)/shard_map/pack/pallas_call | solution.py:77
  32.5 1.4 %mul.32.corr_ref = f32[96,96]{1,0:T(8,128)S(1)} reshape(f32[12,8,12,8]{3,2,1,0:T(8,128)} %broadcast_multiply_fusion) | data formatting | bytes 73728 | tf_op jit(solution)/shard_map/mul | solution.py:539
  33.9 0.0 collective-permute-done.4.refs_6_.refs_2_
  33.9 2.4 %collective-permute-start.9 = (f32[384,128]{1,0:T(8,128)S(1)}, f32[384,128]{1,0:T(8,128)S(1)}, u32[]{:S(2)}, u32[]{:S(2)}) collective-permute-start(f32[384,128]{1,0:T(8,128)S(1)} %get-tuple-element.68), channel_id=1, source_target_pairs={{0,8},{4,12},{8,0},{12,4},{1,9},{5,13},{9,1},{13,5},{2,10},{6,14},... | collective-permute-start | bytes 589832 | tf_op jit(solution)/shard_map/ppermute | solution.py:43
  36.4 2.5 %collective-permute-start.10 = (f32[384,128]{1,0:T(8,128)S(1)}, f32[384,128]{1,0:T(8,128)S(1)}, u32[]{:S(2)}, u32[]{:S(2)}) collective-permute-start(f32[384,128]{1,0:T(8,128)S(1)} %get-tuple-element.69), channel_id=1, source_target_pairs={{0,12},{4,8},{8,4},{12,0},{1,13},{5,9},{9,5},{13,1},{2,14},{6,10},... | collective-permute-start | bytes 589832 | tf_op jit(solution)/shard_map/ppermute | solution.py:43
  38.8 0.0 collective-permute-done.5.refs_8_
  38.9 0.0 copy-start.5
  38.9 0.8 copy-done.5
  39.7 7.3 %chebyshev.2 = (f32[3,128,128]{2,1,0:T(8,128)S(1)}, f32[3,128,128]{2,1,0:T(8,128)S(1)}, f32[3,128,128]{2,1,0:T(8,128)S(1)}, f32[3,128,128]{2,1,0:T(8,128)S(1)}, f32[6,32,8,128]{3,2,1,0:T(8,128)S(1)}) custom-call(s32[4]{0:T(128)S(1)} %pad_add_fusion.place, f32[96,128]{1,0:T(8,128)S(1)} %bitcast.36, f32[48,128]{1,0:T(8,128)S(1)} %slice.4.refs_1_, ...), custom_call_target="tpu_custom_call" | custom-call | flops 28311552 | bytes 1572864 | tf_op jit(solution)/shard_map/chebyshev/pallas_call | solution.py:182
  46.9 0.1 collective-permute-start.6
  47.0 1.9 %collective-permute-start.7 = (f32[3,128,128]{2,1,0:T(8,128)S(1)}, f32[3,128,128]{2,1,0:T(8,128)S(1)}, u32[]{:S(2)}, u32[]{:S(2)}) collective-permute-start(f32[3,128,128]{2,1,0:T(8,128)S(1)} %get-tuple-element.64), channel_id=1, source_target_pairs={{0,8},{4,12},{8,0},{12,4},{1,9},{5,13},{9,1},{13,5},{2,10},{6,14},... | collective-permute-start | bytes 589832 | tf_op jit(solution)/shard_map/ppermute | solution.py:43
  48.9 2.5 %collective-permute-start.8 = (f32[3,128,128]{2,1,0:T(8,128)S(1)}, f32[3,128,128]{2,1,0:T(8,128)S(1)}, u32[]{:S(2)}, u32[]{:S(2)}) collective-permute-start(f32[3,128,128]{2,1,0:T(8,128)S(1)} %get-tuple-element.65), channel_id=1, source_target_pairs={{0,12},{4,8},{8,4},{12,0},{1,13},{5,9},{9,5},{13,1},{2,14},{6,10},... | collective-permute-start | bytes 589832 | tf_op jit(solution)/shard_map/ppermute | solution.py:43
  51.4 6.9 %chebyshev.3 = (f32[3,128,128]{2,1,0:T(8,128)S(1)}, f32[3,128,128]{2,1,0:T(8,128)S(1)}, f32[3,128,128]{2,1,0:T(8,128)S(1)}, f32[3,128,128]{2,1,0:T(8,128)S(1)}) custom-call(s32[4]{0:T(128)S(1)} %pad_add_fusion.place, f32[6,32,8,128]{3,2,1,0:T(8,128)S(1)} %get-tuple-element.66.refs_0_, f32[384,128]{1,0:T(8,128)S(1)} %get-tuple-element.67.refs_1_, ...), custom_call_target="tpu_custom_call" | custom-call | flops 28311552 | bytes 1572864 | tf_op jit(solution)/shard_map/chebyshev/pallas_call | solution.py:182
  58.3 12.9 %collective-permute-start.12 = (f32[3,128,128]{2,1,0:T(8,128)S(1)}, f32[3,128,128]{2,1,0:T(8,128)S(1)}, u32[]{:S(2)}, u32[]{:S(2)}) collective-permute-start(f32[3,128,128]{2,1,0:T(8,128)S(1)} %get-tuple-element.80), channel_id=1, source_target_pairs={{0,4},{4,0},{8,12},{12,8},{1,5},{5,1},{9,13},{13,9},{2,6},{6,2},{1... | collective-permute-start | bytes 589832 | tf_op jit(solution)/shard_map/ppermute | solution.py:43
  71.2 0.6 collective-permute-start.13
  71.9 1.8 %collective-permute-start.14 = (f32[3,128,128]{2,1,0:T(8,128)S(1)}, f32[3,128,128]{2,1,0:T(8,128)S(1)}, u32[]{:S(2)}, u32[]{:S(2)}) collective-permute-start(f32[3,128,128]{2,1,0:T(8,128)S(1)} %get-tuple-element.82), channel_id=1, source_target_pairs={{0,12},{4,8},{8,4},{12,0},{1,13},{5,9},{9,5},{13,1},{2,14},{6,10},... | collective-permute-start | bytes 589832 | tf_op jit(solution)/shard_map/ppermute | solution.py:43
  73.7 11.5 %projectors.1 = (bf16[576,6144]{1,0:T(8,128)(2,1)S(1)}, bf16[576,6144]{1,0:T(8,128)(2,1)S(1)}) custom-call(s32[4]{0:T(128)S(1)} %pad_add_fusion.place, s32[3,48,128]{2,1,0:T(8,128)S(1)} %bitcast.37, f32[48,3,8,128]{3,2,1,0:T(8,128)S(1)} %copy-done.6), custom_call_target="tpu_custom_call" | custom-call | flops 1811939328 | bytes 28311552 | tf_op jit(solution)/shard_map/projectors/pallas_call | solution.py:313
  85.2 0.0 collective-permute-done.8
  85.2 0.7 cell_first.2
  85.8 1.6 %collective-permute-start.11 = (f32[48,16,128]{2,1,0:T(8,128)S(1)}, f32[48,16,128]{2,1,0:T(8,128)S(1)}, u32[]{:S(2)}, u32[]{:S(2)}) collective-permute-start(f32[48,16,128]{2,1,0:T(8,128)S(1)} %get-tuple-element.78), channel_id=1, source_target_pairs={{0,2},{2,0},{1,3},{3,1},{4,6},{6,4},{5,7},{7,5},{8,10},{10,8},{9,1... | collective-permute-start | bytes 1179656 | tf_op jit(solution)/shard_map/ppermute | solution.py:43
  87.4 1.0 collective-permute-done.13
  88.4 0.0 collective-permute-done.14
  88.4 0.7 cell_first.3
  89.1 1.6 %collective-permute-start.15 = (f32[48,16,128]{2,1,0:T(8,128)S(1)}, f32[48,16,128]{2,1,0:T(8,128)S(1)}, u32[]{:S(2)}, u32[]{:S(2)}) collective-permute-start(f32[48,16,128]{2,1,0:T(8,128)S(1)} %get-tuple-element.89), channel_id=1, source_target_pairs={{0,2},{2,0},{1,3},{3,1},{4,6},{6,4},{5,7},{7,5},{8,10},{10,8},{9,1... | collective-permute-start | bytes 1179656 | tf_op jit(solution)/shard_map/ppermute | solution.py:43
  90.6 0.1 pad_maximum_fusion
  90.7 0.1 collective-permute-start.16
  90.8 1.8 %orbital_first.1 = f32[32,96,128]{2,1,0:T(8,128)} custom-call(s32[4]{0:T(128)S(1)} %pad_add_fusion.place, f32[384,128]{1,0:T(8,128)S(1)} %bitcast.19, f32[384,128]{1,0:T(8,128)S(1)} %bitcast.21, f32[384,128]{1,0:T(8,128)S(1)} %bitcast.23, f32[384,128]{1,0:T(8,128)S(1)} %bitcast.25, f32[384,128]{1,0:T(8,128)S(1)} %bitcast.27, f32[384,128]{1,0:T(8,128)S(1)} %bitcast.29, ...), custom_call_target="tpu_custom_call" | custom-call | flops 393216 | bytes 3145728 | tf_op jit(solution)/shard_map/orbital_first/pallas_call | solution.py:249
  92.6 5.4 %collective-permute-done.11.refs_2_ = f32[48,16,128]{2,1,0:T(8,128)S(1)} collective-permute-done((f32[48,16,128]{2,1,0:T(8,128)S(1)}, f32[48,16,128]{2,1,0:T(8,128)S(1)}, u32[]{:S(2)}, u32[]{:S(2)}) %collective-permute-start.11) | collective-permute-done | bytes 393248 | tf_op jit(solution)/shard_map/ppermute | solution.py:43
  97.9 0.0 collective-permute-start.17
  98.0 6.2 %collective-permute-done.15.refs_3_ = f32[48,16,128]{2,1,0:T(8,128)S(1)} collective-permute-done((f32[48,16,128]{2,1,0:T(8,128)S(1)}, f32[48,16,128]{2,1,0:T(8,128)S(1)}, u32[]{:S(2)}, u32[]{:S(2)}) %collective-permute-start.15) | collective-permute-done | bytes 393248 | tf_op jit(solution)/shard_map/ppermute | solution.py:43
  104.1 1.7 %collective-permute-done.18.refs_6_ = f32[48,16,128]{2,1,0:T(8,128)S(1)} collective-permute-done((f32[48,16,128]{2,1,0:T(8,128)S(1)}, f32[48,16,128]{2,1,0:T(8,128)S(1)}, u32[]{:S(2)}, u32[]{:S(2)}) %collective-permute-start.18) | collective-permute-done | bytes 393248 | tf_op jit(solution)/shard_map/ppermute | solution.py:43
  105.8 4.5 %products.2 = (f32[96,128]{1,0:T(8,128)S(1)}, f32[96,128]{1,0:T(8,128)S(1)}, f32[96,128]{1,0:T(8,128)S(1)}, f32[96,128]{1,0:T(8,128)S(1)}, f32[96,128]{1,0:T(8,128)S(1)}) custom-call(s32[4]{0:T(128)S(1)} %pad_add_fusion.place, bf16[576,6144]{1,0:T(8,128)(2,1)S(1)} %get-tuple-element.84.w_high, bf16[576,6144]{1,0:T(8,128)(2,1)S(1)} %get-tuple-element.85.w_low, ...), custom_call_target="tpu_custom_call" | custom-call | flops 4529848320 | bytes 11796480 | tf_op jit(solution)/shard_map/products/pallas_call | solution.py:387
  110.3 2.5 %collective-permute-start.19 = (f32[96,128]{1,0:T(8,128)S(1)}, f32[96,128]{1,0:T(8,128)S(1)}, u32[]{:S(2)}, u32[]{:S(2)}) collective-permute-start(f32[96,128]{1,0:T(8,128)S(1)} %get-tuple-element.99), channel_id=1, source_target_pairs={{0,12},{2,14},{4,0},{6,2},{8,4},{10,6},{12,8},{14,10},{1,13},{3,15... | collective-permute-start | bytes 147464 | tf_op jit(solution)/shard_map/ppermute | solution.py:607
  112.8 1.7 %collective-permute-start.20 = (f32[96,128]{1,0:T(8,128)S(1)}, f32[96,128]{1,0:T(8,128)S(1)}, u32[]{:S(2)}, u32[]{:S(2)}) collective-permute-start(f32[96,128]{1,0:T(8,128)S(1)} %get-tuple-element.100), channel_id=1, source_target_pairs={{0,14},{2,12},{4,2},{6,0},{8,6},{10,4},{12,10},{14,8},{1,15},{3,13... | collective-permute-start | bytes 147464 | tf_op jit(solution)/shard_map/ppermute | solution.py:607
  114.5 1.3 collective-permute-start.21
  115.8 1.5 %collective-permute-start.23 = (f32[96,128]{1,0:T(8,128)S(1)}, f32[96,128]{1,0:T(8,128)S(1)}, u32[]{:S(2)}, u32[]{:S(2)}) collective-permute-start(f32[96,128]{1,0:T(8,128)S(1)} %get-tuple-element.103), channel_id=1, source_target_pairs={{0,2},{2,0},{4,6},{6,4},{8,10},{10,8},{12,14},{14,12},{1,3},{3,1},... | collective-permute-start | bytes 147464 | tf_op jit(solution)/shard_map/ppermute | solution.py:607
  117.2 3.7 %products.3 = (f32[128,128]{1,0:T(8,128)S(1)}, f32[96,128]{1,0:T(8,128)S(1)}) custom-call(s32[4]{0:T(128)S(1)} %pad_add_fusion.place, bf16[576,6144]{1,0:T(8,128)(2,1)S(1)} %get-tuple-element.84.w_high, bf16[576,6144]{1,0:T(8,128)(2,1)S(1)} %get-tuple-element.85.w_low, f32[48,16,128]{2,1,0:T(8,128)S(1)} %get-tuple-element.86.refs_0_, ...), custom_call_target="tpu_custom_call" | custom-call | flops 905969664 | bytes 2359296 | tf_op jit(solution)/shard_map/products/pallas_call | solution.py:387
  120.9 1.6 %collective-permute-done.22.refs_3_ = f32[96,128]{1,0:T(8,128)S(1)} collective-permute-done((f32[96,128]{1,0:T(8,128)S(1)}, f32[96,128]{1,0:T(8,128)S(1)}, u32[]{:S(2)}, u32[]{:S(2)}) %collective-permute-start.22) | collective-permute-done | bytes 49184 | tf_op jit(solution)/shard_map/ppermute | solution.py:607
  122.5 1.2 gram_share.1
  123.8 0.6 collective-permute-start.25
  124.4 1.6 %collective-permute-start.24 = (f32[32,128]{1,0:T(8,128)S(1)}, f32[32,128]{1,0:T(8,128)S(1)}, u32[]{:S(2)}, u32[]{:S(2)}) collective-permute-start(f32[32,128]{1,0:T(8,128)S(1)} %get-tuple-element.105), channel_id=1, source_target_pairs={{0,1},{1,0},{2,3},{3,2},{4,5},{5,4},{6,7},{7,6},{8,9},{9,8},{10,11... | collective-permute-start | bytes 49160 | tf_op jit(solution)/shard_map/ppermute | solution.py:43
  126.0 1.7 %collective-permute-done.25 = f32[32,128]{1,0:T(8,128)S(1)} collective-permute-done((f32[32,128]{1,0:T(8,128)S(1)}, f32[32,128]{1,0:T(8,128)S(1)}, u32[]{:S(2)}, u32[]{:S(2)}) %collective-permute-start.25) | collective-permute-done | bytes 16416 | tf_op jit(solution)/shard_map/ppermute | solution.py:43
  127.7 1.6 %collective-permute-start.28 = (f32[32,128]{1,0:T(8,128)S(1)}, f32[32,128]{1,0:T(8,128)S(1)}, u32[]{:S(2)}, u32[]{:S(2)}) collective-permute-start(f32[32,128]{1,0:T(8,128)S(1)} %add_add_fusion.1), channel_id=1, source_target_pairs={{0,8},{4,12},{8,0},{12,4},{1,9},{5,13},{9,1},{13,5},{2,10},{6,14},... | collective-permute-start | bytes 49160 | tf_op jit(solution)/shard_map/ppermute | solution.py:43
  129.3 0.8 collective-permute-start.29
  130.1 1.2 collective-permute-start.27
  131.3 1.1 collective-permute-done.28
  132.4 2.4 %collective-permute-done.29 = f32[32,128]{1,0:T(8,128)S(1)} collective-permute-done((f32[32,128]{1,0:T(8,128)S(1)}, f32[32,128]{1,0:T(8,128)S(1)}, u32[]{:S(2)}, u32[]{:S(2)}) %collective-permute-start.29) | collective-permute-done | bytes 16416 | tf_op jit(solution)/shard_map/ppermute | solution.py:43
  134.9 0.6 add_add_fusion
  (33 shorter events, 0.1 us)
Async XLA Ops:
  0.6 9.7 %copy-start = (f32[48,8,8]{0,2,1:T(8,128)S(1)}, f32[48,8,8]{0,2,1:T(8,128)}, u32[]{:S(2)}) copy-start(f32[48,8,8]{0,2,1:T(8,128)} %param.9) | copy-start | bytes 36868
  0.7 1.4 %copy-start.1 = (f32[32,3,32,128]{3,2,1,0:T(8,128)S(1)}, f32[32,3,32,128]{3,2,1,0:T(8,128)}, u32[]{:S(2)}) copy-start(f32[32,3,32,128]{3,2,1,0:T(8,128)} %param.5) | copy-start | bytes 4718596
  2.1 0.8 copy-start.3
  2.9 70.7 %copy-start.6 = (f32[48,3,8,128]{3,2,1,0:T(8,128)S(1)}, f32[48,3,8,128]{3,2,1,0:T(8,128)}, u32[]{:S(2)}) copy-start(f32[48,3,8,128]{3,2,1,0:T(8,128)} %coefs_ref.1) | copy-start | bytes 1769476
  2.9 70.7 %copy-start.7 = (s32[48,3,128]{2,0,1:T(8,128)S(1)}, s32[48,3,128]{2,0,1:T(8,128)}, u32[]{:S(2)}) copy-start(s32[48,3,128]{2,0,1:T(8,128)} %param.7) | copy-start | bytes 221188
  4.7 15.1 %collective-permute-start = (f32[432,128]{1,0:T(8,128)S(1)}, f32[432,128]{1,0:T(8,128)S(1)}, u32[]{:S(2)}, u32[]{:S(2)}) collective-permute-start(f32[432,128]{1,0:T(8,128)S(1)} %get-tuple-element.55), channel_id=1, source_target_pairs={{0,8},{4,12},{8,0},{12,4},{1,9},{5,13},{9,1},{13,5},{2,10},{6,14},... | collective-permute-start | bytes 663560 | tf_op jit(solution)/shard_map/ppermute | solution.py:43
  8.8 25.2 %collective-permute-start.4 = (f32[864,128]{1,0:T(8,128)S(1)}, f32[864,128]{1,0:T(8,128)S(1)}, u32[]{:S(2)}, u32[]{:S(2)}) collective-permute-start(f32[864,128]{1,0:T(8,128)S(1)} %get-tuple-element.57), channel_id=1, source_target_pairs={{0,4},{4,0},{8,12},{12,8},{1,5},{5,1},{9,13},{13,9},{2,6},{6,2},{1... | collective-permute-start | bytes 1327112 | tf_op jit(solution)/shard_map/ppermute | solution.py:43
  10.3 28.5 %collective-permute-start.5 = (f32[384,128]{1,0:T(8,128)S(1)}, f32[384,128]{1,0:T(8,128)S(1)}, u32[]{:S(2)}, u32[]{:S(2)}) collective-permute-start(f32[384,128]{1,0:T(8,128)S(1)} %get-tuple-element.61), channel_id=1, source_target_pairs={{0,12},{4,8},{8,4},{12,0},{1,13},{5,9},{9,5},{13,1},{2,14},{6,10},... | collective-permute-start | bytes 589832 | tf_op jit(solution)/shard_map/ppermute | solution.py:43
  19.8 7.9 %collective-permute-start.2 = (f32[48,128]{1,0:T(8,128)S(1)}, f32[48,128]{1,0:T(8,128)S(1)}, u32[]{:S(2)}, u32[]{:S(2)}) collective-permute-start(f32[48,128]{1,0:T(8,128)S(1)} %slice.4.refs_1_), channel_id=1, source_target_pairs={{0,4},{4,0},{8,12},{12,8},{1,5},{5,1},{9,13},{13,9},{2,6},{6,2},{1... | collective-permute-start | bytes 73736 | tf_op jit(solution)/shard_map/ppermute | solution.py:43
  19.9 18.9 %collective-permute-start.1 = (f32[48,128]{1,0:T(8,128)S(1)}, f32[48,128]{1,0:T(8,128)S(1)}, u32[]{:S(2)}, u32[]{:S(2)}) collective-permute-start(f32[48,128]{1,0:T(8,128)S(1)} %slice.4.refs_1_), channel_id=1, source_target_pairs={{0,1},{1,0},{2,3},{3,2},{4,5},{5,4},{6,7},{7,6},{8,9},{9,8},{10,11... | collective-permute-start | bytes 73736 | tf_op jit(solution)/shard_map/ppermute | solution.py:43
  27.7 11.1 %collective-permute-start.3 = (f32[48,128]{1,0:T(8,128)S(1)}, f32[48,128]{1,0:T(8,128)S(1)}, u32[]{:S(2)}, u32[]{:S(2)}) collective-permute-start(f32[48,128]{1,0:T(8,128)S(1)} %collective-permute-done.2.refs_3_), channel_id=1, source_target_pairs={{0,1},{1,0},{2,3},{3,2},{4,5},{5,4},{6,7},{7,6},{8,9},{9,8},{10,11... | collective-permute-start | bytes 73736 | tf_op jit(solution)/shard_map/ppermute | solution.py:43
  28.7 1.4 %copy-start.2 = (f32[32,3,32,128]{3,2,1,0:T(8,128)S(1)}, f32[32,3,32,128]{3,2,1,0:T(8,128)}, u32[]{:S(2)}) copy-start(f32[32,3,32,128]{3,2,1,0:T(8,128)} %param.5) | copy-start | bytes 4718596
  30.1 0.8 copy-start.4
  33.9 17.4 %collective-permute-start.9 = (f32[384,128]{1,0:T(8,128)S(1)}, f32[384,128]{1,0:T(8,128)S(1)}, u32[]{:S(2)}, u32[]{:S(2)}) collective-permute-start(f32[384,128]{1,0:T(8,128)S(1)} %get-tuple-element.68), channel_id=1, source_target_pairs={{0,8},{4,12},{8,0},{12,4},{1,9},{5,13},{9,1},{13,5},{2,10},{6,14},... | collective-permute-start | bytes 589832 | tf_op jit(solution)/shard_map/ppermute | solution.py:43
  36.4 15.0 %collective-permute-start.10 = (f32[384,128]{1,0:T(8,128)S(1)}, f32[384,128]{1,0:T(8,128)S(1)}, u32[]{:S(2)}, u32[]{:S(2)}) collective-permute-start(f32[384,128]{1,0:T(8,128)S(1)} %get-tuple-element.69), channel_id=1, source_target_pairs={{0,12},{4,8},{8,4},{12,0},{1,13},{5,9},{9,5},{13,1},{2,14},{6,10},... | collective-permute-start | bytes 589832 | tf_op jit(solution)/shard_map/ppermute | solution.py:43
  38.9 0.8 copy-start.5
  46.9 24.9 %collective-permute-start.6 = (f32[3,128,128]{2,1,0:T(8,128)S(1)}, f32[3,128,128]{2,1,0:T(8,128)S(1)}, u32[]{:S(2)}, u32[]{:S(2)}) collective-permute-start(f32[3,128,128]{2,1,0:T(8,128)S(1)} %get-tuple-element.63), channel_id=1, source_target_pairs={{0,4},{4,0},{8,12},{12,8},{1,5},{5,1},{9,13},{13,9},{2,6},{6,2},{1... | collective-permute-start | bytes 589832 | tf_op jit(solution)/shard_map/ppermute | solution.py:43
  47.0 38.1 %collective-permute-start.7 = (f32[3,128,128]{2,1,0:T(8,128)S(1)}, f32[3,128,128]{2,1,0:T(8,128)S(1)}, u32[]{:S(2)}, u32[]{:S(2)}) collective-permute-start(f32[3,128,128]{2,1,0:T(8,128)S(1)} %get-tuple-element.64), channel_id=1, source_target_pairs={{0,8},{4,12},{8,0},{12,4},{1,9},{5,13},{9,1},{13,5},{2,10},{6,14},... | collective-permute-start | bytes 589832 | tf_op jit(solution)/shard_map/ppermute | solution.py:43
  48.9 36.2 %collective-permute-start.8 = (f32[3,128,128]{2,1,0:T(8,128)S(1)}, f32[3,128,128]{2,1,0:T(8,128)S(1)}, u32[]{:S(2)}, u32[]{:S(2)}) collective-permute-start(f32[3,128,128]{2,1,0:T(8,128)S(1)} %get-tuple-element.65), channel_id=1, source_target_pairs={{0,12},{4,8},{8,4},{12,0},{1,13},{5,9},{9,5},{13,1},{2,14},{6,10},... | collective-permute-start | bytes 589832 | tf_op jit(solution)/shard_map/ppermute | solution.py:43
  58.3 29.1 %collective-permute-start.12 = (f32[3,128,128]{2,1,0:T(8,128)S(1)}, f32[3,128,128]{2,1,0:T(8,128)S(1)}, u32[]{:S(2)}, u32[]{:S(2)}) collective-permute-start(f32[3,128,128]{2,1,0:T(8,128)S(1)} %get-tuple-element.80), channel_id=1, source_target_pairs={{0,4},{4,0},{8,12},{12,8},{1,5},{5,1},{9,13},{13,9},{2,6},{6,2},{1... | collective-permute-start | bytes 589832 | tf_op jit(solution)/shard_map/ppermute | solution.py:43
  71.2 17.2 %collective-permute-start.13 = (f32[3,128,128]{2,1,0:T(8,128)S(1)}, f32[3,128,128]{2,1,0:T(8,128)S(1)}, u32[]{:S(2)}, u32[]{:S(2)}) collective-permute-start(f32[3,128,128]{2,1,0:T(8,128)S(1)} %get-tuple-element.81), channel_id=1, source_target_pairs={{0,8},{4,12},{8,0},{12,4},{1,9},{5,13},{9,1},{13,5},{2,10},{6,14},... | collective-permute-start | bytes 589832 | tf_op jit(solution)/shard_map/ppermute | solution.py:43
  71.9 16.5 %collective-permute-start.14 = (f32[3,128,128]{2,1,0:T(8,128)S(1)}, f32[3,128,128]{2,1,0:T(8,128)S(1)}, u32[]{:S(2)}, u32[]{:S(2)}) collective-permute-start(f32[3,128,128]{2,1,0:T(8,128)S(1)} %get-tuple-element.82), channel_id=1, source_target_pairs={{0,12},{4,8},{8,4},{12,0},{1,13},{5,9},{9,5},{13,1},{2,14},{6,10},... | collective-permute-start | bytes 589832 | tf_op jit(solution)/shard_map/ppermute | solution.py:43
  85.8 12.1 %collective-permute-start.11 = (f32[48,16,128]{2,1,0:T(8,128)S(1)}, f32[48,16,128]{2,1,0:T(8,128)S(1)}, u32[]{:S(2)}, u32[]{:S(2)}) collective-permute-start(f32[48,16,128]{2,1,0:T(8,128)S(1)} %get-tuple-element.78), channel_id=1, source_target_pairs={{0,2},{2,0},{1,3},{3,1},{4,6},{6,4},{5,7},{7,5},{8,10},{10,8},{9,1... | collective-permute-start | bytes 1179656 | tf_op jit(solution)/shard_map/ppermute | solution.py:43
  89.1 15.1 %collective-permute-start.15 = (f32[48,16,128]{2,1,0:T(8,128)S(1)}, f32[48,16,128]{2,1,0:T(8,128)S(1)}, u32[]{:S(2)}, u32[]{:S(2)}) collective-permute-start(f32[48,16,128]{2,1,0:T(8,128)S(1)} %get-tuple-element.89), channel_id=1, source_target_pairs={{0,2},{2,0},{1,3},{3,1},{4,6},{6,4},{5,7},{7,5},{8,10},{10,8},{9,1... | collective-permute-start | bytes 1179656 | tf_op jit(solution)/shard_map/ppermute | solution.py:43
  90.7 13.4 %collective-permute-start.16 = (f32[48,32,128]{2,1,0:T(8,128)S(1)}, f32[48,32,128]{2,1,0:T(8,128)S(1)}, u32[]{:S(2)}, u32[]{:S(2)}) collective-permute-start(f32[48,32,128]{2,1,0:T(8,128)S(1)} %pad_maximum_fusion), channel_id=1, source_target_pairs={{0,1},{1,0},{2,3},{3,2},{4,5},{5,4},{6,7},{7,6},{8,9},{9,8},{10,11... | collective-permute-start | bytes 2359304 | tf_op jit(solution)/shard_map/ppermute | solution.py:43
  97.9 6.2 %collective-permute-start.17 = (f32[48,16,128]{2,1,0:T(8,128)S(1)}, f32[48,16,128]{2,1,0:T(8,128)S(1)}, u32[]{:S(2)}, u32[]{:S(2)}) collective-permute-start(f32[48,16,128]{2,1,0:T(8,128)S(1)} %collective-permute-done.11.refs_2_), channel_id=1, source_target_pairs={{0,1},{1,0},{2,3},{3,2},{4,5},{5,4},{6,7},{7,6},{8,9},{9,8},{10,11... | collective-permute-start | bytes 1179656 | tf_op jit(solution)/shard_map/ppermute | solution.py:43
  104.1 1.7 %collective-permute-start.18 = (f32[48,16,128]{2,1,0:T(8,128)S(1)}, f32[48,16,128]{2,1,0:T(8,128)S(1)}, u32[]{:S(2)}, u32[]{:S(2)}) collective-permute-start(f32[48,16,128]{2,1,0:T(8,128)S(1)} %collective-permute-done.15.refs_3_), channel_id=1, source_target_pairs={{0,1},{1,0},{2,3},{3,2},{4,5},{5,4},{6,7},{7,6},{8,9},{9,8},{10,11... | collective-permute-start | bytes 1179656 | tf_op jit(solution)/shard_map/ppermute | solution.py:43
  110.3 10.6 %collective-permute-start.19 = (f32[96,128]{1,0:T(8,128)S(1)}, f32[96,128]{1,0:T(8,128)S(1)}, u32[]{:S(2)}, u32[]{:S(2)}) collective-permute-start(f32[96,128]{1,0:T(8,128)S(1)} %get-tuple-element.99), channel_id=1, source_target_pairs={{0,12},{2,14},{4,0},{6,2},{8,4},{10,6},{12,8},{14,10},{1,13},{3,15... | collective-permute-start | bytes 147464 | tf_op jit(solution)/shard_map/ppermute | solution.py:607
  112.8 8.1 %collective-permute-start.20 = (f32[96,128]{1,0:T(8,128)S(1)}, f32[96,128]{1,0:T(8,128)S(1)}, u32[]{:S(2)}, u32[]{:S(2)}) collective-permute-start(f32[96,128]{1,0:T(8,128)S(1)} %get-tuple-element.100), channel_id=1, source_target_pairs={{0,14},{2,12},{4,2},{6,0},{8,6},{10,4},{12,10},{14,8},{1,15},{3,13... | collective-permute-start | bytes 147464 | tf_op jit(solution)/shard_map/ppermute | solution.py:607
  114.5 6.4 %collective-permute-start.21 = (f32[96,128]{1,0:T(8,128)S(1)}, f32[96,128]{1,0:T(8,128)S(1)}, u32[]{:S(2)}, u32[]{:S(2)}) collective-permute-start(f32[96,128]{1,0:T(8,128)S(1)} %get-tuple-element.101), channel_id=1, source_target_pairs={{0,4},{2,6},{4,8},{6,10},{8,12},{10,14},{12,0},{14,2},{1,5},{3,7},... | collective-permute-start | bytes 147464 | tf_op jit(solution)/shard_map/ppermute | solution.py:607
  115.8 6.8 %collective-permute-start.22 = (f32[96,128]{1,0:T(8,128)S(1)}, f32[96,128]{1,0:T(8,128)S(1)}, u32[]{:S(2)}, u32[]{:S(2)}) collective-permute-start(f32[96,128]{1,0:T(8,128)S(1)} %get-tuple-element.102), channel_id=1, source_target_pairs={{0,6},{2,4},{4,10},{6,8},{8,14},{10,12},{12,2},{14,0},{1,7},{3,5},... | collective-permute-start | bytes 147464 | tf_op jit(solution)/shard_map/ppermute | solution.py:607
  115.8 6.8 %collective-permute-start.23 = (f32[96,128]{1,0:T(8,128)S(1)}, f32[96,128]{1,0:T(8,128)S(1)}, u32[]{:S(2)}, u32[]{:S(2)}) collective-permute-start(f32[96,128]{1,0:T(8,128)S(1)} %get-tuple-element.103), channel_id=1, source_target_pairs={{0,2},{2,0},{4,6},{6,4},{8,10},{10,8},{12,14},{14,12},{1,3},{3,1},... | collective-permute-start | bytes 147464 | tf_op jit(solution)/shard_map/ppermute | solution.py:607
  123.8 3.9 %collective-permute-start.25 = (f32[32,128]{1,0:T(8,128)S(1)}, f32[32,128]{1,0:T(8,128)S(1)}, u32[]{:S(2)}, u32[]{:S(2)}) collective-permute-start(f32[32,128]{1,0:T(8,128)S(1)} %get-tuple-element.106), channel_id=1, source_target_pairs={{0,2},{1,3},{2,0},{3,1},{4,6},{5,7},{6,4},{7,5},{8,10},{9,11},{10,... | collective-permute-start | bytes 49160 | tf_op jit(solution)/shard_map/ppermute | solution.py:43
  124.4 3.3 %collective-permute-start.26 = (f32[32,128]{1,0:T(8,128)S(1)}, f32[32,128]{1,0:T(8,128)S(1)}, u32[]{:S(2)}, u32[]{:S(2)}) collective-permute-start(f32[32,128]{1,0:T(8,128)S(1)} %get-tuple-element.107), channel_id=1, source_target_pairs={{0,3},{1,2},{2,1},{3,0},{4,7},{5,6},{6,5},{7,4},{8,11},{9,10},{10,... | collective-permute-start | bytes 49160 | tf_op jit(solution)/shard_map/ppermute | solution.py:43
  124.4 3.3 %collective-permute-start.24 = (f32[32,128]{1,0:T(8,128)S(1)}, f32[32,128]{1,0:T(8,128)S(1)}, u32[]{:S(2)}, u32[]{:S(2)}) collective-permute-start(f32[32,128]{1,0:T(8,128)S(1)} %get-tuple-element.105), channel_id=1, source_target_pairs={{0,1},{1,0},{2,3},{3,2},{4,5},{5,4},{6,7},{7,6},{8,9},{9,8},{10,11... | collective-permute-start | bytes 49160 | tf_op jit(solution)/shard_map/ppermute | solution.py:43
  127.7 4.7 %collective-permute-start.28 = (f32[32,128]{1,0:T(8,128)S(1)}, f32[32,128]{1,0:T(8,128)S(1)}, u32[]{:S(2)}, u32[]{:S(2)}) collective-permute-start(f32[32,128]{1,0:T(8,128)S(1)} %add_add_fusion.1), channel_id=1, source_target_pairs={{0,8},{4,12},{8,0},{12,4},{1,9},{5,13},{9,1},{13,5},{2,10},{6,14},... | collective-permute-start | bytes 49160 | tf_op jit(solution)/shard_map/ppermute | solution.py:43
  129.3 5.5 %collective-permute-start.29 = (f32[32,128]{1,0:T(8,128)S(1)}, f32[32,128]{1,0:T(8,128)S(1)}, u32[]{:S(2)}, u32[]{:S(2)}) collective-permute-start(f32[32,128]{1,0:T(8,128)S(1)} %add_add_fusion.1), channel_id=1, source_target_pairs={{0,12},{4,8},{8,4},{12,0},{1,13},{5,9},{9,5},{13,1},{2,14},{6,10},... | collective-permute-start | bytes 49160 | tf_op jit(solution)/shard_map/ppermute | solution.py:43
  130.1 4.8 %collective-permute-start.27 = (f32[32,128]{1,0:T(8,128)S(1)}, f32[32,128]{1,0:T(8,128)S(1)}, u32[]{:S(2)}, u32[]{:S(2)}) collective-permute-start(f32[32,128]{1,0:T(8,128)S(1)} %add_add_fusion.1), channel_id=1, source_target_pairs={{0,4},{4,0},{8,12},{12,8},{1,5},{5,1},{9,13},{13,9},{2,6},{6,2},{1... | collective-permute-start | bytes 49160 | tf_op jit(solution)/shard_map/ppermute | solution.py:43

commit v8 on v6

--- a/solution.py
+++ b/solution.py
@@ -213,7 +213,9 @@
 
     def two_atoms(step, carry):
         shell = lax.rem(2 * (step // (n_band * pairs)), shells)
-        band = place[BAND] ^ ((step // pairs) % n_band)
+        seen = (step // pairs) % n_band
+        seen = jnp.where(shell == 1, n_band - 1 - seen, seen)
+        band = place[BAND] ^ seen
         first_atom = (place[SUB] * n_band + band) * own + 2 * (step % pairs)
         dense = []
         for i in range(2):
@@ -397,22 +399,17 @@
     def sent(x, m):
         return swapped(x, "dom", n_dom, m)
 
-    far = [jnp.concatenate([block(0, m), levels], axis=0) for m in range(2, n_dom)]
-    far, flat, levels = lax.optimization_barrier((far, flat, levels))
-    near = [block(0, 1), levels] + [block(c, 1) for c in range(1, n_chunks)]
-    near = sent(jnp.concatenate(near, axis=0), 1)
-    own = [block(c, 0) for c in range(n_chunks)]
-    own[0] = jnp.concatenate([own[0], levels], axis=0)
-    arrived = [[own[0], near] + [sent(x, m) for m, x in enumerate(far, start=2)]]
+    own = []
+    for m in range(n_dom):
+        blocks = [block(c, m) for c in range(n_chunks)]
+        blocks[0] = jnp.concatenate([blocks[0], levels], axis=0)
+        own.append(blocks)
+    near = sent(jnp.concatenate(own[1], axis=0), 1)
+    arrived = [[own[0][0], near] + [sent(own[m][0], m) for m in range(2, n_dom)]]
     for c in range(1, n_chunks):
-        blocks = [own[c], near]
-        for m in range(2, n_dom):
-            x = block(c, m)
-            arrived[c - 1][m - 1], x = lax.optimization_barrier((arrived[c - 1][m - 1], x))
-            blocks.append(sent(x, m))
-        arrived.append(blocks)
-    for blocks in arrived:
-        blocks[1] = arrived[0][1]
+        far = [own[m][c] for m in range(2, n_dom)]
+        near, far = lax.optimization_barrier((near, far))
+        arrived.append([own[0][c], near] + [sent(x, m) for m, x in enumerate(far, start=2)])
     diagonal = None
     done = []
     for c, blocks in enumerate(arrived):
@@ -473,12 +470,6 @@
     def build(offsets):
         return build_projectors(n_band, n_sub, place, offsets, point_coefs, share, lanes)
 
-    place, corr_matrix = lax.optimization_barrier((place, corr_matrix))
-
-    def build(offsets):
-        return build_projectors(n_band, n_sub, place, offsets, point_coefs, share, lanes)
-
-    filtered, parts = [], []
     if n_dom in (2, 4) and orbitals % (n_dom * TOGETHER) == 0 and planes * n_dom % 2 == 0:
         chunks = whole_columns(panel, potential, place, me)
         chunks[-1][0], point_offsets = lax.optimization_barrier((chunks[-1][0], point_offsets))
@@ -502,6 +493,7 @@
     arrays += [
         swapped(by_band[m], "band", n_band, m) for by_band in parts for m in range(1, n_band)
     ]
+    arrays[chunks], filtered = lax.optimization_barrier((arrays[chunks], filtered))
     pieces = [jnp.concatenate(arrays[:chunks], axis=1)] + arrays[chunks:]
     arrays += [swapped(x, "sub", n_sub, k) for k in range(1, n_sub) for x in pieces]
     width = arrays[0].shape[1]
@@ -519,30 +511,30 @@
                     else:
                         spots.append((base, c * width, width))
 
-    rows = own_atoms * channels * n_band
-    outer = products(
-        n_sub, 0, 2 * rows, 2 * n_band, False, place, projectors, arrays, spots
-    )
-    outer, place = lax.optimization_barrier((outer, place))
-    grid_part, *inner = products(
-        n_sub, 2 * rows, rows, n_band, True, place, projectors, arrays, spots
+    rows = own_atoms * channels
+    n_sent = 3 * n_band - 1
+    outgoing = products(
+        n_sub, 0, n_sent * rows, n_sent, False, place, projectors, arrays, spots
+    )
+    outgoing, place = lax.optimization_barrier((outgoing, place))
+    grid_part, own_proj = products(
+        n_sub, n_sent * rows, rows, 1, True, place, projectors, arrays, spots
     )
     sums, seen = [], []
-    for by, blocks in ((1, outer[:n_band]), (-1, outer[n_band:]), (0, inner)):
-        for m, x in enumerate(blocks):
-            if by == 0 and m == 0:
-                continue
-            pairs = [
-                (d * n_band + b, (d - by) % n_dom * n_band + (b ^ m))
-                for d in range(n_dom)
-                for b in range(n_band)
-            ]
-            seen.append(m * n_sub)
-            sums.append(lax.ppermute(x, ("dom", "band"), pairs))
+    to = [(by, m) for by in (1, -1) for m in range(n_band)]
+    to += [(0, m) for m in range(n_band - 1, 0, -1)]
+    for x, (by, m) in zip(outgoing, to):
+        pairs = [
+            (d * n_band + b, (d - by) % n_dom * n_band + (b ^ m))
+            for d in range(n_dom)
+            for b in range(n_band)
+        ]
+        seen.append(m * n_sub)
+        sums.append(lax.ppermute(x, ("dom", "band"), pairs))
     scale_point = 1.0 / (cells * lanes * n_dom)
     scale_atom = 1.0 / math.sqrt(own_atoms * groups * n_dom)
     shares = gram_share(
-        (scale_point, scale_atom), groups, seen, place, corr_matrix, grid_part, inner[0], sums
+        (scale_point, scale_atom), groups, seen, place, corr_matrix, grid_part, own_proj, sums
     )
     gram_rows = added(
         [swapped(x, ("band", "sub"), groups, m) if m else x for m, x in enumerate(shares)]

time: 128 us -> 125 us (0.977)
  waiting for transfers between devices: 38 us -> 33.7 us
    ppermute x22, waiting for transfers between devices: 34.7 us -> 31.4 us  [swapped(): return lax.ppermute(x, axes, [(i, i ^ by) for i in range(size)])]
  transfers between devices with their start and end apart: 27 -> 27, of which waited for: 12 -> 12; matrix products, arithmetic and copies ran while one was open for 1% -> 1% of each run, Pallas kernels for 25% -> 26%
where the time goes in v8:
time: 125 us; the launch traced here: 124 us
  starting transfers between devices  48.1 us (38%)
  Pallas kernels  38 us (30%)
  waiting for transfers between devices  33.7 us (27%)
  local copies, waits for them, and re-layouts  2.76 us (2%)
    ppermute x22, starting transfers between devices, swapped(): return lax.ppermute(x, axes, [(i, i ^ by) for i in range(size)])  40.2 us
    ppermute x22, waiting for transfers between devices, swapped(): return lax.ppermute(x, axes, [(i, i ^ by) for i in range(size)])  31.4 us
    pallas_call x2, Pallas kernels, filter_orbitals(): pl.pallas_call(functools.partial(filter_kernel, n_dom, planes, rows, star...  14 us
    pallas_call x1, Pallas kernels, build_projectors(): pl.pallas_call(functools.partial(projector_kernel, n_band, n_sub), out_sh...  11.5 us
    pallas_call x2, Pallas kernels, products(): pl.pallas_call(functools.partial(product_kernel, spots, n_sub, first_row,...  8.18 us
    ppermute x5, starting transfers between devices, on_device(): sums.append(lax.ppermute(x, ('dom', 'band'), pairs))  7.93 us
  transfers between devices with their start and end apart: 27, of which 12 were waited for; matrix products, arithmetic and copies ran while one was open for 1% of the time, Pallas kernels for 26%

profile of v8, /device:TPU:0, one launch (start us, length us, event | category | flops | bytes accessed | tf_op | source)
XLA Modules:
  0.0 124.4 jit_solution(10801180002603391598)
XLA Ops:
  0.6 0.0 copy-start
  0.7 2.3 %constant_dynamic-slice_fusion = (f32[384,128]{1,0:T(8,128)S(1)}, f32[384,128]{1,0:T(8,128)}, f32[384,128]{1,0:T(8,128)S(1)}, f32[384,128]{1,0:T(8,128)S(1)}, f3...) fusion(f32[3072,128]{1,0:T(8,128)} %bitcast.33, ...), kind=kLoop, calls=%fused_computation.10 | loop fusion | bytes 3145760 | tf_op jit(solution)/shard_map/dynamic_slice | solution.py:397
  3.0 3.1 %collective-permute-start = (f32[864,128]{1,0:T(8,128)S(1)}, f32[864,128]{1,0:T(8,128)S(1)}, u32[]{:S(2)}, u32[]{:S(2)}) collective-permute-start(f32[864,128]{1,0:T(8,128)S(1)} %pad_maximum_fusion.1), channel_id=1, source_target_pairs={{0,4},{4,0},{8,12},{12,8},{1,5},{5,1},{9,13},{13,9},{2,6},{6,2},{1... | collective-permute-start | bytes 1327112 | tf_op jit(solution)/shard_map/ppermute | solution.py:43
  6.1 2.7 %collective-permute-start.1 = (f32[480,128]{1,0:T(8,128)S(1)}, f32[480,128]{1,0:T(8,128)S(1)}, u32[]{:S(2)}, u32[]{:S(2)}) collective-permute-start(f32[480,128]{1,0:T(8,128)S(1)} %get-tuple-element.105), channel_id=1, source_target_pairs={{0,8},{4,12},{8,0},{12,4},{1,9},{5,13},{9,1},{13,5},{2,10},{6,14},... | collective-permute-start | bytes 737288 | tf_op jit(solution)/shard_map/ppermute | solution.py:43
  8.8 0.0 collective-permute-start.2
  8.8 0.1 constant_dynamic-slice_fusion.8
  8.9 0.1 copy.8
  9.0 0.1 broadcast_multiply_fusion
  9.2 0.3 mul.56.corr_ref
  9.4 0.0 copy-start.2
  9.5 0.1 pad_add_fusion.place
  9.5 12.0 %collective-permute-done.refs_1_.refs_2_ = f32[864,128]{1,0:T(8,128)S(1)} collective-permute-done((f32[864,128]{1,0:T(8,128)S(1)}, f32[864,128]{1,0:T(8,128)S(1)}, u32[]{:S(2)}, u32[]{:S(2)}) %collective-permute-start) | collective-permute-done | bytes 442400 | tf_op jit(solution)/shard_map/ppermute | solution.py:43
  21.5 3.0 %collective-permute-start.6 = (f32[384,128]{1,0:T(8,128)}, f32[384,128]{1,0:T(8,128)S(1)}, u32[]{:S(2)}, u32[]{:S(2)}) collective-permute-start(f32[384,128]{1,0:T(8,128)} %get-tuple-element.56), channel_id=1, source_target_pairs={{0,8},{4,12},{8,0},{12,4},{1,9},{5,13},{9,1},{13,5},{2,10},{6,14},... | collective-permute-start | bytes 589832 | tf_op jit(solution)/shard_map/ppermute | solution.py:43
  24.5 5.0 %collective-permute-start.7 = (f32[384,128]{1,0:T(8,128)S(1)}, f32[384,128]{1,0:T(8,128)S(1)}, u32[]{:S(2)}, u32[]{:S(2)}) collective-permute-start(f32[384,128]{1,0:T(8,128)S(1)} %get-tuple-element.57), channel_id=1, source_target_pairs={{0,12},{4,8},{8,4},{12,0},{1,13},{5,9},{9,5},{13,1},{2,14},{6,10},... | collective-permute-start | bytes 589832 | tf_op jit(solution)/shard_map/ppermute | solution.py:43
  29.5 0.0 collective-permute-done.1.refs_2_
  29.5 0.7 collective-permute-done.2.refs_3_
  30.2 7.2 %chebyshev.2 = (f32[3,128,128]{2,1,0:T(8,128)S(1)}, f32[3,128,128]{2,1,0:T(8,128)S(1)}, f32[3,128,128]{2,1,0:T(8,128)S(1)}, f32[3,128,128]{2,1,0:T(8,128)S(1)}, f32[6,32,8,128]{3,2,1,0:T(8,128)S(1)}) custom-call(s32[4]{0:T(128)S(1)} %pad_add_fusion.place, f32[480,128]{1,0:T(8,128)S(1)} %get-tuple-element.106.refs_0_, ...), custom_call_target="tpu_custom_call" | custom-call | flops 28311552 | bytes 1572864 | tf_op jit(solution)/shard_map/chebyshev/pallas_call | solution.py:129
  37.4 10.4 %collective-permute-start.3 = (f32[3,128,128]{2,1,0:T(8,128)S(1)}, f32[3,128,128]{2,1,0:T(8,128)S(1)}, u32[]{:S(2)}, u32[]{:S(2)}) collective-permute-start(f32[3,128,128]{2,1,0:T(8,128)S(1)} %get-tuple-element.51), channel_id=1, source_target_pairs={{0,4},{4,0},{8,12},{12,8},{1,5},{5,1},{9,13},{13,9},{2,6},{6,2},{1... | collective-permute-start | bytes 589832 | tf_op jit(solution)/shard_map/ppermute | solution.py:43
  47.8 1.3 %collective-permute-start.4 = (f32[3,128,128]{2,1,0:T(8,128)S(1)}, f32[3,128,128]{2,1,0:T(8,128)S(1)}, u32[]{:S(2)}, u32[]{:S(2)}) collective-permute-start(f32[3,128,128]{2,1,0:T(8,128)S(1)} %get-tuple-element.52), channel_id=1, source_target_pairs={{0,8},{4,12},{8,0},{12,4},{1,9},{5,13},{9,1},{13,5},{2,10},{6,14},... | collective-permute-start | bytes 589832 | tf_op jit(solution)/shard_map/ppermute | solution.py:43
  49.1 1.4 %collective-permute-start.5 = (f32[3,128,128]{2,1,0:T(8,128)S(1)}, f32[3,128,128]{2,1,0:T(8,128)S(1)}, u32[]{:S(2)}, u32[]{:S(2)}) collective-permute-start(f32[3,128,128]{2,1,0:T(8,128)S(1)} %get-tuple-element.53), channel_id=1, source_target_pairs={{0,12},{4,8},{8,4},{12,0},{1,13},{5,9},{9,5},{13,1},{2,14},{6,10},... | collective-permute-start | bytes 589832 | tf_op jit(solution)/shard_map/ppermute | solution.py:43
  50.5 0.0 collective-permute-done.6.refs_3_
  50.5 0.0 collective-permute-done.7.refs_4_
  50.5 6.8 %chebyshev.3 = (f32[3,128,128]{2,1,0:T(8,128)S(1)}, f32[3,128,128]{2,1,0:T(8,128)S(1)}, f32[3,128,128]{2,1,0:T(8,128)S(1)}, f32[3,128,128]{2,1,0:T(8,128)S(1)}) custom-call(s32[4]{0:T(128)S(1)} %pad_add_fusion.place, f32[6,32,8,128]{3,2,1,0:T(8,128)S(1)} %get-tuple-element.54.refs_0_, f32[384,128]{1,0:T(8,128)S(1)} %get-tuple-element.98.refs_1_, ...), custom_call_target="tpu_custom_call" | custom-call | flops 28311552 | bytes 1572864 | tf_op jit(solution)/shard_map/chebyshev/pallas_call | solution.py:129
  57.3 0.9 collective-permute-start.9
  58.2 2.2 %collective-permute-start.10 = (f32[3,128,128]{2,1,0:T(8,128)S(1)}, f32[3,128,128]{2,1,0:T(8,128)S(1)}, u32[]{:S(2)}, u32[]{:S(2)}) collective-permute-start(f32[3,128,128]{2,1,0:T(8,128)S(1)} %get-tuple-element.69), channel_id=1, source_target_pairs={{0,8},{4,12},{8,0},{12,4},{1,9},{5,13},{9,1},{13,5},{2,10},{6,14},... | collective-permute-start | bytes 589832 | tf_op jit(solution)/shard_map/ppermute | solution.py:43
  60.4 1.4 %collective-permute-start.11 = (f32[3,128,128]{2,1,0:T(8,128)S(1)}, f32[3,128,128]{2,1,0:T(8,128)S(1)}, u32[]{:S(2)}, u32[]{:S(2)}) collective-permute-start(f32[3,128,128]{2,1,0:T(8,128)S(1)} %get-tuple-element.70), channel_id=1, source_target_pairs={{0,12},{4,8},{8,4},{12,0},{1,13},{5,9},{9,5},{13,1},{2,14},{6,10},... | collective-permute-start | bytes 589832 | tf_op jit(solution)/shard_map/ppermute | solution.py:43
  61.8 11.5 %projectors.1 = (bf16[576,6144]{1,0:T(8,128)(2,1)S(1)}, bf16[576,6144]{1,0:T(8,128)(2,1)S(1)}) custom-call(s32[4]{0:T(128)S(1)} %pad_add_fusion.place, s32[3,48,128]{2,1,0:T(8,128)S(1)} %bitcast.32, f32[48,3,8,128]{3,2,1,0:T(8,128)S(1)} %copy-done.1), custom_call_target="tpu_custom_call" | custom-call | flops 1811939328 | bytes 28311552 | tf_op jit(solution)/shard_map/projectors/pallas_call | solution.py:255
  73.3 0.0 collective-permute-done.5
  73.3 0.7 cell_first.2
  73.9 1.6 %collective-permute-start.8 = (f32[48,16,128]{2,1,0:T(8,128)S(1)}, f32[48,16,128]{2,1,0:T(8,128)S(1)}, u32[]{:S(2)}, u32[]{:S(2)}) collective-permute-start(f32[48,16,128]{2,1,0:T(8,128)S(1)} %get-tuple-element.66), channel_id=1, source_target_pairs={{0,2},{2,0},{1,3},{3,1},{4,6},{6,4},{5,7},{7,5},{8,10},{10,8},{9,1... | collective-permute-start | bytes 1179656 | tf_op jit(solution)/shard_map/ppermute | solution.py:43
  75.5 3.8 %collective-permute-done.10 = f32[3,128,128]{2,1,0:T(8,128)S(1)} collective-permute-done((f32[3,128,128]{2,1,0:T(8,128)S(1)}, f32[3,128,128]{2,1,0:T(8,128)S(1)}, u32[]{:S(2)}, u32[]{:S(2)}) %collective-permute-start.10) | collective-permute-done | bytes 196640 | tf_op jit(solution)/shard_map/ppermute | solution.py:43
  79.3 0.7 cell_first.3
  80.0 1.6 %collective-permute-start.12 = (f32[48,16,128]{2,1,0:T(8,128)S(1)}, f32[48,16,128]{2,1,0:T(8,128)S(1)}, u32[]{:S(2)}, u32[]{:S(2)}) collective-permute-start(f32[48,16,128]{2,1,0:T(8,128)S(1)} %get-tuple-element.77), channel_id=1, source_target_pairs={{0,2},{2,0},{1,3},{3,1},{4,6},{6,4},{5,7},{7,5},{8,10},{10,8},{9,1... | collective-permute-start | bytes 1179656 | tf_op jit(solution)/shard_map/ppermute | solution.py:43
  81.5 0.1 pad_maximum_fusion
  81.6 0.1 collective-permute-start.13
  81.7 1.8 %orbital_first.1 = f32[32,96,128]{2,1,0:T(8,128)} custom-call(s32[4]{0:T(128)S(1)} %pad_add_fusion.place, f32[384,128]{1,0:T(8,128)S(1)} %bitcast.17, f32[384,128]{1,0:T(8,128)S(1)} %bitcast.19, f32[384,128]{1,0:T(8,128)S(1)} %bitcast.21, f32[384,128]{1,0:T(8,128)S(1)} %bitcast.23, f32[384,128]{1,0:T(8,128)S(1)} %bitcast.25, f32[384,128]{1,0:T(8,128)S(1)} %bitcast.27, ...), custom_call_target="tpu_custom_call" | custom-call | tf_op jit(solution)/shard_map/orbital_first/pallas_call | solution.py:194
  83.5 2.3 %collective-permute-done.8.refs_2_ = f32[48,16,128]{2,1,0:T(8,128)S(1)} collective-permute-done((f32[48,16,128]{2,1,0:T(8,128)S(1)}, f32[48,16,128]{2,1,0:T(8,128)S(1)}, u32[]{:S(2)}, u32[]{:S(2)}) %collective-permute-start.8) | collective-permute-done | bytes 393248 | tf_op jit(solution)/shard_map/ppermute | solution.py:43
  85.8 4.2 %collective-permute-done.12.refs_3_ = f32[48,16,128]{2,1,0:T(8,128)S(1)} collective-permute-done((f32[48,16,128]{2,1,0:T(8,128)S(1)}, f32[48,16,128]{2,1,0:T(8,128)S(1)}, u32[]{:S(2)}, u32[]{:S(2)}) %collective-permute-start.12) | collective-permute-done | bytes 393248 | tf_op jit(solution)/shard_map/ppermute | solution.py:43
  90.0 0.0 collective-permute-start.15
  90.0 0.0 collective-permute-done.14.refs_5_
  90.0 0.0 collective-permute-done.13.refs_4_
  90.0 1.7 %collective-permute-done.15.refs_6_ = f32[48,16,128]{2,1,0:T(8,128)S(1)} collective-permute-done((f32[48,16,128]{2,1,0:T(8,128)S(1)}, f32[48,16,128]{2,1,0:T(8,128)S(1)}, u32[]{:S(2)}, u32[]{:S(2)}) %collective-permute-start.15) | collective-permute-done | bytes 393248 | tf_op jit(solution)/shard_map/ppermute | solution.py:43
  91.7 4.5 %products.2 = (f32[96,128]{1,0:T(8,128)S(1)}, f32[96,128]{1,0:T(8,128)S(1)}, f32[96,128]{1,0:T(8,128)S(1)}, f32[96,128]{1,0:T(8,128)S(1)}, f32[96,128]{1,0:T(8,128)S(1)}) custom-call(s32[4]{0:T(128)S(1)} %pad_add_fusion.place, bf16[576,6144]{1,0:T(8,128)(2,1)S(1)} %get-tuple-element.72.w_high, bf16[576,6144]{1,0:T(8,128)(2,1)S(1)} %get-tuple-element.73.w_low, ...), custom_call_target="tpu_custom_call" | custom-call | flops 4529848320 | bytes 11796480 | tf_op jit(solution)/shard_map/products/pallas_call | solution.py:322
  96.2 2.7 %collective-permute-start.16 = (f32[96,128]{1,0:T(8,128)S(1)}, f32[96,128]{1,0:T(8,128)S(1)}, u32[]{:S(2)}, u32[]{:S(2)}) collective-permute-start(f32[96,128]{1,0:T(8,128)S(1)} %get-tuple-element.87), channel_id=1, source_target_pairs={{0,12},{2,14},{4,0},{6,2},{8,4},{10,6},{12,8},{14,10},{1,13},{3,15... | collective-permute-start | bytes 147464 | tf_op jit(solution)/shard_map/ppermute | solution.py:533
  98.9 4.4 %collective-permute-start.17 = (f32[96,128]{1,0:T(8,128)S(1)}, f32[96,128]{1,0:T(8,128)S(1)}, u32[]{:S(2)}, u32[]{:S(2)}) collective-permute-start(f32[96,128]{1,0:T(8,128)S(1)} %get-tuple-element.88), channel_id=1, source_target_pairs={{0,14},{2,12},{4,2},{6,0},{8,6},{10,4},{12,10},{14,8},{1,15},{3,13... | collective-permute-start | bytes 147464 | tf_op jit(solution)/shard_map/ppermute | solution.py:533
  103.4 0.0 collective-permute-start.18
  103.4 0.0 collective-permute-start.19
  103.4 0.8 collective-permute-start.20
  104.1 3.7 %products.3 = (f32[128,128]{1,0:T(8,128)S(1)}, f32[96,128]{1,0:T(8,128)S(1)}) custom-call(s32[4]{0:T(128)S(1)} %pad_add_fusion.place, bf16[576,6144]{1,0:T(8,128)(2,1)S(1)} %get-tuple-element.72.w_high, bf16[576,6144]{1,0:T(8,128)(2,1)S(1)} %get-tuple-element.73.w_low, f32[48,16,128]{2,1,0:T(8,128)S(1)} %get-tuple-element.74.refs_0_, ...), custom_call_target="tpu_custom_call" | custom-call | flops 905969664 | bytes 2359296 | tf_op jit(solution)/shard_map/products/pallas_call | solution.py:322
  107.9 0.0 collective-permute-done.17.refs_1_
  107.9 1.4 %collective-permute-done.18.refs_2_ = f32[96,128]{1,0:T(8,128)S(1)} collective-permute-done((f32[96,128]{1,0:T(8,128)S(1)}, f32[96,128]{1,0:T(8,128)S(1)}, u32[]{:S(2)}, u32[]{:S(2)}) %collective-permute-start.18) | collective-permute-done | bytes 49184 | tf_op jit(solution)/shard_map/ppermute | solution.py:533
  109.2 0.9 collective-permute-done.19.refs_3_
  110.1 1.2 gram_share.1
  111.4 1.2 collective-permute-start.22
  112.5 1.0 collective-permute-start.21
  113.6 1.6 %collective-permute-done.22 = f32[32,128]{1,0:T(8,128)S(1)} collective-permute-done((f32[32,128]{1,0:T(8,128)S(1)}, f32[32,128]{1,0:T(8,128)S(1)}, u32[]{:S(2)}, u32[]{:S(2)}) %collective-permute-start.22) | collective-permute-done | bytes 16416 | tf_op jit(solution)/shard_map/ppermute | solution.py:43
  115.2 0.5 collective-permute-done.23
  115.7 0.0 collective-permute-done.21
  115.7 2.5 %collective-permute-start.25 = (f32[32,128]{1,0:T(8,128)S(1)}, f32[32,128]{1,0:T(8,128)S(1)}, u32[]{:S(2)}, u32[]{:S(2)}) collective-permute-start(f32[32,128]{1,0:T(8,128)S(1)} %add_add_fusion.1), channel_id=1, source_target_pairs={{0,8},{4,12},{8,0},{12,4},{1,9},{5,13},{9,1},{13,5},{2,10},{6,14},... | collective-permute-start | bytes 49160 | tf_op jit(solution)/shard_map/ppermute | solution.py:43
  118.2 0.0 collective-permute-start.26
  118.2 1.0 collective-permute-start.24
  119.3 1.3 %collective-permute-done.25 = f32[32,128]{1,0:T(8,128)S(1)} collective-permute-done((f32[32,128]{1,0:T(8,128)S(1)}, f32[32,128]{1,0:T(8,128)S(1)}, u32[]{:S(2)}, u32[]{:S(2)}) %collective-permute-start.25) | collective-permute-done | bytes 16416 | tf_op jit(solution)/shard_map/ppermute | solution.py:43
  120.6 3.2 %collective-permute-done.26 = f32[32,128]{1,0:T(8,128)S(1)} collective-permute-done((f32[32,128]{1,0:T(8,128)S(1)}, f32[32,128]{1,0:T(8,128)S(1)}, u32[]{:S(2)}, u32[]{:S(2)}) %collective-permute-start.26) | collective-permute-done | bytes 16416 | tf_op jit(solution)/shard_map/ppermute | solution.py:43
  123.8 0.6 add_add_fusion
  (19 shorter events, 0.1 us)
Async XLA Ops:
  0.6 8.2 %copy-start = (f32[48,8,8]{0,2,1:T(8,128)S(1)}, f32[48,8,8]{0,2,1:T(8,128)}, u32[]{:S(2)}) copy-start(f32[48,8,8]{0,2,1:T(8,128)} %param.9) | copy-start | bytes 36868
  0.7 2.3 %copy-start.3 = (f32[3,32,128]{2,1,0:T(8,128)S(1)}, f32[3,32,128]{2,1,0:T(8,128)}, u32[]{:S(2)}) copy-start(f32[3,32,128]{2,1,0:T(8,128)} %param.6) | copy-start | bytes 147460
  3.0 18.5 %collective-permute-start = (f32[864,128]{1,0:T(8,128)S(1)}, f32[864,128]{1,0:T(8,128)S(1)}, u32[]{:S(2)}, u32[]{:S(2)}) collective-permute-start(f32[864,128]{1,0:T(8,128)S(1)} %pad_maximum_fusion.1), channel_id=1, source_target_pairs={{0,4},{4,0},{8,12},{12,8},{1,5},{5,1},{9,13},{13,9},{2,6},{6,2},{1... | collective-permute-start | bytes 1327112 | tf_op jit(solution)/shard_map/ppermute | solution.py:43
  6.1 23.4 %collective-permute-start.1 = (f32[480,128]{1,0:T(8,128)S(1)}, f32[480,128]{1,0:T(8,128)S(1)}, u32[]{:S(2)}, u32[]{:S(2)}) collective-permute-start(f32[480,128]{1,0:T(8,128)S(1)} %get-tuple-element.105), channel_id=1, source_target_pairs={{0,8},{4,12},{8,0},{12,4},{1,9},{5,13},{9,1},{13,5},{2,10},{6,14},... | collective-permute-start | bytes 737288 | tf_op jit(solution)/shard_map/ppermute | solution.py:43
  8.8 21.4 %collective-permute-start.2 = (f32[480,128]{1,0:T(8,128)S(1)}, f32[480,128]{1,0:T(8,128)S(1)}, u32[]{:S(2)}, u32[]{:S(2)}) collective-permute-start(f32[480,128]{1,0:T(8,128)S(1)} %get-tuple-element.104), channel_id=1, source_target_pairs={{0,12},{4,8},{8,4},{12,0},{1,13},{5,9},{9,5},{13,1},{2,14},{6,10},... | collective-permute-start | bytes 737288 | tf_op jit(solution)/shard_map/ppermute | solution.py:43
  9.4 52.4 %copy-start.1 = (f32[48,3,8,128]{3,2,1,0:T(8,128)S(1)}, f32[48,3,8,128]{3,2,1,0:T(8,128)}, u32[]{:S(2)}) copy-start(f32[48,3,8,128]{3,2,1,0:T(8,128)} %coefs_ref.1) | copy-start | bytes 1769476
  9.4 52.4 %copy-start.2 = (s32[48,3,128]{2,0,1:T(8,128)S(1)}, s32[48,3,128]{2,0,1:T(8,128)}, u32[]{:S(2)}) copy-start(s32[48,3,128]{2,0,1:T(8,128)} %param.7) | copy-start | bytes 221188
  21.5 29.0 %collective-permute-start.6 = (f32[384,128]{1,0:T(8,128)}, f32[384,128]{1,0:T(8,128)S(1)}, u32[]{:S(2)}, u32[]{:S(2)}) collective-permute-start(f32[384,128]{1,0:T(8,128)} %get-tuple-element.56), channel_id=1, source_target_pairs={{0,8},{4,12},{8,0},{12,4},{1,9},{5,13},{9,1},{13,5},{2,10},{6,14},... | collective-permute-start | bytes 589832 | tf_op jit(solution)/shard_map/ppermute | solution.py:43
  24.5 26.0 %collective-permute-start.7 = (f32[384,128]{1,0:T(8,128)S(1)}, f32[384,128]{1,0:T(8,128)S(1)}, u32[]{:S(2)}, u32[]{:S(2)}) collective-permute-start(f32[384,128]{1,0:T(8,128)S(1)} %get-tuple-element.57), channel_id=1, source_target_pairs={{0,12},{4,8},{8,4},{12,0},{1,13},{5,9},{9,5},{13,1},{2,14},{6,10},... | collective-permute-start | bytes 589832 | tf_op jit(solution)/shard_map/ppermute | solution.py:43
  37.4 23.0 %collective-permute-start.3 = (f32[3,128,128]{2,1,0:T(8,128)S(1)}, f32[3,128,128]{2,1,0:T(8,128)S(1)}, u32[]{:S(2)}, u32[]{:S(2)}) collective-permute-start(f32[3,128,128]{2,1,0:T(8,128)S(1)} %get-tuple-element.51), channel_id=1, source_target_pairs={{0,4},{4,0},{8,12},{12,8},{1,5},{5,1},{9,13},{13,9},{2,6},{6,2},{1... | collective-permute-start | bytes 589832 | tf_op jit(solution)/shard_map/ppermute | solution.py:43
  47.8 25.5 %collective-permute-start.4 = (f32[3,128,128]{2,1,0:T(8,128)S(1)}, f32[3,128,128]{2,1,0:T(8,128)S(1)}, u32[]{:S(2)}, u32[]{:S(2)}) collective-permute-start(f32[3,128,128]{2,1,0:T(8,128)S(1)} %get-tuple-element.52), channel_id=1, source_target_pairs={{0,8},{4,12},{8,0},{12,4},{1,9},{5,13},{9,1},{13,5},{2,10},{6,14},... | collective-permute-start | bytes 589832 | tf_op jit(solution)/shard_map/ppermute | solution.py:43
  49.1 24.2 %collective-permute-start.5 = (f32[3,128,128]{2,1,0:T(8,128)S(1)}, f32[3,128,128]{2,1,0:T(8,128)S(1)}, u32[]{:S(2)}, u32[]{:S(2)}) collective-permute-start(f32[3,128,128]{2,1,0:T(8,128)S(1)} %get-tuple-element.53), channel_id=1, source_target_pairs={{0,12},{4,8},{8,4},{12,0},{1,13},{5,9},{9,5},{13,1},{2,14},{6,10},... | collective-permute-start | bytes 589832 | tf_op jit(solution)/shard_map/ppermute | solution.py:43
  57.3 18.2 %collective-permute-start.9 = (f32[3,128,128]{2,1,0:T(8,128)S(1)}, f32[3,128,128]{2,1,0:T(8,128)S(1)}, u32[]{:S(2)}, u32[]{:S(2)}) collective-permute-start(f32[3,128,128]{2,1,0:T(8,128)S(1)} %get-tuple-element.68), channel_id=1, source_target_pairs={{0,4},{4,0},{8,12},{12,8},{1,5},{5,1},{9,13},{13,9},{2,6},{6,2},{1... | collective-permute-start | bytes 589832 | tf_op jit(solution)/shard_map/ppermute | solution.py:43
  58.2 21.1 %collective-permute-start.10 = (f32[3,128,128]{2,1,0:T(8,128)S(1)}, f32[3,128,128]{2,1,0:T(8,128)S(1)}, u32[]{:S(2)}, u32[]{:S(2)}) collective-permute-start(f32[3,128,128]{2,1,0:T(8,128)S(1)} %get-tuple-element.69), channel_id=1, source_target_pairs={{0,8},{4,12},{8,0},{12,4},{1,9},{5,13},{9,1},{13,5},{2,10},{6,14},... | collective-permute-start | bytes 589832 | tf_op jit(solution)/shard_map/ppermute | solution.py:43
  60.4 18.9 %collective-permute-start.11 = (f32[3,128,128]{2,1,0:T(8,128)S(1)}, f32[3,128,128]{2,1,0:T(8,128)S(1)}, u32[]{:S(2)}, u32[]{:S(2)}) collective-permute-start(f32[3,128,128]{2,1,0:T(8,128)S(1)} %get-tuple-element.70), channel_id=1, source_target_pairs={{0,12},{4,8},{8,4},{12,0},{1,13},{5,9},{9,5},{13,1},{2,14},{6,10},... | collective-permute-start | bytes 589832 | tf_op jit(solution)/shard_map/ppermute | solution.py:43
  73.9 11.9 %collective-permute-start.8 = (f32[48,16,128]{2,1,0:T(8,128)S(1)}, f32[48,16,128]{2,1,0:T(8,128)S(1)}, u32[]{:S(2)}, u32[]{:S(2)}) collective-permute-start(f32[48,16,128]{2,1,0:T(8,128)S(1)} %get-tuple-element.66), channel_id=1, source_target_pairs={{0,2},{2,0},{1,3},{3,1},{4,6},{6,4},{5,7},{7,5},{8,10},{10,8},{9,1... | collective-permute-start | bytes 1179656 | tf_op jit(solution)/shard_map/ppermute | solution.py:43
  80.0 10.1 %collective-permute-start.12 = (f32[48,16,128]{2,1,0:T(8,128)S(1)}, f32[48,16,128]{2,1,0:T(8,128)S(1)}, u32[]{:S(2)}, u32[]{:S(2)}) collective-permute-start(f32[48,16,128]{2,1,0:T(8,128)S(1)} %get-tuple-element.77), channel_id=1, source_target_pairs={{0,2},{2,0},{1,3},{3,1},{4,6},{6,4},{5,7},{7,5},{8,10},{10,8},{9,1... | collective-permute-start | bytes 1179656 | tf_op jit(solution)/shard_map/ppermute | solution.py:43
  81.6 8.4 %collective-permute-start.13 = (f32[48,32,128]{2,1,0:T(8,128)S(1)}, f32[48,32,128]{2,1,0:T(8,128)S(1)}, u32[]{:S(2)}, u32[]{:S(2)}) collective-permute-start(f32[48,32,128]{2,1,0:T(8,128)S(1)} %pad_maximum_fusion), channel_id=1, source_target_pairs={{0,1},{1,0},{2,3},{3,2},{4,5},{5,4},{6,7},{7,6},{8,9},{9,8},{10,11... | collective-permute-start | bytes 2359304 | tf_op jit(solution)/shard_map/ppermute | solution.py:43
  85.8 4.2 %collective-permute-start.14 = (f32[48,16,128]{2,1,0:T(8,128)S(1)}, f32[48,16,128]{2,1,0:T(8,128)S(1)}, u32[]{:S(2)}, u32[]{:S(2)}) collective-permute-start(f32[48,16,128]{2,1,0:T(8,128)S(1)} %collective-permute-done.8.refs_2_), channel_id=1, source_target_pairs={{0,1},{1,0},{2,3},{3,2},{4,5},{5,4},{6,7},{7,6},{8,9},{9,8},{10,11... | collective-permute-start | bytes 1179656 | tf_op jit(solution)/shard_map/ppermute | solution.py:43
  90.0 1.7 %collective-permute-start.15 = (f32[48,16,128]{2,1,0:T(8,128)S(1)}, f32[48,16,128]{2,1,0:T(8,128)S(1)}, u32[]{:S(2)}, u32[]{:S(2)}) collective-permute-start(f32[48,16,128]{2,1,0:T(8,128)S(1)} %collective-permute-done.12.refs_3_), channel_id=1, source_target_pairs={{0,1},{1,0},{2,3},{3,2},{4,5},{5,4},{6,7},{7,6},{8,9},{9,8},{10,11... | collective-permute-start | bytes 1179656 | tf_op jit(solution)/shard_map/ppermute | solution.py:43
  96.2 11.6 %collective-permute-start.16 = (f32[96,128]{1,0:T(8,128)S(1)}, f32[96,128]{1,0:T(8,128)S(1)}, u32[]{:S(2)}, u32[]{:S(2)}) collective-permute-start(f32[96,128]{1,0:T(8,128)S(1)} %get-tuple-element.87), channel_id=1, source_target_pairs={{0,12},{2,14},{4,0},{6,2},{8,4},{10,6},{12,8},{14,10},{1,13},{3,15... | collective-permute-start | bytes 147464 | tf_op jit(solution)/shard_map/ppermute | solution.py:533
  98.9 9.0 %collective-permute-start.17 = (f32[96,128]{1,0:T(8,128)S(1)}, f32[96,128]{1,0:T(8,128)S(1)}, u32[]{:S(2)}, u32[]{:S(2)}) collective-permute-start(f32[96,128]{1,0:T(8,128)S(1)} %get-tuple-element.88), channel_id=1, source_target_pairs={{0,14},{2,12},{4,2},{6,0},{8,6},{10,4},{12,10},{14,8},{1,15},{3,13... | collective-permute-start | bytes 147464 | tf_op jit(solution)/shard_map/ppermute | solution.py:533
  103.4 5.9 %collective-permute-start.18 = (f32[96,128]{1,0:T(8,128)S(1)}, f32[96,128]{1,0:T(8,128)S(1)}, u32[]{:S(2)}, u32[]{:S(2)}) collective-permute-start(f32[96,128]{1,0:T(8,128)S(1)} %get-tuple-element.89), channel_id=1, source_target_pairs={{0,4},{2,6},{4,8},{6,10},{8,12},{10,14},{12,0},{14,2},{1,5},{3,7},... | collective-permute-start | bytes 147464 | tf_op jit(solution)/shard_map/ppermute | solution.py:533
  103.4 6.8 %collective-permute-start.19 = (f32[96,128]{1,0:T(8,128)S(1)}, f32[96,128]{1,0:T(8,128)S(1)}, u32[]{:S(2)}, u32[]{:S(2)}) collective-permute-start(f32[96,128]{1,0:T(8,128)S(1)} %get-tuple-element.90), channel_id=1, source_target_pairs={{0,6},{2,4},{4,10},{6,8},{8,14},{10,12},{12,2},{14,0},{1,7},{3,5},... | collective-permute-start | bytes 147464 | tf_op jit(solution)/shard_map/ppermute | solution.py:533
  103.4 6.8 %collective-permute-start.20 = (f32[96,128]{1,0:T(8,128)S(1)}, f32[96,128]{1,0:T(8,128)S(1)}, u32[]{:S(2)}, u32[]{:S(2)}) collective-permute-start(f32[96,128]{1,0:T(8,128)S(1)} %get-tuple-element.91), channel_id=1, source_target_pairs={{0,2},{2,0},{4,6},{6,4},{8,10},{10,8},{12,14},{14,12},{1,3},{3,1},... | collective-permute-start | bytes 147464 | tf_op jit(solution)/shard_map/ppermute | solution.py:533
  111.4 3.8 %collective-permute-start.22 = (f32[32,128]{1,0:T(8,128)S(1)}, f32[32,128]{1,0:T(8,128)S(1)}, u32[]{:S(2)}, u32[]{:S(2)}) collective-permute-start(f32[32,128]{1,0:T(8,128)S(1)} %get-tuple-element.94), channel_id=1, source_target_pairs={{0,2},{1,3},{2,0},{3,1},{4,6},{5,7},{6,4},{7,5},{8,10},{9,11},{10,... | collective-permute-start | bytes 49160 | tf_op jit(solution)/shard_map/ppermute | solution.py:43
  112.5 3.2 %collective-permute-start.23 = (f32[32,128]{1,0:T(8,128)S(1)}, f32[32,128]{1,0:T(8,128)S(1)}, u32[]{:S(2)}, u32[]{:S(2)}) collective-permute-start(f32[32,128]{1,0:T(8,128)S(1)} %get-tuple-element.95), channel_id=1, source_target_pairs={{0,3},{1,2},{2,1},{3,0},{4,7},{5,6},{6,5},{7,4},{8,11},{9,10},{10,... | collective-permute-start | bytes 49160 | tf_op jit(solution)/shard_map/ppermute | solution.py:43
  112.5 3.2 %collective-permute-start.21 = (f32[32,128]{1,0:T(8,128)S(1)}, f32[32,128]{1,0:T(8,128)S(1)}, u32[]{:S(2)}, u32[]{:S(2)}) collective-permute-start(f32[32,128]{1,0:T(8,128)S(1)} %get-tuple-element.93), channel_id=1, source_target_pairs={{0,1},{1,0},{2,3},{3,2},{4,5},{5,4},{6,7},{7,6},{8,9},{9,8},{10,11... | collective-permute-start | bytes 49160 | tf_op jit(solution)/shard_map/ppermute | solution.py:43
  115.7 4.9 %collective-permute-start.25 = (f32[32,128]{1,0:T(8,128)S(1)}, f32[32,128]{1,0:T(8,128)S(1)}, u32[]{:S(2)}, u32[]{:S(2)}) collective-permute-start(f32[32,128]{1,0:T(8,128)S(1)} %add_add_fusion.1), channel_id=1, source_target_pairs={{0,8},{4,12},{8,0},{12,4},{1,9},{5,13},{9,1},{13,5},{2,10},{6,14},... | collective-permute-start | bytes 49160 | tf_op jit(solution)/shard_map/ppermute | solution.py:43
  118.2 5.5 %collective-permute-start.26 = (f32[32,128]{1,0:T(8,128)S(1)}, f32[32,128]{1,0:T(8,128)S(1)}, u32[]{:S(2)}, u32[]{:S(2)}) collective-permute-start(f32[32,128]{1,0:T(8,128)S(1)} %add_add_fusion.1), channel_id=1, source_target_pairs={{0,12},{4,8},{8,4},{12,0},{1,13},{5,9},{9,5},{13,1},{2,14},{6,10},... | collective-permute-start | bytes 49160 | tf_op jit(solution)/shard_map/ppermute | solution.py:43
  118.2 5.5 %collective-permute-start.24 = (f32[32,128]{1,0:T(8,128)S(1)}, f32[32,128]{1,0:T(8,128)S(1)}, u32[]{:S(2)}, u32[]{:S(2)}) collective-permute-start(f32[32,128]{1,0:T(8,128)S(1)} %add_add_fusion.1), channel_id=1, source_target_pairs={{0,4},{4,0},{8,12},{12,8},{1,5},{5,1},{9,13},{13,9},{2,6},{6,2},{1... | collective-permute-start | bytes 49160 | tf_op jit(solution)/shard_map/ppermute | solution.py:43

commit v9 on v8

--- a/solution.py
+++ b/solution.py
@@ -43,8 +43,8 @@
     return lax.ppermute(x, axes, [(i, i ^ by) for i in range(size)])
 
 
-def filter_kernel(n_dom, planes, rows, starts, first, place, *refs):
-    refs = list(refs)
+def filter_kernel(n_dom, planes, rows, starts, first, n_levels, place, *refs):
+    levels, refs = refs[:n_levels], list(refs[n_levels:])
     given = None if first else refs.pop(0)
     ins, outs = refs[:n_dom], refs[n_dom : 2 * n_dom]
     refs = refs[2 * n_dom :]
@@ -65,7 +65,10 @@
             for y in range(rows):
                 even[x, y, part] = ins[m][pl.ds(base + y, TOGETHER, stride=cells), :]
                 if first:
-                    level = ins[m][pl.ds(base + (TOGETHER * cells + y), 1), :]
+                    if m >= 3:
+                        level = levels[m - 3][pl.ds(plane_at[i] * rows + y, 1), :]
+                    else:
+                        level = ins[m][pl.ds(base + (TOGETHER * cells + y), 1), :]
                     diagonal[x, y, part] = jnp.broadcast_to(
                         (level + (SHIFT - CENTER_LEVEL)) * (2.0 * scale), (TOGETHER, lanes)
                     )
@@ -117,7 +120,7 @@
                 outs[m][plane_at[i], here, :] = even[x, y, part]
 
 
-def filter_orbitals(place, diagonal, blocks, starts, planes, rows):
+def filter_orbitals(place, diagonal, levels, blocks, starts, planes, rows):
     n_dom = len(blocks)
     first = diagonal is None
     lanes = blocks[0].shape[1]
@@ -127,9 +130,9 @@
     given = [] if first else [diagonal]
     size = n_dom * planes * rows * TOGETHER * lanes
     return pl.pallas_call(
-        functools.partial(filter_kernel, n_dom, planes, rows, starts, first),
+        functools.partial(filter_kernel, n_dom, planes, rows, starts, first, len(levels)),
         out_shape=[out] * n_dom + extra,
-        in_specs=[SMEM] + [VMEM] * (n_dom + len(given)),
+        in_specs=[SMEM] + [VMEM] * (len(levels) + n_dom + len(given)),
         out_specs=[VMEM] * (n_dom + len(extra)),
         scratch_shapes=[pltpu.VMEM(field, jnp.float32)] * 2,
         compiler_params=params(8),
@@ -137,7 +140,7 @@
             flops=12 * DEGREE * size, bytes_accessed=8 * size, transcendentals=0
         ),
         name="chebyshev",
-    )(place, *given, *blocks)
+    )(place, *levels, *given, *blocks)
 
 
 def cell_first_kernel(n_band, place, *refs):
@@ -402,10 +405,12 @@
     own = []
     for m in range(n_dom):
         blocks = [block(c, m) for c in range(n_chunks)]
-        blocks[0] = jnp.concatenate([blocks[0], levels], axis=0)
+        if m < 3:
+            blocks[0] = jnp.concatenate([blocks[0], levels], axis=0)
         own.append(blocks)
     near = sent(jnp.concatenate(own[1], axis=0), 1)
     arrived = [[own[0][0], near] + [sent(own[m][0], m) for m in range(2, n_dom)]]
+    handed_on = [sent(arrived[0][2][size:], 1)] if n_dom > 3 else []
     for c in range(1, n_chunks):
         far = [own[m][c] for m in range(2, n_dom)]
         near, far = lax.optimization_barrier((near, far))
@@ -415,7 +420,9 @@
     for c, blocks in enumerate(arrived):
         starts = [0] * n_dom
         starts[1] = c * size + (cells if c else 0)
-        filtered = filter_orbitals(place, diagonal, blocks, starts, planes, rows)
+        filtered = filter_orbitals(
+            place, diagonal, [] if c else handed_on, blocks, starts, planes, rows
+        )
         if diagonal is None:
             diagonal = filtered[n_dom]
         done.append(filtered[:n_dom])

time: 125 us -> 125 us (level)
  waiting for transfers between devices: 33.7 us -> 40.2 us
  starting transfers between devices: 48.1 us -> 42.4 us
    ppermute x22 -> x23, waiting for transfers between devices: 31.4 us -> 38.6 us  [swapped(): return lax.ppermute(x, axes, [(i, i ^ by) for i in range(size)])]
    ppermute x22 -> x23, starting transfers between devices: 40.2 us -> 35.5 us  [swapped(): return lax.ppermute(x, axes, [(i, i ^ by) for i in range(size)])]
  transfers between devices with their start and end apart: 27 -> 28, of which waited for: 12 -> 12; matrix products, arithmetic and copies ran while one was open for 1% -> 1% of each run, Pallas kernels for 26% -> 26%
where the time goes in v9:
time: 125 us
  starting transfers between devices  42.4 us (34%)
  waiting for transfers between devices  40.2 us (32%)
  Pallas kernels  38 us (30%)
  local copies, waits for them, and re-layouts  2.08 us (2%)
    ppermute x23, waiting for transfers between devices, swapped(): return lax.ppermute(x, axes, [(i, i ^ by) for i in range(size)])  38.6 us
    ppermute x23, starting transfers between devices, swapped(): return lax.ppermute(x, axes, [(i, i ^ by) for i in range(size)])  35.5 us
    pallas_call x2, Pallas kernels, filter_orbitals(): pl.pallas_call(functools.partial(filter_kernel, n_dom, planes, rows, star...  14 us
    pallas_call x1, Pallas kernels, build_projectors(): pl.pallas_call(functools.partial(projector_kernel, n_band, n_sub), out_sh...  11.5 us
    pallas_call x2, Pallas kernels, products(): pl.pallas_call(functools.partial(product_kernel, spots, n_sub, first_row,...  8.16 us
    ppermute x5, starting transfers between devices, on_device(): sums.append(lax.ppermute(x, ('dom', 'band'), pairs))  6.91 us
  transfers between devices with their start and end apart: 28, of which 12 were waited for; matrix products, arithmetic and copies ran while one was open for 1% of the time, Pallas kernels for 26%

profile of v9, /device:TPU:0, one launch (start us, length us, event | category | flops | bytes accessed | tf_op | source)
XLA Modules:
  0.0 124.6 jit_solution(2448425090973091620)
XLA Ops:
  0.6 0.0 copy-start
  0.7 1.6 %constant_dynamic-slice_fusion = (f32[384,128]{1,0:T(8,128)S(1)}, f32[384,128]{1,0:T(8,128)S(1)}, f32[384,128]{1,0:T(8,128)S(1)}, f32[384,128]{1,0:T(8,128)S(1)}...) fusion(f32[3072,128]{1,0:T(8,128)} %bitcast.33, ...), kind=kLoop, calls=%fused_computation.9 | loop fusion | bytes 3145760 | tf_op jit(solution)/shard_map/dynamic_slice | solution.py:400
  2.3 4.1 %collective-permute-start = (f32[480,128]{1,0:T(8,128)S(1)}, f32[480,128]{1,0:T(8,128)S(1)}, u32[]{:S(2)}, u32[]{:S(2)}) collective-permute-start(f32[480,128]{1,0:T(8,128)S(1)} %get-tuple-element.105), channel_id=1, source_target_pairs={{0,8},{4,12},{8,0},{12,4},{1,9},{5,13},{9,1},{13,5},{2,10},{6,14},... | collective-permute-start | bytes 737288 | tf_op jit(solution)/shard_map/ppermute | solution.py:43
  6.5 1.6 %collective-permute-start.2 = (f32[864,128]{1,0:T(8,128)S(1)}, f32[864,128]{1,0:T(8,128)S(1)}, u32[]{:S(2)}, u32[]{:S(2)}) collective-permute-start(f32[864,128]{1,0:T(8,128)S(1)} %pad_maximum_fusion.1), channel_id=1, source_target_pairs={{0,4},{4,0},{8,12},{12,8},{1,5},{5,1},{9,13},{13,9},{2,6},{6,2},{1... | collective-permute-start | bytes 1327112 | tf_op jit(solution)/shard_map/ppermute | solution.py:43
  8.1 0.1 constant_dynamic-slice_fusion.8
  8.2 0.1 copy.8
  8.3 0.1 broadcast_multiply_fusion
  8.5 10.1 %collective-permute-done.refs_3_ = f32[480,128]{1,0:T(8,128)S(1)} collective-permute-done((f32[480,128]{1,0:T(8,128)S(1)}, f32[480,128]{1,0:T(8,128)S(1)}, u32[]{:S(2)}, u32[]{:S(2)}) %collective-permute-start) | collective-permute-done | bytes 245792 | tf_op jit(solution)/shard_map/ppermute | solution.py:43
  18.5 0.0 collective-permute-start.1
  18.5 0.1 pad_add_fusion.place
  18.6 0.3 mul.56.corr_ref
  18.9 0.0 copy-start.2
  18.9 4.8 %collective-permute-done.2.refs_2_ = f32[864,128]{1,0:T(8,128)S(1)} collective-permute-done((f32[864,128]{1,0:T(8,128)S(1)}, f32[864,128]{1,0:T(8,128)S(1)}, u32[]{:S(2)}, u32[]{:S(2)}) %collective-permute-start.2) | collective-permute-done | bytes 442400 | tf_op jit(solution)/shard_map/ppermute | solution.py:43
  23.7 0.9 collective-permute-start.7
  24.6 2.5 %collective-permute-start.8 = (f32[384,128]{1,0:T(8,128)S(1)}, f32[384,128]{1,0:T(8,128)S(1)}, u32[]{:S(2)}, u32[]{:S(2)}) collective-permute-start(f32[384,128]{1,0:T(8,128)S(1)} %get-tuple-element.57), channel_id=1, source_target_pairs={{0,12},{4,8},{8,4},{12,0},{1,13},{5,9},{9,5},{13,1},{2,14},{6,10},... | collective-permute-start | bytes 589832 | tf_op jit(solution)/shard_map/ppermute | solution.py:43
  27.2 1.2 collective-permute-done.3.refs_4_
  28.4 0.0 collective-permute-done.1.refs_0_
  28.4 7.2 %chebyshev.2 = (f32[3,128,128]{2,1,0:T(8,128)S(1)}, f32[3,128,128]{2,1,0:T(8,128)S(1)}, f32[3,128,128]{2,1,0:T(8,128)S(1)}, f32[3,128,128]{2,1,0:T(8,128)S(1)}, f32[6,32,8,128]{3,2,1,0:T(8,128)S(1)}) custom-call(s32[4]{0:T(128)S(1)} %pad_add_fusion.place, f32[96,128]{1,0:T(8,128)S(1)} %collective-permute-done.1.refs_0_, ...), custom_call_target="tpu_custom_call" | custom-call | flops 28311552 | bytes 1572864 | tf_op jit(solution)/shard_map/chebyshev/pallas_call | solution.py:132
  35.5 1.8 %collective-permute-start.4 = (f32[3,128,128]{2,1,0:T(8,128)S(1)}, f32[3,128,128]{2,1,0:T(8,128)S(1)}, u32[]{:S(2)}, u32[]{:S(2)}) collective-permute-start(f32[3,128,128]{2,1,0:T(8,128)S(1)} %get-tuple-element.51), channel_id=1, source_target_pairs={{0,4},{4,0},{8,12},{12,8},{1,5},{5,1},{9,13},{13,9},{2,6},{6,2},{1... | collective-permute-start | bytes 589832 | tf_op jit(solution)/shard_map/ppermute | solution.py:43
  37.4 1.3 %collective-permute-start.5 = (f32[3,128,128]{2,1,0:T(8,128)S(1)}, f32[3,128,128]{2,1,0:T(8,128)S(1)}, u32[]{:S(2)}, u32[]{:S(2)}) collective-permute-start(f32[3,128,128]{2,1,0:T(8,128)S(1)} %get-tuple-element.52), channel_id=1, source_target_pairs={{0,8},{4,12},{8,0},{12,4},{1,9},{5,13},{9,1},{13,5},{2,10},{6,14},... | collective-permute-start | bytes 589832 | tf_op jit(solution)/shard_map/ppermute | solution.py:43
  38.7 1.3 %collective-permute-start.6 = (f32[3,128,128]{2,1,0:T(8,128)S(1)}, f32[3,128,128]{2,1,0:T(8,128)S(1)}, u32[]{:S(2)}, u32[]{:S(2)}) collective-permute-start(f32[3,128,128]{2,1,0:T(8,128)S(1)} %get-tuple-element.53), channel_id=1, source_target_pairs={{0,12},{4,8},{8,4},{12,0},{1,13},{5,9},{9,5},{13,1},{2,14},{6,10},... | collective-permute-start | bytes 589832 | tf_op jit(solution)/shard_map/ppermute | solution.py:43
  40.0 3.3 %collective-permute-done.7.refs_3_ = f32[384,128]{1,0:T(8,128)S(1)} collective-permute-done((f32[384,128]{1,0:T(8,128)S(1)}, f32[384,128]{1,0:T(8,128)S(1)}, u32[]{:S(2)}, u32[]{:S(2)}) %collective-permute-start.7) | collective-permute-done | bytes 196640 | tf_op jit(solution)/shard_map/ppermute | solution.py:43
  43.3 0.0 collective-permute-done.8.refs_4_
  43.3 6.8 %chebyshev.3 = (f32[3,128,128]{2,1,0:T(8,128)S(1)}, f32[3,128,128]{2,1,0:T(8,128)S(1)}, f32[3,128,128]{2,1,0:T(8,128)S(1)}, f32[3,128,128]{2,1,0:T(8,128)S(1)}) custom-call(s32[4]{0:T(128)S(1)} %pad_add_fusion.place, f32[6,32,8,128]{3,2,1,0:T(8,128)S(1)} %get-tuple-element.54.refs_0_, f32[384,128]{1,0:T(8,128)S(1)} %get-tuple-element.98.refs_1_, ...), custom_call_target="tpu_custom_call" | custom-call | flops 28311552 | bytes 1572864 | tf_op jit(solution)/shard_map/chebyshev/pallas_call | solution.py:132
  50.2 10.5 %collective-permute-start.10 = (f32[3,128,128]{2,1,0:T(8,128)S(1)}, f32[3,128,128]{2,1,0:T(8,128)S(1)}, u32[]{:S(2)}, u32[]{:S(2)}) collective-permute-start(f32[3,128,128]{2,1,0:T(8,128)S(1)} %get-tuple-element.68), channel_id=1, source_target_pairs={{0,4},{4,0},{8,12},{12,8},{1,5},{5,1},{9,13},{13,9},{2,6},{6,2},{1... | collective-permute-start | bytes 589832 | tf_op jit(solution)/shard_map/ppermute | solution.py:43
  60.7 1.1 collective-permute-start.11
  61.7 0.0 collective-permute-done.4
  61.7 1.4 %collective-permute-start.12 = (f32[3,128,128]{2,1,0:T(8,128)S(1)}, f32[3,128,128]{2,1,0:T(8,128)S(1)}, u32[]{:S(2)}, u32[]{:S(2)}) collective-permute-start(f32[3,128,128]{2,1,0:T(8,128)S(1)} %get-tuple-element.70), channel_id=1, source_target_pairs={{0,12},{4,8},{8,4},{12,0},{1,13},{5,9},{9,5},{13,1},{2,14},{6,10},... | collective-permute-start | bytes 589832 | tf_op jit(solution)/shard_map/ppermute | solution.py:43
  63.1 11.5 %projectors.1 = (bf16[576,6144]{1,0:T(8,128)(2,1)S(1)}, bf16[576,6144]{1,0:T(8,128)(2,1)S(1)}) custom-call(s32[4]{0:T(128)S(1)} %pad_add_fusion.place, s32[3,48,128]{2,1,0:T(8,128)S(1)} %bitcast.32, f32[48,3,8,128]{3,2,1,0:T(8,128)S(1)} %copy-done.1), custom_call_target="tpu_custom_call" | custom-call | flops 1811939328 | bytes 28311552 | tf_op jit(solution)/shard_map/projectors/pallas_call | solution.py:258
  74.6 0.0 collective-permute-done.5
  74.6 0.0 collective-permute-done.6
  74.6 0.7 cell_first.2
  75.3 1.6 %collective-permute-start.9 = (f32[48,16,128]{2,1,0:T(8,128)S(1)}, f32[48,16,128]{2,1,0:T(8,128)S(1)}, u32[]{:S(2)}, u32[]{:S(2)}) collective-permute-start(f32[48,16,128]{2,1,0:T(8,128)S(1)} %get-tuple-element.66), channel_id=1, source_target_pairs={{0,2},{2,0},{1,3},{3,1},{4,6},{6,4},{5,7},{7,5},{8,10},{10,8},{9,1... | collective-permute-start | bytes 1179656 | tf_op jit(solution)/shard_map/ppermute | solution.py:43
  76.8 0.0 collective-permute-done.10
  76.8 0.7 collective-permute-done.11
  77.6 0.7 cell_first.3
  78.2 1.5 %collective-permute-start.13 = (f32[48,16,128]{2,1,0:T(8,128)S(1)}, f32[48,16,128]{2,1,0:T(8,128)S(1)}, u32[]{:S(2)}, u32[]{:S(2)}) collective-permute-start(f32[48,16,128]{2,1,0:T(8,128)S(1)} %get-tuple-element.77), channel_id=1, source_target_pairs={{0,2},{2,0},{1,3},{3,1},{4,6},{6,4},{5,7},{7,5},{8,10},{10,8},{9,1... | collective-permute-start | bytes 1179656 | tf_op jit(solution)/shard_map/ppermute | solution.py:43
  79.7 0.1 pad_maximum_fusion
  79.8 0.1 collective-permute-start.14
  79.9 1.8 %orbital_first.1 = f32[32,96,128]{2,1,0:T(8,128)} custom-call(s32[4]{0:T(128)S(1)} %pad_add_fusion.place, f32[384,128]{1,0:T(8,128)S(1)} %bitcast.17, f32[384,128]{1,0:T(8,128)S(1)} %bitcast.19, f32[384,128]{1,0:T(8,128)S(1)} %bitcast.21, f32[384,128]{1,0:T(8,128)S(1)} %bitcast.23, f32[384,128]{1,0:T(8,128)S(1)} %bitcast.25, f32[384,128]{1,0:T(8,128)S(1)} %bitcast.27, ...), custom_call_target="tpu_custom_call" | custom-call | tf_op jit(solution)/shard_map/orbital_first/pallas_call | solution.py:197
  81.7 5.7 %collective-permute-done.9.refs_2_ = f32[48,16,128]{2,1,0:T(8,128)S(1)} collective-permute-done((f32[48,16,128]{2,1,0:T(8,128)S(1)}, f32[48,16,128]{2,1,0:T(8,128)S(1)}, u32[]{:S(2)}, u32[]{:S(2)}) %collective-permute-start.9) | collective-permute-done | bytes 393248 | tf_op jit(solution)/shard_map/ppermute | solution.py:43
  87.4 5.8 %collective-permute-done.13.refs_3_ = f32[48,16,128]{2,1,0:T(8,128)S(1)} collective-permute-done((f32[48,16,128]{2,1,0:T(8,128)S(1)}, f32[48,16,128]{2,1,0:T(8,128)S(1)}, u32[]{:S(2)}, u32[]{:S(2)}) %collective-permute-start.13) | collective-permute-done | bytes 393248 | tf_op jit(solution)/shard_map/ppermute | solution.py:43
  93.2 0.0 collective-permute-start.16
  93.2 0.0 collective-permute-done.15.refs_5_
  93.2 0.0 collective-permute-done.14.refs_4_
  93.2 1.7 %collective-permute-done.16.refs_6_ = f32[48,16,128]{2,1,0:T(8,128)S(1)} collective-permute-done((f32[48,16,128]{2,1,0:T(8,128)S(1)}, f32[48,16,128]{2,1,0:T(8,128)S(1)}, u32[]{:S(2)}, u32[]{:S(2)}) %collective-permute-start.16) | collective-permute-done | bytes 393248 | tf_op jit(solution)/shard_map/ppermute | solution.py:43
  94.9 4.5 %products.2 = (f32[96,128]{1,0:T(8,128)S(1)}, f32[96,128]{1,0:T(8,128)S(1)}, f32[96,128]{1,0:T(8,128)S(1)}, f32[96,128]{1,0:T(8,128)S(1)}, f32[96,128]{1,0:T(8,128)S(1)}) custom-call(s32[4]{0:T(128)S(1)} %pad_add_fusion.place, bf16[576,6144]{1,0:T(8,128)(2,1)S(1)} %get-tuple-element.72.w_high, bf16[576,6144]{1,0:T(8,128)(2,1)S(1)} %get-tuple-element.73.w_low, ...), custom_call_target="tpu_custom_call" | custom-call | flops 4529848320 | bytes 11796480 | tf_op jit(solution)/shard_map/products/pallas_call | solution.py:325
  99.4 2.5 %collective-permute-start.17 = (f32[96,128]{1,0:T(8,128)S(1)}, f32[96,128]{1,0:T(8,128)S(1)}, u32[]{:S(2)}, u32[]{:S(2)}) collective-permute-start(f32[96,128]{1,0:T(8,128)S(1)} %get-tuple-element.87), channel_id=1, source_target_pairs={{0,12},{2,14},{4,0},{6,2},{8,4},{10,6},{12,8},{14,10},{1,13},{3,15... | collective-permute-start | bytes 147464 | tf_op jit(solution)/shard_map/ppermute | solution.py:540
  101.9 1.7 %collective-permute-start.18 = (f32[96,128]{1,0:T(8,128)S(1)}, f32[96,128]{1,0:T(8,128)S(1)}, u32[]{:S(2)}, u32[]{:S(2)}) collective-permute-start(f32[96,128]{1,0:T(8,128)S(1)} %get-tuple-element.88), channel_id=1, source_target_pairs={{0,14},{2,12},{4,2},{6,0},{8,6},{10,4},{12,10},{14,8},{1,15},{3,13... | collective-permute-start | bytes 147464 | tf_op jit(solution)/shard_map/ppermute | solution.py:540
  103.5 1.3 %collective-permute-start.19 = (f32[96,128]{1,0:T(8,128)S(1)}, f32[96,128]{1,0:T(8,128)S(1)}, u32[]{:S(2)}, u32[]{:S(2)}) collective-permute-start(f32[96,128]{1,0:T(8,128)S(1)} %get-tuple-element.89), channel_id=1, source_target_pairs={{0,4},{2,6},{4,8},{6,10},{8,12},{10,14},{12,0},{14,2},{1,5},{3,7},... | collective-permute-start | bytes 147464 | tf_op jit(solution)/shard_map/ppermute | solution.py:540
  104.8 0.0 collective-permute-start.20
  104.8 1.5 %collective-permute-start.21 = (f32[96,128]{1,0:T(8,128)S(1)}, f32[96,128]{1,0:T(8,128)S(1)}, u32[]{:S(2)}, u32[]{:S(2)}) collective-permute-start(f32[96,128]{1,0:T(8,128)S(1)} %get-tuple-element.91), channel_id=1, source_target_pairs={{0,2},{2,0},{4,6},{6,4},{8,10},{10,8},{12,14},{14,12},{1,3},{3,1},... | collective-permute-start | bytes 147464 | tf_op jit(solution)/shard_map/ppermute | solution.py:540
  106.3 3.7 %products.3 = (f32[128,128]{1,0:T(8,128)S(1)}, f32[96,128]{1,0:T(8,128)S(1)}) custom-call(s32[4]{0:T(128)S(1)} %pad_add_fusion.place, bf16[576,6144]{1,0:T(8,128)(2,1)S(1)} %get-tuple-element.72.w_high, bf16[576,6144]{1,0:T(8,128)(2,1)S(1)} %get-tuple-element.73.w_low, f32[48,16,128]{2,1,0:T(8,128)S(1)} %get-tuple-element.74.refs_0_, ...), custom_call_target="tpu_custom_call" | custom-call | flops 905969664 | bytes 2359296 | tf_op jit(solution)/shard_map/products/pallas_call | solution.py:325
  110.0 1.6 %collective-permute-done.20.refs_3_ = f32[96,128]{1,0:T(8,128)S(1)} collective-permute-done((f32[96,128]{1,0:T(8,128)S(1)}, f32[96,128]{1,0:T(8,128)S(1)}, u32[]{:S(2)}, u32[]{:S(2)}) %collective-permute-start.20) | collective-permute-done | bytes 49184 | tf_op jit(solution)/shard_map/ppermute | solution.py:540
  111.6 1.2 gram_share.1
  112.8 0.6 collective-permute-start.23
  113.4 1.6 %collective-permute-start.22 = (f32[32,128]{1,0:T(8,128)S(1)}, f32[32,128]{1,0:T(8,128)S(1)}, u32[]{:S(2)}, u32[]{:S(2)}) collective-permute-start(f32[32,128]{1,0:T(8,128)S(1)} %get-tuple-element.93), channel_id=1, source_target_pairs={{0,1},{1,0},{2,3},{3,2},{4,5},{5,4},{6,7},{7,6},{8,9},{9,8},{10,11... | collective-permute-start | bytes 49160 | tf_op jit(solution)/shard_map/ppermute | solution.py:43
  115.0 1.7 %collective-permute-done.23 = f32[32,128]{1,0:T(8,128)S(1)} collective-permute-done((f32[32,128]{1,0:T(8,128)S(1)}, f32[32,128]{1,0:T(8,128)S(1)}, u32[]{:S(2)}, u32[]{:S(2)}) %collective-permute-start.23) | collective-permute-done | bytes 16416 | tf_op jit(solution)/shard_map/ppermute | solution.py:43
  116.8 1.6 %collective-permute-start.26 = (f32[32,128]{1,0:T(8,128)S(1)}, f32[32,128]{1,0:T(8,128)S(1)}, u32[]{:S(2)}, u32[]{:S(2)}) collective-permute-start(f32[32,128]{1,0:T(8,128)S(1)} %add_add_fusion.1), channel_id=1, source_target_pairs={{0,8},{4,12},{8,0},{12,4},{1,9},{5,13},{9,1},{13,5},{2,10},{6,14},... | collective-permute-start | bytes 49160 | tf_op jit(solution)/shard_map/ppermute | solution.py:43
  118.4 0.8 collective-permute-start.27
  119.2 1.2 collective-permute-start.25
  120.3 1.1 collective-permute-done.26
  121.5 2.4 %collective-permute-done.27 = f32[32,128]{1,0:T(8,128)S(1)} collective-permute-done((f32[32,128]{1,0:T(8,128)S(1)}, f32[32,128]{1,0:T(8,128)S(1)}, u32[]{:S(2)}, u32[]{:S(2)}) %collective-permute-start.27) | collective-permute-done | bytes 16416 | tf_op jit(solution)/shard_map/ppermute | solution.py:43
  123.9 0.6 add_add_fusion
  (22 shorter events, 0.1 us)
Async XLA Ops:
  0.6 7.5 %copy-start = (f32[48,8,8]{0,2,1:T(8,128)S(1)}, f32[48,8,8]{0,2,1:T(8,128)}, u32[]{:S(2)}) copy-start(f32[48,8,8]{0,2,1:T(8,128)} %param.9) | copy-start | bytes 36868
  0.7 1.6 %copy-start.3 = (f32[3,32,128]{2,1,0:T(8,128)S(1)}, f32[3,32,128]{2,1,0:T(8,128)}, u32[]{:S(2)}) copy-start(f32[3,32,128]{2,1,0:T(8,128)} %param.6) | copy-start | bytes 147460
  2.3 16.2 %collective-permute-start = (f32[480,128]{1,0:T(8,128)S(1)}, f32[480,128]{1,0:T(8,128)S(1)}, u32[]{:S(2)}, u32[]{:S(2)}) collective-permute-start(f32[480,128]{1,0:T(8,128)S(1)} %get-tuple-element.105), channel_id=1, source_target_pairs={{0,8},{4,12},{8,0},{12,4},{1,9},{5,13},{9,1},{13,5},{2,10},{6,14},... | collective-permute-start | bytes 737288 | tf_op jit(solution)/shard_map/ppermute | solution.py:43
  6.5 17.2 %collective-permute-start.2 = (f32[864,128]{1,0:T(8,128)S(1)}, f32[864,128]{1,0:T(8,128)S(1)}, u32[]{:S(2)}, u32[]{:S(2)}) collective-permute-start(f32[864,128]{1,0:T(8,128)S(1)} %pad_maximum_fusion.1), channel_id=1, source_target_pairs={{0,4},{4,0},{8,12},{12,8},{1,5},{5,1},{9,13},{13,9},{2,6},{6,2},{1... | collective-permute-start | bytes 1327112 | tf_op jit(solution)/shard_map/ppermute | solution.py:43
  8.1 20.2 %collective-permute-start.3 = (f32[384,128]{1,0:T(8,128)S(1)}, f32[384,128]{1,0:T(8,128)S(1)}, u32[]{:S(2)}, u32[]{:S(2)}) collective-permute-start(f32[384,128]{1,0:T(8,128)S(1)} %get-tuple-element.99), channel_id=1, source_target_pairs={{0,12},{4,8},{8,4},{12,0},{1,13},{5,9},{9,5},{13,1},{2,14},{6,10},... | collective-permute-start | bytes 589832 | tf_op jit(solution)/shard_map/ppermute | solution.py:43
  18.5 9.8 %collective-permute-start.1 = (f32[96,128]{1,0:T(8,128)S(1)}, f32[96,128]{1,0:T(8,128)S(1)}, u32[]{:S(2)}, u32[]{:S(2)}) collective-permute-start(f32[96,128]{1,0:T(8,128)S(1)} %slice.4), channel_id=1, source_target_pairs={{0,4},{4,0},{8,12},{12,8},{1,5},{5,1},{9,13},{13,9},{2,6},{6,2},{1... | collective-permute-start | bytes 147464 | tf_op jit(solution)/shard_map/ppermute | solution.py:43
  18.9 44.2 %copy-start.1 = (f32[48,3,8,128]{3,2,1,0:T(8,128)S(1)}, f32[48,3,8,128]{3,2,1,0:T(8,128)}, u32[]{:S(2)}) copy-start(f32[48,3,8,128]{3,2,1,0:T(8,128)} %coefs_ref.1) | copy-start | bytes 1769476
  18.9 44.2 %copy-start.2 = (s32[48,3,128]{2,0,1:T(8,128)S(1)}, s32[48,3,128]{2,0,1:T(8,128)}, u32[]{:S(2)}) copy-start(s32[48,3,128]{2,0,1:T(8,128)} %param.7) | copy-start | bytes 221188
  23.7 19.6 %collective-permute-start.7 = (f32[384,128]{1,0:T(8,128)S(1)}, f32[384,128]{1,0:T(8,128)S(1)}, u32[]{:S(2)}, u32[]{:S(2)}) collective-permute-start(f32[384,128]{1,0:T(8,128)S(1)} %get-tuple-element.56), channel_id=1, source_target_pairs={{0,8},{4,12},{8,0},{12,4},{1,9},{5,13},{9,1},{13,5},{2,10},{6,14},... | collective-permute-start | bytes 589832 | tf_op jit(solution)/shard_map/ppermute | solution.py:43
  24.6 18.7 %collective-permute-start.8 = (f32[384,128]{1,0:T(8,128)S(1)}, f32[384,128]{1,0:T(8,128)S(1)}, u32[]{:S(2)}, u32[]{:S(2)}) collective-permute-start(f32[384,128]{1,0:T(8,128)S(1)} %get-tuple-element.57), channel_id=1, source_target_pairs={{0,12},{4,8},{8,4},{12,0},{1,13},{5,9},{9,5},{13,1},{2,14},{6,10},... | collective-permute-start | bytes 589832 | tf_op jit(solution)/shard_map/ppermute | solution.py:43
  35.5 26.2 %collective-permute-start.4 = (f32[3,128,128]{2,1,0:T(8,128)S(1)}, f32[3,128,128]{2,1,0:T(8,128)S(1)}, u32[]{:S(2)}, u32[]{:S(2)}) collective-permute-start(f32[3,128,128]{2,1,0:T(8,128)S(1)} %get-tuple-element.51), channel_id=1, source_target_pairs={{0,4},{4,0},{8,12},{12,8},{1,5},{5,1},{9,13},{13,9},{2,6},{6,2},{1... | collective-permute-start | bytes 589832 | tf_op jit(solution)/shard_map/ppermute | solution.py:43
  37.4 37.2 %collective-permute-start.5 = (f32[3,128,128]{2,1,0:T(8,128)S(1)}, f32[3,128,128]{2,1,0:T(8,128)S(1)}, u32[]{:S(2)}, u32[]{:S(2)}) collective-permute-start(f32[3,128,128]{2,1,0:T(8,128)S(1)} %get-tuple-element.52), channel_id=1, source_target_pairs={{0,8},{4,12},{8,0},{12,4},{1,9},{5,13},{9,1},{13,5},{2,10},{6,14},... | collective-permute-start | bytes 589832 | tf_op jit(solution)/shard_map/ppermute | solution.py:43
  38.7 35.9 %collective-permute-start.6 = (f32[3,128,128]{2,1,0:T(8,128)S(1)}, f32[3,128,128]{2,1,0:T(8,128)S(1)}, u32[]{:S(2)}, u32[]{:S(2)}) collective-permute-start(f32[3,128,128]{2,1,0:T(8,128)S(1)} %get-tuple-element.53), channel_id=1, source_target_pairs={{0,12},{4,8},{8,4},{12,0},{1,13},{5,9},{9,5},{13,1},{2,14},{6,10},... | collective-permute-start | bytes 589832 | tf_op jit(solution)/shard_map/ppermute | solution.py:43
  50.2 26.7 %collective-permute-start.10 = (f32[3,128,128]{2,1,0:T(8,128)S(1)}, f32[3,128,128]{2,1,0:T(8,128)S(1)}, u32[]{:S(2)}, u32[]{:S(2)}) collective-permute-start(f32[3,128,128]{2,1,0:T(8,128)S(1)} %get-tuple-element.68), channel_id=1, source_target_pairs={{0,4},{4,0},{8,12},{12,8},{1,5},{5,1},{9,13},{13,9},{2,6},{6,2},{1... | collective-permute-start | bytes 589832 | tf_op jit(solution)/shard_map/ppermute | solution.py:43
  60.7 16.9 %collective-permute-start.11 = (f32[3,128,128]{2,1,0:T(8,128)S(1)}, f32[3,128,128]{2,1,0:T(8,128)S(1)}, u32[]{:S(2)}, u32[]{:S(2)}) collective-permute-start(f32[3,128,128]{2,1,0:T(8,128)S(1)} %get-tuple-element.69), channel_id=1, source_target_pairs={{0,8},{4,12},{8,0},{12,4},{1,9},{5,13},{9,1},{13,5},{2,10},{6,14},... | collective-permute-start | bytes 589832 | tf_op jit(solution)/shard_map/ppermute | solution.py:43
  61.7 15.8 %collective-permute-start.12 = (f32[3,128,128]{2,1,0:T(8,128)S(1)}, f32[3,128,128]{2,1,0:T(8,128)S(1)}, u32[]{:S(2)}, u32[]{:S(2)}) collective-permute-start(f32[3,128,128]{2,1,0:T(8,128)S(1)} %get-tuple-element.70), channel_id=1, source_target_pairs={{0,12},{4,8},{8,4},{12,0},{1,13},{5,9},{9,5},{13,1},{2,14},{6,10},... | collective-permute-start | bytes 589832 | tf_op jit(solution)/shard_map/ppermute | solution.py:43
  75.3 12.1 %collective-permute-start.9 = (f32[48,16,128]{2,1,0:T(8,128)S(1)}, f32[48,16,128]{2,1,0:T(8,128)S(1)}, u32[]{:S(2)}, u32[]{:S(2)}) collective-permute-start(f32[48,16,128]{2,1,0:T(8,128)S(1)} %get-tuple-element.66), channel_id=1, source_target_pairs={{0,2},{2,0},{1,3},{3,1},{4,6},{6,4},{5,7},{7,5},{8,10},{10,8},{9,1... | collective-permute-start | bytes 1179656 | tf_op jit(solution)/shard_map/ppermute | solution.py:43
  78.2 14.9 %collective-permute-start.13 = (f32[48,16,128]{2,1,0:T(8,128)S(1)}, f32[48,16,128]{2,1,0:T(8,128)S(1)}, u32[]{:S(2)}, u32[]{:S(2)}) collective-permute-start(f32[48,16,128]{2,1,0:T(8,128)S(1)} %get-tuple-element.77), channel_id=1, source_target_pairs={{0,2},{2,0},{1,3},{3,1},{4,6},{6,4},{5,7},{7,5},{8,10},{10,8},{9,1... | collective-permute-start | bytes 1179656 | tf_op jit(solution)/shard_map/ppermute | solution.py:43
  79.8 13.3 %collective-permute-start.14 = (f32[48,32,128]{2,1,0:T(8,128)S(1)}, f32[48,32,128]{2,1,0:T(8,128)S(1)}, u32[]{:S(2)}, u32[]{:S(2)}) collective-permute-start(f32[48,32,128]{2,1,0:T(8,128)S(1)} %pad_maximum_fusion), channel_id=1, source_target_pairs={{0,1},{1,0},{2,3},{3,2},{4,5},{5,4},{6,7},{7,6},{8,9},{9,8},{10,11... | collective-permute-start | bytes 2359304 | tf_op jit(solution)/shard_map/ppermute | solution.py:43
  87.4 5.8 %collective-permute-start.15 = (f32[48,16,128]{2,1,0:T(8,128)S(1)}, f32[48,16,128]{2,1,0:T(8,128)S(1)}, u32[]{:S(2)}, u32[]{:S(2)}) collective-permute-start(f32[48,16,128]{2,1,0:T(8,128)S(1)} %collective-permute-done.9.refs_2_), channel_id=1, source_target_pairs={{0,1},{1,0},{2,3},{3,2},{4,5},{5,4},{6,7},{7,6},{8,9},{9,8},{10,11... | collective-permute-start | bytes 1179656 | tf_op jit(solution)/shard_map/ppermute | solution.py:43
  93.2 1.7 %collective-permute-start.16 = (f32[48,16,128]{2,1,0:T(8,128)S(1)}, f32[48,16,128]{2,1,0:T(8,128)S(1)}, u32[]{:S(2)}, u32[]{:S(2)}) collective-permute-start(f32[48,16,128]{2,1,0:T(8,128)S(1)} %collective-permute-done.13.refs_3_), channel_id=1, source_target_pairs={{0,1},{1,0},{2,3},{3,2},{4,5},{5,4},{6,7},{7,6},{8,9},{9,8},{10,11... | collective-permute-start | bytes 1179656 | tf_op jit(solution)/shard_map/ppermute | solution.py:43
  99.4 10.6 %collective-permute-start.17 = (f32[96,128]{1,0:T(8,128)S(1)}, f32[96,128]{1,0:T(8,128)S(1)}, u32[]{:S(2)}, u32[]{:S(2)}) collective-permute-start(f32[96,128]{1,0:T(8,128)S(1)} %get-tuple-element.87), channel_id=1, source_target_pairs={{0,12},{2,14},{4,0},{6,2},{8,4},{10,6},{12,8},{14,10},{1,13},{3,15... | collective-permute-start | bytes 147464 | tf_op jit(solution)/shard_map/ppermute | solution.py:540
  101.9 8.1 %collective-permute-start.18 = (f32[96,128]{1,0:T(8,128)S(1)}, f32[96,128]{1,0:T(8,128)S(1)}, u32[]{:S(2)}, u32[]{:S(2)}) collective-permute-start(f32[96,128]{1,0:T(8,128)S(1)} %get-tuple-element.88), channel_id=1, source_target_pairs={{0,14},{2,12},{4,2},{6,0},{8,6},{10,4},{12,10},{14,8},{1,15},{3,13... | collective-permute-start | bytes 147464 | tf_op jit(solution)/shard_map/ppermute | solution.py:540
  103.5 6.4 %collective-permute-start.19 = (f32[96,128]{1,0:T(8,128)S(1)}, f32[96,128]{1,0:T(8,128)S(1)}, u32[]{:S(2)}, u32[]{:S(2)}) collective-permute-start(f32[96,128]{1,0:T(8,128)S(1)} %get-tuple-element.89), channel_id=1, source_target_pairs={{0,4},{2,6},{4,8},{6,10},{8,12},{10,14},{12,0},{14,2},{1,5},{3,7},... | collective-permute-start | bytes 147464 | tf_op jit(solution)/shard_map/ppermute | solution.py:540
  104.8 6.8 %collective-permute-start.20 = (f32[96,128]{1,0:T(8,128)S(1)}, f32[96,128]{1,0:T(8,128)S(1)}, u32[]{:S(2)}, u32[]{:S(2)}) collective-permute-start(f32[96,128]{1,0:T(8,128)S(1)} %get-tuple-element.90), channel_id=1, source_target_pairs={{0,6},{2,4},{4,10},{6,8},{8,14},{10,12},{12,2},{14,0},{1,7},{3,5},... | collective-permute-start | bytes 147464 | tf_op jit(solution)/shard_map/ppermute | solution.py:540
  104.8 6.8 %collective-permute-start.21 = (f32[96,128]{1,0:T(8,128)S(1)}, f32[96,128]{1,0:T(8,128)S(1)}, u32[]{:S(2)}, u32[]{:S(2)}) collective-permute-start(f32[96,128]{1,0:T(8,128)S(1)} %get-tuple-element.91), channel_id=1, source_target_pairs={{0,2},{2,0},{4,6},{6,4},{8,10},{10,8},{12,14},{14,12},{1,3},{3,1},... | collective-permute-start | bytes 147464 | tf_op jit(solution)/shard_map/ppermute | solution.py:540
  112.8 3.9 %collective-permute-start.23 = (f32[32,128]{1,0:T(8,128)S(1)}, f32[32,128]{1,0:T(8,128)S(1)}, u32[]{:S(2)}, u32[]{:S(2)}) collective-permute-start(f32[32,128]{1,0:T(8,128)S(1)} %get-tuple-element.94), channel_id=1, source_target_pairs={{0,2},{1,3},{2,0},{3,1},{4,6},{5,7},{6,4},{7,5},{8,10},{9,11},{10,... | collective-permute-start | bytes 49160 | tf_op jit(solution)/shard_map/ppermute | solution.py:43
  113.4 3.3 %collective-permute-start.24 = (f32[32,128]{1,0:T(8,128)S(1)}, f32[32,128]{1,0:T(8,128)S(1)}, u32[]{:S(2)}, u32[]{:S(2)}) collective-permute-start(f32[32,128]{1,0:T(8,128)S(1)} %get-tuple-element.95), channel_id=1, source_target_pairs={{0,3},{1,2},{2,1},{3,0},{4,7},{5,6},{6,5},{7,4},{8,11},{9,10},{10,... | collective-permute-start | bytes 49160 | tf_op jit(solution)/shard_map/ppermute | solution.py:43
  113.4 3.3 %collective-permute-start.22 = (f32[32,128]{1,0:T(8,128)S(1)}, f32[32,128]{1,0:T(8,128)S(1)}, u32[]{:S(2)}, u32[]{:S(2)}) collective-permute-start(f32[32,128]{1,0:T(8,128)S(1)} %get-tuple-element.93), channel_id=1, source_target_pairs={{0,1},{1,0},{2,3},{3,2},{4,5},{5,4},{6,7},{7,6},{8,9},{9,8},{10,11... | collective-permute-start | bytes 49160 | tf_op jit(solution)/shard_map/ppermute | solution.py:43
  116.8 4.7 %collective-permute-start.26 = (f32[32,128]{1,0:T(8,128)S(1)}, f32[32,128]{1,0:T(8,128)S(1)}, u32[]{:S(2)}, u32[]{:S(2)}) collective-permute-start(f32[32,128]{1,0:T(8,128)S(1)} %add_add_fusion.1), channel_id=1, source_target_pairs={{0,8},{4,12},{8,0},{12,4},{1,9},{5,13},{9,1},{13,5},{2,10},{6,14},... | collective-permute-start | bytes 49160 | tf_op jit(solution)/shard_map/ppermute | solution.py:43
  118.4 5.5 %collective-permute-start.27 = (f32[32,128]{1,0:T(8,128)S(1)}, f32[32,128]{1,0:T(8,128)S(1)}, u32[]{:S(2)}, u32[]{:S(2)}) collective-permute-start(f32[32,128]{1,0:T(8,128)S(1)} %add_add_fusion.1), channel_id=1, source_target_pairs={{0,12},{4,8},{8,4},{12,0},{1,13},{5,9},{9,5},{13,1},{2,14},{6,10},... | collective-permute-start | bytes 49160 | tf_op jit(solution)/shard_map/ppermute | solution.py:43
  119.2 4.8 %collective-permute-start.25 = (f32[32,128]{1,0:T(8,128)S(1)}, f32[32,128]{1,0:T(8,128)S(1)}, u32[]{:S(2)}, u32[]{:S(2)}) collective-permute-start(f32[32,128]{1,0:T(8,128)S(1)} %add_add_fusion.1), channel_id=1, source_target_pairs={{0,4},{4,0},{8,12},{12,8},{1,5},{5,1},{9,13},{13,9},{2,6},{6,2},{1... | collective-permute-start | bytes 49160 | tf_op jit(solution)/shard_map/ppermute | solution.py:43

commit v10 on v9

--- a/solution.py
+++ b/solution.py
@@ -387,7 +387,7 @@
     return terms[0]
 
 
-def whole_columns(panel, potential, place, me):
+def whole_columns(panel, potential, place, me, build):
     n_dom = lax.axis_size("dom")
     orbitals, planes, rows, lanes = panel.shape
     cells = planes * rows
@@ -425,11 +425,14 @@
         )
         if diagonal is None:
             diagonal = filtered[n_dom]
-        done.append(filtered[:n_dom])
+        done.append(list(filtered[:n_dom]))
+        if c == 0:
+            done[0][0], place = lax.optimization_barrier((done[0][0], place))
+            place, projectors = lax.optimization_barrier((place, build(place)))
     return [
         [(sent(x, m) if m else x).reshape(size, lanes) for m, x in enumerate(blocks)]
         for blocks in done
-    ]
+    ], projectors
 
 
 def plane_by_plane(panel, potential):
@@ -474,18 +477,15 @@
 
     place, corr_matrix = lax.optimization_barrier((place, corr_matrix))
 
-    def build(offsets):
-        return build_projectors(n_band, n_sub, place, offsets, point_coefs, share, lanes)
+    def build(place):
+        return build_projectors(n_band, n_sub, place, point_offsets, point_coefs, share, lanes)
 
     if n_dom in (2, 4) and orbitals % (n_dom * TOGETHER) == 0 and planes * n_dom % 2 == 0:
-        chunks = whole_columns(panel, potential, place, me)
-        chunks[-1][0], point_offsets = lax.optimization_barrier((chunks[-1][0], point_offsets))
-        projectors = build(point_offsets)
-        chunks[0], projectors = lax.optimization_barrier((chunks[0], projectors))
+        chunks, projectors = whole_columns(panel, potential, place, me, build)
         filtered = orbital_first(place, n_dom, [piece for pieces in chunks for piece in pieces])
         parts = [cell_first(place, n_band, pieces) for pieces in chunks]
     else:
-        projectors = build(point_offsets)
+        projectors = build(place)
         filtered = plane_by_plane(panel, potential)
         by_cell = filtered.reshape(orbitals, cells, lanes).swapaxes(0, 1)
         parts = [

time: 125 us -> 121 us (0.968)
  starting transfers between devices: 42.4 us -> 35.5 us
  waiting for transfers between devices: 40.2 us -> 43.2 us
    ppermute x23, starting transfers between devices: 35.5 us -> 26.5 us  [swapped(): return lax.ppermute(x, axes, [(i, i ^ by) for i in range(size)])]
    ppermute x5, starting transfers between devices: 6.91 us -> 9 us  [on_device(): sums.append(lax.ppermute(x, ('dom', 'band'), pairs))]
    ppermute x23, waiting for transfers between devices: 38.6 us -> 40.6 us  [swapped(): return lax.ppermute(x, axes, [(i, i ^ by) for i in range(size)])]
  transfers between devices with their start and end apart: 28 -> 28, of which waited for: 12 -> 11; matrix products, arithmetic and copies ran while one was open for 1% -> 1% of each run, Pallas kernels for 26% -> 26%
where the time goes in v10:
time: 121 us
  waiting for transfers between devices  43.2 us (36%)
  Pallas kernels  37.1 us (31%)
  starting transfers between devices  35.5 us (29%)
  local copies, waits for them, and re-layouts  2.83 us (2%)
  other arithmetic  1.77 us (1%)
    ppermute x23, waiting for transfers between devices, swapped(): return lax.ppermute(x, axes, [(i, i ^ by) for i in range(size)])  40.6 us
    ppermute x23, starting transfers between devices, swapped(): return lax.ppermute(x, axes, [(i, i ^ by) for i in range(size)])  26.5 us
    pallas_call x2, Pallas kernels, filter_orbitals(): pl.pallas_call(functools.partial(filter_kernel, n_dom, planes, rows, star...  13.2 us
    pallas_call x1, Pallas kernels, build_projectors(): pl.pallas_call(functools.partial(projector_kernel, n_band, n_sub), out_sh...  11.5 us
    ppermute x5, starting transfers between devices, on_device(): sums.append(lax.ppermute(x, ('dom', 'band'), pairs))  9 us
    pallas_call x2, Pallas kernels, products(): pl.pallas_call(functools.partial(product_kernel, spots, n_sub, first_row,...  8.1 us
    ppermute x5, waiting for transfers between devices, on_device(): sums.append(lax.ppermute(x, ('dom', 'band'), pairs))  2.56 us
  transfers between devices with their start and end apart: 28, of which 11 were waited for; matrix products, arithmetic and copies ran while one was open for 1% of the time, Pallas kernels for 26%

profile of v10, /device:TPU:0, one launch (start us, length us, event | category | flops | bytes accessed | tf_op | source)
XLA Modules:
  0.0 121.3 jit_solution(11949418659642941838)
XLA Ops:
  0.6 0.0 copy-start
  0.7 2.3 %constant_dynamic-slice_fusion = (f32[384,128]{1,0:T(8,128)S(1)}, f32[384,128]{1,0:T(8,128)}, f32[384,128]{1,0:T(8,128)S(1)}, f32[384,128]{1,0:T(8,128)}, f32[38...) fusion(f32[3072,128]{1,0:T(8,128)} %bitcast.33, s32[]{:T(128)S(6)} %select_n.35, ...), kind=kLoop, calls=%fused_computation.9 | loop fusion | bytes 3145760 | tf_op jit(solution)/shard_map/dynamic_slice | solution.py:400
  3.1 4.1 %collective-permute-start = (f32[480,128]{1,0:T(8,128)S(1)}, f32[480,128]{1,0:T(8,128)S(1)}, u32[]{:S(2)}, u32[]{:S(2)}) collective-permute-start(f32[480,128]{1,0:T(8,128)S(1)} %get-tuple-element.99), channel_id=1, source_target_pairs={{0,8},{4,12},{8,0},{12,4},{1,9},{5,13},{9,1},{13,5},{2,10},{6,14},... | collective-permute-start | bytes 737288 | tf_op jit(solution)/shard_map/ppermute | solution.py:43
  7.2 0.8 pad_maximum_fusion.1
  8.0 1.6 %collective-permute-start.2 = (f32[864,128]{1,0:T(8,128)}, f32[864,128]{1,0:T(8,128)S(1)}, u32[]{:S(2)}, u32[]{:S(2)}) collective-permute-start(f32[864,128]{1,0:T(8,128)} %pad_maximum_fusion.1), channel_id=1, source_target_pairs={{0,4},{4,0},{8,12},{12,8},{1,5},{5,1},{9,13},{13,9},{2,6},{6,2},{1... | collective-permute-start | bytes 1327112 | tf_op jit(solution)/shard_map/ppermute | solution.py:43
  9.6 0.1 constant_dynamic-slice_fusion.8
  9.6 0.1 copy.8
  9.8 0.1 broadcast_multiply_fusion
  9.9 9.4 %collective-permute-done.refs_3_ = f32[480,128]{1,0:T(8,128)S(1)} collective-permute-done((f32[480,128]{1,0:T(8,128)S(1)}, f32[480,128]{1,0:T(8,128)S(1)}, u32[]{:S(2)}, u32[]{:S(2)}) %collective-permute-start) | collective-permute-done | bytes 245792 | tf_op jit(solution)/shard_map/ppermute | solution.py:43
  19.3 0.0 collective-permute-start.1
  19.3 0.1 pad_add_fusion.place
  19.4 9.9 %collective-permute-done.2.refs_2_ = f32[864,128]{1,0:T(8,128)S(1)} collective-permute-done((f32[864,128]{1,0:T(8,128)}, f32[864,128]{1,0:T(8,128)S(1)}, u32[]{:S(2)}, u32[]{:S(2)}) %collective-permute-start.2) | collective-permute-done | bytes 442400 | tf_op jit(solution)/shard_map/ppermute | solution.py:43
  29.2 0.5 collective-permute-start.8
  29.7 2.0 %collective-permute-start.9 = (f32[384,128]{1,0:T(8,128)S(1)}, f32[384,128]{1,0:T(8,128)S(1)}, u32[]{:S(2)}, u32[]{:S(2)}) collective-permute-start(f32[384,128]{1,0:T(8,128)S(1)} %get-tuple-element.60), channel_id=1, source_target_pairs={{0,12},{4,8},{8,4},{12,0},{1,13},{5,9},{9,5},{13,1},{2,14},{6,10},... | collective-permute-start | bytes 589832 | tf_op jit(solution)/shard_map/ppermute | solution.py:43
  31.7 0.3 mul.56.corr_ref
  32.0 0.0 collective-permute-done.3.refs_4_
  32.0 6.8 %chebyshev.2 = (f32[3,128,128]{2,1,0:T(8,128)S(1)}, f32[3,128,128]{2,1,0:T(8,128)S(1)}, f32[3,128,128]{2,1,0:T(8,128)S(1)}, f32[3,128,128]{2,1,0:T(8,128)S(1)}, f32[6,32,8,128]{3,2,1,0:T(8,128)S(1)}) custom-call(s32[4]{0:T(128)S(1)} %pad_add_fusion.place, f32[96,128]{1,0:T(8,128)S(1)} %collective-permute-done.1.refs_0_, ...), custom_call_target="tpu_custom_call" | custom-call | flops 28311552 | bytes 1572864 | tf_op jit(solution)/shard_map/chebyshev/pallas_call | solution.py:132
  38.8 1.1 collective-permute-start.4
  39.9 1.4 %collective-permute-start.5 = (f32[3,128,128]{2,1,0:T(8,128)S(1)}, f32[3,128,128]{2,1,0:T(8,128)S(1)}, u32[]{:S(2)}, u32[]{:S(2)}) collective-permute-start(f32[3,128,128]{2,1,0:T(8,128)S(1)} %get-tuple-element.50), channel_id=1, source_target_pairs={{0,8},{4,12},{8,0},{12,4},{1,9},{5,13},{9,1},{13,5},{2,10},{6,14},... | collective-permute-start | bytes 589832 | tf_op jit(solution)/shard_map/ppermute | solution.py:43
  41.3 2.0 %collective-permute-start.6 = (f32[3,128,128]{2,1,0:T(8,128)S(1)}, f32[3,128,128]{2,1,0:T(8,128)S(1)}, u32[]{:S(2)}, u32[]{:S(2)}) collective-permute-start(f32[3,128,128]{2,1,0:T(8,128)S(1)} %get-tuple-element.51), channel_id=1, source_target_pairs={{0,12},{4,8},{8,4},{12,0},{1,13},{5,9},{9,5},{13,1},{2,14},{6,10},... | collective-permute-start | bytes 589832 | tf_op jit(solution)/shard_map/ppermute | solution.py:43
  43.3 11.5 %projectors.1 = (bf16[576,6144]{1,0:T(8,128)(2,1)S(1)}, bf16[576,6144]{1,0:T(8,128)(2,1)S(1)}) custom-call(s32[4]{0:T(128)S(1)} %pad_add_fusion.place, s32[3,48,128]{2,1,0:T(8,128)S(1)} %bitcast.32, f32[48,3,8,128]{3,2,1,0:T(8,128)S(1)} %copy-done.1), custom_call_target="tpu_custom_call" | custom-call | flops 1811939328 | bytes 28311552 | tf_op jit(solution)/shard_map/projectors/pallas_call | solution.py:258
  54.7 0.0 collective-permute-done.8.refs_3_
  54.7 0.0 collective-permute-done.9.refs_4_
  54.8 6.4 %chebyshev.3 = (f32[3,128,128]{2,1,0:T(8,128)S(1)}, f32[3,128,128]{2,1,0:T(8,128)S(1)}, f32[3,128,128]{2,1,0:T(8,128)S(1)}, f32[3,128,128]{2,1,0:T(8,128)S(1)}) custom-call(s32[4]{0:T(128)S(1)} %pad_add_fusion.place, f32[6,32,8,128]{3,2,1,0:T(8,128)S(1)} %get-tuple-element.57.refs_0_, f32[384,128]{1,0:T(8,128)S(1)} %get-tuple-element.92.refs_1_, ...), custom_call_target="tpu_custom_call" | custom-call | flops 28311552 | bytes 1572864 | tf_op jit(solution)/shard_map/chebyshev/pallas_call | solution.py:132
  61.2 0.5 collective-permute-start.10
  61.7 2.0 %collective-permute-start.11 = (f32[3,128,128]{2,1,0:T(8,128)S(1)}, f32[3,128,128]{2,1,0:T(8,128)S(1)}, u32[]{:S(2)}, u32[]{:S(2)}) collective-permute-start(f32[3,128,128]{2,1,0:T(8,128)S(1)} %get-tuple-element.63), channel_id=1, source_target_pairs={{0,8},{4,12},{8,0},{12,4},{1,9},{5,13},{9,1},{13,5},{2,10},{6,14},... | collective-permute-start | bytes 589832 | tf_op jit(solution)/shard_map/ppermute | solution.py:43
  63.7 0.0 collective-permute-done.4
  63.7 2.0 %collective-permute-start.12 = (f32[3,128,128]{2,1,0:T(8,128)S(1)}, f32[3,128,128]{2,1,0:T(8,128)S(1)}, u32[]{:S(2)}, u32[]{:S(2)}) collective-permute-start(f32[3,128,128]{2,1,0:T(8,128)S(1)} %get-tuple-element.64), channel_id=1, source_target_pairs={{0,12},{4,8},{8,4},{12,0},{1,13},{5,9},{9,5},{13,1},{2,14},{6,10},... | collective-permute-start | bytes 589832 | tf_op jit(solution)/shard_map/ppermute | solution.py:43
  65.7 0.0 collective-permute-done.5
  65.7 0.0 collective-permute-done.6
  65.7 0.7 cell_first.2
  66.3 1.6 %collective-permute-start.7 = (f32[48,16,128]{2,1,0:T(8,128)S(1)}, f32[48,16,128]{2,1,0:T(8,128)S(1)}, u32[]{:S(2)}, u32[]{:S(2)}) collective-permute-start(f32[48,16,128]{2,1,0:T(8,128)S(1)} %get-tuple-element.52), channel_id=1, source_target_pairs={{0,2},{2,0},{1,3},{3,1},{4,6},{6,4},{5,7},{7,5},{8,10},{10,8},{9,1... | collective-permute-start | bytes 1179656 | tf_op jit(solution)/shard_map/ppermute | solution.py:43
  67.9 9.2 %collective-permute-done.11 = f32[3,128,128]{2,1,0:T(8,128)S(1)} collective-permute-done((f32[3,128,128]{2,1,0:T(8,128)S(1)}, f32[3,128,128]{2,1,0:T(8,128)S(1)}, u32[]{:S(2)}, u32[]{:S(2)}) %collective-permute-start.11) | collective-permute-done | bytes 196640 | tf_op jit(solution)/shard_map/ppermute | solution.py:43
  77.1 0.0 collective-permute-done.12
  77.1 0.7 cell_first.3
  77.8 1.6 %collective-permute-start.13 = (f32[48,16,128]{2,1,0:T(8,128)S(1)}, f32[48,16,128]{2,1,0:T(8,128)S(1)}, u32[]{:S(2)}, u32[]{:S(2)}) collective-permute-start(f32[48,16,128]{2,1,0:T(8,128)S(1)} %get-tuple-element.71), channel_id=1, source_target_pairs={{0,2},{2,0},{1,3},{3,1},{4,6},{6,4},{5,7},{7,5},{8,10},{10,8},{9,1... | collective-permute-start | bytes 1179656 | tf_op jit(solution)/shard_map/ppermute | solution.py:43
  79.4 0.1 pad_maximum_fusion
  79.5 0.1 collective-permute-start.14
  79.5 1.8 %orbital_first.1 = f32[32,96,128]{2,1,0:T(8,128)} custom-call(s32[4]{0:T(128)S(1)} %pad_add_fusion.place, f32[384,128]{1,0:T(8,128)S(1)} %bitcast.17, f32[384,128]{1,0:T(8,128)S(1)} %bitcast.19, f32[384,128]{1,0:T(8,128)S(1)} %bitcast.21, f32[384,128]{1,0:T(8,128)S(1)} %bitcast.23, f32[384,128]{1,0:T(8,128)S(1)} %bitcast.25, f32[384,128]{1,0:T(8,128)S(1)} %bitcast.27, ...), custom_call_target="tpu_custom_call" | custom-call | tf_op jit(solution)/shard_map/orbital_first/pallas_call | solution.py:197
  81.3 0.0 collective-permute-done.7.refs_2_
  81.3 0.5 collective-permute-start.15
  81.8 3.8 %collective-permute-done.13.refs_3_ = f32[48,16,128]{2,1,0:T(8,128)S(1)} collective-permute-done((f32[48,16,128]{2,1,0:T(8,128)S(1)}, f32[48,16,128]{2,1,0:T(8,128)S(1)}, u32[]{:S(2)}, u32[]{:S(2)}) %collective-permute-start.13) | collective-permute-done | bytes 393248 | tf_op jit(solution)/shard_map/ppermute | solution.py:43
  85.6 0.0 collective-permute-start.16
  85.6 0.0 collective-permute-done.15.refs_5_
  85.6 0.0 collective-permute-done.14.refs_4_
  85.7 1.7 %collective-permute-done.16.refs_6_ = f32[48,16,128]{2,1,0:T(8,128)S(1)} collective-permute-done((f32[48,16,128]{2,1,0:T(8,128)S(1)}, f32[48,16,128]{2,1,0:T(8,128)S(1)}, u32[]{:S(2)}, u32[]{:S(2)}) %collective-permute-start.16) | collective-permute-done | bytes 393248 | tf_op jit(solution)/shard_map/ppermute | solution.py:43
  87.4 4.4 %products.2 = (f32[96,128]{1,0:T(8,128)S(1)}, f32[96,128]{1,0:T(8,128)S(1)}, f32[96,128]{1,0:T(8,128)S(1)}, f32[96,128]{1,0:T(8,128)S(1)}, f32[96,128]{1,0:T(8,128)S(1)}) custom-call(s32[4]{0:T(128)S(1)} %pad_add_fusion.place, bf16[576,6144]{1,0:T(8,128)(2,1)S(1)} %get-tuple-element.66.w_high, bf16[576,6144]{1,0:T(8,128)(2,1)S(1)} %get-tuple-element.67.w_low, ...), custom_call_target="tpu_custom_call" | custom-call | flops 4529848320 | bytes 11796480 | tf_op jit(solution)/shard_map/products/pallas_call | solution.py:325
  91.8 2.8 %collective-permute-start.17 = (f32[96,128]{1,0:T(8,128)S(1)}, f32[96,128]{1,0:T(8,128)S(1)}, u32[]{:S(2)}, u32[]{:S(2)}) collective-permute-start(f32[96,128]{1,0:T(8,128)S(1)} %get-tuple-element.81), channel_id=1, source_target_pairs={{0,12},{2,14},{4,0},{6,2},{8,4},{10,6},{12,8},{14,10},{1,13},{3,15... | collective-permute-start | bytes 147464 | tf_op jit(solution)/shard_map/ppermute | solution.py:540
  94.6 5.7 %collective-permute-start.18 = (f32[96,128]{1,0:T(8,128)S(1)}, f32[96,128]{1,0:T(8,128)S(1)}, u32[]{:S(2)}, u32[]{:S(2)}) collective-permute-start(f32[96,128]{1,0:T(8,128)S(1)} %get-tuple-element.82), channel_id=1, source_target_pairs={{0,14},{2,12},{4,2},{6,0},{8,6},{10,4},{12,10},{14,8},{1,15},{3,13... | collective-permute-start | bytes 147464 | tf_op jit(solution)/shard_map/ppermute | solution.py:540
  100.3 0.0 collective-permute-start.19
  100.3 0.5 collective-permute-start.21
  100.8 3.7 %products.3 = (f32[128,128]{1,0:T(8,128)S(1)}, f32[96,128]{1,0:T(8,128)S(1)}) custom-call(s32[4]{0:T(128)S(1)} %pad_add_fusion.place, bf16[576,6144]{1,0:T(8,128)(2,1)S(1)} %get-tuple-element.66.w_high, bf16[576,6144]{1,0:T(8,128)(2,1)S(1)} %get-tuple-element.67.w_low, f32[48,16,128]{2,1,0:T(8,128)S(1)} %get-tuple-element.68.refs_0_, ...), custom_call_target="tpu_custom_call" | custom-call | flops 905969664 | bytes 2359296 | tf_op jit(solution)/shard_map/products/pallas_call | solution.py:325
  104.5 1.6 %collective-permute-done.19.refs_2_ = f32[96,128]{1,0:T(8,128)S(1)} collective-permute-done((f32[96,128]{1,0:T(8,128)S(1)}, f32[96,128]{1,0:T(8,128)S(1)}, u32[]{:S(2)}, u32[]{:S(2)}) %collective-permute-start.19) | collective-permute-done | bytes 49184 | tf_op jit(solution)/shard_map/ppermute | solution.py:540
  106.1 0.9 collective-permute-done.20.refs_3_
  107.1 1.2 %gram_share.1 = (f32[32,128]{1,0:T(8,128)S(1)}, f32[32,128]{1,0:T(8,128)S(1)}, f32[32,128]{1,0:T(8,128)S(1)}, f32[32,128]{1,0:T(8,128)S(1)}) custom-call(s32[4]{0:T(128)S(1)} %pad_add_fusion.place, f32[96,96]{1,0:T(8,128)S(1)} %mul.56.corr_ref, f32[128,128]{1,0:T(8,128)S(1)} %get-tuple-element.79.grid_ref, f32[96,128]{1,0:T(8,128)S(1)} %get-tuple-element.80.proj_ref, ...), custom_call_target="tpu_custom_call" | custom-call | tf_op jit(solution)/shard_map/gram_share/pallas_call | solution.py:374
  108.3 1.2 collective-permute-start.23
  109.4 1.0 collective-permute-start.22
  110.5 1.6 %collective-permute-done.23 = f32[32,128]{1,0:T(8,128)S(1)} collective-permute-done((f32[32,128]{1,0:T(8,128)S(1)}, f32[32,128]{1,0:T(8,128)S(1)}, u32[]{:S(2)}, u32[]{:S(2)}) %collective-permute-start.23) | collective-permute-done | bytes 16416 | tf_op jit(solution)/shard_map/ppermute | solution.py:43
  112.1 0.5 collective-permute-done.24
  112.6 2.5 %collective-permute-start.26 = (f32[32,128]{1,0:T(8,128)S(1)}, f32[32,128]{1,0:T(8,128)S(1)}, u32[]{:S(2)}, u32[]{:S(2)}) collective-permute-start(f32[32,128]{1,0:T(8,128)S(1)} %add_add_fusion.1), channel_id=1, source_target_pairs={{0,8},{4,12},{8,0},{12,4},{1,9},{5,13},{9,1},{13,5},{2,10},{6,14},... | collective-permute-start | bytes 49160 | tf_op jit(solution)/shard_map/ppermute | solution.py:43
  115.1 1.1 collective-permute-start.25
  116.2 1.2 %collective-permute-done.26 = f32[32,128]{1,0:T(8,128)S(1)} collective-permute-done((f32[32,128]{1,0:T(8,128)S(1)}, f32[32,128]{1,0:T(8,128)S(1)}, u32[]{:S(2)}, u32[]{:S(2)}) %collective-permute-start.26) | collective-permute-done | bytes 16416 | tf_op jit(solution)/shard_map/ppermute | solution.py:43
  117.4 3.2 %collective-permute-done.27 = f32[32,128]{1,0:T(8,128)S(1)} collective-permute-done((f32[32,128]{1,0:T(8,128)S(1)}, f32[32,128]{1,0:T(8,128)S(1)}, u32[]{:S(2)}, u32[]{:S(2)}) %collective-permute-start.27) | collective-permute-done | bytes 16416 | tf_op jit(solution)/shard_map/ppermute | solution.py:43
  120.6 0.6 add_add_fusion
  (22 shorter events, 0.1 us)
Async XLA Ops:
  0.6 8.9 %copy-start = (f32[48,8,8]{0,2,1:T(8,128)S(1)}, f32[48,8,8]{0,2,1:T(8,128)}, u32[]{:S(2)}) copy-start(f32[48,8,8]{0,2,1:T(8,128)} %param.9) | copy-start | bytes 36868
  0.7 2.3 %copy-start.3 = (f32[3,32,128]{2,1,0:T(8,128)S(1)}, f32[3,32,128]{2,1,0:T(8,128)}, u32[]{:S(2)}) copy-start(f32[3,32,128]{2,1,0:T(8,128)} %param.6) | copy-start | bytes 147460
  3.1 16.2 %collective-permute-start = (f32[480,128]{1,0:T(8,128)S(1)}, f32[480,128]{1,0:T(8,128)S(1)}, u32[]{:S(2)}, u32[]{:S(2)}) collective-permute-start(f32[480,128]{1,0:T(8,128)S(1)} %get-tuple-element.99), channel_id=1, source_target_pairs={{0,8},{4,12},{8,0},{12,4},{1,9},{5,13},{9,1},{13,5},{2,10},{6,14},... | collective-permute-start | bytes 737288 | tf_op jit(solution)/shard_map/ppermute | solution.py:43
  8.0 21.3 %collective-permute-start.2 = (f32[864,128]{1,0:T(8,128)}, f32[864,128]{1,0:T(8,128)S(1)}, u32[]{:S(2)}, u32[]{:S(2)}) collective-permute-start(f32[864,128]{1,0:T(8,128)} %pad_maximum_fusion.1), channel_id=1, source_target_pairs={{0,4},{4,0},{8,12},{12,8},{1,5},{5,1},{9,13},{13,9},{2,6},{6,2},{1... | collective-permute-start | bytes 1327112 | tf_op jit(solution)/shard_map/ppermute | solution.py:43
  9.5 22.4 %collective-permute-start.3 = (f32[384,128]{1,0:T(8,128)}, f32[384,128]{1,0:T(8,128)S(1)}, u32[]{:S(2)}, u32[]{:S(2)}) collective-permute-start(f32[384,128]{1,0:T(8,128)} %get-tuple-element.93), channel_id=1, source_target_pairs={{0,12},{4,8},{8,4},{12,0},{1,13},{5,9},{9,5},{13,1},{2,14},{6,10},... | collective-permute-start | bytes 589832 | tf_op jit(solution)/shard_map/ppermute | solution.py:43
  9.5 33.7 %copy-start.1 = (f32[48,3,8,128]{3,2,1,0:T(8,128)S(1)}, f32[48,3,8,128]{3,2,1,0:T(8,128)}, u32[]{:S(2)}) copy-start(f32[48,3,8,128]{3,2,1,0:T(8,128)} %coefs_ref.1) | copy-start | bytes 1769476
  9.5 33.7 %copy-start.2 = (s32[48,3,128]{2,0,1:T(8,128)S(1)}, s32[48,3,128]{2,0,1:T(8,128)}, u32[]{:S(2)}) copy-start(s32[48,3,128]{2,0,1:T(8,128)} %param.7) | copy-start | bytes 221188
  19.3 12.7 %collective-permute-start.1 = (f32[96,128]{1,0:T(8,128)S(1)}, f32[96,128]{1,0:T(8,128)S(1)}, u32[]{:S(2)}, u32[]{:S(2)}) collective-permute-start(f32[96,128]{1,0:T(8,128)S(1)} %slice.4), channel_id=1, source_target_pairs={{0,4},{4,0},{8,12},{12,8},{1,5},{5,1},{9,13},{13,9},{2,6},{6,2},{1... | collective-permute-start | bytes 147464 | tf_op jit(solution)/shard_map/ppermute | solution.py:43
  29.2 25.5 %collective-permute-start.8 = (f32[384,128]{1,0:T(8,128)}, f32[384,128]{1,0:T(8,128)S(1)}, u32[]{:S(2)}, u32[]{:S(2)}) collective-permute-start(f32[384,128]{1,0:T(8,128)} %get-tuple-element.59), channel_id=1, source_target_pairs={{0,8},{4,12},{8,0},{12,4},{1,9},{5,13},{9,1},{13,5},{2,10},{6,14},... | collective-permute-start | bytes 589832 | tf_op jit(solution)/shard_map/ppermute | solution.py:43
  29.7 25.0 %collective-permute-start.9 = (f32[384,128]{1,0:T(8,128)S(1)}, f32[384,128]{1,0:T(8,128)S(1)}, u32[]{:S(2)}, u32[]{:S(2)}) collective-permute-start(f32[384,128]{1,0:T(8,128)S(1)} %get-tuple-element.60), channel_id=1, source_target_pairs={{0,12},{4,8},{8,4},{12,0},{1,13},{5,9},{9,5},{13,1},{2,14},{6,10},... | collective-permute-start | bytes 589832 | tf_op jit(solution)/shard_map/ppermute | solution.py:43
  38.8 24.9 %collective-permute-start.4 = (f32[3,128,128]{2,1,0:T(8,128)S(1)}, f32[3,128,128]{2,1,0:T(8,128)S(1)}, u32[]{:S(2)}, u32[]{:S(2)}) collective-permute-start(f32[3,128,128]{2,1,0:T(8,128)S(1)} %get-tuple-element.49), channel_id=1, source_target_pairs={{0,4},{4,0},{8,12},{12,8},{1,5},{5,1},{9,13},{13,9},{2,6},{6,2},{1... | collective-permute-start | bytes 589832 | tf_op jit(solution)/shard_map/ppermute | solution.py:43
  39.9 25.8 %collective-permute-start.5 = (f32[3,128,128]{2,1,0:T(8,128)S(1)}, f32[3,128,128]{2,1,0:T(8,128)S(1)}, u32[]{:S(2)}, u32[]{:S(2)}) collective-permute-start(f32[3,128,128]{2,1,0:T(8,128)S(1)} %get-tuple-element.50), channel_id=1, source_target_pairs={{0,8},{4,12},{8,0},{12,4},{1,9},{5,13},{9,1},{13,5},{2,10},{6,14},... | collective-permute-start | bytes 589832 | tf_op jit(solution)/shard_map/ppermute | solution.py:43
  41.3 24.4 %collective-permute-start.6 = (f32[3,128,128]{2,1,0:T(8,128)S(1)}, f32[3,128,128]{2,1,0:T(8,128)S(1)}, u32[]{:S(2)}, u32[]{:S(2)}) collective-permute-start(f32[3,128,128]{2,1,0:T(8,128)S(1)} %get-tuple-element.51), channel_id=1, source_target_pairs={{0,12},{4,8},{8,4},{12,0},{1,13},{5,9},{9,5},{13,1},{2,14},{6,10},... | collective-permute-start | bytes 589832 | tf_op jit(solution)/shard_map/ppermute | solution.py:43
  61.2 6.7 %collective-permute-start.10 = (f32[3,128,128]{2,1,0:T(8,128)S(1)}, f32[3,128,128]{2,1,0:T(8,128)S(1)}, u32[]{:S(2)}, u32[]{:S(2)}) collective-permute-start(f32[3,128,128]{2,1,0:T(8,128)S(1)} %get-tuple-element.62), channel_id=1, source_target_pairs={{0,4},{4,0},{8,12},{12,8},{1,5},{5,1},{9,13},{13,9},{2,6},{6,2},{1... | collective-permute-start | bytes 589832 | tf_op jit(solution)/shard_map/ppermute | solution.py:43
  61.7 15.4 %collective-permute-start.11 = (f32[3,128,128]{2,1,0:T(8,128)S(1)}, f32[3,128,128]{2,1,0:T(8,128)S(1)}, u32[]{:S(2)}, u32[]{:S(2)}) collective-permute-start(f32[3,128,128]{2,1,0:T(8,128)S(1)} %get-tuple-element.63), channel_id=1, source_target_pairs={{0,8},{4,12},{8,0},{12,4},{1,9},{5,13},{9,1},{13,5},{2,10},{6,14},... | collective-permute-start | bytes 589832 | tf_op jit(solution)/shard_map/ppermute | solution.py:43
  63.7 13.4 %collective-permute-start.12 = (f32[3,128,128]{2,1,0:T(8,128)S(1)}, f32[3,128,128]{2,1,0:T(8,128)S(1)}, u32[]{:S(2)}, u32[]{:S(2)}) collective-permute-start(f32[3,128,128]{2,1,0:T(8,128)S(1)} %get-tuple-element.64), channel_id=1, source_target_pairs={{0,12},{4,8},{8,4},{12,0},{1,13},{5,9},{9,5},{13,1},{2,14},{6,10},... | collective-permute-start | bytes 589832 | tf_op jit(solution)/shard_map/ppermute | solution.py:43
  66.3 15.0 %collective-permute-start.7 = (f32[48,16,128]{2,1,0:T(8,128)S(1)}, f32[48,16,128]{2,1,0:T(8,128)S(1)}, u32[]{:S(2)}, u32[]{:S(2)}) collective-permute-start(f32[48,16,128]{2,1,0:T(8,128)S(1)} %get-tuple-element.52), channel_id=1, source_target_pairs={{0,2},{2,0},{1,3},{3,1},{4,6},{6,4},{5,7},{7,5},{8,10},{10,8},{9,1... | collective-permute-start | bytes 1179656 | tf_op jit(solution)/shard_map/ppermute | solution.py:43
  77.8 7.8 %collective-permute-start.13 = (f32[48,16,128]{2,1,0:T(8,128)S(1)}, f32[48,16,128]{2,1,0:T(8,128)S(1)}, u32[]{:S(2)}, u32[]{:S(2)}) collective-permute-start(f32[48,16,128]{2,1,0:T(8,128)S(1)} %get-tuple-element.71), channel_id=1, source_target_pairs={{0,2},{2,0},{1,3},{3,1},{4,6},{6,4},{5,7},{7,5},{8,10},{10,8},{9,1... | collective-permute-start | bytes 1179656 | tf_op jit(solution)/shard_map/ppermute | solution.py:43
  79.5 6.2 %collective-permute-start.14 = (f32[48,32,128]{2,1,0:T(8,128)S(1)}, f32[48,32,128]{2,1,0:T(8,128)S(1)}, u32[]{:S(2)}, u32[]{:S(2)}) collective-permute-start(f32[48,32,128]{2,1,0:T(8,128)S(1)} %pad_maximum_fusion), channel_id=1, source_target_pairs={{0,1},{1,0},{2,3},{3,2},{4,5},{5,4},{6,7},{7,6},{8,9},{9,8},{10,11... | collective-permute-start | bytes 2359304 | tf_op jit(solution)/shard_map/ppermute | solution.py:43
  81.3 4.3 %collective-permute-start.15 = (f32[48,16,128]{2,1,0:T(8,128)S(1)}, f32[48,16,128]{2,1,0:T(8,128)S(1)}, u32[]{:S(2)}, u32[]{:S(2)}) collective-permute-start(f32[48,16,128]{2,1,0:T(8,128)S(1)} %collective-permute-done.7.refs_2_), channel_id=1, source_target_pairs={{0,1},{1,0},{2,3},{3,2},{4,5},{5,4},{6,7},{7,6},{8,9},{9,8},{10,11... | collective-permute-start | bytes 1179656 | tf_op jit(solution)/shard_map/ppermute | solution.py:43
  85.6 1.7 %collective-permute-start.16 = (f32[48,16,128]{2,1,0:T(8,128)S(1)}, f32[48,16,128]{2,1,0:T(8,128)S(1)}, u32[]{:S(2)}, u32[]{:S(2)}) collective-permute-start(f32[48,16,128]{2,1,0:T(8,128)S(1)} %collective-permute-done.13.refs_3_), channel_id=1, source_target_pairs={{0,1},{1,0},{2,3},{3,2},{4,5},{5,4},{6,7},{7,6},{8,9},{9,8},{10,11... | collective-permute-start | bytes 1179656 | tf_op jit(solution)/shard_map/ppermute | solution.py:43
  91.8 12.7 %collective-permute-start.17 = (f32[96,128]{1,0:T(8,128)S(1)}, f32[96,128]{1,0:T(8,128)S(1)}, u32[]{:S(2)}, u32[]{:S(2)}) collective-permute-start(f32[96,128]{1,0:T(8,128)S(1)} %get-tuple-element.81), channel_id=1, source_target_pairs={{0,12},{2,14},{4,0},{6,2},{8,4},{10,6},{12,8},{14,10},{1,13},{3,15... | collective-permute-start | bytes 147464 | tf_op jit(solution)/shard_map/ppermute | solution.py:540
  94.6 9.9 %collective-permute-start.18 = (f32[96,128]{1,0:T(8,128)S(1)}, f32[96,128]{1,0:T(8,128)S(1)}, u32[]{:S(2)}, u32[]{:S(2)}) collective-permute-start(f32[96,128]{1,0:T(8,128)S(1)} %get-tuple-element.82), channel_id=1, source_target_pairs={{0,14},{2,12},{4,2},{6,0},{8,6},{10,4},{12,10},{14,8},{1,15},{3,13... | collective-permute-start | bytes 147464 | tf_op jit(solution)/shard_map/ppermute | solution.py:540
  100.3 5.9 %collective-permute-start.19 = (f32[96,128]{1,0:T(8,128)S(1)}, f32[96,128]{1,0:T(8,128)S(1)}, u32[]{:S(2)}, u32[]{:S(2)}) collective-permute-start(f32[96,128]{1,0:T(8,128)S(1)} %get-tuple-element.83), channel_id=1, source_target_pairs={{0,4},{2,6},{4,8},{6,10},{8,12},{10,14},{12,0},{14,2},{1,5},{3,7},... | collective-permute-start | bytes 147464 | tf_op jit(solution)/shard_map/ppermute | solution.py:540
  100.3 6.8 %collective-permute-start.20 = (f32[96,128]{1,0:T(8,128)S(1)}, f32[96,128]{1,0:T(8,128)S(1)}, u32[]{:S(2)}, u32[]{:S(2)}) collective-permute-start(f32[96,128]{1,0:T(8,128)S(1)} %get-tuple-element.84), channel_id=1, source_target_pairs={{0,6},{2,4},{4,10},{6,8},{8,14},{10,12},{12,2},{14,0},{1,7},{3,5},... | collective-permute-start | bytes 147464 | tf_op jit(solution)/shard_map/ppermute | solution.py:540
  100.3 6.8 %collective-permute-start.21 = (f32[96,128]{1,0:T(8,128)S(1)}, f32[96,128]{1,0:T(8,128)S(1)}, u32[]{:S(2)}, u32[]{:S(2)}) collective-permute-start(f32[96,128]{1,0:T(8,128)S(1)} %get-tuple-element.85), channel_id=1, source_target_pairs={{0,2},{2,0},{4,6},{6,4},{8,10},{10,8},{12,14},{14,12},{1,3},{3,1},... | collective-permute-start | bytes 147464 | tf_op jit(solution)/shard_map/ppermute | solution.py:540
  108.3 3.8 %collective-permute-start.23 = (f32[32,128]{1,0:T(8,128)S(1)}, f32[32,128]{1,0:T(8,128)S(1)}, u32[]{:S(2)}, u32[]{:S(2)}) collective-permute-start(f32[32,128]{1,0:T(8,128)S(1)} %get-tuple-element.88), channel_id=1, source_target_pairs={{0,2},{1,3},{2,0},{3,1},{4,6},{5,7},{6,4},{7,5},{8,10},{9,11},{10,... | collective-permute-start | bytes 49160 | tf_op jit(solution)/shard_map/ppermute | solution.py:43
  109.4 3.2 %collective-permute-start.24 = (f32[32,128]{1,0:T(8,128)S(1)}, f32[32,128]{1,0:T(8,128)S(1)}, u32[]{:S(2)}, u32[]{:S(2)}) collective-permute-start(f32[32,128]{1,0:T(8,128)S(1)} %get-tuple-element.89), channel_id=1, source_target_pairs={{0,3},{1,2},{2,1},{3,0},{4,7},{5,6},{6,5},{7,4},{8,11},{9,10},{10,... | collective-permute-start | bytes 49160 | tf_op jit(solution)/shard_map/ppermute | solution.py:43
  109.4 3.2 %collective-permute-start.22 = (f32[32,128]{1,0:T(8,128)S(1)}, f32[32,128]{1,0:T(8,128)S(1)}, u32[]{:S(2)}, u32[]{:S(2)}) collective-permute-start(f32[32,128]{1,0:T(8,128)S(1)} %get-tuple-element.87), channel_id=1, source_target_pairs={{0,1},{1,0},{2,3},{3,2},{4,5},{5,4},{6,7},{7,6},{8,9},{9,8},{10,11... | collective-permute-start | bytes 49160 | tf_op jit(solution)/shard_map/ppermute | solution.py:43
  112.6 4.8 %collective-permute-start.26 = (f32[32,128]{1,0:T(8,128)S(1)}, f32[32,128]{1,0:T(8,128)S(1)}, u32[]{:S(2)}, u32[]{:S(2)}) collective-permute-start(f32[32,128]{1,0:T(8,128)S(1)} %add_add_fusion.1), channel_id=1, source_target_pairs={{0,8},{4,12},{8,0},{12,4},{1,9},{5,13},{9,1},{13,5},{2,10},{6,14},... | collective-permute-start | bytes 49160 | tf_op jit(solution)/shard_map/ppermute | solution.py:43
  115.1 5.5 %collective-permute-start.27 = (f32[32,128]{1,0:T(8,128)S(1)}, f32[32,128]{1,0:T(8,128)S(1)}, u32[]{:S(2)}, u32[]{:S(2)}) collective-permute-start(f32[32,128]{1,0:T(8,128)S(1)} %add_add_fusion.1), channel_id=1, source_target_pairs={{0,12},{4,8},{8,4},{12,0},{1,13},{5,9},{9,5},{13,1},{2,14},{6,10},... | collective-permute-start | bytes 49160 | tf_op jit(solution)/shard_map/ppermute | solution.py:43
  115.1 5.5 %collective-permute-start.25 = (f32[32,128]{1,0:T(8,128)S(1)}, f32[32,128]{1,0:T(8,128)S(1)}, u32[]{:S(2)}, u32[]{:S(2)}) collective-permute-start(f32[32,128]{1,0:T(8,128)S(1)} %add_add_fusion.1), channel_id=1, source_target_pairs={{0,4},{4,0},{8,12},{12,8},{1,5},{5,1},{9,13},{13,9},{2,6},{6,2},{1... | collective-permute-start | bytes 49160 | tf_op jit(solution)/shard_map/ppermute | solution.py:43

commit v11 on v10

--- a/solution.py
+++ b/solution.py
@@ -181,27 +181,44 @@
     )(place, *pieces)
 
 
-def orbital_first_kernel(n_dom, place, *refs):
-    *pieces, out = refs
+def orbital_first_kernel(n_dom, which, place, *refs):
+    pieces, (out, laid_out, sems) = refs[: len(which)], refs[-3:]
     cells = out.shape[1]
-    for k, piece in enumerate(pieces):
-        chunk, m = divmod(k, n_dom)
+    copies = []
+    for k, (chunk, m) in enumerate(which):
+        for t in range(TOGETHER):
+            laid_out[k * TOGETHER + t] = pieces[k][pl.ds(t, cells, stride=TOGETHER), :]
         start = (chunk * n_dom + (place[ME] ^ m)) * TOGETHER
-        for t in range(TOGETHER):
-            out[start + t] = piece[pl.ds(t, cells, stride=TOGETHER), :]
-
-
-def orbital_first(place, n_dom, pieces):
+        copies.append(
+            pltpu.make_async_copy(
+                laid_out.at[pl.ds(k * TOGETHER, TOGETHER)],
+                out.at[pl.ds(start, TOGETHER)],
+                sems.at[k],
+            )
+        )
+        copies[-1].start()
+    for copy in copies:
+        copy.wait()
+
+
+def orbital_first(place, n_dom, orbitals, pieces, which, onto=None):
     rows, lanes = pieces[0].shape
-    shape = (len(pieces) * TOGETHER, rows // TOGETHER, lanes)
+    cells = rows // TOGETHER
+    hbm = pl.BlockSpec(memory_space=pltpu.HBM)
+    given = [] if onto is None else [onto]
     return pl.pallas_call(
-        functools.partial(orbital_first_kernel, n_dom),
-        out_shape=jax.ShapeDtypeStruct(shape, jnp.float32),
-        in_specs=[SMEM] + [VMEM] * len(pieces),
-        out_specs=VMEM,
+        functools.partial(orbital_first_kernel, n_dom, which),
+        out_shape=jax.ShapeDtypeStruct((orbitals, cells, lanes), jnp.float32),
+        in_specs=[SMEM] + [VMEM] * len(pieces) + [hbm] * len(given),
+        out_specs=hbm,
+        input_output_aliases={len(pieces) + 1: 0} if given else {},
+        scratch_shapes=[
+            pltpu.VMEM((len(pieces) * TOGETHER, cells, lanes), jnp.float32),
+            pltpu.SemaphoreType.DMA((len(pieces),)),
+        ],
         compiler_params=params(8),
         name="orbital_first",
-    )(place, *pieces)
+    )(place, *pieces, *given)
 
 
 def projector_kernel(n_band, n_sub, place, offsets_ref, coefs_ref, high_out, low_out):
@@ -277,11 +294,18 @@
     rows, orbitals = proj_out.shape
     cells, _, lanes = arrays[0].shape
     block = 12
+    swap = (place[ME] & 2) != 0
 
     def parts(start):
         highs, lows = [], []
-        for at, first, width in spots:
-            high, low = split_bf16(arrays[at][pl.ds(start, block), first : first + width])
+        for spot in spots:
+            tiles = [
+                arrays[at][pl.ds(start, block), first : first + width] for at, first, width in spot
+            ]
+            if len(tiles) == 2:
+                near, far = tiles
+                tiles = [jnp.where(swap, far, near), jnp.where(swap, near, far)]
+            high, low = split_bf16(jnp.concatenate(tiles, axis=1))
             highs.append(jnp.concatenate([high[k] for k in range(block)], axis=1))
             lows.append(jnp.concatenate([low[k] for k in range(block)], axis=1))
         return jnp.concatenate(highs, axis=0), jnp.concatenate(lows, axis=0)
@@ -318,7 +342,7 @@
 
 
 def products(n_sub, first_row, rows, n_blocks, with_grid, place, projectors, arrays, spots):
-    orbitals = sum(width for _, _, width in spots)
+    orbitals = sum(width for spot in spots for _, _, width in spot)
     grid = [jax.ShapeDtypeStruct((orbitals, orbitals), jnp.float32)] if with_grid else []
     block = jax.ShapeDtypeStruct((rows // n_blocks, orbitals), jnp.float32)
     flops = 12 * rows * orbitals * projectors[0].shape[1]
@@ -482,8 +506,32 @@
 
     if n_dom in (2, 4) and orbitals % (n_dom * TOGETHER) == 0 and planes * n_dom % 2 == 0:
         chunks, projectors = whole_columns(panel, potential, place, me, build)
-        filtered = orbital_first(place, n_dom, [piece for pieces in chunks for piece in pieces])
-        parts = [cell_first(place, n_band, pieces) for pieces in chunks]
+        sooner = place
+        which = [(c, m) for c in range(len(chunks)) for m in range(n_dom)]
+        pieces = [chunks[c][m] for c, m in which]
+        n_late = 2 if n_dom == 4 else 0
+        first = len(pieces) - n_late
+        filtered = orbital_first(place, n_dom, orbitals, pieces[:first], which[:first])
+        early, place = lax.optimization_barrier((filtered, place))
+        if n_late:
+            filtered = orbital_first(
+                place, n_dom, orbitals, pieces[first:], which[first:], early
+            )
+        parts = [cell_first(sooner, n_band, pieces) for pieces in chunks[:-1]]
+        tiles = [[c] for c in range(len(chunks))]
+        last = [chunks[-1]]
+        if n_dom == 4:
+            last = [chunks[-1][:2], chunks[-1][2:]]
+            tiles[-1].append(len(chunks))
+        if len(parts) and len(last) == 2:
+            parts[-1], last[0] = lax.optimization_barrier((parts[-1], last[0]))
+        parts.append(cell_first(place, n_band, last[0]))
+        if len(last) == 2:
+            near = parts[-1]
+            crossed = [swapped(x, "band", n_band, m) if m else x for m, x in enumerate(near)]
+            crossed, last[1] = lax.optimization_barrier((crossed, last[1]))
+            parts.append(cell_first(place, n_band, last[1]))
+            parts[-2] = crossed
     else:
         projectors = build(place)
         filtered = plane_by_plane(panel, potential)
@@ -494,29 +542,32 @@
                 for m in range(n_band)
             ]
         ]
+        tiles = [[0]]
     filtered = filtered.reshape(panel.shape)
-    chunks = len(parts)
-    arrays = [x for by_band in parts for x in by_band[:1]]
-    arrays += [
-        swapped(by_band[m], "band", n_band, m) for by_band in parts for m in range(1, n_band)
-    ]
-    arrays[chunks], filtered = lax.optimization_barrier((arrays[chunks], filtered))
-    pieces = [jnp.concatenate(arrays[:chunks], axis=1)] + arrays[chunks:]
+    own = [part[0] for part in parts]
+    pieces = []
+    for at, part in enumerate(parts):
+        crossed = len(tiles[-1]) == 2 and at == len(parts) - 2
+        for m in range(1, n_band):
+            pieces.append(part[m] if crossed else swapped(part[m], "band", n_band, m))
+    arrays = own + pieces
+    pieces = [jnp.concatenate(own, axis=1)] + pieces
     arrays += [swapped(x, "sub", n_sub, k) for k in range(1, n_sub) for x in pieces]
-    width = arrays[0].shape[1]
+    starts = [sum(x.shape[1] for x in own[:at]) for at in range(len(own))]
     spots = []
     for m in range(n_band):
         for k in range(n_sub):
-            for c in range(chunks):
-                at = chunks + c * (n_band - 1) + m - 1 if m else c
-                if k == 0:
-                    spots.append((at, 0, width))
-                else:
-                    base = chunks * n_band + (k - 1) * len(pieces)
+            for tile in tiles:
+                spot = []
+                for at in tile:
+                    index, first = at, 0
                     if m:
-                        spots.append((base + 1 + at - chunks, 0, width))
-                    else:
-                        spots.append((base, c * width, width))
+                        index = len(own) + at * (n_band - 1) + m - 1 + k * len(pieces)
+                    elif k:
+                        index = len(own) * n_band + (k - 1) * len(pieces)
+                        first = starts[at]
+                    spot.append((index, first, own[at].shape[1]))
+                spots.append(spot)
 
     rows = own_atoms * channels
     n_sent = 3 * n_band - 1

time: 121 us -> 119 us (0.983)
  waiting for transfers between devices: 43.2 us -> 38.5 us
  Pallas kernels: 37.1 us -> 38.9 us
    ppermute x23 -> x25, waiting for transfers between devices: 40.6 us -> 36.9 us  [swapped(): return lax.ppermute(x, axes, [(i, i ^ by) for i in range(size)])]
    pallas_call x1 -> x2, Pallas kernels: 1.79 us -> 2.92 us  [orbital_first(): pl.pallas_call(functools.partial(orbital_first_kernel, n_dom, which), out...]
    ppermute x23 -> x25, starting transfers between devices: 26.5 us -> 27.1 us  [swapped(): return lax.ppermute(x, axes, [(i, i ^ by) for i in range(size)])]
  transfers between devices with their start and end apart: 28 -> 30, of which waited for: 11 -> 10; matrix products, arithmetic and copies ran while one was open for 1% -> 1% of each run, Pallas kernels for 26% -> 28%
where the time goes in v11:
time: 119 us
  Pallas kernels  38.9 us (33%)
  waiting for transfers between devices  38.5 us (32%)
  starting transfers between devices  35.7 us (30%)
  local copies, waits for them, and re-layouts  2.83 us (2%)
  other arithmetic  1.72 us (1%)
    ppermute x25, waiting for transfers between devices, swapped(): return lax.ppermute(x, axes, [(i, i ^ by) for i in range(size)])  36.9 us
    ppermute x25, starting transfers between devices, swapped(): return lax.ppermute(x, axes, [(i, i ^ by) for i in range(size)])  27.1 us
    pallas_call x2, Pallas kernels, filter_orbitals(): pl.pallas_call(functools.partial(filter_kernel, n_dom, planes, rows, star...  13.2 us
    pallas_call x1, Pallas kernels, build_projectors(): pl.pallas_call(functools.partial(projector_kernel, n_band, n_sub), out_sh...  11.5 us
    ppermute x5, starting transfers between devices, on_device(): sums.append(lax.ppermute(x, ('dom', 'band'), pairs))  8.66 us
    pallas_call x2, Pallas kernels, products(): pl.pallas_call(functools.partial(product_kernel, spots, n_sub, first_row,...  8.16 us
    pallas_call x2, Pallas kernels, orbital_first(): pl.pallas_call(functools.partial(orbital_first_kernel, n_dom, which), out...  2.92 us
  transfers between devices with their start and end apart: 30, of which 10 were waited for; matrix products, arithmetic and copies ran while one was open for 1% of the time, Pallas kernels for 28%

profile of v11, /device:TPU:0, one launch (start us, length us, event | category | flops | bytes accessed | tf_op | source)
XLA Modules:
  0.0 118.5 jit_solution(12516984913864181479)
XLA Ops:
  0.6 0.0 copy-start
  0.7 2.3 %constant_dynamic-slice_fusion = (f32[384,128]{1,0:T(8,128)S(1)}, f32[384,128]{1,0:T(8,128)}, f32[384,128]{1,0:T(8,128)S(1)}, f32[384,128]{1,0:T(8,128)}, f32[38...) fusion(f32[3072,128]{1,0:T(8,128)} %bitcast.34, s32[]{:T(128)S(6)} %select_n.35, ...), kind=kLoop, calls=%fused_computation.9 | loop fusion | bytes 3145760 | tf_op jit(solution)/shard_map/dynamic_slice | solution.py:424
  3.1 4.1 %collective-permute-start = (f32[480,128]{1,0:T(8,128)S(1)}, f32[480,128]{1,0:T(8,128)S(1)}, u32[]{:S(2)}, u32[]{:S(2)}) collective-permute-start(f32[480,128]{1,0:T(8,128)S(1)} %get-tuple-element.119), channel_id=1, source_target_pairs={{0,8},{4,12},{8,0},{12,4},{1,9},{5,13},{9,1},{13,5},{2,10},{6,14},... | collective-permute-start | bytes 737288 | tf_op jit(solution)/shard_map/ppermute | solution.py:43
  7.2 0.8 pad_maximum_fusion.1
  8.0 1.6 %collective-permute-start.2 = (f32[864,128]{1,0:T(8,128)}, f32[864,128]{1,0:T(8,128)S(1)}, u32[]{:S(2)}, u32[]{:S(2)}) collective-permute-start(f32[864,128]{1,0:T(8,128)} %pad_maximum_fusion.1), channel_id=1, source_target_pairs={{0,4},{4,0},{8,12},{12,8},{1,5},{5,1},{9,13},{13,9},{2,6},{6,2},{1... | collective-permute-start | bytes 1327112 | tf_op jit(solution)/shard_map/ppermute | solution.py:43
  9.5 0.0 collective-permute-start.3
  9.6 0.1 constant_dynamic-slice_fusion.8
  9.6 0.1 copy.9
  9.7 0.1 broadcast_multiply_fusion
  9.9 9.4 %collective-permute-done.refs_3_ = f32[480,128]{1,0:T(8,128)S(1)} collective-permute-done((f32[480,128]{1,0:T(8,128)S(1)}, f32[480,128]{1,0:T(8,128)S(1)}, u32[]{:S(2)}, u32[]{:S(2)}) %collective-permute-start) | collective-permute-done | bytes 245792 | tf_op jit(solution)/shard_map/ppermute | solution.py:43
  19.3 9.9 %collective-permute-done.2.refs_2_ = f32[864,128]{1,0:T(8,128)S(1)} collective-permute-done((f32[864,128]{1,0:T(8,128)}, f32[864,128]{1,0:T(8,128)S(1)}, u32[]{:S(2)}, u32[]{:S(2)}) %collective-permute-start.2) | collective-permute-done | bytes 442400 | tf_op jit(solution)/shard_map/ppermute | solution.py:43
  29.2 0.5 collective-permute-start.7
  29.7 2.0 %collective-permute-start.8 = (f32[384,128]{1,0:T(8,128)S(1)}, f32[384,128]{1,0:T(8,128)S(1)}, u32[]{:S(2)}, u32[]{:S(2)}) collective-permute-start(f32[384,128]{1,0:T(8,128)S(1)} %get-tuple-element.69), channel_id=1, source_target_pairs={{0,12},{4,8},{8,4},{12,0},{1,13},{5,9},{9,5},{13,1},{2,14},{6,10},... | collective-permute-start | bytes 589832 | tf_op jit(solution)/shard_map/ppermute | solution.py:43
  31.7 0.1 pad_add_fusion.place
  31.8 0.3 mul.56.corr_ref
  32.1 0.0 collective-permute-done.3.refs_4_
  32.1 0.0 collective-permute-done.1.refs_0_
  32.1 6.8 %chebyshev.2 = (f32[3,128,128]{2,1,0:T(8,128)S(1)}, f32[3,128,128]{2,1,0:T(8,128)S(1)}, f32[3,128,128]{2,1,0:T(8,128)S(1)}, f32[3,128,128]{2,1,0:T(8,128)S(1)}, f32[6,32,8,128]{3,2,1,0:T(8,128)S(1)}) custom-call(s32[4]{0:T(128)S(1)} %pad_add_fusion.place, f32[96,128]{1,0:T(8,128)S(1)} %collective-permute-done.1.refs_0_, ...), custom_call_target="tpu_custom_call" | custom-call | flops 28311552 | bytes 1572864 | tf_op jit(solution)/shard_map/chebyshev/pallas_call | solution.py:132
  38.9 1.1 collective-permute-start.4
  39.9 1.4 %collective-permute-start.5 = (f32[3,128,128]{2,1,0:T(8,128)S(1)}, f32[3,128,128]{2,1,0:T(8,128)S(1)}, u32[]{:S(2)}, u32[]{:S(2)}) collective-permute-start(f32[3,128,128]{2,1,0:T(8,128)S(1)} %get-tuple-element.60), channel_id=1, source_target_pairs={{0,8},{4,12},{8,0},{12,4},{1,9},{5,13},{9,1},{13,5},{2,10},{6,14},... | collective-permute-start | bytes 589832 | tf_op jit(solution)/shard_map/ppermute | solution.py:43
  41.4 2.0 %collective-permute-start.6 = (f32[3,128,128]{2,1,0:T(8,128)S(1)}, f32[3,128,128]{2,1,0:T(8,128)S(1)}, u32[]{:S(2)}, u32[]{:S(2)}) collective-permute-start(f32[3,128,128]{2,1,0:T(8,128)S(1)} %get-tuple-element.61), channel_id=1, source_target_pairs={{0,12},{4,8},{8,4},{12,0},{1,13},{5,9},{9,5},{13,1},{2,14},{6,10},... | collective-permute-start | bytes 589832 | tf_op jit(solution)/shard_map/ppermute | solution.py:43
  43.3 11.5 %projectors.1 = (bf16[576,6144]{1,0:T(8,128)(2,1)S(1)}, bf16[576,6144]{1,0:T(8,128)(2,1)S(1)}) custom-call(s32[4]{0:T(128)S(1)} %pad_add_fusion.place, s32[3,48,128]{2,1,0:T(8,128)S(1)} %bitcast.32, f32[48,3,8,128]{3,2,1,0:T(8,128)S(1)} %copy-done.1), custom_call_target="tpu_custom_call" | custom-call | flops 1811939328 | bytes 28311552 | tf_op jit(solution)/shard_map/projectors/pallas_call | solution.py:275
  54.8 6.4 %chebyshev.3 = (f32[3,128,128]{2,1,0:T(8,128)S(1)}, f32[3,128,128]{2,1,0:T(8,128)S(1)}, f32[3,128,128]{2,1,0:T(8,128)S(1)}, f32[3,128,128]{2,1,0:T(8,128)S(1)}) custom-call(s32[4]{0:T(128)S(1)} %pad_add_fusion.place, f32[6,32,8,128]{3,2,1,0:T(8,128)S(1)} %get-tuple-element.66.refs_0_, f32[384,128]{1,0:T(8,128)S(1)} %get-tuple-element.112.refs_1_, ...), custom_call_target="tpu_custom_call" | custom-call | flops 28311552 | bytes 1572864 | tf_op jit(solution)/shard_map/chebyshev/pallas_call | solution.py:132
  61.3 0.4 collective-permute-start.9
  61.7 2.1 %collective-permute-start.10 = (f32[3,128,128]{2,1,0:T(8,128)S(1)}, f32[3,128,128]{2,1,0:T(8,128)S(1)}, u32[]{:S(2)}, u32[]{:S(2)}) collective-permute-start(f32[3,128,128]{2,1,0:T(8,128)S(1)} %get-tuple-element.73), channel_id=1, source_target_pairs={{0,8},{4,12},{8,0},{12,4},{1,9},{5,13},{9,1},{13,5},{2,10},{6,14},... | collective-permute-start | bytes 589832 | tf_op jit(solution)/shard_map/ppermute | solution.py:43
  63.8 2.0 %collective-permute-start.11 = (f32[3,128,128]{2,1,0:T(8,128)S(1)}, f32[3,128,128]{2,1,0:T(8,128)S(1)}, u32[]{:S(2)}, u32[]{:S(2)}) collective-permute-start(f32[3,128,128]{2,1,0:T(8,128)S(1)} %get-tuple-element.74), channel_id=1, source_target_pairs={{0,12},{4,8},{8,4},{12,0},{1,13},{5,9},{9,5},{13,1},{2,14},{6,10},... | collective-permute-start | bytes 589832 | tf_op jit(solution)/shard_map/ppermute | solution.py:43
  65.7 0.7 cell_first.3
  66.4 0.9 collective-permute-done.9
  67.3 1.6 %orbital_first.2.refs_2_ = f32[32,96,128]{2,1,0:T(8,128)} custom-call(s32[4]{0:T(128)S(1)} %pad_add_fusion.place, f32[384,128]{1,0:T(8,128)S(1)} %bitcast.21, f32[384,128]{1,0:T(8,128)S(1)} %bitcast.23, f32[384,128]{1,0:T(8,128)S(1)} %bitcast.25, f32[384,128]{1,0:T(8,128)S(1)} %bitcast.27, f32[384,128]{1,0:T(8,128)S(1)} %bitcast.16, f32[384,128]{1,0:T(8,128)S(1)} %bitcast.18), custom_call_target="tpu_custom_call" | custom-call | tf_op jit(solution)/shard_map/orbital_first/pallas_call | solution.py:209
  68.9 0.6 cell_first.4
  69.5 1.5 %collective-permute-start.12 = (f32[48,8,128]{2,1,0:T(8,128)S(1)}, f32[48,8,128]{2,1,0:T(8,128)S(1)}, u32[]{:S(2)}, u32[]{:S(2)}) collective-permute-start(f32[48,8,128]{2,1,0:T(8,128)S(1)} %get-tuple-element.84), channel_id=1, source_target_pairs={{0,2},{2,0},{1,3},{3,1},{4,6},{6,4},{5,7},{7,5},{8,10},{10,8},{9,1... | collective-permute-start | bytes 589832 | tf_op jit(solution)/shard_map/ppermute | solution.py:43
  71.0 0.5 collective-permute-start.13
  71.6 5.5 %collective-permute-done.10 = f32[3,128,128]{2,1,0:T(8,128)S(1)} collective-permute-done((f32[3,128,128]{2,1,0:T(8,128)S(1)}, f32[3,128,128]{2,1,0:T(8,128)S(1)}, u32[]{:S(2)}, u32[]{:S(2)}) %collective-permute-start.10) | collective-permute-done | bytes 196640 | tf_op jit(solution)/shard_map/ppermute | solution.py:43
  77.1 0.0 collective-permute-done.11
  77.1 0.6 cell_first.5
  77.7 0.1 pad_maximum_fusion
  77.8 0.1 collective-permute-start.15
  77.9 1.6 %collective-permute-start.14 = (f32[48,8,128]{2,1,0:T(8,128)S(1)}, f32[48,8,128]{2,1,0:T(8,128)S(1)}, u32[]{:S(2)}, u32[]{:S(2)}) collective-permute-start(f32[48,8,128]{2,1,0:T(8,128)S(1)} %get-tuple-element.91), channel_id=1, source_target_pairs={{0,2},{2,0},{1,3},{3,1},{4,6},{6,4},{5,7},{7,5},{8,10},{10,8},{9,1... | collective-permute-start | bytes 589832 | tf_op jit(solution)/shard_map/ppermute | solution.py:43
  79.4 0.1 collective-permute-done.13.refs_3_
  79.5 0.1 collective-permute-start.16
  79.6 0.4 collective-permute-start.17
  80.0 5.2 %collective-permute-done.14.refs_5_ = f32[48,8,128]{2,1,0:T(8,128)S(1)} collective-permute-done((f32[48,8,128]{2,1,0:T(8,128)S(1)}, f32[48,8,128]{2,1,0:T(8,128)S(1)}, u32[]{:S(2)}, u32[]{:S(2)}) %collective-permute-start.14) | collective-permute-done | bytes 196640 | tf_op jit(solution)/shard_map/ppermute | solution.py:43
  85.2 0.0 collective-permute-done.17.refs_8_
  85.2 1.4 %collective-permute-done.18.refs_9_ = f32[48,8,128]{2,1,0:T(8,128)S(1)} collective-permute-done((f32[48,8,128]{2,1,0:T(8,128)S(1)}, f32[48,8,128]{2,1,0:T(8,128)S(1)}, u32[]{:S(2)}, u32[]{:S(2)}) %collective-permute-start.18) | collective-permute-done | bytes 196640 | tf_op jit(solution)/shard_map/ppermute | solution.py:43
  86.6 0.0 collective-permute-done.16.refs_7_
  86.6 0.0 collective-permute-done.15.refs_6_
  86.6 4.5 %products.2 = (f32[96,128]{1,0:T(8,128)S(1)}, f32[96,128]{1,0:T(8,128)S(1)}, f32[96,128]{1,0:T(8,128)S(1)}, f32[96,128]{1,0:T(8,128)S(1)}, f32[96,128]{1,0:T(8,128)S(1)}) custom-call(s32[4]{0:T(128)S(1)} %pad_add_fusion.place, bf16[576,6144]{1,0:T(8,128)(2,1)S(1)} %get-tuple-element.76.w_high, bf16[576,6144]{1,0:T(8,128)(2,1)S(1)} %get-tuple-element.77.w_low, ...), custom_call_target="tpu_custom_call" | custom-call | flops 4529848320 | bytes 11796480 | tf_op jit(solution)/shard_map/products/pallas_call | solution.py:349
  91.1 4.2 %collective-permute-start.19 = (f32[96,128]{1,0:T(8,128)S(1)}, f32[96,128]{1,0:T(8,128)S(1)}, u32[]{:S(2)}, u32[]{:S(2)}) collective-permute-start(f32[96,128]{1,0:T(8,128)S(1)} %get-tuple-element.101), channel_id=1, source_target_pairs={{0,12},{2,14},{4,0},{6,2},{8,4},{10,6},{12,8},{14,10},{1,13},{3,15... | collective-permute-start | bytes 147464 | tf_op jit(solution)/shard_map/ppermute | solution.py:591
  95.4 2.2 %collective-permute-start.20 = (f32[96,128]{1,0:T(8,128)S(1)}, f32[96,128]{1,0:T(8,128)S(1)}, u32[]{:S(2)}, u32[]{:S(2)}) collective-permute-start(f32[96,128]{1,0:T(8,128)S(1)} %get-tuple-element.102), channel_id=1, source_target_pairs={{0,14},{2,12},{4,2},{6,0},{8,6},{10,4},{12,10},{14,8},{1,15},{3,13... | collective-permute-start | bytes 147464 | tf_op jit(solution)/shard_map/ppermute | solution.py:591
  97.5 0.8 collective-permute-start.21
  98.3 0.0 collective-permute-start.22
  98.3 1.5 %collective-permute-start.23 = (f32[96,128]{1,0:T(8,128)S(1)}, f32[96,128]{1,0:T(8,128)S(1)}, u32[]{:S(2)}, u32[]{:S(2)}) collective-permute-start(f32[96,128]{1,0:T(8,128)S(1)} %get-tuple-element.105), channel_id=1, source_target_pairs={{0,2},{2,0},{4,6},{6,4},{8,10},{10,8},{12,14},{14,12},{1,3},{3,1},... | collective-permute-start | bytes 147464 | tf_op jit(solution)/shard_map/ppermute | solution.py:591
  99.8 3.7 %products.3 = (f32[128,128]{1,0:T(8,128)S(1)}, f32[96,128]{1,0:T(8,128)S(1)}) custom-call(s32[4]{0:T(128)S(1)} %pad_add_fusion.place, bf16[576,6144]{1,0:T(8,128)(2,1)S(1)} %get-tuple-element.76.w_high, bf16[576,6144]{1,0:T(8,128)(2,1)S(1)} %get-tuple-element.77.w_low, f32[48,16,128]{2,1,0:T(8,128)S(1)} %get-tuple-element.80.refs_0_, ...), custom_call_target="tpu_custom_call" | custom-call | flops 905969664 | bytes 2359296 | tf_op jit(solution)/shard_map/products/pallas_call | solution.py:349
  103.5 1.6 %collective-permute-done.22.refs_3_ = f32[96,128]{1,0:T(8,128)S(1)} collective-permute-done((f32[96,128]{1,0:T(8,128)S(1)}, f32[96,128]{1,0:T(8,128)S(1)}, u32[]{:S(2)}, u32[]{:S(2)}) %collective-permute-start.22) | collective-permute-done | bytes 49184 | tf_op jit(solution)/shard_map/ppermute | solution.py:591
  105.1 1.2 %gram_share.1 = (f32[32,128]{1,0:T(8,128)S(1)}, f32[32,128]{1,0:T(8,128)S(1)}, f32[32,128]{1,0:T(8,128)S(1)}, f32[32,128]{1,0:T(8,128)S(1)}) custom-call(s32[4]{0:T(128)S(1)} %pad_add_fusion.place, f32[96,96]{1,0:T(8,128)S(1)} %mul.56.corr_ref, f32[128,128]{1,0:T(8,128)S(1)} %get-tuple-element.99.grid_ref, f32[96,128]{1,0:T(8,128)S(1)} %get-tuple-element.100.proj_ref, ...), custom_call_target="tpu_custom_call" | custom-call | tf_op jit(solution)/shard_map/gram_share/pallas_call | solution.py:398
  106.3 0.6 collective-permute-start.25
  106.9 1.6 %collective-permute-start.24 = (f32[32,128]{1,0:T(8,128)S(1)}, f32[32,128]{1,0:T(8,128)S(1)}, u32[]{:S(2)}, u32[]{:S(2)}) collective-permute-start(f32[32,128]{1,0:T(8,128)S(1)} %get-tuple-element.107), channel_id=1, source_target_pairs={{0,1},{1,0},{2,3},{3,2},{4,5},{5,4},{6,7},{7,6},{8,9},{9,8},{10,11... | collective-permute-start | bytes 49160 | tf_op jit(solution)/shard_map/ppermute | solution.py:43
  108.5 1.7 %collective-permute-done.25 = f32[32,128]{1,0:T(8,128)S(1)} collective-permute-done((f32[32,128]{1,0:T(8,128)S(1)}, f32[32,128]{1,0:T(8,128)S(1)}, u32[]{:S(2)}, u32[]{:S(2)}) %collective-permute-start.25) | collective-permute-done | bytes 16416 | tf_op jit(solution)/shard_map/ppermute | solution.py:43
  110.3 2.1 %collective-permute-start.28 = (f32[32,128]{1,0:T(8,128)S(1)}, f32[32,128]{1,0:T(8,128)S(1)}, u32[]{:S(2)}, u32[]{:S(2)}) collective-permute-start(f32[32,128]{1,0:T(8,128)S(1)} %add_add_fusion.1), channel_id=1, source_target_pairs={{0,8},{4,12},{8,0},{12,4},{1,9},{5,13},{9,1},{13,5},{2,10},{6,14},... | collective-permute-start | bytes 49160 | tf_op jit(solution)/shard_map/ppermute | solution.py:43
  112.4 0.3 collective-permute-start.29
  112.7 1.2 collective-permute-start.27
  113.8 1.3 %orbital_first.3 = f32[32,96,128]{2,1,0:T(8,128)} custom-call(s32[4]{0:T(128)S(1)} %pad_add_fusion.place, f32[384,128]{1,0:T(8,128)S(1)} %bitcast.29, f32[384,128]{1,0:T(8,128)S(1)} %bitcast.31, f32[32,96,128]{2,1,0:T(8,128)} %orbital_first.2.refs_2_), custom_call_target="tpu_custom_call", output_to_operand_aliasing={{}: (3, {})} | custom-call | tf_op jit(solution)/shard_map/orbital_first/pallas_call | solution.py:209
  115.2 2.7 %collective-permute-done.29 = f32[32,128]{1,0:T(8,128)S(1)} collective-permute-done((f32[32,128]{1,0:T(8,128)S(1)}, f32[32,128]{1,0:T(8,128)S(1)}, u32[]{:S(2)}, u32[]{:S(2)}) %collective-permute-start.29) | collective-permute-done | bytes 16416 | tf_op jit(solution)/shard_map/ppermute | solution.py:43
  117.9 0.6 add_add_fusion
  (28 shorter events, 0.1 us)
Async XLA Ops:
  0.6 8.9 %copy-start = (f32[48,8,8]{0,2,1:T(8,128)S(1)}, f32[48,8,8]{0,2,1:T(8,128)}, u32[]{:S(2)}) copy-start(f32[48,8,8]{0,2,1:T(8,128)} %param.9) | copy-start | bytes 36868
  0.7 2.3 %copy-start.3 = (f32[3,32,128]{2,1,0:T(8,128)S(1)}, f32[3,32,128]{2,1,0:T(8,128)}, u32[]{:S(2)}) copy-start(f32[3,32,128]{2,1,0:T(8,128)} %param.6) | copy-start | bytes 147460
  3.1 16.2 %collective-permute-start = (f32[480,128]{1,0:T(8,128)S(1)}, f32[480,128]{1,0:T(8,128)S(1)}, u32[]{:S(2)}, u32[]{:S(2)}) collective-permute-start(f32[480,128]{1,0:T(8,128)S(1)} %get-tuple-element.119), channel_id=1, source_target_pairs={{0,8},{4,12},{8,0},{12,4},{1,9},{5,13},{9,1},{13,5},{2,10},{6,14},... | collective-permute-start | bytes 737288 | tf_op jit(solution)/shard_map/ppermute | solution.py:43
  8.0 21.3 %collective-permute-start.2 = (f32[864,128]{1,0:T(8,128)}, f32[864,128]{1,0:T(8,128)S(1)}, u32[]{:S(2)}, u32[]{:S(2)}) collective-permute-start(f32[864,128]{1,0:T(8,128)} %pad_maximum_fusion.1), channel_id=1, source_target_pairs={{0,4},{4,0},{8,12},{12,8},{1,5},{5,1},{9,13},{13,9},{2,6},{6,2},{1... | collective-permute-start | bytes 1327112 | tf_op jit(solution)/shard_map/ppermute | solution.py:43
  9.5 22.5 %collective-permute-start.3 = (f32[384,128]{1,0:T(8,128)}, f32[384,128]{1,0:T(8,128)S(1)}, u32[]{:S(2)}, u32[]{:S(2)}) collective-permute-start(f32[384,128]{1,0:T(8,128)} %get-tuple-element.113), channel_id=1, source_target_pairs={{0,12},{4,8},{8,4},{12,0},{1,13},{5,9},{9,5},{13,1},{2,14},{6,10},... | collective-permute-start | bytes 589832 | tf_op jit(solution)/shard_map/ppermute | solution.py:43
  9.5 33.8 %copy-start.1 = (f32[48,3,8,128]{3,2,1,0:T(8,128)S(1)}, f32[48,3,8,128]{3,2,1,0:T(8,128)}, u32[]{:S(2)}) copy-start(f32[48,3,8,128]{3,2,1,0:T(8,128)} %coefs_ref.1) | copy-start | bytes 1769476
  9.5 33.8 %copy-start.2 = (s32[48,3,128]{2,0,1:T(8,128)S(1)}, s32[48,3,128]{2,0,1:T(8,128)}, u32[]{:S(2)}) copy-start(s32[48,3,128]{2,0,1:T(8,128)} %param.7) | copy-start | bytes 221188
  19.3 12.8 %collective-permute-start.1 = (f32[96,128]{1,0:T(8,128)S(1)}, f32[96,128]{1,0:T(8,128)S(1)}, u32[]{:S(2)}, u32[]{:S(2)}) collective-permute-start(f32[96,128]{1,0:T(8,128)S(1)} %slice.4), channel_id=1, source_target_pairs={{0,4},{4,0},{8,12},{12,8},{1,5},{5,1},{9,13},{13,9},{2,6},{6,2},{1... | collective-permute-start | bytes 147464 | tf_op jit(solution)/shard_map/ppermute | solution.py:43
  29.2 25.6 %collective-permute-start.7 = (f32[384,128]{1,0:T(8,128)}, f32[384,128]{1,0:T(8,128)S(1)}, u32[]{:S(2)}, u32[]{:S(2)}) collective-permute-start(f32[384,128]{1,0:T(8,128)} %get-tuple-element.68), channel_id=1, source_target_pairs={{0,8},{4,12},{8,0},{12,4},{1,9},{5,13},{9,1},{13,5},{2,10},{6,14},... | collective-permute-start | bytes 589832 | tf_op jit(solution)/shard_map/ppermute | solution.py:43
  29.7 25.1 %collective-permute-start.8 = (f32[384,128]{1,0:T(8,128)S(1)}, f32[384,128]{1,0:T(8,128)S(1)}, u32[]{:S(2)}, u32[]{:S(2)}) collective-permute-start(f32[384,128]{1,0:T(8,128)S(1)} %get-tuple-element.69), channel_id=1, source_target_pairs={{0,12},{4,8},{8,4},{12,0},{1,13},{5,9},{9,5},{13,1},{2,14},{6,10},... | collective-permute-start | bytes 589832 | tf_op jit(solution)/shard_map/ppermute | solution.py:43
  38.9 24.9 %collective-permute-start.4 = (f32[3,128,128]{2,1,0:T(8,128)S(1)}, f32[3,128,128]{2,1,0:T(8,128)S(1)}, u32[]{:S(2)}, u32[]{:S(2)}) collective-permute-start(f32[3,128,128]{2,1,0:T(8,128)S(1)} %get-tuple-element.59), channel_id=1, source_target_pairs={{0,4},{4,0},{8,12},{12,8},{1,5},{5,1},{9,13},{13,9},{2,6},{6,2},{1... | collective-permute-start | bytes 589832 | tf_op jit(solution)/shard_map/ppermute | solution.py:43
  39.9 25.8 %collective-permute-start.5 = (f32[3,128,128]{2,1,0:T(8,128)S(1)}, f32[3,128,128]{2,1,0:T(8,128)S(1)}, u32[]{:S(2)}, u32[]{:S(2)}) collective-permute-start(f32[3,128,128]{2,1,0:T(8,128)S(1)} %get-tuple-element.60), channel_id=1, source_target_pairs={{0,8},{4,12},{8,0},{12,4},{1,9},{5,13},{9,1},{13,5},{2,10},{6,14},... | collective-permute-start | bytes 589832 | tf_op jit(solution)/shard_map/ppermute | solution.py:43
  41.4 24.4 %collective-permute-start.6 = (f32[3,128,128]{2,1,0:T(8,128)S(1)}, f32[3,128,128]{2,1,0:T(8,128)S(1)}, u32[]{:S(2)}, u32[]{:S(2)}) collective-permute-start(f32[3,128,128]{2,1,0:T(8,128)S(1)} %get-tuple-element.61), channel_id=1, source_target_pairs={{0,12},{4,8},{8,4},{12,0},{1,13},{5,9},{9,5},{13,1},{2,14},{6,10},... | collective-permute-start | bytes 589832 | tf_op jit(solution)/shard_map/ppermute | solution.py:43
  61.3 6.0 %collective-permute-start.9 = (f32[3,128,128]{2,1,0:T(8,128)S(1)}, f32[3,128,128]{2,1,0:T(8,128)S(1)}, u32[]{:S(2)}, u32[]{:S(2)}) collective-permute-start(f32[3,128,128]{2,1,0:T(8,128)S(1)} %get-tuple-element.71), channel_id=1, source_target_pairs={{0,4},{4,0},{8,12},{12,8},{1,5},{5,1},{9,13},{13,9},{2,6},{6,2},{1... | collective-permute-start | bytes 589832 | tf_op jit(solution)/shard_map/ppermute | solution.py:43
  61.7 15.4 %collective-permute-start.10 = (f32[3,128,128]{2,1,0:T(8,128)S(1)}, f32[3,128,128]{2,1,0:T(8,128)S(1)}, u32[]{:S(2)}, u32[]{:S(2)}) collective-permute-start(f32[3,128,128]{2,1,0:T(8,128)S(1)} %get-tuple-element.73), channel_id=1, source_target_pairs={{0,8},{4,12},{8,0},{12,4},{1,9},{5,13},{9,1},{13,5},{2,10},{6,14},... | collective-permute-start | bytes 589832 | tf_op jit(solution)/shard_map/ppermute | solution.py:43
  63.8 13.3 %collective-permute-start.11 = (f32[3,128,128]{2,1,0:T(8,128)S(1)}, f32[3,128,128]{2,1,0:T(8,128)S(1)}, u32[]{:S(2)}, u32[]{:S(2)}) collective-permute-start(f32[3,128,128]{2,1,0:T(8,128)S(1)} %get-tuple-element.74), channel_id=1, source_target_pairs={{0,12},{4,8},{8,4},{12,0},{1,13},{5,9},{9,5},{13,1},{2,14},{6,10},... | collective-permute-start | bytes 589832 | tf_op jit(solution)/shard_map/ppermute | solution.py:43
  69.5 7.6 %collective-permute-start.12 = (f32[48,8,128]{2,1,0:T(8,128)S(1)}, f32[48,8,128]{2,1,0:T(8,128)S(1)}, u32[]{:S(2)}, u32[]{:S(2)}) collective-permute-start(f32[48,8,128]{2,1,0:T(8,128)S(1)} %get-tuple-element.84), channel_id=1, source_target_pairs={{0,2},{2,0},{1,3},{3,1},{4,6},{6,4},{5,7},{7,5},{8,10},{10,8},{9,1... | collective-permute-start | bytes 589832 | tf_op jit(solution)/shard_map/ppermute | solution.py:43
  71.0 8.5 %collective-permute-start.13 = (f32[48,16,128]{2,1,0:T(8,128)S(1)}, f32[48,16,128]{2,1,0:T(8,128)S(1)}, u32[]{:S(2)}, u32[]{:S(2)}) collective-permute-start(f32[48,16,128]{2,1,0:T(8,128)S(1)} %get-tuple-element.89), channel_id=1, source_target_pairs={{0,2},{2,0},{1,3},{3,1},{4,6},{6,4},{5,7},{7,5},{8,10},{10,8},{9,1... | collective-permute-start | bytes 1179656 | tf_op jit(solution)/shard_map/ppermute | solution.py:43
  77.8 8.8 %collective-permute-start.15 = (f32[48,32,128]{2,1,0:T(8,128)S(1)}, f32[48,32,128]{2,1,0:T(8,128)S(1)}, u32[]{:S(2)}, u32[]{:S(2)}) collective-permute-start(f32[48,32,128]{2,1,0:T(8,128)S(1)} %pad_maximum_fusion), channel_id=1, source_target_pairs={{0,1},{1,0},{2,3},{3,2},{4,5},{5,4},{6,7},{7,6},{8,9},{9,8},{10,11... | collective-permute-start | bytes 2359304 | tf_op jit(solution)/shard_map/ppermute | solution.py:43
  77.9 7.3 %collective-permute-start.14 = (f32[48,8,128]{2,1,0:T(8,128)S(1)}, f32[48,8,128]{2,1,0:T(8,128)S(1)}, u32[]{:S(2)}, u32[]{:S(2)}) collective-permute-start(f32[48,8,128]{2,1,0:T(8,128)S(1)} %get-tuple-element.91), channel_id=1, source_target_pairs={{0,2},{2,0},{1,3},{3,1},{4,6},{6,4},{5,7},{7,5},{8,10},{10,8},{9,1... | collective-permute-start | bytes 589832 | tf_op jit(solution)/shard_map/ppermute | solution.py:43
  79.5 7.1 %collective-permute-start.16 = (f32[48,16,128]{2,1,0:T(8,128)S(1)}, f32[48,16,128]{2,1,0:T(8,128)S(1)}, u32[]{:S(2)}, u32[]{:S(2)}) collective-permute-start(f32[48,16,128]{2,1,0:T(8,128)S(1)} %collective-permute-done.13.refs_3_), channel_id=1, source_target_pairs={{0,1},{1,0},{2,3},{3,2},{4,5},{5,4},{6,7},{7,6},{8,9},{9,8},{10,11... | collective-permute-start | bytes 1179656 | tf_op jit(solution)/shard_map/ppermute | solution.py:43
  79.6 5.6 %collective-permute-start.17 = (f32[48,8,128]{2,1,0:T(8,128)S(1)}, f32[48,8,128]{2,1,0:T(8,128)S(1)}, u32[]{:S(2)}, u32[]{:S(2)}) collective-permute-start(f32[48,8,128]{2,1,0:T(8,128)S(1)} %collective-permute-done.12.refs_4_), channel_id=1, source_target_pairs={{0,1},{1,0},{2,3},{3,2},{4,5},{5,4},{6,7},{7,6},{8,9},{9,8},{10,11... | collective-permute-start | bytes 589832 | tf_op jit(solution)/shard_map/ppermute | solution.py:43
  85.2 1.4 %collective-permute-start.18 = (f32[48,8,128]{2,1,0:T(8,128)S(1)}, f32[48,8,128]{2,1,0:T(8,128)S(1)}, u32[]{:S(2)}, u32[]{:S(2)}) collective-permute-start(f32[48,8,128]{2,1,0:T(8,128)S(1)} %collective-permute-done.14.refs_5_), channel_id=1, source_target_pairs={{0,1},{1,0},{2,3},{3,2},{4,5},{5,4},{6,7},{7,6},{8,9},{9,8},{10,11... | collective-permute-start | bytes 589832 | tf_op jit(solution)/shard_map/ppermute | solution.py:43
  91.1 12.4 %collective-permute-start.19 = (f32[96,128]{1,0:T(8,128)S(1)}, f32[96,128]{1,0:T(8,128)S(1)}, u32[]{:S(2)}, u32[]{:S(2)}) collective-permute-start(f32[96,128]{1,0:T(8,128)S(1)} %get-tuple-element.101), channel_id=1, source_target_pairs={{0,12},{2,14},{4,0},{6,2},{8,4},{10,6},{12,8},{14,10},{1,13},{3,15... | collective-permute-start | bytes 147464 | tf_op jit(solution)/shard_map/ppermute | solution.py:591
  95.4 8.1 %collective-permute-start.20 = (f32[96,128]{1,0:T(8,128)S(1)}, f32[96,128]{1,0:T(8,128)S(1)}, u32[]{:S(2)}, u32[]{:S(2)}) collective-permute-start(f32[96,128]{1,0:T(8,128)S(1)} %get-tuple-element.102), channel_id=1, source_target_pairs={{0,14},{2,12},{4,2},{6,0},{8,6},{10,4},{12,10},{14,8},{1,15},{3,13... | collective-permute-start | bytes 147464 | tf_op jit(solution)/shard_map/ppermute | solution.py:591
  97.5 6.0 %collective-permute-start.21 = (f32[96,128]{1,0:T(8,128)S(1)}, f32[96,128]{1,0:T(8,128)S(1)}, u32[]{:S(2)}, u32[]{:S(2)}) collective-permute-start(f32[96,128]{1,0:T(8,128)S(1)} %get-tuple-element.103), channel_id=1, source_target_pairs={{0,4},{2,6},{4,8},{6,10},{8,12},{10,14},{12,0},{14,2},{1,5},{3,7},... | collective-permute-start | bytes 147464 | tf_op jit(solution)/shard_map/ppermute | solution.py:591
  98.3 6.8 %collective-permute-start.22 = (f32[96,128]{1,0:T(8,128)S(1)}, f32[96,128]{1,0:T(8,128)S(1)}, u32[]{:S(2)}, u32[]{:S(2)}) collective-permute-start(f32[96,128]{1,0:T(8,128)S(1)} %get-tuple-element.104), channel_id=1, source_target_pairs={{0,6},{2,4},{4,10},{6,8},{8,14},{10,12},{12,2},{14,0},{1,7},{3,5},... | collective-permute-start | bytes 147464 | tf_op jit(solution)/shard_map/ppermute | solution.py:591
  98.3 6.8 %collective-permute-start.23 = (f32[96,128]{1,0:T(8,128)S(1)}, f32[96,128]{1,0:T(8,128)S(1)}, u32[]{:S(2)}, u32[]{:S(2)}) collective-permute-start(f32[96,128]{1,0:T(8,128)S(1)} %get-tuple-element.105), channel_id=1, source_target_pairs={{0,2},{2,0},{4,6},{6,4},{8,10},{10,8},{12,14},{14,12},{1,3},{3,1},... | collective-permute-start | bytes 147464 | tf_op jit(solution)/shard_map/ppermute | solution.py:591
  106.3 3.9 %collective-permute-start.25 = (f32[32,128]{1,0:T(8,128)S(1)}, f32[32,128]{1,0:T(8,128)S(1)}, u32[]{:S(2)}, u32[]{:S(2)}) collective-permute-start(f32[32,128]{1,0:T(8,128)S(1)} %get-tuple-element.108), channel_id=1, source_target_pairs={{0,2},{1,3},{2,0},{3,1},{4,6},{5,7},{6,4},{7,5},{8,10},{9,11},{10,... | collective-permute-start | bytes 49160 | tf_op jit(solution)/shard_map/ppermute | solution.py:43
  106.9 3.3 %collective-permute-start.26 = (f32[32,128]{1,0:T(8,128)S(1)}, f32[32,128]{1,0:T(8,128)S(1)}, u32[]{:S(2)}, u32[]{:S(2)}) collective-permute-start(f32[32,128]{1,0:T(8,128)S(1)} %get-tuple-element.109), channel_id=1, source_target_pairs={{0,3},{1,2},{2,1},{3,0},{4,7},{5,6},{6,5},{7,4},{8,11},{9,10},{10,... | collective-permute-start | bytes 49160 | tf_op jit(solution)/shard_map/ppermute | solution.py:43
  106.9 3.3 %collective-permute-start.24 = (f32[32,128]{1,0:T(8,128)S(1)}, f32[32,128]{1,0:T(8,128)S(1)}, u32[]{:S(2)}, u32[]{:S(2)}) collective-permute-start(f32[32,128]{1,0:T(8,128)S(1)} %get-tuple-element.107), channel_id=1, source_target_pairs={{0,1},{1,0},{2,3},{3,2},{4,5},{5,4},{6,7},{7,6},{8,9},{9,8},{10,11... | collective-permute-start | bytes 49160 | tf_op jit(solution)/shard_map/ppermute | solution.py:43
  110.3 4.9 %collective-permute-start.28 = (f32[32,128]{1,0:T(8,128)S(1)}, f32[32,128]{1,0:T(8,128)S(1)}, u32[]{:S(2)}, u32[]{:S(2)}) collective-permute-start(f32[32,128]{1,0:T(8,128)S(1)} %add_add_fusion.1), channel_id=1, source_target_pairs={{0,8},{4,12},{8,0},{12,4},{1,9},{5,13},{9,1},{13,5},{2,10},{6,14},... | collective-permute-start | bytes 49160 | tf_op jit(solution)/shard_map/ppermute | solution.py:43
  112.4 5.5 %collective-permute-start.29 = (f32[32,128]{1,0:T(8,128)S(1)}, f32[32,128]{1,0:T(8,128)S(1)}, u32[]{:S(2)}, u32[]{:S(2)}) collective-permute-start(f32[32,128]{1,0:T(8,128)S(1)} %add_add_fusion.1), channel_id=1, source_target_pairs={{0,12},{4,8},{8,4},{12,0},{1,13},{5,9},{9,5},{13,1},{2,14},{6,10},... | collective-permute-start | bytes 49160 | tf_op jit(solution)/shard_map/ppermute | solution.py:43
  112.7 5.2 %collective-permute-start.27 = (f32[32,128]{1,0:T(8,128)S(1)}, f32[32,128]{1,0:T(8,128)S(1)}, u32[]{:S(2)}, u32[]{:S(2)}) collective-permute-start(f32[32,128]{1,0:T(8,128)S(1)} %add_add_fusion.1), channel_id=1, source_target_pairs={{0,4},{4,0},{8,12},{12,8},{1,5},{5,1},{9,13},{13,9},{2,6},{6,2},{1... | collective-permute-start | bytes 49160 | tf_op jit(solution)/shard_map/ppermute | solution.py:43

commit v12 on v11

--- a/solution.py
+++ b/solution.py
@@ -287,77 +287,87 @@
     )(place, offsets.swapaxes(0, 1), coefs)
 
 
-def product_kernel(spots, n_sub, first_row, n_blocks, with_grid, place, w_high, w_low, *refs):
-    refs, proj_out = refs[:-1], refs[-1]
-    n_outs = n_blocks + (1 if with_grid else 0)
-    arrays, outs = refs[:-n_outs], list(refs[-n_outs:])
-    rows, orbitals = proj_out.shape
+CELLS = 12
+
+
+def split_orbitals(spots, place, arrays, start):
+    swap = (place[ME] & 2) != 0
+    highs, lows = [], []
+    for spot in spots:
+        tiles = [arrays[at][pl.ds(start, CELLS), f : f + width] for at, f, width in spot]
+        if len(tiles) == 2:
+            near, far = tiles
+            tiles = [jnp.where(swap, far, near), jnp.where(swap, near, far)]
+        high, low = split_bf16(jnp.concatenate(tiles, axis=1))
+        highs.append(jnp.concatenate([high[k] for k in range(CELLS)], axis=1))
+        lows.append(jnp.concatenate([low[k] for k in range(CELLS)], axis=1))
+    return jnp.concatenate(highs, axis=0), jnp.concatenate(lows, axis=0)
+
+
+def product(left_high, left_low, high, low):
+    orbitals = high.shape[0]
+    right = jnp.concatenate([high, low], axis=0)
+    wide = lax.dot_general(left_high, right, NT, preferred_element_type=jnp.float32)
+    narrow = lax.dot_general(left_low, high, NT, preferred_element_type=jnp.float32)
+    return wide[:, :orbitals] + wide[:, orbitals:] + narrow
+
+
+def product_kernel(spots, n_blocks, place, w_high, w_low, *refs):
+    arrays, outs, total = refs[: -n_blocks - 1], refs[-n_blocks - 1 : -1], refs[-1]
     cells, _, lanes = arrays[0].shape
-    block = 12
-    swap = (place[ME] & 2) != 0
-
-    def parts(start):
-        highs, lows = [], []
-        for spot in spots:
-            tiles = [
-                arrays[at][pl.ds(start, block), first : first + width] for at, first, width in spot
-            ]
-            if len(tiles) == 2:
-                near, far = tiles
-                tiles = [jnp.where(swap, far, near), jnp.where(swap, near, far)]
-            high, low = split_bf16(jnp.concatenate(tiles, axis=1))
-            highs.append(jnp.concatenate([high[k] for k in range(block)], axis=1))
-            lows.append(jnp.concatenate([low[k] for k in range(block)], axis=1))
-        return jnp.concatenate(highs, axis=0), jnp.concatenate(lows, axis=0)
-
-    def product(left_high, left_low, high, low):
-        right = jnp.concatenate([high, low], axis=0)
-        wide = lax.dot_general(left_high, right, NT, preferred_element_type=jnp.float32)
-        narrow = lax.dot_general(left_low, high, NT, preferred_element_type=jnp.float32)
-        return wide[:, :orbitals] + wide[:, orbitals:] + narrow
-
-    if with_grid:
-        grid_out = outs.pop(0)
-        grid_out[...] = jnp.zeros_like(grid_out)
-
-        def grid_block(step, carry):
-            high, low = parts(place[SUB] * (cells // n_sub) + step * block)
-            grid_out[...] += product(high, low, high, low)
-            return carry
-
-        lax.fori_loop(0, cells // (n_sub * block), grid_block, 0)
-
-    def proj_block(step, carry):
-        high, low = parts(step * block)
-        depth = block * lanes
+
+    def one_block(step, carry):
+        high, low = split_orbitals(spots, place, arrays, step * CELLS)
+        depth = CELLS * lanes
         here = pl.ds(pl.multiple_of(step * depth, depth), depth)
-        some = slice(first_row, first_row + rows)
-        proj_out[...] += product(w_high[some, here], w_low[some, here], high, low)
+        total[...] += product(w_high[:, here], w_low[:, here], high, low)
         return carry
 
-    proj_out[...] = jnp.zeros_like(proj_out)
-    lax.fori_loop(0, cells // block, proj_block, 0)
+    total[...] = jnp.zeros_like(total)
+    lax.fori_loop(0, cells // CELLS, one_block, 0)
+    rows = outs[0].shape[0]
     for k, out in enumerate(outs):
-        out[...] = proj_out[k * (rows // n_blocks) : (k + 1) * (rows // n_blocks), :]
-
-
-def products(n_sub, first_row, rows, n_blocks, with_grid, place, projectors, arrays, spots):
+        out[...] = total[k * rows : (k + 1) * rows, :]
+
+
+def products(n_sub, n_blocks, place, projectors, arrays, spots):
     orbitals = sum(width for spot in spots for _, _, width in spot)
-    grid = [jax.ShapeDtypeStruct((orbitals, orbitals), jnp.float32)] if with_grid else []
+    rows = projectors[0].shape[0]
     block = jax.ShapeDtypeStruct((rows // n_blocks, orbitals), jnp.float32)
-    flops = 12 * rows * orbitals * projectors[0].shape[1]
     return pl.pallas_call(
-        functools.partial(product_kernel, spots, n_sub, first_row, n_blocks, with_grid),
-        out_shape=grid + [block] * n_blocks,
+        functools.partial(product_kernel, spots, n_blocks),
+        out_shape=[block] * n_blocks,
         in_specs=[SMEM] + [VMEM] * (2 + len(arrays)),
-        out_specs=[VMEM] * (len(grid) + n_blocks),
+        out_specs=[VMEM] * n_blocks,
         scratch_shapes=[pltpu.VMEM((rows, orbitals), jnp.float32)],
         compiler_params=params(8),
-        cost_estimate=pl.CostEstimate(
-            flops=flops, bytes_accessed=4 * rows * projectors[0].shape[1], transcendentals=0
-        ),
         name="products",
     )(place, *projectors, *arrays)
+
+
+def grid_kernel(spots, n_sub, place, *refs):
+    *arrays, out = refs
+    share = arrays[0].shape[0] // n_sub
+    out[...] = jnp.zeros_like(out)
+
+    def one_block(step, carry):
+        high, low = split_orbitals(spots, place, arrays, place[SUB] * share + step * CELLS)
+        out[...] += product(high, low, high, low)
+        return carry
+
+    lax.fori_loop(0, share // CELLS, one_block, 0)
+
+
+def grid_sums(n_sub, place, arrays, spots):
+    orbitals = sum(width for spot in spots for _, _, width in spot)
+    return pl.pallas_call(
+        functools.partial(grid_kernel, spots, n_sub),
+        out_shape=jax.ShapeDtypeStruct((orbitals, orbitals), jnp.float32),
+        in_specs=[SMEM] + [VMEM] * len(arrays),
+        out_specs=VMEM,
+        compiler_params=params(8),
+        name="grid_sums",
+    )(place, *arrays)
 
 
 def reordered(x, width, by):
@@ -379,12 +389,18 @@
             if by & bit:
                 columns = reordered(columns, width, bit)
         projections += columns
-    highest = lax.Precision.HIGHEST
+    corr, rows = split_bf16(corr_ref[...]), split_bf16(projections)
     weighted = jnp.dot(
-        corr_ref[...], projections, precision=highest, preferred_element_type=jnp.float32
-    )
+        jnp.concatenate([corr[0], corr[0], corr[1]], axis=1),
+        jnp.concatenate([rows[0], rows[1], rows[0]], axis=0),
+        preferred_element_type=jnp.float32,
+    )
+    parts = split_bf16(weighted)
     atom_part = lax.dot_general(
-        projections, weighted, TN, precision=highest, preferred_element_type=jnp.float32
+        jnp.concatenate([rows[0], rows[0], rows[1]], axis=0),
+        jnp.concatenate([parts[0], parts[1], parts[0]], axis=0),
+        TN,
+        preferred_element_type=jnp.float32,
     )
     share = grid_ref[...] * scales[0] + atom_part * scales[1]
     for bit in bits:
@@ -550,34 +566,37 @@
         crossed = len(tiles[-1]) == 2 and at == len(parts) - 2
         for m in range(1, n_band):
             pieces.append(part[m] if crossed else swapped(part[m], "band", n_band, m))
-    arrays = own + pieces
-    pieces = [jnp.concatenate(own, axis=1)] + pieces
-    arrays += [swapped(x, "sub", n_sub, k) for k in range(1, n_sub) for x in pieces]
-    starts = [sum(x.shape[1] for x in own[:at]) for at in range(len(own))]
-    spots = []
-    for m in range(n_band):
-        for k in range(n_sub):
-            for tile in tiles:
-                spot = []
-                for at in tile:
-                    index, first = at, 0
-                    if m:
-                        index = len(own) + at * (n_band - 1) + m - 1 + k * len(pieces)
-                    elif k:
-                        index = len(own) * n_band + (k - 1) * len(pieces)
-                        first = starts[at]
-                    spot.append((index, first, own[at].shape[1]))
-                spots.append(spot)
+    sooner = own
+    firsts = [sum(x.shape[1] for x in own[:at]) for at in range(len(sooner))]
+    over_sub = [(jnp.concatenate(sooner, axis=1), [(at, 0, f) for at, f in enumerate(firsts)])]
+    over_sub += [(x, [(len(sooner), 0, 0)]) for x in own[len(sooner) :]]
+    over_sub += [
+        (x, [(k // (n_band - 1), k % (n_band - 1) + 1, 0)]) for k, x in enumerate(pieces)
+    ]
+    arrays, where = [], {}
+    for at, x in enumerate(own):
+        where[at, 0, 0] = (len(arrays), 0)
+        arrays.append(x)
+    for x, held in over_sub[len(over_sub) - len(pieces) :]:
+        where[held[0][0], held[0][1], 0] = (len(arrays), 0)
+        arrays.append(x)
+    for k in range(1, n_sub):
+        for x, held in over_sub:
+            for at, m, first in held:
+                where[at, m, k] = (len(arrays), first)
+            arrays.append(swapped(x, "sub", n_sub, k))
+    spots = [
+        [where[at, m, k] + (own[at].shape[1],) for at in tile]
+        for m in range(n_band)
+        for k in range(n_sub)
+        for tile in tiles
+    ]
 
     rows = own_atoms * channels
     n_sent = 3 * n_band - 1
-    outgoing = products(
-        n_sub, 0, n_sent * rows, n_sent, False, place, projectors, arrays, spots
-    )
+    *outgoing, own_proj = products(n_sub, n_sent + 1, place, projectors, arrays, spots)
     outgoing, place = lax.optimization_barrier((outgoing, place))
-    grid_part, own_proj = products(
-        n_sub, n_sent * rows, rows, 1, True, place, projectors, arrays, spots
-    )
+    grid_part = grid_sums(n_sub, place, arrays, spots)
     sums, seen = [], []
     to = [(by, m) for by in (1, -1) for m in range(n_band)]
     to += [(0, m) for m in range(n_band - 1, 0, -1)]

time: 119 us -> 119 us (level)
  waiting for transfers between devices: 38.5 us -> 40.2 us
  Pallas kernels: 38.9 us -> 37.3 us
    ppermute x5, waiting for transfers between devices: 1.6 us -> 3.71 us  [on_device(): sums.append(lax.ppermute(x, ('dom', 'band'), pairs))]
    pallas_call x2, Pallas kernels: 8.16 us -> 6.69 us  [the longest x1 5.1 us: products(): pl.pallas_call(functools.partial(product_kernel, spots, n_blocks), out_sh...]
  transfers between devices with their start and end apart: 30 -> 30, of which waited for: 10 -> 11; matrix products, arithmetic and copies ran while one was open for 1% -> 1% of each run, Pallas kernels for 28% -> 26%
where the time goes in v12:
time: 119 us
  waiting for transfers between devices  40.2 us (34%)
  Pallas kernels  37.3 us (31%)
  starting transfers between devices  35.7 us (30%)
  local copies, waits for them, and re-layouts  2.82 us (2%)
  other arithmetic  1.72 us (1%)
    ppermute x25, waiting for transfers between devices, swapped(): return lax.ppermute(x, axes, [(i, i ^ by) for i in range(size)])  36.5 us
    ppermute x25, starting transfers between devices, swapped(): return lax.ppermute(x, axes, [(i, i ^ by) for i in range(size)])  27.1 us
    pallas_call x2, Pallas kernels, filter_orbitals(): pl.pallas_call(functools.partial(filter_kernel, n_dom, planes, rows, star...  13.2 us
    pallas_call x1, Pallas kernels, build_projectors(): pl.pallas_call(functools.partial(projector_kernel, n_band, n_sub), out_sh...  11.5 us
    ppermute x5, starting transfers between devices, on_device(): sums.append(lax.ppermute(x, ('dom', 'band'), pairs))  8.66 us
    pallas_call x1, Pallas kernels, products(): pl.pallas_call(functools.partial(product_kernel, spots, n_blocks), out_sh...  5.1 us
    ppermute x5, waiting for transfers between devices, on_device(): sums.append(lax.ppermute(x, ('dom', 'band'), pairs))  3.71 us
    pallas_call x2, Pallas kernels, orbital_first(): pl.pallas_call(functools.partial(orbital_first_kernel, n_dom, which), out...  2.92 us
  transfers between devices with their start and end apart: 30, of which 11 were waited for; matrix products, arithmetic and copies ran while one was open for 1% of the time, Pallas kernels for 26%

profile of v12, /device:TPU:0, one launch (start us, length us, event | category | flops | bytes accessed | tf_op | source)
XLA Modules:
  0.0 118.7 jit_solution(5890220537788712583)
XLA Ops:
  0.6 0.0 copy-start
  0.7 2.3 %constant_dynamic-slice_fusion = (f32[384,128]{1,0:T(8,128)S(1)}, f32[384,128]{1,0:T(8,128)}, f32[384,128]{1,0:T(8,128)S(1)}, f32[384,128]{1,0:T(8,128)}, f32[38...) fusion(f32[3072,128]{1,0:T(8,128)} %bitcast.34, s32[]{:T(128)S(6)} %select_n.35, ...), kind=kLoop, calls=%fused_computation.9 | loop fusion | bytes 3145760 | tf_op jit(solution)/shard_map/dynamic_slice | solution.py:440
  3.1 4.1 %collective-permute-start = (f32[480,128]{1,0:T(8,128)S(1)}, f32[480,128]{1,0:T(8,128)S(1)}, u32[]{:S(2)}, u32[]{:S(2)}) collective-permute-start(f32[480,128]{1,0:T(8,128)S(1)} %get-tuple-element.117), channel_id=1, source_target_pairs={{0,8},{4,12},{8,0},{12,4},{1,9},{5,13},{9,1},{13,5},{2,10},{6,14},... | collective-permute-start | bytes 737288 | tf_op jit(solution)/shard_map/ppermute | solution.py:43
  7.2 0.8 pad_maximum_fusion.1
  8.0 1.6 %collective-permute-start.2 = (f32[864,128]{1,0:T(8,128)}, f32[864,128]{1,0:T(8,128)S(1)}, u32[]{:S(2)}, u32[]{:S(2)}) collective-permute-start(f32[864,128]{1,0:T(8,128)} %pad_maximum_fusion.1), channel_id=1, source_target_pairs={{0,4},{4,0},{8,12},{12,8},{1,5},{5,1},{9,13},{13,9},{2,6},{6,2},{1... | collective-permute-start | bytes 1327112 | tf_op jit(solution)/shard_map/ppermute | solution.py:43
  9.5 0.1 constant_dynamic-slice_fusion.8
  9.6 0.1 copy.9
  9.7 0.1 broadcast_multiply_fusion
  9.9 9.4 %collective-permute-done.refs_3_ = f32[480,128]{1,0:T(8,128)S(1)} collective-permute-done((f32[480,128]{1,0:T(8,128)S(1)}, f32[480,128]{1,0:T(8,128)S(1)}, u32[]{:S(2)}, u32[]{:S(2)}) %collective-permute-start) | collective-permute-done | bytes 245792 | tf_op jit(solution)/shard_map/ppermute | solution.py:43
  19.3 0.0 collective-permute-start.1
  19.3 9.9 %collective-permute-done.2.refs_2_ = f32[864,128]{1,0:T(8,128)S(1)} collective-permute-done((f32[864,128]{1,0:T(8,128)}, f32[864,128]{1,0:T(8,128)S(1)}, u32[]{:S(2)}, u32[]{:S(2)}) %collective-permute-start.2) | collective-permute-done | bytes 442400 | tf_op jit(solution)/shard_map/ppermute | solution.py:43
  29.2 0.5 collective-permute-start.7
  29.7 2.0 %collective-permute-start.8 = (f32[384,128]{1,0:T(8,128)S(1)}, f32[384,128]{1,0:T(8,128)S(1)}, u32[]{:S(2)}, u32[]{:S(2)}) collective-permute-start(f32[384,128]{1,0:T(8,128)S(1)} %get-tuple-element.68), channel_id=1, source_target_pairs={{0,12},{4,8},{8,4},{12,0},{1,13},{5,9},{9,5},{13,1},{2,14},{6,10},... | collective-permute-start | bytes 589832 | tf_op jit(solution)/shard_map/ppermute | solution.py:43
  31.7 0.1 pad_add_fusion.place
  31.8 0.3 mul.56.corr_ref
  32.1 0.0 collective-permute-done.1.refs_0_
  32.1 6.8 %chebyshev.2 = (f32[3,128,128]{2,1,0:T(8,128)S(1)}, f32[3,128,128]{2,1,0:T(8,128)S(1)}, f32[3,128,128]{2,1,0:T(8,128)S(1)}, f32[3,128,128]{2,1,0:T(8,128)S(1)}, f32[6,32,8,128]{3,2,1,0:T(8,128)S(1)}) custom-call(s32[4]{0:T(128)S(1)} %pad_add_fusion.place, f32[96,128]{1,0:T(8,128)S(1)} %collective-permute-done.1.refs_0_, ...), custom_call_target="tpu_custom_call" | custom-call | flops 28311552 | bytes 1572864 | tf_op jit(solution)/shard_map/chebyshev/pallas_call | solution.py:132
  38.9 1.1 collective-permute-start.4
  39.9 1.4 %collective-permute-start.5 = (f32[3,128,128]{2,1,0:T(8,128)S(1)}, f32[3,128,128]{2,1,0:T(8,128)S(1)}, u32[]{:S(2)}, u32[]{:S(2)}) collective-permute-start(f32[3,128,128]{2,1,0:T(8,128)S(1)} %get-tuple-element.59), channel_id=1, source_target_pairs={{0,8},{4,12},{8,0},{12,4},{1,9},{5,13},{9,1},{13,5},{2,10},{6,14},... | collective-permute-start | bytes 589832 | tf_op jit(solution)/shard_map/ppermute | solution.py:43
  41.4 2.0 %collective-permute-start.6 = (f32[3,128,128]{2,1,0:T(8,128)S(1)}, f32[3,128,128]{2,1,0:T(8,128)S(1)}, u32[]{:S(2)}, u32[]{:S(2)}) collective-permute-start(f32[3,128,128]{2,1,0:T(8,128)S(1)} %get-tuple-element.60), channel_id=1, source_target_pairs={{0,12},{4,8},{8,4},{12,0},{1,13},{5,9},{9,5},{13,1},{2,14},{6,10},... | collective-permute-start | bytes 589832 | tf_op jit(solution)/shard_map/ppermute | solution.py:43
  43.3 11.5 %projectors.1 = (bf16[576,6144]{1,0:T(8,128)(2,1)S(1)}, bf16[576,6144]{1,0:T(8,128)(2,1)S(1)}) custom-call(s32[4]{0:T(128)S(1)} %pad_add_fusion.place, s32[3,48,128]{2,1,0:T(8,128)S(1)} %bitcast.32, f32[48,3,8,128]{3,2,1,0:T(8,128)S(1)} %copy-done.1), custom_call_target="tpu_custom_call" | custom-call | flops 1811939328 | bytes 28311552 | tf_op jit(solution)/shard_map/projectors/pallas_call | solution.py:275
  54.8 0.0 collective-permute-done.7.refs_3_
  54.8 0.0 collective-permute-done.8.refs_4_
  54.8 6.4 %chebyshev.3 = (f32[3,128,128]{2,1,0:T(8,128)S(1)}, f32[3,128,128]{2,1,0:T(8,128)S(1)}, f32[3,128,128]{2,1,0:T(8,128)S(1)}, f32[3,128,128]{2,1,0:T(8,128)S(1)}) custom-call(s32[4]{0:T(128)S(1)} %pad_add_fusion.place, f32[6,32,8,128]{3,2,1,0:T(8,128)S(1)} %get-tuple-element.65.refs_0_, f32[384,128]{1,0:T(8,128)S(1)} %get-tuple-element.110.refs_1_, ...), custom_call_target="tpu_custom_call" | custom-call | flops 28311552 | bytes 1572864 | tf_op jit(solution)/shard_map/chebyshev/pallas_call | solution.py:132
  61.3 0.4 collective-permute-start.9
  61.7 2.1 %collective-permute-start.10 = (f32[3,128,128]{2,1,0:T(8,128)S(1)}, f32[3,128,128]{2,1,0:T(8,128)S(1)}, u32[]{:S(2)}, u32[]{:S(2)}) collective-permute-start(f32[3,128,128]{2,1,0:T(8,128)S(1)} %get-tuple-element.72), channel_id=1, source_target_pairs={{0,8},{4,12},{8,0},{12,4},{1,9},{5,13},{9,1},{13,5},{2,10},{6,14},... | collective-permute-start | bytes 589832 | tf_op jit(solution)/shard_map/ppermute | solution.py:43
  63.8 0.0 collective-permute-done.4
  63.8 2.0 %collective-permute-start.11 = (f32[3,128,128]{2,1,0:T(8,128)S(1)}, f32[3,128,128]{2,1,0:T(8,128)S(1)}, u32[]{:S(2)}, u32[]{:S(2)}) collective-permute-start(f32[3,128,128]{2,1,0:T(8,128)S(1)} %get-tuple-element.73), channel_id=1, source_target_pairs={{0,12},{4,8},{8,4},{12,0},{1,13},{5,9},{9,5},{13,1},{2,14},{6,10},... | collective-permute-start | bytes 589832 | tf_op jit(solution)/shard_map/ppermute | solution.py:43
  65.7 0.0 collective-permute-done.5
  65.7 0.0 collective-permute-done.6
  65.7 0.7 cell_first.3
  66.4 0.8 collective-permute-done.9
  67.2 1.6 %orbital_first.2.refs_2_ = f32[32,96,128]{2,1,0:T(8,128)} custom-call(s32[4]{0:T(128)S(1)} %pad_add_fusion.place, f32[384,128]{1,0:T(8,128)S(1)} %bitcast.21, f32[384,128]{1,0:T(8,128)S(1)} %bitcast.23, f32[384,128]{1,0:T(8,128)S(1)} %bitcast.25, f32[384,128]{1,0:T(8,128)S(1)} %bitcast.27, f32[384,128]{1,0:T(8,128)S(1)} %bitcast.16, f32[384,128]{1,0:T(8,128)S(1)} %bitcast.18), custom_call_target="tpu_custom_call" | custom-call | tf_op jit(solution)/shard_map/orbital_first/pallas_call | solution.py:209
  68.9 0.6 cell_first.4
  69.5 1.6 %collective-permute-start.12 = (f32[48,8,128]{2,1,0:T(8,128)S(1)}, f32[48,8,128]{2,1,0:T(8,128)S(1)}, u32[]{:S(2)}, u32[]{:S(2)}) collective-permute-start(f32[48,8,128]{2,1,0:T(8,128)S(1)} %get-tuple-element.83), channel_id=1, source_target_pairs={{0,2},{2,0},{1,3},{3,1},{4,6},{6,4},{5,7},{7,5},{8,10},{10,8},{9,1... | collective-permute-start | bytes 589832 | tf_op jit(solution)/shard_map/ppermute | solution.py:43
  71.0 0.5 collective-permute-start.13
  71.6 5.6 %collective-permute-done.10 = f32[3,128,128]{2,1,0:T(8,128)S(1)} collective-permute-done((f32[3,128,128]{2,1,0:T(8,128)S(1)}, f32[3,128,128]{2,1,0:T(8,128)S(1)}, u32[]{:S(2)}, u32[]{:S(2)}) %collective-permute-start.10) | collective-permute-done | bytes 196640 | tf_op jit(solution)/shard_map/ppermute | solution.py:43
  77.1 0.6 cell_first.5
  77.7 0.1 pad_maximum_fusion
  77.8 0.1 collective-permute-start.15
  77.9 1.6 %collective-permute-start.14 = (f32[48,8,128]{2,1,0:T(8,128)S(1)}, f32[48,8,128]{2,1,0:T(8,128)S(1)}, u32[]{:S(2)}, u32[]{:S(2)}) collective-permute-start(f32[48,8,128]{2,1,0:T(8,128)S(1)} %get-tuple-element.90), channel_id=1, source_target_pairs={{0,2},{2,0},{1,3},{3,1},{4,6},{6,4},{5,7},{7,5},{8,10},{10,8},{9,1... | collective-permute-start | bytes 589832 | tf_op jit(solution)/shard_map/ppermute | solution.py:43
  79.4 0.1 collective-permute-done.13.refs_3_
  79.5 0.1 collective-permute-start.16
  79.6 0.4 collective-permute-start.17
  80.0 5.2 %collective-permute-done.14.refs_5_ = f32[48,8,128]{2,1,0:T(8,128)S(1)} collective-permute-done((f32[48,8,128]{2,1,0:T(8,128)S(1)}, f32[48,8,128]{2,1,0:T(8,128)S(1)}, u32[]{:S(2)}, u32[]{:S(2)}) %collective-permute-start.14) | collective-permute-done | bytes 196640 | tf_op jit(solution)/shard_map/ppermute | solution.py:43
  85.2 1.4 %collective-permute-done.18.refs_9_ = f32[48,8,128]{2,1,0:T(8,128)S(1)} collective-permute-done((f32[48,8,128]{2,1,0:T(8,128)S(1)}, f32[48,8,128]{2,1,0:T(8,128)S(1)}, u32[]{:S(2)}, u32[]{:S(2)}) %collective-permute-start.18) | collective-permute-done | bytes 196640 | tf_op jit(solution)/shard_map/ppermute | solution.py:43
  86.6 5.1 %products.1 = (f32[96,128]{1,0:T(8,128)S(1)}, f32[96,128]{1,0:T(8,128)S(1)}, f32[96,128]{1,0:T(8,128)S(1)}, f32[96,128]{1,0:T(8,128)S(1)}, f32[96,128]{1,0:T(8,128)S(1)}, /*index=5*/f32[96,128]{1,0:T(8,128)S(1)}) custom-call(s32[4]{0:T(128)S(1)} %pad_add_fusion.place, bf16[576,6144]{1,0:T(8,128)(2,1)S(1)} %get-tuple-element.75.w_high, ...), custom_call_target="tpu_custom_call" | custom-call | tf_op jit(solution)/shard_map/products/pallas_call | solution.py:337
  91.7 4.2 %collective-permute-start.19 = (f32[96,128]{1,0:T(8,128)S(1)}, f32[96,128]{1,0:T(8,128)S(1)}, u32[]{:S(2)}, u32[]{:S(2)}) collective-permute-start(f32[96,128]{1,0:T(8,128)S(1)} %get-tuple-element.99), channel_id=1, source_target_pairs={{0,12},{2,14},{4,0},{6,2},{8,4},{10,6},{12,8},{14,10},{1,13},{3,15... | collective-permute-start | bytes 147464 | tf_op jit(solution)/shard_map/ppermute | solution.py:610
  96.0 2.2 %collective-permute-start.20 = (f32[96,128]{1,0:T(8,128)S(1)}, f32[96,128]{1,0:T(8,128)S(1)}, u32[]{:S(2)}, u32[]{:S(2)}) collective-permute-start(f32[96,128]{1,0:T(8,128)S(1)} %get-tuple-element.100), channel_id=1, source_target_pairs={{0,14},{2,12},{4,2},{6,0},{8,6},{10,4},{12,10},{14,8},{1,15},{3,13... | collective-permute-start | bytes 147464 | tf_op jit(solution)/shard_map/ppermute | solution.py:610
  98.1 0.8 collective-permute-start.21
  98.9 1.5 %collective-permute-start.23 = (f32[96,128]{1,0:T(8,128)S(1)}, f32[96,128]{1,0:T(8,128)S(1)}, u32[]{:S(2)}, u32[]{:S(2)}) collective-permute-start(f32[96,128]{1,0:T(8,128)S(1)} %get-tuple-element.103), channel_id=1, source_target_pairs={{0,2},{2,0},{4,6},{6,4},{8,10},{10,8},{12,14},{14,12},{1,3},{3,1},... | collective-permute-start | bytes 147464 | tf_op jit(solution)/shard_map/ppermute | solution.py:610
  100.4 1.6 %grid_sums.1.grid_ref = f32[128,128]{1,0:T(8,128)S(1)} custom-call(s32[4]{0:T(128)S(1)} %pad_add_fusion.place, f32[48,16,128]{2,1,0:T(8,128)S(1)} %get-tuple-element.79.refs_0_, f32[48,8,128]{2,1,0:T(8,128)S(1)} %get-tuple-element.84.refs_1_, f32[48,8,128]{2,1,0:T(8,128)S(1)} %get-tuple-element.87.refs_2_, ...), custom_call_target="tpu_custom_call" | custom-call | tf_op jit(solution)/shard_map/grid_sums/pallas_call | solution.py:363
  102.0 2.0 %collective-permute-done.21.refs_2_ = f32[96,128]{1,0:T(8,128)S(1)} collective-permute-done((f32[96,128]{1,0:T(8,128)S(1)}, f32[96,128]{1,0:T(8,128)S(1)}, u32[]{:S(2)}, u32[]{:S(2)}) %collective-permute-start.21) | collective-permute-done | bytes 49184 | tf_op jit(solution)/shard_map/ppermute | solution.py:610
  104.0 1.7 %collective-permute-done.22.refs_3_ = f32[96,128]{1,0:T(8,128)S(1)} collective-permute-done((f32[96,128]{1,0:T(8,128)S(1)}, f32[96,128]{1,0:T(8,128)S(1)}, u32[]{:S(2)}, u32[]{:S(2)}) %collective-permute-start.22) | collective-permute-done | bytes 49184 | tf_op jit(solution)/shard_map/ppermute | solution.py:610
  105.7 1.1 gram_share.1
  106.8 0.6 collective-permute-start.25
  107.5 1.6 %collective-permute-start.24 = (f32[32,128]{1,0:T(8,128)S(1)}, f32[32,128]{1,0:T(8,128)S(1)}, u32[]{:S(2)}, u32[]{:S(2)}) collective-permute-start(f32[32,128]{1,0:T(8,128)S(1)} %get-tuple-element.105), channel_id=1, source_target_pairs={{0,1},{1,0},{2,3},{3,2},{4,5},{5,4},{6,7},{7,6},{8,9},{9,8},{10,11... | collective-permute-start | bytes 49160 | tf_op jit(solution)/shard_map/ppermute | solution.py:43
  109.1 1.7 %collective-permute-done.25 = f32[32,128]{1,0:T(8,128)S(1)} collective-permute-done((f32[32,128]{1,0:T(8,128)S(1)}, f32[32,128]{1,0:T(8,128)S(1)}, u32[]{:S(2)}, u32[]{:S(2)}) %collective-permute-start.25) | collective-permute-done | bytes 16416 | tf_op jit(solution)/shard_map/ppermute | solution.py:43
  110.8 1.7 %collective-permute-start.28 = (f32[32,128]{1,0:T(8,128)S(1)}, f32[32,128]{1,0:T(8,128)S(1)}, u32[]{:S(2)}, u32[]{:S(2)}) collective-permute-start(f32[32,128]{1,0:T(8,128)S(1)} %add_add_fusion.1), channel_id=1, source_target_pairs={{0,8},{4,12},{8,0},{12,4},{1,9},{5,13},{9,1},{13,5},{2,10},{6,14},... | collective-permute-start | bytes 49160 | tf_op jit(solution)/shard_map/ppermute | solution.py:43
  112.5 0.3 collective-permute-start.29
  112.8 1.5 %collective-permute-start.27 = (f32[32,128]{1,0:T(8,128)S(1)}, f32[32,128]{1,0:T(8,128)S(1)}, u32[]{:S(2)}, u32[]{:S(2)}) collective-permute-start(f32[32,128]{1,0:T(8,128)S(1)} %add_add_fusion.1), channel_id=1, source_target_pairs={{0,4},{4,0},{8,12},{12,8},{1,5},{5,1},{9,13},{13,9},{2,6},{6,2},{1... | collective-permute-start | bytes 49160 | tf_op jit(solution)/shard_map/ppermute | solution.py:43
  114.4 1.3 %orbital_first.3 = f32[32,96,128]{2,1,0:T(8,128)} custom-call(s32[4]{0:T(128)S(1)} %pad_add_fusion.place, f32[384,128]{1,0:T(8,128)S(1)} %bitcast.29, f32[384,128]{1,0:T(8,128)S(1)} %bitcast.31, f32[32,96,128]{2,1,0:T(8,128)} %orbital_first.2.refs_2_), custom_call_target="tpu_custom_call", output_to_operand_aliasing={{}: (3, {})} | custom-call | tf_op jit(solution)/shard_map/orbital_first/pallas_call | solution.py:209
  115.7 2.3 %collective-permute-done.29 = f32[32,128]{1,0:T(8,128)S(1)} collective-permute-done((f32[32,128]{1,0:T(8,128)S(1)}, f32[32,128]{1,0:T(8,128)S(1)}, u32[]{:S(2)}, u32[]{:S(2)}) %collective-permute-start.29) | collective-permute-done | bytes 16416 | tf_op jit(solution)/shard_map/ppermute | solution.py:43
  118.0 0.6 add_add_fusion
  (28 shorter events, 0.1 us)
Async XLA Ops:
  0.6 8.9 %copy-start = (f32[48,8,8]{0,2,1:T(8,128)S(1)}, f32[48,8,8]{0,2,1:T(8,128)}, u32[]{:S(2)}) copy-start(f32[48,8,8]{0,2,1:T(8,128)} %param.9) | copy-start | bytes 36868
  0.7 2.3 %copy-start.3 = (f32[3,32,128]{2,1,0:T(8,128)S(1)}, f32[3,32,128]{2,1,0:T(8,128)}, u32[]{:S(2)}) copy-start(f32[3,32,128]{2,1,0:T(8,128)} %param.6) | copy-start | bytes 147460
  3.1 16.2 %collective-permute-start = (f32[480,128]{1,0:T(8,128)S(1)}, f32[480,128]{1,0:T(8,128)S(1)}, u32[]{:S(2)}, u32[]{:S(2)}) collective-permute-start(f32[480,128]{1,0:T(8,128)S(1)} %get-tuple-element.117), channel_id=1, source_target_pairs={{0,8},{4,12},{8,0},{12,4},{1,9},{5,13},{9,1},{13,5},{2,10},{6,14},... | collective-permute-start | bytes 737288 | tf_op jit(solution)/shard_map/ppermute | solution.py:43
  8.0 21.3 %collective-permute-start.2 = (f32[864,128]{1,0:T(8,128)}, f32[864,128]{1,0:T(8,128)S(1)}, u32[]{:S(2)}, u32[]{:S(2)}) collective-permute-start(f32[864,128]{1,0:T(8,128)} %pad_maximum_fusion.1), channel_id=1, source_target_pairs={{0,4},{4,0},{8,12},{12,8},{1,5},{5,1},{9,13},{13,9},{2,6},{6,2},{1... | collective-permute-start | bytes 1327112 | tf_op jit(solution)/shard_map/ppermute | solution.py:43
  9.5 22.5 %collective-permute-start.3 = (f32[384,128]{1,0:T(8,128)}, f32[384,128]{1,0:T(8,128)S(1)}, u32[]{:S(2)}, u32[]{:S(2)}) collective-permute-start(f32[384,128]{1,0:T(8,128)} %get-tuple-element.111), channel_id=1, source_target_pairs={{0,12},{4,8},{8,4},{12,0},{1,13},{5,9},{9,5},{13,1},{2,14},{6,10},... | collective-permute-start | bytes 589832 | tf_op jit(solution)/shard_map/ppermute | solution.py:43
  9.5 33.8 %copy-start.1 = (f32[48,3,8,128]{3,2,1,0:T(8,128)S(1)}, f32[48,3,8,128]{3,2,1,0:T(8,128)}, u32[]{:S(2)}) copy-start(f32[48,3,8,128]{3,2,1,0:T(8,128)} %coefs_ref.1) | copy-start | bytes 1769476
  9.5 33.8 %copy-start.2 = (s32[48,3,128]{2,0,1:T(8,128)S(1)}, s32[48,3,128]{2,0,1:T(8,128)}, u32[]{:S(2)}) copy-start(s32[48,3,128]{2,0,1:T(8,128)} %param.7) | copy-start | bytes 221188
  19.3 12.8 %collective-permute-start.1 = (f32[96,128]{1,0:T(8,128)S(1)}, f32[96,128]{1,0:T(8,128)S(1)}, u32[]{:S(2)}, u32[]{:S(2)}) collective-permute-start(f32[96,128]{1,0:T(8,128)S(1)} %slice.4), channel_id=1, source_target_pairs={{0,4},{4,0},{8,12},{12,8},{1,5},{5,1},{9,13},{13,9},{2,6},{6,2},{1... | collective-permute-start | bytes 147464 | tf_op jit(solution)/shard_map/ppermute | solution.py:43
  29.2 25.6 %collective-permute-start.7 = (f32[384,128]{1,0:T(8,128)}, f32[384,128]{1,0:T(8,128)S(1)}, u32[]{:S(2)}, u32[]{:S(2)}) collective-permute-start(f32[384,128]{1,0:T(8,128)} %get-tuple-element.67), channel_id=1, source_target_pairs={{0,8},{4,12},{8,0},{12,4},{1,9},{5,13},{9,1},{13,5},{2,10},{6,14},... | collective-permute-start | bytes 589832 | tf_op jit(solution)/shard_map/ppermute | solution.py:43
  29.7 25.1 %collective-permute-start.8 = (f32[384,128]{1,0:T(8,128)S(1)}, f32[384,128]{1,0:T(8,128)S(1)}, u32[]{:S(2)}, u32[]{:S(2)}) collective-permute-start(f32[384,128]{1,0:T(8,128)S(1)} %get-tuple-element.68), channel_id=1, source_target_pairs={{0,12},{4,8},{8,4},{12,0},{1,13},{5,9},{9,5},{13,1},{2,14},{6,10},... | collective-permute-start | bytes 589832 | tf_op jit(solution)/shard_map/ppermute | solution.py:43
  38.9 24.9 %collective-permute-start.4 = (f32[3,128,128]{2,1,0:T(8,128)S(1)}, f32[3,128,128]{2,1,0:T(8,128)S(1)}, u32[]{:S(2)}, u32[]{:S(2)}) collective-permute-start(f32[3,128,128]{2,1,0:T(8,128)S(1)} %get-tuple-element.58), channel_id=1, source_target_pairs={{0,4},{4,0},{8,12},{12,8},{1,5},{5,1},{9,13},{13,9},{2,6},{6,2},{1... | collective-permute-start | bytes 589832 | tf_op jit(solution)/shard_map/ppermute | solution.py:43
  39.9 25.8 %collective-permute-start.5 = (f32[3,128,128]{2,1,0:T(8,128)S(1)}, f32[3,128,128]{2,1,0:T(8,128)S(1)}, u32[]{:S(2)}, u32[]{:S(2)}) collective-permute-start(f32[3,128,128]{2,1,0:T(8,128)S(1)} %get-tuple-element.59), channel_id=1, source_target_pairs={{0,8},{4,12},{8,0},{12,4},{1,9},{5,13},{9,1},{13,5},{2,10},{6,14},... | collective-permute-start | bytes 589832 | tf_op jit(solution)/shard_map/ppermute | solution.py:43
  41.4 24.4 %collective-permute-start.6 = (f32[3,128,128]{2,1,0:T(8,128)S(1)}, f32[3,128,128]{2,1,0:T(8,128)S(1)}, u32[]{:S(2)}, u32[]{:S(2)}) collective-permute-start(f32[3,128,128]{2,1,0:T(8,128)S(1)} %get-tuple-element.60), channel_id=1, source_target_pairs={{0,12},{4,8},{8,4},{12,0},{1,13},{5,9},{9,5},{13,1},{2,14},{6,10},... | collective-permute-start | bytes 589832 | tf_op jit(solution)/shard_map/ppermute | solution.py:43
  61.3 6.0 %collective-permute-start.9 = (f32[3,128,128]{2,1,0:T(8,128)S(1)}, f32[3,128,128]{2,1,0:T(8,128)S(1)}, u32[]{:S(2)}, u32[]{:S(2)}) collective-permute-start(f32[3,128,128]{2,1,0:T(8,128)S(1)} %get-tuple-element.70), channel_id=1, source_target_pairs={{0,4},{4,0},{8,12},{12,8},{1,5},{5,1},{9,13},{13,9},{2,6},{6,2},{1... | collective-permute-start | bytes 589832 | tf_op jit(solution)/shard_map/ppermute | solution.py:43
  61.7 15.4 %collective-permute-start.10 = (f32[3,128,128]{2,1,0:T(8,128)S(1)}, f32[3,128,128]{2,1,0:T(8,128)S(1)}, u32[]{:S(2)}, u32[]{:S(2)}) collective-permute-start(f32[3,128,128]{2,1,0:T(8,128)S(1)} %get-tuple-element.72), channel_id=1, source_target_pairs={{0,8},{4,12},{8,0},{12,4},{1,9},{5,13},{9,1},{13,5},{2,10},{6,14},... | collective-permute-start | bytes 589832 | tf_op jit(solution)/shard_map/ppermute | solution.py:43
  63.8 13.3 %collective-permute-start.11 = (f32[3,128,128]{2,1,0:T(8,128)S(1)}, f32[3,128,128]{2,1,0:T(8,128)S(1)}, u32[]{:S(2)}, u32[]{:S(2)}) collective-permute-start(f32[3,128,128]{2,1,0:T(8,128)S(1)} %get-tuple-element.73), channel_id=1, source_target_pairs={{0,12},{4,8},{8,4},{12,0},{1,13},{5,9},{9,5},{13,1},{2,14},{6,10},... | collective-permute-start | bytes 589832 | tf_op jit(solution)/shard_map/ppermute | solution.py:43
  69.5 7.7 %collective-permute-start.12 = (f32[48,8,128]{2,1,0:T(8,128)S(1)}, f32[48,8,128]{2,1,0:T(8,128)S(1)}, u32[]{:S(2)}, u32[]{:S(2)}) collective-permute-start(f32[48,8,128]{2,1,0:T(8,128)S(1)} %get-tuple-element.83), channel_id=1, source_target_pairs={{0,2},{2,0},{1,3},{3,1},{4,6},{6,4},{5,7},{7,5},{8,10},{10,8},{9,1... | collective-permute-start | bytes 589832 | tf_op jit(solution)/shard_map/ppermute | solution.py:43
  71.0 8.5 %collective-permute-start.13 = (f32[48,16,128]{2,1,0:T(8,128)S(1)}, f32[48,16,128]{2,1,0:T(8,128)S(1)}, u32[]{:S(2)}, u32[]{:S(2)}) collective-permute-start(f32[48,16,128]{2,1,0:T(8,128)S(1)} %get-tuple-element.88), channel_id=1, source_target_pairs={{0,2},{2,0},{1,3},{3,1},{4,6},{6,4},{5,7},{7,5},{8,10},{10,8},{9,1... | collective-permute-start | bytes 1179656 | tf_op jit(solution)/shard_map/ppermute | solution.py:43
  77.8 8.8 %collective-permute-start.15 = (f32[48,32,128]{2,1,0:T(8,128)S(1)}, f32[48,32,128]{2,1,0:T(8,128)S(1)}, u32[]{:S(2)}, u32[]{:S(2)}) collective-permute-start(f32[48,32,128]{2,1,0:T(8,128)S(1)} %pad_maximum_fusion), channel_id=1, source_target_pairs={{0,1},{1,0},{2,3},{3,2},{4,5},{5,4},{6,7},{7,6},{8,9},{9,8},{10,11... | collective-permute-start | bytes 2359304 | tf_op jit(solution)/shard_map/ppermute | solution.py:43
  77.9 7.3 %collective-permute-start.14 = (f32[48,8,128]{2,1,0:T(8,128)S(1)}, f32[48,8,128]{2,1,0:T(8,128)S(1)}, u32[]{:S(2)}, u32[]{:S(2)}) collective-permute-start(f32[48,8,128]{2,1,0:T(8,128)S(1)} %get-tuple-element.90), channel_id=1, source_target_pairs={{0,2},{2,0},{1,3},{3,1},{4,6},{6,4},{5,7},{7,5},{8,10},{10,8},{9,1... | collective-permute-start | bytes 589832 | tf_op jit(solution)/shard_map/ppermute | solution.py:43
  79.5 7.1 %collective-permute-start.16 = (f32[48,16,128]{2,1,0:T(8,128)S(1)}, f32[48,16,128]{2,1,0:T(8,128)S(1)}, u32[]{:S(2)}, u32[]{:S(2)}) collective-permute-start(f32[48,16,128]{2,1,0:T(8,128)S(1)} %collective-permute-done.13.refs_3_), channel_id=1, source_target_pairs={{0,1},{1,0},{2,3},{3,2},{4,5},{5,4},{6,7},{7,6},{8,9},{9,8},{10,11... | collective-permute-start | bytes 1179656 | tf_op jit(solution)/shard_map/ppermute | solution.py:43
  79.6 5.6 %collective-permute-start.17 = (f32[48,8,128]{2,1,0:T(8,128)S(1)}, f32[48,8,128]{2,1,0:T(8,128)S(1)}, u32[]{:S(2)}, u32[]{:S(2)}) collective-permute-start(f32[48,8,128]{2,1,0:T(8,128)S(1)} %collective-permute-done.12.refs_4_), channel_id=1, source_target_pairs={{0,1},{1,0},{2,3},{3,2},{4,5},{5,4},{6,7},{7,6},{8,9},{9,8},{10,11... | collective-permute-start | bytes 589832 | tf_op jit(solution)/shard_map/ppermute | solution.py:43
  85.2 1.4 %collective-permute-start.18 = (f32[48,8,128]{2,1,0:T(8,128)S(1)}, f32[48,8,128]{2,1,0:T(8,128)S(1)}, u32[]{:S(2)}, u32[]{:S(2)}) collective-permute-start(f32[48,8,128]{2,1,0:T(8,128)S(1)} %collective-permute-done.14.refs_5_), channel_id=1, source_target_pairs={{0,1},{1,0},{2,3},{3,2},{4,5},{5,4},{6,7},{7,6},{8,9},{9,8},{10,11... | collective-permute-start | bytes 589832 | tf_op jit(solution)/shard_map/ppermute | solution.py:43
  91.7 10.3 %collective-permute-start.19 = (f32[96,128]{1,0:T(8,128)S(1)}, f32[96,128]{1,0:T(8,128)S(1)}, u32[]{:S(2)}, u32[]{:S(2)}) collective-permute-start(f32[96,128]{1,0:T(8,128)S(1)} %get-tuple-element.99), channel_id=1, source_target_pairs={{0,12},{2,14},{4,0},{6,2},{8,4},{10,6},{12,8},{14,10},{1,13},{3,15... | collective-permute-start | bytes 147464 | tf_op jit(solution)/shard_map/ppermute | solution.py:610
  96.0 6.0 %collective-permute-start.20 = (f32[96,128]{1,0:T(8,128)S(1)}, f32[96,128]{1,0:T(8,128)S(1)}, u32[]{:S(2)}, u32[]{:S(2)}) collective-permute-start(f32[96,128]{1,0:T(8,128)S(1)} %get-tuple-element.100), channel_id=1, source_target_pairs={{0,14},{2,12},{4,2},{6,0},{8,6},{10,4},{12,10},{14,8},{1,15},{3,13... | collective-permute-start | bytes 147464 | tf_op jit(solution)/shard_map/ppermute | solution.py:610
  98.1 5.9 %collective-permute-start.21 = (f32[96,128]{1,0:T(8,128)S(1)}, f32[96,128]{1,0:T(8,128)S(1)}, u32[]{:S(2)}, u32[]{:S(2)}) collective-permute-start(f32[96,128]{1,0:T(8,128)S(1)} %get-tuple-element.101), channel_id=1, source_target_pairs={{0,4},{2,6},{4,8},{6,10},{8,12},{10,14},{12,0},{14,2},{1,5},{3,7},... | collective-permute-start | bytes 147464 | tf_op jit(solution)/shard_map/ppermute | solution.py:610
  98.9 6.8 %collective-permute-start.22 = (f32[96,128]{1,0:T(8,128)S(1)}, f32[96,128]{1,0:T(8,128)S(1)}, u32[]{:S(2)}, u32[]{:S(2)}) collective-permute-start(f32[96,128]{1,0:T(8,128)S(1)} %get-tuple-element.102), channel_id=1, source_target_pairs={{0,6},{2,4},{4,10},{6,8},{8,14},{10,12},{12,2},{14,0},{1,7},{3,5},... | collective-permute-start | bytes 147464 | tf_op jit(solution)/shard_map/ppermute | solution.py:610
  98.9 6.8 %collective-permute-start.23 = (f32[96,128]{1,0:T(8,128)S(1)}, f32[96,128]{1,0:T(8,128)S(1)}, u32[]{:S(2)}, u32[]{:S(2)}) collective-permute-start(f32[96,128]{1,0:T(8,128)S(1)} %get-tuple-element.103), channel_id=1, source_target_pairs={{0,2},{2,0},{4,6},{6,4},{8,10},{10,8},{12,14},{14,12},{1,3},{3,1},... | collective-permute-start | bytes 147464 | tf_op jit(solution)/shard_map/ppermute | solution.py:610
  106.8 3.9 %collective-permute-start.25 = (f32[32,128]{1,0:T(8,128)S(1)}, f32[32,128]{1,0:T(8,128)S(1)}, u32[]{:S(2)}, u32[]{:S(2)}) collective-permute-start(f32[32,128]{1,0:T(8,128)S(1)} %get-tuple-element.106), channel_id=1, source_target_pairs={{0,2},{1,3},{2,0},{3,1},{4,6},{5,7},{6,4},{7,5},{8,10},{9,11},{10,... | collective-permute-start | bytes 49160 | tf_op jit(solution)/shard_map/ppermute | solution.py:43
  107.5 3.3 %collective-permute-start.26 = (f32[32,128]{1,0:T(8,128)S(1)}, f32[32,128]{1,0:T(8,128)S(1)}, u32[]{:S(2)}, u32[]{:S(2)}) collective-permute-start(f32[32,128]{1,0:T(8,128)S(1)} %get-tuple-element.107), channel_id=1, source_target_pairs={{0,3},{1,2},{2,1},{3,0},{4,7},{5,6},{6,5},{7,4},{8,11},{9,10},{10,... | collective-permute-start | bytes 49160 | tf_op jit(solution)/shard_map/ppermute | solution.py:43
  107.5 3.3 %collective-permute-start.24 = (f32[32,128]{1,0:T(8,128)S(1)}, f32[32,128]{1,0:T(8,128)S(1)}, u32[]{:S(2)}, u32[]{:S(2)}) collective-permute-start(f32[32,128]{1,0:T(8,128)S(1)} %get-tuple-element.105), channel_id=1, source_target_pairs={{0,1},{1,0},{2,3},{3,2},{4,5},{5,4},{6,7},{7,6},{8,9},{9,8},{10,11... | collective-permute-start | bytes 49160 | tf_op jit(solution)/shard_map/ppermute | solution.py:43
  110.8 4.9 %collective-permute-start.28 = (f32[32,128]{1,0:T(8,128)S(1)}, f32[32,128]{1,0:T(8,128)S(1)}, u32[]{:S(2)}, u32[]{:S(2)}) collective-permute-start(f32[32,128]{1,0:T(8,128)S(1)} %add_add_fusion.1), channel_id=1, source_target_pairs={{0,8},{4,12},{8,0},{12,4},{1,9},{5,13},{9,1},{13,5},{2,10},{6,14},... | collective-permute-start | bytes 49160 | tf_op jit(solution)/shard_map/ppermute | solution.py:43
  112.5 5.5 %collective-permute-start.29 = (f32[32,128]{1,0:T(8,128)S(1)}, f32[32,128]{1,0:T(8,128)S(1)}, u32[]{:S(2)}, u32[]{:S(2)}) collective-permute-start(f32[32,128]{1,0:T(8,128)S(1)} %add_add_fusion.1), channel_id=1, source_target_pairs={{0,12},{4,8},{8,4},{12,0},{1,13},{5,9},{9,5},{13,1},{2,14},{6,10},... | collective-permute-start | bytes 49160 | tf_op jit(solution)/shard_map/ppermute | solution.py:43
  112.8 5.2 %collective-permute-start.27 = (f32[32,128]{1,0:T(8,128)S(1)}, f32[32,128]{1,0:T(8,128)S(1)}, u32[]{:S(2)}, u32[]{:S(2)}) collective-permute-start(f32[32,128]{1,0:T(8,128)S(1)} %add_add_fusion.1), channel_id=1, source_target_pairs={{0,4},{4,0},{8,12},{12,8},{1,5},{5,1},{9,13},{13,9},{2,6},{6,2},{1... | collective-permute-start | bytes 49160 | tf_op jit(solution)/shard_map/ppermute | solution.py:43

commit v13 on v12

--- a/solution.py
+++ b/solution.py
@@ -43,7 +43,32 @@
     return lax.ppermute(x, axes, [(i, i ^ by) for i in range(size)])
 
 
-def filter_kernel(n_dom, planes, rows, starts, first, n_levels, place, *refs):
+def slot_partners(n_dom, odd):
+    partners = list(range(1, n_dom))
+    return partners[1::-1] + partners[2:] if odd else partners
+
+
+def sent(x, slot):
+    n_dom, n_sub = lax.axis_size("dom"), lax.axis_size("sub")
+    pairs = [
+        (d * n_sub + k, (d ^ slot_partners(n_dom, k % 2)[slot]) * n_sub + k)
+        for d in range(n_dom)
+        for k in range(n_sub)
+    ]
+    return lax.ppermute(x, ("dom", "sub"), pairs)
+
+
+def by_partner(slots, odd):
+    partners = slot_partners(len(slots), odd)
+    return slots[:1] + [slots[1 + partners.index(m)] for m in range(1, len(slots))]
+
+
+def for_each_order(place, body):
+    for odd in range(2):
+        pl.when((place[SUB] & 1) == odd)(functools.partial(body, odd))
+
+
+def filter_kernel(n_dom, planes, rows, first, n_levels, place, *refs):
     levels, refs = refs[:n_levels], list(refs[n_levels:])
     given = None if first else refs.pop(0)
     ins, outs = refs[:n_dom], refs[n_dom : 2 * n_dom]
@@ -57,22 +82,26 @@
     mirrored = (place[ME] & 1) != 0
     plane_at = [jnp.where(mirrored, planes - 1 - i, i) for i in range(planes)]
 
-    for x in range(half_planes):
-        for half in range(2):
-            m, i = divmod(half * half_planes + x, planes)
-            part = slice(half * TOGETHER, (half + 1) * TOGETHER)
-            base = starts[m] + plane_at[i] * rows
-            for y in range(rows):
-                even[x, y, part] = ins[m][pl.ds(base + y, TOGETHER, stride=cells), :]
-                if first:
+    def take(odd):
+        blocks = by_partner(list(ins), odd)
+        for x in range(half_planes):
+            for half in range(2):
+                m, i = divmod(half * half_planes + x, planes)
+                part = slice(half * TOGETHER, (half + 1) * TOGETHER)
+                base = plane_at[i] * rows
+                for y in range(rows):
+                    even[x, y, part] = blocks[m][pl.ds(base + y, TOGETHER, stride=cells), :]
+                    if not first:
+                        continue
                     if m >= 3:
-                        level = levels[m - 3][pl.ds(plane_at[i] * rows + y, 1), :]
+                        level = levels[m - 3][pl.ds(base + y, 1), :]
                     else:
-                        level = ins[m][pl.ds(base + (TOGETHER * cells + y), 1), :]
+                        level = blocks[m][pl.ds(base + (TOGETHER * cells + y), 1), :]
                     diagonal[x, y, part] = jnp.broadcast_to(
                         (level + (SHIFT - CENTER_LEVEL)) * (2.0 * scale), (TOGETHER, lanes)
                     )
 
+    for_each_order(place, take)
     block = SUBLANES
     lane = lax.broadcasted_iota(jnp.int32, (block, SUBLANES, lanes), 2)
     at_start, at_end = lane == 0, lane == lanes - 1
@@ -111,16 +140,21 @@
         return carry
 
     lax.fori_loop(0, DEGREE // 2 - 1, two_steps, 0)
-    for m in range(n_dom):
-        for i in range(planes):
-            half, x = divmod(m * planes + i, half_planes)
-            part = slice(half * TOGETHER, (half + 1) * TOGETHER)
-            for y in range(rows):
-                here = slice(y * TOGETHER, (y + 1) * TOGETHER)
-                outs[m][plane_at[i], here, :] = even[x, y, part]
-
-
-def filter_orbitals(place, diagonal, levels, blocks, starts, planes, rows):
+
+    def give(odd):
+        blocks = by_partner(list(outs), odd)
+        for m in range(n_dom):
+            for i in range(planes):
+                half, x = divmod(m * planes + i, half_planes)
+                part = slice(half * TOGETHER, (half + 1) * TOGETHER)
+                for y in range(rows):
+                    here = slice(y * TOGETHER, (y + 1) * TOGETHER)
+                    blocks[m][plane_at[i], here, :] = even[x, y, part]
+
+    for_each_order(place, give)
+
+
+def filter_orbitals(place, diagonal, levels, blocks, planes, rows):
     n_dom = len(blocks)
     first = diagonal is None
     lanes = blocks[0].shape[1]
@@ -130,7 +164,7 @@
     given = [] if first else [diagonal]
     size = n_dom * planes * rows * TOGETHER * lanes
     return pl.pallas_call(
-        functools.partial(filter_kernel, n_dom, planes, rows, starts, first, len(levels)),
+        functools.partial(filter_kernel, n_dom, planes, rows, first, len(levels)),
         out_shape=[out] * n_dom + extra,
         in_specs=[SMEM] + [VMEM] * (len(levels) + n_dom + len(given)),
         out_specs=[VMEM] * (n_dom + len(extra)),
@@ -143,8 +177,17 @@
     )(place, *levels, *given, *blocks)
 
 
-def cell_first_kernel(n_band, place, *refs):
-    pieces, parts = refs[:-n_band], refs[-n_band:]
+def cell_first_kernel(n_band, chosen, place, *refs):
+    given, parts = list(refs[:-n_band]), refs[-n_band:]
+
+    def body(odd):
+        pieces = [by_partner(given, odd)[m] for m in chosen]
+        cell_first_pieces(place, pieces, parts)
+
+    for_each_order(place, body)
+
+
+def cell_first_pieces(place, pieces, parts):
     share = parts[0].shape[0]
     me = place[ME]
     together = SUBLANES // TOGETHER
@@ -167,12 +210,12 @@
                         part[first + k, pl.ds(row, SUBLANES), :] = tile
 
 
-def cell_first(place, n_band, pieces):
+def cell_first(place, n_band, chosen, pieces):
     rows, lanes = pieces[0].shape
-    orbitals = len(pieces) * TOGETHER
+    orbitals = len(chosen) * TOGETHER
     part = jax.ShapeDtypeStruct((rows // (TOGETHER * n_band), orbitals, lanes), jnp.float32)
     return pl.pallas_call(
-        functools.partial(cell_first_kernel, n_band),
+        functools.partial(cell_first_kernel, n_band, chosen),
         out_shape=[part] * n_band,
         in_specs=[SMEM] + [VMEM] * len(pieces),
         out_specs=[VMEM] * n_band,
@@ -181,13 +224,23 @@
     )(place, *pieces)
 
 
-def orbital_first_kernel(n_dom, which, place, *refs):
-    pieces, (out, laid_out, sems) = refs[: len(which)], refs[-3:]
+def orbital_first_kernel(n_dom, counts, which, place, *refs):
+    given, (out, laid_out, sems) = list(refs[: sum(counts)]), refs[-3:]
     cells = out.shape[1]
+
+    def body(odd):
+        pieces, at = [], 0
+        for count in counts:
+            some = given[at : at + count]
+            pieces.append(by_partner(some + [None] * (n_dom - count), odd))
+            at += count
+        for k, (at, chunk, m) in enumerate(which):
+            for t in range(TOGETHER):
+                laid_out[k * TOGETHER + t] = pieces[at][m][pl.ds(t, cells, stride=TOGETHER), :]
+
+    for_each_order(place, body)
     copies = []
-    for k, (chunk, m) in enumerate(which):
-        for t in range(TOGETHER):
-            laid_out[k * TOGETHER + t] = pieces[k][pl.ds(t, cells, stride=TOGETHER), :]
+    for k, (_, chunk, m) in enumerate(which):
         start = (chunk * n_dom + (place[ME] ^ m)) * TOGETHER
         copies.append(
             pltpu.make_async_copy(
@@ -201,20 +254,21 @@
         copy.wait()
 
 
-def orbital_first(place, n_dom, orbitals, pieces, which, onto=None):
-    rows, lanes = pieces[0].shape
+def orbital_first(place, n_dom, orbitals, chunks, which, onto=None):
+    rows, lanes = chunks[0][0].shape
     cells = rows // TOGETHER
     hbm = pl.BlockSpec(memory_space=pltpu.HBM)
+    pieces = [piece for chunk in chunks for piece in chunk]
     given = [] if onto is None else [onto]
     return pl.pallas_call(
-        functools.partial(orbital_first_kernel, n_dom, which),
+        functools.partial(orbital_first_kernel, n_dom, [len(x) for x in chunks], which),
         out_shape=jax.ShapeDtypeStruct((orbitals, cells, lanes), jnp.float32),
         in_specs=[SMEM] + [VMEM] * len(pieces) + [hbm] * len(given),
         out_specs=hbm,
         input_output_aliases={len(pieces) + 1: 0} if given else {},
         scratch_shapes=[
-            pltpu.VMEM((len(pieces) * TOGETHER, cells, lanes), jnp.float32),
-            pltpu.SemaphoreType.DMA((len(pieces),)),
+            pltpu.VMEM((len(which) * TOGETHER, cells, lanes), jnp.float32),
+            pltpu.SemaphoreType.DMA((len(which),)),
         ],
         compiler_params=params(8),
         name="orbital_first",
@@ -439,38 +493,36 @@
     def block(c, m):
         return lax.dynamic_slice_in_dim(flat, (c * n_dom + (me ^ m)) * size, size, 0)
 
-    def sent(x, m):
-        return swapped(x, "dom", n_dom, m)
-
-    own = []
-    for m in range(n_dom):
-        blocks = [block(c, m) for c in range(n_chunks)]
-        if m < 3:
-            blocks[0] = jnp.concatenate([blocks[0], levels], axis=0)
-        own.append(blocks)
-    near = sent(jnp.concatenate(own[1], axis=0), 1)
-    arrived = [[own[0][0], near] + [sent(own[m][0], m) for m in range(2, n_dom)]]
-    handed_on = [sent(arrived[0][2][size:], 1)] if n_dom > 3 else []
+    odd = lax.axis_index("sub") & 1
+    partners = [
+        jnp.where(odd == 1, b, a)
+        for a, b in zip(slot_partners(n_dom, 0), slot_partners(n_dom, 1))
+    ]
+    own = [block(c, 0) for c in range(n_chunks)]
+    own[0] = jnp.concatenate([own[0], levels], axis=0)
+    blocks = [block(0, m) for m in partners]
+    blocks[:2] = [jnp.concatenate([x, levels], axis=0) for x in blocks[:2]]
+    arrived = [own[:1] + [sent(x, slot) for slot, x in enumerate(blocks)]]
+    handed_on = []
+    if n_dom > 3:
+        far = jnp.where(odd == 1, arrived[0][1][size:], arrived[0][2][size:])
+        handed_on = [swapped(far, "dom", n_dom, 1)]
     for c in range(1, n_chunks):
-        far = [own[m][c] for m in range(2, n_dom)]
-        near, far = lax.optimization_barrier((near, far))
-        arrived.append([own[0][c], near] + [sent(x, m) for m, x in enumerate(far, start=2)])
+        blocks = [block(c, m) for m in partners]
+        arrived[0][1], blocks = lax.optimization_barrier((arrived[0][1], blocks))
+        arrived.append([own[c]] + [sent(x, slot) for slot, x in enumerate(blocks)])
+    place, projectors = lax.optimization_barrier((place, build(place)))
     diagonal = None
     done = []
     for c, blocks in enumerate(arrived):
-        starts = [0] * n_dom
-        starts[1] = c * size + (cells if c else 0)
         filtered = filter_orbitals(
-            place, diagonal, [] if c else handed_on, blocks, starts, planes, rows
+            place, diagonal, [] if c else handed_on, blocks, planes, rows
         )
         if diagonal is None:
             diagonal = filtered[n_dom]
         done.append(list(filtered[:n_dom]))
-        if c == 0:
-            done[0][0], place = lax.optimization_barrier((done[0][0], place))
-            place, projectors = lax.optimization_barrier((place, build(place)))
     return [
-        [(sent(x, m) if m else x).reshape(size, lanes) for m, x in enumerate(blocks)]
+        [(sent(x, at - 1) if at else x).reshape(size, lanes) for at, x in enumerate(blocks)]
         for blocks in done
     ], projectors
 
@@ -523,31 +575,29 @@
     if n_dom in (2, 4) and orbitals % (n_dom * TOGETHER) == 0 and planes * n_dom % 2 == 0:
         chunks, projectors = whole_columns(panel, potential, place, me, build)
         sooner = place
-        which = [(c, m) for c in range(len(chunks)) for m in range(n_dom)]
-        pieces = [chunks[c][m] for c, m in which]
+        which = [(c, c, m) for c in range(len(chunks)) for m in range(n_dom)]
         n_late = 2 if n_dom == 4 else 0
-        first = len(pieces) - n_late
-        filtered = orbital_first(place, n_dom, orbitals, pieces[:first], which[:first])
-        early, place = lax.optimization_barrier((filtered, place))
+        sooner = chunks[:-1] + [chunks[-1][: n_dom - n_late // 2]]
+        count = len(which) - n_late
+        filtered = orbital_first(place, n_dom, orbitals, sooner, which[:count])
+        written, later = lax.optimization_barrier((filtered, place))
+        parts = [cell_first(place, n_band, range(n_dom), pieces) for pieces in chunks[:-1]]
+        tiles = [[c] for c in range(len(chunks))]
         if n_late:
             filtered = orbital_first(
-                place, n_dom, orbitals, pieces[first:], which[first:], early
+                place, n_dom, orbitals, chunks[-1:], [(0,) + x[1:] for x in which[count:]], written
             )
-        parts = [cell_first(sooner, n_band, pieces) for pieces in chunks[:-1]]
-        tiles = [[c] for c in range(len(chunks))]
-        last = [chunks[-1]]
-        if n_dom == 4:
-            last = [chunks[-1][:2], chunks[-1][2:]]
             tiles[-1].append(len(chunks))
-        if len(parts) and len(last) == 2:
-            parts[-1], last[0] = lax.optimization_barrier((parts[-1], last[0]))
-        parts.append(cell_first(place, n_band, last[0]))
-        if len(last) == 2:
-            near = parts[-1]
+            pieces = sooner[-1]
+            if parts:
+                parts[-1], pieces = lax.optimization_barrier((parts[-1], pieces))
+            near = cell_first(later, n_band, (0, 1), pieces)
             crossed = [swapped(x, "band", n_band, m) if m else x for m, x in enumerate(near)]
-            crossed, last[1] = lax.optimization_barrier((crossed, last[1]))
-            parts.append(cell_first(place, n_band, last[1]))
-            parts[-2] = crossed
+            crossed, pieces = lax.optimization_barrier((crossed, chunks[-1]))
+            parts.append(crossed)
+            parts.append(cell_first(later, n_band, (2, 3), pieces))
+        else:
+            parts.append(cell_first(later, n_band, range(n_dom), chunks[-1]))
     else:
         projectors = build(place)
         filtered = plane_by_plane(panel, potential)

time: 119 us -> 131 us (1.10)
  waiting for transfers between devices: 40.2 us -> 46.2 us
  starting transfers between devices: 35.7 us -> 39.8 us
    ppermute x0 -> x12, waiting for transfers between devices: none -> 25.3 us  [sent(): return lax.ppermute(x, ('dom', 'sub'), pairs)]
    ppermute x0 -> x12, starting transfers between devices: none -> 19.7 us  [sent(): return lax.ppermute(x, ('dom', 'sub'), pairs)]
    ppermute x25 -> x14, waiting for transfers between devices: 36.5 us -> 17.2 us  [swapped(): return lax.ppermute(x, axes, [(i, i ^ by) for i in range(size)])]
    ppermute x25 -> x14, starting transfers between devices: 27.1 us -> 13.4 us  [swapped(): return lax.ppermute(x, axes, [(i, i ^ by) for i in range(size)])]
    ppermute x5, starting transfers between devices: 8.66 us -> 6.74 us  [on_device(): sums.append(lax.ppermute(x, ('dom', 'band'), pairs))]
    pallas_call x7, Pallas kernels: 18 us -> 19.4 us  [the longest x2 14.5 us: filter_orbitals(): pl.pallas_call(functools.partial(filter_kernel, n_dom, planes, rows, firs...]
  transfers between devices with their start and end apart: 30 -> 31, of which waited for: 11 -> 12; matrix products, arithmetic and copies ran while one was open for 1% -> 2% of each run, Pallas kernels for 26% -> 25%
where the time goes in v13:
time: 131 us
  waiting for transfers between devices  46.2 us (35%)
  starting transfers between devices  39.8 us (30%)
  Pallas kernels  38.6 us (29%)
  local copies, waits for them, and re-layouts  2.83 us (2%)
  other arithmetic  2.25 us (2%)
    ppermute x12, waiting for transfers between devices, sent(): return lax.ppermute(x, ('dom', 'sub'), pairs)  25.3 us
    ppermute x12, starting transfers between devices, sent(): return lax.ppermute(x, ('dom', 'sub'), pairs)  19.7 us
    ppermute x14, waiting for transfers between devices, swapped(): return lax.ppermute(x, axes, [(i, i ^ by) for i in range(size)])  17.2 us
    pallas_call x2, Pallas kernels, filter_orbitals(): pl.pallas_call(functools.partial(filter_kernel, n_dom, planes, rows, firs...  14.5 us
    ppermute x14, starting transfers between devices, swapped(): return lax.ppermute(x, axes, [(i, i ^ by) for i in range(size)])  13.4 us
    pallas_call x1, Pallas kernels, build_projectors(): pl.pallas_call(functools.partial(projector_kernel, n_band, n_sub), out_sh...  11.5 us
    ppermute x5, starting transfers between devices, on_device(): sums.append(lax.ppermute(x, ('dom', 'band'), pairs))  6.74 us
    pallas_call x1, Pallas kernels, products(): pl.pallas_call(functools.partial(product_kernel, spots, n_blocks), out_sh...  5.07 us
  transfers between devices with their start and end apart: 31, of which 12 were waited for; matrix products, arithmetic and copies ran while one was open for 2% of the time, Pallas kernels for 25%

profile of v13, /device:TPU:0, one launch (start us, length us, event | category | flops | bytes accessed | tf_op | source)
XLA Modules:
  0.0 130.5 jit_solution(14491990411244031773)
XLA Ops:
  0.6 0.0 copy-start
  0.7 2.3 %constant_dynamic-slice_fusion = (f32[384,128]{1,0:T(8,128)S(1)}, f32[384,128]{1,0:T(8,128)}, f32[384,128]{1,0:T(8,128)S(1)}, f32[384,128]{1,0:T(8,128)S(1)}, f3...) fusion(f32[3072,128]{1,0:T(8,128)} %bitcast.40, s32[]{:T(128)S(6)} %select_n.55, ...), kind=kLoop, calls=%fused_computation.10 | loop fusion | bytes 3145760 | tf_op jit(solution)/shard_map/dynamic_slice | solution.py:494
  3.1 0.1 pad_maximum_fusion.1
  3.1 4.1 %collective-permute-start.1 = (f32[480,128]{1,0:T(8,128)S(1)}, f32[480,128]{1,0:T(8,128)S(1)}, u32[]{:S(2)}, u32[]{:S(2)}) collective-permute-start(f32[480,128]{1,0:T(8,128)S(1)} %get-tuple-element.121), channel_id=1, source_target_pairs={{0,8},{1,5},{4,12},{5,1},{8,0},{9,13},{12,4},{13,9},{2,10},{3,7},{... | collective-permute-start | bytes 737288 | tf_op jit(solution)/shard_map/ppermute | solution.py:58
  7.2 1.6 %collective-permute-start = (f32[480,128]{1,0:T(8,128)S(1)}, f32[480,128]{1,0:T(8,128)S(1)}, u32[]{:S(2)}, u32[]{:S(2)}) collective-permute-start(f32[480,128]{1,0:T(8,128)S(1)} %get-tuple-element.122), channel_id=1, source_target_pairs={{0,4},{1,9},{4,0},{5,13},{8,12},{9,1},{12,8},{13,5},{2,6},{3,11},{... | collective-permute-start | bytes 737288 | tf_op jit(solution)/shard_map/ppermute | solution.py:58
  8.8 0.6 fusion
  9.4 0.1 constant_dynamic-slice_fusion.8
  9.5 0.1 copy.9
  9.6 0.8 broadcast_multiply_fusion
  10.4 0.3 mul.56.corr_ref
  10.7 0.1 pad_add_fusion.place
  10.8 8.0 %collective-permute-done.refs_2_ = f32[480,128]{1,0:T(8,128)S(1)} collective-permute-done((f32[480,128]{1,0:T(8,128)S(1)}, f32[480,128]{1,0:T(8,128)S(1)}, u32[]{:S(2)}, u32[]{:S(2)}) %collective-permute-start) | collective-permute-done | bytes 245792 | tf_op jit(solution)/shard_map/ppermute | solution.py:58
  18.8 2.5 %collective-permute-start.4 = (f32[384,128]{1,0:T(8,128)}, f32[384,128]{1,0:T(8,128)S(1)}, u32[]{:S(2)}, u32[]{:S(2)}) collective-permute-start(f32[384,128]{1,0:T(8,128)} %get-tuple-element.63), channel_id=1, source_target_pairs={{0,4},{1,9},{4,0},{5,13},{8,12},{9,1},{12,8},{13,5},{2,6},{3,11},{... | collective-permute-start | bytes 589832 | tf_op jit(solution)/shard_map/ppermute | solution.py:58
  21.3 0.0 collective-permute-start.5
  21.3 2.4 %collective-permute-start.6 = (f32[384,128]{1,0:T(8,128)S(1)}, f32[384,128]{1,0:T(8,128)S(1)}, u32[]{:S(2)}, u32[]{:S(2)}) collective-permute-start(f32[384,128]{1,0:T(8,128)S(1)} %get-tuple-element.65), channel_id=1, source_target_pairs={{0,12},{1,13},{4,8},{5,9},{8,4},{9,5},{12,0},{13,1},{2,14},{3,15},... | collective-permute-start | bytes 589832 | tf_op jit(solution)/shard_map/ppermute | solution.py:58
  23.7 0.0 collective-permute-done.1.refs_3_
  23.7 1.2 collective-permute-start.2
  24.9 11.5 %projectors.1 = (bf16[576,6144]{1,0:T(8,128)(2,1)S(1)}, bf16[576,6144]{1,0:T(8,128)(2,1)S(1)}) custom-call(s32[4]{0:T(128)S(1)} %pad_add_fusion.place, s32[3,48,128]{2,1,0:T(8,128)S(1)} %bitcast.38, f32[48,3,8,128]{3,2,1,0:T(8,128)S(1)} %copy-done.1), custom_call_target="tpu_custom_call" | custom-call | flops 1811939328 | bytes 28311552 | tf_op jit(solution)/shard_map/projectors/pallas_call | solution.py:329
  36.4 0.0 collective-permute-done.3.refs_4_
  36.4 7.5 %chebyshev.2 = (f32[3,128,128]{2,1,0:T(8,128)S(1)}, f32[3,128,128]{2,1,0:T(8,128)S(1)}, f32[3,128,128]{2,1,0:T(8,128)S(1)}, f32[3,128,128]{2,1,0:T(8,128)S(1)}, f32[6,32,8,128]{3,2,1,0:T(8,128)S(1)}) custom-call(s32[4]{0:T(128)S(1)} %pad_add_fusion.place, f32[96,128]{1,0:T(8,128)S(1)} %collective-permute-done.2.refs_0_, ...), custom_call_target="tpu_custom_call" | custom-call | flops 28311552 | bytes 1572864 | tf_op jit(solution)/shard_map/chebyshev/pallas_call | solution.py:166
  43.9 1.0 collective-permute-start.10
  44.8 2.3 %collective-permute-start.11 = (f32[3,128,128]{2,1,0:T(8,128)S(1)}, f32[3,128,128]{2,1,0:T(8,128)S(1)}, u32[]{:S(2)}, u32[]{:S(2)}) collective-permute-start(f32[3,128,128]{2,1,0:T(8,128)S(1)} %get-tuple-element.72), channel_id=1, source_target_pairs={{0,8},{1,5},{4,12},{5,1},{8,0},{9,13},{12,4},{13,9},{2,10},{3,7},{... | collective-permute-start | bytes 589832 | tf_op jit(solution)/shard_map/ppermute | solution.py:58
  47.1 1.4 %collective-permute-start.12 = (f32[3,128,128]{2,1,0:T(8,128)S(1)}, f32[3,128,128]{2,1,0:T(8,128)S(1)}, u32[]{:S(2)}, u32[]{:S(2)}) collective-permute-start(f32[3,128,128]{2,1,0:T(8,128)S(1)} %get-tuple-element.73), channel_id=1, source_target_pairs={{0,12},{1,13},{4,8},{5,9},{8,4},{9,5},{12,0},{13,1},{2,14},{3,15},... | collective-permute-start | bytes 589832 | tf_op jit(solution)/shard_map/ppermute | solution.py:58
  48.5 7.0 %chebyshev.3 = (f32[3,128,128]{2,1,0:T(8,128)S(1)}, f32[3,128,128]{2,1,0:T(8,128)S(1)}, f32[3,128,128]{2,1,0:T(8,128)S(1)}, f32[3,128,128]{2,1,0:T(8,128)S(1)}) custom-call(s32[4]{0:T(128)S(1)} %pad_add_fusion.place, f32[6,32,8,128]{3,2,1,0:T(8,128)S(1)} %get-tuple-element.62.refs_0_, f32[384,128]{1,0:T(8,128)S(1)} %get-tuple-element.112.refs_1_, ...), custom_call_target="tpu_custom_call" | custom-call | flops 28311552 | bytes 1572864 | tf_op jit(solution)/shard_map/chebyshev/pallas_call | solution.py:166
  55.6 0.6 collective-permute-start.7
  56.2 2.4 %collective-permute-start.8 = (f32[3,128,128]{2,1,0:T(8,128)S(1)}, f32[3,128,128]{2,1,0:T(8,128)S(1)}, u32[]{:S(2)}, u32[]{:S(2)}) collective-permute-start(f32[3,128,128]{2,1,0:T(8,128)S(1)} %get-tuple-element.68), channel_id=1, source_target_pairs={{0,8},{1,5},{4,12},{5,1},{8,0},{9,13},{12,4},{13,9},{2,10},{3,7},{... | collective-permute-start | bytes 589832 | tf_op jit(solution)/shard_map/ppermute | solution.py:58
  58.6 1.4 %collective-permute-start.9 = (f32[3,128,128]{2,1,0:T(8,128)S(1)}, f32[3,128,128]{2,1,0:T(8,128)S(1)}, u32[]{:S(2)}, u32[]{:S(2)}) collective-permute-start(f32[3,128,128]{2,1,0:T(8,128)S(1)} %get-tuple-element.69), channel_id=1, source_target_pairs={{0,12},{1,13},{4,8},{5,9},{8,4},{9,5},{12,0},{13,1},{2,14},{3,15},... | collective-permute-start | bytes 589832 | tf_op jit(solution)/shard_map/ppermute | solution.py:58
  60.0 1.5 %collective-permute-done.12 = f32[3,128,128]{2,1,0:T(8,128)S(1)} collective-permute-done((f32[3,128,128]{2,1,0:T(8,128)S(1)}, f32[3,128,128]{2,1,0:T(8,128)S(1)}, u32[]{:S(2)}, u32[]{:S(2)}) %collective-permute-start.12) | collective-permute-done | bytes 196640 | tf_op jit(solution)/shard_map/ppermute | solution.py:58
  61.5 0.7 cell_first.3
  62.2 4.5 %collective-permute-done.7 = f32[3,128,128]{2,1,0:T(8,128)S(1)} collective-permute-done((f32[3,128,128]{2,1,0:T(8,128)S(1)}, f32[3,128,128]{2,1,0:T(8,128)S(1)}, u32[]{:S(2)}, u32[]{:S(2)}) %collective-permute-start.7) | collective-permute-done | bytes 196640 | tf_op jit(solution)/shard_map/ppermute | solution.py:58
  66.6 11.3 %collective-permute-done.8 = f32[3,128,128]{2,1,0:T(8,128)S(1)} collective-permute-done((f32[3,128,128]{2,1,0:T(8,128)S(1)}, f32[3,128,128]{2,1,0:T(8,128)S(1)}, u32[]{:S(2)}, u32[]{:S(2)}) %collective-permute-start.8) | collective-permute-done | bytes 196640 | tf_op jit(solution)/shard_map/ppermute | solution.py:58
  77.9 1.7 %orbital_first.2.refs_4_ = f32[32,96,128]{2,1,0:T(8,128)} custom-call(s32[4]{0:T(128)S(1)} %pad_add_fusion.place, f32[384,128]{1,0:T(8,128)S(1)} %bitcast.31, f32[384,128]{1,0:T(8,128)S(1)} %bitcast.33, f32[384,128]{1,0:T(8,128)S(1)} %bitcast.35, f32[384,128]{1,0:T(8,128)S(1)} %bitcast.37, f32[384,128]{1,0:T(8,128)S(1)} %bitcast.16, ...), custom_call_target="tpu_custom_call" | custom-call | tf_op jit(solution)/shard_map/orbital_first/pallas_call | solution.py:263
  79.6 0.6 cell_first.4
  80.2 1.6 %collective-permute-start.13 = (f32[48,8,128]{2,1,0:T(8,128)S(1)}, f32[48,8,128]{2,1,0:T(8,128)S(1)}, u32[]{:S(2)}, u32[]{:S(2)}) collective-permute-start(f32[48,8,128]{2,1,0:T(8,128)S(1)} %get-tuple-element.85), channel_id=1, source_target_pairs={{0,2},{2,0},{1,3},{3,1},{4,6},{6,4},{5,7},{7,5},{8,10},{10,8},{9,1... | collective-permute-start | bytes 589832 | tf_op jit(solution)/shard_map/ppermute | solution.py:43
  81.8 0.5 collective-permute-start.14
  82.3 5.2 %collective-permute-done.13.refs_4_ = f32[48,8,128]{2,1,0:T(8,128)S(1)} collective-permute-done((f32[48,8,128]{2,1,0:T(8,128)S(1)}, f32[48,8,128]{2,1,0:T(8,128)S(1)}, u32[]{:S(2)}, u32[]{:S(2)}) %collective-permute-start.13) | collective-permute-done | bytes 196640 | tf_op jit(solution)/shard_map/ppermute | solution.py:43
  87.5 0.6 cell_first.5
  88.2 0.1 pad_maximum_fusion
  88.2 1.3 collective-permute-start.16
  89.5 1.5 %collective-permute-start.15 = (f32[48,8,128]{2,1,0:T(8,128)S(1)}, f32[48,8,128]{2,1,0:T(8,128)S(1)}, u32[]{:S(2)}, u32[]{:S(2)}) collective-permute-start(f32[48,8,128]{2,1,0:T(8,128)S(1)} %get-tuple-element.94), channel_id=1, source_target_pairs={{0,2},{2,0},{1,3},{3,1},{4,6},{6,4},{5,7},{7,5},{8,10},{10,8},{9,1... | collective-permute-start | bytes 589832 | tf_op jit(solution)/shard_map/ppermute | solution.py:43
  91.0 5.0 %collective-permute-done.14.refs_3_ = f32[48,16,128]{2,1,0:T(8,128)S(1)} collective-permute-done((f32[48,16,128]{2,1,0:T(8,128)S(1)}, f32[48,16,128]{2,1,0:T(8,128)S(1)}, u32[]{:S(2)}, u32[]{:S(2)}) %collective-permute-start.14) | collective-permute-done | bytes 393248 | tf_op jit(solution)/shard_map/ppermute | solution.py:43
  96.0 1.2 collective-permute-start.17
  97.2 0.0 collective-permute-start.18
  97.2 3.0 %collective-permute-done.15.refs_5_ = f32[48,8,128]{2,1,0:T(8,128)S(1)} collective-permute-done((f32[48,8,128]{2,1,0:T(8,128)S(1)}, f32[48,8,128]{2,1,0:T(8,128)S(1)}, u32[]{:S(2)}, u32[]{:S(2)}) %collective-permute-start.15) | collective-permute-done | bytes 196640 | tf_op jit(solution)/shard_map/ppermute | solution.py:43
  100.2 0.4 collective-permute-start.19
  100.6 1.1 collective-permute-done.19.refs_9_
  101.6 5.1 %products.1 = (f32[96,128]{1,0:T(8,128)S(1)}, f32[96,128]{1,0:T(8,128)S(1)}, f32[96,128]{1,0:T(8,128)S(1)}, f32[96,128]{1,0:T(8,128)S(1)}, f32[96,128]{1,0:T(8,128)S(1)}, /*index=5*/f32[96,128]{1,0:T(8,128)S(1)}) custom-call(s32[4]{0:T(128)S(1)} %pad_add_fusion.place, bf16[576,6144]{1,0:T(8,128)(2,1)S(1)} %get-tuple-element.75.w_high, ...), custom_call_target="tpu_custom_call" | custom-call | tf_op jit(solution)/shard_map/products/pallas_call | solution.py:391
  106.7 2.3 %collective-permute-start.20 = (f32[96,128]{1,0:T(8,128)S(1)}, f32[96,128]{1,0:T(8,128)S(1)}, u32[]{:S(2)}, u32[]{:S(2)}) collective-permute-start(f32[96,128]{1,0:T(8,128)S(1)} %get-tuple-element.103), channel_id=1, source_target_pairs={{0,12},{2,14},{4,0},{6,2},{8,4},{10,6},{12,8},{14,10},{1,13},{3,15... | collective-permute-start | bytes 147464 | tf_op jit(solution)/shard_map/ppermute | solution.py:660
  109.1 1.0 collective-permute-start.21
  110.0 2.0 %collective-permute-start.22 = (f32[96,128]{1,0:T(8,128)S(1)}, f32[96,128]{1,0:T(8,128)S(1)}, u32[]{:S(2)}, u32[]{:S(2)}) collective-permute-start(f32[96,128]{1,0:T(8,128)S(1)} %get-tuple-element.105), channel_id=1, source_target_pairs={{0,4},{2,6},{4,8},{6,10},{8,12},{10,14},{12,0},{14,2},{1,5},{3,7},... | collective-permute-start | bytes 147464 | tf_op jit(solution)/shard_map/ppermute | solution.py:660
  112.0 1.5 %collective-permute-start.24 = (f32[96,128]{1,0:T(8,128)S(1)}, f32[96,128]{1,0:T(8,128)S(1)}, u32[]{:S(2)}, u32[]{:S(2)}) collective-permute-start(f32[96,128]{1,0:T(8,128)S(1)} %get-tuple-element.107), channel_id=1, source_target_pairs={{0,2},{2,0},{4,6},{6,4},{8,10},{10,8},{12,14},{14,12},{1,3},{3,1},... | collective-permute-start | bytes 147464 | tf_op jit(solution)/shard_map/ppermute | solution.py:660
  113.4 1.6 %grid_sums.1.grid_ref = f32[128,128]{1,0:T(8,128)S(1)} custom-call(s32[4]{0:T(128)S(1)} %pad_add_fusion.place, f32[48,16,128]{2,1,0:T(8,128)S(1)} %get-tuple-element.79.refs_0_, f32[48,8,128]{2,1,0:T(8,128)S(1)} %get-tuple-element.86.refs_1_, f32[48,8,128]{2,1,0:T(8,128)S(1)} %get-tuple-element.91.refs_2_, ...), custom_call_target="tpu_custom_call" | custom-call | tf_op jit(solution)/shard_map/grid_sums/pallas_call | solution.py:417
  115.1 1.1 collective-permute-done.22.refs_2_
  116.2 2.6 %collective-permute-done.23.refs_3_ = f32[96,128]{1,0:T(8,128)S(1)} collective-permute-done((f32[96,128]{1,0:T(8,128)S(1)}, f32[96,128]{1,0:T(8,128)S(1)}, u32[]{:S(2)}, u32[]{:S(2)}) %collective-permute-start.23) | collective-permute-done | bytes 49184 | tf_op jit(solution)/shard_map/ppermute | solution.py:660
  118.8 1.1 gram_share.1
  119.9 0.6 collective-permute-start.26
  120.5 1.6 %collective-permute-start.25 = (f32[32,128]{1,0:T(8,128)S(1)}, f32[32,128]{1,0:T(8,128)S(1)}, u32[]{:S(2)}, u32[]{:S(2)}) collective-permute-start(f32[32,128]{1,0:T(8,128)S(1)} %get-tuple-element.109), channel_id=1, source_target_pairs={{0,1},{1,0},{2,3},{3,2},{4,5},{5,4},{6,7},{7,6},{8,9},{9,8},{10,11... | collective-permute-start | bytes 49160 | tf_op jit(solution)/shard_map/ppermute | solution.py:43
  122.1 1.8 %collective-permute-done.26 = f32[32,128]{1,0:T(8,128)S(1)} collective-permute-done((f32[32,128]{1,0:T(8,128)S(1)}, f32[32,128]{1,0:T(8,128)S(1)}, u32[]{:S(2)}, u32[]{:S(2)}) %collective-permute-start.26) | collective-permute-done | bytes 16416 | tf_op jit(solution)/shard_map/ppermute | solution.py:43
  123.9 0.5 collective-permute-start.29
  124.4 1.5 %collective-permute-start.30 = (f32[32,128]{1,0:T(8,128)S(1)}, f32[32,128]{1,0:T(8,128)S(1)}, u32[]{:S(2)}, u32[]{:S(2)}) collective-permute-start(f32[32,128]{1,0:T(8,128)S(1)} %add_add_fusion.1), channel_id=1, source_target_pairs={{0,12},{4,8},{8,4},{12,0},{1,13},{5,9},{9,5},{13,1},{2,14},{6,10},... | collective-permute-start | bytes 49160 | tf_op jit(solution)/shard_map/ppermute | solution.py:43
  125.9 1.6 %collective-permute-start.28 = (f32[32,128]{1,0:T(8,128)S(1)}, f32[32,128]{1,0:T(8,128)S(1)}, u32[]{:S(2)}, u32[]{:S(2)}) collective-permute-start(f32[32,128]{1,0:T(8,128)S(1)} %add_add_fusion.1), channel_id=1, source_target_pairs={{0,4},{4,0},{8,12},{12,8},{1,5},{5,1},{9,13},{13,9},{2,6},{6,2},{1... | collective-permute-start | bytes 49160 | tf_op jit(solution)/shard_map/ppermute | solution.py:43
  127.4 1.3 %orbital_first.3 = f32[32,96,128]{2,1,0:T(8,128)} custom-call(s32[4]{0:T(128)S(1)} %pad_add_fusion.place, f32[384,128]{1,0:T(8,128)S(1)} %bitcast.19, f32[384,128]{1,0:T(8,128)S(1)} %bitcast.23, f32[384,128]{1,0:T(8,128)S(1)} %bitcast.27, f32[384,128]{1,0:T(8,128)S(1)} %bitcast.29, f32[32,96,128]{2,1,0:T(8,128)} %orbital_first.2.refs_4_), custom_call_target="tpu_custom_call", output_to_operand_aliasing={{}: (5, {})} | custom-call | tf_op jit(solution)/shard_map/orbital_first/pallas_call | solution.py:263
  128.8 1.1 collective-permute-done.30
  129.9 0.6 add_add_fusion
  (29 shorter events, 0.1 us)
Async XLA Ops:
  0.6 8.8 %copy-start = (f32[48,8,8]{0,2,1:T(8,128)S(1)}, f32[48,8,8]{0,2,1:T(8,128)}, u32[]{:S(2)}) copy-start(f32[48,8,8]{0,2,1:T(8,128)} %param.9) | copy-start | bytes 36868
  0.7 2.3 %copy-start.3 = (f32[3,32,128]{2,1,0:T(8,128)S(1)}, f32[3,32,128]{2,1,0:T(8,128)}, u32[]{:S(2)}) copy-start(f32[3,32,128]{2,1,0:T(8,128)} %param.6) | copy-start | bytes 147460
  3.0 21.8 %copy-start.1 = (f32[48,3,8,128]{3,2,1,0:T(8,128)S(1)}, f32[48,3,8,128]{3,2,1,0:T(8,128)}, u32[]{:S(2)}) copy-start(f32[48,3,8,128]{3,2,1,0:T(8,128)} %coefs_ref.1) | copy-start | bytes 1769476
  3.0 21.8 %copy-start.2 = (s32[48,3,128]{2,0,1:T(8,128)S(1)}, s32[48,3,128]{2,0,1:T(8,128)}, u32[]{:S(2)}) copy-start(s32[48,3,128]{2,0,1:T(8,128)} %param.7) | copy-start | bytes 221188
  3.1 20.6 %collective-permute-start.1 = (f32[480,128]{1,0:T(8,128)S(1)}, f32[480,128]{1,0:T(8,128)S(1)}, u32[]{:S(2)}, u32[]{:S(2)}) collective-permute-start(f32[480,128]{1,0:T(8,128)S(1)} %get-tuple-element.121), channel_id=1, source_target_pairs={{0,8},{1,5},{4,12},{5,1},{8,0},{9,13},{12,4},{13,9},{2,10},{3,7},{... | collective-permute-start | bytes 737288 | tf_op jit(solution)/shard_map/ppermute | solution.py:58
  7.2 11.6 %collective-permute-start = (f32[480,128]{1,0:T(8,128)S(1)}, f32[480,128]{1,0:T(8,128)S(1)}, u32[]{:S(2)}, u32[]{:S(2)}) collective-permute-start(f32[480,128]{1,0:T(8,128)S(1)} %get-tuple-element.122), channel_id=1, source_target_pairs={{0,4},{1,9},{4,0},{5,13},{8,12},{9,1},{12,8},{13,5},{2,6},{3,11},{... | collective-permute-start | bytes 737288 | tf_op jit(solution)/shard_map/ppermute | solution.py:58
  8.8 27.6 %collective-permute-start.3 = (f32[384,128]{1,0:T(8,128)}, f32[384,128]{1,0:T(8,128)S(1)}, u32[]{:S(2)}, u32[]{:S(2)}) collective-permute-start(f32[384,128]{1,0:T(8,128)} %get-tuple-element.113), channel_id=1, source_target_pairs={{0,12},{1,13},{4,8},{5,9},{8,4},{9,5},{12,0},{13,1},{2,14},{3,15},... | collective-permute-start | bytes 589832 | tf_op jit(solution)/shard_map/ppermute | solution.py:58
  18.8 28.3 %collective-permute-start.4 = (f32[384,128]{1,0:T(8,128)}, f32[384,128]{1,0:T(8,128)S(1)}, u32[]{:S(2)}, u32[]{:S(2)}) collective-permute-start(f32[384,128]{1,0:T(8,128)} %get-tuple-element.63), channel_id=1, source_target_pairs={{0,4},{1,9},{4,0},{5,13},{8,12},{9,1},{12,8},{13,5},{2,6},{3,11},{... | collective-permute-start | bytes 589832 | tf_op jit(solution)/shard_map/ppermute | solution.py:58
  21.3 27.2 %collective-permute-start.5 = (f32[384,128]{1,0:T(8,128)S(1)}, f32[384,128]{1,0:T(8,128)S(1)}, u32[]{:S(2)}, u32[]{:S(2)}) collective-permute-start(f32[384,128]{1,0:T(8,128)S(1)} %get-tuple-element.64), channel_id=1, source_target_pairs={{0,8},{1,5},{4,12},{5,1},{8,0},{9,13},{12,4},{13,9},{2,10},{3,7},{... | collective-permute-start | bytes 589832 | tf_op jit(solution)/shard_map/ppermute | solution.py:58
  21.3 27.2 %collective-permute-start.6 = (f32[384,128]{1,0:T(8,128)S(1)}, f32[384,128]{1,0:T(8,128)S(1)}, u32[]{:S(2)}, u32[]{:S(2)}) collective-permute-start(f32[384,128]{1,0:T(8,128)S(1)} %get-tuple-element.65), channel_id=1, source_target_pairs={{0,12},{1,13},{4,8},{5,9},{8,4},{9,5},{12,0},{13,1},{2,14},{3,15},... | collective-permute-start | bytes 589832 | tf_op jit(solution)/shard_map/ppermute | solution.py:58
  23.7 12.7 %collective-permute-start.2 = (f32[96,128]{1,0:T(8,128)S(1)}, f32[96,128]{1,0:T(8,128)S(1)}, u32[]{:S(2)}, u32[]{:S(2)}) collective-permute-start(f32[96,128]{1,0:T(8,128)S(1)} %slice_select_fusion), channel_id=1, source_target_pairs={{0,4},{4,0},{8,12},{12,8},{1,5},{5,1},{9,13},{13,9},{2,6},{6,2},{1... | collective-permute-start | bytes 147464 | tf_op jit(solution)/shard_map/ppermute | solution.py:43
  43.9 14.8 %collective-permute-start.10 = (f32[3,128,128]{2,1,0:T(8,128)S(1)}, f32[3,128,128]{2,1,0:T(8,128)S(1)}, u32[]{:S(2)}, u32[]{:S(2)}) collective-permute-start(f32[3,128,128]{2,1,0:T(8,128)S(1)} %get-tuple-element.71), channel_id=1, source_target_pairs={{0,4},{1,9},{4,0},{5,13},{8,12},{9,1},{12,8},{13,5},{2,6},{3,11},{... | collective-permute-start | bytes 589832 | tf_op jit(solution)/shard_map/ppermute | solution.py:58
  44.8 15.2 %collective-permute-start.11 = (f32[3,128,128]{2,1,0:T(8,128)S(1)}, f32[3,128,128]{2,1,0:T(8,128)S(1)}, u32[]{:S(2)}, u32[]{:S(2)}) collective-permute-start(f32[3,128,128]{2,1,0:T(8,128)S(1)} %get-tuple-element.72), channel_id=1, source_target_pairs={{0,8},{1,5},{4,12},{5,1},{8,0},{9,13},{12,4},{13,9},{2,10},{3,7},{... | collective-permute-start | bytes 589832 | tf_op jit(solution)/shard_map/ppermute | solution.py:58
  47.1 14.4 %collective-permute-start.12 = (f32[3,128,128]{2,1,0:T(8,128)S(1)}, f32[3,128,128]{2,1,0:T(8,128)S(1)}, u32[]{:S(2)}, u32[]{:S(2)}) collective-permute-start(f32[3,128,128]{2,1,0:T(8,128)S(1)} %get-tuple-element.73), channel_id=1, source_target_pairs={{0,12},{1,13},{4,8},{5,9},{8,4},{9,5},{12,0},{13,1},{2,14},{3,15},... | collective-permute-start | bytes 589832 | tf_op jit(solution)/shard_map/ppermute | solution.py:58
  55.6 11.1 %collective-permute-start.7 = (f32[3,128,128]{2,1,0:T(8,128)S(1)}, f32[3,128,128]{2,1,0:T(8,128)S(1)}, u32[]{:S(2)}, u32[]{:S(2)}) collective-permute-start(f32[3,128,128]{2,1,0:T(8,128)S(1)} %get-tuple-element.67), channel_id=1, source_target_pairs={{0,4},{1,9},{4,0},{5,13},{8,12},{9,1},{12,8},{13,5},{2,6},{3,11},{... | collective-permute-start | bytes 589832 | tf_op jit(solution)/shard_map/ppermute | solution.py:58
  56.2 21.7 %collective-permute-start.8 = (f32[3,128,128]{2,1,0:T(8,128)S(1)}, f32[3,128,128]{2,1,0:T(8,128)S(1)}, u32[]{:S(2)}, u32[]{:S(2)}) collective-permute-start(f32[3,128,128]{2,1,0:T(8,128)S(1)} %get-tuple-element.68), channel_id=1, source_target_pairs={{0,8},{1,5},{4,12},{5,1},{8,0},{9,13},{12,4},{13,9},{2,10},{3,7},{... | collective-permute-start | bytes 589832 | tf_op jit(solution)/shard_map/ppermute | solution.py:58
  58.6 23.7 %collective-permute-start.9 = (f32[3,128,128]{2,1,0:T(8,128)S(1)}, f32[3,128,128]{2,1,0:T(8,128)S(1)}, u32[]{:S(2)}, u32[]{:S(2)}) collective-permute-start(f32[3,128,128]{2,1,0:T(8,128)S(1)} %get-tuple-element.69), channel_id=1, source_target_pairs={{0,12},{1,13},{4,8},{5,9},{8,4},{9,5},{12,0},{13,1},{2,14},{3,15},... | collective-permute-start | bytes 589832 | tf_op jit(solution)/shard_map/ppermute | solution.py:58
  80.2 7.3 %collective-permute-start.13 = (f32[48,8,128]{2,1,0:T(8,128)S(1)}, f32[48,8,128]{2,1,0:T(8,128)S(1)}, u32[]{:S(2)}, u32[]{:S(2)}) collective-permute-start(f32[48,8,128]{2,1,0:T(8,128)S(1)} %get-tuple-element.85), channel_id=1, source_target_pairs={{0,2},{2,0},{1,3},{3,1},{4,6},{6,4},{5,7},{7,5},{8,10},{10,8},{9,1... | collective-permute-start | bytes 589832 | tf_op jit(solution)/shard_map/ppermute | solution.py:43
  81.8 14.2 %collective-permute-start.14 = (f32[48,16,128]{2,1,0:T(8,128)S(1)}, f32[48,16,128]{2,1,0:T(8,128)S(1)}, u32[]{:S(2)}, u32[]{:S(2)}) collective-permute-start(f32[48,16,128]{2,1,0:T(8,128)S(1)} %get-tuple-element.92), channel_id=1, source_target_pairs={{0,2},{2,0},{1,3},{3,1},{4,6},{6,4},{5,7},{7,5},{8,10},{10,8},{9,1... | collective-permute-start | bytes 1179656 | tf_op jit(solution)/shard_map/ppermute | solution.py:43
  88.2 13.4 %collective-permute-start.16 = (f32[48,32,128]{2,1,0:T(8,128)S(1)}, f32[48,32,128]{2,1,0:T(8,128)S(1)}, u32[]{:S(2)}, u32[]{:S(2)}) collective-permute-start(f32[48,32,128]{2,1,0:T(8,128)S(1)} %pad_maximum_fusion), channel_id=1, source_target_pairs={{0,1},{1,0},{2,3},{3,2},{4,5},{5,4},{6,7},{7,6},{8,9},{9,8},{10,11... | collective-permute-start | bytes 2359304 | tf_op jit(solution)/shard_map/ppermute | solution.py:43
  89.5 10.7 %collective-permute-start.15 = (f32[48,8,128]{2,1,0:T(8,128)S(1)}, f32[48,8,128]{2,1,0:T(8,128)S(1)}, u32[]{:S(2)}, u32[]{:S(2)}) collective-permute-start(f32[48,8,128]{2,1,0:T(8,128)S(1)} %get-tuple-element.94), channel_id=1, source_target_pairs={{0,2},{2,0},{1,3},{3,1},{4,6},{6,4},{5,7},{7,5},{8,10},{10,8},{9,1... | collective-permute-start | bytes 589832 | tf_op jit(solution)/shard_map/ppermute | solution.py:43
  96.0 5.7 %collective-permute-start.17 = (f32[48,16,128]{2,1,0:T(8,128)S(1)}, f32[48,16,128]{2,1,0:T(8,128)S(1)}, u32[]{:S(2)}, u32[]{:S(2)}) collective-permute-start(f32[48,16,128]{2,1,0:T(8,128)S(1)} %collective-permute-done.14.refs_3_), channel_id=1, source_target_pairs={{0,1},{1,0},{2,3},{3,2},{4,5},{5,4},{6,7},{7,6},{8,9},{9,8},{10,11... | collective-permute-start | bytes 1179656 | tf_op jit(solution)/shard_map/ppermute | solution.py:43
  97.2 3.4 %collective-permute-start.18 = (f32[48,8,128]{2,1,0:T(8,128)S(1)}, f32[48,8,128]{2,1,0:T(8,128)S(1)}, u32[]{:S(2)}, u32[]{:S(2)}) collective-permute-start(f32[48,8,128]{2,1,0:T(8,128)S(1)} %collective-permute-done.13.refs_4_), channel_id=1, source_target_pairs={{0,1},{1,0},{2,3},{3,2},{4,5},{5,4},{6,7},{7,6},{8,9},{9,8},{10,11... | collective-permute-start | bytes 589832 | tf_op jit(solution)/shard_map/ppermute | solution.py:43
  100.2 1.4 %collective-permute-start.19 = (f32[48,8,128]{2,1,0:T(8,128)S(1)}, f32[48,8,128]{2,1,0:T(8,128)S(1)}, u32[]{:S(2)}, u32[]{:S(2)}) collective-permute-start(f32[48,8,128]{2,1,0:T(8,128)S(1)} %collective-permute-done.15.refs_5_), channel_id=1, source_target_pairs={{0,1},{1,0},{2,3},{3,2},{4,5},{5,4},{6,7},{7,6},{8,9},{9,8},{10,11... | collective-permute-start | bytes 589832 | tf_op jit(solution)/shard_map/ppermute | solution.py:43
  106.7 8.3 %collective-permute-start.20 = (f32[96,128]{1,0:T(8,128)S(1)}, f32[96,128]{1,0:T(8,128)S(1)}, u32[]{:S(2)}, u32[]{:S(2)}) collective-permute-start(f32[96,128]{1,0:T(8,128)S(1)} %get-tuple-element.103), channel_id=1, source_target_pairs={{0,12},{2,14},{4,0},{6,2},{8,4},{10,6},{12,8},{14,10},{1,13},{3,15... | collective-permute-start | bytes 147464 | tf_op jit(solution)/shard_map/ppermute | solution.py:660
  109.1 6.0 %collective-permute-start.21 = (f32[96,128]{1,0:T(8,128)S(1)}, f32[96,128]{1,0:T(8,128)S(1)}, u32[]{:S(2)}, u32[]{:S(2)}) collective-permute-start(f32[96,128]{1,0:T(8,128)S(1)} %get-tuple-element.104), channel_id=1, source_target_pairs={{0,14},{2,12},{4,2},{6,0},{8,6},{10,4},{12,10},{14,8},{1,15},{3,13... | collective-permute-start | bytes 147464 | tf_op jit(solution)/shard_map/ppermute | solution.py:660
  110.0 6.1 %collective-permute-start.22 = (f32[96,128]{1,0:T(8,128)S(1)}, f32[96,128]{1,0:T(8,128)S(1)}, u32[]{:S(2)}, u32[]{:S(2)}) collective-permute-start(f32[96,128]{1,0:T(8,128)S(1)} %get-tuple-element.105), channel_id=1, source_target_pairs={{0,4},{2,6},{4,8},{6,10},{8,12},{10,14},{12,0},{14,2},{1,5},{3,7},... | collective-permute-start | bytes 147464 | tf_op jit(solution)/shard_map/ppermute | solution.py:660
  112.0 6.8 %collective-permute-start.23 = (f32[96,128]{1,0:T(8,128)S(1)}, f32[96,128]{1,0:T(8,128)S(1)}, u32[]{:S(2)}, u32[]{:S(2)}) collective-permute-start(f32[96,128]{1,0:T(8,128)S(1)} %get-tuple-element.106), channel_id=1, source_target_pairs={{0,6},{2,4},{4,10},{6,8},{8,14},{10,12},{12,2},{14,0},{1,7},{3,5},... | collective-permute-start | bytes 147464 | tf_op jit(solution)/shard_map/ppermute | solution.py:660
  112.0 6.8 %collective-permute-start.24 = (f32[96,128]{1,0:T(8,128)S(1)}, f32[96,128]{1,0:T(8,128)S(1)}, u32[]{:S(2)}, u32[]{:S(2)}) collective-permute-start(f32[96,128]{1,0:T(8,128)S(1)} %get-tuple-element.107), channel_id=1, source_target_pairs={{0,2},{2,0},{4,6},{6,4},{8,10},{10,8},{12,14},{14,12},{1,3},{3,1},... | collective-permute-start | bytes 147464 | tf_op jit(solution)/shard_map/ppermute | solution.py:660
  119.9 4.0 %collective-permute-start.26 = (f32[32,128]{1,0:T(8,128)S(1)}, f32[32,128]{1,0:T(8,128)S(1)}, u32[]{:S(2)}, u32[]{:S(2)}) collective-permute-start(f32[32,128]{1,0:T(8,128)S(1)} %get-tuple-element.110), channel_id=1, source_target_pairs={{0,2},{1,3},{2,0},{3,1},{4,6},{5,7},{6,4},{7,5},{8,10},{9,11},{10,... | collective-permute-start | bytes 49160 | tf_op jit(solution)/shard_map/ppermute | solution.py:43
  120.5 3.3 %collective-permute-start.27 = (f32[32,128]{1,0:T(8,128)S(1)}, f32[32,128]{1,0:T(8,128)S(1)}, u32[]{:S(2)}, u32[]{:S(2)}) collective-permute-start(f32[32,128]{1,0:T(8,128)S(1)} %get-tuple-element.111), channel_id=1, source_target_pairs={{0,3},{1,2},{2,1},{3,0},{4,7},{5,6},{6,5},{7,4},{8,11},{9,10},{10,... | collective-permute-start | bytes 49160 | tf_op jit(solution)/shard_map/ppermute | solution.py:43
  120.5 3.3 %collective-permute-start.25 = (f32[32,128]{1,0:T(8,128)S(1)}, f32[32,128]{1,0:T(8,128)S(1)}, u32[]{:S(2)}, u32[]{:S(2)}) collective-permute-start(f32[32,128]{1,0:T(8,128)S(1)} %get-tuple-element.109), channel_id=1, source_target_pairs={{0,1},{1,0},{2,3},{3,2},{4,5},{5,4},{6,7},{7,6},{8,9},{9,8},{10,11... | collective-permute-start | bytes 49160 | tf_op jit(solution)/shard_map/ppermute | solution.py:43
  123.9 4.9 %collective-permute-start.29 = (f32[32,128]{1,0:T(8,128)S(1)}, f32[32,128]{1,0:T(8,128)S(1)}, u32[]{:S(2)}, u32[]{:S(2)}) collective-permute-start(f32[32,128]{1,0:T(8,128)S(1)} %add_add_fusion.1), channel_id=1, source_target_pairs={{0,8},{4,12},{8,0},{12,4},{1,9},{5,13},{9,1},{13,5},{2,10},{6,14},... | collective-permute-start | bytes 49160 | tf_op jit(solution)/shard_map/ppermute | solution.py:43
  124.4 5.5 %collective-permute-start.30 = (f32[32,128]{1,0:T(8,128)S(1)}, f32[32,128]{1,0:T(8,128)S(1)}, u32[]{:S(2)}, u32[]{:S(2)}) collective-permute-start(f32[32,128]{1,0:T(8,128)S(1)} %add_add_fusion.1), channel_id=1, source_target_pairs={{0,12},{4,8},{8,4},{12,0},{1,13},{5,9},{9,5},{13,1},{2,14},{6,10},... | collective-permute-start | bytes 49160 | tf_op jit(solution)/shard_map/ppermute | solution.py:43
  125.9 4.1 %collective-permute-start.28 = (f32[32,128]{1,0:T(8,128)S(1)}, f32[32,128]{1,0:T(8,128)S(1)}, u32[]{:S(2)}, u32[]{:S(2)}) collective-permute-start(f32[32,128]{1,0:T(8,128)S(1)} %add_add_fusion.1), channel_id=1, source_target_pairs={{0,4},{4,0},{8,12},{12,8},{1,5},{5,1},{9,13},{13,9},{2,6},{6,2},{1... | collective-permute-start | bytes 49160 | tf_op jit(solution)/shard_map/ppermute | solution.py:43

commit v14 on v11

--- a/solution.py
+++ b/solution.py
@@ -379,12 +379,18 @@
             if by & bit:
                 columns = reordered(columns, width, bit)
         projections += columns
-    highest = lax.Precision.HIGHEST
+    corr, rows = split_bf16(corr_ref[...]), split_bf16(projections)
     weighted = jnp.dot(
-        corr_ref[...], projections, precision=highest, preferred_element_type=jnp.float32
-    )
+        jnp.concatenate([corr[0], corr[0], corr[1]], axis=1),
+        jnp.concatenate([rows[0], rows[1], rows[0]], axis=0),
+        preferred_element_type=jnp.float32,
+    )
+    parts = split_bf16(weighted)
     atom_part = lax.dot_general(
-        projections, weighted, TN, precision=highest, preferred_element_type=jnp.float32
+        jnp.concatenate([rows[0], rows[0], rows[1]], axis=0),
+        jnp.concatenate([parts[0], parts[1], parts[0]], axis=0),
+        TN,
+        preferred_element_type=jnp.float32,
     )
     share = grid_ref[...] * scales[0] + atom_part * scales[1]
     for bit in bits:
@@ -432,7 +438,10 @@
         if m < 3:
             blocks[0] = jnp.concatenate([blocks[0], levels], axis=0)
         own.append(blocks)
-    near = sent(jnp.concatenate(own[1], axis=0), 1)
+    near = jnp.concatenate(own[1], axis=0)
+    if n_dom > 2:
+        near, own[2][0] = lax.optimization_barrier((near, own[2][0]))
+    near = sent(near, 1)
     arrived = [[own[0][0], near] + [sent(own[m][0], m) for m in range(2, n_dom)]]
     handed_on = [sent(arrived[0][2][size:], 1)] if n_dom > 3 else []
     for c in range(1, n_chunks):

time: 119 us -> 120 us (level)
    ppermute x25, starting transfers between devices: 27.1 us -> 28.7 us  [swapped(): return lax.ppermute(x, axes, [(i, i ^ by) for i in range(size)])]
    ppermute x5, starting transfers between devices: 8.66 us -> 7.2 us  [on_device(): sums.append(lax.ppermute(x, ('dom', 'band'), pairs))]
  transfers between devices with their start and end apart: 30 -> 30, of which waited for: 10 -> 13; matrix products, arithmetic and copies ran while one was open for 1% -> 1% of each run, Pallas kernels for 28% -> 28%
where the time goes in v14:
time: 120 us; the launch traced here: 119 us
  waiting for transfers between devices  39.4 us (33%)
  Pallas kernels  38.7 us (32%)
  starting transfers between devices  35.9 us (30%)
  local copies, waits for them, and re-layouts  2.82 us (2%)
  other arithmetic  1.72 us (1%)
    ppermute x25, waiting for transfers between devices, swapped(): return lax.ppermute(x, axes, [(i, i ^ by) for i in range(size)])  37.5 us
    ppermute x25, starting transfers between devices, swapped(): return lax.ppermute(x, axes, [(i, i ^ by) for i in range(size)])  28.7 us
    pallas_call x2, Pallas kernels, filter_orbitals(): pl.pallas_call(functools.partial(filter_kernel, n_dom, planes, rows, star...  13.2 us
    pallas_call x1, Pallas kernels, build_projectors(): pl.pallas_call(functools.partial(projector_kernel, n_band, n_sub), out_sh...  11.5 us
    pallas_call x2, Pallas kernels, products(): pl.pallas_call(functools.partial(product_kernel, spots, n_sub, first_row,...  8.16 us
    ppermute x5, starting transfers between devices, on_device(): sums.append(lax.ppermute(x, ('dom', 'band'), pairs))  7.2 us
    pallas_call x2, Pallas kernels, orbital_first(): pl.pallas_call(functools.partial(orbital_first_kernel, n_dom, which), out...  2.92 us
  transfers between devices with their start and end apart: 30, of which 13 were waited for; matrix products, arithmetic and copies ran while one was open for 1% of the time, Pallas kernels for 28%

profile of v14, /device:TPU:0, one launch (start us, length us, event | category | flops | bytes accessed | tf_op | source)
XLA Modules:
  0.0 119.5 jit_solution(10557100086161537123)
XLA Ops:
  0.6 0.0 copy-start
  0.7 2.3 %constant_dynamic-slice_fusion = (f32[384,128]{1,0:T(8,128)S(1)}, f32[384,128]{1,0:T(8,128)}, f32[384,128]{1,0:T(8,128)S(1)}, f32[384,128]{1,0:T(8,128)}, f32[38...) fusion(f32[3072,128]{1,0:T(8,128)} %bitcast.34, s32[]{:T(128)S(6)} %select_n.35, ...), kind=kLoop, calls=%fused_computation.9 | loop fusion | bytes 3145760 | tf_op jit(solution)/shard_map/dynamic_slice | solution.py:430
  3.0 0.8 pad_maximum_fusion.1
  3.9 4.1 %collective-permute-start = (f32[480,128]{1,0:T(8,128)S(1)}, f32[480,128]{1,0:T(8,128)S(1)}, u32[]{:S(2)}, u32[]{:S(2)}) collective-permute-start(f32[480,128]{1,0:T(8,128)S(1)} %get-tuple-element.59), channel_id=1, source_target_pairs={{0,8},{4,12},{8,0},{12,4},{1,9},{5,13},{9,1},{13,5},{2,10},{6,14},... | collective-permute-start | bytes 737288 | tf_op jit(solution)/shard_map/ppermute | solution.py:43
  8.0 1.6 %collective-permute-start.2 = (f32[864,128]{1,0:T(8,128)}, f32[864,128]{1,0:T(8,128)S(1)}, u32[]{:S(2)}, u32[]{:S(2)}) collective-permute-start(f32[864,128]{1,0:T(8,128)} %pad_maximum_fusion.1), channel_id=1, source_target_pairs={{0,4},{4,0},{8,12},{12,8},{1,5},{5,1},{9,13},{13,9},{2,6},{6,2},{1... | collective-permute-start | bytes 1327112 | tf_op jit(solution)/shard_map/ppermute | solution.py:43
  9.5 0.1 constant_dynamic-slice_fusion.8
  9.6 0.1 copy.9
  9.7 0.1 broadcast_multiply_fusion
  9.9 10.2 %collective-permute-done.refs_3_ = f32[480,128]{1,0:T(8,128)S(1)} collective-permute-done((f32[480,128]{1,0:T(8,128)S(1)}, f32[480,128]{1,0:T(8,128)S(1)}, u32[]{:S(2)}, u32[]{:S(2)}) %collective-permute-start) | collective-permute-done | bytes 245792 | tf_op jit(solution)/shard_map/ppermute | solution.py:43
  20.1 5.4 %collective-permute-done.2.refs_2_ = f32[864,128]{1,0:T(8,128)S(1)} collective-permute-done((f32[864,128]{1,0:T(8,128)}, f32[864,128]{1,0:T(8,128)S(1)}, u32[]{:S(2)}, u32[]{:S(2)}) %collective-permute-start.2) | collective-permute-done | bytes 442400 | tf_op jit(solution)/shard_map/ppermute | solution.py:43
  25.4 0.7 collective-permute-start.7
  26.2 2.5 %collective-permute-start.8 = (f32[384,128]{1,0:T(8,128)S(1)}, f32[384,128]{1,0:T(8,128)S(1)}, u32[]{:S(2)}, u32[]{:S(2)}) collective-permute-start(f32[384,128]{1,0:T(8,128)S(1)} %get-tuple-element.73), channel_id=1, source_target_pairs={{0,12},{4,8},{8,4},{12,0},{1,13},{5,9},{9,5},{13,1},{2,14},{6,10},... | collective-permute-start | bytes 589832 | tf_op jit(solution)/shard_map/ppermute | solution.py:43
  28.7 0.1 pad_add_fusion.place
  28.8 0.3 mul.56.corr_ref
  29.0 0.8 collective-permute-done.3.refs_4_
  29.8 0.0 collective-permute-done.1.refs_0_
  29.8 6.8 %chebyshev.2 = (f32[3,128,128]{2,1,0:T(8,128)S(1)}, f32[3,128,128]{2,1,0:T(8,128)S(1)}, f32[3,128,128]{2,1,0:T(8,128)S(1)}, f32[3,128,128]{2,1,0:T(8,128)S(1)}, f32[6,32,8,128]{3,2,1,0:T(8,128)S(1)}) custom-call(s32[4]{0:T(128)S(1)} %pad_add_fusion.place, f32[96,128]{1,0:T(8,128)S(1)} %collective-permute-done.1.refs_0_, ...), custom_call_target="tpu_custom_call" | custom-call | flops 28311552 | bytes 1572864 | tf_op jit(solution)/shard_map/chebyshev/pallas_call | solution.py:132
  36.7 1.8 %collective-permute-start.4 = (f32[3,128,128]{2,1,0:T(8,128)S(1)}, f32[3,128,128]{2,1,0:T(8,128)S(1)}, u32[]{:S(2)}, u32[]{:S(2)}) collective-permute-start(f32[3,128,128]{2,1,0:T(8,128)S(1)} %get-tuple-element.63), channel_id=1, source_target_pairs={{0,4},{4,0},{8,12},{12,8},{1,5},{5,1},{9,13},{13,9},{2,6},{6,2},{1... | collective-permute-start | bytes 589832 | tf_op jit(solution)/shard_map/ppermute | solution.py:43
  38.5 1.3 %collective-permute-start.5 = (f32[3,128,128]{2,1,0:T(8,128)S(1)}, f32[3,128,128]{2,1,0:T(8,128)S(1)}, u32[]{:S(2)}, u32[]{:S(2)}) collective-permute-start(f32[3,128,128]{2,1,0:T(8,128)S(1)} %get-tuple-element.64), channel_id=1, source_target_pairs={{0,8},{4,12},{8,0},{12,4},{1,9},{5,13},{9,1},{13,5},{2,10},{6,14},... | collective-permute-start | bytes 589832 | tf_op jit(solution)/shard_map/ppermute | solution.py:43
  39.8 1.3 %collective-permute-start.6 = (f32[3,128,128]{2,1,0:T(8,128)S(1)}, f32[3,128,128]{2,1,0:T(8,128)S(1)}, u32[]{:S(2)}, u32[]{:S(2)}) collective-permute-start(f32[3,128,128]{2,1,0:T(8,128)S(1)} %get-tuple-element.65), channel_id=1, source_target_pairs={{0,12},{4,8},{8,4},{12,0},{1,13},{5,9},{9,5},{13,1},{2,14},{6,10},... | collective-permute-start | bytes 589832 | tf_op jit(solution)/shard_map/ppermute | solution.py:43
  41.1 11.5 %projectors.1 = (bf16[576,6144]{1,0:T(8,128)(2,1)S(1)}, bf16[576,6144]{1,0:T(8,128)(2,1)S(1)}) custom-call(s32[4]{0:T(128)S(1)} %pad_add_fusion.place, s32[3,48,128]{2,1,0:T(8,128)S(1)} %bitcast.32, f32[48,3,8,128]{3,2,1,0:T(8,128)S(1)} %copy-done.1), custom_call_target="tpu_custom_call" | custom-call | flops 1811939328 | bytes 28311552 | tf_op jit(solution)/shard_map/projectors/pallas_call | solution.py:275
  52.6 0.0 collective-permute-done.7.refs_3_
  52.6 6.4 %chebyshev.3 = (f32[3,128,128]{2,1,0:T(8,128)S(1)}, f32[3,128,128]{2,1,0:T(8,128)S(1)}, f32[3,128,128]{2,1,0:T(8,128)S(1)}, f32[3,128,128]{2,1,0:T(8,128)S(1)}) custom-call(s32[4]{0:T(128)S(1)} %pad_add_fusion.place, f32[6,32,8,128]{3,2,1,0:T(8,128)S(1)} %get-tuple-element.70.refs_0_, f32[384,128]{1,0:T(8,128)S(1)} %get-tuple-element.116.refs_1_, ...), custom_call_target="tpu_custom_call" | custom-call | flops 28311552 | bytes 1572864 | tf_op jit(solution)/shard_map/chebyshev/pallas_call | solution.py:132
  59.0 2.8 %collective-permute-start.9 = (f32[3,128,128]{2,1,0:T(8,128)S(1)}, f32[3,128,128]{2,1,0:T(8,128)S(1)}, u32[]{:S(2)}, u32[]{:S(2)}) collective-permute-start(f32[3,128,128]{2,1,0:T(8,128)S(1)} %get-tuple-element.75), channel_id=1, source_target_pairs={{0,4},{4,0},{8,12},{12,8},{1,5},{5,1},{9,13},{13,9},{2,6},{6,2},{1... | collective-permute-start | bytes 589832 | tf_op jit(solution)/shard_map/ppermute | solution.py:43
  61.9 1.1 collective-permute-start.10
  63.0 0.0 collective-permute-done.4
  63.0 1.4 %collective-permute-start.11 = (f32[3,128,128]{2,1,0:T(8,128)S(1)}, f32[3,128,128]{2,1,0:T(8,128)S(1)}, u32[]{:S(2)}, u32[]{:S(2)}) collective-permute-start(f32[3,128,128]{2,1,0:T(8,128)S(1)} %get-tuple-element.78), channel_id=1, source_target_pairs={{0,12},{4,8},{8,4},{12,0},{1,13},{5,9},{9,5},{13,1},{2,14},{6,10},... | collective-permute-start | bytes 589832 | tf_op jit(solution)/shard_map/ppermute | solution.py:43
  64.4 0.0 collective-permute-done.5
  64.4 0.0 collective-permute-done.6
  64.4 0.7 cell_first.3
  65.1 3.1 %collective-permute-done.9 = f32[3,128,128]{2,1,0:T(8,128)S(1)} collective-permute-done((f32[3,128,128]{2,1,0:T(8,128)S(1)}, f32[3,128,128]{2,1,0:T(8,128)S(1)}, u32[]{:S(2)}, u32[]{:S(2)}) %collective-permute-start.9) | collective-permute-done | bytes 196640 | tf_op jit(solution)/shard_map/ppermute | solution.py:43
  68.1 1.6 %orbital_first.2.refs_2_ = f32[32,96,128]{2,1,0:T(8,128)} custom-call(s32[4]{0:T(128)S(1)} %pad_add_fusion.place, f32[384,128]{1,0:T(8,128)S(1)} %bitcast.21, f32[384,128]{1,0:T(8,128)S(1)} %bitcast.23, f32[384,128]{1,0:T(8,128)S(1)} %bitcast.25, f32[384,128]{1,0:T(8,128)S(1)} %bitcast.27, f32[384,128]{1,0:T(8,128)S(1)} %bitcast.16, f32[384,128]{1,0:T(8,128)S(1)} %bitcast.18), custom_call_target="tpu_custom_call" | custom-call | tf_op jit(solution)/shard_map/orbital_first/pallas_call | solution.py:209
  69.8 0.6 cell_first.4
  70.4 1.5 %collective-permute-start.12 = (f32[48,8,128]{2,1,0:T(8,128)S(1)}, f32[48,8,128]{2,1,0:T(8,128)S(1)}, u32[]{:S(2)}, u32[]{:S(2)}) collective-permute-start(f32[48,8,128]{2,1,0:T(8,128)S(1)} %get-tuple-element.88), channel_id=1, source_target_pairs={{0,2},{2,0},{1,3},{3,1},{4,6},{6,4},{5,7},{7,5},{8,10},{10,8},{9,1... | collective-permute-start | bytes 589832 | tf_op jit(solution)/shard_map/ppermute | solution.py:43
  71.8 0.6 collective-permute-start.13
  72.5 6.1 %collective-permute-done.10 = f32[3,128,128]{2,1,0:T(8,128)S(1)} collective-permute-done((f32[3,128,128]{2,1,0:T(8,128)S(1)}, f32[3,128,128]{2,1,0:T(8,128)S(1)}, u32[]{:S(2)}, u32[]{:S(2)}) %collective-permute-start.10) | collective-permute-done | bytes 196640 | tf_op jit(solution)/shard_map/ppermute | solution.py:43
  78.5 0.0 collective-permute-done.11
  78.5 0.0 collective-permute-done.12.refs_4_
  78.5 0.6 cell_first.5
  79.1 0.1 pad_maximum_fusion
  79.2 0.1 collective-permute-start.15
  79.3 1.6 %collective-permute-start.14 = (f32[48,8,128]{2,1,0:T(8,128)S(1)}, f32[48,8,128]{2,1,0:T(8,128)S(1)}, u32[]{:S(2)}, u32[]{:S(2)}) collective-permute-start(f32[48,8,128]{2,1,0:T(8,128)S(1)} %get-tuple-element.95), channel_id=1, source_target_pairs={{0,2},{2,0},{1,3},{3,1},{4,6},{6,4},{5,7},{7,5},{8,10},{10,8},{9,1... | collective-permute-start | bytes 589832 | tf_op jit(solution)/shard_map/ppermute | solution.py:43
  80.8 0.4 collective-permute-done.13.refs_3_
  81.2 0.0 collective-permute-start.16
  81.2 0.5 collective-permute-start.17
  81.7 4.9 %collective-permute-done.14.refs_5_ = f32[48,8,128]{2,1,0:T(8,128)S(1)} collective-permute-done((f32[48,8,128]{2,1,0:T(8,128)S(1)}, f32[48,8,128]{2,1,0:T(8,128)S(1)}, u32[]{:S(2)}, u32[]{:S(2)}) %collective-permute-start.14) | collective-permute-done | bytes 196640 | tf_op jit(solution)/shard_map/ppermute | solution.py:43
  86.6 1.4 %collective-permute-done.18.refs_9_ = f32[48,8,128]{2,1,0:T(8,128)S(1)} collective-permute-done((f32[48,8,128]{2,1,0:T(8,128)S(1)}, f32[48,8,128]{2,1,0:T(8,128)S(1)}, u32[]{:S(2)}, u32[]{:S(2)}) %collective-permute-start.18) | collective-permute-done | bytes 196640 | tf_op jit(solution)/shard_map/ppermute | solution.py:43
  88.0 4.5 %products.2 = (f32[96,128]{1,0:T(8,128)S(1)}, f32[96,128]{1,0:T(8,128)S(1)}, f32[96,128]{1,0:T(8,128)S(1)}, f32[96,128]{1,0:T(8,128)S(1)}, f32[96,128]{1,0:T(8,128)S(1)}) custom-call(s32[4]{0:T(128)S(1)} %pad_add_fusion.place, bf16[576,6144]{1,0:T(8,128)(2,1)S(1)} %get-tuple-element.80.w_high, bf16[576,6144]{1,0:T(8,128)(2,1)S(1)} %get-tuple-element.81.w_low, ...), custom_call_target="tpu_custom_call" | custom-call | flops 4529848320 | bytes 11796480 | tf_op jit(solution)/shard_map/products/pallas_call | solution.py:349
  92.5 2.1 %collective-permute-start.19 = (f32[96,128]{1,0:T(8,128)S(1)}, f32[96,128]{1,0:T(8,128)S(1)}, u32[]{:S(2)}, u32[]{:S(2)}) collective-permute-start(f32[96,128]{1,0:T(8,128)S(1)} %get-tuple-element.105), channel_id=1, source_target_pairs={{0,12},{2,14},{4,0},{6,2},{8,4},{10,6},{12,8},{14,10},{1,13},{3,15... | collective-permute-start | bytes 147464 | tf_op jit(solution)/shard_map/ppermute | solution.py:600
  94.6 4.0 %collective-permute-start.20 = (f32[96,128]{1,0:T(8,128)S(1)}, f32[96,128]{1,0:T(8,128)S(1)}, u32[]{:S(2)}, u32[]{:S(2)}) collective-permute-start(f32[96,128]{1,0:T(8,128)S(1)} %get-tuple-element.106), channel_id=1, source_target_pairs={{0,14},{2,12},{4,2},{6,0},{8,6},{10,4},{12,10},{14,8},{1,15},{3,13... | collective-permute-start | bytes 147464 | tf_op jit(solution)/shard_map/ppermute | solution.py:600
  98.6 1.1 collective-permute-start.23
  99.7 3.7 %products.3 = (f32[128,128]{1,0:T(8,128)S(1)}, f32[96,128]{1,0:T(8,128)S(1)}) custom-call(s32[4]{0:T(128)S(1)} %pad_add_fusion.place, bf16[576,6144]{1,0:T(8,128)(2,1)S(1)} %get-tuple-element.80.w_high, bf16[576,6144]{1,0:T(8,128)(2,1)S(1)} %get-tuple-element.81.w_low, f32[48,16,128]{2,1,0:T(8,128)S(1)} %get-tuple-element.84.refs_0_, ...), custom_call_target="tpu_custom_call" | custom-call | flops 905969664 | bytes 2359296 | tf_op jit(solution)/shard_map/products/pallas_call | solution.py:349
  103.4 1.0 collective-permute-done.21.refs_2_
  104.5 0.9 collective-permute-done.22.refs_3_
  105.4 1.1 gram_share.1
  106.5 1.2 collective-permute-start.25
  107.6 1.1 collective-permute-start.24
  108.7 1.6 %collective-permute-done.25 = f32[32,128]{1,0:T(8,128)S(1)} collective-permute-done((f32[32,128]{1,0:T(8,128)S(1)}, f32[32,128]{1,0:T(8,128)S(1)}, u32[]{:S(2)}, u32[]{:S(2)}) %collective-permute-start.25) | collective-permute-done | bytes 16416 | tf_op jit(solution)/shard_map/ppermute | solution.py:43
  110.3 0.5 collective-permute-done.26
  110.8 2.5 %collective-permute-start.28 = (f32[32,128]{1,0:T(8,128)S(1)}, f32[32,128]{1,0:T(8,128)S(1)}, u32[]{:S(2)}, u32[]{:S(2)}) collective-permute-start(f32[32,128]{1,0:T(8,128)S(1)} %add_add_fusion.1), channel_id=1, source_target_pairs={{0,8},{4,12},{8,0},{12,4},{1,9},{5,13},{9,1},{13,5},{2,10},{6,14},... | collective-permute-start | bytes 49160 | tf_op jit(solution)/shard_map/ppermute | solution.py:43
  113.3 1.1 collective-permute-start.27
  114.4 1.3 %orbital_first.3 = f32[32,96,128]{2,1,0:T(8,128)} custom-call(s32[4]{0:T(128)S(1)} %pad_add_fusion.place, f32[384,128]{1,0:T(8,128)S(1)} %bitcast.29, f32[384,128]{1,0:T(8,128)S(1)} %bitcast.31, f32[32,96,128]{2,1,0:T(8,128)} %orbital_first.2.refs_2_), custom_call_target="tpu_custom_call", output_to_operand_aliasing={{}: (3, {})} | custom-call | tf_op jit(solution)/shard_map/orbital_first/pallas_call | solution.py:209
  115.7 3.1 %collective-permute-done.29 = f32[32,128]{1,0:T(8,128)S(1)} collective-permute-done((f32[32,128]{1,0:T(8,128)S(1)}, f32[32,128]{1,0:T(8,128)S(1)}, u32[]{:S(2)}, u32[]{:S(2)}) %collective-permute-start.29) | collective-permute-done | bytes 16416 | tf_op jit(solution)/shard_map/ppermute | solution.py:43
  118.9 0.6 add_add_fusion
  (28 shorter events, 0.1 us)
Async XLA Ops:
  0.6 8.9 %copy-start = (f32[48,8,8]{0,2,1:T(8,128)S(1)}, f32[48,8,8]{0,2,1:T(8,128)}, u32[]{:S(2)}) copy-start(f32[48,8,8]{0,2,1:T(8,128)} %param.9) | copy-start | bytes 36868
  0.7 2.3 %copy-start.3 = (f32[3,32,128]{2,1,0:T(8,128)S(1)}, f32[3,32,128]{2,1,0:T(8,128)}, u32[]{:S(2)}) copy-start(f32[3,32,128]{2,1,0:T(8,128)} %param.6) | copy-start | bytes 147460
  3.9 16.2 %collective-permute-start = (f32[480,128]{1,0:T(8,128)S(1)}, f32[480,128]{1,0:T(8,128)S(1)}, u32[]{:S(2)}, u32[]{:S(2)}) collective-permute-start(f32[480,128]{1,0:T(8,128)S(1)} %get-tuple-element.59), channel_id=1, source_target_pairs={{0,8},{4,12},{8,0},{12,4},{1,9},{5,13},{9,1},{13,5},{2,10},{6,14},... | collective-permute-start | bytes 737288 | tf_op jit(solution)/shard_map/ppermute | solution.py:43
  8.0 17.5 %collective-permute-start.2 = (f32[864,128]{1,0:T(8,128)}, f32[864,128]{1,0:T(8,128)S(1)}, u32[]{:S(2)}, u32[]{:S(2)}) collective-permute-start(f32[864,128]{1,0:T(8,128)} %pad_maximum_fusion.1), channel_id=1, source_target_pairs={{0,4},{4,0},{8,12},{12,8},{1,5},{5,1},{9,13},{13,9},{2,6},{6,2},{1... | collective-permute-start | bytes 1327112 | tf_op jit(solution)/shard_map/ppermute | solution.py:43
  9.5 20.3 %collective-permute-start.3 = (f32[384,128]{1,0:T(8,128)}, f32[384,128]{1,0:T(8,128)S(1)}, u32[]{:S(2)}, u32[]{:S(2)}) collective-permute-start(f32[384,128]{1,0:T(8,128)} %get-tuple-element.117), channel_id=1, source_target_pairs={{0,12},{4,8},{8,4},{12,0},{1,13},{5,9},{9,5},{13,1},{2,14},{6,10},... | collective-permute-start | bytes 589832 | tf_op jit(solution)/shard_map/ppermute | solution.py:43
  9.5 31.6 %copy-start.1 = (f32[48,3,8,128]{3,2,1,0:T(8,128)S(1)}, f32[48,3,8,128]{3,2,1,0:T(8,128)}, u32[]{:S(2)}) copy-start(f32[48,3,8,128]{3,2,1,0:T(8,128)} %coefs_ref.1) | copy-start | bytes 1769476
  9.5 31.6 %copy-start.2 = (s32[48,3,128]{2,0,1:T(8,128)S(1)}, s32[48,3,128]{2,0,1:T(8,128)}, u32[]{:S(2)}) copy-start(s32[48,3,128]{2,0,1:T(8,128)} %param.7) | copy-start | bytes 221188
  20.1 9.8 %collective-permute-start.1 = (f32[96,128]{1,0:T(8,128)S(1)}, f32[96,128]{1,0:T(8,128)S(1)}, u32[]{:S(2)}, u32[]{:S(2)}) collective-permute-start(f32[96,128]{1,0:T(8,128)S(1)} %slice.4), channel_id=1, source_target_pairs={{0,4},{4,0},{8,12},{12,8},{1,5},{5,1},{9,13},{13,9},{2,6},{6,2},{1... | collective-permute-start | bytes 147464 | tf_op jit(solution)/shard_map/ppermute | solution.py:43
  25.4 27.1 %collective-permute-start.7 = (f32[384,128]{1,0:T(8,128)}, f32[384,128]{1,0:T(8,128)S(1)}, u32[]{:S(2)}, u32[]{:S(2)}) collective-permute-start(f32[384,128]{1,0:T(8,128)} %get-tuple-element.72), channel_id=1, source_target_pairs={{0,8},{4,12},{8,0},{12,4},{1,9},{5,13},{9,1},{13,5},{2,10},{6,14},... | collective-permute-start | bytes 589832 | tf_op jit(solution)/shard_map/ppermute | solution.py:43
  26.2 26.4 %collective-permute-start.8 = (f32[384,128]{1,0:T(8,128)S(1)}, f32[384,128]{1,0:T(8,128)S(1)}, u32[]{:S(2)}, u32[]{:S(2)}) collective-permute-start(f32[384,128]{1,0:T(8,128)S(1)} %get-tuple-element.73), channel_id=1, source_target_pairs={{0,12},{4,8},{8,4},{12,0},{1,13},{5,9},{9,5},{13,1},{2,14},{6,10},... | collective-permute-start | bytes 589832 | tf_op jit(solution)/shard_map/ppermute | solution.py:43
  36.7 26.4 %collective-permute-start.4 = (f32[3,128,128]{2,1,0:T(8,128)S(1)}, f32[3,128,128]{2,1,0:T(8,128)S(1)}, u32[]{:S(2)}, u32[]{:S(2)}) collective-permute-start(f32[3,128,128]{2,1,0:T(8,128)S(1)} %get-tuple-element.63), channel_id=1, source_target_pairs={{0,4},{4,0},{8,12},{12,8},{1,5},{5,1},{9,13},{13,9},{2,6},{6,2},{1... | collective-permute-start | bytes 589832 | tf_op jit(solution)/shard_map/ppermute | solution.py:43
  38.5 25.9 %collective-permute-start.5 = (f32[3,128,128]{2,1,0:T(8,128)S(1)}, f32[3,128,128]{2,1,0:T(8,128)S(1)}, u32[]{:S(2)}, u32[]{:S(2)}) collective-permute-start(f32[3,128,128]{2,1,0:T(8,128)S(1)} %get-tuple-element.64), channel_id=1, source_target_pairs={{0,8},{4,12},{8,0},{12,4},{1,9},{5,13},{9,1},{13,5},{2,10},{6,14},... | collective-permute-start | bytes 589832 | tf_op jit(solution)/shard_map/ppermute | solution.py:43
  39.8 24.6 %collective-permute-start.6 = (f32[3,128,128]{2,1,0:T(8,128)S(1)}, f32[3,128,128]{2,1,0:T(8,128)S(1)}, u32[]{:S(2)}, u32[]{:S(2)}) collective-permute-start(f32[3,128,128]{2,1,0:T(8,128)S(1)} %get-tuple-element.65), channel_id=1, source_target_pairs={{0,12},{4,8},{8,4},{12,0},{1,13},{5,9},{9,5},{13,1},{2,14},{6,10},... | collective-permute-start | bytes 589832 | tf_op jit(solution)/shard_map/ppermute | solution.py:43
  59.0 9.1 %collective-permute-start.9 = (f32[3,128,128]{2,1,0:T(8,128)S(1)}, f32[3,128,128]{2,1,0:T(8,128)S(1)}, u32[]{:S(2)}, u32[]{:S(2)}) collective-permute-start(f32[3,128,128]{2,1,0:T(8,128)S(1)} %get-tuple-element.75), channel_id=1, source_target_pairs={{0,4},{4,0},{8,12},{12,8},{1,5},{5,1},{9,13},{13,9},{2,6},{6,2},{1... | collective-permute-start | bytes 589832 | tf_op jit(solution)/shard_map/ppermute | solution.py:43
  61.9 16.7 %collective-permute-start.10 = (f32[3,128,128]{2,1,0:T(8,128)S(1)}, f32[3,128,128]{2,1,0:T(8,128)S(1)}, u32[]{:S(2)}, u32[]{:S(2)}) collective-permute-start(f32[3,128,128]{2,1,0:T(8,128)S(1)} %get-tuple-element.77), channel_id=1, source_target_pairs={{0,8},{4,12},{8,0},{12,4},{1,9},{5,13},{9,1},{13,5},{2,10},{6,14},... | collective-permute-start | bytes 589832 | tf_op jit(solution)/shard_map/ppermute | solution.py:43
  63.0 15.5 %collective-permute-start.11 = (f32[3,128,128]{2,1,0:T(8,128)S(1)}, f32[3,128,128]{2,1,0:T(8,128)S(1)}, u32[]{:S(2)}, u32[]{:S(2)}) collective-permute-start(f32[3,128,128]{2,1,0:T(8,128)S(1)} %get-tuple-element.78), channel_id=1, source_target_pairs={{0,12},{4,8},{8,4},{12,0},{1,13},{5,9},{9,5},{13,1},{2,14},{6,10},... | collective-permute-start | bytes 589832 | tf_op jit(solution)/shard_map/ppermute | solution.py:43
  70.4 8.2 %collective-permute-start.12 = (f32[48,8,128]{2,1,0:T(8,128)S(1)}, f32[48,8,128]{2,1,0:T(8,128)S(1)}, u32[]{:S(2)}, u32[]{:S(2)}) collective-permute-start(f32[48,8,128]{2,1,0:T(8,128)S(1)} %get-tuple-element.88), channel_id=1, source_target_pairs={{0,2},{2,0},{1,3},{3,1},{4,6},{6,4},{5,7},{7,5},{8,10},{10,8},{9,1... | collective-permute-start | bytes 589832 | tf_op jit(solution)/shard_map/ppermute | solution.py:43
  71.8 9.3 %collective-permute-start.13 = (f32[48,16,128]{2,1,0:T(8,128)S(1)}, f32[48,16,128]{2,1,0:T(8,128)S(1)}, u32[]{:S(2)}, u32[]{:S(2)}) collective-permute-start(f32[48,16,128]{2,1,0:T(8,128)S(1)} %get-tuple-element.93), channel_id=1, source_target_pairs={{0,2},{2,0},{1,3},{3,1},{4,6},{6,4},{5,7},{7,5},{8,10},{10,8},{9,1... | collective-permute-start | bytes 1179656 | tf_op jit(solution)/shard_map/ppermute | solution.py:43
  79.2 8.8 %collective-permute-start.15 = (f32[48,32,128]{2,1,0:T(8,128)S(1)}, f32[48,32,128]{2,1,0:T(8,128)S(1)}, u32[]{:S(2)}, u32[]{:S(2)}) collective-permute-start(f32[48,32,128]{2,1,0:T(8,128)S(1)} %pad_maximum_fusion), channel_id=1, source_target_pairs={{0,1},{1,0},{2,3},{3,2},{4,5},{5,4},{6,7},{7,6},{8,9},{9,8},{10,11... | collective-permute-start | bytes 2359304 | tf_op jit(solution)/shard_map/ppermute | solution.py:43
  79.3 7.3 %collective-permute-start.14 = (f32[48,8,128]{2,1,0:T(8,128)S(1)}, f32[48,8,128]{2,1,0:T(8,128)S(1)}, u32[]{:S(2)}, u32[]{:S(2)}) collective-permute-start(f32[48,8,128]{2,1,0:T(8,128)S(1)} %get-tuple-element.95), channel_id=1, source_target_pairs={{0,2},{2,0},{1,3},{3,1},{4,6},{6,4},{5,7},{7,5},{8,10},{10,8},{9,1... | collective-permute-start | bytes 589832 | tf_op jit(solution)/shard_map/ppermute | solution.py:43
  81.2 6.9 %collective-permute-start.16 = (f32[48,16,128]{2,1,0:T(8,128)S(1)}, f32[48,16,128]{2,1,0:T(8,128)S(1)}, u32[]{:S(2)}, u32[]{:S(2)}) collective-permute-start(f32[48,16,128]{2,1,0:T(8,128)S(1)} %collective-permute-done.13.refs_3_), channel_id=1, source_target_pairs={{0,1},{1,0},{2,3},{3,2},{4,5},{5,4},{6,7},{7,6},{8,9},{9,8},{10,11... | collective-permute-start | bytes 1179656 | tf_op jit(solution)/shard_map/ppermute | solution.py:43
  81.2 5.4 %collective-permute-start.17 = (f32[48,8,128]{2,1,0:T(8,128)S(1)}, f32[48,8,128]{2,1,0:T(8,128)S(1)}, u32[]{:S(2)}, u32[]{:S(2)}) collective-permute-start(f32[48,8,128]{2,1,0:T(8,128)S(1)} %collective-permute-done.12.refs_4_), channel_id=1, source_target_pairs={{0,1},{1,0},{2,3},{3,2},{4,5},{5,4},{6,7},{7,6},{8,9},{9,8},{10,11... | collective-permute-start | bytes 589832 | tf_op jit(solution)/shard_map/ppermute | solution.py:43
  86.6 1.4 %collective-permute-start.18 = (f32[48,8,128]{2,1,0:T(8,128)S(1)}, f32[48,8,128]{2,1,0:T(8,128)S(1)}, u32[]{:S(2)}, u32[]{:S(2)}) collective-permute-start(f32[48,8,128]{2,1,0:T(8,128)S(1)} %collective-permute-done.14.refs_5_), channel_id=1, source_target_pairs={{0,1},{1,0},{2,3},{3,2},{4,5},{5,4},{6,7},{7,6},{8,9},{9,8},{10,11... | collective-permute-start | bytes 589832 | tf_op jit(solution)/shard_map/ppermute | solution.py:43
  92.5 10.9 %collective-permute-start.19 = (f32[96,128]{1,0:T(8,128)S(1)}, f32[96,128]{1,0:T(8,128)S(1)}, u32[]{:S(2)}, u32[]{:S(2)}) collective-permute-start(f32[96,128]{1,0:T(8,128)S(1)} %get-tuple-element.105), channel_id=1, source_target_pairs={{0,12},{2,14},{4,0},{6,2},{8,4},{10,6},{12,8},{14,10},{1,13},{3,15... | collective-permute-start | bytes 147464 | tf_op jit(solution)/shard_map/ppermute | solution.py:600
  94.6 8.8 %collective-permute-start.20 = (f32[96,128]{1,0:T(8,128)S(1)}, f32[96,128]{1,0:T(8,128)S(1)}, u32[]{:S(2)}, u32[]{:S(2)}) collective-permute-start(f32[96,128]{1,0:T(8,128)S(1)} %get-tuple-element.106), channel_id=1, source_target_pairs={{0,14},{2,12},{4,2},{6,0},{8,6},{10,4},{12,10},{14,8},{1,15},{3,13... | collective-permute-start | bytes 147464 | tf_op jit(solution)/shard_map/ppermute | solution.py:600
  98.6 5.9 %collective-permute-start.21 = (f32[96,128]{1,0:T(8,128)S(1)}, f32[96,128]{1,0:T(8,128)S(1)}, u32[]{:S(2)}, u32[]{:S(2)}) collective-permute-start(f32[96,128]{1,0:T(8,128)S(1)} %get-tuple-element.107), channel_id=1, source_target_pairs={{0,4},{2,6},{4,8},{6,10},{8,12},{10,14},{12,0},{14,2},{1,5},{3,7},... | collective-permute-start | bytes 147464 | tf_op jit(solution)/shard_map/ppermute | solution.py:600
  98.6 6.8 %collective-permute-start.22 = (f32[96,128]{1,0:T(8,128)S(1)}, f32[96,128]{1,0:T(8,128)S(1)}, u32[]{:S(2)}, u32[]{:S(2)}) collective-permute-start(f32[96,128]{1,0:T(8,128)S(1)} %get-tuple-element.108), channel_id=1, source_target_pairs={{0,6},{2,4},{4,10},{6,8},{8,14},{10,12},{12,2},{14,0},{1,7},{3,5},... | collective-permute-start | bytes 147464 | tf_op jit(solution)/shard_map/ppermute | solution.py:600
  98.6 6.8 %collective-permute-start.23 = (f32[96,128]{1,0:T(8,128)S(1)}, f32[96,128]{1,0:T(8,128)S(1)}, u32[]{:S(2)}, u32[]{:S(2)}) collective-permute-start(f32[96,128]{1,0:T(8,128)S(1)} %get-tuple-element.109), channel_id=1, source_target_pairs={{0,2},{2,0},{4,6},{6,4},{8,10},{10,8},{12,14},{14,12},{1,3},{3,1},... | collective-permute-start | bytes 147464 | tf_op jit(solution)/shard_map/ppermute | solution.py:600
  106.5 3.8 %collective-permute-start.25 = (f32[32,128]{1,0:T(8,128)S(1)}, f32[32,128]{1,0:T(8,128)S(1)}, u32[]{:S(2)}, u32[]{:S(2)}) collective-permute-start(f32[32,128]{1,0:T(8,128)S(1)} %get-tuple-element.112), channel_id=1, source_target_pairs={{0,2},{1,3},{2,0},{3,1},{4,6},{5,7},{6,4},{7,5},{8,10},{9,11},{10,... | collective-permute-start | bytes 49160 | tf_op jit(solution)/shard_map/ppermute | solution.py:43
  107.6 3.2 %collective-permute-start.26 = (f32[32,128]{1,0:T(8,128)S(1)}, f32[32,128]{1,0:T(8,128)S(1)}, u32[]{:S(2)}, u32[]{:S(2)}) collective-permute-start(f32[32,128]{1,0:T(8,128)S(1)} %get-tuple-element.113), channel_id=1, source_target_pairs={{0,3},{1,2},{2,1},{3,0},{4,7},{5,6},{6,5},{7,4},{8,11},{9,10},{10,... | collective-permute-start | bytes 49160 | tf_op jit(solution)/shard_map/ppermute | solution.py:43
  107.6 3.2 %collective-permute-start.24 = (f32[32,128]{1,0:T(8,128)S(1)}, f32[32,128]{1,0:T(8,128)S(1)}, u32[]{:S(2)}, u32[]{:S(2)}) collective-permute-start(f32[32,128]{1,0:T(8,128)S(1)} %get-tuple-element.111), channel_id=1, source_target_pairs={{0,1},{1,0},{2,3},{3,2},{4,5},{5,4},{6,7},{7,6},{8,9},{9,8},{10,11... | collective-permute-start | bytes 49160 | tf_op jit(solution)/shard_map/ppermute | solution.py:43
  110.8 4.9 %collective-permute-start.28 = (f32[32,128]{1,0:T(8,128)S(1)}, f32[32,128]{1,0:T(8,128)S(1)}, u32[]{:S(2)}, u32[]{:S(2)}) collective-permute-start(f32[32,128]{1,0:T(8,128)S(1)} %add_add_fusion.1), channel_id=1, source_target_pairs={{0,8},{4,12},{8,0},{12,4},{1,9},{5,13},{9,1},{13,5},{2,10},{6,14},... | collective-permute-start | bytes 49160 | tf_op jit(solution)/shard_map/ppermute | solution.py:43
  113.3 5.5 %collective-permute-start.29 = (f32[32,128]{1,0:T(8,128)S(1)}, f32[32,128]{1,0:T(8,128)S(1)}, u32[]{:S(2)}, u32[]{:S(2)}) collective-permute-start(f32[32,128]{1,0:T(8,128)S(1)} %add_add_fusion.1), channel_id=1, source_target_pairs={{0,12},{4,8},{8,4},{12,0},{1,13},{5,9},{9,5},{13,1},{2,14},{6,10},... | collective-permute-start | bytes 49160 | tf_op jit(solution)/shard_map/ppermute | solution.py:43
  113.3 5.5 %collective-permute-start.27 = (f32[32,128]{1,0:T(8,128)S(1)}, f32[32,128]{1,0:T(8,128)S(1)}, u32[]{:S(2)}, u32[]{:S(2)}) collective-permute-start(f32[32,128]{1,0:T(8,128)S(1)} %add_add_fusion.1), channel_id=1, source_target_pairs={{0,4},{4,0},{8,12},{12,8},{1,5},{5,1},{9,13},{13,9},{2,6},{6,2},{1... | collective-permute-start | bytes 49160 | tf_op jit(solution)/shard_map/ppermute | solution.py:43

commit v15 on v11

--- a/solution.py
+++ b/solution.py
@@ -550,6 +550,7 @@
         crossed = len(tiles[-1]) == 2 and at == len(parts) - 2
         for m in range(1, n_band):
             pieces.append(part[m] if crossed else swapped(part[m], "band", n_band, m))
+    pieces[-1], filtered = lax.optimization_barrier((pieces[-1], filtered))
     arrays = own + pieces
     pieces = [jnp.concatenate(own, axis=1)] + pieces
     arrays += [swapped(x, "sub", n_sub, k) for k in range(1, n_sub) for x in pieces]

time: 119 us -> 119 us (level)
  transfers between devices with their start and end apart: 30 -> 30, of which waited for: 10 -> 11; matrix products, arithmetic and copies ran while one was open for 1% -> 1% of each run, Pallas kernels for 28% -> 28%
where the time goes in v15:
time: 119 us
  Pallas kernels  38.9 us (33%)
  waiting for transfers between devices  38.5 us (32%)
  starting transfers between devices  35.8 us (30%)
  local copies, waits for them, and re-layouts  2.83 us (2%)
  other arithmetic  1.72 us (1%)
    ppermute x25, waiting for transfers between devices, swapped(): return lax.ppermute(x, axes, [(i, i ^ by) for i in range(size)])  36.9 us
    ppermute x25, starting transfers between devices, swapped(): return lax.ppermute(x, axes, [(i, i ^ by) for i in range(size)])  27.1 us
    pallas_call x2, Pallas kernels, filter_orbitals(): pl.pallas_call(functools.partial(filter_kernel, n_dom, planes, rows, star...  13.2 us
    pallas_call x1, Pallas kernels, build_projectors(): pl.pallas_call(functools.partial(projector_kernel, n_band, n_sub), out_sh...  11.5 us
    ppermute x5, starting transfers between devices, on_device(): sums.append(lax.ppermute(x, ('dom', 'band'), pairs))  8.66 us
    pallas_call x2, Pallas kernels, products(): pl.pallas_call(functools.partial(product_kernel, spots, n_sub, first_row,...  8.15 us
    pallas_call x2, Pallas kernels, orbital_first(): pl.pallas_call(functools.partial(orbital_first_kernel, n_dom, which), out...  2.92 us
  transfers between devices with their start and end apart: 30, of which 11 were waited for; matrix products, arithmetic and copies ran while one was open for 1% of the time, Pallas kernels for 28%

profile of v15, /device:TPU:0, one launch (start us, length us, event | category | flops | bytes accessed | tf_op | source)
XLA Modules:
  0.0 118.6 jit_solution(1668316459028402437)
XLA Ops:
  0.6 0.0 copy-start
  0.7 2.3 %constant_dynamic-slice_fusion = (f32[384,128]{1,0:T(8,128)S(1)}, f32[384,128]{1,0:T(8,128)}, f32[384,128]{1,0:T(8,128)S(1)}, f32[384,128]{1,0:T(8,128)}, f32[38...) fusion(f32[3072,128]{1,0:T(8,128)} %bitcast.34, s32[]{:T(128)S(6)} %select_n.35, ...), kind=kLoop, calls=%fused_computation.9 | loop fusion | bytes 3145760 | tf_op jit(solution)/shard_map/dynamic_slice | solution.py:424
  3.1 4.1 %collective-permute-start = (f32[480,128]{1,0:T(8,128)S(1)}, f32[480,128]{1,0:T(8,128)S(1)}, u32[]{:S(2)}, u32[]{:S(2)}) collective-permute-start(f32[480,128]{1,0:T(8,128)S(1)} %get-tuple-element.123), channel_id=1, source_target_pairs={{0,8},{4,12},{8,0},{12,4},{1,9},{5,13},{9,1},{13,5},{2,10},{6,14},... | collective-permute-start | bytes 737288 | tf_op jit(solution)/shard_map/ppermute | solution.py:43
  7.2 0.8 pad_maximum_fusion.1
  8.0 1.6 %collective-permute-start.2 = (f32[864,128]{1,0:T(8,128)}, f32[864,128]{1,0:T(8,128)S(1)}, u32[]{:S(2)}, u32[]{:S(2)}) collective-permute-start(f32[864,128]{1,0:T(8,128)} %pad_maximum_fusion.1), channel_id=1, source_target_pairs={{0,4},{4,0},{8,12},{12,8},{1,5},{5,1},{9,13},{13,9},{2,6},{6,2},{1... | collective-permute-start | bytes 1327112 | tf_op jit(solution)/shard_map/ppermute | solution.py:43
  9.6 0.1 constant_dynamic-slice_fusion.8
  9.6 0.1 copy.9
  9.7 0.1 broadcast_multiply_fusion
  9.9 9.4 %collective-permute-done.refs_3_ = f32[480,128]{1,0:T(8,128)S(1)} collective-permute-done((f32[480,128]{1,0:T(8,128)S(1)}, f32[480,128]{1,0:T(8,128)S(1)}, u32[]{:S(2)}, u32[]{:S(2)}) %collective-permute-start) | collective-permute-done | bytes 245792 | tf_op jit(solution)/shard_map/ppermute | solution.py:43
  19.3 9.9 %collective-permute-done.2.refs_2_ = f32[864,128]{1,0:T(8,128)S(1)} collective-permute-done((f32[864,128]{1,0:T(8,128)}, f32[864,128]{1,0:T(8,128)S(1)}, u32[]{:S(2)}, u32[]{:S(2)}) %collective-permute-start.2) | collective-permute-done | bytes 442400 | tf_op jit(solution)/shard_map/ppermute | solution.py:43
  29.2 0.5 collective-permute-start.7
  29.7 2.0 %collective-permute-start.8 = (f32[384,128]{1,0:T(8,128)S(1)}, f32[384,128]{1,0:T(8,128)S(1)}, u32[]{:S(2)}, u32[]{:S(2)}) collective-permute-start(f32[384,128]{1,0:T(8,128)S(1)} %get-tuple-element.71), channel_id=1, source_target_pairs={{0,12},{4,8},{8,4},{12,0},{1,13},{5,9},{9,5},{13,1},{2,14},{6,10},... | collective-permute-start | bytes 589832 | tf_op jit(solution)/shard_map/ppermute | solution.py:43
  31.7 0.1 pad_add_fusion.place
  31.8 0.3 mul.56.corr_ref
  32.1 0.0 collective-permute-done.1.refs_0_
  32.1 6.8 %chebyshev.2 = (f32[3,128,128]{2,1,0:T(8,128)S(1)}, f32[3,128,128]{2,1,0:T(8,128)S(1)}, f32[3,128,128]{2,1,0:T(8,128)S(1)}, f32[3,128,128]{2,1,0:T(8,128)S(1)}, f32[6,32,8,128]{3,2,1,0:T(8,128)S(1)}) custom-call(s32[4]{0:T(128)S(1)} %pad_add_fusion.place, f32[96,128]{1,0:T(8,128)S(1)} %collective-permute-done.1.refs_0_, ...), custom_call_target="tpu_custom_call" | custom-call | flops 28311552 | bytes 1572864 | tf_op jit(solution)/shard_map/chebyshev/pallas_call | solution.py:132
  38.9 1.1 collective-permute-start.4
  39.9 1.4 %collective-permute-start.5 = (f32[3,128,128]{2,1,0:T(8,128)S(1)}, f32[3,128,128]{2,1,0:T(8,128)S(1)}, u32[]{:S(2)}, u32[]{:S(2)}) collective-permute-start(f32[3,128,128]{2,1,0:T(8,128)S(1)} %get-tuple-element.62), channel_id=1, source_target_pairs={{0,8},{4,12},{8,0},{12,4},{1,9},{5,13},{9,1},{13,5},{2,10},{6,14},... | collective-permute-start | bytes 589832 | tf_op jit(solution)/shard_map/ppermute | solution.py:43
  41.4 2.0 %collective-permute-start.6 = (f32[3,128,128]{2,1,0:T(8,128)S(1)}, f32[3,128,128]{2,1,0:T(8,128)S(1)}, u32[]{:S(2)}, u32[]{:S(2)}) collective-permute-start(f32[3,128,128]{2,1,0:T(8,128)S(1)} %get-tuple-element.63), channel_id=1, source_target_pairs={{0,12},{4,8},{8,4},{12,0},{1,13},{5,9},{9,5},{13,1},{2,14},{6,10},... | collective-permute-start | bytes 589832 | tf_op jit(solution)/shard_map/ppermute | solution.py:43
  43.3 11.5 %projectors.1 = (bf16[576,6144]{1,0:T(8,128)(2,1)S(1)}, bf16[576,6144]{1,0:T(8,128)(2,1)S(1)}) custom-call(s32[4]{0:T(128)S(1)} %pad_add_fusion.place, s32[3,48,128]{2,1,0:T(8,128)S(1)} %bitcast.32, f32[48,3,8,128]{3,2,1,0:T(8,128)S(1)} %copy-done.1), custom_call_target="tpu_custom_call" | custom-call | flops 1811939328 | bytes 28311552 | tf_op jit(solution)/shard_map/projectors/pallas_call | solution.py:275
  54.8 0.0 collective-permute-done.7.refs_3_
  54.8 6.4 %chebyshev.3 = (f32[3,128,128]{2,1,0:T(8,128)S(1)}, f32[3,128,128]{2,1,0:T(8,128)S(1)}, f32[3,128,128]{2,1,0:T(8,128)S(1)}, f32[3,128,128]{2,1,0:T(8,128)S(1)}) custom-call(s32[4]{0:T(128)S(1)} %pad_add_fusion.place, f32[6,32,8,128]{3,2,1,0:T(8,128)S(1)} %get-tuple-element.68.refs_0_, f32[384,128]{1,0:T(8,128)S(1)} %get-tuple-element.116.refs_1_, ...), custom_call_target="tpu_custom_call" | custom-call | flops 28311552 | bytes 1572864 | tf_op jit(solution)/shard_map/chebyshev/pallas_call | solution.py:132
  61.3 0.4 collective-permute-start.9
  61.7 2.1 %collective-permute-start.11 = (f32[3,128,128]{2,1,0:T(8,128)S(1)}, f32[3,128,128]{2,1,0:T(8,128)S(1)}, u32[]{:S(2)}, u32[]{:S(2)}) collective-permute-start(f32[3,128,128]{2,1,0:T(8,128)S(1)} %get-tuple-element.81), channel_id=1, source_target_pairs={{0,8},{4,12},{8,0},{12,4},{1,9},{5,13},{9,1},{13,5},{2,10},{6,14},... | collective-permute-start | bytes 589832 | tf_op jit(solution)/shard_map/ppermute | solution.py:43
  63.8 0.0 collective-permute-done.4
  63.8 2.0 %collective-permute-start.12 = (f32[3,128,128]{2,1,0:T(8,128)S(1)}, f32[3,128,128]{2,1,0:T(8,128)S(1)}, u32[]{:S(2)}, u32[]{:S(2)}) collective-permute-start(f32[3,128,128]{2,1,0:T(8,128)S(1)} %get-tuple-element.82), channel_id=1, source_target_pairs={{0,12},{4,8},{8,4},{12,0},{1,13},{5,9},{9,5},{13,1},{2,14},{6,10},... | collective-permute-start | bytes 589832 | tf_op jit(solution)/shard_map/ppermute | solution.py:43
  65.7 0.0 collective-permute-done.5
  65.7 0.0 collective-permute-done.6
  65.7 0.7 cell_first.3
  66.4 0.9 collective-permute-done.9
  67.3 1.6 %orbital_first.2.refs_2_ = f32[32,96,128]{2,1,0:T(8,128)} custom-call(s32[4]{0:T(128)S(1)} %pad_add_fusion.place, f32[384,128]{1,0:T(8,128)S(1)} %bitcast.21, f32[384,128]{1,0:T(8,128)S(1)} %bitcast.23, f32[384,128]{1,0:T(8,128)S(1)} %bitcast.25, f32[384,128]{1,0:T(8,128)S(1)} %bitcast.27, f32[384,128]{1,0:T(8,128)S(1)} %bitcast.16, f32[384,128]{1,0:T(8,128)S(1)} %bitcast.18), custom_call_target="tpu_custom_call" | custom-call | tf_op jit(solution)/shard_map/orbital_first/pallas_call | solution.py:209
  68.9 0.6 cell_first.4
  69.5 1.5 %collective-permute-start.10 = (f32[48,8,128]{2,1,0:T(8,128)S(1)}, f32[48,8,128]{2,1,0:T(8,128)S(1)}, u32[]{:S(2)}, u32[]{:S(2)}) collective-permute-start(f32[48,8,128]{2,1,0:T(8,128)S(1)} %get-tuple-element.80), channel_id=1, source_target_pairs={{0,2},{2,0},{1,3},{3,1},{4,6},{6,4},{5,7},{7,5},{8,10},{10,8},{9,1... | collective-permute-start | bytes 589832 | tf_op jit(solution)/shard_map/ppermute | solution.py:43
  71.0 0.5 collective-permute-start.14
  71.6 5.5 %collective-permute-done.11 = f32[3,128,128]{2,1,0:T(8,128)S(1)} collective-permute-done((f32[3,128,128]{2,1,0:T(8,128)S(1)}, f32[3,128,128]{2,1,0:T(8,128)S(1)}, u32[]{:S(2)}, u32[]{:S(2)}) %collective-permute-start.11) | collective-permute-done | bytes 196640 | tf_op jit(solution)/shard_map/ppermute | solution.py:43
  77.1 0.6 cell_first.5
  77.7 0.1 pad_maximum_fusion
  77.8 0.1 collective-permute-start.15
  77.9 1.6 %collective-permute-start.13 = (f32[48,8,128]{2,1,0:T(8,128)S(1)}, f32[48,8,128]{2,1,0:T(8,128)S(1)}, u32[]{:S(2)}, u32[]{:S(2)}) collective-permute-start(f32[48,8,128]{2,1,0:T(8,128)S(1)} %get-tuple-element.85), channel_id=1, source_target_pairs={{0,2},{2,0},{1,3},{3,1},{4,6},{6,4},{5,7},{7,5},{8,10},{10,8},{9,1... | collective-permute-start | bytes 589832 | tf_op jit(solution)/shard_map/ppermute | solution.py:43
  79.4 0.1 collective-permute-done.14.refs_3_
  79.5 0.1 collective-permute-start.16
  79.6 1.3 %orbital_first.3 = f32[32,96,128]{2,1,0:T(8,128)} custom-call(s32[4]{0:T(128)S(1)} %pad_add_fusion.place, f32[384,128]{1,0:T(8,128)S(1)} %bitcast.29, f32[384,128]{1,0:T(8,128)S(1)} %bitcast.31, f32[32,96,128]{2,1,0:T(8,128)} %orbital_first.2.refs_2_), custom_call_target="tpu_custom_call", output_to_operand_aliasing={{}: (3, {})} | custom-call | tf_op jit(solution)/shard_map/orbital_first/pallas_call | solution.py:209
  80.9 0.5 collective-permute-start.17
  81.4 3.8 %collective-permute-done.13.refs_5_ = f32[48,8,128]{2,1,0:T(8,128)S(1)} collective-permute-done((f32[48,8,128]{2,1,0:T(8,128)S(1)}, f32[48,8,128]{2,1,0:T(8,128)S(1)}, u32[]{:S(2)}, u32[]{:S(2)}) %collective-permute-start.13) | collective-permute-done | bytes 196640 | tf_op jit(solution)/shard_map/ppermute | solution.py:43
  85.2 0.0 collective-permute-start.18
  85.2 0.0 collective-permute-done.17.refs_8_
  85.2 1.4 %collective-permute-done.18.refs_9_ = f32[48,8,128]{2,1,0:T(8,128)S(1)} collective-permute-done((f32[48,8,128]{2,1,0:T(8,128)S(1)}, f32[48,8,128]{2,1,0:T(8,128)S(1)}, u32[]{:S(2)}, u32[]{:S(2)}) %collective-permute-start.18) | collective-permute-done | bytes 196640 | tf_op jit(solution)/shard_map/ppermute | solution.py:43
  86.6 4.5 %products.2 = (f32[96,128]{1,0:T(8,128)S(1)}, f32[96,128]{1,0:T(8,128)S(1)}, f32[96,128]{1,0:T(8,128)S(1)}, f32[96,128]{1,0:T(8,128)S(1)}, f32[96,128]{1,0:T(8,128)S(1)}) custom-call(s32[4]{0:T(128)S(1)} %pad_add_fusion.place, bf16[576,6144]{1,0:T(8,128)(2,1)S(1)} %get-tuple-element.88.w_high, bf16[576,6144]{1,0:T(8,128)(2,1)S(1)} %get-tuple-element.89.w_low, ...), custom_call_target="tpu_custom_call" | custom-call | flops 4529848320 | bytes 11796480 | tf_op jit(solution)/shard_map/products/pallas_call | solution.py:349
  91.1 4.3 %collective-permute-start.19 = (f32[96,128]{1,0:T(8,128)S(1)}, f32[96,128]{1,0:T(8,128)S(1)}, u32[]{:S(2)}, u32[]{:S(2)}) collective-permute-start(f32[96,128]{1,0:T(8,128)S(1)} %get-tuple-element.105), channel_id=1, source_target_pairs={{0,12},{2,14},{4,0},{6,2},{8,4},{10,6},{12,8},{14,10},{1,13},{3,15... | collective-permute-start | bytes 147464 | tf_op jit(solution)/shard_map/ppermute | solution.py:592
  95.4 2.2 %collective-permute-start.20 = (f32[96,128]{1,0:T(8,128)S(1)}, f32[96,128]{1,0:T(8,128)S(1)}, u32[]{:S(2)}, u32[]{:S(2)}) collective-permute-start(f32[96,128]{1,0:T(8,128)S(1)} %get-tuple-element.106), channel_id=1, source_target_pairs={{0,14},{2,12},{4,2},{6,0},{8,6},{10,4},{12,10},{14,8},{1,15},{3,13... | collective-permute-start | bytes 147464 | tf_op jit(solution)/shard_map/ppermute | solution.py:592
  97.5 0.8 collective-permute-start.21
  98.3 1.5 %collective-permute-start.23 = (f32[96,128]{1,0:T(8,128)S(1)}, f32[96,128]{1,0:T(8,128)S(1)}, u32[]{:S(2)}, u32[]{:S(2)}) collective-permute-start(f32[96,128]{1,0:T(8,128)S(1)} %get-tuple-element.109), channel_id=1, source_target_pairs={{0,2},{2,0},{4,6},{6,4},{8,10},{10,8},{12,14},{14,12},{1,3},{3,1},... | collective-permute-start | bytes 147464 | tf_op jit(solution)/shard_map/ppermute | solution.py:592
  99.8 3.7 %products.3 = (f32[128,128]{1,0:T(8,128)S(1)}, f32[96,128]{1,0:T(8,128)S(1)}) custom-call(s32[4]{0:T(128)S(1)} %pad_add_fusion.place, bf16[576,6144]{1,0:T(8,128)(2,1)S(1)} %get-tuple-element.88.w_high, bf16[576,6144]{1,0:T(8,128)(2,1)S(1)} %get-tuple-element.89.w_low, f32[48,16,128]{2,1,0:T(8,128)S(1)} %get-tuple-element.90.refs_0_, ...), custom_call_target="tpu_custom_call" | custom-call | flops 905969664 | bytes 2359296 | tf_op jit(solution)/shard_map/products/pallas_call | solution.py:349
  103.5 1.6 %collective-permute-done.22.refs_3_ = f32[96,128]{1,0:T(8,128)S(1)} collective-permute-done((f32[96,128]{1,0:T(8,128)S(1)}, f32[96,128]{1,0:T(8,128)S(1)}, u32[]{:S(2)}, u32[]{:S(2)}) %collective-permute-start.22) | collective-permute-done | bytes 49184 | tf_op jit(solution)/shard_map/ppermute | solution.py:592
  105.1 1.2 %gram_share.1 = (f32[32,128]{1,0:T(8,128)S(1)}, f32[32,128]{1,0:T(8,128)S(1)}, f32[32,128]{1,0:T(8,128)S(1)}, f32[32,128]{1,0:T(8,128)S(1)}) custom-call(s32[4]{0:T(128)S(1)} %pad_add_fusion.place, f32[96,96]{1,0:T(8,128)S(1)} %mul.56.corr_ref, f32[128,128]{1,0:T(8,128)S(1)} %get-tuple-element.103.grid_ref, f32[96,128]{1,0:T(8,128)S(1)} %get-tuple-element.104.proj_ref, ...), custom_call_target="tpu_custom_call" | custom-call | tf_op jit(solution)/shard_map/gram_share/pallas_call | solution.py:398
  106.3 0.6 collective-permute-start.25
  106.9 1.6 %collective-permute-start.24 = (f32[32,128]{1,0:T(8,128)S(1)}, f32[32,128]{1,0:T(8,128)S(1)}, u32[]{:S(2)}, u32[]{:S(2)}) collective-permute-start(f32[32,128]{1,0:T(8,128)S(1)} %get-tuple-element.111), channel_id=1, source_target_pairs={{0,1},{1,0},{2,3},{3,2},{4,5},{5,4},{6,7},{7,6},{8,9},{9,8},{10,11... | collective-permute-start | bytes 49160 | tf_op jit(solution)/shard_map/ppermute | solution.py:43
  108.5 1.7 %collective-permute-done.25 = f32[32,128]{1,0:T(8,128)S(1)} collective-permute-done((f32[32,128]{1,0:T(8,128)S(1)}, f32[32,128]{1,0:T(8,128)S(1)}, u32[]{:S(2)}, u32[]{:S(2)}) %collective-permute-start.25) | collective-permute-done | bytes 16416 | tf_op jit(solution)/shard_map/ppermute | solution.py:43
  110.3 2.1 %collective-permute-start.28 = (f32[32,128]{1,0:T(8,128)S(1)}, f32[32,128]{1,0:T(8,128)S(1)}, u32[]{:S(2)}, u32[]{:S(2)}) collective-permute-start(f32[32,128]{1,0:T(8,128)S(1)} %add_add_fusion.1), channel_id=1, source_target_pairs={{0,8},{4,12},{8,0},{12,4},{1,9},{5,13},{9,1},{13,5},{2,10},{6,14},... | collective-permute-start | bytes 49160 | tf_op jit(solution)/shard_map/ppermute | solution.py:43
  112.4 0.3 collective-permute-start.29
  112.7 1.2 collective-permute-start.27
  113.8 1.1 collective-permute-done.28
  115.0 2.9 %collective-permute-done.29 = f32[32,128]{1,0:T(8,128)S(1)} collective-permute-done((f32[32,128]{1,0:T(8,128)S(1)}, f32[32,128]{1,0:T(8,128)S(1)}, u32[]{:S(2)}, u32[]{:S(2)}) %collective-permute-start.29) | collective-permute-done | bytes 16416 | tf_op jit(solution)/shard_map/ppermute | solution.py:43
  117.9 0.6 add_add_fusion
  (28 shorter events, 0.1 us)
Async XLA Ops:
  0.6 8.9 %copy-start = (f32[48,8,8]{0,2,1:T(8,128)S(1)}, f32[48,8,8]{0,2,1:T(8,128)}, u32[]{:S(2)}) copy-start(f32[48,8,8]{0,2,1:T(8,128)} %param.9) | copy-start | bytes 36868
  0.7 2.3 %copy-start.3 = (f32[3,32,128]{2,1,0:T(8,128)S(1)}, f32[3,32,128]{2,1,0:T(8,128)}, u32[]{:S(2)}) copy-start(f32[3,32,128]{2,1,0:T(8,128)} %param.6) | copy-start | bytes 147460
  3.1 16.2 %collective-permute-start = (f32[480,128]{1,0:T(8,128)S(1)}, f32[480,128]{1,0:T(8,128)S(1)}, u32[]{:S(2)}, u32[]{:S(2)}) collective-permute-start(f32[480,128]{1,0:T(8,128)S(1)} %get-tuple-element.123), channel_id=1, source_target_pairs={{0,8},{4,12},{8,0},{12,4},{1,9},{5,13},{9,1},{13,5},{2,10},{6,14},... | collective-permute-start | bytes 737288 | tf_op jit(solution)/shard_map/ppermute | solution.py:43
  8.0 21.3 %collective-permute-start.2 = (f32[864,128]{1,0:T(8,128)}, f32[864,128]{1,0:T(8,128)S(1)}, u32[]{:S(2)}, u32[]{:S(2)}) collective-permute-start(f32[864,128]{1,0:T(8,128)} %pad_maximum_fusion.1), channel_id=1, source_target_pairs={{0,4},{4,0},{8,12},{12,8},{1,5},{5,1},{9,13},{13,9},{2,6},{6,2},{1... | collective-permute-start | bytes 1327112 | tf_op jit(solution)/shard_map/ppermute | solution.py:43
  9.5 22.5 %collective-permute-start.3 = (f32[384,128]{1,0:T(8,128)}, f32[384,128]{1,0:T(8,128)S(1)}, u32[]{:S(2)}, u32[]{:S(2)}) collective-permute-start(f32[384,128]{1,0:T(8,128)} %get-tuple-element.117), channel_id=1, source_target_pairs={{0,12},{4,8},{8,4},{12,0},{1,13},{5,9},{9,5},{13,1},{2,14},{6,10},... | collective-permute-start | bytes 589832 | tf_op jit(solution)/shard_map/ppermute | solution.py:43
  9.5 33.8 %copy-start.1 = (f32[48,3,8,128]{3,2,1,0:T(8,128)S(1)}, f32[48,3,8,128]{3,2,1,0:T(8,128)}, u32[]{:S(2)}) copy-start(f32[48,3,8,128]{3,2,1,0:T(8,128)} %coefs_ref.1) | copy-start | bytes 1769476
  9.5 33.8 %copy-start.2 = (s32[48,3,128]{2,0,1:T(8,128)S(1)}, s32[48,3,128]{2,0,1:T(8,128)}, u32[]{:S(2)}) copy-start(s32[48,3,128]{2,0,1:T(8,128)} %param.7) | copy-start | bytes 221188
  19.3 12.8 %collective-permute-start.1 = (f32[96,128]{1,0:T(8,128)S(1)}, f32[96,128]{1,0:T(8,128)S(1)}, u32[]{:S(2)}, u32[]{:S(2)}) collective-permute-start(f32[96,128]{1,0:T(8,128)S(1)} %slice.4), channel_id=1, source_target_pairs={{0,4},{4,0},{8,12},{12,8},{1,5},{5,1},{9,13},{13,9},{2,6},{6,2},{1... | collective-permute-start | bytes 147464 | tf_op jit(solution)/shard_map/ppermute | solution.py:43
  29.2 25.6 %collective-permute-start.7 = (f32[384,128]{1,0:T(8,128)}, f32[384,128]{1,0:T(8,128)S(1)}, u32[]{:S(2)}, u32[]{:S(2)}) collective-permute-start(f32[384,128]{1,0:T(8,128)} %get-tuple-element.70), channel_id=1, source_target_pairs={{0,8},{4,12},{8,0},{12,4},{1,9},{5,13},{9,1},{13,5},{2,10},{6,14},... | collective-permute-start | bytes 589832 | tf_op jit(solution)/shard_map/ppermute | solution.py:43
  29.7 25.1 %collective-permute-start.8 = (f32[384,128]{1,0:T(8,128)S(1)}, f32[384,128]{1,0:T(8,128)S(1)}, u32[]{:S(2)}, u32[]{:S(2)}) collective-permute-start(f32[384,128]{1,0:T(8,128)S(1)} %get-tuple-element.71), channel_id=1, source_target_pairs={{0,12},{4,8},{8,4},{12,0},{1,13},{5,9},{9,5},{13,1},{2,14},{6,10},... | collective-permute-start | bytes 589832 | tf_op jit(solution)/shard_map/ppermute | solution.py:43
  38.9 24.9 %collective-permute-start.4 = (f32[3,128,128]{2,1,0:T(8,128)S(1)}, f32[3,128,128]{2,1,0:T(8,128)S(1)}, u32[]{:S(2)}, u32[]{:S(2)}) collective-permute-start(f32[3,128,128]{2,1,0:T(8,128)S(1)} %get-tuple-element.61), channel_id=1, source_target_pairs={{0,4},{4,0},{8,12},{12,8},{1,5},{5,1},{9,13},{13,9},{2,6},{6,2},{1... | collective-permute-start | bytes 589832 | tf_op jit(solution)/shard_map/ppermute | solution.py:43
  39.9 25.8 %collective-permute-start.5 = (f32[3,128,128]{2,1,0:T(8,128)S(1)}, f32[3,128,128]{2,1,0:T(8,128)S(1)}, u32[]{:S(2)}, u32[]{:S(2)}) collective-permute-start(f32[3,128,128]{2,1,0:T(8,128)S(1)} %get-tuple-element.62), channel_id=1, source_target_pairs={{0,8},{4,12},{8,0},{12,4},{1,9},{5,13},{9,1},{13,5},{2,10},{6,14},... | collective-permute-start | bytes 589832 | tf_op jit(solution)/shard_map/ppermute | solution.py:43
  41.4 24.4 %collective-permute-start.6 = (f32[3,128,128]{2,1,0:T(8,128)S(1)}, f32[3,128,128]{2,1,0:T(8,128)S(1)}, u32[]{:S(2)}, u32[]{:S(2)}) collective-permute-start(f32[3,128,128]{2,1,0:T(8,128)S(1)} %get-tuple-element.63), channel_id=1, source_target_pairs={{0,12},{4,8},{8,4},{12,0},{1,13},{5,9},{9,5},{13,1},{2,14},{6,10},... | collective-permute-start | bytes 589832 | tf_op jit(solution)/shard_map/ppermute | solution.py:43
  61.3 6.0 %collective-permute-start.9 = (f32[3,128,128]{2,1,0:T(8,128)S(1)}, f32[3,128,128]{2,1,0:T(8,128)S(1)}, u32[]{:S(2)}, u32[]{:S(2)}) collective-permute-start(f32[3,128,128]{2,1,0:T(8,128)S(1)} %get-tuple-element.73), channel_id=1, source_target_pairs={{0,4},{4,0},{8,12},{12,8},{1,5},{5,1},{9,13},{13,9},{2,6},{6,2},{1... | collective-permute-start | bytes 589832 | tf_op jit(solution)/shard_map/ppermute | solution.py:43
  61.7 15.4 %collective-permute-start.11 = (f32[3,128,128]{2,1,0:T(8,128)S(1)}, f32[3,128,128]{2,1,0:T(8,128)S(1)}, u32[]{:S(2)}, u32[]{:S(2)}) collective-permute-start(f32[3,128,128]{2,1,0:T(8,128)S(1)} %get-tuple-element.81), channel_id=1, source_target_pairs={{0,8},{4,12},{8,0},{12,4},{1,9},{5,13},{9,1},{13,5},{2,10},{6,14},... | collective-permute-start | bytes 589832 | tf_op jit(solution)/shard_map/ppermute | solution.py:43
  63.8 13.3 %collective-permute-start.12 = (f32[3,128,128]{2,1,0:T(8,128)S(1)}, f32[3,128,128]{2,1,0:T(8,128)S(1)}, u32[]{:S(2)}, u32[]{:S(2)}) collective-permute-start(f32[3,128,128]{2,1,0:T(8,128)S(1)} %get-tuple-element.82), channel_id=1, source_target_pairs={{0,12},{4,8},{8,4},{12,0},{1,13},{5,9},{9,5},{13,1},{2,14},{6,10},... | collective-permute-start | bytes 589832 | tf_op jit(solution)/shard_map/ppermute | solution.py:43
  69.5 7.6 %collective-permute-start.10 = (f32[48,8,128]{2,1,0:T(8,128)S(1)}, f32[48,8,128]{2,1,0:T(8,128)S(1)}, u32[]{:S(2)}, u32[]{:S(2)}) collective-permute-start(f32[48,8,128]{2,1,0:T(8,128)S(1)} %get-tuple-element.80), channel_id=1, source_target_pairs={{0,2},{2,0},{1,3},{3,1},{4,6},{6,4},{5,7},{7,5},{8,10},{10,8},{9,1... | collective-permute-start | bytes 589832 | tf_op jit(solution)/shard_map/ppermute | solution.py:43
  71.0 8.5 %collective-permute-start.14 = (f32[48,16,128]{2,1,0:T(8,128)S(1)}, f32[48,16,128]{2,1,0:T(8,128)S(1)}, u32[]{:S(2)}, u32[]{:S(2)}) collective-permute-start(f32[48,16,128]{2,1,0:T(8,128)S(1)} %get-tuple-element.93), channel_id=1, source_target_pairs={{0,2},{2,0},{1,3},{3,1},{4,6},{6,4},{5,7},{7,5},{8,10},{10,8},{9,1... | collective-permute-start | bytes 1179656 | tf_op jit(solution)/shard_map/ppermute | solution.py:43
  77.8 8.8 %collective-permute-start.15 = (f32[48,32,128]{2,1,0:T(8,128)S(1)}, f32[48,32,128]{2,1,0:T(8,128)S(1)}, u32[]{:S(2)}, u32[]{:S(2)}) collective-permute-start(f32[48,32,128]{2,1,0:T(8,128)S(1)} %pad_maximum_fusion), channel_id=1, source_target_pairs={{0,1},{1,0},{2,3},{3,2},{4,5},{5,4},{6,7},{7,6},{8,9},{9,8},{10,11... | collective-permute-start | bytes 2359304 | tf_op jit(solution)/shard_map/ppermute | solution.py:43
  77.9 7.3 %collective-permute-start.13 = (f32[48,8,128]{2,1,0:T(8,128)S(1)}, f32[48,8,128]{2,1,0:T(8,128)S(1)}, u32[]{:S(2)}, u32[]{:S(2)}) collective-permute-start(f32[48,8,128]{2,1,0:T(8,128)S(1)} %get-tuple-element.85), channel_id=1, source_target_pairs={{0,2},{2,0},{1,3},{3,1},{4,6},{6,4},{5,7},{7,5},{8,10},{10,8},{9,1... | collective-permute-start | bytes 589832 | tf_op jit(solution)/shard_map/ppermute | solution.py:43
  79.5 7.1 %collective-permute-start.16 = (f32[48,16,128]{2,1,0:T(8,128)S(1)}, f32[48,16,128]{2,1,0:T(8,128)S(1)}, u32[]{:S(2)}, u32[]{:S(2)}) collective-permute-start(f32[48,16,128]{2,1,0:T(8,128)S(1)} %collective-permute-done.14.refs_3_), channel_id=1, source_target_pairs={{0,1},{1,0},{2,3},{3,2},{4,5},{5,4},{6,7},{7,6},{8,9},{9,8},{10,11... | collective-permute-start | bytes 1179656 | tf_op jit(solution)/shard_map/ppermute | solution.py:43
  80.9 4.3 %collective-permute-start.17 = (f32[48,8,128]{2,1,0:T(8,128)S(1)}, f32[48,8,128]{2,1,0:T(8,128)S(1)}, u32[]{:S(2)}, u32[]{:S(2)}) collective-permute-start(f32[48,8,128]{2,1,0:T(8,128)S(1)} %collective-permute-done.10.refs_4_), channel_id=1, source_target_pairs={{0,1},{1,0},{2,3},{3,2},{4,5},{5,4},{6,7},{7,6},{8,9},{9,8},{10,11... | collective-permute-start | bytes 589832 | tf_op jit(solution)/shard_map/ppermute | solution.py:43
  85.2 1.4 %collective-permute-start.18 = (f32[48,8,128]{2,1,0:T(8,128)S(1)}, f32[48,8,128]{2,1,0:T(8,128)S(1)}, u32[]{:S(2)}, u32[]{:S(2)}) collective-permute-start(f32[48,8,128]{2,1,0:T(8,128)S(1)} %collective-permute-done.13.refs_5_), channel_id=1, source_target_pairs={{0,1},{1,0},{2,3},{3,2},{4,5},{5,4},{6,7},{7,6},{8,9},{9,8},{10,11... | collective-permute-start | bytes 589832 | tf_op jit(solution)/shard_map/ppermute | solution.py:43
  91.1 12.4 %collective-permute-start.19 = (f32[96,128]{1,0:T(8,128)S(1)}, f32[96,128]{1,0:T(8,128)S(1)}, u32[]{:S(2)}, u32[]{:S(2)}) collective-permute-start(f32[96,128]{1,0:T(8,128)S(1)} %get-tuple-element.105), channel_id=1, source_target_pairs={{0,12},{2,14},{4,0},{6,2},{8,4},{10,6},{12,8},{14,10},{1,13},{3,15... | collective-permute-start | bytes 147464 | tf_op jit(solution)/shard_map/ppermute | solution.py:592
  95.4 8.1 %collective-permute-start.20 = (f32[96,128]{1,0:T(8,128)S(1)}, f32[96,128]{1,0:T(8,128)S(1)}, u32[]{:S(2)}, u32[]{:S(2)}) collective-permute-start(f32[96,128]{1,0:T(8,128)S(1)} %get-tuple-element.106), channel_id=1, source_target_pairs={{0,14},{2,12},{4,2},{6,0},{8,6},{10,4},{12,10},{14,8},{1,15},{3,13... | collective-permute-start | bytes 147464 | tf_op jit(solution)/shard_map/ppermute | solution.py:592
  97.5 6.0 %collective-permute-start.21 = (f32[96,128]{1,0:T(8,128)S(1)}, f32[96,128]{1,0:T(8,128)S(1)}, u32[]{:S(2)}, u32[]{:S(2)}) collective-permute-start(f32[96,128]{1,0:T(8,128)S(1)} %get-tuple-element.107), channel_id=1, source_target_pairs={{0,4},{2,6},{4,8},{6,10},{8,12},{10,14},{12,0},{14,2},{1,5},{3,7},... | collective-permute-start | bytes 147464 | tf_op jit(solution)/shard_map/ppermute | solution.py:592
  98.3 6.8 %collective-permute-start.22 = (f32[96,128]{1,0:T(8,128)S(1)}, f32[96,128]{1,0:T(8,128)S(1)}, u32[]{:S(2)}, u32[]{:S(2)}) collective-permute-start(f32[96,128]{1,0:T(8,128)S(1)} %get-tuple-element.108), channel_id=1, source_target_pairs={{0,6},{2,4},{4,10},{6,8},{8,14},{10,12},{12,2},{14,0},{1,7},{3,5},... | collective-permute-start | bytes 147464 | tf_op jit(solution)/shard_map/ppermute | solution.py:592
  98.3 6.8 %collective-permute-start.23 = (f32[96,128]{1,0:T(8,128)S(1)}, f32[96,128]{1,0:T(8,128)S(1)}, u32[]{:S(2)}, u32[]{:S(2)}) collective-permute-start(f32[96,128]{1,0:T(8,128)S(1)} %get-tuple-element.109), channel_id=1, source_target_pairs={{0,2},{2,0},{4,6},{6,4},{8,10},{10,8},{12,14},{14,12},{1,3},{3,1},... | collective-permute-start | bytes 147464 | tf_op jit(solution)/shard_map/ppermute | solution.py:592
  106.3 3.9 %collective-permute-start.25 = (f32[32,128]{1,0:T(8,128)S(1)}, f32[32,128]{1,0:T(8,128)S(1)}, u32[]{:S(2)}, u32[]{:S(2)}) collective-permute-start(f32[32,128]{1,0:T(8,128)S(1)} %get-tuple-element.112), channel_id=1, source_target_pairs={{0,2},{1,3},{2,0},{3,1},{4,6},{5,7},{6,4},{7,5},{8,10},{9,11},{10,... | collective-permute-start | bytes 49160 | tf_op jit(solution)/shard_map/ppermute | solution.py:43
  106.9 3.3 %collective-permute-start.26 = (f32[32,128]{1,0:T(8,128)S(1)}, f32[32,128]{1,0:T(8,128)S(1)}, u32[]{:S(2)}, u32[]{:S(2)}) collective-permute-start(f32[32,128]{1,0:T(8,128)S(1)} %get-tuple-element.113), channel_id=1, source_target_pairs={{0,3},{1,2},{2,1},{3,0},{4,7},{5,6},{6,5},{7,4},{8,11},{9,10},{10,... | collective-permute-start | bytes 49160 | tf_op jit(solution)/shard_map/ppermute | solution.py:43
  106.9 3.3 %collective-permute-start.24 = (f32[32,128]{1,0:T(8,128)S(1)}, f32[32,128]{1,0:T(8,128)S(1)}, u32[]{:S(2)}, u32[]{:S(2)}) collective-permute-start(f32[32,128]{1,0:T(8,128)S(1)} %get-tuple-element.111), channel_id=1, source_target_pairs={{0,1},{1,0},{2,3},{3,2},{4,5},{5,4},{6,7},{7,6},{8,9},{9,8},{10,11... | collective-permute-start | bytes 49160 | tf_op jit(solution)/shard_map/ppermute | solution.py:43
  110.3 4.7 %collective-permute-start.28 = (f32[32,128]{1,0:T(8,128)S(1)}, f32[32,128]{1,0:T(8,128)S(1)}, u32[]{:S(2)}, u32[]{:S(2)}) collective-permute-start(f32[32,128]{1,0:T(8,128)S(1)} %add_add_fusion.1), channel_id=1, source_target_pairs={{0,8},{4,12},{8,0},{12,4},{1,9},{5,13},{9,1},{13,5},{2,10},{6,14},... | collective-permute-start | bytes 49160 | tf_op jit(solution)/shard_map/ppermute | solution.py:43
  112.4 5.5 %collective-permute-start.29 = (f32[32,128]{1,0:T(8,128)S(1)}, f32[32,128]{1,0:T(8,128)S(1)}, u32[]{:S(2)}, u32[]{:S(2)}) collective-permute-start(f32[32,128]{1,0:T(8,128)S(1)} %add_add_fusion.1), channel_id=1, source_target_pairs={{0,12},{4,8},{8,4},{12,0},{1,13},{5,9},{9,5},{13,1},{2,14},{6,10},... | collective-permute-start | bytes 49160 | tf_op jit(solution)/shard_map/ppermute | solution.py:43
  112.7 5.3 %collective-permute-start.27 = (f32[32,128]{1,0:T(8,128)S(1)}, f32[32,128]{1,0:T(8,128)S(1)}, u32[]{:S(2)}, u32[]{:S(2)}) collective-permute-start(f32[32,128]{1,0:T(8,128)S(1)} %add_add_fusion.1), channel_id=1, source_target_pairs={{0,4},{4,0},{8,12},{12,8},{1,5},{5,1},{9,13},{13,9},{2,6},{6,2},{1... | collective-permute-start | bytes 49160 | tf_op jit(solution)/shard_map/ppermute | solution.py:43
